TPU v7x, 32 devices: a whole 2x2x4 slice. The times are simulated.
32 devices in a mesh: groups: 2 (over x), sample: 16 (over z, y, core).
Axes of the slice: x: 2, y: 2, z: 4, core: 2. Of those that a mesh axis runs over, the one named last changes fastest.
Arguments:
- prompt_states: bfloat16 [16384, 8192], P(('groups', 'sample')), parts along dimension 0, may hold values from -6 to 6
- page_table: int32 [128], P('groups'), parts along dimension 0, may hold values from 0 to 63, each once
- step_states: bfloat16 [2, 64, 8192], P(None, 'groups'), parts along dimension 1, may hold values from -15 to 15
- sample_order: int32 [64], P('groups'), parts along dimension 0, may hold values from 0 to 31, each once
- key_weight: bfloat16 [8192, 512], P('sample'), may hold values from -0.088388348 to 0.088388348
- value_weight: bfloat16 [8192, 512], P('sample'), may hold values from -0.0625 to 0.0625
- query_weight: bfloat16 [8192, 4096], P(None, 'sample'), may hold values from -0.121533978 to 0.121533978
- out_weight: bfloat16 [4096, 8192], P('sample'), may hold values from -0.125 to 0.125
Outputs:
- attn_out: bfloat16 [2, 64, 8192], P(None, 'groups', 'sample'), parts along dimension 1
There are 2 independent parts, one for each index of `groups`. A program takes and returns all parts, laid end to end along the dimension named above; an argument that names none is the same for every part. Nothing has to cross between parts.
Inputs may be any that keep to these rules, and one draw needn't show every extreme that they name: `page_table`: A permutation: entry p * 64 + j is the physical page that holds logical page j of prompt p; physical page r is rows r * 128 to (r + 1) * 128 - 1 of prompt_states. `sample_order`: A permutation; completion i continues prompt sample_order[i] // 32.
All inputs are finite; a program needn't handle non-finite values.
Results may differ from a plain program's by a relative error of at most 0.034.
Values may be sent and summed in bfloat16 or wider, within the bound.
No kernel may reach another device: no remote copies, remote signals or barrier semaphores. Data moves between devices by JAX's collectives and lax.ppermute only.
A program may use at most 128 MiB of HBM per device.

v0:
```python
import jax
import jax.numpy as jnp
from jax import lax
from jax.sharding import PartitionSpec as P

D = 8192
HEAD_DIM = 128
KV_HEADS = 4
GQA = 8
PAGE = 128
PROMPT_PAGES = 64


rope_base = 1000000.0


def rotate(vector, position):
    half_dim = vector.shape[-1] // 2
    frequency = rope_base ** (-jnp.arange(half_dim, dtype=jnp.float32) * 2.0 / vector.shape[-1])
    angles = position.astype(jnp.float32)[..., None] * frequency
    cosine = jnp.cos(angles)
    sine_part = jnp.sin(angles)
    first_half = vector[..., :half_dim]
    second_half = vector[..., half_dim:]
    return jnp.concatenate(
        [
            first_half * cosine - second_half * sine_part,
            second_half * cosine + first_half * sine_part,
        ],
        axis=-1,
    )


def finish_heads(prefix_top, prefix_total, prefix_sum, queries, new_keys, new_values):
    score_scale = queries.shape[-1] ** (-0.5)
    query_wide = queries.astype(jnp.float32)
    key_wide = new_keys.astype(jnp.float32)
    value_wide = new_values.astype(jnp.float32)
    own_score = jnp.sum(query_wide * key_wide, axis=-1) * score_scale
    back_score = jnp.sum(query_wide[1] * key_wide[0], axis=-1) * score_scale
    first_high = jnp.maximum(prefix_top[0], own_score[0])
    first_old = jnp.exp(prefix_top[0] - first_high)
    first_own = jnp.exp(own_score[0] - first_high)
    first_out = (first_old[..., None] * prefix_sum[0] + first_own[..., None] * value_wide[0]) / (
        first_old * prefix_total[0] + first_own
    )[..., None]
    second_high = jnp.maximum(jnp.maximum(prefix_top[1], own_score[1]), back_score)
    second_old = jnp.exp(prefix_top[1] - second_high)
    second_back = jnp.exp(back_score - second_high)
    second_own = jnp.exp(own_score[1] - second_high)
    second_num = (
        second_old[..., None] * prefix_sum[1]
        + second_back[..., None] * value_wide[0]
        + second_own[..., None] * value_wide[1]
    )
    second_out = second_num / (second_old * prefix_total[1] + second_back + second_own)[..., None]
    return jnp.stack([first_out, second_out]).astype(jnp.bfloat16)


def on_device(
    prompt_states,
    page_table,
    step_states,
    sample_order,
    key_weight,
    value_weight,
    query_weight,
    out_weight,
):
    devices = lax.axis_size("sample")
    own_index = lax.axis_index("sample")
    row_count = prompt_states.shape[0]
    pages_here = row_count // PAGE
    heads_here = query_weight.shape[1] // HEAD_DIM
    total_pages = page_table.shape[0]
    prompts = total_pages // PROMPT_PAGES
    samples = sample_order.shape[0]
    group_size = samples // prompts
    score_scale = HEAD_DIM ** (-0.5)
    own_kv = own_index * heads_here // GQA
    slot_of = (
        jnp.zeros((total_pages,), jnp.int32)
        .at[page_table]
        .set(jnp.arange(total_pages, dtype=jnp.int32))
    )
    local_slots = lax.dynamic_slice_in_dim(slot_of, own_index * pages_here, pages_here)
    positions = (local_slots % PROMPT_PAGES * PAGE)[:, None] + jnp.arange(PAGE, dtype=jnp.int32)[
        None, :
    ]
    positions = positions.reshape(row_count)
    wide_states = step_states.reshape(2 * samples, D)
    key_piece = lax.all_gather(key_weight, "sample", axis=0, tiled=True)
    value_piece = lax.all_gather(value_weight, "sample", axis=0, tiled=True)
    piece_rows = key_piece.shape[0]
    key_acc = jnp.einsum(
        "rn,nkd->krd",
        prompt_states,
        key_piece.reshape(piece_rows, KV_HEADS, HEAD_DIM),
        preferred_element_type=jnp.float32,
    )
    value_acc = jnp.einsum(
        "rn,nkd->krd",
        prompt_states,
        value_piece.reshape(piece_rows, KV_HEADS, HEAD_DIM),
        preferred_element_type=jnp.float32,
    )
    key_head = lax.dynamic_slice_in_dim(key_piece, own_kv * HEAD_DIM, HEAD_DIM, 1)
    value_head = lax.dynamic_slice_in_dim(value_piece, own_kv * HEAD_DIM, HEAD_DIM, 1)
    key_step = jnp.dot(wide_states, key_head, preferred_element_type=jnp.float32)
    value_step = jnp.dot(wide_states, value_head, preferred_element_type=jnp.float32)
    key_acc, value_acc, key_step, value_step = (key_acc, value_acc, key_step, value_step)
    page_keys = rotate(key_acc, positions[None, :]).astype(jnp.bfloat16)
    page_values = value_acc.astype(jnp.bfloat16)
    step_place = (PROMPT_PAGES * PAGE + jnp.arange(2, dtype=jnp.int32))[:, None, None]
    queries = jnp.dot(wide_states, query_weight, preferred_element_type=jnp.float32).reshape(
        2, samples, heads_here, HEAD_DIM
    )
    queries = rotate(queries, step_place).astype(jnp.bfloat16)
    new_keys = rotate(key_step.reshape(2, samples, HEAD_DIM), step_place[:, :, 0]).astype(
        jnp.bfloat16
    )
    new_values = value_step.reshape(2, samples, HEAD_DIM).astype(jnp.bfloat16)
    inverse = (
        jnp.zeros((samples,), jnp.int32).at[sample_order].set(jnp.arange(samples, dtype=jnp.int32))
    )
    spread = devices // KV_HEADS
    send_keys = jnp.repeat(page_keys, spread, axis=0)
    send_values = jnp.repeat(page_values, spread, axis=0)
    all_keys, all_values = (
        lax.all_to_all(send_keys, "sample", split_axis=0, concat_axis=1, tiled=True),
        lax.all_to_all(send_values, "sample", split_axis=0, concat_axis=1, tiled=True),
    )
    logical = page_table.reshape(prompts, PROMPT_PAGES)
    all_keys = all_keys.reshape(total_pages, PAGE, HEAD_DIM)[logical].reshape(
        prompts, PROMPT_PAGES * PAGE, HEAD_DIM
    )
    all_values = all_values.reshape(total_pages, PAGE, HEAD_DIM)[logical].reshape(
        prompts, PROMPT_PAGES * PAGE, HEAD_DIM
    )
    sorted_query = queries[:, inverse].reshape(2, prompts, group_size, heads_here, HEAD_DIM)
    scores = (
        jnp.einsum("spmhd,pld->spmhl", sorted_query, all_keys, preferred_element_type=jnp.float32)
        * score_scale
    )
    prefix_top = jnp.max(scores, axis=-1)
    weights = jnp.exp(scores - prefix_top[..., None])
    prefix_total = jnp.sum(weights, axis=-1)
    prefix_sum = jnp.einsum(
        "spmhl,pld->spmhd",
        weights.astype(jnp.bfloat16),
        all_values,
        preferred_element_type=jnp.float32,
    )
    prefix_top = prefix_top.reshape(2, samples, heads_here)[:, sample_order]
    prefix_total = prefix_total.reshape(2, samples, heads_here)[:, sample_order]
    prefix_sum = prefix_sum.reshape(2, samples, heads_here, HEAD_DIM)[:, sample_order]
    head_out = finish_heads(
        prefix_top,
        prefix_total,
        prefix_sum,
        queries,
        new_keys[:, :, None, :],
        new_values[:, :, None, :],
    )
    flat_heads = head_out.reshape(2, samples, heads_here * HEAD_DIM)
    head_terms = jnp.einsum(
        "srk,kd->srd", flat_heads, out_weight, preferred_element_type=jnp.float32
    )
    return lax.psum_scatter(
        head_terms.astype(jnp.bfloat16), "sample", scatter_dimension=2, tiled=True
    )


def solution(mesh):
    in_specs = (
        P(("groups", "sample"), None),
        P("groups"),
        P(None, "groups", None),
        P("groups"),
        P("sample", None),
        P("sample", None),
        P(None, "sample"),
        P("sample", None),
    )
    out_specs = P(None, "groups", "sample")
    return jax.shard_map(
        on_device, mesh=mesh, in_specs=in_specs, out_specs=out_specs, check_vma=False
    )
```

profile of v0, /device:TPU:0, one launch (start us, length us, event | category | flops | bytes accessed | tf_op | source)
XLA Modules:
  0.0 351.3 jit_solution(6273337491218514646)
XLA Ops:
  6.5 0.7 all-gather.3.cloned.1.call-update
  7.3 0.0 all-gather.5.cloned.1.call-start
  7.3 0.7 all-gather.5.cloned.1.call-update
  8.0 0.7 compare_select_fusion.2
  8.7 0.8 scatter_custom_fusion
  9.5 0.1 fusion.61
  9.6 0.1 convert_bitcast_fusion
  9.6 0.5 multiply_cosine_fusion
  10.2 77.0 %all-gather.3.cloned.1.call-done = bf16[8192,512]{1,0:T(8,128)(2,1)} async-done(((bf16[512,512]{1,0:T(8,128)(2,1)}), bf16[8192,512]{1,0:T(8,128)(2,1)}) %all-gather.3.cloned.1.call-update) | async-done | bytes 8388624 | tf_op jit(solution)/shard_map/all_gather | solution.py:92
  87.2 11.5 %copy.36 = bf16[8192,512]{0,1:T(8,128)(2,1)} copy(bf16[8192,512]{1,0:T(8,128)(2,1)} %all-gather.3.cloned.1.call-done) | data formatting | bytes 16777216 | tf_op jit(solution)/shard_map/all_gather | solution.py:92
  98.6 9.5 %fusion.16 = f32[4,512,128]{1,2,0:T(8,128)S(1)} fusion(bf16[8192,4,128]{0,2,1:T(8,128)(2,1)} %bitcast.153, bf16[512,8192]{1,0:T(8,128)(2,1)} %param.8), kind=kOutput, calls=%fused_computation.26 | convolution fusion | flops 4294967296 | bytes 17825792 | tf_op jit(solution)/shard_map/rn,nkd->krd/dot_general | solution.py:95
  108.2 0.2 subtract_convert_fusion
  108.4 0.3 copy.37
  108.7 1.8 broadcast_in_dim.13
  110.5 3.7 %all-to-all-start = ((bf16[16,512,128]{2,1,0:T(8,128)(2,1)}), bf16[16,512,128]{2,1,0:T(8,128)(2,1)S(1)}, u32[]{:S(2)}, u32[]{:S(2)}) async-start(bf16[16,512,128]{2,1,0:T(8,128)(2,1)} %bitcast.4), calls=%async_computation | async-start | bytes 4194304 | tf_op jit(solution)/shard_map/all_to_all | solution.py:130
  114.2 6.4 %copy.61 = bf16[256,8192]{1,0:T(8,128)(2,1)} copy(bf16[256,8192]{0,1:T(8,128)(2,1)} %bitcast.158) | data formatting | bytes 8388608 | tf_op jit(solution)/shard_map/dot_general | solution.py:115
  120.6 0.1 multiply_cosine_fusion.1
  120.7 4.3 %fusion.37 = f32[2,32,2,128]{3,1,2,0:T(8,128)S(1)} fusion(bf16[2,128,8192,1]{2,1,0,3:T(8,128)(2,1)} %bitcast.152, bf16[2,32,8192]{2,1,0:T(8,128)(2,1)S(1)} %copy-done), kind=kOutput, calls=%fused_computation.33 | convolution fusion | flops 268435456 | bytes 5308416 | tf_op jit(solution)/shard_map/dot_general | solution.py:115
  125.1 69.1 %all-gather.5.cloned.1.call-done = bf16[8192,512]{1,0:T(8,128)(2,1)} async-done(((bf16[512,512]{1,0:T(8,128)(2,1)}), bf16[8192,512]{1,0:T(8,128)(2,1)}) %all-gather.5.cloned.1.call-update) | async-done | bytes 8388624 | tf_op jit(solution)/shard_map/all_gather | solution.py:93
  194.2 11.4 %copy.44 = bf16[8192,512]{0,1:T(8,128)(2,1)} copy(bf16[8192,512]{1,0:T(8,128)(2,1)} %all-gather.5.cloned.1.call-done) | data formatting | bytes 16777216 | tf_op jit(solution)/shard_map/all_gather | solution.py:93
  205.6 11.1 %fusion.22 = bf16[4,512,128]{1,2,0:T(8,128)(2,1)} fusion(bf16[8192,4,128]{0,2,1:T(8,128)(2,1)} %bitcast.154, bf16[512,8192]{1,0:T(8,128)(2,1)} %param.8), kind=kOutput, calls=%fused_computation.28 | convolution fusion | flops 4295229440 | bytes 17301504 | tf_op jit(solution)/shard_map/rn,nkd->krd/dot_general | solution.py:101
  216.7 2.1 copy.45
  218.7 0.0 all-to-all-done
  218.7 2.8 broadcast_in_dim.17
  221.6 7.3 %all-to-all-start.1 = ((bf16[16,512,128]{2,1,0:T(8,128)(2,1)}), bf16[16,512,128]{2,1,0:T(8,128)(2,1)}, u32[]{:S(2)}, u32[]{:S(2)}) async-start(bf16[16,512,128]{2,1,0:T(8,128)(2,1)} %bitcast.26), calls=%async_computation.1 | async-start | bytes 4194304 | tf_op jit(solution)/shard_map/all_to_all | solution.py:131
  228.9 0.0 reduce-scatter.2.cloned.1.call-start
  228.9 0.1 subtract_convert_fusion.1
  229.0 0.1 fusion.73
  229.2 0.9 scatter_custom_fusion.1
  230.1 0.6 gather_fusion.1
  230.7 2.1 fusion.14
  232.8 0.1 subtract_convert_fusion.2
  232.9 0.1 fusion.53
  233.0 0.1 maximum_convert_fusion
  233.1 0.1 fusion.43
  233.2 0.1 multiply_reduce_fusion
  233.3 2.1 fusion.34
  235.4 2.1 gather_fusion
  237.5 4.2 %fusion.77 = (f32[2,32,2]{1,2,0:T(2,128)S(1)}, f32[2,1,32,2,8192]{4,2,3,0,1:T(8,128)}) fusion(bf16[8192,128,1,1]{1,0,3,2:T(8,128)(2,1)} %bitcast.156, bf16[2,32,2,128]{3,2,0,1:T(2,128)(2,1)S(1)} %bitcast.163), kind=kOutput, calls=%fused_computation.111 | convolution fusion | flops 270532480 | bytes 6324736 | tf_op jit(solution)/shard_map/spmhd,pld->spmhl/dot_general | solution.py:142
  241.8 0.1 copy.41
  241.9 2.9 fusion.6
  244.8 0.1 copy.48
  244.9 0.6 gather_fusion.5
  245.6 0.1 copy.49
  245.6 0.1 copy.56
  245.7 0.6 gather_fusion.2
  246.4 0.1 copy.42
  246.4 0.1 copy.51
  246.5 0.1 copy.43
  246.6 0.1 copy.47
  246.7 0.1 copy.50
  246.8 0.1 copy.53
  246.9 0.1 copy.54
  247.0 0.1 copy.55
  247.1 0.1 copy.57
  247.2 22.9 %all-to-all-done.1 = bf16[16,512,128]{2,1,0:T(8,128)(2,1)} async-done(((bf16[16,512,128]{2,1,0:T(8,128)(2,1)}), bf16[16,512,128]{2,1,0:T(8,128)(2,1)}, u32[]{:S(2)}, u32[]{:S(2)}) %all-to-all-start.1) | async-done | bytes 2097184 | tf_op jit(solution)/shard_map/all_to_all | solution.py:131
  270.0 2.5 gather_fusion.3
  272.6 3.0 fusion.25
  275.6 0.1 copy.46
  275.6 0.6 gather_fusion.4
  276.3 0.3 fusion.50
  276.7 4.0 %convolution_convert_fusion = bf16[2,32,8192]{2,1,0:T(8,128)(2,1)} fusion(bf16[256,8192]{1,0:T(8,128)(2,1)} %param.15, bf16[1,32,256]{2,1,0:T(8,128)(2,1)S(1)} %stack.10, bf16[1,32,256]{2,1,0:T(8,128)(2,1)S(1)} %stack.9), kind=kOutput, calls=%fused_computation.10 | convolution fusion | flops 268976128 | bytes 5275648 | tf_op jit(solution)/shard_map/srk,kd->srd/dot_general | solution.py:166
  280.7 0.0 reduce-scatter.2.cloned.1.call-update
  280.7 64.1 %reduce-scatter.2.cloned.1.call-done = bf16[2,32,512]{2,1,0:T(8,128)(2,1)} async-done(((bf16[2,32,8192]{2,1,0:T(8,128)(2,1)}), bf16[2,32,512]{2,1,0:T(8,128)(2,1)}) %reduce-scatter.2.cloned.1.call-update) | async-done | bytes 65552 | tf_op jit(solution)/shard_map/reduce_scatter | solution.py:169
  (23 shorter events, 0.2 us)
Async XLA Ops:
  6.5 114.2 %copy-start = (bf16[2,32,8192]{2,1,0:T(8,128)(2,1)S(1)}, bf16[2,32,8192]{2,1,0:T(8,128)(2,1)}, u32[]{:S(2)}) copy-start(bf16[2,32,8192]{2,1,0:T(8,128)(2,1)} %param.10) | copy-start | bytes 3145732
  6.5 80.6 %all-gather.3.cloned.1.call-start = ((), (), s32[]{:S(2)}) async-start(), calls=%async_computation.3 | async-start | bytes 8912896 | tf_op jit(solution)/shard_map/all_gather | solution.py:92
  7.3 186.9 %all-gather.5.cloned.1.call-start = ((), (), s32[]{:S(2)}) async-start(), calls=%async_computation.4 | async-start | bytes 8912896 | tf_op jit(solution)/shard_map/all_gather | solution.py:93
  110.5 108.3 %all-to-all-start = ((bf16[16,512,128]{2,1,0:T(8,128)(2,1)}), bf16[16,512,128]{2,1,0:T(8,128)(2,1)S(1)}, u32[]{:S(2)}, u32[]{:S(2)}) async-start(bf16[16,512,128]{2,1,0:T(8,128)(2,1)} %bitcast.4), calls=%async_computation | async-start | bytes 4194304 | tf_op jit(solution)/shard_map/all_to_all | solution.py:130
  216.7 12.5 %copy-start.1 = (s32[32]{0:T(128)S(1)}, s32[32]{0:T(128)}, u32[]{:S(2)}) copy-start(s32[32]{0:T(128)} %param.11) | copy-start | bytes 388
  221.6 48.4 %all-to-all-start.1 = ((bf16[16,512,128]{2,1,0:T(8,128)(2,1)}), bf16[16,512,128]{2,1,0:T(8,128)(2,1)}, u32[]{:S(2)}, u32[]{:S(2)}) async-start(bf16[16,512,128]{2,1,0:T(8,128)(2,1)} %bitcast.26), calls=%async_computation.1 | async-start | bytes 4194304 | tf_op jit(solution)/shard_map/all_to_all | solution.py:131
  228.9 115.9 %reduce-scatter.2.cloned.1.call-start = ((), (), s32[]{:S(2)}) async-start(), calls=%async_computation.5 | async-start | bytes 1114112 | tf_op jit(solution)/shard_map/reduce_scatter | solution.py:169
Sparse Core Ops, SparseCore 0:
  9.5 77.5 all-gather.2
  89.3 104.7 all-gather.4
  280.8 63.8 reduce-scatter.1
where the time goes:
time: 352 us; the launch traced here: 351 us
  waiting for transfers between devices  234 us (66%)
  local copies, waits for them, and re-layouts  46.4 us (13%)
  matrix products  40.4 us (11%)
  between operations  13.4 us (4%)
  starting transfers between devices  11.1 us (3%)
  other arithmetic  5.57 us (2%)
    all_gather x1, waiting for transfers between devices, on_device(): key_piece = lax.all_gather(key_weight, 'sample', axis=0, tiled=True)  77 us
    all_gather x1, waiting for transfers between devices, on_device(): value_piece = lax.all_gather(value_weight, 'sample', axis=0, tiled=True)  69.1 us
    reduce_scatter x1, waiting for transfers between devices, on_device(): lax.psum_scatter(head_terms.astype(jnp.bfloat16), 'sample', scatter_dimen...  64.1 us
    all_to_all x1, waiting for transfers between devices, on_device(): lax.all_to_all(send_values, 'sample', split_axis=0, concat_axis=1, tiled=...  22.9 us
    all_gather x1, local copies, waits for them, and re-layouts, on_device(): key_piece = lax.all_gather(key_weight, 'sample', axis=0, tiled=True)  11.5 us
    all_gather x1, local copies, waits for them, and re-layouts, on_device(): value_piece = lax.all_gather(value_weight, 'sample', axis=0, tiled=True)  11.4 us
    dot_general x1, matrix products, on_device(): jnp.einsum('rn,nkd->krd', prompt_states, value_piece.reshape(piece_rows,...  11.1 us
    dot_general x1, matrix products, on_device(): jnp.einsum('rn,nkd->krd', prompt_states, key_piece.reshape(piece_rows, KV...  9.54 us
  transfers between devices with their start and end apart: 5, of which 4 were waited for; matrix products, arithmetic and copies ran while one was open for 22% of the time, Pallas kernels for 0%

commit v1 on v0

v1 whole, which is shorter than its diff:
```python
import jax
import jax.numpy as jnp
from jax import lax
from jax.sharding import PartitionSpec as P

D = 8192
HEAD_DIM = 128
KV_HEADS = 4
GQA = 8
PAGE = 128
PROMPT_PAGES = 64
LINE = 4

rope_base = 1000000.0


def rope_tables(position):
    half_dim = HEAD_DIM // 2
    frequency = rope_base ** (-jnp.arange(half_dim, dtype=jnp.float32) * 2.0 / HEAD_DIM)
    angles = position.astype(jnp.float32)[..., None] * frequency
    return jnp.cos(angles), jnp.sin(angles)


def turn(vector, tables):
    cosine, sine_part = tables
    half_dim = HEAD_DIM // 2
    first_half = vector[..., :half_dim]
    second_half = vector[..., half_dim:]
    return jnp.concatenate(
        [
            first_half * cosine - second_half * sine_part,
            second_half * cosine + first_half * sine_part,
        ],
        axis=-1,
    )


def finish_heads(prefix_top, prefix_total, prefix_sum, queries, new_keys, new_values):
    score_scale = queries.shape[-1] ** (-0.5)
    query_wide = queries.astype(jnp.float32)
    key_wide = new_keys.astype(jnp.float32)
    value_wide = new_values.astype(jnp.float32)
    own_score = jnp.sum(query_wide * key_wide, axis=-1) * score_scale
    back_score = jnp.sum(query_wide[1] * key_wide[0], axis=-1) * score_scale
    first_high = jnp.maximum(prefix_top[0], own_score[0])
    first_old = jnp.exp(prefix_top[0] - first_high)
    first_own = jnp.exp(own_score[0] - first_high)
    first_out = (first_old[..., None] * prefix_sum[0] + first_own[..., None] * value_wide[0]) / (
        first_old * prefix_total[0] + first_own
    )[..., None]
    second_high = jnp.maximum(jnp.maximum(prefix_top[1], own_score[1]), back_score)
    second_old = jnp.exp(prefix_top[1] - second_high)
    second_back = jnp.exp(back_score - second_high)
    second_own = jnp.exp(own_score[1] - second_high)
    second_num = (
        second_old[..., None] * prefix_sum[1]
        + second_back[..., None] * value_wide[0]
        + second_own[..., None] * value_wide[1]
    )
    second_out = second_num / (second_old * prefix_total[1] + second_back + second_own)[..., None]
    return jnp.stack([first_out, second_out]).astype(jnp.bfloat16)


def mover(groups, devices):
    deep = devices // LINE

    def move(value, step):
        pairs = []
        for g in range(groups):
            for s in range(devices):
                a, b, c = s // LINE, s // 2 % 2, s % 2
                to_g, to_a, to_b, to_c = step(g, a, b, c)
                to_s = (to_a % deep) * LINE + to_b * 2 + to_c
                pairs.append((g * devices + s, to_g * devices + to_s))
        return lax.ppermute(value, ("groups", "sample"), pairs)

    along_z = lambda v: move(v, lambda g, a, b, c: (g, a + 1, b, c))
    along_y = lambda v: move(v, lambda g, a, b, c: (g, a, 1 - b, c))
    along_x = lambda v: move(v, lambda g, a, b, c: (g ^ 1, a, b, c))
    in_chip = lambda v: move(v, lambda g, a, b, c: (g, a, b, 1 - c))
    return along_z, along_y, along_x, in_chip


def on_device(
    prompt_states,
    page_table,
    step_states,
    sample_order,
    key_weight,
    value_weight,
    query_weight,
    out_weight,
):
    devices = lax.axis_size("sample")
    groups = lax.axis_size("groups")
    own_index = lax.axis_index("sample")
    plane = lax.axis_index("groups") % 2
    deep = devices // LINE
    own_a, own_b, own_c = own_index // LINE, own_index // 2 % 2, own_index % 2
    along_z, along_y, along_x, in_chip = mover(groups, devices)
    row_count = prompt_states.shape[0]
    pages_here = row_count // PAGE
    heads_here = query_weight.shape[1] // HEAD_DIM
    total_pages = page_table.shape[0]
    prompts = total_pages // PROMPT_PAGES
    samples = sample_order.shape[0]
    group_size = samples // prompts
    score_scale = HEAD_DIM ** (-0.5)
    own_kv = own_index * heads_here // GQA
    wide_states = step_states.reshape(2 * samples, D)
    width = key_weight.shape[0]
    kv_cols = key_weight.shape[1]
    half = kv_cols // 2
    quarter = kv_cols // 4

    first = plane == 0
    key_mine = jnp.where(first, key_weight[:, :half], key_weight[:, half:])
    key_other = jnp.where(first, key_weight[:, half:], key_weight[:, :half])
    value_mine = jnp.concatenate(
        [
            jnp.where(first, value_weight[:, :quarter], value_weight[:, quarter:half]),
            value_weight[:, half:],
        ],
        axis=1,
    )
    value_other = jnp.where(first, value_weight[:, quarter:half], value_weight[:, :quarter])

    def columns(source, k, flip, core):
        block = ((own_a + deep - k) % deep) * LINE + (own_b ^ flip) * 2 + core
        return lax.dynamic_slice_in_dim(source, block * width, width, 1)

    places = [(k, flip) for k in range(deep) for flip in (0, 1)]
    sent = jnp.stack([columns(prompt_states, k, flip, 1 - own_c) for k, flip in places])
    got = in_chip(sent)
    left = {
        place: jnp.concatenate(
            [columns(prompt_states, *place, own_c), got[i], columns(wide_states, *place, own_c)]
        )
        for i, place in enumerate(places)
    }

    def gather(mine, other, swapped):
        pieces = {}
        held = mine
        for k in range(deep):
            if k:
                held = along_z(held)
            pieces[k, 0] = held
            pieces[k, 1] = along_y(held)
        others = {}
        for place in places:
            others[place] = other if place == (0, 0) else along_x(pieces[place][:, :swapped])
        mine_acc = other_acc = 0.0
        for place in places:
            mine_acc = mine_acc + jnp.dot(
                left[place], pieces[place], preferred_element_type=jnp.float32
            )
            other_acc = other_acc + jnp.dot(
                left[place], others[place], preferred_element_type=jnp.float32
            )
        return mine_acc, other_acc

    def close(acc):
        back = in_chip(acc[row_count:])
        return jnp.concatenate([acc[:row_count] + back[:row_count], acc[2 * row_count :] + back[row_count:]])

    step_place = PROMPT_PAGES * PAGE + jnp.arange(2, dtype=jnp.int32)
    step_tables = tuple(t[:, None, :] for t in rope_tables(step_place))
    queries = jnp.dot(wide_states, query_weight, preferred_element_type=jnp.float32)
    queries = queries.reshape(2, samples, heads_here, HEAD_DIM).transpose(2, 0, 1, 3)
    queries = turn(queries, step_tables).astype(jnp.bfloat16)
    rows = heads_here * 2 * samples
    all_queries = lax.all_gather(queries.reshape(rows, HEAD_DIM), "sample", axis=0, tiled=True)
    all_queries = all_queries.reshape(KV_HEADS, devices // KV_HEADS * rows, HEAD_DIM)

    own_pages = own_index * pages_here + jnp.arange(pages_here, dtype=jnp.int32)
    slots = jnp.sum(
        jnp.where(
            page_table[None, :] == own_pages[:, None],
            jnp.arange(total_pages, dtype=jnp.int32)[None, :],
            0,
        ),
        axis=1,
    )
    positions = (slots % PROMPT_PAGES * PAGE)[:, None] + jnp.arange(PAGE, dtype=jnp.int32)[None, :]
    cosine, sine_part = rope_tables(positions.reshape(row_count))

    key_m, key_o = gather(key_mine, key_other, half)
    keys = close(jnp.concatenate([key_m, key_o], axis=1))
    keys = jnp.where(
        first, keys, jnp.concatenate([keys[:, half:], keys[:, :half]], axis=1)
    ).reshape(-1, KV_HEADS, HEAD_DIM)
    prefix_keys = turn(keys[:row_count], (cosine[:, None], sine_part[:, None])).astype(jnp.bfloat16)
    key_step = lax.dynamic_slice_in_dim(keys[row_count:], own_kv, 1, 1)
    new_keys = turn(key_step.reshape(2, samples, HEAD_DIM), step_tables).astype(jnp.bfloat16)

    scores = (
        jnp.einsum("krd,lkd->krl", all_queries, prefix_keys, preferred_element_type=jnp.float32)
        * score_scale
    )
    if prompts > 1:
        token_prompt = jnp.repeat(slots // PROMPT_PAGES, PAGE)
        row_prompt = jnp.tile(sample_order // group_size, scores.shape[1] // samples)
        scores = jnp.where(row_prompt[:, None] == token_prompt[None, :], scores, -1e30)
    top = jnp.max(scores, axis=-1)
    weights = jnp.exp(scores - top[..., None])
    total = jnp.sum(weights, axis=-1)
    stats = jnp.stack([top.reshape(devices, rows), total.reshape(devices, rows)], axis=1)
    stats = lax.all_to_all(stats, "sample", split_axis=0, concat_axis=0, tiled=True)
    tops, totals = stats[:, 0], stats[:, 1]
    prefix_top = jnp.max(tops, axis=0)
    factors = jnp.exp(tops - prefix_top[None])
    prefix_total = jnp.sum(factors * totals, axis=0)

    value_m, value_o = gather(value_mine, value_other, quarter)
    values = close(jnp.concatenate([value_m[:, :quarter], value_o, value_m[:, quarter:]], axis=1))
    values = jnp.where(
        first,
        values,
        jnp.concatenate([values[:, quarter:half], values[:, :quarter], values[:, half:]], axis=1),
    ).astype(jnp.bfloat16).reshape(-1, KV_HEADS, HEAD_DIM)
    new_values = lax.dynamic_slice_in_dim(values[row_count:], own_kv, 1, 1)
    new_values = new_values.reshape(2, samples, HEAD_DIM)

    partial = jnp.einsum(
        "krl,lkd->krd",
        weights.astype(jnp.bfloat16),
        values[:row_count],
        preferred_element_type=jnp.float32,
    ).astype(jnp.bfloat16)
    partial = lax.all_to_all(
        partial.reshape(devices, rows, HEAD_DIM), "sample", split_axis=0, concat_axis=0, tiled=True
    )
    prefix_sum = jnp.sum(partial.astype(jnp.float32) * factors[..., None], axis=0)

    by_head = (heads_here, 2, samples)
    head_out = finish_heads(
        prefix_top.reshape(by_head).swapaxes(0, 1),
        prefix_total.reshape(by_head).swapaxes(0, 1),
        prefix_sum.reshape(by_head + (HEAD_DIM,)).swapaxes(0, 1),
        queries.swapaxes(0, 1),
        new_keys[:, None],
        new_values[:, None],
    )
    flat_heads = head_out.transpose(0, 2, 1, 3).reshape(2 * samples, heads_here * HEAD_DIM)
    terms = jnp.dot(flat_heads, out_weight, preferred_element_type=jnp.float32).astype(jnp.bfloat16)
    terms = terms.reshape(2 * samples, devices, -1).swapaxes(0, 1)
    terms = lax.all_to_all(terms, "sample", split_axis=0, concat_axis=0, tiled=True)
    attn_out = jnp.sum(terms.astype(jnp.float32), axis=0).astype(jnp.bfloat16)
    return attn_out.reshape(2, samples, -1)


def solution(mesh):
    in_specs = (
        P(("groups", "sample"), None),
        P("groups"),
        P(None, "groups", None),
        P("groups"),
        P("sample", None),
        P("sample", None),
        P(None, "sample"),
        P("sample", None),
    )
    out_specs = P(None, "groups", "sample")
    return jax.shard_map(
        on_device, mesh=mesh, in_specs=in_specs, out_specs=out_specs, check_vma=False
    )
```

time: 352 us -> 258 us (0.73)
  waiting for transfers between devices: 234 us -> 77 us
  blocking collectives: 0 us -> 53 us
  starting transfers between devices: 11.1 us -> 40.6 us
  between operations: 13.4 us -> 0.87 us
  other arithmetic: 5.57 us -> 17.1 us
  local copies, waits for them, and re-layouts: 46.4 us -> 36 us
  matrix products: 40.4 us -> 32.3 us
    all_gather x2 -> x0, waiting for transfers between devices: 146 us -> none  [the longest x1 77 us: on_device(): key_piece = lax.all_gather(key_weight, 'sample', axis=0, tiled=True)]
    reduce_scatter x1 -> x0, waiting for transfers between devices: 64.1 us -> none  [on_device(): lax.psum_scatter(head_terms.astype(jnp.bfloat16), 'sample', scatter_dimen...]
    ppermute x0 -> x31, waiting for transfers between devices: none -> 56.7 us  [move(): return lax.ppermute(value, ('groups', 'sample'), pairs)]
    ppermute x0 -> x31, starting transfers between devices: none -> 33.5 us  [move(): return lax.ppermute(value, ('groups', 'sample'), pairs)]
    all_to_all x0 -> x1, blocking collectives: none -> 28.7 us  [on_device(): lax.all_to_all(terms, 'sample', split_axis=0, concat_axis=0, tiled=True)]
    all_gather x0 -> x1, blocking collectives: none -> 24.3 us  [on_device(): lax.all_gather(queries.reshape(rows, HEAD_DIM), 'sample', axis=0, tiled=T...]
    all_gather x2 -> x0, local copies, waits for them, and re-layouts: 22.9 us -> none  [the longest x1 11.5 us: on_device(): key_piece = lax.all_gather(key_weight, 'sample', axis=0, tiled=True)]
    unnamed x4 -> x35, local copies, waits for them, and re-layouts: 0.01 us -> 17 us
  transfers between devices with their start and end apart: 5 -> 33, of which waited for: 4 -> 12; matrix products, arithmetic and copies ran while one was open for 22% -> 19% of each run, Pallas kernels for 0% -> 0%
where the time goes in v1:
time: 258 us; the launch traced here: 257 us
  waiting for transfers between devices  77 us (30%)
  blocking collectives  53 us (21%)
  starting transfers between devices  40.6 us (16%)
  local copies, waits for them, and re-layouts  36 us (14%)
  matrix products  32.3 us (13%)
  other arithmetic  17.1 us (7%)
    ppermute x31, waiting for transfers between devices, move(): return lax.ppermute(value, ('groups', 'sample'), pairs)  56.7 us
    ppermute x31, starting transfers between devices, move(): return lax.ppermute(value, ('groups', 'sample'), pairs)  33.5 us
    all_to_all x1, blocking collectives, on_device(): lax.all_to_all(terms, 'sample', split_axis=0, concat_axis=0, tiled=True)  28.7 us
    all_gather x1, blocking collectives, on_device(): lax.all_gather(queries.reshape(rows, HEAD_DIM), 'sample', axis=0, tiled=T...  24.3 us
    unnamed x35, local copies, waits for them, and re-layouts  17 us
    all_to_all x1, waiting for transfers between devices, on_device(): lax.all_to_all(partial.reshape(devices, rows, HEAD_DIM), 'sample', split_...  14.1 us
    dot_general x16, matrix products, gather(): jnp.dot(left[place], pieces[place], preferred_element_type=jnp.float32)  13.5 us
    dot_general x16, matrix products, gather(): jnp.dot(left[place], others[place], preferred_element_type=jnp.float32)  7.51 us
  transfers between devices with their start and end apart: 33, of which 12 were waited for; matrix products, arithmetic and copies ran while one was open for 19% of the time, Pallas kernels for 0%

profile of v1, /device:TPU:0, one launch (start us, length us, event | category | flops | bytes accessed | tf_op | source)
XLA Modules:
  0.0 256.9 jit_solution(7988110919610893164)
XLA Ops:
  0.0 1.9 bitcast_dynamic-update-slice_fusion.7
  1.9 1.9 bitcast_dynamic-update-slice_fusion.6
  3.8 1.9 bitcast_dynamic-update-slice_fusion.5
  5.7 1.9 bitcast_dynamic-update-slice_fusion.4
  7.5 1.9 bitcast_dynamic-update-slice_fusion.3
  9.4 1.9 bitcast_dynamic-update-slice_fusion.2
  11.3 2.0 bitcast_dynamic-update-slice_fusion.1
  13.3 1.9 bitcast_dynamic-update-slice_fusion
  16.5 2.5 collective-permute-start.16
  19.0 1.6 collective-permute-start.17
  21.3 1.6 collective-permute-start.2
  23.0 6.4 %copy.47 = bf16[256,8192]{1,0:T(8,128)(2,1)} copy(bf16[256,8192]{0,1:T(8,128)(2,1)} %bitcast.164) | data formatting | bytes 8388608 | tf_op jit(solution)/shard_map/dot_general | solution.py:169
  29.5 3.6 %convolution_bitcast_fusion = f32[2,2,32,128]{3,2,0,1:T(8,128)S(1)} fusion(bf16[2,128,8192,1]{2,1,0,3:T(8,128)(2,1)} %bitcast.162, bf16[2,32,8192]{2,1,0:T(8,128)(2,1)S(1)} %copy-done.7), kind=kOutput, calls=%fused_computation.58 | convolution fusion | flops 268435456 | bytes 5308416 | tf_op jit(solution)/shard_map/dot_general | solution.py:169
  33.1 1.6 collective-permute-start.19
  35.0 11.5 %collective-permute-done.19 = bf16[512,384]{1,0:T(8,128)(2,1)} collective-permute-done((bf16[512,384]{1,0:T(8,128)(2,1)S(1)}, bf16[512,384]{1,0:T(8,128)(2,1)}, u32[]{:S(2)}, u32[]{:S(2)}) %collective-permute-start.19) | collective-permute-done | bytes 393248 | tf_op jit(solution)/shard_map/ppermute | solution.py:75
  47.3 1.5 collective-permute-start.20
  48.8 10.4 %collective-permute-done.21 = bf16[512,384]{1,0:T(8,128)(2,1)} collective-permute-done((bf16[512,384]{1,0:T(8,128)(2,1)}, bf16[512,384]{1,0:T(8,128)(2,1)}, u32[]{:S(2)}, u32[]{:S(2)}) %collective-permute-start.21) | collective-permute-done | bytes 393248 | tf_op jit(solution)/shard_map/ppermute | solution.py:75
  59.7 2.4 constant_dynamic-slice_fusion.2
  62.1 1.6 collective-permute-start.1
  63.8 1.8 multiply_cosine_fusion
  65.7 0.9 slice.305
  66.6 0.9 slice.307
  67.5 1.6 collective-permute-start.9
  69.1 10.6 %collective-permute-done.1 = bf16[512,256]{1,0:T(8,128)(2,1)S(1)} collective-permute-done((bf16[512,256]{1,0:T(8,128)(2,1)}, bf16[512,256]{1,0:T(8,128)(2,1)S(1)}, u32[]{:S(2)}, u32[]{:S(2)}) %collective-permute-start.1) | collective-permute-done | bytes 262176 | tf_op jit(solution)/shard_map/ppermute | solution.py:75
  80.2 1.5 collective-permute-start.8
  83.0 2.4 slice_bitcast_fusion.1
  85.5 1.4 fusion.68
  88.8 1.7 fusion.76
  90.6 1.7 fusion.71
  94.6 1.4 convolution_add_fusion.13
  96.4 1.6 collective-permute-start.5
  98.5 1.6 collective-permute-start.24
  100.5 2.4 collective-permute-done.5
  102.9 1.5 collective-permute-start.11
  106.4 1.6 collective-permute-start.13
  108.4 3.7 %collective-permute-done.11 = bf16[512,256]{1,0:T(8,128)(2,1)S(1)} collective-permute-done((bf16[512,256]{1,0:T(8,128)(2,1)S(1)}, bf16[512,256]{1,0:T(8,128)(2,1)S(1)}, u32[]{:S(2)}, u32[]{:S(2)}) %collective-permute-start.11) | collective-permute-done | bytes 262176 | tf_op jit(solution)/shard_map/ppermute | solution.py:75
  112.1 1.5 collective-permute-start.12
  114.1 3.7 %collective-permute-done.10 = bf16[512,256]{1,0:T(8,128)(2,1)S(1)} collective-permute-done((bf16[512,256]{1,0:T(8,128)(2,1)S(1)}, bf16[512,256]{1,0:T(8,128)(2,1)S(1)}, u32[]{:S(2)}, u32[]{:S(2)}) %collective-permute-start.10) | collective-permute-done | bytes 262176 | tf_op jit(solution)/shard_map/ppermute | solution.py:75
  117.7 1.5 collective-permute-start.7
  119.7 3.6 %collective-permute-done.13 = bf16[512,256]{1,0:T(8,128)(2,1)S(1)} collective-permute-done((bf16[512,256]{1,0:T(8,128)(2,1)S(1)}, bf16[512,256]{1,0:T(8,128)(2,1)S(1)}, u32[]{:S(2)}, u32[]{:S(2)}) %collective-permute-start.13) | collective-permute-done | bytes 262176 | tf_op jit(solution)/shard_map/ppermute | solution.py:75
  123.4 1.5 collective-permute-start.26
  125.3 3.7 %collective-permute-done.12 = bf16[512,256]{1,0:T(8,128)(2,1)S(1)} collective-permute-done((bf16[512,256]{1,0:T(8,128)(2,1)S(1)}, bf16[512,256]{1,0:T(8,128)(2,1)S(1)}, u32[]{:S(2)}, u32[]{:S(2)}) %collective-permute-start.12) | collective-permute-done | bytes 262176 | tf_op jit(solution)/shard_map/ppermute | solution.py:75
  129.0 1.5 collective-permute-start.25
  132.7 6.3 %collective-permute-done.14 = bf16[512,256]{1,0:T(8,128)(2,1)S(1)} collective-permute-done((bf16[512,256]{1,0:T(8,128)(2,1)S(1)}, bf16[512,256]{1,0:T(8,128)(2,1)S(1)}, u32[]{:S(2)}, u32[]{:S(2)}) %collective-permute-start.14) | collective-permute-done | bytes 262176 | tf_op jit(solution)/shard_map/ppermute | solution.py:75
  139.0 1.2 collective-permute-start.27
  142.7 1.3 collective-permute-start.29
  144.4 1.2 fusion.23
  150.1 1.4 copy-done.1
  151.4 1.1 slice.311
  152.7 24.3 %all_gather.3 = bf16[2048,128]{1,0:T(8,128)(2,1)} all-gather(bf16[128,128]{1,0:T(8,128)(2,1)S(1)} %pad_maximum_fusion.13), channel_id=1, replica_groups=mesh['groups'=2,'sample'=16] {'sample'}, dimensions={0}, use_global_device_ids=true | all-gather | bytes 557056 | tf_op jit(solution)/shard_map/all_gather | solution.py:173
  177.0 0.9 slice_add_fusion.2
  178.0 1.4 fusion.25
  179.7 2.1 slice_add_fusion
  181.9 0.9 slice_add_fusion.1
  182.9 1.2 slice-done.1
  186.5 2.7 %multiply_reduce_fusion = (f32[4,512]{1,0:T(4,128)S(1)}, f32[4,512,512]{1,2,0:T(8,128)}) fusion(bf16[4,512,128]{2,1,0:T(8,128)(2,1)S(1)} %bitcast.167, bf16[512,4,64]{2,0,1:T(8,128)(2,1)S(1)} %get-tuple-element.31, bf16[512,4,64]{2,0,1:T(8,128)(2,1)S(1)} %get-tuple-element.30), kind=kOutput, calls=%fused_computation.2 | convolution fusion | flops 271579136 | bytes 5251072 | tf_op jit(solution)/shard_map/krd,lkd->krl/dot_general | solution.py:198
  189.3 3.0 %fusion.1 = f32[4,512]{1,0:T(4,128)S(1)} fusion(f32[4,512,512]{1,2,0:T(8,128)} %get-tuple-element.69, f32[4,512]{1,0:T(4,128)S(1)} %get-tuple-element.68), kind=kLoop, calls=%fused_computation.4 | loop fusion | flops 3143680 | bytes 4210688 | tf_op jit(solution)/shard_map/reduce_sum | solution.py:207
  192.7 1.9 fusion.17
  195.8 3.5 %all-to-all-start = ((f32[16,2,128]{2,1,0:T(2,128)}), f32[16,2,128]{2,1,0:T(2,128)S(1)}, u32[]{:S(2)}, u32[]{:S(2)}) async-start(f32[16,2,128]{2,1,0:T(2,128)} %pad_maximum_fusion.14), calls=%async_computation | async-start | bytes 32768 | tf_op jit(solution)/shard_map/all_to_all | solution.py:209
  199.5 6.2 %all-to-all-done = f32[16,2,128]{2,1,0:T(2,128)S(1)} async-done(((f32[16,2,128]{2,1,0:T(2,128)}), f32[16,2,128]{2,1,0:T(2,128)S(1)}, u32[]{:S(2)}, u32[]{:S(2)}) %all-to-all-start) | async-done | bytes 16416 | tf_op jit(solution)/shard_map/all_to_all | solution.py:209
  205.7 3.6 %all-to-all-start.1 = ((bf16[16,128,128]{2,1,0:T(8,128)(2,1)}), bf16[16,128,128]{2,1,0:T(8,128)(2,1)S(1)}, u32[]{:S(2)}, u32[]{:S(2)}) async-start(bf16[16,128,128]{2,1,0:T(8,128)(2,1)} %bitcast.32), calls=%async_computation.1 | async-start | bytes 1048576 | tf_op jit(solution)/shard_map/all_to_all | solution.py:231
  209.6 14.1 %all-to-all-done.1 = bf16[16,128,128]{2,1,0:T(8,128)(2,1)S(1)} async-done(((bf16[16,128,128]{2,1,0:T(8,128)(2,1)}), bf16[16,128,128]{2,1,0:T(8,128)(2,1)S(1)}, u32[]{:S(2)}, u32[]{:S(2)}) %all-to-all-start.1) | async-done | bytes 524320 | tf_op jit(solution)/shard_map/all_to_all | solution.py:231
  224.3 3.0 %convolution_convert_fusion = bf16[64,8192]{1,0:T(8,128)(2,1)S(1)} fusion(bf16[256,8192]{1,0:T(8,128)(2,1)} %param.14, bf16[8,8,2,128]{3,2,1,0:T(2,128)(2,1)S(1)} %bitcast.172), kind=kOutput, calls=%fused_computation | convolution fusion | flops 268959744 | bytes 5275648 | tf_op jit(solution)/shard_map/dot_general | solution.py:246
  227.4 28.7 %all_to_all.15 = bf16[16,64,512]{2,1,0:T(8,128)(2,1)S(1)} all-to-all(bf16[16,64,512]{2,1,0:T(8,128)(2,1)S(1)} %bitcast.165), channel_id=1, replica_groups=mesh['groups'=2,'sample'=16] {'sample'}, dimensions={0} | all-to-all | bytes 2097152 | tf_op jit(solution)/shard_map/all_to_all | solution.py:248
  (155 shorter events, 30.8 us)
Async XLA Ops:
  9.4 6.3 %copy-start.12 = (bf16[512,512]{1,0:T(8,128)(2,1)S(1)}, bf16[512,512]{1,0:T(8,128)(2,1)}, u32[]{:S(2)}) copy-start(bf16[512,512]{1,0:T(8,128)(2,1)} %param.12) | copy-start | bytes 1572868
  11.3 9.3 %copy-start.11 = (bf16[512,512]{1,0:T(8,128)(2,1)S(1)}, bf16[512,512]{1,0:T(8,128)(2,1)}, u32[]{:S(2)}) copy-start(bf16[512,512]{1,0:T(8,128)(2,1)} %param.11) | copy-start | bytes 1572868
  15.2 67.1 %collective-permute-start = (bf16[8,512,512]{2,1,0:T(8,128)(2,1)}, bf16[8,512,512]{2,1,0:T(8,128)(2,1)}, u32[]{:S(2)}, u32[]{:S(2)}) collective-permute-start(bf16[8,512,512]{2,1,0:T(8,128)(2,1)} %bitcast_dynamic-update-slice_fusion), channel_id=1, source_target_pairs={{0,1},{1,0},{2,3},{3,2},{4,5},{5,4},{6,7},{7,6},{8,9},{9,8},{10,11... | collective-permute-start | bytes 12582920 | tf_op jit(solution)/shard_map/ppermute | solution.py:75
  16.5 45.6 %collective-permute-start.16 = (bf16[512,384]{1,0:T(8,128)(2,1)}, bf16[512,384]{1,0:T(8,128)(2,1)S(1)}, u32[]{:S(2)}, u32[]{:S(2)}) collective-permute-start(bf16[512,384]{1,0:T(8,128)(2,1)} %pad_maximum_fusion.11), channel_id=1, source_target_pairs={{0,2},{1,3},{2,0},{3,1},{4,6},{5,7},{6,4},{7,5},{8,10},{9,11},{10,... | collective-permute-start | bytes 1179656 | tf_op jit(solution)/shard_map/ppermute | solution.py:75
  19.0 14.1 %collective-permute-start.17 = (bf16[512,384]{1,0:T(8,128)(2,1)}, bf16[512,384]{1,0:T(8,128)(2,1)S(1)}, u32[]{:S(2)}, u32[]{:S(2)}) collective-permute-start(bf16[512,384]{1,0:T(8,128)(2,1)} %pad_maximum_fusion.11), channel_id=1, source_target_pairs={{0,4},{1,5},{2,6},{3,7},{4,8},{5,9},{6,10},{7,11},{8,12},{9,13},{1... | collective-permute-start | bytes 1179656 | tf_op jit(solution)/shard_map/ppermute | solution.py:75
  21.3 25.9 %collective-permute-start.2 = (bf16[512,256]{1,0:T(8,128)(2,1)}, bf16[512,256]{1,0:T(8,128)(2,1)}, u32[]{:S(2)}, u32[]{:S(2)}) collective-permute-start(bf16[512,256]{1,0:T(8,128)(2,1)} %broadcast_select_fusion), channel_id=1, source_target_pairs={{0,4},{1,5},{2,6},{3,7},{4,8},{5,9},{6,10},{7,11},{8,12},{9,13},{1... | collective-permute-start | bytes 786440 | tf_op jit(solution)/shard_map/ppermute | solution.py:75
  23.0 6.5 %copy-start.7 = (bf16[2,32,8192]{2,1,0:T(8,128)(2,1)S(1)}, bf16[2,32,8192]{2,1,0:T(8,128)(2,1)}, u32[]{:S(2)}) copy-start(bf16[2,32,8192]{2,1,0:T(8,128)(2,1)} %param.10) | copy-start | bytes 3145732
  29.5 5.2 %copy-start.13 = (s32[64]{0:T(128)S(1)}, s32[64]{0:T(128)}, u32[]{:S(2)}) copy-start(s32[64]{0:T(128)} %param.9) | copy-start | bytes 772
  33.1 13.4 %collective-permute-start.19 = (bf16[512,384]{1,0:T(8,128)(2,1)S(1)}, bf16[512,384]{1,0:T(8,128)(2,1)}, u32[]{:S(2)}, u32[]{:S(2)}) collective-permute-start(bf16[512,384]{1,0:T(8,128)(2,1)S(1)} %collective-permute-done.17), channel_id=1, source_target_pairs={{0,4},{1,5},{2,6},{3,7},{4,8},{5,9},{6,10},{7,11},{8,12},{9,13},{1... | collective-permute-start | bytes 1179656 | tf_op jit(solution)/shard_map/ppermute | solution.py:75
  46.5 12.6 %collective-permute-start.21 = (bf16[512,384]{1,0:T(8,128)(2,1)}, bf16[512,384]{1,0:T(8,128)(2,1)}, u32[]{:S(2)}, u32[]{:S(2)}) collective-permute-start(bf16[512,384]{1,0:T(8,128)(2,1)} %collective-permute-done.19), channel_id=1, source_target_pairs={{0,4},{1,5},{2,6},{3,7},{4,8},{5,9},{6,10},{7,11},{8,12},{9,13},{1... | collective-permute-start | bytes 1179656 | tf_op jit(solution)/shard_map/ppermute | solution.py:75
  46.6 17.1 %collective-permute-start.18 = (bf16[512,384]{1,0:T(8,128)(2,1)S(1)}, bf16[512,384]{1,0:T(8,128)(2,1)S(1)}, u32[]{:S(2)}, u32[]{:S(2)}) collective-permute-start(bf16[512,384]{1,0:T(8,128)(2,1)S(1)} %collective-permute-done.17), channel_id=1, source_target_pairs={{0,2},{1,3},{2,0},{3,1},{4,6},{5,7},{6,4},{7,5},{8,10},{9,11},{10,... | collective-permute-start | bytes 1179656 | tf_op jit(solution)/shard_map/ppermute | solution.py:75
  47.3 20.3 %collective-permute-start.20 = (bf16[512,384]{1,0:T(8,128)(2,1)}, bf16[512,384]{1,0:T(8,128)(2,1)S(1)}, u32[]{:S(2)}, u32[]{:S(2)}) collective-permute-start(bf16[512,384]{1,0:T(8,128)(2,1)} %collective-permute-done.19), channel_id=1, source_target_pairs={{0,2},{1,3},{2,0},{3,1},{4,6},{5,7},{6,4},{7,5},{8,10},{9,11},{10,... | collective-permute-start | bytes 1179656 | tf_op jit(solution)/shard_map/ppermute | solution.py:75
  59.2 21.0 %collective-permute-start.22 = (bf16[512,384]{1,0:T(8,128)(2,1)}, bf16[512,384]{1,0:T(8,128)(2,1)S(1)}, u32[]{:S(2)}, u32[]{:S(2)}) collective-permute-start(bf16[512,384]{1,0:T(8,128)(2,1)} %collective-permute-done.21), channel_id=1, source_target_pairs={{0,2},{1,3},{2,0},{3,1},{4,6},{5,7},{6,4},{7,5},{8,10},{9,11},{10,... | collective-permute-start | bytes 1179656 | tf_op jit(solution)/shard_map/ppermute | solution.py:75
  62.1 17.5 %collective-permute-start.1 = (bf16[512,256]{1,0:T(8,128)(2,1)}, bf16[512,256]{1,0:T(8,128)(2,1)S(1)}, u32[]{:S(2)}, u32[]{:S(2)}) collective-permute-start(bf16[512,256]{1,0:T(8,128)(2,1)} %broadcast_select_fusion), channel_id=1, source_target_pairs={{0,2},{1,3},{2,0},{3,1},{4,6},{5,7},{6,4},{7,5},{8,10},{9,11},{10,... | collective-permute-start | bytes 786440 | tf_op jit(solution)/shard_map/ppermute | solution.py:75
  63.7 18.0 %collective-permute-start.4 = (bf16[512,256]{1,0:T(8,128)(2,1)}, bf16[512,256]{1,0:T(8,128)(2,1)S(1)}, u32[]{:S(2)}, u32[]{:S(2)}) collective-permute-start(bf16[512,256]{1,0:T(8,128)(2,1)} %collective-permute-done.2), channel_id=1, source_target_pairs={{0,4},{1,5},{2,6},{3,7},{4,8},{5,9},{6,10},{7,11},{8,12},{9,13},{1... | collective-permute-start | bytes 786440 | tf_op jit(solution)/shard_map/ppermute | solution.py:75
  67.5 38.9 %collective-permute-start.9 = (bf16[512,256]{1,0:T(8,128)(2,1)}, bf16[512,256]{1,0:T(8,128)(2,1)S(1)}, u32[]{:S(2)}, u32[]{:S(2)}) collective-permute-start(bf16[512,256]{1,0:T(8,128)(2,1)} %collective-permute-done.2), channel_id=1, source_target_pairs={{0,16},{1,17},{2,18},{3,19},{4,20},{5,21},{6,22},{7,23},{8,24},{9,... | collective-permute-start | bytes 786440 | tf_op jit(solution)/shard_map/ppermute | solution.py:75
  79.7 16.8 %collective-permute-start.3 = (bf16[512,256]{1,0:T(8,128)(2,1)}, bf16[512,256]{1,0:T(8,128)(2,1)S(1)}, u32[]{:S(2)}, u32[]{:S(2)}) collective-permute-start(bf16[512,256]{1,0:T(8,128)(2,1)} %collective-permute-done.2), channel_id=1, source_target_pairs={{0,2},{1,3},{2,0},{3,1},{4,6},{5,7},{6,4},{7,5},{8,10},{9,11},{10,... | collective-permute-start | bytes 786440 | tf_op jit(solution)/shard_map/ppermute | solution.py:75
  80.2 25.1 %collective-permute-start.8 = (bf16[512,256]{1,0:T(8,128)(2,1)S(1)}, bf16[512,256]{1,0:T(8,128)(2,1)S(1)}, u32[]{:S(2)}, u32[]{:S(2)}) collective-permute-start(bf16[512,256]{1,0:T(8,128)(2,1)S(1)} %collective-permute-done.1), channel_id=1, source_target_pairs={{0,16},{1,17},{2,18},{3,19},{4,20},{5,21},{6,22},{7,23},{8,24},{9,... | collective-permute-start | bytes 786440 | tf_op jit(solution)/shard_map/ppermute | solution.py:75
  81.7 61.0 %collective-permute-start.23 = (bf16[512,128]{1,0:T(8,128)(2,1)S(1)}, bf16[512,128]{1,0:T(8,128)(2,1)S(1)}, u32[]{:S(2)}, u32[]{:S(2)}) collective-permute-start(bf16[512,128]{1,0:T(8,128)(2,1)S(1)} %slice.302), channel_id=1, source_target_pairs={{0,16},{1,17},{2,18},{3,19},{4,20},{5,21},{6,22},{7,23},{8,24},{9,... | collective-permute-start | bytes 393224 | tf_op jit(solution)/shard_map/ppermute | solution.py:75
  82.3 16.2 %collective-permute-start.6 = (bf16[512,256]{1,0:T(8,128)(2,1)S(1)}, bf16[512,256]{1,0:T(8,128)(2,1)S(1)}, u32[]{:S(2)}, u32[]{:S(2)}) collective-permute-start(bf16[512,256]{1,0:T(8,128)(2,1)S(1)} %collective-permute-done.4), channel_id=1, source_target_pairs={{0,4},{1,5},{2,6},{3,7},{4,8},{5,9},{6,10},{7,11},{8,12},{9,13},{1... | collective-permute-start | bytes 786440 | tf_op jit(solution)/shard_map/ppermute | solution.py:75
  96.4 6.4 %collective-permute-start.5 = (bf16[512,256]{1,0:T(8,128)(2,1)S(1)}, bf16[512,256]{1,0:T(8,128)(2,1)S(1)}, u32[]{:S(2)}, u32[]{:S(2)}) collective-permute-start(bf16[512,256]{1,0:T(8,128)(2,1)S(1)} %collective-permute-done.4), channel_id=1, source_target_pairs={{0,2},{1,3},{2,0},{3,1},{4,6},{5,7},{6,4},{7,5},{8,10},{9,11},{10,... | collective-permute-start | bytes 786440 | tf_op jit(solution)/shard_map/ppermute | solution.py:75
  98.5 49.9 %collective-permute-start.24 = (bf16[512,128]{1,0:T(8,128)(2,1)S(1)}, bf16[512,128]{1,0:T(8,128)(2,1)S(1)}, u32[]{:S(2)}, u32[]{:S(2)}) collective-permute-start(bf16[512,128]{1,0:T(8,128)(2,1)S(1)} %slice.303), channel_id=1, source_target_pairs={{0,16},{1,17},{2,18},{3,19},{4,20},{5,21},{6,22},{7,23},{8,24},{9,... | collective-permute-start | bytes 393224 | tf_op jit(solution)/shard_map/ppermute | solution.py:75
  102.9 9.2 %collective-permute-start.11 = (bf16[512,256]{1,0:T(8,128)(2,1)S(1)}, bf16[512,256]{1,0:T(8,128)(2,1)S(1)}, u32[]{:S(2)}, u32[]{:S(2)}) collective-permute-start(bf16[512,256]{1,0:T(8,128)(2,1)S(1)} %collective-permute-done.4), channel_id=1, source_target_pairs={{0,16},{1,17},{2,18},{3,19},{4,20},{5,21},{6,22},{7,23},{8,24},{9,... | collective-permute-start | bytes 786440 | tf_op jit(solution)/shard_map/ppermute | solution.py:75
  105.3 12.4 %collective-permute-start.10 = (bf16[512,256]{1,0:T(8,128)(2,1)S(1)}, bf16[512,256]{1,0:T(8,128)(2,1)S(1)}, u32[]{:S(2)}, u32[]{:S(2)}) collective-permute-start(bf16[512,256]{1,0:T(8,128)(2,1)S(1)} %collective-permute-done.3), channel_id=1, source_target_pairs={{0,16},{1,17},{2,18},{3,19},{4,20},{5,21},{6,22},{7,23},{8,24},{9,... | collective-permute-start | bytes 786440 | tf_op jit(solution)/shard_map/ppermute | solution.py:75
  106.4 17.0 %collective-permute-start.13 = (bf16[512,256]{1,0:T(8,128)(2,1)S(1)}, bf16[512,256]{1,0:T(8,128)(2,1)S(1)}, u32[]{:S(2)}, u32[]{:S(2)}) collective-permute-start(bf16[512,256]{1,0:T(8,128)(2,1)S(1)} %collective-permute-done.6), channel_id=1, source_target_pairs={{0,16},{1,17},{2,18},{3,19},{4,20},{5,21},{6,22},{7,23},{8,24},{9,... | collective-permute-start | bytes 786440 | tf_op jit(solution)/shard_map/ppermute | solution.py:75
  112.1 16.9 %collective-permute-start.12 = (bf16[512,256]{1,0:T(8,128)(2,1)S(1)}, bf16[512,256]{1,0:T(8,128)(2,1)S(1)}, u32[]{:S(2)}, u32[]{:S(2)}) collective-permute-start(bf16[512,256]{1,0:T(8,128)(2,1)S(1)} %collective-permute-done.5), channel_id=1, source_target_pairs={{0,16},{1,17},{2,18},{3,19},{4,20},{5,21},{6,22},{7,23},{8,24},{9,... | collective-permute-start | bytes 786440 | tf_op jit(solution)/shard_map/ppermute | solution.py:75
  117.7 12.7 %collective-permute-start.7 = (bf16[512,256]{1,0:T(8,128)(2,1)S(1)}, bf16[512,256]{1,0:T(8,128)(2,1)S(1)}, u32[]{:S(2)}, u32[]{:S(2)}) collective-permute-start(bf16[512,256]{1,0:T(8,128)(2,1)S(1)} %collective-permute-done.6), channel_id=1, source_target_pairs={{0,2},{1,3},{2,0},{3,1},{4,6},{5,7},{6,4},{7,5},{8,10},{9,11},{10,... | collective-permute-start | bytes 786440 | tf_op jit(solution)/shard_map/ppermute | solution.py:75
  123.4 18.0 %collective-permute-start.26 = (bf16[512,128]{1,0:T(8,128)(2,1)S(1)}, bf16[512,128]{1,0:T(8,128)(2,1)S(1)}, u32[]{:S(2)}, u32[]{:S(2)}) collective-permute-start(bf16[512,128]{1,0:T(8,128)(2,1)S(1)} %slice.305), channel_id=1, source_target_pairs={{0,16},{1,17},{2,18},{3,19},{4,20},{5,21},{6,22},{7,23},{8,24},{9,... | collective-permute-start | bytes 393224 | tf_op jit(solution)/shard_map/ppermute | solution.py:75
  129.0 16.6 %collective-permute-start.25 = (bf16[512,128]{1,0:T(8,128)(2,1)S(1)}, bf16[512,128]{1,0:T(8,128)(2,1)S(1)}, u32[]{:S(2)}, u32[]{:S(2)}) collective-permute-start(bf16[512,128]{1,0:T(8,128)(2,1)S(1)} %slice.304), channel_id=1, source_target_pairs={{0,16},{1,17},{2,18},{3,19},{4,20},{5,21},{6,22},{7,23},{8,24},{9,... | collective-permute-start | bytes 393224 | tf_op jit(solution)/shard_map/ppermute | solution.py:75
  130.5 8.6 %collective-permute-start.14 = (bf16[512,256]{1,0:T(8,128)(2,1)S(1)}, bf16[512,256]{1,0:T(8,128)(2,1)S(1)}, u32[]{:S(2)}, u32[]{:S(2)}) collective-permute-start(bf16[512,256]{1,0:T(8,128)(2,1)S(1)} %collective-permute-done.7), channel_id=1, source_target_pairs={{0,16},{1,17},{2,18},{3,19},{4,20},{5,21},{6,22},{7,23},{8,24},{9,... | collective-permute-start | bytes 786440 | tf_op jit(solution)/shard_map/ppermute | solution.py:75
  139.0 7.1 %collective-permute-start.27 = (bf16[512,128]{1,0:T(8,128)(2,1)S(1)}, bf16[512,128]{1,0:T(8,128)(2,1)S(1)}, u32[]{:S(2)}, u32[]{:S(2)}) collective-permute-start(bf16[512,128]{1,0:T(8,128)(2,1)S(1)} %slice.306), channel_id=1, source_target_pairs={{0,16},{1,17},{2,18},{3,19},{4,20},{5,21},{6,22},{7,23},{8,24},{9,... | collective-permute-start | bytes 393224 | tf_op jit(solution)/shard_map/ppermute | solution.py:75
  141.4 5.2 %collective-permute-start.28 = (bf16[512,128]{1,0:T(8,128)(2,1)S(1)}, bf16[512,128]{1,0:T(8,128)(2,1)S(1)}, u32[]{:S(2)}, u32[]{:S(2)}) collective-permute-start(bf16[512,128]{1,0:T(8,128)(2,1)S(1)} %slice.307), channel_id=1, source_target_pairs={{0,16},{1,17},{2,18},{3,19},{4,20},{5,21},{6,22},{7,23},{8,24},{9,... | collective-permute-start | bytes 393224 | tf_op jit(solution)/shard_map/ppermute | solution.py:75
  142.7 5.1 %collective-permute-start.29 = (bf16[512,128]{1,0:T(8,128)(2,1)S(1)}, bf16[512,128]{1,0:T(8,128)(2,1)S(1)}, u32[]{:S(2)}, u32[]{:S(2)}) collective-permute-start(bf16[512,128]{1,0:T(8,128)(2,1)S(1)} %slice.308), channel_id=1, source_target_pairs={{0,16},{1,17},{2,18},{3,19},{4,20},{5,21},{6,22},{7,23},{8,24},{9,... | collective-permute-start | bytes 393224 | tf_op jit(solution)/shard_map/ppermute | solution.py:75
  145.6 31.4 %collective-permute-start.15 = (f32[576,512]{1,0:T(8,128)}, f32[576,512]{1,0:T(8,128)}, u32[]{:S(2)}, u32[]{:S(2)}) collective-permute-start(f32[576,512]{1,0:T(8,128)} %fusion.23), channel_id=1, source_target_pairs={{0,1},{1,0},{2,3},{3,2},{4,5},{5,4},{6,7},{7,6},{8,9},{9,8},{10,11... | collective-permute-start | bytes 3538952 | tf_op jit(solution)/shard_map/ppermute | solution.py:75
  148.4 0.8 copy-start.4
  149.2 0.9 copy-start.2
  150.1 1.4 copy-start.1
  152.5 27.2 %collective-permute-start.30 = (f32[576,512]{1,0:T(8,128)}, f32[576,512]{1,0:T(8,128)}, u32[]{:S(2)}, u32[]{:S(2)}) collective-permute-start(f32[576,512]{1,0:T(8,128)} %slice.311), channel_id=1, source_target_pairs={{0,1},{1,0},{2,3},{3,2},{4,5},{5,4},{6,7},{7,6},{8,9},{9,8},{10,11... | collective-permute-start | bytes 3538952 | tf_op jit(solution)/shard_map/ppermute | solution.py:75
  179.6 2.2 copy-start.6
  179.7 2.2 copy-start.3
  179.7 2.3 copy-start.5
  182.9 1.2 slice-start.1
  184.4 1.0 copy-start.9
  184.5 1.0 copy-start.10
  185.5 1.0 copy-start.8
  189.3 3.4 %copy-start = (f32[4,512,512]{1,2,0:T(8,128)S(1)}, f32[4,512,512]{1,2,0:T(8,128)}, u32[]{:S(2)}) copy-start(f32[4,512,512]{1,2,0:T(8,128)} %get-tuple-element.69) | copy-start | bytes 12582916
  192.7 2.0 slice-start
  195.8 10.0 %all-to-all-start = ((f32[16,2,128]{2,1,0:T(2,128)}), f32[16,2,128]{2,1,0:T(2,128)S(1)}, u32[]{:S(2)}, u32[]{:S(2)}) async-start(f32[16,2,128]{2,1,0:T(2,128)} %pad_maximum_fusion.14), calls=%async_computation | async-start | bytes 32768 | tf_op jit(solution)/shard_map/all_to_all | solution.py:209
  205.7 18.0 %all-to-all-start.1 = ((bf16[16,128,128]{2,1,0:T(8,128)(2,1)}), bf16[16,128,128]{2,1,0:T(8,128)(2,1)S(1)}, u32[]{:S(2)}, u32[]{:S(2)}) async-start(bf16[16,128,128]{2,1,0:T(8,128)(2,1)} %bitcast.32), calls=%async_computation.1 | async-start | bytes 1048576 | tf_op jit(solution)/shard_map/all_to_all | solution.py:231

commit v2 on v1

v2 whole, which is shorter than its diff:
```python
import jax
import jax.numpy as jnp
from jax import lax
from jax.sharding import PartitionSpec as P

D = 8192
HEAD_DIM = 128
KV_HEADS = 4
GQA = 8
PAGE = 128
PROMPT_PAGES = 64
CORES = 2

rope_base = 1000000.0


def rope_tables(position):
    half_dim = HEAD_DIM // 2
    frequency = rope_base ** (-jnp.arange(half_dim, dtype=jnp.float32) * 2.0 / HEAD_DIM)
    angles = position.astype(jnp.float32)[..., None] * frequency
    return jnp.cos(angles), jnp.sin(angles)


def turn(vector, tables):
    cosine, sine_part = tables
    half_dim = HEAD_DIM // 2
    first_half = vector[..., :half_dim]
    second_half = vector[..., half_dim:]
    return jnp.concatenate(
        [
            first_half * cosine - second_half * sine_part,
            second_half * cosine + first_half * sine_part,
        ],
        axis=-1,
    )


def finish_heads(prefix_top, prefix_total, prefix_sum, queries, new_keys, new_values):
    score_scale = queries.shape[-1] ** (-0.5)
    query_wide = queries.astype(jnp.float32)
    key_wide = new_keys.astype(jnp.float32)
    value_wide = new_values.astype(jnp.float32)
    own_score = jnp.sum(query_wide * key_wide, axis=-1) * score_scale
    back_score = jnp.sum(query_wide[1] * key_wide[0], axis=-1) * score_scale
    first_high = jnp.maximum(prefix_top[0], own_score[0])
    first_old = jnp.exp(prefix_top[0] - first_high)
    first_own = jnp.exp(own_score[0] - first_high)
    first_out = (first_old[..., None] * prefix_sum[0] + first_own[..., None] * value_wide[0]) / (
        first_old * prefix_total[0] + first_own
    )[..., None]
    second_high = jnp.maximum(jnp.maximum(prefix_top[1], own_score[1]), back_score)
    second_old = jnp.exp(prefix_top[1] - second_high)
    second_back = jnp.exp(back_score - second_high)
    second_own = jnp.exp(own_score[1] - second_high)
    second_num = (
        second_old[..., None] * prefix_sum[1]
        + second_back[..., None] * value_wide[0]
        + second_own[..., None] * value_wide[1]
    )
    second_out = second_num / (second_old * prefix_total[1] + second_back + second_own)[..., None]
    return jnp.stack([first_out, second_out]).astype(jnp.bfloat16)


def on_device(
    prompt_states,
    page_table,
    step_states,
    sample_order,
    key_weight,
    value_weight,
    query_weight,
    out_weight,
):
    devices = lax.axis_size("sample")
    groups = lax.axis_size("groups")
    own_index = lax.axis_index("sample")
    core = own_index % CORES
    chips = devices // CORES
    first_core = core == 0
    first_plane = lax.axis_index("groups") % 2 == 0
    same_core = [[c + CORES * i for i in range(chips)] for c in range(CORES)]
    core_pairs = [(s, s ^ 1) for s in range(devices)]
    plane_pairs = [(g, g ^ 1) for g in range(groups)]

    def in_chip(value):
        return lax.ppermute(value, "sample", core_pairs)

    def across(value):
        return lax.ppermute(value, "groups", plane_pairs)

    def gather(value):
        return lax.all_gather(value, "sample", axis=0, tiled=True, axis_index_groups=same_core)

    def exchange(value):
        return lax.all_to_all(
            value, "sample", split_axis=0, concat_axis=0, tiled=True, axis_index_groups=same_core
        )

    row_count = prompt_states.shape[0]
    pages_here = row_count // PAGE
    heads_here = query_weight.shape[1] // HEAD_DIM
    total_pages = page_table.shape[0]
    prompts = total_pages // PROMPT_PAGES
    samples = sample_order.shape[0]
    group_size = samples // prompts
    score_scale = HEAD_DIM ** (-0.5)
    own_kv = own_index * heads_here // GQA
    wide_states = step_states.reshape(2 * samples, D)
    rows = heads_here * 2 * samples

    def weight_parts(weight):
        quarter = weight.shape[1] // 4
        low, high = weight[:, :quarter], weight[:, quarter : 2 * quarter]
        mine = gather(jnp.where(first_plane, low, high))
        other = across(mine)
        both = gather(weight[:, 2 * quarter :])
        return mine, other, both

    def project(left, parts):
        mine, other, both = (
            jnp.dot(left, part, preferred_element_type=jnp.float32) for part in parts
        )
        low = jnp.where(first_plane, mine, other)
        high = jnp.where(first_plane, other, mine)
        return jnp.concatenate([low, high, both], axis=1)

    key_parts = weight_parts(key_weight)
    value_parts = weight_parts(value_weight)

    def halves(source):
        parts = jnp.split(source, devices, axis=1)
        kept = [jnp.where(first_core, *parts[i : i + 2]) for i in range(0, devices, 2)]
        sent = [jnp.where(first_core, *parts[i : i + 2][::-1]) for i in range(0, devices, 2)]
        return kept, sent

    kept, sent = (jnp.concatenate(part, axis=1) for part in halves(prompt_states))
    kept_step = jnp.concatenate(halves(wide_states)[0], axis=1)
    left = jnp.concatenate([kept, in_chip(sent), kept_step])

    step_place = PROMPT_PAGES * PAGE + jnp.arange(2, dtype=jnp.int32)
    step_tables = tuple(t[:, None, :] for t in rope_tables(step_place))
    queries = jnp.dot(wide_states, query_weight, preferred_element_type=jnp.float32)
    queries = queries.reshape(2, samples, heads_here, HEAD_DIM).transpose(2, 0, 1, 3)
    queries = turn(queries, step_tables).astype(jnp.bfloat16)
    flat_queries = queries.reshape(1, rows, HEAD_DIM)
    core_queries = exchange(jnp.broadcast_to(flat_queries, (chips, rows, HEAD_DIM)))
    core_queries = core_queries.reshape(KV_HEADS, chips // KV_HEADS * rows, HEAD_DIM)
    owned = core_queries.shape[1]
    all_queries = jnp.concatenate([core_queries, in_chip(core_queries)], axis=1)

    own_pages = jnp.concatenate(
        [
            holder * pages_here + jnp.arange(pages_here, dtype=jnp.int32)
            for holder in (own_index, own_index ^ 1)
        ]
    )
    slots = jnp.sum(
        jnp.where(
            page_table[None, :] == own_pages[:, None],
            jnp.arange(total_pages, dtype=jnp.int32)[None, :],
            0,
        ),
        axis=1,
    )
    positions = (slots % PROMPT_PAGES * PAGE)[:, None] + jnp.arange(PAGE, dtype=jnp.int32)[None, :]
    chip_rows = 2 * row_count
    cosine, sine_part = rope_tables(positions.reshape(chip_rows))

    keys = project(left, key_parts)
    back = in_chip(keys)
    keys = keys + jnp.concatenate([back[row_count:chip_rows], back[:row_count], back[chip_rows:]])
    keys = keys.reshape(-1, KV_HEADS, HEAD_DIM)
    prefix_keys = turn(keys[:chip_rows], (cosine[:, None], sine_part[:, None])).astype(jnp.bfloat16)
    key_step = lax.dynamic_slice_in_dim(keys[chip_rows:], own_kv, 1, 1)
    new_keys = turn(key_step.reshape(2, samples, HEAD_DIM), step_tables).astype(jnp.bfloat16)

    scores = (
        jnp.einsum("krd,lkd->krl", all_queries, prefix_keys, preferred_element_type=jnp.float32)
        * score_scale
    )
    if prompts > 1:
        token_prompt = jnp.repeat(slots // PROMPT_PAGES, PAGE)
        row_prompt = jnp.tile(sample_order // group_size, scores.shape[1] // samples)
        scores = jnp.where(row_prompt[:, None] == token_prompt[None, :], scores, -1e30)
    top = jnp.max(scores, axis=-1)
    weights = jnp.exp(scores - top[..., None])
    total = jnp.sum(weights, axis=-1)
    stats = jnp.stack(
        [top[:, :owned].reshape(chips, rows), total[:, :owned].reshape(chips, rows)], axis=1
    )
    stats = exchange(stats)
    tops, totals = stats[:, 0], stats[:, 1]
    prefix_top = jnp.max(tops, axis=0)
    factors = jnp.exp(tops - prefix_top[None])
    prefix_total = jnp.sum(factors * totals, axis=0)

    values = project(left, value_parts)
    step_values = values[chip_rows:]
    step_values = step_values + in_chip(step_values)
    new_values = lax.dynamic_slice_in_dim(step_values.reshape(-1, KV_HEADS, HEAD_DIM), own_kv, 1, 1)
    new_values = new_values.reshape(2, samples, HEAD_DIM).astype(jnp.bfloat16)
    values = values[:chip_rows].astype(jnp.bfloat16).reshape(chip_rows, KV_HEADS, HEAD_DIM)
    partial = jnp.einsum(
        "krl,lkd->krd", weights.astype(jnp.bfloat16), values, preferred_element_type=jnp.float32
    )
    partial = partial[:, :owned] + in_chip(partial[:, owned:].astype(jnp.bfloat16)).astype(
        jnp.float32
    )
    partial = exchange(partial.astype(jnp.bfloat16).reshape(chips, rows, HEAD_DIM))
    prefix_sum = jnp.sum(partial.astype(jnp.float32) * factors[..., None], axis=0)

    by_head = (heads_here, 2, samples)
    head_out = finish_heads(
        prefix_top.reshape(by_head).swapaxes(0, 1),
        prefix_total.reshape(by_head).swapaxes(0, 1),
        prefix_sum.reshape(by_head + (HEAD_DIM,)).swapaxes(0, 1),
        queries.swapaxes(0, 1),
        new_keys[:, None],
        new_values[:, None],
    )
    flat_heads = head_out.transpose(0, 2, 1, 3).reshape(2 * samples, heads_here * HEAD_DIM)
    terms = jnp.dot(flat_heads, out_weight, preferred_element_type=jnp.float32).astype(jnp.bfloat16)
    kept, sent = (jnp.stack(part) for part in halves(terms))
    terms = kept.astype(jnp.float32) + in_chip(sent).astype(jnp.float32)
    terms = exchange(terms.astype(jnp.bfloat16))
    attn_out = jnp.sum(terms.astype(jnp.float32), axis=0).astype(jnp.bfloat16)
    return attn_out.reshape(2, samples, -1)


def solution(mesh):
    in_specs = (
        P(("groups", "sample"), None),
        P("groups"),
        P(None, "groups", None),
        P("groups"),
        P("sample", None),
        P("sample", None),
        P(None, "sample"),
        P("sample", None),
    )
    out_specs = P(None, "groups", "sample")
    return jax.shard_map(
        on_device, mesh=mesh, in_specs=in_specs, out_specs=out_specs, check_vma=False
    )
```

time: 258 us -> 276 us (1.070)
  waiting for transfers between devices: 77 us -> 126 us
  blocking collectives: 53 us -> 18.2 us
  other arithmetic: 17.1 us -> 40.7 us
  starting transfers between devices: 40.6 us -> 19.4 us
  local copies, waits for them, and re-layouts: 36 us -> 18.8 us
  between operations: 0.87 us -> 13.8 us
  matrix products: 32.3 us -> 38.7 us
    all_gather x0 -> x4, waiting for transfers between devices: none -> 107 us  [gather(): lax.all_gather(value, 'sample', axis=0, tiled=True, axis_index_groups=sam...]
    ppermute x31 -> x8, waiting for transfers between devices: 56.7 us -> 2.15 us  [the longest x6 2.14 us: in_chip(): return lax.ppermute(value, 'sample', core_pairs)]
    ppermute x31 -> x8, starting transfers between devices: 33.5 us -> 3.87 us  [the longest x2 2.94 us: across(): return lax.ppermute(value, 'groups', plane_pairs)]
    all_gather x1 -> x0, blocking collectives: 24.3 us -> none  [on_device(): lax.all_gather(queries.reshape(rows, HEAD_DIM), 'sample', axis=0, tiled=T...]
    unnamed x35 -> x24, local copies, waits for them, and re-layouts: 17 us -> 1.43 us
    unnamed x0 -> x33, other arithmetic: none -> 15.4 us
    all_to_all x1, blocking collectives: 28.7 us -> 18.2 us  [exchange(): lax.all_to_all(value, 'sample', split_axis=0, concat_axis=0, tiled=True,...]
    concatenate x6 -> x7, other arithmetic: 2.39 us -> 12.3 us  [the longest x1 7.35 us: on_device(): left = jnp.concatenate([kept, in_chip(sent), kept_step])]
  transfers between devices with their start and end apart: 33 -> 15, of which waited for: 12 -> 8; matrix products, arithmetic and copies ran while one was open for 19% -> 31% of each run, Pallas kernels for 0% -> 0%
where the time goes in v2:
time: 276 us; the launch traced here: 275 us
  waiting for transfers between devices  126 us (46%)
  other arithmetic  40.7 us (15%)
  matrix products  38.7 us (14%)
  starting transfers between devices  19.4 us (7%)
  local copies, waits for them, and re-layouts  18.8 us (7%)
  blocking collectives  18.2 us (7%)
  between operations  13.8 us (5%)
    all_gather x4, waiting for transfers between devices, gather(): lax.all_gather(value, 'sample', axis=0, tiled=True, axis_index_groups=sam...  107 us
    dot_general x6, matrix products, project(): jnp.dot(left, part, preferred_element_type=jnp.float32)  24.9 us
    all_to_all x1, blocking collectives, exchange(): lax.all_to_all(value, 'sample', split_axis=0, concat_axis=0, tiled=True,...  18.2 us
    all_to_all x3, waiting for transfers between devices, exchange(): lax.all_to_all(value, 'sample', split_axis=0, concat_axis=0, tiled=True,...  16.2 us
    all_to_all x3, starting transfers between devices, exchange(): lax.all_to_all(value, 'sample', split_axis=0, concat_axis=0, tiled=True,...  15.4 us
    unnamed x33, other arithmetic  15.4 us
    concatenate x1, other arithmetic, on_device(): left = jnp.concatenate([kept, in_chip(sent), kept_step])  7.35 us
    dot_general x1, local copies, waits for them, and re-layouts, on_device(): jnp.dot(wide_states, query_weight, preferred_element_type=jnp.float32)  6.51 us
  transfers between devices with their start and end apart: 15, of which 8 were waited for; matrix products, arithmetic and copies ran while one was open for 31% of the time, Pallas kernels for 0%

profile of v2, /device:TPU:0, one launch (start us, length us, event | category | flops | bytes accessed | tf_op | source)
XLA Modules:
  0.0 275.3 jit_solution(4501644148899700067)
XLA Ops:
  6.5 1.6 slice_select_fusion
  8.3 1.6 slice_select_fusion.1
  10.0 1.7 slice.131
  11.7 1.5 select_dynamic-update-slice_fusion.15
  13.2 1.6 select_dynamic-update-slice_fusion.14
  14.8 1.3 select_dynamic-update-slice_fusion.13
  16.2 1.4 select_dynamic-update-slice_fusion.12
  17.5 1.3 select_dynamic-update-slice_fusion.11
  18.9 1.4 select_dynamic-update-slice_fusion.10
  20.4 1.2 select_dynamic-update-slice_fusion.8
  21.6 1.1 select_dynamic-update-slice_fusion.6
  22.7 1.3 select_dynamic-update-slice_fusion.5
  24.0 1.0 select_dynamic-update-slice_fusion.4
  25.0 1.0 select_dynamic-update-slice_fusion.3
  26.0 0.9 select_dynamic-update-slice_fusion.2
  27.0 1.0 select_dynamic-update-slice_fusion.1
  27.9 1.0 select_dynamic-update-slice_fusion
  28.9 0.5 collective-permute-start.1
  29.3 6.5 %copy.40 = bf16[256,8192]{1,0:T(8,128)(2,1)} copy(bf16[256,8192]{0,1:T(8,128)(2,1)} %bitcast.138) | data formatting | bytes 8388608 | tf_op jit(solution)/shard_map/dot_general | solution.py:142
  36.0 3.7 %convolution_bitcast_fusion = f32[2,2,32,128]{3,2,0,1:T(8,128)S(1)} fusion(bf16[2,128,8192,1]{2,1,0,3:T(8,128)(2,1)} %bitcast.137, bf16[2,32,8192]{2,1,0:T(8,128)(2,1)S(1)} %copy-done.4), kind=kOutput, calls=%fused_computation.15 | convolution fusion | flops 268435456 | bytes 5308416 | tf_op jit(solution)/shard_map/dot_general | solution.py:142
  39.9 0.7 broadcast_in_dim.10
  40.7 6.7 %all-to-all-start = ((bf16[8,128,128]{2,1,0:T(8,128)(2,1)}), bf16[8,128,128]{2,1,0:T(8,128)(2,1)}, u32[]{:S(2)}, u32[]{:S(2)}) async-start(bf16[8,128,128]{2,1,0:T(8,128)(2,1)} %broadcast_in_dim.10), calls=%async_computation | async-start | bytes 524288 | tf_op jit(solution)/shard_map/all_to_all | solution.py:95
  47.5 0.7 slice.150
  48.3 0.2 select_reduce_fusion
  48.9 3.1 %multiply_cosine_fusion = (f32[1024,64]{1,0:T(8,128)}, f32[1024,64]{1,0:T(8,128)}) fusion(f32[64]{0:T(128)S(1)} %multiply_power_fusion, f32[1024]{0:T(1024)S(1)} %convert_bitcast_fusion.1), kind=kLoop, calls=%fused_computation.26 | loop fusion | flops 65536 | bytes 528640 | tf_op jit(solution)/shard_map/cos | solution.py:21
  52.0 5.6 %all-to-all-done = bf16[8,128,128]{2,1,0:T(8,128)(2,1)} async-done(((bf16[8,128,128]{2,1,0:T(8,128)(2,1)}), bf16[8,128,128]{2,1,0:T(8,128)(2,1)}, u32[]{:S(2)}, u32[]{:S(2)}) %all-to-all-start) | async-done | bytes 262176 | tf_op jit(solution)/shard_map/all_to_all | solution.py:95
  57.5 1.5 collective-permute-start.4
  59.0 35.9 %all-gather.5.cloned.1.call-done = bf16[4096,128]{1,0:T(8,128)(2,1)} async-done(((bf16[512,128]{1,0:T(8,128)(2,1)}), bf16[4096,128]{1,0:T(8,128)(2,1)}) %all-gather.5.cloned.1.call-update) | async-done | bytes 1048592 | tf_op jit(solution)/shard_map/all_gather | solution.py:92
  94.9 1.5 collective-permute-start.2
  96.4 7.3 %pad_maximum_fusion = bf16[1088,4096]{1,0:T(8,128)(2,1)} fusion(bf16[64,4096]{1,0:T(8,128)(2,1)S(1)} %constant_dynamic-update-slice_fusion, bf16[512,4096]{1,0:T(8,128)(2,1)} %collective-permute-done.1, bf16[512,4096]{1,0:T(8,128)(2,1)} %copy-done.3), kind=kLoop, calls=%fused_computation.1 | loop fusion | flops 26738688 | bytes 17825792 | tf_op jit(solution)/shard_map/concatenate | solution.py:138
  103.7 41.4 %all-gather.7.cloned.1.call-done = bf16[4096,256]{1,0:T(8,128)(2,1)} async-done(((bf16[512,256]{1,0:T(8,128)(2,1)}), bf16[4096,256]{1,0:T(8,128)(2,1)}) %all-gather.7.cloned.1.call-update) | async-done | bytes 2097168 | tf_op jit(solution)/shard_map/all_gather | solution.py:92
  145.1 6.8 %fusion.46 = f32[1088,256]{1,0:T(8,128)S(1)} fusion(bf16[1088,4096]{1,0:T(8,128)(2,1)} %pad_maximum_fusion, bf16[4096,256]{1,0:T(8,128)(2,1)} %all-gather.7.cloned.1.call-done), kind=kOutput, calls=%fused_computation.156 | convolution fusion | flops 2281701376 | bytes 12124160 | tf_op jit(solution)/shard_map/dot_general | solution.py:121
  151.9 2.5 fusion.45
  154.4 2.5 broadcast_select_fusion.3
  156.9 1.6 pad_maximum_fusion.1
  158.5 3.8 %fusion.47 = f32[1088,128]{1,0:T(8,128)S(1)} fusion(bf16[1088,4096]{1,0:T(8,128)(2,1)S(1)} %copy-done, bf16[4096,128]{1,0:T(8,128)(2,1)} %collective-permute-done.4), kind=kOutput, calls=%fused_computation.157 | convolution fusion | flops 1140850688 | bytes 10518528 | tf_op jit(solution)/shard_map/dot_general | solution.py:121
  162.4 2.5 broadcast_select_fusion.1
  164.9 30.0 %all-gather.11.cloned.1.call-done = bf16[4096,256]{1,0:T(8,128)(2,1)} async-done(((bf16[512,256]{1,0:T(8,128)(2,1)}), bf16[4096,256]{1,0:T(8,128)(2,1)}) %all-gather.11.cloned.1.call-update) | async-done | bytes 2097168 | tf_op jit(solution)/shard_map/all_gather | solution.py:92
  194.9 6.9 %fusion.48 = f32[1088,256]{1,0:T(8,128)S(1)} fusion(bf16[1088,4096]{1,0:T(8,128)(2,1)} %pad_maximum_fusion, bf16[4096,256]{1,0:T(8,128)(2,1)} %all-gather.11.cloned.1.call-done), kind=kOutput, calls=%fused_computation.158 | convolution fusion | flops 2281701376 | bytes 12124160 | tf_op jit(solution)/shard_map/dot_general | solution.py:121
  201.9 1.1 pad_maximum_fusion.2
  203.0 0.2 collective-permute-done.6
  203.3 1.7 fusion.39
  205.0 0.9 slice.170
  206.0 0.4 maximum_add_fusion
  206.4 1.5 slice.171
  208.1 1.9 slice.136
  210.0 1.2 fusion.40
  211.3 0.5 subtract_convert_fusion
  212.1 2.6 multiply_reduce_fusion
  214.7 1.9 fusion.1
  216.6 1.4 copy-done.2
  218.0 0.6 pad_maximum_fusion.6
  218.6 3.3 %all-to-all-start.1 = ((f32[8,2,128]{2,1,0:T(2,128)}), f32[8,2,128]{2,1,0:T(2,128)S(1)}, u32[]{:S(2)}, u32[]{:S(2)}) async-start(f32[8,2,128]{2,1,0:T(2,128)} %pad_maximum_fusion.6), calls=%async_computation.1 | async-start | bytes 16384 | tf_op jit(solution)/shard_map/all_to_all | solution.py:95
  221.9 4.4 %fusion.2 = f32[4,512,128]{2,1,0:T(8,128)S(1)} fusion(f32[4,512,1024]{2,1,0:T(8,128)} %copy-done.2, f32[4,512]{1,0:T(4,128)S(1)} %get-tuple-element.50, bf16[1088,512]{1,0:T(8,128)(2,1)S(1)} %copy-done.7), kind=kOutput, calls=%fused_computation.6 | convolution fusion | flops 543162368 | bytes 10493952 | tf_op jit(solution)/shard_map/krl,lkd->krd/dot_general | solution.py:203
  226.4 0.3 collective-permute-start.5
  226.9 1.5 all-to-all-done.1
  228.5 0.8 fusion.14
  229.3 5.3 %all-to-all-start.2 = ((bf16[8,128,128]{2,1,0:T(8,128)(2,1)}), bf16[8,128,128]{2,1,0:T(8,128)(2,1)S(1)}, u32[]{:S(2)}, u32[]{:S(2)}) async-start(bf16[8,128,128]{2,1,0:T(8,128)(2,1)} %bitcast.16), calls=%async_computation.2 | async-start | bytes 524288 | tf_op jit(solution)/shard_map/all_to_all | solution.py:95
  234.8 9.1 %all-to-all-done.2 = bf16[8,128,128]{2,1,0:T(8,128)(2,1)S(1)} async-done(((bf16[8,128,128]{2,1,0:T(8,128)(2,1)}), bf16[8,128,128]{2,1,0:T(8,128)(2,1)S(1)}, u32[]{:S(2)}, u32[]{:S(2)}) %all-to-all-start.2) | async-done | bytes 262176 | tf_op jit(solution)/shard_map/all_to_all | solution.py:95
  243.9 0.2 multiply_reduce_fusion.1
  244.3 3.0 %convolution_convert_fusion = bf16[64,8192]{1,0:T(8,128)(2,1)S(1)} fusion(bf16[256,8192]{1,0:T(8,128)(2,1)} %param.14, bf16[8,8,2,128]{3,2,1,0:T(2,128)(2,1)S(1)} %bitcast.151), kind=kOutput, calls=%fused_computation | convolution fusion | flops 268959744 | bytes 5275648 | tf_op jit(solution)/shard_map/dot_general | solution.py:222
  247.8 1.9 collective-permute-done.7
  249.8 18.2 %all_to_all.20 = bf16[8,64,512]{2,1,0:T(8,128)(2,1)S(1)} all-to-all(bf16[8,64,512]{2,1,0:T(8,128)(2,1)S(1)} %add_convert_fusion.1), channel_id=1, replica_groups={{0,2,4,6,8,10,12,14},{1,3,5,7,9,11,13,15},{16,18,20,22,24,26,28,30},{17..., dimensions={0} | all-to-all | bytes 1048576 | tf_op jit(solution)/shard_map/all_to_all | solution.py:95
  268.0 0.7 reduce_sum.72
  (109 shorter events, 2.9 us)
Async XLA Ops:
  6.5 51.0 %all-gather.9.cloned.1.call-start = ((), (), s32[]{:S(2)}) async-start(), calls=%async_computation.6 | async-start | bytes 1179648 | tf_op jit(solution)/shard_map/all_gather | solution.py:92
  8.2 86.7 %all-gather.5.cloned.1.call-start = ((), (), s32[]{:S(2)}) async-start(), calls=%async_computation.4 | async-start | bytes 1179648 | tf_op jit(solution)/shard_map/all_gather | solution.py:92
  9.9 135.2 %all-gather.7.cloned.1.call-start = ((), (), s32[]{:S(2)}) async-start(), calls=%async_computation.5 | async-start | bytes 2359296 | tf_op jit(solution)/shard_map/all_gather | solution.py:92
  11.7 8.6 %copy-start.1 = (bf16[512,8192]{1,0:T(8,128)(2,1)S(1)}, bf16[512,8192]{1,0:T(8,128)(2,1)}, u32[]{:S(2)}) copy-start(bf16[512,8192]{1,0:T(8,128)(2,1)} %param.8) | copy-start | bytes 25165828
  21.6 6.3 %copy-start.3 = (bf16[512,4096]{1,0:T(8,128)(2,1)}, bf16[512,4096]{1,0:T(8,128)(2,1)S(1)}, u32[]{:S(2)}) copy-start(bf16[512,4096]{1,0:T(8,128)(2,1)S(1)} %get-tuple-element.14) | copy-start | bytes 12582916
  28.9 67.5 %collective-permute-start.1 = (bf16[512,4096]{1,0:T(8,128)(2,1)}, bf16[512,4096]{1,0:T(8,128)(2,1)}, u32[]{:S(2)}, u32[]{:S(2)}) collective-permute-start(bf16[512,4096]{1,0:T(8,128)(2,1)} %select_dynamic-update-slice_fusion), channel_id=1, source_target_pairs={{0,1},{1,0},{2,3},{3,2},{4,5},{5,4},{6,7},{7,6},{8,9},{9,8},{10,11... | collective-permute-start | bytes 12582920 | tf_op jit(solution)/shard_map/ppermute | solution.py:86
  29.3 6.6 %copy-start.4 = (bf16[2,32,8192]{2,1,0:T(8,128)(2,1)S(1)}, bf16[2,32,8192]{2,1,0:T(8,128)(2,1)}, u32[]{:S(2)}) copy-start(bf16[2,32,8192]{2,1,0:T(8,128)(2,1)} %param.10) | copy-start | bytes 3145732
  35.8 11.6 %copy-start.10 = (bf16[512,512]{1,0:T(8,128)(2,1)S(1)}, bf16[512,512]{1,0:T(8,128)(2,1)}, u32[]{:S(2)}) copy-start(bf16[512,512]{1,0:T(8,128)(2,1)} %param.12) | copy-start | bytes 1572868
  35.8 12.5 %copy-start.11 = (s32[64]{0:T(128)S(1)}, s32[64]{0:T(128)}, u32[]{:S(2)}) copy-start(s32[64]{0:T(128)} %param.9) | copy-start | bytes 772
  40.7 16.8 %all-to-all-start = ((bf16[8,128,128]{2,1,0:T(8,128)(2,1)}), bf16[8,128,128]{2,1,0:T(8,128)(2,1)}, u32[]{:S(2)}, u32[]{:S(2)}) async-start(bf16[8,128,128]{2,1,0:T(8,128)(2,1)} %broadcast_in_dim.10), calls=%async_computation | async-start | bytes 524288 | tf_op jit(solution)/shard_map/all_to_all | solution.py:95
  47.4 147.5 %all-gather.11.cloned.1.call-start = ((), (), s32[]{:S(2)}) async-start(), calls=%async_computation.7 | async-start | bytes 2359296 | tf_op jit(solution)/shard_map/all_gather | solution.py:92
  57.5 154.6 %collective-permute-start = (bf16[4,256,128]{2,1,0:T(8,128)(2,1)}, bf16[4,256,128]{2,1,0:T(8,128)(2,1)}, u32[]{:S(2)}, u32[]{:S(2)}) collective-permute-start(bf16[4,256,128]{2,1,0:T(8,128)(2,1)} %bitcast.8), channel_id=1, source_target_pairs={{0,1},{1,0},{2,3},{3,2},{4,5},{5,4},{6,7},{7,6},{8,9},{9,8},{10,11... | collective-permute-start | bytes 786440 | tf_op jit(solution)/shard_map/ppermute | solution.py:86
  57.5 101.0 %collective-permute-start.4 = (bf16[4096,128]{1,0:T(8,128)(2,1)}, bf16[4096,128]{1,0:T(8,128)(2,1)}, u32[]{:S(2)}, u32[]{:S(2)}) collective-permute-start(bf16[4096,128]{1,0:T(8,128)(2,1)} %all-gather.9.cloned.1.call-done), channel_id=1, source_target_pairs={{0,16},{16,0},{1,17},{17,1},{2,18},{18,2},{3,19},{19,3},{4,20},{20... | collective-permute-start | bytes 3145736 | tf_op jit(solution)/shard_map/ppermute | solution.py:89
  94.9 57.0 %collective-permute-start.2 = (bf16[4096,128]{1,0:T(8,128)(2,1)}, bf16[4096,128]{1,0:T(8,128)(2,1)S(1)}, u32[]{:S(2)}, u32[]{:S(2)}) collective-permute-start(bf16[4096,128]{1,0:T(8,128)(2,1)} %all-gather.5.cloned.1.call-done), channel_id=1, source_target_pairs={{0,16},{16,0},{1,17},{17,1},{2,18},{18,2},{3,19},{19,3},{4,20},{20... | collective-permute-start | bytes 3145736 | tf_op jit(solution)/shard_map/ppermute | solution.py:89
  145.1 6.8 %copy-start = (bf16[1088,4096]{1,0:T(8,128)(2,1)S(1)}, bf16[1088,4096]{1,0:T(8,128)(2,1)}, u32[]{:S(2)}) copy-start(bf16[1088,4096]{1,0:T(8,128)(2,1)} %pad_maximum_fusion) | copy-start | bytes 26738692
  151.9 2.5 copy-start.9
  158.5 3.8 %copy-start.8 = (bf16[4096,128]{1,0:T(8,128)(2,1)S(1)}, bf16[4096,128]{1,0:T(8,128)(2,1)}, u32[]{:S(2)}) copy-start(bf16[4096,128]{1,0:T(8,128)(2,1)} %all-gather.9.cloned.1.call-done) | copy-start | bytes 3145732
  158.5 44.8 %collective-permute-start.3 = (f32[1088,512]{1,0:T(8,128)}, f32[1088,512]{1,0:T(8,128)}, u32[]{:S(2)}, u32[]{:S(2)}) collective-permute-start(f32[1088,512]{1,0:T(8,128)} %pad_maximum_fusion.1), channel_id=1, source_target_pairs={{0,1},{1,0},{2,3},{3,2},{4,5},{5,4},{6,7},{7,6},{8,9},{9,8},{10,11... | collective-permute-start | bytes 6684680 | tf_op jit(solution)/shard_map/ppermute | solution.py:86
  201.8 1.4 collective-permute-start.6
  210.0 1.3 copy-start.5
  210.0 1.3 copy-start.6
  214.7 3.3 %copy-start.2 = (f32[4,512,1024]{2,1,0:T(8,128)}, f32[4,512,1024]{2,1,0:T(8,128)S(1)}, u32[]{:S(2)}) copy-start(f32[4,512,1024]{2,1,0:T(8,128)S(1)} %get-tuple-element.51) | copy-start | bytes 25165828
  214.7 7.2 %copy-start.7 = (bf16[1088,512]{1,0:T(8,128)(2,1)S(1)}, bf16[1088,512]{1,0:T(8,128)(2,1)}, u32[]{:S(2)}) copy-start(bf16[1088,512]{1,0:T(8,128)(2,1)} %pad_maximum_fusion.2) | copy-start | bytes 3342340
  218.6 9.8 %all-to-all-start.1 = ((f32[8,2,128]{2,1,0:T(2,128)}), f32[8,2,128]{2,1,0:T(2,128)S(1)}, u32[]{:S(2)}, u32[]{:S(2)}) async-start(f32[8,2,128]{2,1,0:T(2,128)} %pad_maximum_fusion.6), calls=%async_computation.1 | async-start | bytes 16384 | tf_op jit(solution)/shard_map/all_to_all | solution.py:95
  226.4 2.2 collective-permute-start.5
  229.3 14.6 %all-to-all-start.2 = ((bf16[8,128,128]{2,1,0:T(8,128)(2,1)}), bf16[8,128,128]{2,1,0:T(8,128)(2,1)S(1)}, u32[]{:S(2)}, u32[]{:S(2)}) async-start(bf16[8,128,128]{2,1,0:T(8,128)(2,1)} %bitcast.16), calls=%async_computation.2 | async-start | bytes 524288 | tf_op jit(solution)/shard_map/all_to_all | solution.py:95
  247.7 2.0 collective-permute-start.7
Sparse Core Ops, SparseCore 0:
  9.5 43.0 all-gather.8
  54.7 40.1 all-gather.4
  97.0 48.0 all-gather.6
  147.1 47.7 all-gather.10

commit v3 on v1

v3 whole, which is shorter than its diff:
```python
import jax
import jax.numpy as jnp
from jax import lax
from jax.experimental import pallas as pl
from jax.experimental.pallas import tpu as pltpu
from jax.sharding import PartitionSpec as P

D = 8192
HEAD_DIM = 128
KV_HEADS = 4
GQA = 8
PAGE = 128
PROMPT_PAGES = 64
LINE = 4

rope_base = 1000000.0


def rope_tables(position):
    half_dim = HEAD_DIM // 2
    frequency = rope_base ** (-jnp.arange(half_dim, dtype=jnp.float32) * 2.0 / HEAD_DIM)
    angles = position.astype(jnp.float32)[..., None] * frequency
    return jnp.cos(angles), jnp.sin(angles)


def turn(vector, tables):
    cosine, sine_part = tables
    half_dim = HEAD_DIM // 2
    first_half = vector[..., :half_dim]
    second_half = vector[..., half_dim:]
    return jnp.concatenate(
        [
            first_half * cosine - second_half * sine_part,
            second_half * cosine + first_half * sine_part,
        ],
        axis=-1,
    )


def finish_heads(prefix_top, prefix_total, prefix_sum, queries, new_keys, new_values):
    score_scale = queries.shape[-1] ** (-0.5)
    query_wide = queries.astype(jnp.float32)
    key_wide = new_keys.astype(jnp.float32)
    value_wide = new_values.astype(jnp.float32)
    own_score = jnp.sum(query_wide * key_wide, axis=-1) * score_scale
    back_score = jnp.sum(query_wide[1] * key_wide[0], axis=-1) * score_scale
    first_high = jnp.maximum(prefix_top[0], own_score[0])
    first_old = jnp.exp(prefix_top[0] - first_high)
    first_own = jnp.exp(own_score[0] - first_high)
    first_out = (first_old[..., None] * prefix_sum[0] + first_own[..., None] * value_wide[0]) / (
        first_old * prefix_total[0] + first_own
    )[..., None]
    second_high = jnp.maximum(jnp.maximum(prefix_top[1], own_score[1]), back_score)
    second_old = jnp.exp(prefix_top[1] - second_high)
    second_back = jnp.exp(back_score - second_high)
    second_own = jnp.exp(own_score[1] - second_high)
    second_num = (
        second_old[..., None] * prefix_sum[1]
        + second_back[..., None] * value_wide[0]
        + second_own[..., None] * value_wide[1]
    )
    second_out = second_num / (second_old * prefix_total[1] + second_back + second_own)[..., None]
    return jnp.stack([first_out, second_out]).astype(jnp.bfloat16)


def mover(groups, devices):
    deep = devices // LINE

    def move(value, step):
        pairs = []
        for g in range(groups):
            for s in range(devices):
                a, b, c = s // LINE, s // 2 % 2, s % 2
                to_g, to_a, to_b, to_c = step(g, a, b, c)
                to_s = (to_a % deep) * LINE + to_b * 2 + to_c
                pairs.append((g * devices + s, to_g * devices + to_s))
        return lax.ppermute(value, ("groups", "sample"), pairs)

    along_z = lambda v, k=1: move(v, lambda g, a, b, c: (g, a + k, b, c))
    along_y = lambda v: move(v, lambda g, a, b, c: (g, a, 1 - b, c))
    along_x = lambda v: move(v, lambda g, a, b, c: (g ^ 1, a, b, c))
    in_chip = lambda v: move(v, lambda g, a, b, c: (g, a, b, 1 - c))
    return along_z, along_y, along_x, in_chip


def after(value, done):
    return lax.optimization_barrier((value, done))[0]


def pick(sources, blocks, width):
    heights = [source.shape[0] for source in sources]
    height = sum(heights)

    def body(block_ref, *refs):
        start = 0
        for ref, rows in zip(refs[:-1], heights):
            refs[-1][start : start + rows, :] = ref[...]
            start += rows

    return pl.pallas_call(
        body,
        grid_spec=pltpu.PrefetchScalarGridSpec(
            num_scalar_prefetch=1,
            grid=(blocks.shape[0],),
            in_specs=[
                pl.BlockSpec((rows, width), lambda i, block_ref: (0, block_ref[i]))
                for rows in heights
            ],
            out_specs=pl.BlockSpec((height, width), lambda i, block_ref: (0, i)),
        ),
        out_shape=jax.ShapeDtypeStruct((height, blocks.shape[0] * width), sources[0].dtype),
        cost_estimate=pl.CostEstimate(
            flops=0, bytes_accessed=4 * height * blocks.shape[0] * width, transcendentals=0
        ),
    )(blocks, *sources)


def on_device(
    prompt_states,
    page_table,
    step_states,
    sample_order,
    key_weight,
    value_weight,
    query_weight,
    out_weight,
):
    devices = lax.axis_size("sample")
    groups = lax.axis_size("groups")
    own_index = lax.axis_index("sample")
    first = lax.axis_index("groups") % 2 == 0
    deep = devices // LINE
    own_a, own_b, own_c = own_index // LINE, own_index // 2 % 2, own_index % 2
    along_z, along_y, along_x, in_chip = mover(groups, devices)
    row_count = prompt_states.shape[0]
    chip_rows = 2 * row_count
    pages_here = row_count // PAGE
    heads_here = query_weight.shape[1] // HEAD_DIM
    total_pages = page_table.shape[0]
    prompts = total_pages // PROMPT_PAGES
    samples = sample_order.shape[0]
    steps = 2 * samples
    group_size = samples // prompts
    score_scale = HEAD_DIM ** (-0.5)
    own_kv = own_index * heads_here // GQA
    wide_states = step_states.reshape(steps, D)
    rows = heads_here * steps
    width = key_weight.shape[0]
    half = key_weight.shape[1] // 2

    def in_order(mine, other):
        return jnp.where(
            first,
            jnp.concatenate([mine, other], axis=1),
            jnp.concatenate([other, mine], axis=1),
        )

    places = [(k, flip) for k in range(deep) for flip in (0, 1)]

    def blocks(core, turns):
        return jnp.stack(
            [
                ((own_a + deep + k) % deep) * LINE + (own_b ^ flip) * 2 + core
                for k, flip in turns
            ]
        )

    back = [(-k, flip) for k, flip in places]
    sent = pick([prompt_states], blocks(1 - own_c, back), width)
    got = in_chip(sent)
    kept = pick([prompt_states, wide_states], after(blocks(own_c, back), sent), width)

    key_mine = jnp.where(first, key_weight[:, :half], key_weight[:, half:])
    value_mine = jnp.where(first, value_weight[:, :half], value_weight[:, half:])
    value_other = jnp.where(first, value_weight[:, half:], value_weight[:, :half])
    done = {0: [got]}

    def send(move, value, turn_at):
        if turn_at > 1:
            value = after(value, done[turn_at - 2])
        done.setdefault(turn_at, []).append(move(value))
        return done[turn_at][-1]

    key_z, key_full, key_y = {0: key_mine}, {0: key_weight}, {}
    value_pairs, other_pairs = {}, {}
    for r in range(2 * deep - 1):
        late = r - deep + 2
        if r + 1 < deep:
            key_z[r + 1] = send(along_z, key_z[r], r)
        elif late < deep:
            value_pairs[late] = send(along_z, value_pairs[late - 1], r)
        if r == 0:
            value_y = send(along_y, value_mine, r)
            value_pairs[0] = jnp.concatenate([value_mine, value_y])
        elif r == 1:
            key_y[0] = send(along_y, key_weight, r)
        if 0 < r < deep:
            key_full[r] = in_order(key_z[r], send(along_x, key_z[r], r))
        elif r:
            other_pairs[late - 1] = send(along_x, value_pairs[late - 1], r)
        if r == deep - 1:
            other_pairs[0] = jnp.concatenate([value_other, send(along_x, value_y, r)])
        if 0 < late < deep:
            key_y[late] = send(along_y, key_full[late], r)

    step_place = PROMPT_PAGES * PAGE + jnp.arange(2, dtype=jnp.int32)
    step_tables = tuple(t[:, None, :] for t in rope_tables(step_place))
    queries = jnp.dot(after(wide_states, sent), query_weight, preferred_element_type=jnp.float32)
    queries = queries.reshape(2, samples, heads_here, HEAD_DIM).transpose(2, 0, 1, 3)
    queries = turn(queries, step_tables).astype(jnp.bfloat16)
    flat_queries = queries.reshape(rows, HEAD_DIM)
    pair_queries = jnp.stack([flat_queries, along_y(flat_queries)])
    ring = [pair_queries] + [along_z(pair_queries, deep - j) for j in range(1, deep)]
    line = lax.dynamic_slice_in_dim(jnp.stack(ring + ring), deep - own_a, deep)
    all_queries = jnp.stack([line, in_chip(line)], axis=1)
    by_owner = (deep, 2, 2, rows)
    all_queries = all_queries.reshape(KV_HEADS, -1, HEAD_DIM)

    own_pages = jnp.concatenate(
        [
            holder * pages_here + jnp.arange(pages_here, dtype=jnp.int32)
            for holder in (own_index, own_index ^ 1)
        ]
    )
    slots = jnp.sum(
        jnp.where(
            page_table[None, :] == own_pages[:, None],
            jnp.arange(total_pages, dtype=jnp.int32)[None, :],
            0,
        ),
        axis=1,
    )
    positions = (slots % PROMPT_PAGES * PAGE)[:, None] + jnp.arange(PAGE, dtype=jnp.int32)[None, :]
    cosine, sine_part = rope_tables(positions.reshape(chip_rows))

    turns = [(k, flip) for flip in (0, 1) for k in range(deep)]
    out_width = out_weight.shape[1] // devices
    out_sent = pick([out_weight], after(blocks(1 - own_c, turns), key_y[0]), out_width)
    out_kept = pick([out_weight], after(blocks(own_c, turns), out_sent), out_width)
    out_got = in_chip(out_sent)

    def columns(source, start, count):
        return lax.slice_in_dim(source, start * width, (start + count) * width, axis=1)

    key_own = key_sib = 0.0
    for i, (k, flip) in enumerate(places):
        piece = key_y[k] if flip else key_full[k]
        key_own += jnp.dot(columns(kept, i, 1), piece, preferred_element_type=jnp.float32)
        key_sib += jnp.dot(columns(got, i, 1), piece, preferred_element_type=jnp.float32)
    own_back, sib_back = in_chip(key_own), in_chip(key_sib)
    step_keys = key_own[row_count:] + own_back[row_count:]
    prefix_keys = jnp.concatenate([key_own[:row_count] + sib_back, key_sib + own_back[:row_count]])
    prefix_keys = turn(
        prefix_keys.reshape(chip_rows, KV_HEADS, HEAD_DIM), (cosine[:, None], sine_part[:, None])
    ).astype(jnp.bfloat16)
    step_keys = lax.dynamic_slice_in_dim(step_keys, own_kv * HEAD_DIM, HEAD_DIM, 1)
    new_keys = turn(step_keys.reshape(2, samples, HEAD_DIM), step_tables).astype(jnp.bfloat16)

    scores = (
        jnp.einsum("krd,lkd->krl", all_queries, prefix_keys, preferred_element_type=jnp.float32)
        * score_scale
    )
    if prompts > 1:
        token_prompt = jnp.repeat(slots // PROMPT_PAGES, PAGE)
        row_prompt = jnp.tile(sample_order // group_size, scores.shape[1] // samples)
        scores = jnp.where(row_prompt[:, None] == token_prompt[None, :], scores, -1e30)
    top = jnp.max(scores, axis=-1)
    weights = jnp.exp(scores - top[..., None])
    total = jnp.sum(weights, axis=-1)
    weights = weights.astype(jnp.bfloat16)

    stats = jnp.stack([top.reshape(by_owner), total.reshape(by_owner)])
    stats = jnp.stack([stats, along_y(stats)[:, :, :, ::-1]])
    stats = jnp.concatenate([stats] + [along_z(stats, k) for k in range(1, deep)])
    prefix_top = jnp.max(stats[:, 0], axis=0)
    prefix_total = jnp.sum(jnp.exp(stats[:, 0] - prefix_top) * stats[:, 1], axis=0)
    factor = jnp.exp(top.reshape(by_owner) - prefix_top)
    prefix_top = lax.dynamic_index_in_dim(prefix_top, own_a, 0, False)[0, 0]
    prefix_total = lax.dynamic_index_in_dim(prefix_total, own_a, 0, False)[0, 0]

    def project(pieces):
        own = sib = 0.0
        for k in range(deep):
            own += jnp.dot(columns(kept, 2 * k, 2), pieces[k], preferred_element_type=jnp.float32)
            sib += jnp.dot(columns(got, 2 * k, 2), pieces[k], preferred_element_type=jnp.float32)
        return own, sib

    own_m, sib_m = project(value_pairs)
    own_o, sib_o = project(other_pairs)
    step_values = in_order(own_m[row_count:], own_o[row_count:])
    step_values = step_values + in_chip(step_values)
    new_values = lax.dynamic_slice_in_dim(step_values, own_kv * HEAD_DIM, HEAD_DIM, 1)
    new_values = new_values.reshape(2, samples, HEAD_DIM).astype(jnp.bfloat16)
    values = in_order(
        jnp.concatenate([own_m[:row_count], sib_m]).astype(jnp.bfloat16),
        jnp.concatenate([own_o[:row_count], sib_o]).astype(jnp.bfloat16),
    ).reshape(chip_rows, KV_HEADS, HEAD_DIM)
    partial = jnp.einsum("krl,lkd->krd", weights, values, preferred_element_type=jnp.float32)
    partial = partial.reshape(by_owner + (HEAD_DIM,)) * factor[..., None]

    def narrow(value):
        return value.astype(jnp.bfloat16)

    partial = partial[:, 0] + in_chip(narrow(partial[:, 1])).astype(jnp.float32)
    partial = partial[:, 0] + along_y(narrow(partial[:, 1])).astype(jnp.float32)
    narrowed = narrow(partial)
    prefix_sum = lax.dynamic_index_in_dim(partial, own_a, 0, False)
    for k in range(1, deep):
        piece = lax.dynamic_index_in_dim(narrowed, (own_a + k) % deep, 0, False)
        prefix_sum = prefix_sum + along_z(piece, k).astype(jnp.float32)

    by_head = (heads_here, 2, samples)
    head_out = finish_heads(
        prefix_top.reshape(by_head).swapaxes(0, 1),
        prefix_total.reshape(by_head).swapaxes(0, 1),
        prefix_sum.reshape(by_head + (HEAD_DIM,)).swapaxes(0, 1),
        queries.swapaxes(0, 1),
        new_keys[:, None],
        new_values[:, None],
    )
    flat_heads = head_out.transpose(0, 2, 1, 3).reshape(steps, heads_here * HEAD_DIM)
    terms = jnp.dot(flat_heads, out_kept, preferred_element_type=jnp.float32)
    terms += jnp.dot(in_chip(flat_heads), out_got, preferred_element_type=jnp.float32)
    share = deep * out_width
    terms = terms[:, :share] + along_y(narrow(terms[:, share:])).astype(jnp.float32)
    attn_out = terms[:, :out_width]
    for k in range(1, deep):
        piece = narrow(terms[:, k * out_width : (k + 1) * out_width])
        attn_out = attn_out + along_z(piece, k).astype(jnp.float32)
    return narrow(attn_out).reshape(2, samples, -1)


def solution(mesh):
    in_specs = (
        P(("groups", "sample"), None),
        P("groups"),
        P(None, "groups", None),
        P("groups"),
        P("sample", None),
        P("sample", None),
        P(None, "sample"),
        P("sample", None),
    )
    out_specs = P(None, "groups", "sample")
    return jax.shard_map(
        on_device, mesh=mesh, in_specs=in_specs, out_specs=out_specs, check_vma=False
    )
```

time: 258 us -> 250 us (0.969)
  blocking collectives: 53 us -> 0 us
  matrix products: 32.3 us -> 74.8 us
  Pallas kernels: 0 us -> 28 us
  local copies, waits for them, and re-layouts: 36 us -> 16.6 us
  waiting for transfers between devices: 77 us -> 63.4 us
  starting transfers between devices: 40.6 us -> 45.3 us
    dot_general x35 -> x36, matrix products: 29.6 us -> 70.1 us  [the longest x8 21.7 us: on_device(): jnp.dot(columns(got, i, 1), piece, preferred_element_type=jnp.float32)]
    all_to_all x1 -> x0, blocking collectives: 28.7 us -> none  [on_device(): lax.all_to_all(terms, 'sample', split_axis=0, concat_axis=0, tiled=True)]
    pallas_call x0 -> x4, Pallas kernels: none -> 28 us  [pick(): pl.pallas_call(body, grid_spec=pltpu.PrefetchScalarGridSpec(num_scalar_pr...]
    all_gather x1 -> x0, blocking collectives: 24.3 us -> none  [on_device(): lax.all_gather(queries.reshape(rows, HEAD_DIM), 'sample', axis=0, tiled=T...]
    all_to_all x2 -> x0, waiting for transfers between devices: 20.4 us -> none  [the longest x1 14.1 us: on_device(): lax.all_to_all(partial.reshape(devices, rows, HEAD_DIM), 'sample', split_...]
    unnamed x35 -> x74, local copies, waits for them, and re-layouts: 17 us -> 2.43 us
    ppermute x31 -> x42, starting transfers between devices: 33.5 us -> 45.3 us  [move(): return lax.ppermute(value, ('groups', 'sample'), pairs)]
    all_to_all x2 -> x0, starting transfers between devices: 7.07 us -> none  [the longest x1 3.57 us: on_device(): lax.all_to_all(partial.reshape(devices, rows, HEAD_DIM), 'sample', split_...]
  transfers between devices with their start and end apart: 33 -> 42, of which waited for: 12 -> 20; matrix products, arithmetic and copies ran while one was open for 19% -> 42% of each run, Pallas kernels for 0% -> 11%
where the time goes in v3:
time: 250 us; the launch traced here: 248 us
  matrix products  74.8 us (30%)
  waiting for transfers between devices  63.4 us (25%)
  starting transfers between devices  45.3 us (18%)
  Pallas kernels  28 us (11%)
  other arithmetic  19.3 us (8%)
  local copies, waits for them, and re-layouts  16.6 us (7%)
    ppermute x42, waiting for transfers between devices, move(): return lax.ppermute(value, ('groups', 'sample'), pairs)  63.4 us
    ppermute x42, starting transfers between devices, move(): return lax.ppermute(value, ('groups', 'sample'), pairs)  45.3 us
    pallas_call x4, Pallas kernels, pick(): pl.pallas_call(body, grid_spec=pltpu.PrefetchScalarGridSpec(num_scalar_pr...  28 us
    dot_general x8, matrix products, on_device(): jnp.dot(columns(got, i, 1), piece, preferred_element_type=jnp.float32)  21.7 us
    dot_general x8, matrix products, project(): jnp.dot(columns(got, 2 * k, 2), pieces[k], preferred_element_type=jnp.flo...  15.3 us
    dot_general x8, matrix products, project(): jnp.dot(columns(kept, 2 * k, 2), pieces[k], preferred_element_type=jnp.fl...  12.4 us
    dot_general x1, matrix products, on_device(): jnp.einsum('krl,lkd->krd', weights, values, preferred_element_type=jnp.fl...  7.68 us
    dot_general x8, matrix products, on_device(): jnp.dot(columns(kept, i, 1), piece, preferred_element_type=jnp.float32)  7.46 us
  transfers between devices with their start and end apart: 42, of which 20 were waited for; matrix products, arithmetic and copies ran while one was open for 42% of the time, Pallas kernels for 11%

profile of v3, /device:TPU:0, one launch (start us, length us, event | category | flops | bytes accessed | tf_op | source)
XLA Modules:
  0.0 248.3 jit_solution(8112645481385640057)
XLA Ops:
  0.0 3.0 %collective-permute-start.5 = (bf16[512,512]{1,0:T(8,128)(2,1)}, bf16[512,512]{1,0:T(8,128)(2,1)}, u32[]{:S(2)}, u32[]{:S(2)}) collective-permute-start(bf16[512,512]{1,0:T(8,128)(2,1)} %param.11), channel_id=1, source_target_pairs={{0,2},{1,3},{2,0},{3,1},{4,6},{5,7},{6,4},{7,5},{8,10},{9,11},{10,... | collective-permute-start | bytes 1572872 | tf_op jit(solution)/shard_map/ppermute | solution.py:77
  3.0 1.8 slice_select_fusion
  4.7 1.6 collective-permute-start.6
  7.0 7.5 %shard_map.73 = bf16[512,4096]{1,0:T(8,128)(2,1)} custom-call(s32[8]{0:T(128)} %stack.160.block_ref, bf16[512,8192]{1,0:T(8,128)(2,1)} %refs_0_.5), custom_call_target="tpu_custom_call" | custom-call | bytes 8388608 | tf_op jit(solution)/shard_map/pallas_call | solution.py:100
  15.1 3.0 %fusion.150 = f32[64,256]{1,0:T(8,128)S(1)} fusion(bf16[64,8192]{1,0:T(8,128)(2,1)S(1)} %bitcast.197, bf16[8192,256]{1,0:T(8,128)(2,1)} %param.13), kind=kOutput, calls=%fused_computation.255 | convolution fusion | flops 268435456 | bytes 5308416 | tf_op jit(solution)/shard_map/dot_general | solution.py:208
  18.9 1.6 collective-permute-start
  21.5 7.7 %shard_map.74 = bf16[576,4096]{1,0:T(8,128)(2,1)} custom-call(s32[8]{0:T(128)} %stack.179.block_ref, bf16[512,8192]{1,0:T(8,128)(2,1)} %refs_0_.5, bf16[64,8192]{1,0:T(8,128)(2,1)} %bitcast.196), custom_call_target="tpu_custom_call" | custom-call | bytes 9437184 | tf_op jit(solution)/shard_map/pallas_call | solution.py:100
  29.2 1.5 fusion.83
  30.7 3.1 %multiply_cosine_fusion = (f32[1024,64]{1,0:T(8,128)}, f32[1024,64]{1,0:T(8,128)}) fusion(f32[64]{0:T(128)S(1)} %multiply_power_fusion, f32[1024]{0:T(1024)S(1)} %convert_bitcast_fusion.1), kind=kLoop, calls=%fused_computation.89 | loop fusion | flops 65536 | bytes 528640 | tf_op jit(solution)/shard_map/cos | solution.py:23
  35.2 2.3 collective-permute-start.1
  39.5 2.6 %collective-permute-start.2 = (bf16[2,128,128]{2,1,0:T(8,128)(2,1)S(1)}, bf16[2,128,128]{2,1,0:T(8,128)(2,1)S(1)}, u32[]{:S(2)}, u32[]{:S(2)}) collective-permute-start(bf16[2,128,128]{2,1,0:T(8,128)(2,1)S(1)} %get-tuple-element.45), channel_id=1, source_target_pairs={{0,8},{1,9},{2,10},{3,11},{4,12},{5,13},{6,14},{7,15},{8,0},{9,1},... | collective-permute-start | bytes 196616 | tf_op jit(solution)/shard_map/ppermute | solution.py:77
  42.1 2.6 %collective-permute-done.2 = bf16[2,128,128]{2,1,0:T(8,128)(2,1)S(1)} collective-permute-done((bf16[2,128,128]{2,1,0:T(8,128)(2,1)S(1)}, bf16[2,128,128]{2,1,0:T(8,128)(2,1)S(1)}, u32[]{:S(2)}, u32[]{:S(2)}) %collective-permute-start.2) | collective-permute-done | bytes 65568 | tf_op jit(solution)/shard_map/ppermute | solution.py:77
  44.6 1.8 collective-permute-start.3
  46.5 5.0 %collective-permute-done.3 = bf16[2,128,128]{2,1,0:T(8,128)(2,1)S(1)} collective-permute-done((bf16[2,128,128]{2,1,0:T(8,128)(2,1)S(1)}, bf16[2,128,128]{2,1,0:T(8,128)(2,1)S(1)}, u32[]{:S(2)}, u32[]{:S(2)}) %collective-permute-start.3) | collective-permute-done | bytes 65568 | tf_op jit(solution)/shard_map/ppermute | solution.py:77
  51.6 1.6 collective-permute-start.7
  53.3 5.0 %collective-permute-done.7 = bf16[512,256]{1,0:T(8,128)(2,1)S(1)} collective-permute-done((bf16[512,256]{1,0:T(8,128)(2,1)}, bf16[512,256]{1,0:T(8,128)(2,1)S(1)}, u32[]{:S(2)}, u32[]{:S(2)}) %collective-permute-start.7) | collective-permute-done | bytes 262176 | tf_op jit(solution)/shard_map/ppermute | solution.py:77
  59.4 2.2 collective-permute-done.8
  64.4 6.4 %shard_map.75 = bf16[256,4096]{1,0:T(8,128)(2,1)} custom-call(s32[8]{0:T(128)} %stack.198.block_ref, bf16[256,8192]{1,0:T(8,128)(2,1)} %refs_0_.7), custom_call_target="tpu_custom_call" | custom-call | bytes 4194304 | tf_op jit(solution)/shard_map/pallas_call | solution.py:100
  70.7 6.5 %shard_map.76 = bf16[256,4096]{1,0:T(8,128)(2,1)} custom-call(s32[8]{0:T(128)} %stack.191.block_ref, bf16[256,8192]{1,0:T(8,128)(2,1)} %refs_0_.7), custom_call_target="tpu_custom_call" | custom-call | bytes 4194304 | tf_op jit(solution)/shard_map/pallas_call | solution.py:100
  77.3 1.8 convolution_add_fusion.3
  79.1 1.7 fusion.79
  80.8 1.9 fusion.54
  85.2 2.6 %fusion.94 = f32[512,512]{1,0:T(8,128)} fusion(bf16[512,512]{1,0:T(8,128)(2,1)} %collective-permute-done.9, bf16[512,4096]{1,0:T(8,128)(2,1)} %collective-permute-done.10), kind=kOutput, calls=%fused_computation.118 | convolution fusion | flops 268435456 | bytes 2097152 | tf_op jit(solution)/shard_map/dot_general | solution.py:249
  87.8 2.5 %fusion.96 = f32[512,512]{1,0:T(8,128)} fusion(bf16[512,512]{1,0:T(8,128)(2,1)S(1)} %maximum_select_fusion.2, bf16[512,4096]{1,0:T(8,128)(2,1)} %collective-permute-done.10), kind=kOutput, calls=%fused_computation.120 | convolution fusion | flops 268435456 | bytes 2097152 | tf_op jit(solution)/shard_map/dot_general | solution.py:249
  90.3 2.6 %fusion.98 = f32[512,512]{1,0:T(8,128)} fusion(bf16[512,512]{1,0:T(8,128)(2,1)} %collective-permute-done.5, bf16[512,4096]{1,0:T(8,128)(2,1)} %collective-permute-done.10), kind=kOutput, calls=%fused_computation.122 | convolution fusion | flops 268435456 | bytes 2097152 | tf_op jit(solution)/shard_map/dot_general | solution.py:249
  92.9 1.8 fusion.68
  98.9 2.5 %fusion.92 = f32[512,512]{1,0:T(8,128)} fusion(bf16[512,512]{1,0:T(8,128)(2,1)S(1)} %maximum_select_fusion.3, bf16[512,4096]{1,0:T(8,128)(2,1)} %collective-permute-done.10), kind=kOutput, calls=%fused_computation.116 | convolution fusion | flops 268435456 | bytes 2097152 | tf_op jit(solution)/shard_map/dot_general | solution.py:249
  101.4 14.7 %collective-permute-done.15 = bf16[512,256]{1,0:T(8,128)(2,1)S(1)} collective-permute-done((bf16[512,256]{1,0:T(8,128)(2,1)S(1)}, bf16[512,256]{1,0:T(8,128)(2,1)S(1)}, u32[]{:S(2)}, u32[]{:S(2)}) %collective-permute-start.15) | collective-permute-done | bytes 262176 | tf_op jit(solution)/shard_map/ppermute | solution.py:77
  116.1 1.5 collective-permute-start.14
  118.8 2.5 %fusion.88 = f32[512,512]{1,0:T(8,128)} fusion(bf16[512,512]{1,0:T(8,128)(2,1)S(1)} %maximum_select_fusion.4, bf16[512,4096]{1,0:T(8,128)(2,1)} %collective-permute-done.10), kind=kOutput, calls=%fused_computation.112 | convolution fusion | flops 268435456 | bytes 2097152 | tf_op jit(solution)/shard_map/dot_general | solution.py:249
  121.3 3.0 %collective-permute-start.26 = (bf16[1024,256]{1,0:T(8,128)(2,1)}, bf16[1024,256]{1,0:T(8,128)(2,1)}, u32[]{:S(2)}, u32[]{:S(2)}) collective-permute-start(bf16[1024,256]{1,0:T(8,128)(2,1)} %collective-permute-done.25), channel_id=1, source_target_pairs={{0,4},{1,5},{2,6},{3,7},{4,8},{5,9},{6,10},{7,11},{8,12},{9,13},{1... | collective-permute-start | bytes 1572872 | tf_op jit(solution)/shard_map/ppermute | solution.py:77
  124.3 1.8 fusion.64
  126.2 4.8 %collective-permute-done.14 = bf16[512,512]{1,0:T(8,128)(2,1)S(1)} collective-permute-done((bf16[512,512]{1,0:T(8,128)(2,1)S(1)}, bf16[512,512]{1,0:T(8,128)(2,1)S(1)}, u32[]{:S(2)}, u32[]{:S(2)}) %collective-permute-start.14) | collective-permute-done | bytes 524320 | tf_op jit(solution)/shard_map/ppermute | solution.py:77
  132.2 2.4 fusion.90
  136.5 2.5 %fusion.66 = f32[512,256]{0,1:T(8,128)} fusion(bf16[1024,256]{1,0:T(8,128)(2,1)S(1)} %collective-permute-done.27, bf16[512,4096]{1,0:T(8,128)(2,1)} %collective-permute-done.10), kind=kOutput, calls=%fused_computation.82 | convolution fusion | flops 268435456 | bytes 2097152 | tf_op jit(solution)/shard_map/dot_general | solution.py:285
  139.0 1.5 fusion.50
  142.2 2.6 %fusion.86 = f32[512,512]{1,0:T(8,128)} fusion(bf16[512,512]{1,0:T(8,128)(2,1)S(1)} %collective-permute-done.18, bf16[512,4096]{1,0:T(8,128)(2,1)} %collective-permute-done.10), kind=kOutput, calls=%fused_computation.110 | convolution fusion | flops 268435456 | bytes 2097152 | tf_op jit(solution)/shard_map/dot_general | solution.py:249
  145.6 1.5 fusion.46
  148.5 1.8 fusion.60
  150.4 1.7 fusion.24
  152.9 1.8 fusion.62
  154.8 1.9 fusion.48
  156.7 2.7 %collective-permute-done.29 = bf16[1024,256]{1,0:T(8,128)(2,1)} collective-permute-done((bf16[1024,256]{1,0:T(8,128)(2,1)}, bf16[1024,256]{1,0:T(8,128)(2,1)}, u32[]{:S(2)}, u32[]{:S(2)}) %collective-permute-start.29) | collective-permute-done | bytes 524320 | tf_op jit(solution)/shard_map/ppermute | solution.py:77
  159.5 1.9 fusion.44
  161.3 1.8 fusion.17
  163.3 1.9 fusion.58
  165.2 1.8 fusion.25
  167.0 1.9 copy_bitcast_fusion
  169.8 4.0 %slice_add_fusion = (f32[512,512]{1,0:T(8,128)S(1)}, f32[512,512]{1,0:T(8,128)S(1)}) fusion(f32[576,512]{1,0:T(8,128)} %collective-permute-done.20, f32[512,512]{1,0:T(8,128)} %fusion.86, f32[512,512]{1,0:T(8,128)} %fusion.88, f32[512,512]{1,0:T(8,128)} %fusion.90, f32[512,512]{1,0:T(8,128)} %fusion.92, f32[512,512]{1,0:T(8,128)S(1)} %copy-done.2, ...), kind=kOutput, calls=%fused_computation.39 | convolution fusion | flops 270532608 | bytes 11534336 | tf_op jit(solution)/shard_map/dot_general | solution.py:249
  179.4 1.9 reshape.456
  183.6 4.8 %multiply_reduce_fusion = (f32[4,512]{1,0:T(4,128)S(1)}, f32[4,512,1024]{2,1,0:T(8,128)}) fusion(bf16[4,512,128]{2,1,0:T(8,128)(2,1)S(1)} %bitcast.198, bf16[1024,4,64]{2,0,1:T(8,128)(2,1)S(1)} %get-tuple-element.47, bf16[1024,4,64]{2,0,1:T(8,128)(2,1)S(1)} %get-tuple-element.46), kind=kOutput, calls=%fused_computation.1 | convolution fusion | flops 543160320 | bytes 9969664 | tf_op jit(solution)/shard_map/krd,lkd->krl/dot_general | solution.py:260
  188.4 4.4 %fusion.1 = f32[4,512]{1,0:T(4,128)S(1)} fusion(f32[4,512,1024]{2,1,0:T(8,128)} %get-tuple-element.79, f32[4,512]{1,0:T(4,128)S(1)} %get-tuple-element.78), kind=kLoop, calls=%fused_computation.3 | loop fusion | flops 6289408 | bytes 8404992 | tf_op jit(solution)/shard_map/reduce_sum | solution.py:269
  192.9 1.6 collective-permute-start.21
  194.5 7.7 %fusion.2 = f32[4,512,128]{2,1,0:T(8,128)S(1)} fusion(f32[4,512,1024]{2,1,0:T(8,128)} %get-tuple-element.79, f32[4,512]{1,0:T(4,128)S(1)} %get-tuple-element.78, bf16[512,2,128]{2,0,1:T(8,128)(2,1)S(1)} %copy.71, bf16[512,2,128]{2,0,1:T(8,128)(2,1)S(1)} %copy-done.16, bf16[512,2,128]{2,0,1:T(8,128)(2,1)S(1)} %copy-done.15, ...), kind=kOutput, calls=%fused_computation.5 | convolution fusion | flops 552075264 | bytes 10493953 | tf_op jit(solution)/shard_map/krl,lkd->krd/dot_general | solution.py:298
  202.3 2.5 %collective-permute-start.22 = (f32[2,2,4,2,2,128]{5,4,3,2,1,0:T(2,128)S(1)}, f32[2,2,4,2,2,128]{5,4,3,2,1,0:T(2,128)S(1)}, u32[]{:S(2)}, u32[]{:S(2)}) collective-permute-start(f32[2,2,4,2,2,128]{5,4,3,2,1,0:T(2,128)S(1)} %pad_maximum_fusion.8), channel_id=1, source_target_pairs={{0,4},{1,5},{2,6},{3,7},{4,8},{5,9},{6,10},{7,11},{8,12},{9,13},{1... | collective-permute-start | bytes 98312 | tf_op jit(solution)/shard_map/ppermute | solution.py:77
  205.0 2.8 %collective-permute-start.24 = (f32[2,2,4,2,2,128]{5,4,3,2,1,0:T(2,128)S(1)}, f32[2,2,4,2,2,128]{5,4,3,2,1,0:T(2,128)S(1)}, u32[]{:S(2)}, u32[]{:S(2)}) collective-permute-start(f32[2,2,4,2,2,128]{5,4,3,2,1,0:T(2,128)S(1)} %pad_maximum_fusion.8), channel_id=1, source_target_pairs={{0,12},{1,13},{2,14},{3,15},{4,0},{5,1},{6,2},{7,3},{8,4},{9,5},{1... | collective-permute-start | bytes 98312 | tf_op jit(solution)/shard_map/ppermute | solution.py:77
  208.2 1.8 collective-permute-done.23
  212.1 1.6 collective-permute-done.30
  214.4 5.0 %collective-permute-done.31 = bf16[4,128,128]{2,1,0:T(8,128)(2,1)S(1)} collective-permute-done((bf16[4,128,128]{2,1,0:T(8,128)(2,1)S(1)}, bf16[4,128,128]{2,1,0:T(8,128)(2,1)S(1)}, u32[]{:S(2)}, u32[]{:S(2)}) %collective-permute-start.31) | collective-permute-done | bytes 131104 | tf_op jit(solution)/shard_map/ppermute | solution.py:77
  220.4 3.2 %collective-permute-start.33 = (bf16[128,128]{1,0:T(8,128)(2,1)S(1)}, bf16[128,128]{1,0:T(8,128)(2,1)S(1)}, u32[]{:S(2)}, u32[]{:S(2)}) collective-permute-start(bf16[128,128]{1,0:T(8,128)(2,1)S(1)} %get-tuple-element.57), channel_id=1, source_target_pairs={{0,8},{1,9},{2,10},{3,11},{4,12},{5,13},{6,14},{7,15},{8,0},{9,1},... | collective-permute-start | bytes 98312 | tf_op jit(solution)/shard_map/ppermute | solution.py:77
  229.1 2.1 convolution_add_fusion
  231.7 7.9 %collective-permute-done.38 = bf16[64,2048]{1,0:T(8,128)(2,1)S(1)} collective-permute-done((bf16[64,2048]{1,0:T(8,128)(2,1)S(1)}, bf16[64,2048]{1,0:T(8,128)(2,1)S(1)}, u32[]{:S(2)}, u32[]{:S(2)}) %collective-permute-start.38) | collective-permute-done | bytes 262176 | tf_op jit(solution)/shard_map/ppermute | solution.py:77
  240.0 2.6 %collective-permute-start.40 = (bf16[64,512]{1,0:T(8,128)(2,1)S(1)}, bf16[64,512]{1,0:T(8,128)(2,1)S(1)}, u32[]{:S(2)}, u32[]{:S(2)}) collective-permute-start(bf16[64,512]{1,0:T(8,128)(2,1)S(1)} %get-tuple-element.54), channel_id=1, source_target_pairs={{0,8},{1,9},{2,10},{3,11},{4,12},{5,13},{6,14},{7,15},{8,0},{9,1},... | collective-permute-start | bytes 196616 | tf_op jit(solution)/shard_map/ppermute | solution.py:77
  243.6 2.7 %collective-permute-done.39 = bf16[64,512]{1,0:T(8,128)(2,1)S(1)} collective-permute-done((bf16[64,512]{1,0:T(8,128)(2,1)S(1)}, bf16[64,512]{1,0:T(8,128)(2,1)S(1)}, u32[]{:S(2)}, u32[]{:S(2)}) %collective-permute-start.39) | collective-permute-done | bytes 65568 | tf_op jit(solution)/shard_map/ppermute | solution.py:77
  (224 shorter events, 48.5 us)
Async XLA Ops:
  0.0 59.4 %collective-permute-start.5 = (bf16[512,512]{1,0:T(8,128)(2,1)}, bf16[512,512]{1,0:T(8,128)(2,1)}, u32[]{:S(2)}, u32[]{:S(2)}) collective-permute-start(bf16[512,512]{1,0:T(8,128)(2,1)} %param.11), channel_id=1, source_target_pairs={{0,2},{1,3},{2,0},{3,1},{4,6},{5,7},{6,4},{7,5},{8,10},{9,11},{10,... | collective-permute-start | bytes 1572872 | tf_op jit(solution)/shard_map/ppermute | solution.py:77
  4.7 46.9 %collective-permute-start.6 = (bf16[512,256]{1,0:T(8,128)(2,1)}, bf16[512,256]{1,0:T(8,128)(2,1)}, u32[]{:S(2)}, u32[]{:S(2)}) collective-permute-start(bf16[512,256]{1,0:T(8,128)(2,1)} %slice_select_fusion), channel_id=1, source_target_pairs={{0,4},{1,5},{2,6},{3,7},{4,8},{5,9},{6,10},{7,11},{8,12},{9,13},{1... | collective-permute-start | bytes 786440 | tf_op jit(solution)/shard_map/ppermute | solution.py:77
  7.0 7.5 %copy-start.13 = (bf16[512,512]{1,0:T(8,128)(2,1)S(1)}, bf16[512,512]{1,0:T(8,128)(2,1)}, u32[]{:S(2)}) copy-start(bf16[512,512]{1,0:T(8,128)(2,1)} %param.12) | copy-start | bytes 1572868
  7.0 8.1 %copy-start.3 = (bf16[2,32,8192]{2,1,0:T(8,128)(2,1)S(1)}, bf16[2,32,8192]{2,1,0:T(8,128)(2,1)}, u32[]{:S(2)}) copy-start(bf16[2,32,8192]{2,1,0:T(8,128)(2,1)} %param.10) | copy-start | bytes 3145732
  14.4 68.8 %collective-permute-start.10 = (bf16[512,4096]{1,0:T(8,128)(2,1)}, bf16[512,4096]{1,0:T(8,128)(2,1)}, u32[]{:S(2)}, u32[]{:S(2)}) collective-permute-start(bf16[512,4096]{1,0:T(8,128)(2,1)} %shard_map.73), channel_id=1, source_target_pairs={{0,1},{1,0},{2,3},{3,2},{4,5},{5,4},{6,7},{7,6},{8,9},{9,8},{10,11... | collective-permute-start | bytes 12582920 | tf_op jit(solution)/shard_map/ppermute | solution.py:77
  14.5 47.6 %collective-permute-start.11 = (bf16[512,256]{1,0:T(8,128)(2,1)S(1)}, bf16[512,256]{1,0:T(8,128)(2,1)S(1)}, u32[]{:S(2)}, u32[]{:S(2)}) collective-permute-start(bf16[512,256]{1,0:T(8,128)(2,1)S(1)} %get-tuple-element.51), channel_id=1, source_target_pairs={{0,2},{1,3},{2,0},{3,1},{4,6},{5,7},{6,4},{7,5},{8,10},{9,11},{10,... | collective-permute-start | bytes 786440 | tf_op jit(solution)/shard_map/ppermute | solution.py:77
  15.1 5.5 %copy-start.28 = (s32[64]{0:T(128)S(1)}, s32[64]{0:T(128)}, u32[]{:S(2)}) copy-start(s32[64]{0:T(128)} %param.9) | copy-start | bytes 772
  18.4 19.1 %copy-start.8 = (bf16[2,2,32,64]{3,2,1,0:T(8,128)(2,1)}, bf16[2,2,32,64]{3,2,1,0:T(8,128)(2,1)S(1)}, u32[]{:S(2)}) copy-start(bf16[2,2,32,64]{3,2,1,0:T(8,128)(2,1)S(1)} %get-tuple-element.60) | copy-start | bytes 49156
  18.4 19.1 %copy-start.10 = (bf16[2,2,32,64]{3,2,1,0:T(8,128)(2,1)}, bf16[2,2,32,64]{3,2,1,0:T(8,128)(2,1)S(1)}, u32[]{:S(2)}) copy-start(bf16[2,2,32,64]{3,2,1,0:T(8,128)(2,1)S(1)} %get-tuple-element.61) | copy-start | bytes 49156
  18.9 16.1 %collective-permute-start = (bf16[128,128]{1,0:T(8,128)(2,1)S(1)}, bf16[128,128]{1,0:T(8,128)(2,1)S(1)}, u32[]{:S(2)}, u32[]{:S(2)}) collective-permute-start(bf16[128,128]{1,0:T(8,128)(2,1)S(1)} %pad_maximum_fusion.7), channel_id=1, source_target_pairs={{0,2},{1,3},{2,0},{3,1},{4,6},{5,7},{6,4},{7,5},{8,10},{9,11},{10,... | collective-permute-start | bytes 98312 | tf_op jit(solution)/shard_map/ppermute | solution.py:77
  21.5 7.7 %copy-start.1 = (bf16[512,512]{1,0:T(8,128)(2,1)S(1)}, bf16[512,512]{1,0:T(8,128)(2,1)}, u32[]{:S(2)}) copy-start(bf16[512,512]{1,0:T(8,128)(2,1)} %param.11) | copy-start | bytes 1572868
  35.2 4.3 %collective-permute-start.1 = (bf16[2,128,128]{2,1,0:T(8,128)(2,1)S(1)}, bf16[2,128,128]{2,1,0:T(8,128)(2,1)S(1)}, u32[]{:S(2)}, u32[]{:S(2)}) collective-permute-start(bf16[2,128,128]{2,1,0:T(8,128)(2,1)S(1)} %get-tuple-element.45), channel_id=1, source_target_pairs={{0,12},{1,13},{2,14},{3,15},{4,0},{5,1},{6,2},{7,3},{8,4},{9,5},{1... | collective-permute-start | bytes 196616 | tf_op jit(solution)/shard_map/ppermute | solution.py:77
  39.5 5.2 %collective-permute-start.2 = (bf16[2,128,128]{2,1,0:T(8,128)(2,1)S(1)}, bf16[2,128,128]{2,1,0:T(8,128)(2,1)S(1)}, u32[]{:S(2)}, u32[]{:S(2)}) collective-permute-start(bf16[2,128,128]{2,1,0:T(8,128)(2,1)S(1)} %get-tuple-element.45), channel_id=1, source_target_pairs={{0,8},{1,9},{2,10},{3,11},{4,12},{5,13},{6,14},{7,15},{8,0},{9,1},... | collective-permute-start | bytes 196616 | tf_op jit(solution)/shard_map/ppermute | solution.py:77
  44.6 6.9 %collective-permute-start.3 = (bf16[2,128,128]{2,1,0:T(8,128)(2,1)S(1)}, bf16[2,128,128]{2,1,0:T(8,128)(2,1)S(1)}, u32[]{:S(2)}, u32[]{:S(2)}) collective-permute-start(bf16[2,128,128]{2,1,0:T(8,128)(2,1)S(1)} %get-tuple-element.45), channel_id=1, source_target_pairs={{0,4},{1,5},{2,6},{3,7},{4,8},{5,9},{6,10},{7,11},{8,12},{9,13},{1... | collective-permute-start | bytes 196616 | tf_op jit(solution)/shard_map/ppermute | solution.py:77
  51.6 6.6 %collective-permute-start.7 = (bf16[512,256]{1,0:T(8,128)(2,1)}, bf16[512,256]{1,0:T(8,128)(2,1)S(1)}, u32[]{:S(2)}, u32[]{:S(2)}) collective-permute-start(bf16[512,256]{1,0:T(8,128)(2,1)} %collective-permute-done.6), channel_id=1, source_target_pairs={{0,16},{1,17},{2,18},{3,19},{4,20},{5,21},{6,22},{7,23},{8,24},{9,... | collective-permute-start | bytes 786440 | tf_op jit(solution)/shard_map/ppermute | solution.py:77
  53.2 8.4 %collective-permute-start.8 = (bf16[512,256]{1,0:T(8,128)(2,1)}, bf16[512,256]{1,0:T(8,128)(2,1)S(1)}, u32[]{:S(2)}, u32[]{:S(2)}) collective-permute-start(bf16[512,256]{1,0:T(8,128)(2,1)} %collective-permute-done.6), channel_id=1, source_target_pairs={{0,4},{1,5},{2,6},{3,7},{4,8},{5,9},{6,10},{7,11},{8,12},{9,13},{1... | collective-permute-start | bytes 786440 | tf_op jit(solution)/shard_map/ppermute | solution.py:77
  58.3 4.7 %collective-permute-start.4 = (bf16[4,2,128,128]{3,2,1,0:T(8,128)(2,1)S(1)}, bf16[4,2,128,128]{3,2,1,0:T(8,128)(2,1)S(1)}, u32[]{:S(2)}, u32[]{:S(2)}) collective-permute-start(bf16[4,2,128,128]{3,2,1,0:T(8,128)(2,1)S(1)} %constant_dynamic-slice_fusion.2), channel_id=1, source_target_pairs={{0,1},{1,0},{2,3},{3,2},{4,5},{5,4},{6,7},{7,6},{8,9},{9,8},{10,11... | collective-permute-start | bytes 786440 | tf_op jit(solution)/shard_map/ppermute | solution.py:77
  61.6 17.5 %collective-permute-start.9 = (bf16[512,512]{1,0:T(8,128)(2,1)S(1)}, bf16[512,512]{1,0:T(8,128)(2,1)}, u32[]{:S(2)}, u32[]{:S(2)}) collective-permute-start(bf16[512,512]{1,0:T(8,128)(2,1)S(1)} %maximum_select_fusion.2), channel_id=1, source_target_pairs={{0,2},{1,3},{2,0},{3,1},{4,6},{5,7},{6,4},{7,5},{8,10},{9,11},{10,... | collective-permute-start | bytes 1572872 | tf_op jit(solution)/shard_map/ppermute | solution.py:77
  63.9 17.0 %collective-permute-start.16 = (bf16[1024,256]{1,0:T(8,128)(2,1)}, bf16[1024,256]{1,0:T(8,128)(2,1)}, u32[]{:S(2)}, u32[]{:S(2)}) collective-permute-start(bf16[1024,256]{1,0:T(8,128)(2,1)} %pad_maximum_fusion.2), channel_id=1, source_target_pairs={{0,4},{1,5},{2,6},{3,7},{4,8},{5,9},{6,10},{7,11},{8,12},{9,13},{1... | collective-permute-start | bytes 1572872 | tf_op jit(solution)/shard_map/ppermute | solution.py:77
  63.9 53.9 %collective-permute-start.17 = (bf16[512,256]{1,0:T(8,128)(2,1)S(1)}, bf16[512,256]{1,0:T(8,128)(2,1)}, u32[]{:S(2)}, u32[]{:S(2)}) collective-permute-start(bf16[512,256]{1,0:T(8,128)(2,1)S(1)} %collective-permute-done.11), channel_id=1, source_target_pairs={{0,16},{1,17},{2,18},{3,19},{4,20},{5,21},{6,22},{7,23},{8,24},{9,... | collective-permute-start | bytes 786440 | tf_op jit(solution)/shard_map/ppermute | solution.py:77
  70.7 157.6 %collective-permute-start.37 = (bf16[256,4096]{1,0:T(8,128)(2,1)}, bf16[256,4096]{1,0:T(8,128)(2,1)}, u32[]{:S(2)}, u32[]{:S(2)}) collective-permute-start(bf16[256,4096]{1,0:T(8,128)(2,1)} %shard_map.75), channel_id=1, source_target_pairs={{0,1},{1,0},{2,3},{3,2},{4,5},{5,4},{6,7},{7,6},{8,9},{9,8},{10,11... | collective-permute-start | bytes 6291464 | tf_op jit(solution)/shard_map/ppermute | solution.py:77
  70.7 12.0 %slice-start = ((s8[4718592]{0:T(1024)(128)(4,1)}), s8[524288]{0:T(1024)(128)(4,1)S(1)}, s32[]{:S(2)}) async-start(s8[4718592]{0:T(1024)(128)(4,1)} %bitcast.194), calls=%async_computation | async-start | bytes 1048576
  77.3 5.5 %slice-start.1 = ((s8[4718592]{0:T(1024)(128)(4,1)}), s8[4194304]{0:T(1024)(128)(4,1)S(1)}, s32[]{:S(2)}) async-start(s8[4718592]{0:T(1024)(128)(4,1)} %bitcast.194), calls=%async_computation.1 | async-start | bytes 8388608
  83.7 11.1 %collective-permute-start.12 = (bf16[512,256]{1,0:T(8,128)(2,1)S(1)}, bf16[512,256]{1,0:T(8,128)(2,1)S(1)}, u32[]{:S(2)}, u32[]{:S(2)}) collective-permute-start(bf16[512,256]{1,0:T(8,128)(2,1)S(1)} %copy-done.19), channel_id=1, source_target_pairs={{0,16},{1,17},{2,18},{3,19},{4,20},{5,21},{6,22},{7,23},{8,24},{9,... | collective-permute-start | bytes 786440 | tf_op jit(solution)/shard_map/ppermute | solution.py:77
  85.2 10.5 %collective-permute-start.13 = (bf16[512,256]{1,0:T(8,128)(2,1)S(1)}, bf16[512,256]{1,0:T(8,128)(2,1)S(1)}, u32[]{:S(2)}, u32[]{:S(2)}) collective-permute-start(bf16[512,256]{1,0:T(8,128)(2,1)S(1)} %copy-done.19), channel_id=1, source_target_pairs={{0,4},{1,5},{2,6},{3,7},{4,8},{5,9},{6,10},{7,11},{8,12},{9,13},{1... | collective-permute-start | bytes 786440 | tf_op jit(solution)/shard_map/ppermute | solution.py:77
  95.7 25.6 %collective-permute-start.25 = (bf16[1024,256]{1,0:T(8,128)(2,1)}, bf16[1024,256]{1,0:T(8,128)(2,1)}, u32[]{:S(2)}, u32[]{:S(2)}) collective-permute-start(bf16[1024,256]{1,0:T(8,128)(2,1)} %collective-permute-done.16), channel_id=1, source_target_pairs={{0,4},{1,5},{2,6},{3,7},{4,8},{5,9},{6,10},{7,11},{8,12},{9,13},{1... | collective-permute-start | bytes 1572872 | tf_op jit(solution)/shard_map/ppermute | solution.py:77
  96.8 38.3 %collective-permute-start.27 = (bf16[1024,256]{1,0:T(8,128)(2,1)}, bf16[1024,256]{1,0:T(8,128)(2,1)S(1)}, u32[]{:S(2)}, u32[]{:S(2)}) collective-permute-start(bf16[1024,256]{1,0:T(8,128)(2,1)} %collective-permute-done.16), channel_id=1, source_target_pairs={{0,16},{1,17},{2,18},{3,19},{4,20},{5,21},{6,22},{7,23},{8,24},{9,... | collective-permute-start | bytes 1572872 | tf_op jit(solution)/shard_map/ppermute | solution.py:77
  98.0 18.1 %collective-permute-start.15 = (bf16[512,256]{1,0:T(8,128)(2,1)S(1)}, bf16[512,256]{1,0:T(8,128)(2,1)S(1)}, u32[]{:S(2)}, u32[]{:S(2)}) collective-permute-start(bf16[512,256]{1,0:T(8,128)(2,1)S(1)} %collective-permute-done.13), channel_id=1, source_target_pairs={{0,16},{1,17},{2,18},{3,19},{4,20},{5,21},{6,22},{7,23},{8,24},{9,... | collective-permute-start | bytes 786440 | tf_op jit(solution)/shard_map/ppermute | solution.py:77
  116.1 14.9 %collective-permute-start.14 = (bf16[512,512]{1,0:T(8,128)(2,1)S(1)}, bf16[512,512]{1,0:T(8,128)(2,1)S(1)}, u32[]{:S(2)}, u32[]{:S(2)}) collective-permute-start(bf16[512,512]{1,0:T(8,128)(2,1)S(1)} %maximum_select_fusion.3), channel_id=1, source_target_pairs={{0,2},{1,3},{2,0},{3,1},{4,6},{5,7},{6,4},{7,5},{8,10},{9,11},{10,... | collective-permute-start | bytes 1572872 | tf_op jit(solution)/shard_map/ppermute | solution.py:77
  117.8 22.7 %collective-permute-start.18 = (bf16[512,512]{1,0:T(8,128)(2,1)S(1)}, bf16[512,512]{1,0:T(8,128)(2,1)S(1)}, u32[]{:S(2)}, u32[]{:S(2)}) collective-permute-start(bf16[512,512]{1,0:T(8,128)(2,1)S(1)} %maximum_select_fusion.4), channel_id=1, source_target_pairs={{0,2},{1,3},{2,0},{3,1},{4,6},{5,7},{6,4},{7,5},{8,10},{9,11},{10,... | collective-permute-start | bytes 1572872 | tf_op jit(solution)/shard_map/ppermute | solution.py:77
  121.3 23.5 %collective-permute-start.26 = (bf16[1024,256]{1,0:T(8,128)(2,1)}, bf16[1024,256]{1,0:T(8,128)(2,1)}, u32[]{:S(2)}, u32[]{:S(2)}) collective-permute-start(bf16[1024,256]{1,0:T(8,128)(2,1)} %collective-permute-done.25), channel_id=1, source_target_pairs={{0,4},{1,5},{2,6},{3,7},{4,8},{5,9},{6,10},{7,11},{8,12},{9,13},{1... | collective-permute-start | bytes 1572872 | tf_op jit(solution)/shard_map/ppermute | solution.py:77
  131.0 21.9 %collective-permute-start.28 = (bf16[1024,256]{1,0:T(8,128)(2,1)}, bf16[1024,256]{1,0:T(8,128)(2,1)}, u32[]{:S(2)}, u32[]{:S(2)}) collective-permute-start(bf16[1024,256]{1,0:T(8,128)(2,1)} %collective-permute-done.25), channel_id=1, source_target_pairs={{0,16},{1,17},{2,18},{3,19},{4,20},{5,21},{6,22},{7,23},{8,24},{9,... | collective-permute-start | bytes 1572872 | tf_op jit(solution)/shard_map/ppermute | solution.py:77
  141.5 28.3 %collective-permute-start.20 = (f32[576,512]{1,0:T(8,128)S(1)}, f32[576,512]{1,0:T(8,128)}, u32[]{:S(2)}, u32[]{:S(2)}) collective-permute-start(f32[576,512]{1,0:T(8,128)S(1)} %fusion.8), channel_id=1, source_target_pairs={{0,1},{1,0},{2,3},{3,2},{4,5},{5,4},{6,7},{7,6},{8,9},{9,8},{10,11... | collective-permute-start | bytes 3538952 | tf_op jit(solution)/shard_map/ppermute | solution.py:77
  144.8 14.6 %collective-permute-start.29 = (bf16[1024,256]{1,0:T(8,128)(2,1)}, bf16[1024,256]{1,0:T(8,128)(2,1)}, u32[]{:S(2)}, u32[]{:S(2)}) collective-permute-start(bf16[1024,256]{1,0:T(8,128)(2,1)} %collective-permute-done.26), channel_id=1, source_target_pairs={{0,16},{1,17},{2,18},{3,19},{4,20},{5,21},{6,22},{7,23},{8,24},{9,... | collective-permute-start | bytes 1572872 | tf_op jit(solution)/shard_map/ppermute | solution.py:77
  154.8 6.6 %copy-start.12 = (f32[576,256]{1,0:T(8,128)S(1)}, f32[576,256]{1,0:T(8,128)}, u32[]{:S(2)}) copy-start(f32[576,256]{1,0:T(8,128)} %fusion.52) | copy-start | bytes 1769476
  163.2 6.0 %collective-permute-start.35 = (f32[64,512]{1,0:T(8,128)S(1)}, f32[64,512]{1,0:T(8,128)S(1)}, u32[]{:S(2)}, u32[]{:S(2)}) collective-permute-start(f32[64,512]{1,0:T(8,128)S(1)} %maximum_select_fusion.5), channel_id=1, source_target_pairs={{0,1},{1,0},{2,3},{3,2},{4,5},{5,4},{6,7},{7,6},{8,9},{9,8},{10,11... | collective-permute-start | bytes 393224 | tf_op jit(solution)/shard_map/ppermute | solution.py:77
  165.2 4.7 %copy-start.2 = (f32[512,512]{1,0:T(8,128)S(1)}, f32[512,512]{1,0:T(8,128)}, u32[]{:S(2)}) copy-start(f32[512,512]{1,0:T(8,128)} %fusion.94) | copy-start | bytes 3145732
  169.8 6.2 %copy-start.23 = (f32[2,64]{1,0:T(2,128)S(1)}, f32[2,64]{1,0:T(2,128)}, u32[]{:S(2)}) copy-start(f32[2,64]{1,0:T(2,128)} %copy-done.22) | copy-start | bytes 1540
  169.8 6.2 %copy-start.25 = (f32[2,64]{1,0:T(2,128)S(1)}, f32[2,64]{1,0:T(2,128)}, u32[]{:S(2)}) copy-start(f32[2,64]{1,0:T(2,128)} %copy-done.24) | copy-start | bytes 1540
  169.8 6.5 %copy-start.20 = (f32[2,2,32,128]{3,2,0,1:T(8,128)S(1)}, f32[2,2,32,128]{3,2,0,1:T(8,128)}, u32[]{:S(2)}) copy-start(f32[2,2,32,128]{3,2,0,1:T(8,128)} %convert_bitcast_fusion) | copy-start | bytes 196612
  169.8 7.1 %copy-start.9 = (bf16[2,2,32,64]{3,2,1,0:T(8,128)(2,1)S(1)}, bf16[2,2,32,64]{3,2,1,0:T(8,128)(2,1)}, u32[]{:S(2)}) copy-start(bf16[2,2,32,64]{3,2,1,0:T(8,128)(2,1)} %copy-done.8) | copy-start | bytes 49156
  169.8 7.1 %copy-start.11 = (bf16[2,2,32,64]{3,2,1,0:T(8,128)(2,1)S(1)}, bf16[2,2,32,64]{3,2,1,0:T(8,128)(2,1)}, u32[]{:S(2)}) copy-start(bf16[2,2,32,64]{3,2,1,0:T(8,128)(2,1)} %copy-done.10) | copy-start | bytes 49156
  173.8 3.9 %collective-permute-start.19 = (f32[512,512]{1,0:T(8,128)S(1)}, f32[512,512]{1,0:T(8,128)S(1)}, u32[]{:S(2)}, u32[]{:S(2)}) collective-permute-start(f32[512,512]{1,0:T(8,128)S(1)} %get-tuple-element.77), channel_id=1, source_target_pairs={{0,1},{1,0},{2,3},{3,2},{4,5},{5,4},{6,7},{7,6},{8,9},{9,8},{10,11... | collective-permute-start | bytes 3145736 | tf_op jit(solution)/shard_map/ppermute | solution.py:77
  188.4 6.1 %copy-start.15 = (bf16[512,2,128]{2,0,1:T(8,128)(2,1)S(1)}, bf16[512,2,128]{2,0,1:T(8,128)(2,1)}, u32[]{:S(2)}) copy-start(bf16[512,2,128]{2,0,1:T(8,128)(2,1)} %copy.69) | copy-start | bytes 786436
  188.4 6.1 %copy-start.16 = (bf16[512,2,128]{2,0,1:T(8,128)(2,1)S(1)}, bf16[512,2,128]{2,0,1:T(8,128)(2,1)}, u32[]{:S(2)}) copy-start(bf16[512,2,128]{2,0,1:T(8,128)(2,1)} %get-tuple-element.80) | copy-start | bytes 786436
  188.4 6.1 %copy-start.17 = (bf16[512,2,128]{2,0,1:T(8,128)(2,1)S(1)}, bf16[512,2,128]{2,0,1:T(8,128)(2,1)}, u32[]{:S(2)}) copy-start(bf16[512,2,128]{2,0,1:T(8,128)(2,1)} %get-tuple-element.81) | copy-start | bytes 786436
  192.9 9.3 %collective-permute-start.21 = (f32[2,4,2,2,128]{4,3,2,1,0:T(2,128)S(1)}, f32[2,4,2,2,128]{4,3,2,1,0:T(2,128)S(1)}, u32[]{:S(2)}, u32[]{:S(2)}) collective-permute-start(f32[2,4,2,2,128]{4,3,2,1,0:T(2,128)S(1)} %constant_dynamic-update-slice_fusion), channel_id=1, source_target_pairs={{0,2},{1,3},{2,0},{3,1},{4,6},{5,7},{6,4},{7,5},{8,10},{9,11},{10,... | collective-permute-start | bytes 49160 | tf_op jit(solution)/shard_map/ppermute | solution.py:77
  202.3 5.9 %collective-permute-start.22 = (f32[2,2,4,2,2,128]{5,4,3,2,1,0:T(2,128)S(1)}, f32[2,2,4,2,2,128]{5,4,3,2,1,0:T(2,128)S(1)}, u32[]{:S(2)}, u32[]{:S(2)}) collective-permute-start(f32[2,2,4,2,2,128]{5,4,3,2,1,0:T(2,128)S(1)} %pad_maximum_fusion.8), channel_id=1, source_target_pairs={{0,4},{1,5},{2,6},{3,7},{4,8},{5,9},{6,10},{7,11},{8,12},{9,13},{1... | collective-permute-start | bytes 98312 | tf_op jit(solution)/shard_map/ppermute | solution.py:77
  204.8 5.2 %collective-permute-start.23 = (f32[2,2,4,2,2,128]{5,4,3,2,1,0:T(2,128)S(1)}, f32[2,2,4,2,2,128]{5,4,3,2,1,0:T(2,128)S(1)}, u32[]{:S(2)}, u32[]{:S(2)}) collective-permute-start(f32[2,2,4,2,2,128]{5,4,3,2,1,0:T(2,128)S(1)} %pad_maximum_fusion.8), channel_id=1, source_target_pairs={{0,8},{1,9},{2,10},{3,11},{4,12},{5,13},{6,14},{7,15},{8,0},{9,1},... | collective-permute-start | bytes 98312 | tf_op jit(solution)/shard_map/ppermute | solution.py:77
  205.0 5.0 %collective-permute-start.24 = (f32[2,2,4,2,2,128]{5,4,3,2,1,0:T(2,128)S(1)}, f32[2,2,4,2,2,128]{5,4,3,2,1,0:T(2,128)S(1)}, u32[]{:S(2)}, u32[]{:S(2)}) collective-permute-start(f32[2,2,4,2,2,128]{5,4,3,2,1,0:T(2,128)S(1)} %pad_maximum_fusion.8), channel_id=1, source_target_pairs={{0,12},{1,13},{2,14},{3,15},{4,0},{5,1},{6,2},{7,3},{8,4},{9,5},{1... | collective-permute-start | bytes 98312 | tf_op jit(solution)/shard_map/ppermute | solution.py:77
  210.8 3.5 %copy-start.26 = (f32[2,32]{1,0:T(2,128)S(1)}, f32[2,32]{1,0:T(2,128)}, u32[]{:S(2)}) copy-start(f32[2,32]{1,0:T(2,128)} %fusion.118) | copy-start | bytes 772
  210.8 3.5 %copy-start.27 = (f32[1,2,32]{2,0,1:T(1,128)S(1)}, f32[1,2,32]{2,0,1:T(1,128)}, u32[]{:S(2)}) copy-start(f32[1,2,32]{2,0,1:T(1,128)} %get-tuple-element.69) | copy-start | bytes 772
  211.2 16.4 %copy-start.21 = (f32[32,128]{1,0:T(8,128)S(1)}, f32[32,128]{1,0:T(8,128)}, u32[]{:S(2)}) copy-start(f32[32,128]{1,0:T(8,128)} %get-tuple-element.65) | copy-start | bytes 49156
  211.2 16.7 %copy-start = (bf16[256,4096]{1,0:T(8,128)(2,1)S(1)}, bf16[256,4096]{1,0:T(8,128)(2,1)}, u32[]{:S(2)}) copy-start(bf16[256,4096]{1,0:T(8,128)(2,1)} %shard_map.76) | copy-start | bytes 6291460
  212.0 1.7 collective-permute-start.30
  213.8 5.6 %collective-permute-start.31 = (bf16[4,128,128]{2,1,0:T(8,128)(2,1)S(1)}, bf16[4,128,128]{2,1,0:T(8,128)(2,1)S(1)}, u32[]{:S(2)}, u32[]{:S(2)}) collective-permute-start(bf16[4,128,128]{2,1,0:T(8,128)(2,1)S(1)} %fusion.105), channel_id=1, source_target_pairs={{0,2},{1,3},{2,0},{3,1},{4,6},{5,7},{6,4},{7,5},{8,10},{9,11},{10,... | collective-permute-start | bytes 393224 | tf_op jit(solution)/shard_map/ppermute | solution.py:77
  219.5 6.1 %collective-permute-start.32 = (bf16[128,128]{1,0:T(8,128)(2,1)S(1)}, bf16[128,128]{1,0:T(8,128)(2,1)S(1)}, u32[]{:S(2)}, u32[]{:S(2)}) collective-permute-start(bf16[128,128]{1,0:T(8,128)(2,1)S(1)} %get-tuple-element.55), channel_id=1, source_target_pairs={{0,4},{1,5},{2,6},{3,7},{4,8},{5,9},{6,10},{7,11},{8,12},{9,13},{1... | collective-permute-start | bytes 98312 | tf_op jit(solution)/shard_map/ppermute | solution.py:77
  220.4 5.8 %collective-permute-start.33 = (bf16[128,128]{1,0:T(8,128)(2,1)S(1)}, bf16[128,128]{1,0:T(8,128)(2,1)S(1)}, u32[]{:S(2)}, u32[]{:S(2)}) collective-permute-start(bf16[128,128]{1,0:T(8,128)(2,1)S(1)} %get-tuple-element.57), channel_id=1, source_target_pairs={{0,8},{1,9},{2,10},{3,11},{4,12},{5,13},{6,14},{7,15},{8,0},{9,1},... | collective-permute-start | bytes 98312 | tf_op jit(solution)/shard_map/ppermute | solution.py:77
  223.6 3.9 %collective-permute-start.34 = (bf16[128,128]{1,0:T(8,128)(2,1)S(1)}, bf16[128,128]{1,0:T(8,128)(2,1)S(1)}, u32[]{:S(2)}, u32[]{:S(2)}) collective-permute-start(bf16[128,128]{1,0:T(8,128)(2,1)S(1)} %get-tuple-element.56), channel_id=1, source_target_pairs={{0,12},{1,13},{2,14},{3,15},{4,0},{5,1},{6,2},{7,3},{8,4},{9,5},{1... | collective-permute-start | bytes 98312 | tf_op jit(solution)/shard_map/ppermute | solution.py:77
  227.8 1.3 collective-permute-start.36
  231.2 8.4 %collective-permute-start.38 = (bf16[64,2048]{1,0:T(8,128)(2,1)S(1)}, bf16[64,2048]{1,0:T(8,128)(2,1)S(1)}, u32[]{:S(2)}, u32[]{:S(2)}) collective-permute-start(bf16[64,2048]{1,0:T(8,128)(2,1)S(1)} %slice.499), channel_id=1, source_target_pairs={{0,2},{1,3},{2,0},{3,1},{4,6},{5,7},{6,4},{7,5},{8,10},{9,11},{10,... | collective-permute-start | bytes 786440 | tf_op jit(solution)/shard_map/ppermute | solution.py:77
  239.7 6.6 %collective-permute-start.39 = (bf16[64,512]{1,0:T(8,128)(2,1)S(1)}, bf16[64,512]{1,0:T(8,128)(2,1)S(1)}, u32[]{:S(2)}, u32[]{:S(2)}) collective-permute-start(bf16[64,512]{1,0:T(8,128)(2,1)S(1)} %get-tuple-element.52), channel_id=1, source_target_pairs={{0,4},{1,5},{2,6},{3,7},{4,8},{5,9},{6,10},{7,11},{8,12},{9,13},{1... | collective-permute-start | bytes 196616 | tf_op jit(solution)/shard_map/ppermute | solution.py:77
  240.0 7.6 %collective-permute-start.40 = (bf16[64,512]{1,0:T(8,128)(2,1)S(1)}, bf16[64,512]{1,0:T(8,128)(2,1)S(1)}, u32[]{:S(2)}, u32[]{:S(2)}) collective-permute-start(bf16[64,512]{1,0:T(8,128)(2,1)S(1)} %get-tuple-element.54), channel_id=1, source_target_pairs={{0,8},{1,9},{2,10},{3,11},{4,12},{5,13},{6,14},{7,15},{8,0},{9,1},... | collective-permute-start | bytes 196616 | tf_op jit(solution)/shard_map/ppermute | solution.py:77
  242.6 5.1 %collective-permute-start.41 = (bf16[64,512]{1,0:T(8,128)(2,1)S(1)}, bf16[64,512]{1,0:T(8,128)(2,1)S(1)}, u32[]{:S(2)}, u32[]{:S(2)}) collective-permute-start(bf16[64,512]{1,0:T(8,128)(2,1)S(1)} %get-tuple-element.53), channel_id=1, source_target_pairs={{0,12},{1,13},{2,14},{3,15},{4,0},{5,1},{6,2},{7,3},{8,4},{9,5},{1... | collective-permute-start | bytes 196616 | tf_op jit(solution)/shard_map/ppermute | solution.py:77
  (9 other events, 10.7 us)

commit v4 on v3

v4 whole, which is shorter than its diff:
```python
import jax
import jax.numpy as jnp
from jax import lax
from jax.experimental import pallas as pl
from jax.experimental.pallas import tpu as pltpu
from jax.sharding import PartitionSpec as P

D = 8192
HEAD_DIM = 128
KV_HEADS = 4
GQA = 8
PAGE = 128
PROMPT_PAGES = 64
LINE = 4

rope_base = 1000000.0


def rope_tables(position):
    half_dim = HEAD_DIM // 2
    frequency = rope_base ** (-jnp.arange(half_dim, dtype=jnp.float32) * 2.0 / HEAD_DIM)
    angles = position.astype(jnp.float32)[..., None] * frequency
    return jnp.cos(angles), jnp.sin(angles)


def turn(vector, tables):
    cosine, sine_part = tables
    half_dim = HEAD_DIM // 2
    first_half = vector[..., :half_dim]
    second_half = vector[..., half_dim:]
    return jnp.concatenate(
        [
            first_half * cosine - second_half * sine_part,
            second_half * cosine + first_half * sine_part,
        ],
        axis=-1,
    )


def finish_heads(prefix_top, prefix_total, prefix_sum, queries, new_keys, new_values):
    score_scale = queries.shape[-1] ** (-0.5)
    query_wide = queries.astype(jnp.float32)
    key_wide = new_keys.astype(jnp.float32)
    value_wide = new_values.astype(jnp.float32)
    own_score = jnp.sum(query_wide * key_wide, axis=-1) * score_scale
    back_score = jnp.sum(query_wide[1] * key_wide[0], axis=-1) * score_scale
    first_high = jnp.maximum(prefix_top[0], own_score[0])
    first_old = jnp.exp(prefix_top[0] - first_high)
    first_own = jnp.exp(own_score[0] - first_high)
    first_out = (first_old[..., None] * prefix_sum[0] + first_own[..., None] * value_wide[0]) / (
        first_old * prefix_total[0] + first_own
    )[..., None]
    second_high = jnp.maximum(jnp.maximum(prefix_top[1], own_score[1]), back_score)
    second_old = jnp.exp(prefix_top[1] - second_high)
    second_back = jnp.exp(back_score - second_high)
    second_own = jnp.exp(own_score[1] - second_high)
    second_num = (
        second_old[..., None] * prefix_sum[1]
        + second_back[..., None] * value_wide[0]
        + second_own[..., None] * value_wide[1]
    )
    second_out = second_num / (second_old * prefix_total[1] + second_back + second_own)[..., None]
    return jnp.stack([first_out, second_out]).astype(jnp.bfloat16)


def mover(groups, devices):
    deep = devices // LINE

    def move(value, step):
        pairs = []
        for g in range(groups):
            for s in range(devices):
                a, b, c = s // LINE, s // 2 % 2, s % 2
                to_g, to_a, to_b, to_c = step(g, a, b, c)
                to_s = (to_a % deep) * LINE + to_b * 2 + to_c
                pairs.append((g * devices + s, to_g * devices + to_s))
        return lax.ppermute(value, ("groups", "sample"), pairs)

    along_z = lambda v, k=1: move(v, lambda g, a, b, c: (g, a + k, b, c))
    along_y = lambda v: move(v, lambda g, a, b, c: (g, a, 1 - b, c))
    along_x = lambda v: move(v, lambda g, a, b, c: (g ^ 1, a, b, c))
    in_chip = lambda v: move(v, lambda g, a, b, c: (g, a, b, 1 - c))
    return along_z, along_y, along_x, in_chip


def after(value, done):
    return lax.optimization_barrier((value, done))[0]


VMEM_LIMIT = 48 * 1024 * 1024


def pick(source, blocks, width):
    count = blocks.shape[0]

    def body(block_ref, source_ref, out_ref, sems):
        copies = []
        for i in range(count):
            start = pl.multiple_of(block_ref[i] * width, width)
            copies.append(
                pltpu.make_async_copy(
                    source_ref.at[:, pl.ds(start, width)],
                    out_ref.at[:, pl.ds(i * width, width)],
                    sems.at[i],
                )
            )
            copies[-1].start()
        for copy in copies:
            copy.wait()

    rows = source.shape[0]
    return pl.pallas_call(
        body,
        in_specs=[pl.BlockSpec(memory_space=pltpu.SMEM), pl.BlockSpec(memory_space=pl.ANY)],
        out_specs=pl.BlockSpec(memory_space=pl.ANY),
        out_shape=jax.ShapeDtypeStruct((rows, count * width), source.dtype),
        scratch_shapes=[pltpu.SemaphoreType.DMA((count,))],
        cost_estimate=pl.CostEstimate(
            flops=0, bytes_accessed=4 * rows * count * width, transcendentals=0
        ),
    )(blocks, source)


def project(prompt, steps, got, blocks, begin, pieces, acc):
    arrays = []
    for piece in pieces:
        for array, _ in piece:
            if not any(array is held for held in arrays):
                arrays.append(array)
    width = pieces[0][0][0].shape[0] if len(pieces[0]) == 1 else pieces[0][0][0].shape[0] // 2
    columns = sum(array.shape[1] for array, _ in pieces[0])
    row_count, step_count = prompt.shape[0], steps.shape[0]
    height = 2 * row_count + step_count
    extra = [] if acc is None else [acc]

    def body(block_ref, prompt_ref, got_ref, step_ref, *refs):
        weights, held = refs[: len(arrays)], refs[-1]
        out_ref = refs[-2]
        step = pl.program_id(0)
        for i, piece in enumerate(pieces):

            @pl.when(step == i)
            def _():
                column = 0
                for array, first in piece:
                    ref = weights[[array is other for other in arrays].index(True)]
                    held[:, column : column + array.shape[1]] = ref[first : first + width, :]
                    column += array.shape[1]

        @pl.when(step == 0)
        def _():
            if acc is None:
                out_ref[...] = jnp.zeros_like(out_ref)
            else:
                out_ref[...] = refs[len(arrays)][...]

        start = 0
        for ref, rows in (
            (prompt_ref, row_count),
            (got_ref, row_count),
            (step_ref, step_count),
        ):
            out_ref[start : start + rows, :] += jnp.dot(
                ref[...], held[...], preferred_element_type=jnp.float32
            )
            start += rows

    whole = pl.BlockSpec(memory_space=pltpu.VMEM)
    return pl.pallas_call(
        body,
        grid_spec=pltpu.PrefetchScalarGridSpec(
            num_scalar_prefetch=1,
            grid=(len(pieces),),
            in_specs=[
                pl.BlockSpec((row_count, width), lambda i, ref: (0, ref[i])),
                pl.BlockSpec((row_count, width), lambda i, ref: (0, begin + i)),
                pl.BlockSpec((step_count, width), lambda i, ref: (0, ref[i])),
            ]
            + [whole] * (len(arrays) + len(extra)),
            out_specs=pl.BlockSpec((height, columns), lambda i, ref: (0, 0)),
            scratch_shapes=[pltpu.VMEM((width, columns), jnp.bfloat16)],
        ),
        out_shape=jax.ShapeDtypeStruct((height, columns), jnp.float32),
        compiler_params=pltpu.CompilerParams(vmem_limit_bytes=VMEM_LIMIT),
        cost_estimate=pl.CostEstimate(
            flops=2 * height * width * len(pieces) * columns,
            bytes_accessed=2 * height * width * len(pieces) + 8 * height * columns,
            transcendentals=0,
        ),
    )(blocks, prompt, got, steps, *arrays, *extra)


def attend(places, queries, own, other, cosine, sine, token_prompt, row_prompt):
    kv_heads, count, _ = queries.shape
    tokens = cosine.shape[0]
    half = tokens // 2
    height = own.shape[0]
    masks = [] if token_prompt is None else [token_prompt, row_prompt]

    def body(place_ref, query_ref, own_ref, other_ref, cosine_ref, sine_ref, *refs):
        weight_ref, top_ref, total_ref = refs[-3:]
        keys = jnp.concatenate(
            [
                own_ref[:half, :] + other_ref[half:tokens, :],
                own_ref[half:tokens, :] + other_ref[:half, :],
            ],
            axis=0,
        )
        swapped = pltpu.roll(keys, HEAD_DIM // 2, 1)
        keys = (keys * cosine_ref[...] + swapped * sine_ref[...]).astype(jnp.bfloat16)
        scores = lax.dot_general(
            keys, query_ref[0], (((1,), (1,)), ((), ())), preferred_element_type=jnp.float32
        ) * (HEAD_DIM**-0.5)
        if masks:
            scores = jnp.where(refs[0][...] == refs[1][...], scores, -1e30)
        top = jnp.max(scores, axis=0, keepdims=True)
        weights = jnp.exp(scores - top)
        top_ref[0] = top
        total_ref[0] = jnp.sum(weights, axis=0, keepdims=True)
        weight_ref[0] = weights.astype(jnp.bfloat16)

    row = jax.ShapeDtypeStruct((kv_heads, 1, count), jnp.float32)
    row_spec = pl.BlockSpec((1, 1, count), lambda j, ref: (j, 0, 0))
    fixed = lambda j, ref: (0, 0)
    return pl.pallas_call(
        body,
        grid_spec=pltpu.PrefetchScalarGridSpec(
            num_scalar_prefetch=1,
            grid=(kv_heads,),
            in_specs=[
                pl.BlockSpec((1, count, HEAD_DIM), lambda j, ref: (j, 0, 0)),
                pl.BlockSpec((height, HEAD_DIM), lambda j, ref: (0, ref[j])),
                pl.BlockSpec((height, HEAD_DIM), lambda j, ref: (0, ref[j])),
                pl.BlockSpec((tokens, HEAD_DIM), fixed),
                pl.BlockSpec((tokens, HEAD_DIM), fixed),
            ]
            + [pl.BlockSpec(mask.shape, fixed) for mask in masks],
            out_specs=[
                pl.BlockSpec((1, tokens, count), lambda j, ref: (j, 0, 0)),
                row_spec,
                row_spec,
            ],
        ),
        out_shape=[
            jax.ShapeDtypeStruct((kv_heads, tokens, count), jnp.bfloat16),
            row,
            row,
        ],
        compiler_params=pltpu.CompilerParams(vmem_limit_bytes=VMEM_LIMIT),
        cost_estimate=pl.CostEstimate(
            flops=2 * kv_heads * tokens * count * HEAD_DIM,
            bytes_accessed=8 * height * kv_heads * HEAD_DIM + 2 * kv_heads * tokens * count,
            transcendentals=kv_heads * tokens * count,
        ),
    )(places, queries, own, other, cosine, sine, *masks)


def apply_weights(places, weights, values, factor):
    kv_heads, tokens, count = weights.shape

    def body(place_ref, weight_ref, value_ref, factor_ref, out_ref):
        summed = lax.dot_general(
            value_ref[:tokens, :].astype(jnp.bfloat16),
            weight_ref[0],
            (((0,), (0,)), ((), ())),
            preferred_element_type=jnp.float32,
        )
        out_ref[0] = (summed * factor_ref[0]).T.astype(jnp.bfloat16)

    return pl.pallas_call(
        body,
        grid_spec=pltpu.PrefetchScalarGridSpec(
            num_scalar_prefetch=1,
            grid=(kv_heads,),
            in_specs=[
                pl.BlockSpec((1, tokens, count), lambda j, ref: (j, 0, 0)),
                pl.BlockSpec((values.shape[0], HEAD_DIM), lambda j, ref: (0, ref[j])),
                pl.BlockSpec((1, 1, count), lambda j, ref: (j, 0, 0)),
            ],
            out_specs=pl.BlockSpec((1, count, HEAD_DIM), lambda j, ref: (j, 0, 0)),
        ),
        out_shape=jax.ShapeDtypeStruct((kv_heads, count, HEAD_DIM), jnp.bfloat16),
        compiler_params=pltpu.CompilerParams(vmem_limit_bytes=VMEM_LIMIT),
        cost_estimate=pl.CostEstimate(
            flops=2 * kv_heads * tokens * count * HEAD_DIM,
            bytes_accessed=2 * kv_heads * tokens * count,
            transcendentals=0,
        ),
    )(places, weights, values, factor)


def out_project(blocks, heads, weight, width):
    def body(block_ref, head_ref, weight_ref, out_ref):
        for i in range(blocks.shape[0]):
            start = pl.multiple_of(block_ref[i] * width, width)
            out_ref[:, i * width : (i + 1) * width] = jnp.dot(
                head_ref[...], weight_ref[:, pl.ds(start, width)], preferred_element_type=jnp.float32
            ).astype(jnp.bfloat16)

    whole = pl.BlockSpec(memory_space=pltpu.VMEM)
    shape = (heads.shape[0], weight.shape[1])
    return pl.pallas_call(
        body,
        in_specs=[pl.BlockSpec(memory_space=pltpu.SMEM), whole, whole],
        out_specs=whole,
        out_shape=jax.ShapeDtypeStruct(shape, jnp.bfloat16),
        compiler_params=pltpu.CompilerParams(vmem_limit_bytes=VMEM_LIMIT),
        cost_estimate=pl.CostEstimate(
            flops=2 * heads.shape[1] * shape[0] * shape[1],
            bytes_accessed=2 * (weight.size + heads.size + shape[0] * shape[1]),
            transcendentals=0,
        ),
    )(blocks, heads, weight)


def on_device(
    prompt_states,
    page_table,
    step_states,
    sample_order,
    key_weight,
    value_weight,
    query_weight,
    out_weight,
):
    devices = lax.axis_size("sample")
    groups = lax.axis_size("groups")
    own_index = lax.axis_index("sample")
    first = lax.axis_index("groups") % 2 == 0
    deep = devices // LINE
    own_a, own_b, own_c = own_index // LINE, own_index // 2 % 2, own_index % 2
    along_z, along_y, along_x, in_chip = mover(groups, devices)
    row_count = prompt_states.shape[0]
    chip_rows = 2 * row_count
    pages_here = row_count // PAGE
    heads_here = query_weight.shape[1] // HEAD_DIM
    total_pages = page_table.shape[0]
    prompts = total_pages // PROMPT_PAGES
    samples = sample_order.shape[0]
    steps = 2 * samples
    group_size = samples // prompts
    own_kv = own_index * heads_here // GQA
    wide_states = step_states.reshape(steps, D)
    rows = heads_here * steps
    width = key_weight.shape[0]
    half = key_weight.shape[1] // 2
    kv_places = jnp.where(first, 0, KV_HEADS // 2) + jnp.arange(KV_HEADS, dtype=jnp.int32)
    kv_places = kv_places % KV_HEADS

    def block(turn_z, flip, core):
        return ((own_a + deep + turn_z) % deep) * LINE + (own_b ^ flip) * 2 + core

    def halves(weight):
        low, high = weight[:, :half], weight[:, half:]
        return jnp.where(first, low, high), jnp.where(first, high, low)

    key_mine, key_other = halves(key_weight)
    value_mine, value_other = halves(value_weight)

    places = [(k, flip) for k in range(deep) for flip in (0, 1)]
    own_blocks = jnp.stack([block(-k, flip, own_c) for k, flip in places])
    sent_blocks = jnp.stack([block(-k, flip, 1 - own_c) for k, flip in places])
    sent = pick(prompt_states, after(sent_blocks, (key_mine, value_mine)), width)
    got = in_chip(sent)
    done = {0: [got]}

    def send(move, value, turn_at):
        if turn_at > 1:
            value = after(value, done[turn_at - 2])
        done.setdefault(turn_at, []).append(move(value))
        return done[turn_at][-1]

    step_place = PROMPT_PAGES * PAGE + jnp.arange(2, dtype=jnp.int32)
    step_tables = tuple(t[:, None, :] for t in rope_tables(step_place))
    queries = jnp.dot(after(wide_states, sent), query_weight, preferred_element_type=jnp.float32)
    queries = queries.reshape(2, samples, heads_here, HEAD_DIM).transpose(2, 0, 1, 3)
    queries = turn(queries, step_tables).astype(jnp.bfloat16)
    flat_queries = queries.reshape(rows, HEAD_DIM)

    key_z, key_y = {0: key_mine}, {}
    key_full = {0: jnp.concatenate([key_mine, key_other], axis=1)}
    value_pairs, other_pairs = {}, {}
    ring = {}
    for r in range(2 * deep - 1):
        late = r - deep + 2
        if r + 1 < deep:
            key_z[r + 1] = send(along_z, key_z[r], r)
        elif late < deep:
            value_pairs[late] = send(along_z, value_pairs[late - 1], r)
        if r == 0:
            value_y = send(along_y, value_mine, r)
            value_pairs[0] = jnp.concatenate([value_mine, value_y])
        elif r == 1:
            key_y[0] = send(along_y, key_full[0], r)
            pair_queries = jnp.stack([flat_queries, send(along_y, flat_queries, r)])
        if 0 < r < deep:
            key_full[r] = jnp.concatenate([key_z[r], send(along_x, key_z[r], r)], axis=1)
        elif r:
            other_pairs[late - 1] = send(along_x, value_pairs[late - 1], r)
        if r == deep - 1:
            other_pairs[0] = jnp.concatenate([value_other, send(along_x, value_y, r)])
        if 0 < late < deep:
            key_y[late] = send(along_y, key_full[late], r)
        if 1 < r <= deep:
            ring[r - 1] = send(lambda v: along_z(v, deep - r + 1), pair_queries, r)
    ring = [pair_queries] + [ring[j] for j in range(1, deep)]
    line = lax.dynamic_slice_in_dim(jnp.stack(ring + ring), deep - own_a, deep)
    all_queries = jnp.stack([line, in_chip(line)], axis=1)
    by_owner = (deep, 2, 2, rows)
    all_queries = all_queries.reshape(KV_HEADS, -1, HEAD_DIM)

    own_pages = jnp.concatenate(
        [
            holder * pages_here + jnp.arange(pages_here, dtype=jnp.int32)
            for holder in (own_index, own_index ^ 1)
        ]
    )
    slots = jnp.sum(
        jnp.where(
            page_table[None, :] == own_pages[:, None],
            jnp.arange(total_pages, dtype=jnp.int32)[None, :],
            0,
        ),
        axis=1,
    )
    positions = (slots % PROMPT_PAGES * PAGE)[:, None] + jnp.arange(PAGE, dtype=jnp.int32)[None, :]
    cosine, sine_part = rope_tables(positions.reshape(chip_rows))
    cosine = jnp.concatenate([cosine, cosine], axis=1)
    sine_part = jnp.concatenate([-sine_part, sine_part], axis=1)

    def pieces_of(k_range, key):
        if key:
            return [[((key_y if flip else key_full)[k], 0)] for k in k_range for flip in (0, 1)]
        return [
            [(value_pairs[k], flip * width), (other_pairs[k], flip * width)]
            for k in k_range
            for flip in (0, 1)
        ]

    def project_all(key):
        split = 2 * (deep - 1)
        early = project(
            prompt_states, wide_states, got, own_blocks[:split], 0,
            pieces_of(range(deep - 1), key), None,
        )
        return project(
            prompt_states, wide_states, got, own_blocks[split:], split,
            pieces_of([deep - 1], key), early,
        )

    key_sum = project_all(True)
    key_back = in_chip(key_sum)
    own_place = lax.dynamic_index_in_dim(kv_places, own_kv, 0, False) * HEAD_DIM

    def own_head(sums):
        return lax.dynamic_slice_in_dim(sums, own_place, HEAD_DIM, 1).reshape(2, samples, HEAD_DIM)

    new_keys = own_head(key_sum[chip_rows:]) + own_head(key_back[chip_rows:])
    new_keys = turn(new_keys, step_tables).astype(jnp.bfloat16)
    masks = (None, None)
    if prompts > 1:
        token_prompt = jnp.repeat(slots // PROMPT_PAGES, PAGE)
        row_prompt = jnp.tile(sample_order // group_size, all_queries.shape[1] // samples)
        masks = (token_prompt[:, None], row_prompt[None, :])
    weights, top, total = attend(
        kv_places, all_queries, key_sum, key_back, cosine, sine_part, *masks
    )

    stats = jnp.stack([top.reshape(by_owner), total.reshape(by_owner)])
    stats = jnp.stack([stats, along_y(stats)[:, :, :, ::-1]])
    stats = jnp.concatenate([stats] + [along_z(stats, k) for k in range(1, deep)])
    prefix_top = jnp.max(stats[:, 0], axis=0)
    prefix_total = jnp.sum(jnp.exp(stats[:, 0] - prefix_top) * stats[:, 1], axis=0)
    factor = jnp.exp(top.reshape(by_owner) - prefix_top).reshape(top.shape)
    prefix_top = lax.dynamic_index_in_dim(prefix_top, own_a, 0, False)[0, 0]
    prefix_total = lax.dynamic_index_in_dim(prefix_total, own_a, 0, False)[0, 0]

    value_sum = project_all(False)
    step_values = own_head(value_sum[chip_rows:])
    step_back = lax.dynamic_slice_in_dim(
        in_chip(value_sum[chip_rows:]), own_place, HEAD_DIM, 1
    ).reshape(step_values.shape)
    new_values = (step_values + step_back).astype(jnp.bfloat16)
    partial = apply_weights(kv_places, weights, value_sum, factor)
    partial = partial.reshape(by_owner + (HEAD_DIM,))

    def narrow(value):
        return value.astype(jnp.bfloat16)

    def wide(value):
        return value.astype(jnp.float32)

    partial = narrow(wide(partial[:, 0]) + wide(in_chip(partial[:, 1])))
    partial = narrow(wide(partial[:, 0]) + wide(along_y(partial[:, 1])))
    prefix_sum = wide(lax.dynamic_index_in_dim(partial, own_a, 0, False))
    for k in range(1, deep):
        piece = lax.dynamic_index_in_dim(partial, (own_a + k) % deep, 0, False)
        prefix_sum = prefix_sum + wide(along_z(piece, k))

    by_head = (heads_here, 2, samples)
    head_out = finish_heads(
        prefix_top.reshape(by_head).swapaxes(0, 1),
        prefix_total.reshape(by_head).swapaxes(0, 1),
        prefix_sum.reshape(by_head + (HEAD_DIM,)).swapaxes(0, 1),
        queries.swapaxes(0, 1),
        new_keys[:, None],
        new_values[:, None],
    )
    flat_heads = head_out.transpose(0, 2, 1, 3).reshape(steps, heads_here * HEAD_DIM)

    out_width = out_weight.shape[1] // devices
    out_blocks = jnp.stack(
        [
            block(k, flip, own_c ^ turned)
            for turned in (0, 1)
            for flip in (0, 1)
            for k in range(deep)
        ]
    )
    terms = out_project(out_blocks, flat_heads, out_weight, out_width)
    for move in (in_chip, along_y):
        share = terms.shape[1] // 2
        terms = narrow(wide(terms[:, :share]) + wide(move(terms[:, share:])))
    attn_out = wide(terms[:, :out_width])
    for k in range(1, deep):
        attn_out = attn_out + wide(along_z(terms[:, k * out_width : (k + 1) * out_width], k))
    return narrow(attn_out).reshape(2, samples, -1)


def solution(mesh):
    in_specs = (
        P(("groups", "sample"), None),
        P("groups"),
        P(None, "groups", None),
        P("groups"),
        P("sample", None),
        P("sample", None),
        P(None, "sample"),
        P("sample", None),
    )
    out_specs = P(None, "groups", "sample")
    return jax.shard_map(
        on_device, mesh=mesh, in_specs=in_specs, out_specs=out_specs, check_vma=False
    )
```

time: 250 us -> 320 us (1.28)
  Pallas kernels: 28 us -> 169 us
  matrix products: 74.8 us -> 2.98 us
  waiting for transfers between devices: 63.4 us -> 82.5 us
  starting transfers between devices: 45.3 us -> 33.8 us
  other arithmetic: 19.3 us -> 12.1 us
    pallas_call x4 -> x8, Pallas kernels: 28 us -> 169 us  [the longest x1 129 us: pick(): pl.pallas_call(body, in_specs=[pl.BlockSpec(memory_space=pltpu.SMEM), pl....]
    dot_general x36 -> x0, matrix products: 71.8 us -> none  [the longest x8 21.7 us: on_device(): jnp.dot(columns(got, i, 1), piece, preferred_element_type=jnp.float32)]
    ppermute x42 -> x40, waiting for transfers between devices: 63.4 us -> 82.5 us  [move(): return lax.ppermute(value, ('groups', 'sample'), pairs)]
    ppermute x42 -> x40, starting transfers between devices: 45.3 us -> 33.8 us  [move(): return lax.ppermute(value, ('groups', 'sample'), pairs)]
    unnamed x74 -> x55, local copies, waits for them, and re-layouts: 2.43 us -> 12.7 us
    reduce_sum x1 -> x0, other arithmetic: 4.41 us -> none  [on_device(): total = jnp.sum(weights, axis=-1)]
  transfers between devices with their start and end apart: 42 -> 40, of which waited for: 20 -> 22; matrix products, arithmetic and copies ran while one was open for 42% -> 5% of each run, Pallas kernels for 11% -> 9%
where the time goes in v4:
time: 320 us; the launch traced here: 319 us
  Pallas kernels  169 us (53%)
  waiting for transfers between devices  82.5 us (26%)
  starting transfers between devices  33.8 us (11%)
  local copies, waits for them, and re-layouts  16.7 us (5%)
  other arithmetic  12.1 us (4%)
    pallas_call x1, Pallas kernels, pick(): pl.pallas_call(body, in_specs=[pl.BlockSpec(memory_space=pltpu.SMEM), pl....  129 us
    ppermute x40, waiting for transfers between devices, move(): return lax.ppermute(value, ('groups', 'sample'), pairs)  82.5 us
    ppermute x40, starting transfers between devices, move(): return lax.ppermute(value, ('groups', 'sample'), pairs)  33.8 us
    pallas_call x4, Pallas kernels, project(): pl.pallas_call(body, grid_spec=pltpu.PrefetchScalarGridSpec(num_scalar_pr...  27.9 us
    unnamed x55, local copies, waits for them, and re-layouts  12.7 us
    pallas_call x1, Pallas kernels, attend(): pl.pallas_call(body, grid_spec=pltpu.PrefetchScalarGridSpec(num_scalar_pr...  6.41 us
  transfers between devices with their start and end apart: 40, of which 22 were waited for; matrix products, arithmetic and copies ran while one was open for 5% of the time, Pallas kernels for 9%

profile of v4, /device:TPU:0, one launch (start us, length us, event | category | flops | bytes accessed | tf_op | source)
XLA Modules:
  0.0 318.7 jit_solution(18038613230479984289)
XLA Ops:
  0.0 1.1 broadcast_select_fusion
  1.1 1.1 broadcast_select_fusion.1
  2.7 129.0 %shard_map.73 = bf16[512,4096]{1,0:T(8,128)(2,1)} custom-call(s32[8]{0:T(128)} %stack.180.block_ref, bf16[512,8192]{1,0:T(8,128)(2,1)} %prompt_ref.7), custom_call_target="tpu_custom_call" | custom-call | bytes 8388608 | tf_op jit(solution)/shard_map/pallas_call | solution.py:112
  132.3 2.6 collective-permute-start.3
  134.9 1.6 collective-permute-start.2
  136.5 3.0 fusion.39
  140.5 1.6 collective-permute-start.6
  142.4 1.9 fusion.2
  144.3 1.3 pad_maximum_fusion.3
  145.6 1.6 collective-permute-start.5
  147.2 0.7 convert_bitcast_fusion
  147.9 1.5 collective-permute-start.7
  149.4 1.5 bitcast_dynamic-update-slice_fusion.6
  150.9 1.0 pad_maximum_fusion.2.refs_0_
  151.9 3.4 %collective-permute-done.5 = bf16[512,256]{1,0:T(8,128)(2,1)} collective-permute-done((bf16[512,256]{1,0:T(8,128)(2,1)}, bf16[512,256]{1,0:T(8,128)(2,1)}, u32[]{:S(2)}, u32[]{:S(2)}) %collective-permute-start.5) | collective-permute-done | bytes 262176 | tf_op jit(solution)/shard_map/ppermute | solution.py:77
  155.3 1.5 collective-permute-start.10
  156.8 1.0 constant_dynamic-update-slice_fusion.3
  157.8 1.4 collective-permute-start.14
  160.3 1.0 constant_dynamic-update-slice_fusion.5
  161.3 7.0 %collective-permute-done.9 = bf16[512,256]{1,0:T(8,128)(2,1)} collective-permute-done((bf16[512,256]{1,0:T(8,128)(2,1)}, bf16[512,256]{1,0:T(8,128)(2,1)}, u32[]{:S(2)}, u32[]{:S(2)}) %collective-permute-start.9) | collective-permute-done | bytes 262176 | tf_op jit(solution)/shard_map/ppermute | solution.py:77
  168.9 8.9 %collective-permute-done.4 = bf16[2,128,128]{2,1,0:T(8,128)(2,1)S(1)} collective-permute-done((bf16[2,128,128]{2,1,0:T(8,128)(2,1)S(1)}, bf16[2,128,128]{2,1,0:T(8,128)(2,1)S(1)}, u32[]{:S(2)}, u32[]{:S(2)}) %collective-permute-start.4) | collective-permute-done | bytes 65568 | tf_op jit(solution)/shard_map/ppermute | solution.py:77
  180.6 1.0 constant_dynamic-update-slice_fusion.1
  182.2 1.0 constant_dynamic-update-slice_fusion.refs_0_
  183.1 4.4 %collective-permute-done.8 = bf16[2,128,128]{2,1,0:T(8,128)(2,1)S(1)} collective-permute-done((bf16[2,128,128]{2,1,0:T(8,128)(2,1)S(1)}, bf16[2,128,128]{2,1,0:T(8,128)(2,1)S(1)}, u32[]{:S(2)}, u32[]{:S(2)}) %collective-permute-start.8) | collective-permute-done | bytes 65568 | tf_op jit(solution)/shard_map/ppermute | solution.py:77
  187.5 1.6 collective-permute-start.17
  189.2 1.0 pad_maximum_fusion.5.refs_1_
  190.2 3.1 collective-permute-done.18.refs_5_
  193.4 1.0 copy-done.10
  194.4 9.6 %shard_map.74.refs_2_ = f32[1088,512]{1,0:T(8,128)} custom-call(s32[6]{0:T(128)S(1)} %stack.198.block_ref, bf16[512,8192]{1,0:T(8,128)(2,1)} %prompt_ref.7, bf16[512,4096]{1,0:T(8,128)(2,1)} %collective-permute-done.1.got_ref, bf16[64,8192]{1,0:T(8,128)(2,1)S(1)} %bitcast.169, bf16[512,512]{1,0:T(8,128)(2,1)S(1)} %pad_maximum_fusion.refs_0_, ...), custom_call_target="tpu_custom_call" | custom-call | flops 3422552064 | bytes 11141120 | tf_op jit(solution)/shard_map/pallas_call | solution.py:169
  204.0 4.4 %shard_map.75.own_ref = f32[1088,512]{1,0:T(8,128)S(1)} custom-call(s32[2]{0:T(128)S(1)} %pad_add_fusion.block_ref, bf16[512,8192]{1,0:T(8,128)(2,1)} %prompt_ref.7, bf16[512,4096]{1,0:T(8,128)(2,1)} %collective-permute-done.1.got_ref, bf16[64,8192]{1,0:T(8,128)(2,1)S(1)} %bitcast.170, bf16[512,512]{1,0:T(8,128)(2,1)S(1)} %constant_dynamic-update-slice_fusion.refs_0_, ...), custom_call_target="tpu_custom_call" | custom-call | flops 1140850688 | bytes 6684672 | tf_op jit(solution)/shard_map/pallas_call | solution.py:169
  209.7 5.2 %collective-permute-done.11 = bf16[2,128,128]{2,1,0:T(8,128)(2,1)S(1)} collective-permute-done((bf16[2,128,128]{2,1,0:T(8,128)(2,1)S(1)}, bf16[2,128,128]{2,1,0:T(8,128)(2,1)S(1)}, u32[]{:S(2)}, u32[]{:S(2)}) %collective-permute-start.11) | collective-permute-done | bytes 65568 | tf_op jit(solution)/shard_map/ppermute | solution.py:77
  215.7 8.5 %collective-permute-done.26.refs_3_ = bf16[1024,256]{1,0:T(8,128)(2,1)S(1)} collective-permute-done((bf16[1024,256]{1,0:T(8,128)(2,1)}, bf16[1024,256]{1,0:T(8,128)(2,1)S(1)}, u32[]{:S(2)}, u32[]{:S(2)}) %collective-permute-start.26) | collective-permute-done | bytes 524320 | tf_op jit(solution)/shard_map/ppermute | solution.py:77
  224.2 6.1 %collective-permute-done.25.refs_0_ = bf16[1024,256]{1,0:T(8,128)(2,1)S(1)} collective-permute-done((bf16[1024,256]{1,0:T(8,128)(2,1)S(1)}, bf16[1024,256]{1,0:T(8,128)(2,1)S(1)}, u32[]{:S(2)}, u32[]{:S(2)}) %collective-permute-start.25) | collective-permute-done | bytes 524320 | tf_op jit(solution)/shard_map/ppermute | solution.py:77
  231.0 4.4 %collective-permute-done.28.refs_5_ = bf16[1024,256]{1,0:T(8,128)(2,1)S(1)} collective-permute-done((bf16[1024,256]{1,0:T(8,128)(2,1)S(1)}, bf16[1024,256]{1,0:T(8,128)(2,1)S(1)}, u32[]{:S(2)}, u32[]{:S(2)}) %collective-permute-start.28) | collective-permute-done | bytes 524320 | tf_op jit(solution)/shard_map/ppermute | solution.py:77
  235.4 9.5 %shard_map.77.refs_2_ = f32[1088,512]{1,0:T(8,128)} custom-call(s32[6]{0:T(128)S(1)} %stack.198.block_ref, bf16[512,8192]{1,0:T(8,128)(2,1)} %prompt_ref.7, bf16[512,4096]{1,0:T(8,128)(2,1)} %collective-permute-done.1.got_ref, bf16[64,8192]{1,0:T(8,128)(2,1)S(1)} %bitcast.171, bf16[1024,256]{1,0:T(8,128)(2,1)S(1)} %pad_maximum_fusion.2.refs_0_, ...), custom_call_target="tpu_custom_call" | custom-call | flops 3422552064 | bytes 11141120 | tf_op jit(solution)/shard_map/pallas_call | solution.py:169
  244.9 1.0 collective-permute-done.27.refs_1_
  245.9 4.4 %shard_map.78.value_ref = f32[1088,512]{1,0:T(8,128)S(1)} custom-call(s32[2]{0:T(128)S(1)} %pad_add_fusion.block_ref, bf16[512,8192]{1,0:T(8,128)(2,1)} %prompt_ref.7, bf16[512,4096]{1,0:T(8,128)(2,1)} %collective-permute-done.1.got_ref, bf16[64,8192]{1,0:T(8,128)(2,1)S(1)} %bitcast.172, bf16[1024,256]{1,0:T(8,128)(2,1)S(1)} %collective-permute-done.25.refs_0_, ...), custom_call_target="tpu_custom_call" | custom-call | flops 1140850688 | bytes 6684672 | tf_op jit(solution)/shard_map/pallas_call | solution.py:169
  250.5 0.8 copy.84
  251.4 1.4 copy-done.4
  253.3 1.6 copy-done.2
  254.9 1.6 copy-done.5
  256.5 1.0 copy-done.8
  257.6 6.4 %shard_map.76 = (bf16[4,1024,512]{2,1,0:T(8,128)(2,1)}, f32[4,1,512]{2,1,0:T(1,128)S(1)}, f32[4,1,512]{2,1,0:T(1,128)S(1)}) custom-call(s32[4]{0:T(128)S(1)} %and_select_fusion.1.place_ref, bf16[4,512,128]{2,1,0:T(8,128)(2,1)S(1)} %bitcast.173, f32[1088,512]{1,0:T(8,128)S(1)} %copy-done.2, f32[1088,512]{1,0:T(8,128)S(1)} %copy-done.5, ...), custom_call_target="tpu_custom_call" | custom-call | flops 536870912 | bytes 8650752 | tf_op jit(solution)/shard_map/pallas_call | solution.py:225
  264.9 2.9 collective-permute-done.20
  267.9 1.0 collective-permute-start.21
  268.8 3.2 %collective-permute-start.22 = (f32[2,2,4,2,2,128]{5,4,3,2,1,0:T(2,128)S(1)}, f32[2,2,4,2,2,128]{5,4,3,2,1,0:T(2,128)S(1)}, u32[]{:S(2)}, u32[]{:S(2)}) collective-permute-start(f32[2,2,4,2,2,128]{5,4,3,2,1,0:T(2,128)S(1)} %pad_maximum_fusion.8), channel_id=1, source_target_pairs={{0,8},{1,9},{2,10},{3,11},{4,12},{5,13},{6,14},{7,15},{8,0},{9,1},... | collective-permute-start | bytes 98312 | tf_op jit(solution)/shard_map/ppermute | solution.py:77
  272.0 1.9 collective-permute-done.21
  274.0 0.7 collective-permute-done.22
  274.7 1.2 collective-permute-done.23
  276.2 4.4 %shard_map.79 = bf16[4,512,128]{2,1,0:T(8,128)(2,1)S(1)} custom-call(s32[4]{0:T(128)S(1)} %and_select_fusion.1.place_ref, bf16[4,1024,512]{2,1,0:T(8,128)(2,1)} %get-tuple-element.37.weight_ref, f32[1088,512]{1,0:T(8,128)S(1)} %shard_map.78.value_ref, f32[4,1,512]{2,1,0:T(1,128)S(1)} %subtract_exponential_fusion.factor_ref), custom_call_target="tpu_custom_call" | custom-call | flops 536870912 | bytes 4194304 | tf_op jit(solution)/shard_map/pallas_call | solution.py:270
  280.9 1.4 collective-permute-done.29
  283.0 5.0 %collective-permute-done.30 = bf16[4,128,128]{2,1,0:T(8,128)(2,1)S(1)} collective-permute-done((bf16[4,128,128]{2,1,0:T(8,128)(2,1)S(1)}, bf16[4,128,128]{2,1,0:T(8,128)(2,1)S(1)}, u32[]{:S(2)}, u32[]{:S(2)}) %collective-permute-start.30) | collective-permute-done | bytes 131104 | tf_op jit(solution)/shard_map/ppermute | solution.py:77
  288.6 2.2 collective-permute-start.32
  290.9 1.1 collective-permute-start.33
  292.0 2.0 collective-permute-done.31
  294.0 0.8 collective-permute-done.33
  295.0 2.2 copy-done.3
  297.2 1.4 shard_map.80
  298.7 1.9 collective-permute-done.35
  301.4 7.8 %collective-permute-done.36 = bf16[64,2048]{1,0:T(8,128)(2,1)S(1)} collective-permute-done((bf16[64,2048]{1,0:T(8,128)(2,1)S(1)}, bf16[64,2048]{1,0:T(8,128)(2,1)S(1)}, u32[]{:S(2)}, u32[]{:S(2)}) %collective-permute-start.36) | collective-permute-done | bytes 262176 | tf_op jit(solution)/shard_map/ppermute | solution.py:77
  309.3 1.7 collective-permute-start.37
  311.0 1.8 collective-permute-start.38
  313.5 2.6 collective-permute-done.37
  316.1 1.9 collective-permute-done.38
  (163 shorter events, 15.3 us)
Async XLA Ops:
  2.7 133.7 %copy-start = (bf16[2,32,8192]{2,1,0:T(8,128)(2,1)S(1)}, bf16[2,32,8192]{2,1,0:T(8,128)(2,1)}, u32[]{:S(2)}) copy-start(bf16[2,32,8192]{2,1,0:T(8,128)(2,1)} %param.10) | copy-start | bytes 3145732
  131.8 10.4 %copy-start.19 = (s32[64]{0:T(128)S(1)}, s32[64]{0:T(128)}, u32[]{:S(2)}) copy-start(s32[64]{0:T(128)} %param.9) | copy-start | bytes 772
  131.8 23.5 %collective-permute-start.1 = (bf16[512,4096]{1,0:T(8,128)(2,1)}, bf16[512,4096]{1,0:T(8,128)(2,1)}, u32[]{:S(2)}, u32[]{:S(2)}) collective-permute-start(bf16[512,4096]{1,0:T(8,128)(2,1)} %shard_map.73), channel_id=1, source_target_pairs={{0,1},{1,0},{2,3},{3,2},{4,5},{5,4},{6,7},{7,6},{8,9},{9,8},{10,11... | collective-permute-start | bytes 12582920 | tf_op jit(solution)/shard_map/ppermute | solution.py:77
  132.3 18.6 %collective-permute-start.3 = (bf16[512,256]{1,0:T(8,128)(2,1)S(1)}, bf16[512,256]{1,0:T(8,128)(2,1)}, u32[]{:S(2)}, u32[]{:S(2)}) collective-permute-start(bf16[512,256]{1,0:T(8,128)(2,1)S(1)} %get-tuple-element.53), channel_id=1, source_target_pairs={{0,2},{1,3},{2,0},{3,1},{4,6},{5,7},{6,4},{7,5},{8,10},{9,11},{10,... | collective-permute-start | bytes 786440 | tf_op jit(solution)/shard_map/ppermute | solution.py:77
  134.9 10.7 %collective-permute-start.2 = (bf16[512,256]{1,0:T(8,128)(2,1)S(1)}, bf16[512,256]{1,0:T(8,128)(2,1)}, u32[]{:S(2)}, u32[]{:S(2)}) collective-permute-start(bf16[512,256]{1,0:T(8,128)(2,1)S(1)} %get-tuple-element.55), channel_id=1, source_target_pairs={{0,4},{1,5},{2,6},{3,7},{4,8},{5,9},{6,10},{7,11},{8,12},{9,13},{1... | collective-permute-start | bytes 786440 | tf_op jit(solution)/shard_map/ppermute | solution.py:77
  139.7 29.2 %copy-start.11 = (bf16[2,2,32,64]{3,2,1,0:T(8,128)(2,1)}, bf16[2,2,32,64]{3,2,1,0:T(8,128)(2,1)S(1)}, u32[]{:S(2)}) copy-start(bf16[2,2,32,64]{3,2,1,0:T(8,128)(2,1)S(1)} %get-tuple-element.64) | copy-start | bytes 49156
  139.8 29.2 %copy-start.13 = (bf16[2,2,32,64]{3,2,1,0:T(8,128)(2,1)}, bf16[2,2,32,64]{3,2,1,0:T(8,128)(2,1)S(1)}, u32[]{:S(2)}) copy-start(bf16[2,2,32,64]{3,2,1,0:T(8,128)(2,1)S(1)} %get-tuple-element.65) | copy-start | bytes 49156
  139.9 8.1 %collective-permute-start = (bf16[128,128]{1,0:T(8,128)(2,1)S(1)}, bf16[128,128]{1,0:T(8,128)(2,1)}, u32[]{:S(2)}, u32[]{:S(2)}) collective-permute-start(bf16[128,128]{1,0:T(8,128)(2,1)S(1)} %pad_maximum_fusion.7), channel_id=1, source_target_pairs={{0,2},{1,3},{2,0},{3,1},{4,6},{5,7},{6,4},{7,5},{8,10},{9,11},{10,... | collective-permute-start | bytes 98312 | tf_op jit(solution)/shard_map/ppermute | solution.py:77
  140.5 17.3 %collective-permute-start.6 = (bf16[512,512]{1,0:T(8,128)(2,1)S(1)}, bf16[512,512]{1,0:T(8,128)(2,1)S(1)}, u32[]{:S(2)}, u32[]{:S(2)}) collective-permute-start(bf16[512,512]{1,0:T(8,128)(2,1)S(1)} %pad_maximum_fusion.refs_0_), channel_id=1, source_target_pairs={{0,2},{1,3},{2,0},{3,1},{4,6},{5,7},{6,4},{7,5},{8,10},{9,11},{10,... | collective-permute-start | bytes 1572872 | tf_op jit(solution)/shard_map/ppermute | solution.py:77
  145.6 9.7 %collective-permute-start.5 = (bf16[512,256]{1,0:T(8,128)(2,1)}, bf16[512,256]{1,0:T(8,128)(2,1)}, u32[]{:S(2)}, u32[]{:S(2)}) collective-permute-start(bf16[512,256]{1,0:T(8,128)(2,1)} %collective-permute-done.2), channel_id=1, source_target_pairs={{0,4},{1,5},{2,6},{3,7},{4,8},{5,9},{6,10},{7,11},{8,12},{9,13},{1... | collective-permute-start | bytes 786440 | tf_op jit(solution)/shard_map/ppermute | solution.py:77
  147.9 9.9 %collective-permute-start.7 = (bf16[512,256]{1,0:T(8,128)(2,1)}, bf16[512,256]{1,0:T(8,128)(2,1)S(1)}, u32[]{:S(2)}, u32[]{:S(2)}) collective-permute-start(bf16[512,256]{1,0:T(8,128)(2,1)} %collective-permute-done.2), channel_id=1, source_target_pairs={{0,16},{1,17},{2,18},{3,19},{4,20},{5,21},{6,22},{7,23},{8,24},{9,... | collective-permute-start | bytes 786440 | tf_op jit(solution)/shard_map/ppermute | solution.py:77
  155.3 13.0 %collective-permute-start.10 = (bf16[512,256]{1,0:T(8,128)(2,1)}, bf16[512,256]{1,0:T(8,128)(2,1)S(1)}, u32[]{:S(2)}, u32[]{:S(2)}) collective-permute-start(bf16[512,256]{1,0:T(8,128)(2,1)} %collective-permute-done.5), channel_id=1, source_target_pairs={{0,16},{1,17},{2,18},{3,19},{4,20},{5,21},{6,22},{7,23},{8,24},{9,... | collective-permute-start | bytes 786440 | tf_op jit(solution)/shard_map/ppermute | solution.py:77
  156.8 11.6 %collective-permute-start.9 = (bf16[512,256]{1,0:T(8,128)(2,1)}, bf16[512,256]{1,0:T(8,128)(2,1)}, u32[]{:S(2)}, u32[]{:S(2)}) collective-permute-start(bf16[512,256]{1,0:T(8,128)(2,1)} %collective-permute-done.5), channel_id=1, source_target_pairs={{0,4},{1,5},{2,6},{3,7},{4,8},{5,9},{6,10},{7,11},{8,12},{9,13},{1... | collective-permute-start | bytes 786440 | tf_op jit(solution)/shard_map/ppermute | solution.py:77
  157.8 2.0 copy-start.9
  157.8 29.7 %collective-permute-start.14 = (bf16[1024,256]{1,0:T(8,128)(2,1)S(1)}, bf16[1024,256]{1,0:T(8,128)(2,1)}, u32[]{:S(2)}, u32[]{:S(2)}) collective-permute-start(bf16[1024,256]{1,0:T(8,128)(2,1)S(1)} %pad_maximum_fusion.2.refs_0_), channel_id=1, source_target_pairs={{0,4},{1,5},{2,6},{3,7},{4,8},{5,9},{6,10},{7,11},{8,12},{9,13},{1... | collective-permute-start | bytes 1572872 | tf_op jit(solution)/shard_map/ppermute | solution.py:77
  159.2 28.3 %collective-permute-start.16 = (bf16[512,512]{1,0:T(8,128)(2,1)S(1)}, bf16[512,512]{1,0:T(8,128)(2,1)}, u32[]{:S(2)}, u32[]{:S(2)}) collective-permute-start(bf16[512,512]{1,0:T(8,128)(2,1)S(1)} %constant_dynamic-update-slice_fusion.2.refs_2_), channel_id=1, source_target_pairs={{0,2},{1,3},{2,0},{3,1},{4,6},{5,7},{6,4},{7,5},{8,10},{9,11},{10,... | collective-permute-start | bytes 1572872 | tf_op jit(solution)/shard_map/ppermute | solution.py:77
  159.8 27.7 %collective-permute-start.15 = (bf16[512,256]{1,0:T(8,128)(2,1)}, bf16[512,256]{1,0:T(8,128)(2,1)}, u32[]{:S(2)}, u32[]{:S(2)}) collective-permute-start(bf16[512,256]{1,0:T(8,128)(2,1)} %collective-permute-done.3), channel_id=1, source_target_pairs={{0,16},{1,17},{2,18},{3,19},{4,20},{5,21},{6,22},{7,23},{8,24},{9,... | collective-permute-start | bytes 786440 | tf_op jit(solution)/shard_map/ppermute | solution.py:77
  168.3 9.5 %collective-permute-start.4 = (bf16[2,128,128]{2,1,0:T(8,128)(2,1)S(1)}, bf16[2,128,128]{2,1,0:T(8,128)(2,1)S(1)}, u32[]{:S(2)}, u32[]{:S(2)}) collective-permute-start(bf16[2,128,128]{2,1,0:T(8,128)(2,1)S(1)} %get-tuple-element.28), channel_id=1, source_target_pairs={{0,12},{1,13},{2,14},{3,15},{4,0},{5,1},{6,2},{7,3},{8,4},{9,5},{1... | collective-permute-start | bytes 196616 | tf_op jit(solution)/shard_map/ppermute | solution.py:77
  168.3 13.2 %collective-permute-start.13 = (bf16[512,256]{1,0:T(8,128)(2,1)}, bf16[512,256]{1,0:T(8,128)(2,1)}, u32[]{:S(2)}, u32[]{:S(2)}) collective-permute-start(bf16[512,256]{1,0:T(8,128)(2,1)} %collective-permute-done.9), channel_id=1, source_target_pairs={{0,16},{1,17},{2,18},{3,19},{4,20},{5,21},{6,22},{7,23},{8,24},{9,... | collective-permute-start | bytes 786440 | tf_op jit(solution)/shard_map/ppermute | solution.py:77
  177.9 0.6 copy-start.16
  178.5 14.9 %collective-permute-start.18 = (bf16[512,512]{1,0:T(8,128)(2,1)S(1)}, bf16[512,512]{1,0:T(8,128)(2,1)}, u32[]{:S(2)}, u32[]{:S(2)}) collective-permute-start(bf16[512,512]{1,0:T(8,128)(2,1)S(1)} %constant_dynamic-update-slice_fusion.4.refs_4_), channel_id=1, source_target_pairs={{0,2},{1,3},{2,0},{3,1},{4,6},{5,7},{6,4},{7,5},{8,10},{9,11},{10,... | collective-permute-start | bytes 1572872 | tf_op jit(solution)/shard_map/ppermute | solution.py:77
  181.6 6.0 %collective-permute-start.8 = (bf16[2,128,128]{2,1,0:T(8,128)(2,1)S(1)}, bf16[2,128,128]{2,1,0:T(8,128)(2,1)S(1)}, u32[]{:S(2)}, u32[]{:S(2)}) collective-permute-start(bf16[2,128,128]{2,1,0:T(8,128)(2,1)S(1)} %get-tuple-element.28), channel_id=1, source_target_pairs={{0,8},{1,9},{2,10},{3,11},{4,12},{5,13},{6,14},{7,15},{8,0},{9,1},... | collective-permute-start | bytes 196616 | tf_op jit(solution)/shard_map/ppermute | solution.py:77
  187.5 16.5 %collective-permute-start.17 = (bf16[512,512]{1,0:T(8,128)(2,1)S(1)}, bf16[512,512]{1,0:T(8,128)(2,1)S(1)}, u32[]{:S(2)}, u32[]{:S(2)}) collective-permute-start(bf16[512,512]{1,0:T(8,128)(2,1)S(1)} %constant_dynamic-update-slice_fusion.refs_0_), channel_id=1, source_target_pairs={{0,2},{1,3},{2,0},{3,1},{4,6},{5,7},{6,4},{7,5},{8,10},{9,11},{10,... | collective-permute-start | bytes 1572872 | tf_op jit(solution)/shard_map/ppermute | solution.py:77
  190.2 24.8 %collective-permute-start.24 = (bf16[1024,256]{1,0:T(8,128)(2,1)}, bf16[1024,256]{1,0:T(8,128)(2,1)S(1)}, u32[]{:S(2)}, u32[]{:S(2)}) collective-permute-start(bf16[1024,256]{1,0:T(8,128)(2,1)} %collective-permute-done.14.refs_2_), channel_id=1, source_target_pairs={{0,4},{1,5},{2,6},{3,7},{4,8},{5,9},{6,10},{7,11},{8,12},{9,13},{1... | collective-permute-start | bytes 1572872 | tf_op jit(solution)/shard_map/ppermute | solution.py:77
  193.4 1.0 copy-start.10
  204.0 4.5 %copy-start.15 = (bf16[8,2,128,128]{3,2,1,0:T(8,128)(2,1)S(1)}, bf16[8,2,128,128]{3,2,1,0:T(8,128)(2,1)}, u32[]{:S(2)}) copy-start(bf16[8,2,128,128]{3,2,1,0:T(8,128)(2,1)} %get-tuple-element.48) | copy-start | bytes 1572868
  204.0 4.5 %copy-start.17 = (bf16[2,128,128]{2,1,0:T(8,128)(2,1)S(1)}, bf16[2,128,128]{2,1,0:T(8,128)(2,1)}, u32[]{:S(2)}) copy-start(bf16[2,128,128]{2,1,0:T(8,128)(2,1)} %copy-done.16) | copy-start | bytes 196612
  208.5 42.9 %copy-start.1 = (f32[1088,512]{1,0:T(8,128)}, f32[1088,512]{1,0:T(8,128)S(1)}, u32[]{:S(2)}) copy-start(f32[1088,512]{1,0:T(8,128)S(1)} %shard_map.75.own_ref) | copy-start | bytes 6684676
  208.5 42.9 %collective-permute-start.19 = (f32[1088,512]{1,0:T(8,128)S(1)}, f32[1088,512]{1,0:T(8,128)S(1)}, u32[]{:S(2)}, u32[]{:S(2)}) collective-permute-start(f32[1088,512]{1,0:T(8,128)S(1)} %shard_map.75.own_ref), channel_id=1, source_target_pairs={{0,1},{1,0},{2,3},{3,2},{4,5},{5,4},{6,7},{7,6},{8,9},{9,8},{10,11... | collective-permute-start | bytes 6684680 | tf_op jit(solution)/shard_map/ppermute | solution.py:77
  208.6 6.3 %collective-permute-start.11 = (bf16[2,128,128]{2,1,0:T(8,128)(2,1)S(1)}, bf16[2,128,128]{2,1,0:T(8,128)(2,1)S(1)}, u32[]{:S(2)}, u32[]{:S(2)}) collective-permute-start(bf16[2,128,128]{2,1,0:T(8,128)(2,1)S(1)} %get-tuple-element.28), channel_id=1, source_target_pairs={{0,4},{1,5},{2,6},{3,7},{4,8},{5,9},{6,10},{7,11},{8,12},{9,13},{1... | collective-permute-start | bytes 196616 | tf_op jit(solution)/shard_map/ppermute | solution.py:77
  209.1 15.0 %collective-permute-start.26 = (bf16[1024,256]{1,0:T(8,128)(2,1)}, bf16[1024,256]{1,0:T(8,128)(2,1)S(1)}, u32[]{:S(2)}, u32[]{:S(2)}) collective-permute-start(bf16[1024,256]{1,0:T(8,128)(2,1)} %collective-permute-done.14.refs_2_), channel_id=1, source_target_pairs={{0,16},{1,17},{2,18},{3,19},{4,20},{5,21},{6,22},{7,23},{8,24},{9,... | collective-permute-start | bytes 1572872 | tf_op jit(solution)/shard_map/ppermute | solution.py:77
  214.9 15.4 %collective-permute-start.25 = (bf16[1024,256]{1,0:T(8,128)(2,1)S(1)}, bf16[1024,256]{1,0:T(8,128)(2,1)S(1)}, u32[]{:S(2)}, u32[]{:S(2)}) collective-permute-start(bf16[1024,256]{1,0:T(8,128)(2,1)S(1)} %collective-permute-done.24.refs_4_), channel_id=1, source_target_pairs={{0,4},{1,5},{2,6},{3,7},{4,8},{5,9},{6,10},{7,11},{8,12},{9,13},{1... | collective-permute-start | bytes 1572872 | tf_op jit(solution)/shard_map/ppermute | solution.py:77
  215.0 20.4 %collective-permute-start.28 = (bf16[1024,256]{1,0:T(8,128)(2,1)S(1)}, bf16[1024,256]{1,0:T(8,128)(2,1)S(1)}, u32[]{:S(2)}, u32[]{:S(2)}) collective-permute-start(bf16[1024,256]{1,0:T(8,128)(2,1)S(1)} %collective-permute-done.24.refs_4_), channel_id=1, source_target_pairs={{0,16},{1,17},{2,18},{3,19},{4,20},{5,21},{6,22},{7,23},{8,24},{9,... | collective-permute-start | bytes 1572872 | tf_op jit(solution)/shard_map/ppermute | solution.py:77
  230.3 15.6 %collective-permute-start.27 = (bf16[1024,256]{1,0:T(8,128)(2,1)S(1)}, bf16[1024,256]{1,0:T(8,128)(2,1)S(1)}, u32[]{:S(2)}, u32[]{:S(2)}) collective-permute-start(bf16[1024,256]{1,0:T(8,128)(2,1)S(1)} %collective-permute-done.25.refs_0_), channel_id=1, source_target_pairs={{0,16},{1,17},{2,18},{3,19},{4,20},{5,21},{6,22},{7,23},{8,24},{9,... | collective-permute-start | bytes 1572872 | tf_op jit(solution)/shard_map/ppermute | solution.py:77
  230.9 19.5 %collective-permute-start.12 = (bf16[4,2,128,128]{3,2,1,0:T(8,128)(2,1)S(1)}, bf16[4,2,128,128]{3,2,1,0:T(8,128)(2,1)S(1)}, u32[]{:S(2)}, u32[]{:S(2)}) collective-permute-start(bf16[4,2,128,128]{3,2,1,0:T(8,128)(2,1)S(1)} %constant_dynamic-slice_fusion.2), channel_id=1, source_target_pairs={{0,1},{1,0},{2,3},{3,2},{4,5},{5,4},{6,7},{7,6},{8,9},{9,8},{10,11... | collective-permute-start | bytes 786440 | tf_op jit(solution)/shard_map/ppermute | solution.py:77
  244.9 8.1 %copy-start.12 = (bf16[2,2,32,64]{3,2,1,0:T(8,128)(2,1)S(1)}, bf16[2,2,32,64]{3,2,1,0:T(8,128)(2,1)}, u32[]{:S(2)}) copy-start(bf16[2,2,32,64]{3,2,1,0:T(8,128)(2,1)} %copy-done.11) | copy-start | bytes 49156
  244.9 8.1 %copy-start.14 = (bf16[2,2,32,64]{3,2,1,0:T(8,128)(2,1)S(1)}, bf16[2,2,32,64]{3,2,1,0:T(8,128)(2,1)}, u32[]{:S(2)}) copy-start(bf16[2,2,32,64]{3,2,1,0:T(8,128)(2,1)} %copy-done.13) | copy-start | bytes 49156
  250.3 3.0 copy-start.6
  250.3 3.0 copy-start.7
  250.3 2.4 collective-permute-start.34
  250.5 14.2 %copy-start.18 = (f32[2,2,32,128]{3,2,0,1:T(8,128)S(1)}, f32[2,2,32,128]{3,2,0,1:T(8,128)}, u32[]{:S(2)}) copy-start(f32[2,2,32,128]{3,2,0,1:T(8,128)} %convert_bitcast_fusion) | copy-start | bytes 196612
  251.4 1.4 copy-start.4
  253.3 1.6 copy-start.2
  254.9 1.6 copy-start.5
  256.5 1.0 copy-start.8
  264.0 3.8 %collective-permute-start.20 = (f32[2,4,2,2,128]{4,3,2,1,0:T(2,128)S(1)}, f32[2,4,2,2,128]{4,3,2,1,0:T(2,128)S(1)}, u32[]{:S(2)}, u32[]{:S(2)}) collective-permute-start(f32[2,4,2,2,128]{4,3,2,1,0:T(2,128)S(1)} %get-tuple-element.73), channel_id=1, source_target_pairs={{0,2},{1,3},{2,0},{3,1},{4,6},{5,7},{6,4},{7,5},{8,10},{9,11},{10,... | collective-permute-start | bytes 49160 | tf_op jit(solution)/shard_map/ppermute | solution.py:77
  267.9 6.1 %collective-permute-start.21 = (f32[2,2,4,2,2,128]{5,4,3,2,1,0:T(2,128)S(1)}, f32[2,2,4,2,2,128]{5,4,3,2,1,0:T(2,128)S(1)}, u32[]{:S(2)}, u32[]{:S(2)}) collective-permute-start(f32[2,2,4,2,2,128]{5,4,3,2,1,0:T(2,128)S(1)} %pad_maximum_fusion.8), channel_id=1, source_target_pairs={{0,4},{1,5},{2,6},{3,7},{4,8},{5,9},{6,10},{7,11},{8,12},{9,13},{1... | collective-permute-start | bytes 98312 | tf_op jit(solution)/shard_map/ppermute | solution.py:77
  268.8 5.9 %collective-permute-start.22 = (f32[2,2,4,2,2,128]{5,4,3,2,1,0:T(2,128)S(1)}, f32[2,2,4,2,2,128]{5,4,3,2,1,0:T(2,128)S(1)}, u32[]{:S(2)}, u32[]{:S(2)}) collective-permute-start(f32[2,2,4,2,2,128]{5,4,3,2,1,0:T(2,128)S(1)} %pad_maximum_fusion.8), channel_id=1, source_target_pairs={{0,8},{1,9},{2,10},{3,11},{4,12},{5,13},{6,14},{7,15},{8,0},{9,1},... | collective-permute-start | bytes 98312 | tf_op jit(solution)/shard_map/ppermute | solution.py:77
  272.0 3.9 %collective-permute-start.23 = (f32[2,2,4,2,2,128]{5,4,3,2,1,0:T(2,128)S(1)}, f32[2,2,4,2,2,128]{5,4,3,2,1,0:T(2,128)S(1)}, u32[]{:S(2)}, u32[]{:S(2)}) collective-permute-start(f32[2,2,4,2,2,128]{5,4,3,2,1,0:T(2,128)S(1)} %pad_maximum_fusion.8), channel_id=1, source_target_pairs={{0,12},{1,13},{2,14},{3,15},{4,0},{5,1},{6,2},{7,3},{8,4},{9,5},{1... | collective-permute-start | bytes 98312 | tf_op jit(solution)/shard_map/ppermute | solution.py:77
  280.7 1.6 collective-permute-start.29
  282.4 5.6 %collective-permute-start.30 = (bf16[4,128,128]{2,1,0:T(8,128)(2,1)S(1)}, bf16[4,128,128]{2,1,0:T(8,128)(2,1)S(1)}, u32[]{:S(2)}, u32[]{:S(2)}) collective-permute-start(bf16[4,128,128]{2,1,0:T(8,128)(2,1)S(1)} %slice_bitcast_fusion), channel_id=1, source_target_pairs={{0,2},{1,3},{2,0},{3,1},{4,6},{5,7},{6,4},{7,5},{8,10},{9,11},{10,... | collective-permute-start | bytes 393224 | tf_op jit(solution)/shard_map/ppermute | solution.py:77
  288.1 5.9 %collective-permute-start.31 = (bf16[128,128]{1,0:T(8,128)(2,1)S(1)}, bf16[128,128]{1,0:T(8,128)(2,1)S(1)}, u32[]{:S(2)}, u32[]{:S(2)}) collective-permute-start(bf16[128,128]{1,0:T(8,128)(2,1)S(1)} %get-tuple-element.59), channel_id=1, source_target_pairs={{0,4},{1,5},{2,6},{3,7},{4,8},{5,9},{6,10},{7,11},{8,12},{9,13},{1... | collective-permute-start | bytes 98312 | tf_op jit(solution)/shard_map/ppermute | solution.py:77
  288.6 5.3 %collective-permute-start.32 = (bf16[128,128]{1,0:T(8,128)(2,1)S(1)}, bf16[128,128]{1,0:T(8,128)(2,1)S(1)}, u32[]{:S(2)}, u32[]{:S(2)}) collective-permute-start(bf16[128,128]{1,0:T(8,128)(2,1)S(1)} %get-tuple-element.61), channel_id=1, source_target_pairs={{0,8},{1,9},{2,10},{3,11},{4,12},{5,13},{6,14},{7,15},{8,0},{9,1},... | collective-permute-start | bytes 98312 | tf_op jit(solution)/shard_map/ppermute | solution.py:77
  290.9 3.9 %collective-permute-start.33 = (bf16[128,128]{1,0:T(8,128)(2,1)S(1)}, bf16[128,128]{1,0:T(8,128)(2,1)S(1)}, u32[]{:S(2)}, u32[]{:S(2)}) collective-permute-start(bf16[128,128]{1,0:T(8,128)(2,1)S(1)} %get-tuple-element.60), channel_id=1, source_target_pairs={{0,12},{1,13},{2,14},{3,15},{4,0},{5,1},{6,2},{7,3},{8,4},{9,5},{1... | collective-permute-start | bytes 98312 | tf_op jit(solution)/shard_map/ppermute | solution.py:77
  295.0 2.2 copy-start.3
  298.6 2.0 collective-permute-start.35
  300.8 8.4 %collective-permute-start.36 = (bf16[64,2048]{1,0:T(8,128)(2,1)S(1)}, bf16[64,2048]{1,0:T(8,128)(2,1)S(1)}, u32[]{:S(2)}, u32[]{:S(2)}) collective-permute-start(bf16[64,2048]{1,0:T(8,128)(2,1)S(1)} %slice.201), channel_id=1, source_target_pairs={{0,2},{1,3},{2,0},{3,1},{4,6},{5,7},{6,4},{7,5},{8,10},{9,11},{10,... | collective-permute-start | bytes 786440 | tf_op jit(solution)/shard_map/ppermute | solution.py:77
  309.3 6.8 %collective-permute-start.37 = (bf16[64,512]{1,0:T(8,128)(2,1)S(1)}, bf16[64,512]{1,0:T(8,128)(2,1)S(1)}, u32[]{:S(2)}, u32[]{:S(2)}) collective-permute-start(bf16[64,512]{1,0:T(8,128)(2,1)S(1)} %get-tuple-element.56), channel_id=1, source_target_pairs={{0,4},{1,5},{2,6},{3,7},{4,8},{5,9},{6,10},{7,11},{8,12},{9,13},{1... | collective-permute-start | bytes 196616 | tf_op jit(solution)/shard_map/ppermute | solution.py:77
  311.0 7.0 %collective-permute-start.38 = (bf16[64,512]{1,0:T(8,128)(2,1)S(1)}, bf16[64,512]{1,0:T(8,128)(2,1)S(1)}, u32[]{:S(2)}, u32[]{:S(2)}) collective-permute-start(bf16[64,512]{1,0:T(8,128)(2,1)S(1)} %get-tuple-element.58), channel_id=1, source_target_pairs={{0,8},{1,9},{2,10},{3,11},{4,12},{5,13},{6,14},{7,15},{8,0},{9,1},... | collective-permute-start | bytes 196616 | tf_op jit(solution)/shard_map/ppermute | solution.py:77
  312.8 5.2 %collective-permute-start.39 = (bf16[64,512]{1,0:T(8,128)(2,1)S(1)}, bf16[64,512]{1,0:T(8,128)(2,1)S(1)}, u32[]{:S(2)}, u32[]{:S(2)}) collective-permute-start(bf16[64,512]{1,0:T(8,128)(2,1)S(1)} %get-tuple-element.57), channel_id=1, source_target_pairs={{0,12},{1,13},{2,14},{3,15},{4,0},{5,1},{6,2},{7,3},{8,4},{9,5},{1... | collective-permute-start | bytes 196616 | tf_op jit(solution)/shard_map/ppermute | solution.py:77

commit v5 on v4

--- a/solution.py
+++ b/solution.py
@@ -63,8 +63,13 @@
     return jnp.stack([first_out, second_out]).astype(jnp.bfloat16)
 
 
+def ring_order(deep):
+    return [*range(0, deep, 2), *range(deep - 1 - deep % 2, 0, -2)]
+
+
 def mover(groups, devices):
     deep = devices // LINE
+    order = ring_order(deep)
 
     def move(value, step):
         pairs = []
@@ -76,22 +81,27 @@
                 pairs.append((g * devices + s, to_g * devices + to_s))
         return lax.ppermute(value, ("groups", "sample"), pairs)
 
-    along_z = lambda v, k=1: move(v, lambda g, a, b, c: (g, a + k, b, c))
+    def next_on_ring(a):
+        return order[(order.index(a) + 1) % deep]
+
+    along_ring = lambda v: move(v, lambda g, a, b, c: (g, next_on_ring(a), b, c))
+    along_z = lambda v, k: move(v, lambda g, a, b, c: (g, a + k, b, c))
     along_y = lambda v: move(v, lambda g, a, b, c: (g, a, 1 - b, c))
     along_x = lambda v: move(v, lambda g, a, b, c: (g ^ 1, a, b, c))
     in_chip = lambda v: move(v, lambda g, a, b, c: (g, a, b, 1 - c))
-    return along_z, along_y, along_x, in_chip
+    return along_ring, along_z, along_y, along_x, in_chip
 
 
 def after(value, done):
     return lax.optimization_barrier((value, done))[0]
 
 
-VMEM_LIMIT = 48 * 1024 * 1024
+MIB = 1024 * 1024
 
 
 def pick(source, blocks, width):
     count = blocks.shape[0]
+    rows = source.shape[0]
 
     def body(block_ref, source_ref, out_ref, sems):
         copies = []
@@ -108,13 +118,13 @@
         for copy in copies:
             copy.wait()
 
-    rows = source.shape[0]
     return pl.pallas_call(
         body,
         in_specs=[pl.BlockSpec(memory_space=pltpu.SMEM), pl.BlockSpec(memory_space=pl.ANY)],
-        out_specs=pl.BlockSpec(memory_space=pl.ANY),
+        out_specs=pl.BlockSpec(memory_space=pltpu.VMEM),
         out_shape=jax.ShapeDtypeStruct((rows, count * width), source.dtype),
         scratch_shapes=[pltpu.SemaphoreType.DMA((count,))],
+        compiler_params=pltpu.CompilerParams(vmem_limit_bytes=16 * MIB),
         cost_estimate=pl.CostEstimate(
             flops=0, bytes_accessed=4 * rows * count * width, transcendentals=0
         ),
@@ -127,64 +137,79 @@
         for array, _ in piece:
             if not any(array is held for held in arrays):
                 arrays.append(array)
-    width = pieces[0][0][0].shape[0] if len(pieces[0]) == 1 else pieces[0][0][0].shape[0] // 2
+    width = got.shape[1] // (begin + len(pieces)) if acc is not None else None
+    width = width or prompt.shape[1] // (2 * (len(pieces) + 2))
+    count = len(pieces)
     columns = sum(array.shape[1] for array, _ in pieces[0])
     row_count, step_count = prompt.shape[0], steps.shape[0]
     height = 2 * row_count + step_count
     extra = [] if acc is None else [acc]
 
     def body(block_ref, prompt_ref, got_ref, step_ref, *refs):
-        weights, held = refs[: len(arrays)], refs[-1]
-        out_ref = refs[-2]
-        step = pl.program_id(0)
+        weight_refs = refs[: len(arrays)]
+        out_ref, left, held, sems = refs[-4:]
+        copies = []
         for i, piece in enumerate(pieces):
-
-            @pl.when(step == i)
-            def _():
-                column = 0
-                for array, first in piece:
-                    ref = weights[[array is other for other in arrays].index(True)]
-                    held[:, column : column + array.shape[1]] = ref[first : first + width, :]
-                    column += array.shape[1]
-
-        @pl.when(step == 0)
-        def _():
-            if acc is None:
-                out_ref[...] = jnp.zeros_like(out_ref)
+            start = pl.multiple_of(block_ref[i] * width, width)
+            column = pl.ds(start, width)
+            group = [
+                pltpu.make_async_copy(
+                    prompt_ref.at[:, column], left.at[i, pl.ds(0, row_count), :], sems.at[i, 0]
+                ),
+                pltpu.make_async_copy(
+                    got_ref.at[:, pl.ds((begin + i) * width, width)],
+                    left.at[i, pl.ds(row_count, row_count), :],
+                    sems.at[i, 1],
+                ),
+                pltpu.make_async_copy(
+                    step_ref.at[:, column],
+                    left.at[i, pl.ds(2 * row_count, step_count), :],
+                    sems.at[i, 2],
+                ),
+            ]
+            side = 0
+            for j, (array, first) in enumerate(piece):
+                ref = weight_refs[[array is other for other in arrays].index(True)]
+                group.append(
+                    pltpu.make_async_copy(
+                        ref.at[pl.ds(first, width), :],
+                        held.at[i, :, pl.ds(side, array.shape[1])],
+                        sems.at[i, 3 + j],
+                    )
+                )
+                side += array.shape[1]
+            for copy in group:
+                copy.start()
+            copies.append(group)
+        for i, group in enumerate(copies):
+            for copy in group:
+                copy.wait()
+            product = jnp.dot(left[i], held[i], preferred_element_type=jnp.float32)
+            if i:
+                out_ref[...] += product
+            elif acc is not None:
+                out_ref[...] = refs[len(arrays)][...] + product
             else:
-                out_ref[...] = refs[len(arrays)][...]
-
-        start = 0
-        for ref, rows in (
-            (prompt_ref, row_count),
-            (got_ref, row_count),
-            (step_ref, step_count),
-        ):
-            out_ref[start : start + rows, :] += jnp.dot(
-                ref[...], held[...], preferred_element_type=jnp.float32
-            )
-            start += rows
-
+                out_ref[...] = product
+
+    anywhere = pl.BlockSpec(memory_space=pl.ANY)
     whole = pl.BlockSpec(memory_space=pltpu.VMEM)
     return pl.pallas_call(
         body,
-        grid_spec=pltpu.PrefetchScalarGridSpec(
-            num_scalar_prefetch=1,
-            grid=(len(pieces),),
-            in_specs=[
-                pl.BlockSpec((row_count, width), lambda i, ref: (0, ref[i])),
-                pl.BlockSpec((row_count, width), lambda i, ref: (0, begin + i)),
-                pl.BlockSpec((step_count, width), lambda i, ref: (0, ref[i])),
-            ]
-            + [whole] * (len(arrays) + len(extra)),
-            out_specs=pl.BlockSpec((height, columns), lambda i, ref: (0, 0)),
-            scratch_shapes=[pltpu.VMEM((width, columns), jnp.bfloat16)],
-        ),
+        in_specs=[pl.BlockSpec(memory_space=pltpu.SMEM)]
+        + [anywhere] * (3 + len(arrays))
+        + [whole] * len(extra),
+        out_specs=whole,
         out_shape=jax.ShapeDtypeStruct((height, columns), jnp.float32),
-        compiler_params=pltpu.CompilerParams(vmem_limit_bytes=VMEM_LIMIT),
+        scratch_shapes=[
+            pltpu.VMEM((count, height, width), jnp.bfloat16),
+            pltpu.VMEM((count, width, columns), jnp.bfloat16),
+            pltpu.SemaphoreType.DMA((count, 5)),
+        ],
+        compiler_params=pltpu.CompilerParams(vmem_limit_bytes=24 * MIB),
         cost_estimate=pl.CostEstimate(
-            flops=2 * height * width * len(pieces) * columns,
-            bytes_accessed=2 * height * width * len(pieces) + 8 * height * columns,
+            flops=2 * height * width * count * columns,
+            bytes_accessed=2 * height * width * count + 8 * height * columns,
             transcendentals=0,
         ),
     )(blocks, prompt, got, steps, *arrays, *extra)
@@ -246,7 +271,7 @@
             row,
             row,
         ],
-        compiler_params=pltpu.CompilerParams(vmem_limit_bytes=VMEM_LIMIT),
+        compiler_params=pltpu.CompilerParams(vmem_limit_bytes=20 * MIB),
         cost_estimate=pl.CostEstimate(
             flops=2 * kv_heads * tokens * count * HEAD_DIM,
             bytes_accessed=8 * height * kv_heads * HEAD_DIM + 2 * kv_heads * tokens * count,
@@ -255,17 +280,17 @@
     )(places, queries, own, other, cosine, sine, *masks)
 
 
-def apply_weights(places, weights, values, factor):
+def apply_weights(places, weights, values):
     kv_heads, tokens, count = weights.shape
 
-    def body(place_ref, weight_ref, value_ref, factor_ref, out_ref):
+    def body(place_ref, weight_ref, value_ref, out_ref):
         summed = lax.dot_general(
             value_ref[:tokens, :].astype(jnp.bfloat16),
             weight_ref[0],
             (((0,), (0,)), ((), ())),
             preferred_element_type=jnp.float32,
         )
-        out_ref[0] = (summed * factor_ref[0]).T.astype(jnp.bfloat16)
+        out_ref[0] = summed.T.astype(jnp.bfloat16)
 
     return pl.pallas_call(
         body,
@@ -275,18 +300,17 @@
             in_specs=[
                 pl.BlockSpec((1, tokens, count), lambda j, ref: (j, 0, 0)),
                 pl.BlockSpec((values.shape[0], HEAD_DIM), lambda j, ref: (0, ref[j])),
-                pl.BlockSpec((1, 1, count), lambda j, ref: (j, 0, 0)),
             ],
             out_specs=pl.BlockSpec((1, count, HEAD_DIM), lambda j, ref: (j, 0, 0)),
         ),
         out_shape=jax.ShapeDtypeStruct((kv_heads, count, HEAD_DIM), jnp.bfloat16),
-        compiler_params=pltpu.CompilerParams(vmem_limit_bytes=VMEM_LIMIT),
+        compiler_params=pltpu.CompilerParams(vmem_limit_bytes=20 * MIB),
         cost_estimate=pl.CostEstimate(
             flops=2 * kv_heads * tokens * count * HEAD_DIM,
             bytes_accessed=2 * kv_heads * tokens * count,
             transcendentals=0,
         ),
-    )(places, weights, values, factor)
+    )(places, weights, values)
 
 
 def out_project(blocks, heads, weight, width):
@@ -304,7 +328,7 @@
         in_specs=[pl.BlockSpec(memory_space=pltpu.SMEM), whole, whole],
         out_specs=whole,
         out_shape=jax.ShapeDtypeStruct(shape, jnp.bfloat16),
-        compiler_params=pltpu.CompilerParams(vmem_limit_bytes=VMEM_LIMIT),
+        compiler_params=pltpu.CompilerParams(vmem_limit_bytes=20 * MIB),
         cost_estimate=pl.CostEstimate(
             flops=2 * heads.shape[1] * shape[0] * shape[1],
             bytes_accessed=2 * (weight.size + heads.size + shape[0] * shape[1]),
@@ -329,7 +353,7 @@
     first = lax.axis_index("groups") % 2 == 0
     deep = devices // LINE
     own_a, own_b, own_c = own_index // LINE, own_index // 2 % 2, own_index % 2
-    along_z, along_y, along_x, in_chip = mover(groups, devices)
+    along_ring, along_z, along_y, along_x, in_chip = mover(groups, devices)
     row_count = prompt_states.shape[0]
     chip_rows = 2 * row_count
     pages_here = row_count // PAGE
@@ -347,8 +371,18 @@
     kv_places = jnp.where(first, 0, KV_HEADS // 2) + jnp.arange(KV_HEADS, dtype=jnp.int32)
     kv_places = kv_places % KV_HEADS
 
-    def block(turn_z, flip, core):
-        return ((own_a + deep + turn_z) % deep) * LINE + (own_b ^ flip) * 2 + core
+    order = ring_order(deep)
+
+    def by_place(table):
+        return sum(jnp.where(own_a == a, table[a], 0) for a in range(deep))
+
+    own_turn = by_place([order.index(a) for a in range(deep)])
+
+    def block(place_z, flip, core):
+        return place_z * LINE + (own_b ^ flip) * 2 + core
+
+    def behind(k):
+        return by_place([order[(order.index(a) - k) % deep] for a in range(deep)])
 
     def halves(weight):
         low, high = weight[:, :half], weight[:, half:]
@@ -357,54 +391,60 @@
     key_mine, key_other = halves(key_weight)
     value_mine, value_other = halves(value_weight)
 
-    places = [(k, flip) for k in range(deep) for flip in (0, 1)]
-    own_blocks = jnp.stack([block(-k, flip, own_c) for k, flip in places])
-    sent_blocks = jnp.stack([block(-k, flip, 1 - own_c) for k, flip in places])
-    sent = pick(prompt_states, after(sent_blocks, (key_mine, value_mine)), width)
-    got = in_chip(sent)
-    done = {0: [got]}
-
-    def send(move, value, turn_at):
-        if turn_at > 1:
-            value = after(value, done[turn_at - 2])
-        done.setdefault(turn_at, []).append(move(value))
-        return done[turn_at][-1]
-
     step_place = PROMPT_PAGES * PAGE + jnp.arange(2, dtype=jnp.int32)
     step_tables = tuple(t[:, None, :] for t in rope_tables(step_place))
-    queries = jnp.dot(after(wide_states, sent), query_weight, preferred_element_type=jnp.float32)
+    queries = jnp.dot(wide_states, query_weight, preferred_element_type=jnp.float32)
     queries = queries.reshape(2, samples, heads_here, HEAD_DIM).transpose(2, 0, 1, 3)
     queries = turn(queries, step_tables).astype(jnp.bfloat16)
     flat_queries = queries.reshape(rows, HEAD_DIM)
 
+    places = [(k, flip) for k in range(deep) for flip in (0, 1)]
+    own_blocks = jnp.stack([block(behind(k), flip, own_c) for k, flip in places])
+    done = {}
+
+    def send(move, value, turn_at):
+        if turn_at:
+            value = after(value, done[turn_at - 2] if turn_at > 1 else flat_queries)
+        done.setdefault(turn_at, []).append(move(value))
+        return done[turn_at][-1]
+
     key_z, key_y = {0: key_mine}, {}
     key_full = {0: jnp.concatenate([key_mine, key_other], axis=1)}
     value_pairs, other_pairs = {}, {}
-    ring = {}
     for r in range(2 * deep - 1):
         late = r - deep + 2
         if r + 1 < deep:
-            key_z[r + 1] = send(along_z, key_z[r], r)
+            key_z[r + 1] = send(along_ring, key_z[r], r)
         elif late < deep:
-            value_pairs[late] = send(along_z, value_pairs[late - 1], r)
+            value_pairs[late] = send(along_ring, value_pairs[late - 1], r)
         if r == 0:
             value_y = send(along_y, value_mine, r)
-            value_pairs[0] = jnp.concatenate([value_mine, value_y])
         elif r == 1:
-            key_y[0] = send(along_y, key_full[0], r)
-            pair_queries = jnp.stack([flat_queries, send(along_y, flat_queries, r)])
+            sent_blocks = jnp.stack([block(behind(k), flip, 1 - own_c) for k, flip in places])
+            sent = pick(prompt_states, after(sent_blocks, done[0]), width)
+            got = in_chip(sent)
+            key_y[0] = send(
+                along_y,
+                jnp.concatenate([key_full[0], flat_queries.reshape(-1, key_full[0].shape[1])]),
+                r,
+            )
+            query_pair = jnp.stack([flat_queries, key_y[0][width:].reshape(rows, HEAD_DIM)])
+            value_pairs[0] = jnp.concatenate([value_mine, value_y, query_pair.reshape(-1, half)])
+        elif r == 2:
+            done[r].append(got)
         if 0 < r < deep:
             key_full[r] = jnp.concatenate([key_z[r], send(along_x, key_z[r], r)], axis=1)
         elif r:
-            other_pairs[late - 1] = send(along_x, value_pairs[late - 1], r)
+            other_pairs[late - 1] = send(along_x, value_pairs[late - 1][: 2 * width], r)
         if r == deep - 1:
             other_pairs[0] = jnp.concatenate([value_other, send(along_x, value_y, r)])
         if 0 < late < deep:
             key_y[late] = send(along_y, key_full[late], r)
-        if 1 < r <= deep:
-            ring[r - 1] = send(lambda v: along_z(v, deep - r + 1), pair_queries, r)
-    ring = [pair_queries] + [ring[j] for j in range(1, deep)]
-    line = lax.dynamic_slice_in_dim(jnp.stack(ring + ring), deep - own_a, deep)
+    ring = [
+        value_pairs[(deep - j) % deep][2 * width :].reshape(query_pair.shape) for j in range(deep)
+    ]
+    line = lax.dynamic_slice_in_dim(jnp.stack(ring + ring), deep - own_turn, deep)
+    line = jnp.stack([line[order.index(a)] for a in range(deep)])
     all_queries = jnp.stack([line, in_chip(line)], axis=1)
     by_owner = (deep, 2, 2, rows)
     all_queries = all_queries.reshape(KV_HEADS, -1, HEAD_DIM)
@@ -437,18 +477,18 @@
             for flip in (0, 1)
         ]
 
-    def project_all(key):
+    def project_all(key, ready):
         split = 2 * (deep - 1)
         early = project(
             prompt_states, wide_states, got, own_blocks[:split], 0,
             pieces_of(range(deep - 1), key), None,
         )
         return project(
-            prompt_states, wide_states, got, own_blocks[split:], split,
+            prompt_states, wide_states, got, after(own_blocks[split:], ready), split,
             pieces_of([deep - 1], key), early,
         )
 
-    key_sum = project_all(True)
+    key_sum = project_all(True, got)
     key_back = in_chip(key_sum)
     own_place = lax.dynamic_index_in_dim(kv_places, own_kv, 0, False) * HEAD_DIM
 
@@ -471,17 +511,17 @@
     stats = jnp.concatenate([stats] + [along_z(stats, k) for k in range(1, deep)])
     prefix_top = jnp.max(stats[:, 0], axis=0)
     prefix_total = jnp.sum(jnp.exp(stats[:, 0] - prefix_top) * stats[:, 1], axis=0)
-    factor = jnp.exp(top.reshape(by_owner) - prefix_top).reshape(top.shape)
+    factor = jnp.exp(top.reshape(by_owner) - prefix_top)[:, 0]
     prefix_top = lax.dynamic_index_in_dim(prefix_top, own_a, 0, False)[0, 0]
     prefix_total = lax.dynamic_index_in_dim(prefix_total, own_a, 0, False)[0, 0]
 
-    value_sum = project_all(False)
+    value_sum = project_all(False, weights)
     step_values = own_head(value_sum[chip_rows:])
     step_back = lax.dynamic_slice_in_dim(
         in_chip(value_sum[chip_rows:]), own_place, HEAD_DIM, 1
     ).reshape(step_values.shape)
     new_values = (step_values + step_back).astype(jnp.bfloat16)
-    partial = apply_weights(kv_places, weights, value_sum, factor)
+    partial = apply_weights(kv_places, weights, value_sum)
     partial = partial.reshape(by_owner + (HEAD_DIM,))
 
     def narrow(value):
@@ -490,7 +530,8 @@
     def wide(value):
         return value.astype(jnp.float32)
 
-    partial = narrow(wide(partial[:, 0]) + wide(in_chip(partial[:, 1])))
+    partial = wide(partial[:, 0]) + wide(in_chip(partial[:, 1]))
+    partial = narrow(partial * factor[..., None])
     partial = narrow(wide(partial[:, 0]) + wide(along_y(partial[:, 1])))
     prefix_sum = wide(lax.dynamic_index_in_dim(partial, own_a, 0, False))
     for k in range(1, deep):
@@ -511,7 +552,7 @@
     out_width = out_weight.shape[1] // devices
     out_blocks = jnp.stack(
         [
-            block(k, flip, own_c ^ turned)
+            block((own_a + k) % deep, flip, own_c ^ turned)
             for turned in (0, 1)
             for flip in (0, 1)
             for k in range(deep)

time: 320 us -> 204 us (0.64)
  Pallas kernels: 169 us -> 32.3 us
  local copies, waits for them, and re-layouts: 16.7 us -> 52.1 us
  waiting for transfers between devices: 82.5 us -> 54.2 us
  starting transfers between devices: 33.8 us -> 43.4 us
  other arithmetic: 12.1 us -> 15.6 us
    pallas_call x1, Pallas kernels: 129 us -> 3.22 us  [pick(): pl.pallas_call(body, in_specs=[pl.BlockSpec(memory_space=pltpu.SMEM), pl....]
    ppermute x40 -> x36, waiting for transfers between devices: 82.5 us -> 54.2 us  [move(): return lax.ppermute(value, ('groups', 'sample'), pairs)]
    unnamed x55 -> x56, local copies, waits for them, and re-layouts: 12.7 us -> 26.1 us
    slice x4 -> x10, local copies, waits for them, and re-layouts: 0.19 us -> 10.5 us  [the longest x3 4.93 us: on_device(): other_pairs[late - 1] = send(along_x, value_pairs[late - 1][:2 * width], r)]
    ppermute x40 -> x36, starting transfers between devices: 33.8 us -> 43.4 us  [move(): return lax.ppermute(value, ('groups', 'sample'), pairs)]
    pallas_call x4, Pallas kernels: 27.9 us -> 18.9 us  [project(): pl.pallas_call(body, in_specs=[pl.BlockSpec(memory_space=pltpu.SMEM)] + [...]
    dot_general x0 -> x1, local copies, waits for them, and re-layouts: none -> 6.46 us  [on_device(): jnp.dot(wide_states, query_weight, preferred_element_type=jnp.float32)]
  transfers between devices with their start and end apart: 40 -> 36, of which waited for: 22 -> 17; matrix products, arithmetic and copies ran while one was open for 5% -> 24% of each run, Pallas kernels for 9% -> 11%
where the time goes in v5:
time: 204 us; the launch traced here: 203 us
  waiting for transfers between devices  54.2 us (27%)
  local copies, waits for them, and re-layouts  52.1 us (26%)
  starting transfers between devices  43.4 us (21%)
  Pallas kernels  32.3 us (16%)
  other arithmetic  15.6 us (8%)
  matrix products  3.58 us (2%)
    ppermute x36, waiting for transfers between devices, move(): return lax.ppermute(value, ('groups', 'sample'), pairs)  54.2 us
    ppermute x36, starting transfers between devices, move(): return lax.ppermute(value, ('groups', 'sample'), pairs)  43.4 us
    unnamed x56, local copies, waits for them, and re-layouts  26.1 us
    pallas_call x4, Pallas kernels, project(): pl.pallas_call(body, in_specs=[pl.BlockSpec(memory_space=pltpu.SMEM)] + [...  18.9 us
    dot_general x1, local copies, waits for them, and re-layouts, on_device(): jnp.dot(wide_states, query_weight, preferred_element_type=jnp.float32)  6.46 us
    pallas_call x1, Pallas kernels, attend(): pl.pallas_call(body, grid_spec=pltpu.PrefetchScalarGridSpec(num_scalar_pr...  6.18 us
    slice x3, local copies, waits for them, and re-layouts, on_device(): other_pairs[late - 1] = send(along_x, value_pairs[late - 1][:2 * width], r)  4.93 us
  transfers between devices with their start and end apart: 36, of which 17 were waited for; matrix products, arithmetic and copies ran while one was open for 24% of the time, Pallas kernels for 11%

profile of v5, /device:TPU:0, one launch (start us, length us, event | category | flops | bytes accessed | tf_op | source)
XLA Modules:
  0.0 202.6 jit_solution(359122766052250638)
XLA Ops:
  0.0 1.1 broadcast_select_fusion.3
  1.1 4.1 %collective-permute-start.2 = (bf16[512,256]{1,0:T(8,128)(2,1)S(1)}, bf16[512,256]{1,0:T(8,128)(2,1)S(1)}, u32[]{:S(2)}, u32[]{:S(2)}) collective-permute-start(bf16[512,256]{1,0:T(8,128)(2,1)S(1)} %get-tuple-element.62), channel_id=1, source_target_pairs={{0,8},{1,9},{2,10},{3,11},{4,0},{5,1},{6,2},{7,3},{8,12},{9,13},{1... | collective-permute-start | bytes 786440 | tf_op jit(solution)/shard_map/ppermute | solution.py:82
  5.2 1.8 broadcast_select_fusion
  6.9 1.5 collective-permute-start.1
  8.6 2.2 %collective-permute-done.2 = bf16[512,256]{1,0:T(8,128)(2,1)S(1)} collective-permute-done((bf16[512,256]{1,0:T(8,128)(2,1)S(1)}, bf16[512,256]{1,0:T(8,128)(2,1)S(1)}, u32[]{:S(2)}, u32[]{:S(2)}) %collective-permute-start.2) | collective-permute-done | bytes 262176 | tf_op jit(solution)/shard_map/ppermute | solution.py:82
  10.7 4.0 %collective-permute-done.1 = bf16[512,256]{1,0:T(8,128)(2,1)S(1)} collective-permute-done((bf16[512,256]{1,0:T(8,128)(2,1)S(1)}, bf16[512,256]{1,0:T(8,128)(2,1)S(1)}, u32[]{:S(2)}, u32[]{:S(2)}) %collective-permute-start.1) | collective-permute-done | bytes 262176 | tf_op jit(solution)/shard_map/ppermute | solution.py:82
  14.7 3.4 %copy-done = bf16[512,8192]{1,0:T(8,128)(2,1)S(1)} copy-done((bf16[512,8192]{1,0:T(8,128)(2,1)S(1)}, bf16[512,8192]{1,0:T(8,128)(2,1)}, u32[]{:S(2)}) %copy-start) | copy-done | bytes 8388632
  18.1 3.2 %shard_map.73 = bf16[512,4096]{1,0:T(8,128)(2,1)} custom-call(s32[8]{0:T(128)S(1)} %stack.170.block_ref, bf16[512,8192]{1,0:T(8,128)(2,1)S(1)} %copy-done), custom_call_target="tpu_custom_call" | custom-call | bytes 8388608 | tf_op jit(solution)/shard_map/pallas_call | solution.py:121
  21.4 6.5 %copy.46 = bf16[256,8192]{1,0:T(8,128)(2,1)} copy(bf16[256,8192]{0,1:T(8,128)(2,1)} %bitcast.186) | data formatting | bytes 8388608 | tf_op jit(solution)/shard_map/dot_general | solution.py:396
  28.0 3.6 %convolution_bitcast_fusion = f32[2,2,32,128]{3,2,0,1:T(8,128)S(1)} fusion(bf16[2,128,8192,1]{2,1,0,3:T(8,128)(2,1)} %bitcast.185, bf16[2,32,8192]{2,1,0:T(8,128)(2,1)S(1)} %copy-done.4), kind=kOutput, calls=%fused_computation | convolution fusion | flops 268435456 | bytes 5308416 | tf_op jit(solution)/shard_map/dot_general | solution.py:396
  32.6 1.6 collective-permute-start
  34.4 1.6 collective-permute-start.3
  36.1 1.5 collective-permute-start.4
  37.6 5.4 %collective-permute-done.3 = bf16[512,256]{1,0:T(8,128)(2,1)} collective-permute-done((bf16[512,256]{1,0:T(8,128)(2,1)S(1)}, bf16[512,256]{1,0:T(8,128)(2,1)}, u32[]{:S(2)}, u32[]{:S(2)}) %collective-permute-start.3) | collective-permute-done | bytes 262176 | tf_op jit(solution)/shard_map/ppermute | solution.py:82
  43.0 1.5 collective-permute-start.8
  44.5 2.5 %collective-permute-start.6 = (bf16[512,256]{1,0:T(8,128)(2,1)}, bf16[512,256]{1,0:T(8,128)(2,1)}, u32[]{:S(2)}, u32[]{:S(2)}) collective-permute-start(bf16[512,256]{1,0:T(8,128)(2,1)} %collective-permute-done.3), channel_id=1, source_target_pairs={{0,8},{1,9},{2,10},{3,11},{4,0},{5,1},{6,2},{7,3},{8,12},{9,13},{1... | collective-permute-start | bytes 786440 | tf_op jit(solution)/shard_map/ppermute | solution.py:82
  50.3 1.6 collective-permute-start.5
  52.9 1.6 collective-permute-start.12
  55.4 1.6 collective-permute-start.11
  60.1 8.8 %collective-permute-done.10 = bf16[512,256]{1,0:T(8,128)(2,1)} collective-permute-done((bf16[512,256]{1,0:T(8,128)(2,1)}, bf16[512,256]{1,0:T(8,128)(2,1)}, u32[]{:S(2)}, u32[]{:S(2)}) %collective-permute-start.10) | collective-permute-done | bytes 262176 | tf_op jit(solution)/shard_map/ppermute | solution.py:82
  72.5 1.1 pad_maximum_fusion.2.refs_0_
  73.7 1.9 slice.233
  75.6 1.5 collective-permute-start.22
  77.1 2.1 %collective-permute-done.16.refs_5_ = bf16[512,512]{1,0:T(8,128)(2,1)} collective-permute-done((bf16[512,512]{1,0:T(8,128)(2,1)S(1)}, bf16[512,512]{1,0:T(8,128)(2,1)}, u32[]{:S(2)}, u32[]{:S(2)}) %collective-permute-start.16) | collective-permute-done | bytes 524320 | tf_op jit(solution)/shard_map/ppermute | solution.py:82
  79.1 3.4 %copy-done.1 = bf16[512,8192]{1,0:T(8,128)(2,1)S(1)} copy-done((bf16[512,8192]{1,0:T(8,128)(2,1)S(1)}, bf16[512,8192]{1,0:T(8,128)(2,1)}, u32[]{:S(2)}) %copy-start.1) | copy-done | bytes 8388632
  82.5 6.1 %shard_map.74.refs_2_ = f32[1088,512]{1,0:T(8,128)S(1)} custom-call(s32[6]{0:T(128)S(1)} %stack.185.block_ref, bf16[512,8192]{1,0:T(8,128)(2,1)S(1)} %copy-done.1, bf16[512,4096]{1,0:T(8,128)(2,1)} %collective-permute-done.7.got_ref, bf16[64,8192]{1,0:T(8,128)(2,1)S(1)} %bitcast.173, bf16[512,512]{1,0:T(8,128)(2,1)S(1)} %pad_maximum_fusion.2.refs_0_, ...), custom_call_target="tpu_custom_call" | custom-call | flops 3422552064 | bytes 11141120 | tf_op jit(solution)/shard_map/pallas_call | solution.py:197
  88.7 1.0 copy-done.12
  89.8 3.3 %shard_map.75.own_ref = f32[1088,512]{1,0:T(8,128)S(1)} custom-call(s32[2]{0:T(128)S(1)} %pad_add_fusion.block_ref, bf16[512,8192]{1,0:T(8,128)(2,1)S(1)} %copy-done.1, bf16[512,4096]{1,0:T(8,128)(2,1)} %collective-permute-done.7.got_ref, bf16[64,8192]{1,0:T(8,128)(2,1)S(1)} %bitcast.174, bf16[512,512]{1,0:T(8,128)(2,1)S(1)} %copy-done.12, ...), custom_call_target="tpu_custom_call" | custom-call | flops 1140850688 | bytes 6684672 | tf_op jit(solution)/shard_map/pallas_call | solution.py:197
  94.0 1.9 fusion.4
  96.9 1.0 pad_maximum_fusion.5.sine_ref
  97.9 1.8 pad_maximum_fusion.6.refs_1_
  101.2 1.5 slice.222
  103.6 1.9 slice.234
  105.4 1.5 collective-permute-start.24
  106.9 2.3 %collective-permute-done.13.refs_0_ = bf16[1152,256]{1,0:T(8,128)(2,1)} collective-permute-done((bf16[1152,256]{1,0:T(8,128)(2,1)}, bf16[1152,256]{1,0:T(8,128)(2,1)}, u32[]{:S(2)}, u32[]{:S(2)}) %collective-permute-start.13) | collective-permute-done | bytes 589856 | tf_op jit(solution)/shard_map/ppermute | solution.py:82
  109.3 1.5 slice.221
  110.7 1.5 stack_reshape.23
  112.2 1.2 slice.232
  113.4 1.6 collective-permute-start.23
  114.9 1.5 constant_dynamic-update-slice_fusion.7
  118.3 1.5 constant_dynamic-update-slice_fusion.4
  122.9 3.4 %copy-done.2 = bf16[512,8192]{1,0:T(8,128)(2,1)S(1)} copy-done((bf16[512,8192]{1,0:T(8,128)(2,1)S(1)}, bf16[512,8192]{1,0:T(8,128)(2,1)}, u32[]{:S(2)}) %copy-start.2) | copy-done | bytes 8388632
  126.3 6.1 %shard_map.77.refs_2_ = f32[1088,512]{1,0:T(8,128)S(1)} custom-call(s32[6]{0:T(128)S(1)} %stack.185.block_ref, bf16[512,8192]{1,0:T(8,128)(2,1)S(1)} %copy-done.2, bf16[512,4096]{1,0:T(8,128)(2,1)} %collective-permute-done.7.got_ref, bf16[64,8192]{1,0:T(8,128)(2,1)S(1)} %bitcast.175, bf16[1152,256]{1,0:T(8,128)(2,1)S(1)} %copy-done.7, ...), custom_call_target="tpu_custom_call" | custom-call | flops 3422552064 | bytes 11141120 | tf_op jit(solution)/shard_map/pallas_call | solution.py:197
  133.6 6.2 %shard_map.76 = (bf16[4,1024,512]{2,1,0:T(8,128)(2,1)S(1)}, f32[4,1,512]{2,1,0:T(1,128)S(1)}, f32[4,1,512]{2,1,0:T(1,128)S(1)}) custom-call(s32[4]{0:T(128)S(1)} %and_select_fusion.1.place_ref, bf16[4,512,128]{2,1,0:T(8,128)(2,1)S(1)} %bitcast.177, f32[1088,512]{1,0:T(8,128)S(1)} %shard_map.75.own_ref, f32[1088,512]{1,0:T(8,128)} %collective-permute-done.17.other_ref, ...), custom_call_target="tpu_custom_call" | custom-call | flops 536870912 | bytes 8650752 | tf_op jit(solution)/shard_map/pallas_call | solution.py:250
  139.9 3.4 %copy-done.3 = bf16[512,8192]{1,0:T(8,128)(2,1)S(1)} copy-done((bf16[512,8192]{1,0:T(8,128)(2,1)S(1)}, bf16[512,8192]{1,0:T(8,128)(2,1)}, u32[]{:S(2)}) %copy-start.3) | copy-done | bytes 8388632
  143.2 3.4 %shard_map.78.value_ref = f32[1088,512]{1,0:T(8,128)S(1)} custom-call(s32[2]{0:T(128)S(1)} %pad_add_fusion.block_ref, bf16[512,8192]{1,0:T(8,128)(2,1)S(1)} %copy-done.3, bf16[512,4096]{1,0:T(8,128)(2,1)} %collective-permute-done.7.got_ref, bf16[64,8192]{1,0:T(8,128)(2,1)S(1)} %bitcast.176, bf16[1152,256]{1,0:T(8,128)(2,1)} %collective-permute-done.13.refs_0_, ...), custom_call_target="tpu_custom_call" | custom-call | flops 1140850688 | bytes 6684672 | tf_op jit(solution)/shard_map/pallas_call | solution.py:197
  146.6 2.6 %shard_map.79 = bf16[4,512,128]{2,1,0:T(8,128)(2,1)S(1)} custom-call(s32[4]{0:T(128)S(1)} %and_select_fusion.1.place_ref, bf16[4,1024,512]{2,1,0:T(8,128)(2,1)S(1)} %get-tuple-element.40.weight_ref, f32[1088,512]{1,0:T(8,128)S(1)} %shard_map.78.value_ref), custom_call_target="tpu_custom_call" | custom-call | flops 536870912 | bytes 4194304 | tf_op jit(solution)/shard_map/pallas_call | solution.py:295
  151.3 1.7 collective-permute-start.18
  153.8 1.3 collective-permute-done.18
  155.7 2.5 %collective-permute-start.20 = (f32[2,2,4,2,2,128]{5,4,3,2,1,0:T(2,128)S(1)}, f32[2,2,4,2,2,128]{5,4,3,2,1,0:T(2,128)S(1)}, u32[]{:S(2)}, u32[]{:S(2)}) collective-permute-start(f32[2,2,4,2,2,128]{5,4,3,2,1,0:T(2,128)S(1)} %pad_maximum_fusion.10), channel_id=1, source_target_pairs={{0,8},{1,9},{2,10},{3,11},{4,12},{5,13},{6,14},{7,15},{8,0},{9,1},... | collective-permute-start | bytes 98312 | tf_op jit(solution)/shard_map/ppermute | solution.py:82
  158.7 5.2 %collective-permute-done.19 = f32[2,2,4,2,2,128]{5,4,3,2,1,0:T(2,128)S(1)} collective-permute-done((f32[2,2,4,2,2,128]{5,4,3,2,1,0:T(2,128)S(1)}, f32[2,2,4,2,2,128]{5,4,3,2,1,0:T(2,128)S(1)}, u32[]{:S(2)}, u32[]{:S(2)}) %collective-permute-start.19) | collective-permute-done | bytes 32800 | tf_op jit(solution)/shard_map/ppermute | solution.py:82
  164.6 1.6 collective-permute-start.26
  166.2 3.4 %collective-permute-done.26 = bf16[4,128,128]{2,1,0:T(8,128)(2,1)S(1)} collective-permute-done((bf16[4,128,128]{2,1,0:T(8,128)(2,1)S(1)}, bf16[4,128,128]{2,1,0:T(8,128)(2,1)S(1)}, u32[]{:S(2)}, u32[]{:S(2)}) %collective-permute-start.26) | collective-permute-done | bytes 131104 | tf_op jit(solution)/shard_map/ppermute | solution.py:82
  169.7 3.8 %collective-permute-start.29 = (bf16[128,128]{1,0:T(8,128)(2,1)S(1)}, bf16[128,128]{1,0:T(8,128)(2,1)S(1)}, u32[]{:S(2)}, u32[]{:S(2)}) collective-permute-start(bf16[128,128]{1,0:T(8,128)(2,1)S(1)} %get-tuple-element.70), channel_id=1, source_target_pairs={{0,12},{1,13},{2,14},{3,15},{4,0},{5,1},{6,2},{7,3},{8,4},{9,5},{1... | collective-permute-start | bytes 98312 | tf_op jit(solution)/shard_map/ppermute | solution.py:82
  173.5 1.9 collective-permute-done.27
  175.4 2.9 %collective-permute-done.28 = bf16[128,128]{1,0:T(8,128)(2,1)S(1)} collective-permute-done((bf16[128,128]{1,0:T(8,128)(2,1)S(1)}, bf16[128,128]{1,0:T(8,128)(2,1)S(1)}, u32[]{:S(2)}, u32[]{:S(2)}) %collective-permute-start.28) | collective-permute-done | bytes 32800 | tf_op jit(solution)/shard_map/ppermute | solution.py:82
  178.6 2.2 %copy-done.5 = bf16[256,8192]{1,0:T(8,128)(2,1)S(1)} copy-done((bf16[256,8192]{1,0:T(8,128)(2,1)S(1)}, bf16[256,8192]{1,0:T(8,128)(2,1)}, u32[]{:S(2)}) %copy-start.5) | copy-done | bytes 4194328
  180.8 1.4 shard_map.80
  182.3 1.9 collective-permute-done.31
  184.3 1.6 collective-permute-start.32
  185.9 6.8 %collective-permute-done.32 = bf16[64,2048]{1,0:T(8,128)(2,1)S(1)} collective-permute-done((bf16[64,2048]{1,0:T(8,128)(2,1)S(1)}, bf16[64,2048]{1,0:T(8,128)(2,1)S(1)}, u32[]{:S(2)}, u32[]{:S(2)}) %collective-permute-start.32) | collective-permute-done | bytes 262176 | tf_op jit(solution)/shard_map/ppermute | solution.py:82
  192.9 3.8 %collective-permute-start.35 = (bf16[64,512]{1,0:T(8,128)(2,1)S(1)}, bf16[64,512]{1,0:T(8,128)(2,1)S(1)}, u32[]{:S(2)}, u32[]{:S(2)}) collective-permute-start(bf16[64,512]{1,0:T(8,128)(2,1)S(1)} %get-tuple-element.65), channel_id=1, source_target_pairs={{0,12},{1,13},{2,14},{3,15},{4,0},{5,1},{6,2},{7,3},{8,4},{9,5},{1... | collective-permute-start | bytes 196616 | tf_op jit(solution)/shard_map/ppermute | solution.py:82
  196.7 2.7 %collective-permute-done.33 = bf16[64,512]{1,0:T(8,128)(2,1)S(1)} collective-permute-done((bf16[64,512]{1,0:T(8,128)(2,1)S(1)}, bf16[64,512]{1,0:T(8,128)(2,1)S(1)}, u32[]{:S(2)}, u32[]{:S(2)}) %collective-permute-start.33) | collective-permute-done | bytes 65568 | tf_op jit(solution)/shard_map/ppermute | solution.py:82
  199.5 2.4 %collective-permute-done.34 = bf16[64,512]{1,0:T(8,128)(2,1)S(1)} collective-permute-done((bf16[64,512]{1,0:T(8,128)(2,1)S(1)}, bf16[64,512]{1,0:T(8,128)(2,1)S(1)}, u32[]{:S(2)}, u32[]{:S(2)}) %collective-permute-start.34) | collective-permute-done | bytes 65568 | tf_op jit(solution)/shard_map/ppermute | solution.py:82
  (170 shorter events, 29.2 us)
Async XLA Ops:
  1.1 31.4 %copy-start.15 = (bf16[512,256]{1,0:T(8,128)(2,1)}, bf16[512,256]{1,0:T(8,128)(2,1)S(1)}, u32[]{:S(2)}) copy-start(bf16[512,256]{1,0:T(8,128)(2,1)S(1)} %get-tuple-element.62) | copy-start | bytes 786436
  1.1 31.4 %copy-start.16 = (bf16[512,256]{1,0:T(8,128)(2,1)}, bf16[512,256]{1,0:T(8,128)(2,1)S(1)}, u32[]{:S(2)}) copy-start(bf16[512,256]{1,0:T(8,128)(2,1)S(1)} %get-tuple-element.63) | copy-start | bytes 786436
  1.1 9.7 %collective-permute-start.2 = (bf16[512,256]{1,0:T(8,128)(2,1)S(1)}, bf16[512,256]{1,0:T(8,128)(2,1)S(1)}, u32[]{:S(2)}, u32[]{:S(2)}) collective-permute-start(bf16[512,256]{1,0:T(8,128)(2,1)S(1)} %get-tuple-element.62), channel_id=1, source_target_pairs={{0,8},{1,9},{2,10},{3,11},{4,0},{5,1},{6,2},{7,3},{8,12},{9,13},{1... | collective-permute-start | bytes 786440 | tf_op jit(solution)/shard_map/ppermute | solution.py:82
  6.9 7.8 %collective-permute-start.1 = (bf16[512,256]{1,0:T(8,128)(2,1)S(1)}, bf16[512,256]{1,0:T(8,128)(2,1)S(1)}, u32[]{:S(2)}, u32[]{:S(2)}) collective-permute-start(bf16[512,256]{1,0:T(8,128)(2,1)S(1)} %get-tuple-element.59), channel_id=1, source_target_pairs={{0,2},{1,3},{2,0},{3,1},{4,6},{5,7},{6,4},{7,5},{8,10},{9,11},{10,... | collective-permute-start | bytes 786440 | tf_op jit(solution)/shard_map/ppermute | solution.py:82
  14.7 3.4 %copy-start = (bf16[512,8192]{1,0:T(8,128)(2,1)S(1)}, bf16[512,8192]{1,0:T(8,128)(2,1)}, u32[]{:S(2)}) copy-start(bf16[512,8192]{1,0:T(8,128)(2,1)} %prompt_ref.7) | copy-start | bytes 25165828
  18.1 3.2 %copy-start.18 = (bf16[512,256]{1,0:T(8,128)(2,1)}, bf16[512,256]{1,0:T(8,128)(2,1)S(1)}, u32[]{:S(2)}) copy-start(bf16[512,256]{1,0:T(8,128)(2,1)S(1)} %collective-permute-done.1) | copy-start | bytes 786436
  21.3 37.2 %collective-permute-start.7 = (bf16[512,4096]{1,0:T(8,128)(2,1)}, bf16[512,4096]{1,0:T(8,128)(2,1)}, u32[]{:S(2)}, u32[]{:S(2)}) collective-permute-start(bf16[512,4096]{1,0:T(8,128)(2,1)} %shard_map.73), channel_id=1, source_target_pairs={{0,1},{1,0},{2,3},{3,2},{4,5},{5,4},{6,7},{7,6},{8,9},{9,8},{10,11... | collective-permute-start | bytes 12582920 | tf_op jit(solution)/shard_map/ppermute | solution.py:82
  21.4 6.6 %copy-start.4 = (bf16[2,32,8192]{2,1,0:T(8,128)(2,1)S(1)}, bf16[2,32,8192]{2,1,0:T(8,128)(2,1)}, u32[]{:S(2)}) copy-start(bf16[2,32,8192]{2,1,0:T(8,128)(2,1)} %param.10) | copy-start | bytes 3145732
  28.0 6.2 %copy-start.20 = (s32[64]{0:T(128)S(1)}, s32[64]{0:T(128)}, u32[]{:S(2)}) copy-start(s32[64]{0:T(128)} %param.9) | copy-start | bytes 772
  32.6 15.1 %collective-permute-start = (bf16[544,512]{1,0:T(8,128)(2,1)S(1)}, bf16[544,512]{1,0:T(8,128)(2,1)S(1)}, u32[]{:S(2)}, u32[]{:S(2)}) collective-permute-start(bf16[544,512]{1,0:T(8,128)(2,1)S(1)} %pad_maximum_fusion.1), channel_id=1, source_target_pairs={{0,2},{1,3},{2,0},{3,1},{4,6},{5,7},{6,4},{7,5},{8,10},{9,11},{10,... | collective-permute-start | bytes 1671176 | tf_op jit(solution)/shard_map/ppermute | solution.py:82
  34.4 8.6 %collective-permute-start.3 = (bf16[512,256]{1,0:T(8,128)(2,1)S(1)}, bf16[512,256]{1,0:T(8,128)(2,1)}, u32[]{:S(2)}, u32[]{:S(2)}) collective-permute-start(bf16[512,256]{1,0:T(8,128)(2,1)S(1)} %collective-permute-done.2), channel_id=1, source_target_pairs={{0,8},{1,9},{2,10},{3,11},{4,0},{5,1},{6,2},{7,3},{8,12},{9,13},{1... | collective-permute-start | bytes 786440 | tf_op jit(solution)/shard_map/ppermute | solution.py:82
  36.1 14.1 %collective-permute-start.4 = (bf16[512,256]{1,0:T(8,128)(2,1)S(1)}, bf16[512,256]{1,0:T(8,128)(2,1)}, u32[]{:S(2)}, u32[]{:S(2)}) collective-permute-start(bf16[512,256]{1,0:T(8,128)(2,1)S(1)} %collective-permute-done.2), channel_id=1, source_target_pairs={{0,16},{1,17},{2,18},{3,19},{4,20},{5,21},{6,22},{7,23},{8,24},{9,... | collective-permute-start | bytes 786440 | tf_op jit(solution)/shard_map/ppermute | solution.py:82
  43.0 14.0 %collective-permute-start.8 = (bf16[512,256]{1,0:T(8,128)(2,1)}, bf16[512,256]{1,0:T(8,128)(2,1)}, u32[]{:S(2)}, u32[]{:S(2)}) collective-permute-start(bf16[512,256]{1,0:T(8,128)(2,1)} %collective-permute-done.3), channel_id=1, source_target_pairs={{0,16},{1,17},{2,18},{3,19},{4,20},{5,21},{6,22},{7,23},{8,24},{9,... | collective-permute-start | bytes 786440 | tf_op jit(solution)/shard_map/ppermute | solution.py:82
  44.5 10.9 %collective-permute-start.6 = (bf16[512,256]{1,0:T(8,128)(2,1)}, bf16[512,256]{1,0:T(8,128)(2,1)}, u32[]{:S(2)}, u32[]{:S(2)}) collective-permute-start(bf16[512,256]{1,0:T(8,128)(2,1)} %collective-permute-done.3), channel_id=1, source_target_pairs={{0,8},{1,9},{2,10},{3,11},{4,0},{5,1},{6,2},{7,3},{8,12},{9,13},{1... | collective-permute-start | bytes 786440 | tf_op jit(solution)/shard_map/ppermute | solution.py:82
  47.7 0.8 copy-start.13
  50.2 25.3 %copy-start.6 = (bf16[1152,256]{1,0:T(8,128)(2,1)}, bf16[1152,256]{1,0:T(8,128)(2,1)S(1)}, u32[]{:S(2)}) copy-start(bf16[1152,256]{1,0:T(8,128)(2,1)S(1)} %pad_maximum_fusion.refs_0_) | copy-start | bytes 1769476
  50.3 19.6 %collective-permute-start.5 = (bf16[1152,256]{1,0:T(8,128)(2,1)S(1)}, bf16[1152,256]{1,0:T(8,128)(2,1)}, u32[]{:S(2)}, u32[]{:S(2)}) collective-permute-start(bf16[1152,256]{1,0:T(8,128)(2,1)S(1)} %pad_maximum_fusion.refs_0_), channel_id=1, source_target_pairs={{0,8},{1,9},{2,10},{3,11},{4,0},{5,1},{6,2},{7,3},{8,12},{9,13},{1... | collective-permute-start | bytes 1769480 | tf_op jit(solution)/shard_map/ppermute | solution.py:82
  52.9 17.0 %collective-permute-start.12 = (bf16[512,512]{1,0:T(8,128)(2,1)S(1)}, bf16[512,512]{1,0:T(8,128)(2,1)}, u32[]{:S(2)}, u32[]{:S(2)}) collective-permute-start(bf16[512,512]{1,0:T(8,128)(2,1)S(1)} %constant_dynamic-update-slice_fusion.refs_2_), channel_id=1, source_target_pairs={{0,2},{1,3},{2,0},{3,1},{4,6},{5,7},{6,4},{7,5},{8,10},{9,11},{10,... | collective-permute-start | bytes 1572872 | tf_op jit(solution)/shard_map/ppermute | solution.py:82
  55.4 14.4 %collective-permute-start.11 = (bf16[512,256]{1,0:T(8,128)(2,1)}, bf16[512,256]{1,0:T(8,128)(2,1)}, u32[]{:S(2)}, u32[]{:S(2)}) collective-permute-start(bf16[512,256]{1,0:T(8,128)(2,1)} %copy-done.18), channel_id=1, source_target_pairs={{0,16},{1,17},{2,18},{3,19},{4,20},{5,21},{6,22},{7,23},{8,24},{9,... | collective-permute-start | bytes 786440 | tf_op jit(solution)/shard_map/ppermute | solution.py:82
  57.0 11.9 %collective-permute-start.10 = (bf16[512,256]{1,0:T(8,128)(2,1)}, bf16[512,256]{1,0:T(8,128)(2,1)}, u32[]{:S(2)}, u32[]{:S(2)}) collective-permute-start(bf16[512,256]{1,0:T(8,128)(2,1)} %collective-permute-done.6), channel_id=1, source_target_pairs={{0,16},{1,17},{2,18},{3,19},{4,20},{5,21},{6,22},{7,23},{8,24},{9,... | collective-permute-start | bytes 786440 | tf_op jit(solution)/shard_map/ppermute | solution.py:82
  58.5 20.6 %collective-permute-start.16 = (bf16[512,512]{1,0:T(8,128)(2,1)S(1)}, bf16[512,512]{1,0:T(8,128)(2,1)}, u32[]{:S(2)}, u32[]{:S(2)}) collective-permute-start(bf16[512,512]{1,0:T(8,128)(2,1)S(1)} %constant_dynamic-update-slice_fusion.10.refs_4_), channel_id=1, source_target_pairs={{0,2},{1,3},{2,0},{3,1},{4,6},{5,7},{6,4},{7,5},{8,10},{9,11},{10,... | collective-permute-start | bytes 1572872 | tf_op jit(solution)/shard_map/ppermute | solution.py:82
  69.8 18.8 %copy-start.11 = (bf16[512,512]{1,0:T(8,128)(2,1)}, bf16[512,512]{1,0:T(8,128)(2,1)S(1)}, u32[]{:S(2)}) copy-start(bf16[512,512]{1,0:T(8,128)(2,1)S(1)} %constant_dynamic-update-slice_fusion.8.refs_0_) | copy-start | bytes 1572868
  69.9 18.9 %collective-permute-start.15 = (bf16[512,512]{1,0:T(8,128)(2,1)S(1)}, bf16[512,512]{1,0:T(8,128)(2,1)}, u32[]{:S(2)}, u32[]{:S(2)}) collective-permute-start(bf16[512,512]{1,0:T(8,128)(2,1)S(1)} %constant_dynamic-update-slice_fusion.8.refs_0_), channel_id=1, source_target_pairs={{0,2},{1,3},{2,0},{3,1},{4,6},{5,7},{6,4},{7,5},{8,10},{9,11},{10,... | collective-permute-start | bytes 1572872 | tf_op jit(solution)/shard_map/ppermute | solution.py:82
  70.4 22.8 %collective-permute-start.9 = (bf16[1152,256]{1,0:T(8,128)(2,1)}, bf16[1152,256]{1,0:T(8,128)(2,1)}, u32[]{:S(2)}, u32[]{:S(2)}) collective-permute-start(bf16[1152,256]{1,0:T(8,128)(2,1)} %collective-permute-done.5.refs_2_), channel_id=1, source_target_pairs={{0,8},{1,9},{2,10},{3,11},{4,0},{5,1},{6,2},{7,3},{8,12},{9,13},{1... | collective-permute-start | bytes 1769480 | tf_op jit(solution)/shard_map/ppermute | solution.py:82
  72.5 6.6 %copy-start.14 = (bf16[544,512]{1,0:T(8,128)(2,1)S(1)}, bf16[544,512]{1,0:T(8,128)(2,1)}, u32[]{:S(2)}) copy-start(bf16[544,512]{1,0:T(8,128)(2,1)} %copy-done.13) | copy-start | bytes 1671172
  75.6 37.8 %collective-permute-start.22 = (bf16[1024,256]{1,0:T(8,128)(2,1)}, bf16[1024,256]{1,0:T(8,128)(2,1)}, u32[]{:S(2)}, u32[]{:S(2)}) collective-permute-start(bf16[1024,256]{1,0:T(8,128)(2,1)} %slice.233), channel_id=1, source_target_pairs={{0,16},{1,17},{2,18},{3,19},{4,20},{5,21},{6,22},{7,23},{8,24},{9,... | collective-permute-start | bytes 1572872 | tf_op jit(solution)/shard_map/ppermute | solution.py:82
  79.1 3.4 %copy-start.1 = (bf16[512,8192]{1,0:T(8,128)(2,1)S(1)}, bf16[512,8192]{1,0:T(8,128)(2,1)}, u32[]{:S(2)}) copy-start(bf16[512,8192]{1,0:T(8,128)(2,1)} %prompt_ref.7) | copy-start | bytes 25165828
  88.7 1.0 copy-start.12
  93.1 4.8 %copy-start.17 = (bf16[512,256]{1,0:T(8,128)(2,1)S(1)}, bf16[512,256]{1,0:T(8,128)(2,1)}, u32[]{:S(2)}) copy-start(bf16[512,256]{1,0:T(8,128)(2,1)} %get-tuple-element.58) | copy-start | bytes 786436
  93.1 39.5 %collective-permute-start.17 = (f32[1088,512]{1,0:T(8,128)S(1)}, f32[1088,512]{1,0:T(8,128)}, u32[]{:S(2)}, u32[]{:S(2)}) collective-permute-start(f32[1088,512]{1,0:T(8,128)S(1)} %shard_map.75.own_ref), channel_id=1, source_target_pairs={{0,1},{1,0},{2,3},{3,2},{4,5},{5,4},{6,7},{7,6},{8,9},{9,8},{10,11... | collective-permute-start | bytes 6684680 | tf_op jit(solution)/shard_map/ppermute | solution.py:82
  93.2 16.0 %collective-permute-start.13 = (bf16[1152,256]{1,0:T(8,128)(2,1)}, bf16[1152,256]{1,0:T(8,128)(2,1)}, u32[]{:S(2)}, u32[]{:S(2)}) collective-permute-start(bf16[1152,256]{1,0:T(8,128)(2,1)} %collective-permute-done.9.refs_4_), channel_id=1, source_target_pairs={{0,8},{1,9},{2,10},{3,11},{4,0},{5,1},{6,2},{7,3},{8,12},{9,13},{1... | collective-permute-start | bytes 1769480 | tf_op jit(solution)/shard_map/ppermute | solution.py:82
  105.4 17.5 %collective-permute-start.24 = (bf16[1024,256]{1,0:T(8,128)(2,1)}, bf16[1024,256]{1,0:T(8,128)(2,1)}, u32[]{:S(2)}, u32[]{:S(2)}) collective-permute-start(bf16[1024,256]{1,0:T(8,128)(2,1)} %slice.234), channel_id=1, source_target_pairs={{0,16},{1,17},{2,18},{3,19},{4,20},{5,21},{6,22},{7,23},{8,24},{9,... | collective-permute-start | bytes 1572872 | tf_op jit(solution)/shard_map/ppermute | solution.py:82
  112.2 10.7 %copy-start.7 = (bf16[1152,256]{1,0:T(8,128)(2,1)S(1)}, bf16[1152,256]{1,0:T(8,128)(2,1)}, u32[]{:S(2)}) copy-start(bf16[1152,256]{1,0:T(8,128)(2,1)} %copy-done.6) | copy-start | bytes 1769476
  112.2 10.7 %copy-start.10 = (bf16[1024,256]{1,0:T(8,128)(2,1)S(1)}, bf16[1024,256]{1,0:T(8,128)(2,1)}, u32[]{:S(2)}) copy-start(bf16[1024,256]{1,0:T(8,128)(2,1)} %pad_maximum_fusion.6.refs_1_) | copy-start | bytes 1572868
  113.4 26.4 %collective-permute-start.23 = (bf16[1024,256]{1,0:T(8,128)(2,1)S(1)}, bf16[1024,256]{1,0:T(8,128)(2,1)S(1)}, u32[]{:S(2)}, u32[]{:S(2)}) collective-permute-start(bf16[1024,256]{1,0:T(8,128)(2,1)S(1)} %slice.232), channel_id=1, source_target_pairs={{0,16},{1,17},{2,18},{3,19},{4,20},{5,21},{6,22},{7,23},{8,24},{9,... | collective-permute-start | bytes 1572872 | tf_op jit(solution)/shard_map/ppermute | solution.py:82
  122.8 9.6 %collective-permute-start.14 = (bf16[4,2,128,128]{3,2,1,0:T(8,128)(2,1)S(1)}, bf16[4,2,128,128]{3,2,1,0:T(8,128)(2,1)S(1)}, u32[]{:S(2)}, u32[]{:S(2)}) collective-permute-start(bf16[4,2,128,128]{3,2,1,0:T(8,128)(2,1)S(1)} %get-tuple-element.68), channel_id=1, source_target_pairs={{0,1},{1,0},{2,3},{3,2},{4,5},{5,4},{6,7},{7,6},{8,9},{9,8},{10,11... | collective-permute-start | bytes 786440 | tf_op jit(solution)/shard_map/ppermute | solution.py:82
  122.9 3.4 %copy-start.2 = (bf16[512,8192]{1,0:T(8,128)(2,1)S(1)}, bf16[512,8192]{1,0:T(8,128)(2,1)}, u32[]{:S(2)}) copy-start(bf16[512,8192]{1,0:T(8,128)(2,1)} %prompt_ref.7) | copy-start | bytes 25165828
  132.4 1.0 copy-start.8
  132.5 1.2 copy-start.9
  139.8 3.4 %copy-start.3 = (bf16[512,8192]{1,0:T(8,128)(2,1)S(1)}, bf16[512,8192]{1,0:T(8,128)(2,1)}, u32[]{:S(2)}) copy-start(bf16[512,8192]{1,0:T(8,128)(2,1)} %prompt_ref.7) | copy-start | bytes 25165828
  149.2 4.5 %copy-start.19 = (f32[2,2,32,128]{3,2,1,0:T(8,128)S(1)}, f32[2,2,32,128]{3,2,1,0:T(8,128)}, u32[]{:S(2)}) copy-start(f32[2,2,32,128]{3,2,1,0:T(8,128)} %get-tuple-element.52) | copy-start | bytes 196612
  151.3 3.8 %collective-permute-start.18 = (f32[2,4,2,2,128]{4,3,2,1,0:T(2,128)S(1)}, f32[2,4,2,2,128]{4,3,2,1,0:T(2,128)S(1)}, u32[]{:S(2)}, u32[]{:S(2)}) collective-permute-start(f32[2,4,2,2,128]{4,3,2,1,0:T(2,128)S(1)} %get-tuple-element.81), channel_id=1, source_target_pairs={{0,2},{1,3},{2,0},{3,1},{4,6},{5,7},{6,4},{7,5},{8,10},{9,11},{10,... | collective-permute-start | bytes 49160 | tf_op jit(solution)/shard_map/ppermute | solution.py:82
  153.0 13.2 %collective-permute-start.30 = (f32[64,512]{1,0:T(8,128)S(1)}, f32[64,512]{1,0:T(8,128)S(1)}, u32[]{:S(2)}, u32[]{:S(2)}) collective-permute-start(f32[64,512]{1,0:T(8,128)S(1)} %slice.242), channel_id=1, source_target_pairs={{0,1},{1,0},{2,3},{3,2},{4,5},{5,4},{6,7},{7,6},{8,9},{9,8},{10,11... | collective-permute-start | bytes 393224 | tf_op jit(solution)/shard_map/ppermute | solution.py:82
  153.2 11.1 %collective-permute-start.25 = (bf16[4,2,128,128]{3,2,0,1:T(8,128)(2,1)S(1)}, bf16[4,2,128,128]{3,2,0,1:T(8,128)(2,1)S(1)}, u32[]{:S(2)}, u32[]{:S(2)}) collective-permute-start(bf16[4,2,128,128]{3,2,0,1:T(8,128)(2,1)S(1)} %bitcast.189), channel_id=1, source_target_pairs={{0,1},{1,0},{2,3},{3,2},{4,5},{5,4},{6,7},{7,6},{8,9},{9,8},{10,11... | collective-permute-start | bytes 786440 | tf_op jit(solution)/shard_map/ppermute | solution.py:82
  155.2 8.7 %collective-permute-start.21 = (f32[2,2,4,2,2,128]{5,4,3,2,1,0:T(2,128)S(1)}, f32[2,2,4,2,2,128]{5,4,3,2,1,0:T(2,128)S(1)}, u32[]{:S(2)}, u32[]{:S(2)}) collective-permute-start(f32[2,2,4,2,2,128]{5,4,3,2,1,0:T(2,128)S(1)} %pad_maximum_fusion.10), channel_id=1, source_target_pairs={{0,12},{1,13},{2,14},{3,15},{4,0},{5,1},{6,2},{7,3},{8,4},{9,5},{1... | collective-permute-start | bytes 98312 | tf_op jit(solution)/shard_map/ppermute | solution.py:82
  155.7 8.2 %collective-permute-start.20 = (f32[2,2,4,2,2,128]{5,4,3,2,1,0:T(2,128)S(1)}, f32[2,2,4,2,2,128]{5,4,3,2,1,0:T(2,128)S(1)}, u32[]{:S(2)}, u32[]{:S(2)}) collective-permute-start(f32[2,2,4,2,2,128]{5,4,3,2,1,0:T(2,128)S(1)} %pad_maximum_fusion.10), channel_id=1, source_target_pairs={{0,8},{1,9},{2,10},{3,11},{4,12},{5,13},{6,14},{7,15},{8,0},{9,1},... | collective-permute-start | bytes 98312 | tf_op jit(solution)/shard_map/ppermute | solution.py:82
  158.2 5.7 %collective-permute-start.19 = (f32[2,2,4,2,2,128]{5,4,3,2,1,0:T(2,128)S(1)}, f32[2,2,4,2,2,128]{5,4,3,2,1,0:T(2,128)S(1)}, u32[]{:S(2)}, u32[]{:S(2)}) collective-permute-start(f32[2,2,4,2,2,128]{5,4,3,2,1,0:T(2,128)S(1)} %pad_maximum_fusion.10), channel_id=1, source_target_pairs={{0,4},{1,5},{2,6},{3,7},{4,8},{5,9},{6,10},{7,11},{8,12},{9,13},{1... | collective-permute-start | bytes 98312 | tf_op jit(solution)/shard_map/ppermute | solution.py:82
  164.6 5.0 %collective-permute-start.26 = (bf16[4,128,128]{2,1,0:T(8,128)(2,1)S(1)}, bf16[4,128,128]{2,1,0:T(8,128)(2,1)S(1)}, u32[]{:S(2)}, u32[]{:S(2)}) collective-permute-start(bf16[4,128,128]{2,1,0:T(8,128)(2,1)S(1)} %slice_bitcast_fusion), channel_id=1, source_target_pairs={{0,2},{1,3},{2,0},{3,1},{4,6},{5,7},{6,4},{7,5},{8,10},{9,11},{10,... | collective-permute-start | bytes 393224 | tf_op jit(solution)/shard_map/ppermute | solution.py:82
  169.7 5.8 %collective-permute-start.27 = (bf16[128,128]{1,0:T(8,128)(2,1)S(1)}, bf16[128,128]{1,0:T(8,128)(2,1)S(1)}, u32[]{:S(2)}, u32[]{:S(2)}) collective-permute-start(bf16[128,128]{1,0:T(8,128)(2,1)S(1)} %get-tuple-element.69), channel_id=1, source_target_pairs={{0,4},{1,5},{2,6},{3,7},{4,8},{5,9},{6,10},{7,11},{8,12},{9,13},{1... | collective-permute-start | bytes 98312 | tf_op jit(solution)/shard_map/ppermute | solution.py:82
  169.7 5.7 %collective-permute-start.29 = (bf16[128,128]{1,0:T(8,128)(2,1)S(1)}, bf16[128,128]{1,0:T(8,128)(2,1)S(1)}, u32[]{:S(2)}, u32[]{:S(2)}) collective-permute-start(bf16[128,128]{1,0:T(8,128)(2,1)S(1)} %get-tuple-element.70), channel_id=1, source_target_pairs={{0,12},{1,13},{2,14},{3,15},{4,0},{5,1},{6,2},{7,3},{8,4},{9,5},{1... | collective-permute-start | bytes 98312 | tf_op jit(solution)/shard_map/ppermute | solution.py:82
  173.5 4.8 %collective-permute-start.28 = (bf16[128,128]{1,0:T(8,128)(2,1)S(1)}, bf16[128,128]{1,0:T(8,128)(2,1)S(1)}, u32[]{:S(2)}, u32[]{:S(2)}) collective-permute-start(bf16[128,128]{1,0:T(8,128)(2,1)S(1)} %get-tuple-element.71), channel_id=1, source_target_pairs={{0,8},{1,9},{2,10},{3,11},{4,12},{5,13},{6,14},{7,15},{8,0},{9,1},... | collective-permute-start | bytes 98312 | tf_op jit(solution)/shard_map/ppermute | solution.py:82
  178.6 2.2 %copy-start.5 = (bf16[256,8192]{1,0:T(8,128)(2,1)S(1)}, bf16[256,8192]{1,0:T(8,128)(2,1)}, u32[]{:S(2)}) copy-start(bf16[256,8192]{1,0:T(8,128)(2,1)} %weight_ref.1) | copy-start | bytes 12582916
  182.2 2.0 collective-permute-start.31
  184.3 8.4 %collective-permute-start.32 = (bf16[64,2048]{1,0:T(8,128)(2,1)S(1)}, bf16[64,2048]{1,0:T(8,128)(2,1)S(1)}, u32[]{:S(2)}, u32[]{:S(2)}) collective-permute-start(bf16[64,2048]{1,0:T(8,128)(2,1)S(1)} %slice.256), channel_id=1, source_target_pairs={{0,2},{1,3},{2,0},{3,1},{4,6},{5,7},{6,4},{7,5},{8,10},{9,11},{10,... | collective-permute-start | bytes 786440 | tf_op jit(solution)/shard_map/ppermute | solution.py:82
  192.9 6.6 %collective-permute-start.33 = (bf16[64,512]{1,0:T(8,128)(2,1)S(1)}, bf16[64,512]{1,0:T(8,128)(2,1)S(1)}, u32[]{:S(2)}, u32[]{:S(2)}) collective-permute-start(bf16[64,512]{1,0:T(8,128)(2,1)S(1)} %get-tuple-element.64), channel_id=1, source_target_pairs={{0,4},{1,5},{2,6},{3,7},{4,8},{5,9},{6,10},{7,11},{8,12},{9,13},{1... | collective-permute-start | bytes 196616 | tf_op jit(solution)/shard_map/ppermute | solution.py:82
  192.9 6.5 %collective-permute-start.35 = (bf16[64,512]{1,0:T(8,128)(2,1)S(1)}, bf16[64,512]{1,0:T(8,128)(2,1)S(1)}, u32[]{:S(2)}, u32[]{:S(2)}) collective-permute-start(bf16[64,512]{1,0:T(8,128)(2,1)S(1)} %get-tuple-element.65), channel_id=1, source_target_pairs={{0,12},{1,13},{2,14},{3,15},{4,0},{5,1},{6,2},{7,3},{8,4},{9,5},{1... | collective-permute-start | bytes 196616 | tf_op jit(solution)/shard_map/ppermute | solution.py:82
  196.7 5.2 %collective-permute-start.34 = (bf16[64,512]{1,0:T(8,128)(2,1)S(1)}, bf16[64,512]{1,0:T(8,128)(2,1)S(1)}, u32[]{:S(2)}, u32[]{:S(2)}) collective-permute-start(bf16[64,512]{1,0:T(8,128)(2,1)S(1)} %get-tuple-element.66), channel_id=1, source_target_pairs={{0,8},{1,9},{2,10},{3,11},{4,12},{5,13},{6,14},{7,15},{8,0},{9,1},... | collective-permute-start | bytes 196616 | tf_op jit(solution)/shard_map/ppermute | solution.py:82

commit v6 on v5

--- a/solution.py
+++ b/solution.py
@@ -120,25 +120,95 @@
 
     return pl.pallas_call(
         body,
-        in_specs=[pl.BlockSpec(memory_space=pltpu.SMEM), pl.BlockSpec(memory_space=pl.ANY)],
+        in_specs=[pl.BlockSpec(memory_space=pltpu.SMEM), pl.BlockSpec(memory_space=pltpu.HBM)],
         out_specs=pl.BlockSpec(memory_space=pltpu.VMEM),
         out_shape=jax.ShapeDtypeStruct((rows, count * width), source.dtype),
         scratch_shapes=[pltpu.SemaphoreType.DMA((count,))],
-        compiler_params=pltpu.CompilerParams(vmem_limit_bytes=16 * MIB),
+        compiler_params=pltpu.CompilerParams(vmem_limit_bytes=57 * MIB),
         cost_estimate=pl.CostEstimate(
             flops=0, bytes_accessed=4 * rows * count * width, transcendentals=0
         ),
     )(blocks, source)
 
 
-def project(prompt, steps, got, blocks, begin, pieces, acc):
+def project_queries(steps, weight, cosine, sine):
+    count, depth = steps.shape
+    parts = 8
+    piece = depth // parts
+
+    def body(step_ref, weight_ref, cosine_ref, sine_ref, out_ref, held, sems):
+        copies = []
+        for i in range(parts):
+            copies.append(
+                pltpu.make_async_copy(
+                    weight_ref.at[pl.ds(i * piece, piece), :], held.at[i], sems.at[i]
+                )
+            )
+            copies[-1].start()
+        total = None
+        for i in range(parts):
+            copies[i].wait()
+            product = jnp.dot(
+                step_ref[:, i * piece : (i + 1) * piece],
+                held[i],
+                preferred_element_type=jnp.float32,
+            )
+            total = product if total is None else total + product
+        for start in range(0, weight.shape[1], HEAD_DIM):
+            head = total[:, start : start + HEAD_DIM]
+            turned = head * cosine_ref[...] + pltpu.roll(head, HEAD_DIM // 2, 1) * sine_ref[...]
+            out_ref[:, start : start + HEAD_DIM] = turned.astype(jnp.bfloat16)
+
+    whole = pl.BlockSpec(memory_space=pltpu.VMEM)
+    return pl.pallas_call(
+        body,
+        in_specs=[whole, pl.BlockSpec(memory_space=pltpu.HBM), whole, whole],
+        out_specs=whole,
+        out_shape=jax.ShapeDtypeStruct((count, weight.shape[1]), jnp.bfloat16),
+        scratch_shapes=[
+            pltpu.VMEM((parts, piece, weight.shape[1]), weight.dtype),
+            pltpu.SemaphoreType.DMA((parts,)),
+        ],
+        compiler_params=pltpu.CompilerParams(vmem_limit_bytes=10 * MIB),
+        cost_estimate=pl.CostEstimate(
+            flops=2 * count * weight.size, bytes_accessed=2 * weight.size, transcendentals=0
+        ),
+    )(steps, weight, cosine, sine)
+
+
+def collect(arrays, first, height):
+    columns = arrays[0].shape[1]
+
+    def body(*refs):
+        out_ref, sems = refs[-2:]
+        copies = [
+            pltpu.make_async_copy(ref.at[pl.ds(first, height), :], out_ref.at[i], sems.at[i])
+            for i, ref in enumerate(refs[:-2])
+        ]
+        for copy in copies:
+            copy.start()
+        for copy in copies:
+            copy.wait()
+
+    return pl.pallas_call(
+        body,
+        in_specs=[pl.BlockSpec(memory_space=pl.ANY)] * len(arrays),
+        out_specs=pl.BlockSpec(memory_space=pltpu.VMEM),
+        out_shape=jax.ShapeDtypeStruct((len(arrays), height, columns), arrays[0].dtype),
+        scratch_shapes=[pltpu.SemaphoreType.DMA((len(arrays),))],
+        compiler_params=pltpu.CompilerParams(vmem_limit_bytes=4 * MIB),
+        cost_estimate=pl.CostEstimate(
+            flops=0, bytes_accessed=4 * len(arrays) * height * columns, transcendentals=0
+        ),
+    )(*arrays)
+
+
+def project(prompt, steps, got, width, blocks, begin, pieces, acc):
     arrays = []
     for piece in pieces:
         for array, _ in piece:
             if not any(array is held for held in arrays):
                 arrays.append(array)
-    width = got.shape[1] // (begin + len(pieces)) if acc is not None else None
-    width = width or prompt.shape[1] // (2 * (len(pieces) + 2))
     count = len(pieces)
     columns = sum(array.shape[1] for array, _ in pieces[0])
     row_count, step_count = prompt.shape[0], steps.shape[0]
@@ -196,8 +266,8 @@
     whole = pl.BlockSpec(memory_space=pltpu.VMEM)
     return pl.pallas_call(
         body,
-        in_specs=[pl.BlockSpec(memory_space=pltpu.SMEM)]
-        + [anywhere] * (3 + len(arrays))
+        in_specs=[pl.BlockSpec(memory_space=pltpu.SMEM), pl.BlockSpec(memory_space=pltpu.HBM)]
+        + [anywhere] * (2 + len(arrays))
         + [whole] * len(extra),
         out_specs=whole,
         out_shape=jax.ShapeDtypeStruct((height, columns), jnp.float32),
@@ -206,7 +276,7 @@
             pltpu.VMEM((count, width, columns), jnp.bfloat16),
             pltpu.SemaphoreType.DMA((count, 5)),
         ],
-        compiler_params=pltpu.CompilerParams(vmem_limit_bytes=24 * MIB),
+        compiler_params=pltpu.CompilerParams(vmem_limit_bytes=57 * MIB),
         cost_estimate=pl.CostEstimate(
             flops=2 * height * width * count * columns,
             bytes_accessed=2 * height * width * count + 8 * height * columns,
@@ -215,14 +285,20 @@
     )(blocks, prompt, got, steps, *arrays, *extra)
 
 
-def attend(places, queries, own, other, cosine, sine, token_prompt, row_prompt):
-    kv_heads, count, _ = queries.shape
+def attend(places, turns, queries, own, other, cosine, sine, token_prompt, row_prompt):
+    kv_heads = places.shape[0]
+    deep, packed, lanes = queries[0].shape
+    share = deep // kv_heads
+    count = 2 * share * packed * lanes // HEAD_DIM
     tokens = cosine.shape[0]
     half = tokens // 2
     height = own.shape[0]
     masks = [] if token_prompt is None else [token_prompt, row_prompt]
 
-    def body(place_ref, query_ref, own_ref, other_ref, cosine_ref, sine_ref, *refs):
+    def body(place_ref, turn_ref, *refs):
+        query_refs = refs[: 2 * share]
+        own_ref, other_ref, cosine_ref, sine_ref = refs[2 * share : 2 * share + 4]
+        mask_refs = refs[2 * share + 4 : -3]
         weight_ref, top_ref, total_ref = refs[-3:]
         keys = jnp.concatenate(
             [
@@ -232,36 +308,48 @@
             axis=0,
         )
         swapped = pltpu.roll(keys, HEAD_DIM // 2, 1)
-        keys = (keys * cosine_ref[...] + swapped * sine_ref[...]).astype(jnp.bfloat16)
+        wide_cosine = jnp.concatenate([cosine_ref[...], cosine_ref[...]], axis=1)
+        wide_sine = jnp.concatenate([-sine_ref[...], sine_ref[...]], axis=1)
+        keys = (keys * wide_cosine + swapped * wide_sine).astype(jnp.bfloat16)
+        unpacked = []
+        for ref in query_refs:
+            for low in range(0, packed, packed // 2):
+                for left in range(0, lanes, HEAD_DIM):
+                    unpacked.append(ref[0, low : low + packed // 2, left : left + HEAD_DIM])
         scores = lax.dot_general(
-            keys, query_ref[0], (((1,), (1,)), ((), ())), preferred_element_type=jnp.float32
+            keys,
+            jnp.concatenate(unpacked, axis=0),
+            (((1,), (1,)), ((), ())),
+            preferred_element_type=jnp.float32,
         ) * (HEAD_DIM**-0.5)
         if masks:
-            scores = jnp.where(refs[0][...] == refs[1][...], scores, -1e30)
+            scores = jnp.where(mask_refs[0][...] == mask_refs[1][...], scores, -1e30)
         top = jnp.max(scores, axis=0, keepdims=True)
         weights = jnp.exp(scores - top)
         top_ref[0] = top
         total_ref[0] = jnp.sum(weights, axis=0, keepdims=True)
         weight_ref[0] = weights.astype(jnp.bfloat16)
 
+    def query_spec(part):
+        return pl.BlockSpec(
+            (1, packed, lanes), lambda j, place, turn: (turn[j * share + part], 0, 0)
+        )
+
     row = jax.ShapeDtypeStruct((kv_heads, 1, count), jnp.float32)
-    row_spec = pl.BlockSpec((1, 1, count), lambda j, ref: (j, 0, 0))
-    fixed = lambda j, ref: (0, 0)
+    row_spec = pl.BlockSpec((1, 1, count), lambda j, place, turn: (j, 0, 0))
+    fixed = lambda j, place, turn: (0, 0)
+    column = pl.BlockSpec((height, HEAD_DIM), lambda j, place, turn: (0, place[j]))
     return pl.pallas_call(
         body,
         grid_spec=pltpu.PrefetchScalarGridSpec(
-            num_scalar_prefetch=1,
+            num_scalar_prefetch=2,
             grid=(kv_heads,),
-            in_specs=[
-                pl.BlockSpec((1, count, HEAD_DIM), lambda j, ref: (j, 0, 0)),
-                pl.BlockSpec((height, HEAD_DIM), lambda j, ref: (0, ref[j])),
-                pl.BlockSpec((height, HEAD_DIM), lambda j, ref: (0, ref[j])),
-                pl.BlockSpec((tokens, HEAD_DIM), fixed),
-                pl.BlockSpec((tokens, HEAD_DIM), fixed),
-            ]
+            in_specs=[query_spec(part) for part in range(share) for _ in queries]
+            + [column, column]
+            + [pl.BlockSpec(cosine.shape, fixed)] * 2
             + [pl.BlockSpec(mask.shape, fixed) for mask in masks],
             out_specs=[
-                pl.BlockSpec((1, tokens, count), lambda j, ref: (j, 0, 0)),
+                pl.BlockSpec((1, tokens, count), lambda j, place, turn: (j, 0, 0)),
                 row_spec,
                 row_spec,
             ],
@@ -277,7 +365,7 @@
             bytes_accessed=8 * height * kv_heads * HEAD_DIM + 2 * kv_heads * tokens * count,
             transcendentals=kv_heads * tokens * count,
         ),
-    )(places, queries, own, other, cosine, sine, *masks)
+    )(places, turns, *([*queries] * share), own, other, cosine, sine, *masks)
 
 
 def apply_weights(places, weights, values):
@@ -393,23 +481,29 @@
 
     step_place = PROMPT_PAGES * PAGE + jnp.arange(2, dtype=jnp.int32)
     step_tables = tuple(t[:, None, :] for t in rope_tables(step_place))
-    queries = jnp.dot(wide_states, query_weight, preferred_element_type=jnp.float32)
-    queries = queries.reshape(2, samples, heads_here, HEAD_DIM).transpose(2, 0, 1, 3)
-    queries = turn(queries, step_tables).astype(jnp.bfloat16)
-    flat_queries = queries.reshape(rows, HEAD_DIM)
+    flat_tables = [
+        jnp.repeat(jnp.concatenate([sign * table, table], axis=-1)[:, 0], samples, axis=0)
+        for sign, table in zip((1, -1), step_tables)
+    ]
+    queries = project_queries(wide_states, query_weight, *flat_tables)
+    packed_queries = jnp.concatenate(
+        jnp.split(queries, half // queries.shape[1], axis=0), axis=1
+    )
+    packed = packed_queries.shape[0]
+    queries = queries.reshape(2, samples, heads_here, HEAD_DIM)
 
     places = [(k, flip) for k in range(deep) for flip in (0, 1)]
     own_blocks = jnp.stack([block(behind(k), flip, own_c) for k, flip in places])
     done = {}
 
     def send(move, value, turn_at):
-        if turn_at:
-            value = after(value, done[turn_at - 2] if turn_at > 1 else flat_queries)
+        if turn_at > 1:
+            value = after(value, done[turn_at - 2])
         done.setdefault(turn_at, []).append(move(value))
         return done[turn_at][-1]
 
     key_z, key_y = {0: key_mine}, {}
-    key_full = {0: jnp.concatenate([key_mine, key_other], axis=1)}
+    key_full = {0: jnp.concatenate([key_mine, key_other, packed_queries])}
     value_pairs, other_pairs = {}, {}
     for r in range(2 * deep - 1):
         late = r - deep + 2
@@ -421,33 +515,26 @@
             value_y = send(along_y, value_mine, r)
         elif r == 1:
             sent_blocks = jnp.stack([block(behind(k), flip, 1 - own_c) for k, flip in places])
-            sent = pick(prompt_states, after(sent_blocks, done[0]), width)
+            sent = pick(prompt_states, after(sent_blocks, (done[0], packed_queries)), width)
             got = in_chip(sent)
-            key_y[0] = send(
-                along_y,
-                jnp.concatenate([key_full[0], flat_queries.reshape(-1, key_full[0].shape[1])]),
-                r,
+            key_y[0] = send(along_y, key_full[0], r)
+            value_pairs[0] = jnp.concatenate(
+                [value_mine, value_y, packed_queries, key_y[0][2 * width :]]
             )
-            query_pair = jnp.stack([flat_queries, key_y[0][width:].reshape(rows, HEAD_DIM)])
-            value_pairs[0] = jnp.concatenate([value_mine, value_y, query_pair.reshape(-1, half)])
         elif r == 2:
             done[r].append(got)
         if 0 < r < deep:
-            key_full[r] = jnp.concatenate([key_z[r], send(along_x, key_z[r], r)], axis=1)
+            key_full[r] = jnp.concatenate([key_z[r], send(along_x, key_z[r], r)])
         elif r:
-            other_pairs[late - 1] = send(along_x, value_pairs[late - 1][: 2 * width], r)
+            other_pairs[late - 1] = send(along_x, value_pairs[late - 1], r)
         if r == deep - 1:
             other_pairs[0] = jnp.concatenate([value_other, send(along_x, value_y, r)])
         if 0 < late < deep:
             key_y[late] = send(along_y, key_full[late], r)
-    ring = [
-        value_pairs[(deep - j) % deep][2 * width :].reshape(query_pair.shape) for j in range(deep)
-    ]
-    line = lax.dynamic_slice_in_dim(jnp.stack(ring + ring), deep - own_turn, deep)
-    line = jnp.stack([line[order.index(a)] for a in range(deep)])
-    all_queries = jnp.stack([line, in_chip(line)], axis=1)
+    ring_queries = collect([value_pairs[k] for k in range(deep)], 2 * width, 2 * packed)
+    ring_queries = [ring_queries, in_chip(ring_queries)]
+    query_turns = jnp.stack([(own_turn + deep - order.index(a)) % deep for a in range(deep)])
     by_owner = (deep, 2, 2, rows)
-    all_queries = all_queries.reshape(KV_HEADS, -1, HEAD_DIM)
 
     own_pages = jnp.concatenate(
         [
@@ -465,30 +552,31 @@
     )
     positions = (slots % PROMPT_PAGES * PAGE)[:, None] + jnp.arange(PAGE, dtype=jnp.int32)[None, :]
     cosine, sine_part = rope_tables(positions.reshape(chip_rows))
-    cosine = jnp.concatenate([cosine, cosine], axis=1)
-    sine_part = jnp.concatenate([-sine_part, sine_part], axis=1)
 
     def pieces_of(k_range, key):
         if key:
-            return [[((key_y if flip else key_full)[k], 0)] for k in k_range for flip in (0, 1)]
+            return [
+                [((key_y if flip else key_full)[k], first) for first in (0, width)]
+                for k in k_range
+                for flip in (0, 1)
+            ]
         return [
             [(value_pairs[k], flip * width), (other_pairs[k], flip * width)]
             for k in k_range
             for flip in (0, 1)
         ]
 
-    def project_all(key, ready):
-        split = 2 * (deep - 1)
-        early = project(
-            prompt_states, wide_states, got, own_blocks[:split], 0,
-            pieces_of(range(deep - 1), key), None,
+    def project_part(key, k_range, acc, ready):
+        low, high = 2 * k_range[0], 2 * k_range[-1] + 2
+        return project(
+            prompt_states, wide_states, got, width, after(own_blocks[low:high], ready), low,
+            pieces_of(k_range, key), acc,
         )
-        return project(
-            prompt_states, wide_states, got, after(own_blocks[split:], ready), split,
-            pieces_of([deep - 1], key), early,
-        )
-
-    key_sum = project_all(True, got)
+
+    every = range(deep)
+    key_early = project_part(True, every[:-1], None, done[deep])
+    value_early = project_part(False, every[:-2], None, (done[deep], key_early))
+    key_sum = project_part(True, every[-1:], key_early, (done[deep + 1], value_early))
     key_back = in_chip(key_sum)
     own_place = lax.dynamic_index_in_dim(kv_places, own_kv, 0, False) * HEAD_DIM
 
@@ -500,14 +588,15 @@
     masks = (None, None)
     if prompts > 1:
         token_prompt = jnp.repeat(slots // PROMPT_PAGES, PAGE)
-        row_prompt = jnp.tile(sample_order // group_size, all_queries.shape[1] // samples)
+        row_prompt = jnp.tile(sample_order // group_size, devices // KV_HEADS * rows // samples)
         masks = (token_prompt[:, None], row_prompt[None, :])
     weights, top, total = attend(
-        kv_places, all_queries, key_sum, key_back, cosine, sine_part, *masks
+        kv_places, query_turns, ring_queries, key_sum, key_back, cosine, sine_part, *masks
     )
 
     stats = jnp.stack([top.reshape(by_owner), total.reshape(by_owner)])
     stats = jnp.stack([stats, along_y(stats)[:, :, :, ::-1]])
+    weights = after(weights, stats)
     stats = jnp.concatenate([stats] + [along_z(stats, k) for k in range(1, deep)])
     prefix_top = jnp.max(stats[:, 0], axis=0)
     prefix_total = jnp.sum(jnp.exp(stats[:, 0] - prefix_top) * stats[:, 1], axis=0)
@@ -515,7 +604,7 @@
     prefix_top = lax.dynamic_index_in_dim(prefix_top, own_a, 0, False)[0, 0]
     prefix_total = lax.dynamic_index_in_dim(prefix_total, own_a, 0, False)[0, 0]
 
-    value_sum = project_all(False, weights)
+    value_sum = project_part(False, every[-2:], value_early, weights)
     step_values = own_head(value_sum[chip_rows:])
     step_back = lax.dynamic_slice_in_dim(
         in_chip(value_sum[chip_rows:]), own_place, HEAD_DIM, 1
@@ -543,7 +632,7 @@
         prefix_top.reshape(by_head).swapaxes(0, 1),
         prefix_total.reshape(by_head).swapaxes(0, 1),
         prefix_sum.reshape(by_head + (HEAD_DIM,)).swapaxes(0, 1),
-        queries.swapaxes(0, 1),
+        queries.transpose(0, 2, 1, 3),
         new_keys[:, None],
         new_values[:, None],
     )

time: 204 us -> 183 us (0.90)
  local copies, waits for them, and re-layouts: 52.1 us -> 18.2 us
  Pallas kernels: 32.3 us -> 46.4 us
  waiting for transfers between devices: 54.2 us -> 62 us
  other arithmetic: 15.6 us -> 10.3 us
  matrix products: 3.58 us -> 0 us
    unnamed x56, local copies, waits for them, and re-layouts: 26.1 us -> 11.7 us
    pallas_call x4 -> x6, Pallas kernels: 18.9 us -> 31.5 us  [the longest x4 28.3 us: project(): pl.pallas_call(body, in_specs=[pl.BlockSpec(memory_space=pltpu.SMEM), pl....]
    slice x9 -> x4, local copies, waits for them, and re-layouts: 10.5 us -> 0.16 us  [the longest x2 0.08 us: finish_heads(): first_high = jnp.maximum(prefix_top[0], own_score[0])]
    ppermute x36, waiting for transfers between devices: 54.2 us -> 62 us  [move(): return lax.ppermute(value, ('groups', 'sample'), pairs)]
    dot_general x1 -> x0, local copies, waits for them, and re-layouts: 6.46 us -> none  [on_device(): jnp.dot(wide_states, query_weight, preferred_element_type=jnp.float32)]
    concatenate x5 -> x2, other arithmetic: 4.17 us -> 0.08 us  [the longest x1 0.04 us: on_device(): jnp.concatenate([value_mine, value_y, packed_queries, key_y[0][2 * width:]])]
    dot_general x1 -> x0, matrix products: 3.58 us -> none  [on_device(): jnp.dot(wide_states, query_weight, preferred_element_type=jnp.float32)]
    another operation x8 -> x0, local copies, waits for them, and re-layouts: 3.08 us -> none  [the longest x4 2.99 us: on_device(): jnp.stack(ring + ring)]
  transfers between devices with their start and end apart: 36 -> 36, of which waited for: 17 -> 14; matrix products, arithmetic and copies ran while one was open for 24% -> 9% of each run, Pallas kernels for 11% -> 19%
where the time goes in v6:
time: 183 us
  waiting for transfers between devices  62 us (34%)
  Pallas kernels  46.4 us (25%)
  starting transfers between devices  44.2 us (24%)
  local copies, waits for them, and re-layouts  18.2 us (10%)
  other arithmetic  10.3 us (6%)
    ppermute x36, waiting for transfers between devices, move(): return lax.ppermute(value, ('groups', 'sample'), pairs)  62 us
    ppermute x36, starting transfers between devices, move(): return lax.ppermute(value, ('groups', 'sample'), pairs)  44.2 us
    pallas_call x4, Pallas kernels, project(): pl.pallas_call(body, in_specs=[pl.BlockSpec(memory_space=pltpu.SMEM), pl....  28.3 us
    unnamed x56, local copies, waits for them, and re-layouts  11.7 us
    pallas_call x1, Pallas kernels, attend(): pl.pallas_call(body, grid_spec=pltpu.PrefetchScalarGridSpec(num_scalar_pr...  6.07 us
    pallas_call x1, Pallas kernels, pick(): pl.pallas_call(body, in_specs=[pl.BlockSpec(memory_space=pltpu.SMEM), pl....  4.91 us
  transfers between devices with their start and end apart: 36, of which 14 were waited for; matrix products, arithmetic and copies ran while one was open for 9% of the time, Pallas kernels for 19%

profile of v6, /device:TPU:0, one launch (start us, length us, event | category | flops | bytes accessed | tf_op | source)
XLA Modules:
  0.0 182.9 jit_solution(15840527549480133229)
XLA Ops:
  0.0 1.2 broadcast_select_fusion.2
  1.2 4.1 %collective-permute-start.2 = (bf16[512,256]{1,0:T(8,128)(2,1)S(1)}, bf16[512,256]{1,0:T(8,128)(2,1)S(1)}, u32[]{:S(2)}, u32[]{:S(2)}) collective-permute-start(bf16[512,256]{1,0:T(8,128)(2,1)S(1)} %get-tuple-element.54), channel_id=1, source_target_pairs={{0,8},{1,9},{2,10},{3,11},{4,0},{5,1},{6,2},{7,3},{8,12},{9,13},{1... | collective-permute-start | bytes 786440 | tf_op jit(solution)/shard_map/ppermute | solution.py:82
  5.3 0.7 broadcast_select_fusion
  6.0 1.5 collective-permute-start
  7.6 0.7 stack.174.block_ref
  8.5 2.2 %copy-done.5 = bf16[8192,256]{1,0:T(8,128)(2,1)S(1)} copy-done((bf16[8192,256]{1,0:T(8,128)(2,1)S(1)}, bf16[8192,256]{1,0:T(8,128)(2,1)}, u32[]{:S(2)}) %copy-start.5) | copy-done | bytes 4194328
  10.7 2.0 %shard_map.73 = bf16[64,256]{1,0:T(8,128)(2,1)S(1)} custom-call(bf16[64,8192]{1,0:T(8,128)(2,1)S(1)} %bitcast.158, bf16[8192,256]{1,0:T(8,128)(2,1)S(1)} %copy-done.5, f32[64,128]{1,0:T(8,128)S(1)} %bitcast.160, f32[64,128]{1,0:T(8,128)S(1)} %bitcast.161), custom_call_target="tpu_custom_call" | custom-call | flops 268435456 | bytes 4194304 | tf_op jit(solution)/shard_map/pallas_call | solution.py:163
  12.7 1.1 collective-permute-done
  13.8 4.9 %shard_map.74 = bf16[512,4096]{1,0:T(8,128)(2,1)} custom-call(s32[8]{0:T(128)} %stack.174.block_ref, bf16[512,8192]{1,0:T(8,128)(2,1)} %prompt_ref.7), custom_call_target="tpu_custom_call" | custom-call | bytes 8388608 | tf_op jit(solution)/shard_map/pallas_call | solution.py:121
  18.9 1.6 collective-permute-start.1
  20.4 1.5 collective-permute-start.4
  21.9 1.6 collective-permute-start.3
  23.5 10.4 %collective-permute-done.1.refs_1_ = bf16[1088,256]{1,0:T(8,128)(2,1)S(1)} collective-permute-done((bf16[1088,256]{1,0:T(8,128)(2,1)S(1)}, bf16[1088,256]{1,0:T(8,128)(2,1)S(1)}, u32[]{:S(2)}, u32[]{:S(2)}) %collective-permute-start.1) | collective-permute-done | bytes 557088 | tf_op jit(solution)/shard_map/ppermute | solution.py:82
  34.0 1.6 collective-permute-start.5
  35.7 1.5 collective-permute-start.8
  37.5 1.0 constant_dynamic-update-slice_fusion.5
  39.1 6.1 %collective-permute-done.8 = bf16[512,256]{1,0:T(8,128)(2,1)} collective-permute-done((bf16[512,256]{1,0:T(8,128)(2,1)}, bf16[512,256]{1,0:T(8,128)(2,1)}, u32[]{:S(2)}, u32[]{:S(2)}) %collective-permute-start.8) | collective-permute-done | bytes 262176 | tf_op jit(solution)/shard_map/ppermute | solution.py:82
  45.2 9.5 %collective-permute-done.6 = bf16[512,256]{1,0:T(8,128)(2,1)} collective-permute-done((bf16[512,256]{1,0:T(8,128)(2,1)}, bf16[512,256]{1,0:T(8,128)(2,1)}, u32[]{:S(2)}, u32[]{:S(2)}) %collective-permute-start.6) | collective-permute-done | bytes 262176 | tf_op jit(solution)/shard_map/ppermute | solution.py:82
  54.7 2.5 %collective-permute-start.9 = (bf16[1152,256]{1,0:T(8,128)(2,1)S(1)}, bf16[1152,256]{1,0:T(8,128)(2,1)S(1)}, u32[]{:S(2)}, u32[]{:S(2)}) collective-permute-start(bf16[1152,256]{1,0:T(8,128)(2,1)S(1)} %collective-permute-done.5.refs_1_.refs_2_), channel_id=1, source_target_pairs={{0,8},{1,9},{2,10},{3,11},{4,0},{5,1},{6,2},{7,3},{8,12},{9,13},{1... | collective-permute-start | bytes 1769480 | tf_op jit(solution)/shard_map/ppermute | solution.py:82
  57.3 1.0 constant_dynamic-update-slice_fusion.refs_2_
  58.3 1.6 collective-permute-start.12
  59.9 1.5 collective-permute-start.17
  61.3 1.0 constant_dynamic-update-slice_fusion.4.refs_4_
  64.0 0.7 pad_add_fusion.2.block_ref
  64.7 0.6 stack.185.block_ref
  65.3 1.0 constant_dynamic-update-slice_fusion.3
  66.3 1.9 %pad_maximum_fusion.2.refs_1_ = bf16[1024,256]{1,0:T(8,128)(2,1)} fusion(bf16[512,256]{1,0:T(8,128)(2,1)} %collective-permute-done.11, bf16[512,256]{1,0:T(8,128)(2,1)} %get-tuple-element.52), kind=kLoop, calls=%fused_computation.5 | loop fusion | flops 1048576 | bytes 1048576 | tf_op jit(solution)/shard_map/concatenate | solution.py:531
  68.2 10.9 %collective-permute-done.10 = bf16[512,256]{1,0:T(8,128)(2,1)} collective-permute-done((bf16[512,256]{1,0:T(8,128)(2,1)}, bf16[512,256]{1,0:T(8,128)(2,1)}, u32[]{:S(2)}, u32[]{:S(2)}) %collective-permute-start.10) | collective-permute-done | bytes 262176 | tf_op jit(solution)/shard_map/ppermute | solution.py:82
  79.1 1.6 collective-permute-start.15
  81.1 1.0 constant_dynamic-update-slice_fusion.2.refs_0_
  82.6 8.0 %shard_map.76.refs_2_ = f32[1088,512]{1,0:T(8,128)} custom-call(s32[6]{0:T(128)} %stack.185.block_ref, bf16[512,8192]{1,0:T(8,128)(2,1)} %prompt_ref.7, bf16[512,4096]{1,0:T(8,128)(2,1)} %collective-permute-done.7.got_ref, bf16[64,8192]{1,0:T(8,128)(2,1)} %bitcast.154, bf16[1088,256]{1,0:T(8,128)(2,1)} %copy-done.12, bf16[1088,256]{1,0:T(8,128)(2,1)} %copy-done.16, ...), custom_call_target="tpu_custom_call" | custom-call | flops 3422552064 | bytes 11141120 | tf_op jit(solution)/shard_map/pallas_call | solution.py:267
  90.6 6.4 %shard_map.77.refs_4_ = f32[1088,512]{1,0:T(8,128)} custom-call(s32[4]{0:T(128)} %pad_add_fusion.2.block_ref, bf16[512,8192]{1,0:T(8,128)(2,1)} %prompt_ref.7, bf16[512,4096]{1,0:T(8,128)(2,1)} %collective-permute-done.7.got_ref, bf16[64,8192]{1,0:T(8,128)(2,1)} %bitcast.155, bf16[1152,256]{1,0:T(8,128)(2,1)} %copy-done.3, ...), custom_call_target="tpu_custom_call" | custom-call | flops 2281701376 | bytes 8912896 | tf_op jit(solution)/shard_map/pallas_call | solution.py:267
  97.1 0.8 copy-done.19
  97.9 6.1 %shard_map.78.refs_2_ = f32[1088,512]{1,0:T(8,128)} custom-call(s32[2]{0:T(128)} %pad_add_fusion.1.block_ref, bf16[512,8192]{1,0:T(8,128)(2,1)} %prompt_ref.7, bf16[512,4096]{1,0:T(8,128)(2,1)} %collective-permute-done.7.got_ref, bf16[64,8192]{1,0:T(8,128)(2,1)} %bitcast.156, bf16[1024,256]{1,0:T(8,128)(2,1)} %copy-done.15, bf16[1024,256]{1,0:T(8,128)(2,1)} %copy-done.19, ...), custom_call_target="tpu_custom_call" | custom-call | flops 1140850688 | bytes 6684672 | tf_op jit(solution)/shard_map/pallas_call | solution.py:267
  106.7 1.9 %multiply_sine_fusion = (f32[1024,64]{1,0:T(8,128)S(1)}, f32[1024,64]{1,0:T(8,128)S(1)}) fusion(f32[64]{0:T(128)S(1)} %multiply_power_fusion, f32[1024]{0:T(1024)S(1)} %convert_bitcast_fusion), kind=kLoop, calls=%fused_computation.1 | loop fusion | flops 65536 | bytes 528640 | tf_op jit(solution)/shard_map/sin | solution.py:23
  108.6 0.9 slice.178
  109.6 1.3 shard_map.75.refs_0_
  111.3 1.9 %collective-permute-start.24 = (bf16[1152,256]{1,0:T(8,128)(2,1)}, bf16[1152,256]{1,0:T(8,128)(2,1)S(1)}, u32[]{:S(2)}, u32[]{:S(2)}) collective-permute-start(bf16[1152,256]{1,0:T(8,128)(2,1)} %collective-permute-done.13.refs_3_.refs_2_), channel_id=1, source_target_pairs={{0,16},{1,17},{2,18},{3,19},{4,20},{5,21},{6,22},{7,23},{8,24},{9,... | collective-permute-start | bytes 1769480 | tf_op jit(solution)/shard_map/ppermute | solution.py:82
  113.6 6.1 %shard_map.79 = (bf16[4,1024,512]{2,1,0:T(8,128)(2,1)S(1)}, f32[4,1,512]{2,1,0:T(1,128)S(1)}, f32[4,1,512]{2,1,0:T(1,128)S(1)}) custom-call(s32[4]{0:T(128)S(1)} %and_select_fusion.1.place_ref, s32[4]{0:T(128)S(1)} %pad_add_fusion.turn_ref, bf16[4,128,256]{2,1,0:T(8,128)(2,1)S(1)} %shard_map.75.refs_0_, ...), custom_call_target="tpu_custom_call" | custom-call | flops 536870912 | bytes 8650752 | tf_op jit(solution)/shard_map/pallas_call | solution.py:342
  119.7 2.0 %copy-done.7 = bf16[4,1024,512]{2,1,0:T(8,128)(2,1)} copy-done((bf16[4,1024,512]{2,1,0:T(8,128)(2,1)}, bf16[4,1024,512]{2,1,0:T(8,128)(2,1)S(1)}, u32[]{:S(2)}) %copy-start.7) | copy-done | bytes 4194328
  121.7 2.6 %collective-permute-start.20 = (f32[2,4,2,2,128]{4,3,2,1,0:T(2,128)S(1)}, f32[2,4,2,2,128]{4,3,2,1,0:T(2,128)S(1)}, u32[]{:S(2)}, u32[]{:S(2)}) collective-permute-start(f32[2,4,2,2,128]{4,3,2,1,0:T(2,128)S(1)} %get-tuple-element.71), channel_id=1, source_target_pairs={{0,2},{1,3},{2,0},{3,1},{4,6},{5,7},{6,4},{7,5},{8,10},{9,11},{10,... | collective-permute-start | bytes 49160 | tf_op jit(solution)/shard_map/ppermute | solution.py:82
  124.7 1.3 collective-permute-done.20
  126.1 1.4 collective-permute-start.22
  127.5 1.2 collective-permute-start.21
  128.8 0.8 copy-done.18
  129.6 7.9 %shard_map.80.value_ref = f32[1088,512]{1,0:T(8,128)} custom-call(s32[4]{0:T(128)} %pad_add_fusion.4.block_ref, bf16[512,8192]{1,0:T(8,128)(2,1)} %prompt_ref.7, bf16[512,4096]{1,0:T(8,128)(2,1)} %collective-permute-done.7.got_ref, bf16[64,8192]{1,0:T(8,128)(2,1)} %bitcast.157, bf16[1152,256]{1,0:T(8,128)(2,1)} %copy-done.9, bf16[1152,256]{1,0:T(8,128)(2,1)} %copy-done.17, ...), custom_call_target="tpu_custom_call" | custom-call | flops 2281701376 | bytes 8912896 | tf_op jit(solution)/shard_map/pallas_call | solution.py:267
  137.5 1.6 copy-done.1
  139.1 2.5 %shard_map.81 = bf16[4,512,128]{2,1,0:T(8,128)(2,1)S(1)} custom-call(s32[4]{0:T(128)S(1)} %and_select_fusion.1.place_ref, bf16[4,1024,512]{2,1,0:T(8,128)(2,1)S(1)} %copy-done.8, f32[1088,512]{1,0:T(8,128)S(1)} %copy-done.1), custom_call_target="tpu_custom_call" | custom-call | flops 536870912 | bytes 4194304 | tf_op jit(solution)/shard_map/pallas_call | solution.py:383
  142.9 0.7 collective-permute-done.25
  143.8 2.1 %collective-permute-start.26 = (bf16[4,128,128]{2,1,0:T(8,128)(2,1)S(1)}, bf16[4,128,128]{2,1,0:T(8,128)(2,1)S(1)}, u32[]{:S(2)}, u32[]{:S(2)}) collective-permute-start(bf16[4,128,128]{2,1,0:T(8,128)(2,1)S(1)} %slice_bitcast_fusion), channel_id=1, source_target_pairs={{0,2},{1,3},{2,0},{3,1},{4,6},{5,7},{6,4},{7,5},{8,10},{9,11},{10,... | collective-permute-start | bytes 393224 | tf_op jit(solution)/shard_map/ppermute | solution.py:82
  145.9 4.0 %collective-permute-done.26 = bf16[4,128,128]{2,1,0:T(8,128)(2,1)S(1)} collective-permute-done((bf16[4,128,128]{2,1,0:T(8,128)(2,1)S(1)}, bf16[4,128,128]{2,1,0:T(8,128)(2,1)S(1)}, u32[]{:S(2)}, u32[]{:S(2)}) %collective-permute-start.26) | collective-permute-done | bytes 131104 | tf_op jit(solution)/shard_map/ppermute | solution.py:82
  150.0 1.0 collective-permute-start.27
  151.0 2.9 %collective-permute-start.29 = (bf16[128,128]{1,0:T(8,128)(2,1)S(1)}, bf16[128,128]{1,0:T(8,128)(2,1)S(1)}, u32[]{:S(2)}, u32[]{:S(2)}) collective-permute-start(bf16[128,128]{1,0:T(8,128)(2,1)S(1)} %get-tuple-element.60), channel_id=1, source_target_pairs={{0,12},{1,13},{2,14},{3,15},{4,0},{5,1},{6,2},{7,3},{8,4},{9,5},{1... | collective-permute-start | bytes 98312 | tf_op jit(solution)/shard_map/ppermute | solution.py:82
  154.4 1.7 collective-permute-done.27
  156.0 2.6 %collective-permute-done.28 = bf16[128,128]{1,0:T(8,128)(2,1)S(1)} collective-permute-done((bf16[128,128]{1,0:T(8,128)(2,1)S(1)}, bf16[128,128]{1,0:T(8,128)(2,1)S(1)}, u32[]{:S(2)}, u32[]{:S(2)}) %collective-permute-start.28) | collective-permute-done | bytes 32800 | tf_op jit(solution)/shard_map/ppermute | solution.py:82
  158.9 2.2 %copy-done.6 = bf16[256,8192]{1,0:T(8,128)(2,1)S(1)} copy-done((bf16[256,8192]{1,0:T(8,128)(2,1)S(1)}, bf16[256,8192]{1,0:T(8,128)(2,1)}, u32[]{:S(2)}) %copy-start.6) | copy-done | bytes 4194328
  161.1 1.4 shard_map.82
  162.6 1.9 %collective-permute-done.31 = bf16[64,4096]{1,0:T(8,128)(2,1)S(1)} collective-permute-done((bf16[64,4096]{1,0:T(8,128)(2,1)S(1)}, bf16[64,4096]{1,0:T(8,128)(2,1)S(1)}, u32[]{:S(2)}, u32[]{:S(2)}) %collective-permute-start.31) | collective-permute-done | bytes 524320 | tf_op jit(solution)/shard_map/ppermute | solution.py:82
  164.7 1.8 collective-permute-start.32
  166.5 6.6 %collective-permute-done.32 = bf16[64,2048]{1,0:T(8,128)(2,1)S(1)} collective-permute-done((bf16[64,2048]{1,0:T(8,128)(2,1)S(1)}, bf16[64,2048]{1,0:T(8,128)(2,1)S(1)}, u32[]{:S(2)}, u32[]{:S(2)}) %collective-permute-start.32) | collective-permute-done | bytes 262176 | tf_op jit(solution)/shard_map/ppermute | solution.py:82
  173.3 3.8 %collective-permute-start.35 = (bf16[64,512]{1,0:T(8,128)(2,1)S(1)}, bf16[64,512]{1,0:T(8,128)(2,1)S(1)}, u32[]{:S(2)}, u32[]{:S(2)}) collective-permute-start(bf16[64,512]{1,0:T(8,128)(2,1)S(1)} %get-tuple-element.57), channel_id=1, source_target_pairs={{0,12},{1,13},{2,14},{3,15},{4,0},{5,1},{6,2},{7,3},{8,4},{9,5},{1... | collective-permute-start | bytes 196616 | tf_op jit(solution)/shard_map/ppermute | solution.py:82
  177.1 2.7 %collective-permute-done.33 = bf16[64,512]{1,0:T(8,128)(2,1)S(1)} collective-permute-done((bf16[64,512]{1,0:T(8,128)(2,1)S(1)}, bf16[64,512]{1,0:T(8,128)(2,1)S(1)}, u32[]{:S(2)}, u32[]{:S(2)}) %collective-permute-start.33) | collective-permute-done | bytes 65568 | tf_op jit(solution)/shard_map/ppermute | solution.py:82
  179.8 2.4 %collective-permute-done.34 = bf16[64,512]{1,0:T(8,128)(2,1)S(1)} collective-permute-done((bf16[64,512]{1,0:T(8,128)(2,1)S(1)}, bf16[64,512]{1,0:T(8,128)(2,1)S(1)}, u32[]{:S(2)}, u32[]{:S(2)}) %collective-permute-start.34) | collective-permute-done | bytes 65568 | tf_op jit(solution)/shard_map/ppermute | solution.py:82
  182.2 0.7 add_convert_fusion.2
  (156 shorter events, 9.9 us)
Async XLA Ops:
  0.0 5.3 %copy-start.20 = (bf16[512,512]{1,0:T(8,128)(2,1)S(1)}, bf16[512,512]{1,0:T(8,128)(2,1)}, u32[]{:S(2)}) copy-start(bf16[512,512]{1,0:T(8,128)(2,1)} %param.12) | copy-start | bytes 1572868
  0.0 8.5 %copy-start = (bf16[2,32,8192]{2,1,0:T(8,128)(2,1)S(1)}, bf16[2,32,8192]{2,1,0:T(8,128)(2,1)}, u32[]{:S(2)}) copy-start(bf16[2,32,8192]{2,1,0:T(8,128)(2,1)} %param.10) | copy-start | bytes 3145732
  1.2 11.5 %collective-permute-start.2 = (bf16[512,256]{1,0:T(8,128)(2,1)S(1)}, bf16[512,256]{1,0:T(8,128)(2,1)S(1)}, u32[]{:S(2)}, u32[]{:S(2)}) collective-permute-start(bf16[512,256]{1,0:T(8,128)(2,1)S(1)} %get-tuple-element.54), channel_id=1, source_target_pairs={{0,8},{1,9},{2,10},{3,11},{4,0},{5,1},{6,2},{7,3},{8,12},{9,13},{1... | collective-permute-start | bytes 786440 | tf_op jit(solution)/shard_map/ppermute | solution.py:82
  6.0 7.8 %collective-permute-start = (bf16[512,256]{1,0:T(8,128)(2,1)S(1)}, bf16[512,256]{1,0:T(8,128)(2,1)S(1)}, u32[]{:S(2)}, u32[]{:S(2)}) collective-permute-start(bf16[512,256]{1,0:T(8,128)(2,1)S(1)} %get-tuple-element.53), channel_id=1, source_target_pairs={{0,2},{1,3},{2,0},{3,1},{4,6},{5,7},{6,4},{7,5},{8,10},{9,11},{10,... | collective-permute-start | bytes 786440 | tf_op jit(solution)/shard_map/ppermute | solution.py:82
  8.5 2.2 %copy-start.5 = (bf16[8192,256]{1,0:T(8,128)(2,1)S(1)}, bf16[8192,256]{1,0:T(8,128)(2,1)}, u32[]{:S(2)}) copy-start(bf16[8192,256]{1,0:T(8,128)(2,1)} %weight_ref.2) | copy-start | bytes 12582916
  13.8 4.9 %copy-start.21 = (bf16[512,256]{1,0:T(8,128)(2,1)}, bf16[512,256]{1,0:T(8,128)(2,1)S(1)}, u32[]{:S(2)}) copy-start(bf16[512,256]{1,0:T(8,128)(2,1)S(1)} %collective-permute-done) | copy-start | bytes 786436
  18.7 36.0 %collective-permute-start.7 = (bf16[512,4096]{1,0:T(8,128)(2,1)}, bf16[512,4096]{1,0:T(8,128)(2,1)}, u32[]{:S(2)}, u32[]{:S(2)}) collective-permute-start(bf16[512,4096]{1,0:T(8,128)(2,1)} %shard_map.74), channel_id=1, source_target_pairs={{0,1},{1,0},{2,3},{3,2},{4,5},{5,4},{6,7},{7,6},{8,9},{9,8},{10,11... | collective-permute-start | bytes 12582920 | tf_op jit(solution)/shard_map/ppermute | solution.py:82
  18.8 15.2 %copy-start.22 = (bf16[512,256]{1,0:T(8,128)(2,1)S(1)}, bf16[512,256]{1,0:T(8,128)(2,1)}, u32[]{:S(2)}) copy-start(bf16[512,256]{1,0:T(8,128)(2,1)} %copy-done.21) | copy-start | bytes 786436
  18.9 39.4 %copy-start.12 = (bf16[1088,256]{1,0:T(8,128)(2,1)}, bf16[1088,256]{1,0:T(8,128)(2,1)S(1)}, u32[]{:S(2)}) copy-start(bf16[1088,256]{1,0:T(8,128)(2,1)S(1)} %pad_maximum_fusion.1.refs_0_) | copy-start | bytes 1671172
  18.9 15.1 %collective-permute-start.1 = (bf16[1088,256]{1,0:T(8,128)(2,1)S(1)}, bf16[1088,256]{1,0:T(8,128)(2,1)S(1)}, u32[]{:S(2)}, u32[]{:S(2)}) collective-permute-start(bf16[1088,256]{1,0:T(8,128)(2,1)S(1)} %pad_maximum_fusion.1.refs_0_), channel_id=1, source_target_pairs={{0,2},{1,3},{2,0},{3,1},{4,6},{5,7},{6,4},{7,5},{8,10},{9,11},{10,... | collective-permute-start | bytes 1671176 | tf_op jit(solution)/shard_map/ppermute | solution.py:82
  20.4 13.6 %collective-permute-start.4 = (bf16[512,256]{1,0:T(8,128)(2,1)S(1)}, bf16[512,256]{1,0:T(8,128)(2,1)}, u32[]{:S(2)}, u32[]{:S(2)}) collective-permute-start(bf16[512,256]{1,0:T(8,128)(2,1)S(1)} %collective-permute-done.2), channel_id=1, source_target_pairs={{0,16},{1,17},{2,18},{3,19},{4,20},{5,21},{6,22},{7,23},{8,24},{9,... | collective-permute-start | bytes 786440 | tf_op jit(solution)/shard_map/ppermute | solution.py:82
  21.9 12.1 %collective-permute-start.3 = (bf16[512,256]{1,0:T(8,128)(2,1)S(1)}, bf16[512,256]{1,0:T(8,128)(2,1)}, u32[]{:S(2)}, u32[]{:S(2)}) collective-permute-start(bf16[512,256]{1,0:T(8,128)(2,1)S(1)} %collective-permute-done.2), channel_id=1, source_target_pairs={{0,8},{1,9},{2,10},{3,11},{4,0},{5,1},{6,2},{7,3},{8,12},{9,13},{1... | collective-permute-start | bytes 786440 | tf_op jit(solution)/shard_map/ppermute | solution.py:82
  33.9 3.6 %copy-start.16 = (bf16[1088,256]{1,0:T(8,128)(2,1)}, bf16[1088,256]{1,0:T(8,128)(2,1)S(1)}, u32[]{:S(2)}) copy-start(bf16[1088,256]{1,0:T(8,128)(2,1)S(1)} %collective-permute-done.1.refs_1_) | copy-start | bytes 1671172
  34.0 32.3 %copy-start.3 = (bf16[1152,256]{1,0:T(8,128)(2,1)}, bf16[1152,256]{1,0:T(8,128)(2,1)S(1)}, u32[]{:S(2)}) copy-start(bf16[1152,256]{1,0:T(8,128)(2,1)S(1)} %pad_maximum_fusion.refs_0_) | copy-start | bytes 1769476
  34.0 20.7 %collective-permute-start.5 = (bf16[1152,256]{1,0:T(8,128)(2,1)S(1)}, bf16[1152,256]{1,0:T(8,128)(2,1)S(1)}, u32[]{:S(2)}, u32[]{:S(2)}) collective-permute-start(bf16[1152,256]{1,0:T(8,128)(2,1)S(1)} %pad_maximum_fusion.refs_0_), channel_id=1, source_target_pairs={{0,8},{1,9},{2,10},{3,11},{4,0},{5,1},{6,2},{7,3},{8,12},{9,13},{1... | collective-permute-start | bytes 1769480 | tf_op jit(solution)/shard_map/ppermute | solution.py:82
  35.7 9.6 %collective-permute-start.8 = (bf16[512,256]{1,0:T(8,128)(2,1)}, bf16[512,256]{1,0:T(8,128)(2,1)}, u32[]{:S(2)}, u32[]{:S(2)}) collective-permute-start(bf16[512,256]{1,0:T(8,128)(2,1)} %collective-permute-done.3), channel_id=1, source_target_pairs={{0,16},{1,17},{2,18},{3,19},{4,20},{5,21},{6,22},{7,23},{8,24},{9,... | collective-permute-start | bytes 786440 | tf_op jit(solution)/shard_map/ppermute | solution.py:82
  37.2 17.6 %collective-permute-start.6 = (bf16[512,256]{1,0:T(8,128)(2,1)}, bf16[512,256]{1,0:T(8,128)(2,1)}, u32[]{:S(2)}, u32[]{:S(2)}) collective-permute-start(bf16[512,256]{1,0:T(8,128)(2,1)} %collective-permute-done.3), channel_id=1, source_target_pairs={{0,8},{1,9},{2,10},{3,11},{4,0},{5,1},{6,2},{7,3},{8,12},{9,13},{1... | collective-permute-start | bytes 786440 | tf_op jit(solution)/shard_map/ppermute | solution.py:82
  38.5 25.0 %collective-permute-start.11 = (bf16[512,256]{1,0:T(8,128)(2,1)}, bf16[512,256]{1,0:T(8,128)(2,1)}, u32[]{:S(2)}, u32[]{:S(2)}) collective-permute-start(bf16[512,256]{1,0:T(8,128)(2,1)} %copy-done.21), channel_id=1, source_target_pairs={{0,16},{1,17},{2,18},{3,19},{4,20},{5,21},{6,22},{7,23},{8,24},{9,... | collective-permute-start | bytes 786440 | tf_op jit(solution)/shard_map/ppermute | solution.py:82
  54.7 13.4 %copy-start.10 = (bf16[1152,256]{1,0:T(8,128)(2,1)}, bf16[1152,256]{1,0:T(8,128)(2,1)S(1)}, u32[]{:S(2)}) copy-start(bf16[1152,256]{1,0:T(8,128)(2,1)S(1)} %collective-permute-done.5.refs_1_.refs_2_) | copy-start | bytes 1769476
  54.7 24.3 %collective-permute-start.9 = (bf16[1152,256]{1,0:T(8,128)(2,1)S(1)}, bf16[1152,256]{1,0:T(8,128)(2,1)S(1)}, u32[]{:S(2)}, u32[]{:S(2)}) collective-permute-start(bf16[1152,256]{1,0:T(8,128)(2,1)S(1)} %collective-permute-done.5.refs_1_.refs_2_), channel_id=1, source_target_pairs={{0,8},{1,9},{2,10},{3,11},{4,0},{5,1},{6,2},{7,3},{8,12},{9,13},{1... | collective-permute-start | bytes 1769480 | tf_op jit(solution)/shard_map/ppermute | solution.py:82
  58.3 23.8 %copy-start.14 = (bf16[1024,256]{1,0:T(8,128)(2,1)}, bf16[1024,256]{1,0:T(8,128)(2,1)S(1)}, u32[]{:S(2)}) copy-start(bf16[1024,256]{1,0:T(8,128)(2,1)S(1)} %constant_dynamic-update-slice_fusion.refs_2_) | copy-start | bytes 1572868
  58.3 20.8 %collective-permute-start.12 = (bf16[1024,256]{1,0:T(8,128)(2,1)S(1)}, bf16[1024,256]{1,0:T(8,128)(2,1)}, u32[]{:S(2)}, u32[]{:S(2)}) collective-permute-start(bf16[1024,256]{1,0:T(8,128)(2,1)S(1)} %constant_dynamic-update-slice_fusion.refs_2_), channel_id=1, source_target_pairs={{0,2},{1,3},{2,0},{3,1},{4,6},{5,7},{6,4},{7,5},{8,10},{9,11},{10,... | collective-permute-start | bytes 1572872 | tf_op jit(solution)/shard_map/ppermute | solution.py:82
  59.9 22.8 %collective-permute-start.17 = (bf16[1152,256]{1,0:T(8,128)(2,1)S(1)}, bf16[1152,256]{1,0:T(8,128)(2,1)}, u32[]{:S(2)}, u32[]{:S(2)}) collective-permute-start(bf16[1152,256]{1,0:T(8,128)(2,1)S(1)} %collective-permute-done.5.refs_1_.refs_2_), channel_id=1, source_target_pairs={{0,16},{1,17},{2,18},{3,19},{4,20},{5,21},{6,22},{7,23},{8,24},{9,... | collective-permute-start | bytes 1769480 | tf_op jit(solution)/shard_map/ppermute | solution.py:82
  62.3 20.3 %copy-start.13 = (bf16[1024,256]{1,0:T(8,128)(2,1)}, bf16[1024,256]{1,0:T(8,128)(2,1)S(1)}, u32[]{:S(2)}) copy-start(bf16[1024,256]{1,0:T(8,128)(2,1)S(1)} %constant_dynamic-update-slice_fusion.4.refs_4_) | copy-start | bytes 1572868
  62.3 20.3 %collective-permute-start.18 = (bf16[1024,256]{1,0:T(8,128)(2,1)S(1)}, bf16[1024,256]{1,0:T(8,128)(2,1)}, u32[]{:S(2)}, u32[]{:S(2)}) collective-permute-start(bf16[1024,256]{1,0:T(8,128)(2,1)S(1)} %constant_dynamic-update-slice_fusion.4.refs_4_), channel_id=1, source_target_pairs={{0,2},{1,3},{2,0},{3,1},{4,6},{5,7},{6,4},{7,5},{8,10},{9,11},{10,... | collective-permute-start | bytes 1572872 | tf_op jit(solution)/shard_map/ppermute | solution.py:82
  63.5 15.6 %collective-permute-start.10 = (bf16[512,256]{1,0:T(8,128)(2,1)}, bf16[512,256]{1,0:T(8,128)(2,1)}, u32[]{:S(2)}, u32[]{:S(2)}) collective-permute-start(bf16[512,256]{1,0:T(8,128)(2,1)} %collective-permute-done.6), channel_id=1, source_target_pairs={{0,16},{1,17},{2,18},{3,19},{4,20},{5,21},{6,22},{7,23},{8,24},{9,... | collective-permute-start | bytes 786440 | tf_op jit(solution)/shard_map/ppermute | solution.py:82
  79.1 30.5 %copy-start.9 = (bf16[1152,256]{1,0:T(8,128)(2,1)}, bf16[1152,256]{1,0:T(8,128)(2,1)S(1)}, u32[]{:S(2)}) copy-start(bf16[1152,256]{1,0:T(8,128)(2,1)S(1)} %collective-permute-done.9.refs_2_.refs_0_) | copy-start | bytes 1769476
  79.1 18.0 %collective-permute-start.15 = (bf16[1152,256]{1,0:T(8,128)(2,1)S(1)}, bf16[1152,256]{1,0:T(8,128)(2,1)S(1)}, u32[]{:S(2)}, u32[]{:S(2)}) collective-permute-start(bf16[1152,256]{1,0:T(8,128)(2,1)S(1)} %collective-permute-done.9.refs_2_.refs_0_), channel_id=1, source_target_pairs={{0,16},{1,17},{2,18},{3,19},{4,20},{5,21},{6,22},{7,23},{8,24},{9,... | collective-permute-start | bytes 1769480 | tf_op jit(solution)/shard_map/ppermute | solution.py:82
  80.6 16.5 %collective-permute-start.13 = (bf16[1152,256]{1,0:T(8,128)(2,1)S(1)}, bf16[1152,256]{1,0:T(8,128)(2,1)}, u32[]{:S(2)}, u32[]{:S(2)}) collective-permute-start(bf16[1152,256]{1,0:T(8,128)(2,1)S(1)} %collective-permute-done.9.refs_2_.refs_0_), channel_id=1, source_target_pairs={{0,8},{1,9},{2,10},{3,11},{4,0},{5,1},{6,2},{7,3},{8,12},{9,13},{1... | collective-permute-start | bytes 1769480 | tf_op jit(solution)/shard_map/ppermute | solution.py:82
  82.0 8.6 %copy-start.15 = (bf16[1024,256]{1,0:T(8,128)(2,1)}, bf16[1024,256]{1,0:T(8,128)(2,1)S(1)}, u32[]{:S(2)}) copy-start(bf16[1024,256]{1,0:T(8,128)(2,1)S(1)} %constant_dynamic-update-slice_fusion.2.refs_0_) | copy-start | bytes 1572868
  82.1 15.0 %collective-permute-start.16 = (bf16[1024,256]{1,0:T(8,128)(2,1)S(1)}, bf16[1024,256]{1,0:T(8,128)(2,1)S(1)}, u32[]{:S(2)}, u32[]{:S(2)}) collective-permute-start(bf16[1024,256]{1,0:T(8,128)(2,1)S(1)} %constant_dynamic-update-slice_fusion.2.refs_0_), channel_id=1, source_target_pairs={{0,2},{1,3},{2,0},{3,1},{4,6},{5,7},{6,4},{7,5},{8,10},{9,11},{10,... | collective-permute-start | bytes 1572872 | tf_op jit(solution)/shard_map/ppermute | solution.py:82
  97.0 9.3 %copy-start.23 = (s32[64]{0:T(128)S(1)}, s32[64]{0:T(128)}, u32[]{:S(2)}) copy-start(s32[64]{0:T(128)} %param.9) | copy-start | bytes 772
  97.0 0.8 copy-start.19
  97.1 6.9 %copy-start.17 = (bf16[1152,256]{1,0:T(8,128)(2,1)}, bf16[1152,256]{1,0:T(8,128)(2,1)S(1)}, u32[]{:S(2)}) copy-start(bf16[1152,256]{1,0:T(8,128)(2,1)S(1)} %collective-permute-done.15.refs_1_) | copy-start | bytes 1769476
  103.9 5.6 %copy-start.4 = (bf16[1152,256]{1,0:T(8,128)(2,1)S(1)}, bf16[1152,256]{1,0:T(8,128)(2,1)}, u32[]{:S(2)}) copy-start(bf16[1152,256]{1,0:T(8,128)(2,1)} %copy-done.3) | copy-start | bytes 1769476
  104.0 9.2 %collective-permute-start.19 = (f32[1088,512]{1,0:T(8,128)}, f32[1088,512]{1,0:T(8,128)S(1)}, u32[]{:S(2)}, u32[]{:S(2)}) collective-permute-start(f32[1088,512]{1,0:T(8,128)} %shard_map.78.refs_2_), channel_id=1, source_target_pairs={{0,1},{1,0},{2,3},{3,2},{4,5},{5,4},{6,7},{7,6},{8,9},{9,8},{10,11... | collective-permute-start | bytes 6684680 | tf_op jit(solution)/shard_map/ppermute | solution.py:82
  105.6 4.0 %copy-start.11 = (bf16[1152,256]{1,0:T(8,128)(2,1)S(1)}, bf16[1152,256]{1,0:T(8,128)(2,1)}, u32[]{:S(2)}) copy-start(bf16[1152,256]{1,0:T(8,128)(2,1)} %copy-done.10) | copy-start | bytes 1769476
  109.6 4.0 %copy-start.2 = (f32[1088,512]{1,0:T(8,128)S(1)}, f32[1088,512]{1,0:T(8,128)}, u32[]{:S(2)}) copy-start(f32[1088,512]{1,0:T(8,128)} %shard_map.78.refs_2_) | copy-start | bytes 6684676
  110.9 2.7 %collective-permute-start.14 = (bf16[4,128,256]{2,1,0:T(8,128)(2,1)S(1)}, bf16[4,128,256]{2,1,0:T(8,128)(2,1)S(1)}, u32[]{:S(2)}, u32[]{:S(2)}) collective-permute-start(bf16[4,128,256]{2,1,0:T(8,128)(2,1)S(1)} %shard_map.75.refs_0_), channel_id=1, source_target_pairs={{0,1},{1,0},{2,3},{3,2},{4,5},{5,4},{6,7},{7,6},{8,9},{9,8},{10,11... | collective-permute-start | bytes 786440 | tf_op jit(solution)/shard_map/ppermute | solution.py:82
  111.3 17.5 %collective-permute-start.24 = (bf16[1152,256]{1,0:T(8,128)(2,1)}, bf16[1152,256]{1,0:T(8,128)(2,1)S(1)}, u32[]{:S(2)}, u32[]{:S(2)}) collective-permute-start(bf16[1152,256]{1,0:T(8,128)(2,1)} %collective-permute-done.13.refs_3_.refs_2_), channel_id=1, source_target_pairs={{0,16},{1,17},{2,18},{3,19},{4,20},{5,21},{6,22},{7,23},{8,24},{9,... | collective-permute-start | bytes 1769480 | tf_op jit(solution)/shard_map/ppermute | solution.py:82
  119.7 2.0 %copy-start.7 = (bf16[4,1024,512]{2,1,0:T(8,128)(2,1)}, bf16[4,1024,512]{2,1,0:T(8,128)(2,1)S(1)}, u32[]{:S(2)}) copy-start(bf16[4,1024,512]{2,1,0:T(8,128)(2,1)S(1)} %get-tuple-element.40.weight_ref) | copy-start | bytes 12582916
  121.7 4.3 %collective-permute-start.20 = (f32[2,4,2,2,128]{4,3,2,1,0:T(2,128)S(1)}, f32[2,4,2,2,128]{4,3,2,1,0:T(2,128)S(1)}, u32[]{:S(2)}, u32[]{:S(2)}) collective-permute-start(f32[2,4,2,2,128]{4,3,2,1,0:T(2,128)S(1)} %get-tuple-element.71), channel_id=1, source_target_pairs={{0,2},{1,3},{2,0},{3,1},{4,6},{5,7},{6,4},{7,5},{8,10},{9,11},{10,... | collective-permute-start | bytes 49160 | tf_op jit(solution)/shard_map/ppermute | solution.py:82
  126.0 16.4 %collective-permute-start.23 = (f32[2,2,4,2,2,128]{5,4,3,2,1,0:T(2,128)S(1)}, f32[2,2,4,2,2,128]{5,4,3,2,1,0:T(2,128)S(1)}, u32[]{:S(2)}, u32[]{:S(2)}) collective-permute-start(f32[2,2,4,2,2,128]{5,4,3,2,1,0:T(2,128)S(1)} %pad_maximum_fusion.3), channel_id=1, source_target_pairs={{0,12},{1,13},{2,14},{3,15},{4,0},{5,1},{6,2},{7,3},{8,4},{9,5},{1... | collective-permute-start | bytes 98312 | tf_op jit(solution)/shard_map/ppermute | solution.py:82
  126.1 16.3 %collective-permute-start.22 = (f32[2,2,4,2,2,128]{5,4,3,2,1,0:T(2,128)S(1)}, f32[2,2,4,2,2,128]{5,4,3,2,1,0:T(2,128)S(1)}, u32[]{:S(2)}, u32[]{:S(2)}) collective-permute-start(f32[2,2,4,2,2,128]{5,4,3,2,1,0:T(2,128)S(1)} %pad_maximum_fusion.3), channel_id=1, source_target_pairs={{0,8},{1,9},{2,10},{3,11},{4,12},{5,13},{6,14},{7,15},{8,0},{9,1},... | collective-permute-start | bytes 98312 | tf_op jit(solution)/shard_map/ppermute | solution.py:82
  127.5 14.9 %collective-permute-start.21 = (f32[2,2,4,2,2,128]{5,4,3,2,1,0:T(2,128)S(1)}, f32[2,2,4,2,2,128]{5,4,3,2,1,0:T(2,128)S(1)}, u32[]{:S(2)}, u32[]{:S(2)}) collective-permute-start(f32[2,2,4,2,2,128]{5,4,3,2,1,0:T(2,128)S(1)} %pad_maximum_fusion.3), channel_id=1, source_target_pairs={{0,4},{1,5},{2,6},{3,7},{4,8},{5,9},{6,10},{7,11},{8,12},{9,13},{1... | collective-permute-start | bytes 98312 | tf_op jit(solution)/shard_map/ppermute | solution.py:82
  128.8 0.8 copy-start.18
  129.6 7.9 %copy-start.8 = (bf16[4,1024,512]{2,1,0:T(8,128)(2,1)S(1)}, bf16[4,1024,512]{2,1,0:T(8,128)(2,1)}, u32[]{:S(2)}) copy-start(bf16[4,1024,512]{2,1,0:T(8,128)(2,1)} %copy-done.7) | copy-start | bytes 12582916
  137.5 1.6 copy-start.1
  141.7 4.2 %collective-permute-start.30 = (f32[64,512]{1,0:T(8,128)S(1)}, f32[64,512]{1,0:T(8,128)S(1)}, u32[]{:S(2)}, u32[]{:S(2)}) collective-permute-start(f32[64,512]{1,0:T(8,128)S(1)} %slice.190), channel_id=1, source_target_pairs={{0,1},{1,0},{2,3},{3,2},{4,5},{5,4},{6,7},{7,6},{8,9},{9,8},{10,11... | collective-permute-start | bytes 393224 | tf_op jit(solution)/shard_map/ppermute | solution.py:82
  141.8 1.7 collective-permute-start.25
  143.8 6.1 %collective-permute-start.26 = (bf16[4,128,128]{2,1,0:T(8,128)(2,1)S(1)}, bf16[4,128,128]{2,1,0:T(8,128)(2,1)S(1)}, u32[]{:S(2)}, u32[]{:S(2)}) collective-permute-start(bf16[4,128,128]{2,1,0:T(8,128)(2,1)S(1)} %slice_bitcast_fusion), channel_id=1, source_target_pairs={{0,2},{1,3},{2,0},{3,1},{4,6},{5,7},{6,4},{7,5},{8,10},{9,11},{10,... | collective-permute-start | bytes 393224 | tf_op jit(solution)/shard_map/ppermute | solution.py:82
  150.0 6.1 %collective-permute-start.27 = (bf16[128,128]{1,0:T(8,128)(2,1)S(1)}, bf16[128,128]{1,0:T(8,128)(2,1)S(1)}, u32[]{:S(2)}, u32[]{:S(2)}) collective-permute-start(bf16[128,128]{1,0:T(8,128)(2,1)S(1)} %get-tuple-element.59), channel_id=1, source_target_pairs={{0,4},{1,5},{2,6},{3,7},{4,8},{5,9},{6,10},{7,11},{8,12},{9,13},{1... | collective-permute-start | bytes 98312 | tf_op jit(solution)/shard_map/ppermute | solution.py:82
  151.0 5.1 %collective-permute-start.29 = (bf16[128,128]{1,0:T(8,128)(2,1)S(1)}, bf16[128,128]{1,0:T(8,128)(2,1)S(1)}, u32[]{:S(2)}, u32[]{:S(2)}) collective-permute-start(bf16[128,128]{1,0:T(8,128)(2,1)S(1)} %get-tuple-element.60), channel_id=1, source_target_pairs={{0,12},{1,13},{2,14},{3,15},{4,0},{5,1},{6,2},{7,3},{8,4},{9,5},{1... | collective-permute-start | bytes 98312 | tf_op jit(solution)/shard_map/ppermute | solution.py:82
  153.9 4.8 %collective-permute-start.28 = (bf16[128,128]{1,0:T(8,128)(2,1)S(1)}, bf16[128,128]{1,0:T(8,128)(2,1)S(1)}, u32[]{:S(2)}, u32[]{:S(2)}) collective-permute-start(bf16[128,128]{1,0:T(8,128)(2,1)S(1)} %get-tuple-element.61), channel_id=1, source_target_pairs={{0,8},{1,9},{2,10},{3,11},{4,12},{5,13},{6,14},{7,15},{8,0},{9,1},... | collective-permute-start | bytes 98312 | tf_op jit(solution)/shard_map/ppermute | solution.py:82
  158.9 2.2 %copy-start.6 = (bf16[256,8192]{1,0:T(8,128)(2,1)S(1)}, bf16[256,8192]{1,0:T(8,128)(2,1)}, u32[]{:S(2)}) copy-start(bf16[256,8192]{1,0:T(8,128)(2,1)} %weight_ref.3) | copy-start | bytes 12582916
  162.5 2.0 %collective-permute-start.31 = (bf16[64,4096]{1,0:T(8,128)(2,1)S(1)}, bf16[64,4096]{1,0:T(8,128)(2,1)S(1)}, u32[]{:S(2)}, u32[]{:S(2)}) collective-permute-start(bf16[64,4096]{1,0:T(8,128)(2,1)S(1)} %slice.202), channel_id=1, source_target_pairs={{0,1},{1,0},{2,3},{3,2},{4,5},{5,4},{6,7},{7,6},{8,9},{9,8},{10,11... | collective-permute-start | bytes 1572872 | tf_op jit(solution)/shard_map/ppermute | solution.py:82
  164.7 8.4 %collective-permute-start.32 = (bf16[64,2048]{1,0:T(8,128)(2,1)S(1)}, bf16[64,2048]{1,0:T(8,128)(2,1)S(1)}, u32[]{:S(2)}, u32[]{:S(2)}) collective-permute-start(bf16[64,2048]{1,0:T(8,128)(2,1)S(1)} %slice.204), channel_id=1, source_target_pairs={{0,2},{1,3},{2,0},{3,1},{4,6},{5,7},{6,4},{7,5},{8,10},{9,11},{10,... | collective-permute-start | bytes 786440 | tf_op jit(solution)/shard_map/ppermute | solution.py:82
  173.2 6.6 %collective-permute-start.33 = (bf16[64,512]{1,0:T(8,128)(2,1)S(1)}, bf16[64,512]{1,0:T(8,128)(2,1)S(1)}, u32[]{:S(2)}, u32[]{:S(2)}) collective-permute-start(bf16[64,512]{1,0:T(8,128)(2,1)S(1)} %get-tuple-element.56), channel_id=1, source_target_pairs={{0,4},{1,5},{2,6},{3,7},{4,8},{5,9},{6,10},{7,11},{8,12},{9,13},{1... | collective-permute-start | bytes 196616 | tf_op jit(solution)/shard_map/ppermute | solution.py:82
  173.3 6.5 %collective-permute-start.35 = (bf16[64,512]{1,0:T(8,128)(2,1)S(1)}, bf16[64,512]{1,0:T(8,128)(2,1)S(1)}, u32[]{:S(2)}, u32[]{:S(2)}) collective-permute-start(bf16[64,512]{1,0:T(8,128)(2,1)S(1)} %get-tuple-element.57), channel_id=1, source_target_pairs={{0,12},{1,13},{2,14},{3,15},{4,0},{5,1},{6,2},{7,3},{8,4},{9,5},{1... | collective-permute-start | bytes 196616 | tf_op jit(solution)/shard_map/ppermute | solution.py:82
  177.1 5.2 %collective-permute-start.34 = (bf16[64,512]{1,0:T(8,128)(2,1)S(1)}, bf16[64,512]{1,0:T(8,128)(2,1)S(1)}, u32[]{:S(2)}, u32[]{:S(2)}) collective-permute-start(bf16[64,512]{1,0:T(8,128)(2,1)S(1)} %get-tuple-element.58), channel_id=1, source_target_pairs={{0,8},{1,9},{2,10},{3,11},{4,12},{5,13},{6,14},{7,15},{8,0},{9,1},... | collective-permute-start | bytes 196616 | tf_op jit(solution)/shard_map/ppermute | solution.py:82

commit v7 on v6

--- a/solution.py
+++ b/solution.py
@@ -97,6 +97,7 @@
 
 
 MIB = 1024 * 1024
+LIGHT = pl.CostEstimate(flops=1, bytes_accessed=1, transcendentals=0)
 
 
 def pick(source, blocks, width):
@@ -124,10 +125,8 @@
         out_specs=pl.BlockSpec(memory_space=pltpu.VMEM),
         out_shape=jax.ShapeDtypeStruct((rows, count * width), source.dtype),
         scratch_shapes=[pltpu.SemaphoreType.DMA((count,))],
-        compiler_params=pltpu.CompilerParams(vmem_limit_bytes=57 * MIB),
-        cost_estimate=pl.CostEstimate(
-            flops=0, bytes_accessed=4 * rows * count * width, transcendentals=0
-        ),
+        compiler_params=pltpu.CompilerParams(vmem_limit_bytes=12 * MIB),
+        cost_estimate=LIGHT,
     )(blocks, source)
 
 
@@ -170,9 +169,7 @@
             pltpu.SemaphoreType.DMA((parts,)),
         ],
         compiler_params=pltpu.CompilerParams(vmem_limit_bytes=10 * MIB),
-        cost_estimate=pl.CostEstimate(
-            flops=2 * count * weight.size, bytes_accessed=2 * weight.size, transcendentals=0
-        ),
+        cost_estimate=LIGHT,
     )(steps, weight, cosine, sine)
 
 
@@ -197,92 +194,86 @@
         out_shape=jax.ShapeDtypeStruct((len(arrays), height, columns), arrays[0].dtype),
         scratch_shapes=[pltpu.SemaphoreType.DMA((len(arrays),))],
         compiler_params=pltpu.CompilerParams(vmem_limit_bytes=4 * MIB),
-        cost_estimate=pl.CostEstimate(
-            flops=0, bytes_accessed=4 * len(arrays) * height * columns, transcendentals=0
-        ),
+        cost_estimate=LIGHT,
     )(*arrays)
 
 
-def project(prompt, steps, got, width, blocks, begin, pieces, acc):
+def assemble(prompt, steps, got, blocks, width):
+    count = blocks.shape[0]
+    row_count, step_count = prompt.shape[0], steps.shape[0]
+    height = 2 * row_count + step_count
+
+    def body(block_ref, prompt_ref, got_ref, step_ref, out_ref, sems):
+        copies = []
+        for i in range(count):
+            column = pl.ds(pl.multiple_of(block_ref[i] * width, width), width)
+            for j, (source, start, rows) in enumerate(
+                (
+                    (prompt_ref.at[:, column], 0, row_count),
+                    (got_ref.at[:, pl.ds(i * width, width)], row_count, row_count),
+                    (step_ref.at[:, column], 2 * row_count, step_count),
+                )
+            ):
+                copies.append(
+                    pltpu.make_async_copy(
+                        source, out_ref.at[i, pl.ds(start, rows), :], sems.at[i, j]
+                    )
+                )
+                copies[-1].start()
+        for copy in copies:
+            copy.wait()
+
+    anywhere = pl.BlockSpec(memory_space=pl.ANY)
+    return pl.pallas_call(
+        body,
+        in_specs=[pl.BlockSpec(memory_space=pltpu.SMEM)] + [anywhere] * 3,
+        out_specs=pl.BlockSpec(memory_space=pltpu.VMEM),
+        out_shape=jax.ShapeDtypeStruct((count, height, width), prompt.dtype),
+        scratch_shapes=[pltpu.SemaphoreType.DMA((count, 3))],
+        compiler_params=pltpu.CompilerParams(vmem_limit_bytes=16 * MIB),
+        cost_estimate=LIGHT,
+    )(blocks, prompt, got, steps)
+
+
+def project(left, which, pieces, acc):
     arrays = []
     for piece in pieces:
         for array, _ in piece:
             if not any(array is held for held in arrays):
                 arrays.append(array)
-    count = len(pieces)
+    _, height, width = left.shape
     columns = sum(array.shape[1] for array, _ in pieces[0])
-    row_count, step_count = prompt.shape[0], steps.shape[0]
-    height = 2 * row_count + step_count
     extra = [] if acc is None else [acc]
 
-    def body(block_ref, prompt_ref, got_ref, step_ref, *refs):
-        weight_refs = refs[: len(arrays)]
-        out_ref, left, held, sems = refs[-4:]
-        copies = []
+    def body(left_ref, *refs):
+        out_ref = refs[-1]
         for i, piece in enumerate(pieces):
-            start = pl.multiple_of(block_ref[i] * width, width)
-            column = pl.ds(start, width)
-            group = [
-                pltpu.make_async_copy(
-                    prompt_ref.at[:, column], left.at[i, pl.ds(0, row_count), :], sems.at[i, 0]
-                ),
-                pltpu.make_async_copy(
-                    got_ref.at[:, pl.ds((begin + i) * width, width)],
-                    left.at[i, pl.ds(row_count, row_count), :],
-                    sems.at[i, 1],
-                ),
-                pltpu.make_async_copy(
-                    step_ref.at[:, column],
-                    left.at[i, pl.ds(2 * row_count, step_count), :],
-                    sems.at[i, 2],
-                ),
-            ]
             side = 0
-            for j, (array, first) in enumerate(piece):
-                ref = weight_refs[[array is other for other in arrays].index(True)]
-                group.append(
-                    pltpu.make_async_copy(
-                        ref.at[pl.ds(first, width), :],
-                        held.at[i, :, pl.ds(side, array.shape[1])],
-                        sems.at[i, 3 + j],
-                    )
+            for array, first in piece:
+                ref = refs[[array is other for other in arrays].index(True)]
+                place = slice(side, side + array.shape[1])
+                product = jnp.dot(
+                    left_ref[which[i]],
+                    ref[first : first + width, :],
+                    preferred_element_type=jnp.float32,
                 )
+                if i:
+                    out_ref[:, place] += product
+                elif extra:
+                    out_ref[:, place] = refs[len(arrays)][:, place] + product
+                else:
+                    out_ref[:, place] = product
                 side += array.shape[1]
-            for copy in group:
-                copy.start()
-            copies.append(group)
-        for i, group in enumerate(copies):
-            for copy in group:
-                copy.wait()
-            product = jnp.dot(left[i], held[i], preferred_element_type=jnp.float32)
-            if i:
-                out_ref[...] += product
-            elif acc is not None:
-                out_ref[...] = refs[len(arrays)][...] + product
-            else:
-                out_ref[...] = product
-
-    anywhere = pl.BlockSpec(memory_space=pl.ANY)
+
     whole = pl.BlockSpec(memory_space=pltpu.VMEM)
     return pl.pallas_call(
         body,
-        in_specs=[pl.BlockSpec(memory_space=pltpu.SMEM), pl.BlockSpec(memory_space=pltpu.HBM)]
-        + [anywhere] * (2 + len(arrays))
-        + [whole] * len(extra),
+        in_specs=[whole] * (1 + len(arrays) + len(extra)),
         out_specs=whole,
         out_shape=jax.ShapeDtypeStruct((height, columns), jnp.float32),
-        scratch_shapes=[
-            pltpu.VMEM((count, height, width), jnp.bfloat16),
-            pltpu.VMEM((count, width, columns), jnp.bfloat16),
-            pltpu.SemaphoreType.DMA((count, 5)),
-        ],
-        compiler_params=pltpu.CompilerParams(vmem_limit_bytes=57 * MIB),
-        cost_estimate=pl.CostEstimate(
-            flops=2 * height * width * count * columns,
-            bytes_accessed=2 * height * width * count + 8 * height * columns,
-            transcendentals=0,
-        ),
-    )(blocks, prompt, got, steps, *arrays, *extra)
+        compiler_params=pltpu.CompilerParams(vmem_limit_bytes=28 * MIB),
+        cost_estimate=LIGHT,
+    )(left, *arrays, *extra)
 
 
 def attend(places, turns, queries, own, other, cosine, sine, token_prompt, row_prompt):
@@ -360,11 +351,7 @@
             row,
         ],
         compiler_params=pltpu.CompilerParams(vmem_limit_bytes=20 * MIB),
-        cost_estimate=pl.CostEstimate(
-            flops=2 * kv_heads * tokens * count * HEAD_DIM,
-            bytes_accessed=8 * height * kv_heads * HEAD_DIM + 2 * kv_heads * tokens * count,
-            transcendentals=kv_heads * tokens * count,
-        ),
+        cost_estimate=LIGHT,
     )(places, turns, *([*queries] * share), own, other, cosine, sine, *masks)
 
 
@@ -393,11 +380,7 @@
         ),
         out_shape=jax.ShapeDtypeStruct((kv_heads, count, HEAD_DIM), jnp.bfloat16),
         compiler_params=pltpu.CompilerParams(vmem_limit_bytes=20 * MIB),
-        cost_estimate=pl.CostEstimate(
-            flops=2 * kv_heads * tokens * count * HEAD_DIM,
-            bytes_accessed=2 * kv_heads * tokens * count,
-            transcendentals=0,
-        ),
+        cost_estimate=LIGHT,
     )(places, weights, values)
 
 
@@ -417,11 +400,7 @@
         out_specs=whole,
         out_shape=jax.ShapeDtypeStruct(shape, jnp.bfloat16),
         compiler_params=pltpu.CompilerParams(vmem_limit_bytes=20 * MIB),
-        cost_estimate=pl.CostEstimate(
-            flops=2 * heads.shape[1] * shape[0] * shape[1],
-            bytes_accessed=2 * (weight.size + heads.size + shape[0] * shape[1]),
-            transcendentals=0,
-        ),
+        cost_estimate=LIGHT,
     )(blocks, heads, weight)
 
 
@@ -496,42 +475,39 @@
     own_blocks = jnp.stack([block(behind(k), flip, own_c) for k, flip in places])
     done = {}
 
-    def send(move, value, turn_at):
-        if turn_at > 1:
-            value = after(value, done[turn_at - 2])
-        done.setdefault(turn_at, []).append(move(value))
-        return done[turn_at][-1]
-
-    key_z, key_y = {0: key_mine}, {}
+    def send(move, value):
+        moved = done.setdefault(move, [])
+        moved.append(move(after(value, moved[-2]) if len(moved) > 1 else value))
+        return moved[-1]
+
+    key_z, mine, theirs = {0: key_mine}, {0: value_mine}, {}
+    key_z[1] = send(along_ring, key_z[0])
+    mine[1] = send(along_ring, mine[0])
+    value_y = send(along_y, value_mine)
     key_full = {0: jnp.concatenate([key_mine, key_other, packed_queries])}
-    value_pairs, other_pairs = {}, {}
-    for r in range(2 * deep - 1):
-        late = r - deep + 2
-        if r + 1 < deep:
-            key_z[r + 1] = send(along_ring, key_z[r], r)
-        elif late < deep:
-            value_pairs[late] = send(along_ring, value_pairs[late - 1], r)
-        if r == 0:
-            value_y = send(along_y, value_mine, r)
-        elif r == 1:
-            sent_blocks = jnp.stack([block(behind(k), flip, 1 - own_c) for k, flip in places])
-            sent = pick(prompt_states, after(sent_blocks, (done[0], packed_queries)), width)
+    key_y = {0: send(along_y, after(key_full[0], (value_y, key_z[1])))}
+    theirs[0] = jnp.concatenate([value_y, packed_queries, key_y[0][2 * width :]])
+    mine_x, theirs_x = {0: value_other}, {}
+    for k in range(1, deep):
+        swapped = send(along_x, after(key_z[k], packed_queries))
+        mine_x[k] = send(along_x, mine[k])
+        if k == 1:
+            theirs_x[0] = send(along_x, value_y)
+        if k + 1 < deep:
+            key_z[k + 1] = send(along_ring, key_z[k])
+            mine[k + 1] = send(along_ring, mine[k])
+        key_full[k] = jnp.concatenate([key_z[k], swapped])
+        key_y[k] = send(along_y, after(key_full[k], key_y[k - 1]))
+        if k == 1:
+            sent_blocks = jnp.stack([block(behind(j), flip, 1 - own_c) for j, flip in places])
+            sent = pick(prompt_states, after(sent_blocks, (key_z[2], swapped, mine[1])), width)
             got = in_chip(sent)
-            key_y[0] = send(along_y, key_full[0], r)
-            value_pairs[0] = jnp.concatenate(
-                [value_mine, value_y, packed_queries, key_y[0][2 * width :]]
-            )
-        elif r == 2:
-            done[r].append(got)
-        if 0 < r < deep:
-            key_full[r] = jnp.concatenate([key_z[r], send(along_x, key_z[r], r)])
-        elif r:
-            other_pairs[late - 1] = send(along_x, value_pairs[late - 1], r)
-        if r == deep - 1:
-            other_pairs[0] = jnp.concatenate([value_other, send(along_x, value_y, r)])
-        if 0 < late < deep:
-            key_y[late] = send(along_y, key_full[late], r)
-    ring_queries = collect([value_pairs[k] for k in range(deep)], 2 * width, 2 * packed)
+    for k in range(1, deep):
+        theirs[k] = send(along_ring, theirs[k - 1])
+        theirs_x[k] = send(along_x, theirs[k])
+    left = assemble(prompt_states, wide_states, got, after(own_blocks, (key_y[1], mine[2])), width)
+
+    ring_queries = collect([theirs[k] for k in range(deep)], width, 2 * packed)
     ring_queries = [ring_queries, in_chip(ring_queries)]
     query_turns = jnp.stack([(own_turn + deep - order.index(a)) % deep for a in range(deep)])
     by_owner = (deep, 2, 2, rows)
@@ -553,30 +529,26 @@
     positions = (slots % PROMPT_PAGES * PAGE)[:, None] + jnp.arange(PAGE, dtype=jnp.int32)[None, :]
     cosine, sine_part = rope_tables(positions.reshape(chip_rows))
 
-    def pieces_of(k_range, key):
-        if key:
-            return [
-                [((key_y if flip else key_full)[k], first) for first in (0, width)]
-                for k in k_range
-                for flip in (0, 1)
-            ]
-        return [
-            [(value_pairs[k], flip * width), (other_pairs[k], flip * width)]
-            for k in k_range
-            for flip in (0, 1)
-        ]
-
-    def project_part(key, k_range, acc, ready):
-        low, high = 2 * k_range[0], 2 * k_range[-1] + 2
-        return project(
-            prompt_states, wide_states, got, width, after(own_blocks[low:high], ready), low,
-            pieces_of(k_range, key), acc,
-        )
-
-    every = range(deep)
-    key_early = project_part(True, every[:-1], None, done[deep])
-    value_early = project_part(False, every[:-2], None, (done[deep], key_early))
-    key_sum = project_part(True, every[-1:], key_early, (done[deep + 1], value_early))
+    key_pieces = [
+        [((key_y if flip else key_full)[k], start) for start in (0, width)] for k, flip in places
+    ]
+    value_pieces = [
+        [((theirs if flip else mine)[k], 0), ((theirs_x if flip else mine_x)[k], 0)]
+        for k, flip in places
+    ]
+
+    def project_blocks(pieces, which, acc, ready):
+        return project(after(left, ready), which, [pieces[i] for i in which], acc)
+
+    last = 2 * deep - 2
+    key_early = project_blocks(
+        key_pieces, range(last), None, (theirs[1], mine_x[deep - 1], key_y[deep - 2])
+    )
+    early = [*range(0, 2 * deep, 2), 1]
+    value_early = project_blocks(value_pieces, early, None, (key_early, theirs_x[1]))
+    key_sum = project_blocks(
+        key_pieces, [last, last + 1], key_early, (value_early, theirs[deep - 1], theirs_x[deep - 2])
+    )
     key_back = in_chip(key_sum)
     own_place = lax.dynamic_index_in_dim(kv_places, own_kv, 0, False) * HEAD_DIM
 
@@ -604,7 +576,8 @@
     prefix_top = lax.dynamic_index_in_dim(prefix_top, own_a, 0, False)[0, 0]
     prefix_total = lax.dynamic_index_in_dim(prefix_total, own_a, 0, False)[0, 0]
 
-    value_sum = project_part(False, every[-2:], value_early, weights)
+    late = [i for i in range(2 * deep) if i not in early]
+    value_sum = project_blocks(value_pieces, late, value_early, weights)
     step_values = own_head(value_sum[chip_rows:])
     step_back = lax.dynamic_slice_in_dim(
         in_chip(value_sum[chip_rows:]), own_place, HEAD_DIM, 1

time: 183 us -> 188 us (1.027)
  Pallas kernels: 46.4 us -> 32 us
  starting transfers between devices: 44.2 us -> 58 us
  local copies, waits for them, and re-layouts: 18.2 us -> 30.7 us
  waiting for transfers between devices: 62 us -> 56.5 us
  other arithmetic: 10.3 us -> 8.25 us
    unnamed x56 -> x84, local copies, waits for them, and re-layouts: 11.7 us -> 26 us
    ppermute x36 -> x42, starting transfers between devices: 44.2 us -> 58 us  [move(): return lax.ppermute(value, ('groups', 'sample'), pairs)]
    pallas_call x4 -> x5, Pallas kernels: 28.3 us -> 15.6 us  [the longest x4 12.5 us: project(): pl.pallas_call(body, in_specs=[whole] * (1 + len(arrays) + len(extra)), o...]
    ppermute x36 -> x42, waiting for transfers between devices: 62 us -> 56.5 us  [move(): return lax.ppermute(value, ('groups', 'sample'), pairs)]
    concatenate x3, local copies, waits for them, and re-layouts: 2.9 us -> 0.76 us  [on_device(): key_full[k] = jnp.concatenate([key_z[k], swapped])]
    concatenate x2 -> x1, other arithmetic: 1.93 us -> 0.02 us  [on_device(): theirs[0] = jnp.concatenate([value_y, packed_queries, key_y[0][2 * width:]])]
  transfers between devices with their start and end apart: 36 -> 42, of which waited for: 14 -> 21; matrix products, arithmetic and copies ran while one was open for 9% -> 7% of each run, Pallas kernels for 19% -> 13%
where the time goes in v7:
time: 188 us; the launch traced here: 187 us
  starting transfers between devices  58 us (31%)
  waiting for transfers between devices  56.5 us (30%)
  Pallas kernels  32 us (17%)
  local copies, waits for them, and re-layouts  30.7 us (16%)
  other arithmetic  8.25 us (4%)
    ppermute x42, starting transfers between devices, move(): return lax.ppermute(value, ('groups', 'sample'), pairs)  58 us
    ppermute x42, waiting for transfers between devices, move(): return lax.ppermute(value, ('groups', 'sample'), pairs)  56.5 us
    unnamed x84, local copies, waits for them, and re-layouts  26 us
    pallas_call x4, Pallas kernels, project(): pl.pallas_call(body, in_specs=[whole] * (1 + len(arrays) + len(extra)), o...  12.5 us
    pallas_call x1, Pallas kernels, attend(): pl.pallas_call(body, grid_spec=pltpu.PrefetchScalarGridSpec(num_scalar_pr...  6.79 us
  transfers between devices with their start and end apart: 42, of which 21 were waited for; matrix products, arithmetic and copies ran while one was open for 7% of the time, Pallas kernels for 13%

profile of v7, /device:TPU:0, one launch (start us, length us, event | category | flops | bytes accessed | tf_op | source)
XLA Modules:
  0.0 187.0 jit_solution(8694482197217665048)
XLA Ops:
  0.0 1.2 broadcast_select_fusion.2
  1.2 4.1 %collective-permute-start.1 = (bf16[512,256]{1,0:T(8,128)(2,1)S(1)}, bf16[512,256]{1,0:T(8,128)(2,1)S(1)}, u32[]{:S(2)}, u32[]{:S(2)}) collective-permute-start(bf16[512,256]{1,0:T(8,128)(2,1)S(1)} %get-tuple-element.86), channel_id=1, source_target_pairs={{0,8},{1,9},{2,10},{3,11},{4,0},{5,1},{6,2},{7,3},{8,12},{9,13},{1... | collective-permute-start | bytes 786440 | tf_op jit(solution)/shard_map/ppermute | solution.py:82
  5.3 1.8 broadcast_select_fusion
  7.0 1.6 collective-permute-start.6
  8.9 2.2 %copy-done.6 = bf16[8192,256]{1,0:T(8,128)(2,1)S(1)} copy-done((bf16[8192,256]{1,0:T(8,128)(2,1)S(1)}, bf16[8192,256]{1,0:T(8,128)(2,1)}, u32[]{:S(2)}) %copy-start.6) | copy-done | bytes 4194328
  11.0 2.0 %shard_map.73 = bf16[64,256]{1,0:T(8,128)(2,1)S(1)} custom-call(bf16[64,8192]{1,0:T(8,128)(2,1)S(1)} %bitcast.154, bf16[8192,256]{1,0:T(8,128)(2,1)S(1)} %copy-done.6, f32[64,128]{1,0:T(8,128)S(1)} %bitcast.157, f32[64,128]{1,0:T(8,128)S(1)} %bitcast.158), custom_call_target="tpu_custom_call" | custom-call | flops 1 | bytes 1 | tf_op jit(solution)/shard_map/pallas_call | solution.py:162
  13.1 1.6 collective-permute-start.12
  14.6 2.2 %collective-permute-start.3 = (bf16[512,256]{1,0:T(8,128)(2,1)S(1)}, bf16[512,256]{1,0:T(8,128)(2,1)}, u32[]{:S(2)}, u32[]{:S(2)}) collective-permute-start(bf16[512,256]{1,0:T(8,128)(2,1)S(1)} %collective-permute-done.1), channel_id=1, source_target_pairs={{0,8},{1,9},{2,10},{3,11},{4,0},{5,1},{6,2},{7,3},{8,12},{9,13},{1... | collective-permute-start | bytes 786440 | tf_op jit(solution)/shard_map/ppermute | solution.py:82
  17.6 3.0 %collective-permute-done.12 = bf16[512,256]{1,0:T(8,128)(2,1)S(1)} collective-permute-done((bf16[512,256]{1,0:T(8,128)(2,1)S(1)}, bf16[512,256]{1,0:T(8,128)(2,1)S(1)}, u32[]{:S(2)}, u32[]{:S(2)}) %collective-permute-start.12) | collective-permute-done | bytes 262176 | tf_op jit(solution)/shard_map/ppermute | solution.py:82
  20.6 1.4 collective-permute-done.3
  22.1 3.4 %copy-done.2 = bf16[512,8192]{1,0:T(8,128)(2,1)S(1)} copy-done((bf16[512,8192]{1,0:T(8,128)(2,1)S(1)}, bf16[512,8192]{1,0:T(8,128)(2,1)}, u32[]{:S(2)}) %copy-start.2) | copy-done | bytes 8388632
  25.4 3.3 %shard_map.75 = bf16[512,4096]{1,0:T(8,128)(2,1)} custom-call(s32[8]{0:T(128)S(1)} %stack.177.block_ref, bf16[512,8192]{1,0:T(8,128)(2,1)S(1)} %copy-done.2), custom_call_target="tpu_custom_call" | custom-call | flops 1 | bytes 1 | tf_op jit(solution)/shard_map/pallas_call | solution.py:122
  28.8 1.6 collective-permute-start
  30.5 7.1 %collective-permute-done = bf16[512,256]{1,0:T(8,128)(2,1)S(1)} collective-permute-done((bf16[512,256]{1,0:T(8,128)(2,1)S(1)}, bf16[512,256]{1,0:T(8,128)(2,1)S(1)}, u32[]{:S(2)}, u32[]{:S(2)}) %collective-permute-start) | collective-permute-done | bytes 262176 | tf_op jit(solution)/shard_map/ppermute | solution.py:82
  37.6 1.5 collective-permute-start.2
  39.1 3.5 %collective-permute-start.7 = (bf16[512,256]{1,0:T(8,128)(2,1)S(1)}, bf16[512,256]{1,0:T(8,128)(2,1)S(1)}, u32[]{:S(2)}, u32[]{:S(2)}) collective-permute-start(bf16[512,256]{1,0:T(8,128)(2,1)S(1)} %collective-permute-done.6.refs_2_), channel_id=1, source_target_pairs={{0,8},{1,9},{2,10},{3,11},{4,0},{5,1},{6,2},{7,3},{8,12},{9,13},{1... | collective-permute-start | bytes 786440 | tf_op jit(solution)/shard_map/ppermute | solution.py:82
  42.6 1.6 collective-permute-start.18
  44.2 7.6 %collective-permute-done.2.refs_1_ = bf16[1088,256]{1,0:T(8,128)(2,1)S(1)} collective-permute-done((bf16[1088,256]{1,0:T(8,128)(2,1)S(1)}, bf16[1088,256]{1,0:T(8,128)(2,1)S(1)}, u32[]{:S(2)}, u32[]{:S(2)}) %collective-permute-start.2) | collective-permute-done | bytes 557088 | tf_op jit(solution)/shard_map/ppermute | solution.py:82
  51.7 1.5 collective-permute-start.13
  53.2 3.5 %collective-permute-start.4 = (bf16[512,256]{1,0:T(8,128)(2,1)}, bf16[512,256]{1,0:T(8,128)(2,1)S(1)}, u32[]{:S(2)}, u32[]{:S(2)}) collective-permute-start(bf16[512,256]{1,0:T(8,128)(2,1)} %collective-permute-done.3), channel_id=1, source_target_pairs={{0,8},{1,9},{2,10},{3,11},{4,0},{5,1},{6,2},{7,3},{8,12},{9,13},{1... | collective-permute-start | bytes 786440 | tf_op jit(solution)/shard_map/ppermute | solution.py:82
  57.4 1.5 collective-permute-start.19
  59.5 1.0 constant_dynamic-update-slice_fusion.3
  61.3 3.2 %collective-permute-start.8 = (bf16[512,256]{1,0:T(8,128)(2,1)S(1)}, bf16[512,256]{1,0:T(8,128)(2,1)S(1)}, u32[]{:S(2)}, u32[]{:S(2)}) collective-permute-start(bf16[512,256]{1,0:T(8,128)(2,1)S(1)} %collective-permute-done.7.refs_4_), channel_id=1, source_target_pairs={{0,8},{1,9},{2,10},{3,11},{4,0},{5,1},{6,2},{7,3},{8,12},{9,13},{1... | collective-permute-start | bytes 786440 | tf_op jit(solution)/shard_map/ppermute | solution.py:82
  64.5 2.3 %collective-permute-done.19 = bf16[512,256]{1,0:T(8,128)(2,1)S(1)} collective-permute-done((bf16[512,256]{1,0:T(8,128)(2,1)}, bf16[512,256]{1,0:T(8,128)(2,1)S(1)}, u32[]{:S(2)}, u32[]{:S(2)}) %collective-permute-start.19) | collective-permute-done | bytes 262176 | tf_op jit(solution)/shard_map/ppermute | solution.py:82
  68.2 1.5 collective-permute-done.15.refs_9_
  70.3 1.5 collective-permute-start.16
  73.1 1.7 collective-permute-done.5.refs_1_.refs_0_
  74.8 3.4 %collective-permute-start.9 = (bf16[640,256]{1,0:T(8,128)(2,1)S(1)}, bf16[640,256]{1,0:T(8,128)(2,1)S(1)}, u32[]{:S(2)}, u32[]{:S(2)}) collective-permute-start(bf16[640,256]{1,0:T(8,128)(2,1)S(1)} %collective-permute-done.5.refs_1_.refs_0_), channel_id=1, source_target_pairs={{0,8},{1,9},{2,10},{3,11},{4,0},{5,1},{6,2},{7,3},{8,12},{9,13},{1... | collective-permute-start | bytes 983048 | tf_op jit(solution)/shard_map/ppermute | solution.py:82
  79.3 1.5 collective-permute-start.17
  80.8 4.1 %collective-permute-done.21 = bf16[512,256]{1,0:T(8,128)(2,1)S(1)} collective-permute-done((bf16[512,256]{1,0:T(8,128)(2,1)S(1)}, bf16[512,256]{1,0:T(8,128)(2,1)S(1)}, u32[]{:S(2)}, u32[]{:S(2)}) %collective-permute-start.21) | collective-permute-done | bytes 262176 | tf_op jit(solution)/shard_map/ppermute | solution.py:82
  87.0 1.5 collective-permute-start.22
  88.5 2.1 %collective-permute-done.17.refs_7_ = bf16[512,256]{1,0:T(8,128)(2,1)S(1)} collective-permute-done((bf16[512,256]{1,0:T(8,128)(2,1)S(1)}, bf16[512,256]{1,0:T(8,128)(2,1)S(1)}, u32[]{:S(2)}, u32[]{:S(2)}) %collective-permute-start.17) | collective-permute-done | bytes 262176 | tf_op jit(solution)/shard_map/ppermute | solution.py:82
  91.3 1.5 collective-permute-start.23
  92.8 1.2 collective-permute-start.10
  94.1 3.4 %copy-done.3 = bf16[512,8192]{1,0:T(8,128)(2,1)S(1)} copy-done((bf16[512,8192]{1,0:T(8,128)(2,1)S(1)}, bf16[512,8192]{1,0:T(8,128)(2,1)}, u32[]{:S(2)}) %copy-start.3) | copy-done | bytes 8388632
  97.4 3.2 %shard_map.76.left_ref = bf16[8,1088,512]{2,1,0:T(8,128)(2,1)S(1)} custom-call(s32[8]{0:T(128)S(1)} %stack.168.block_ref, bf16[512,8192]{1,0:T(8,128)(2,1)S(1)} %copy-done.3, bf16[512,4096]{1,0:T(8,128)(2,1)} %collective-permute-done.14.got_ref, bf16[64,8192]{1,0:T(8,128)(2,1)S(1)} %bitcast.155), custom_call_target="tpu_custom_call" | custom-call | flops 1 | bytes 1 | tf_op jit(solution)/shard_map/pallas_call | solution.py:227
  100.8 3.6 %shard_map.77.refs_2_ = f32[1088,512]{1,0:T(8,128)S(1)} custom-call(bf16[8,1088,512]{2,1,0:T(8,128)(2,1)S(1)} %shard_map.76.left_ref, bf16[1088,256]{1,0:T(8,128)(2,1)S(1)} %pad_maximum_fusion.refs_0_, bf16[1088,256]{1,0:T(8,128)(2,1)S(1)} %copy-done.17, bf16[1024,256]{1,0:T(8,128)(2,1)S(1)} %copy-done.12, bf16[1024,256]{1,0:T(8,128)(2,1)S(1)} %copy-done.19, ...), custom_call_target="tpu_custom_call" | custom-call | flops 1 | bytes 1 | tf_op jit(solution)/shard_map/pallas_call | solution.py:269
  104.5 3.1 %shard_map.78.refs_6_ = f32[1088,512]{1,0:T(8,128)S(1)} custom-call(bf16[8,1088,512]{2,1,0:T(8,128)(2,1)S(1)} %shard_map.76.left_ref, bf16[512,256]{1,0:T(8,128)(2,1)S(1)} %copy-done.15, bf16[512,256]{1,0:T(8,128)(2,1)S(1)} %copy-done.13, bf16[512,256]{1,0:T(8,128)(2,1)S(1)} %copy-done.24, bf16[512,256]{1,0:T(8,128)(2,1)S(1)} %copy-done.28, ...), custom_call_target="tpu_custom_call" | custom-call | flops 1 | bytes 1 | tf_op jit(solution)/shard_map/pallas_call | solution.py:269
  107.6 1.3 copy-done.4
  109.0 2.5 %shard_map.79.refs_2_ = f32[1088,512]{1,0:T(8,128)S(1)} custom-call(bf16[8,1088,512]{2,1,0:T(8,128)(2,1)S(1)} %shard_map.76.left_ref, bf16[1024,256]{1,0:T(8,128)(2,1)} %constant_dynamic-update-slice_fusion.4.refs_0_, bf16[1024,256]{1,0:T(8,128)(2,1)} %collective-permute-done.24.refs_1_, f32[1088,512]{1,0:T(8,128)S(1)} %shard_map.77.refs_2_), custom_call_target="tpu_custom_call" | custom-call | flops 1 | bytes 1 | tf_op jit(solution)/shard_map/pallas_call | solution.py:269
  111.6 1.4 reshape.412
  115.7 1.9 %multiply_sine_fusion = (f32[1024,64]{1,0:T(8,128)S(1)}, f32[1024,64]{1,0:T(8,128)S(1)}) fusion(f32[64]{0:T(128)S(1)} %multiply_power_fusion, f32[1024]{0:T(1024)S(1)} %convert_bitcast_fusion), kind=kLoop, calls=%fused_computation.1 | loop fusion | flops 65536 | bytes 528640 | tf_op jit(solution)/shard_map/sin | solution.py:23
  119.0 0.9 slice.171
  120.3 6.8 %shard_map.80 = (bf16[4,1024,512]{2,1,0:T(8,128)(2,1)S(1)}, f32[4,1,512]{2,1,0:T(1,128)S(1)}, f32[4,1,512]{2,1,0:T(1,128)S(1)}) custom-call(s32[4]{0:T(128)S(1)} %and_select_fusion.1.place_ref, s32[4]{0:T(128)S(1)} %pad_add_fusion.turn_ref, bf16[4,128,256]{2,1,0:T(8,128)(2,1)S(1)} %shard_map.74.refs_0_, ...), custom_call_target="tpu_custom_call" | custom-call | flops 1 | bytes 1 | tf_op jit(solution)/shard_map/pallas_call | solution.py:333
  127.2 2.1 %copy-done.8 = bf16[4,1024,512]{2,1,0:T(8,128)(2,1)} copy-done((bf16[4,1024,512]{2,1,0:T(8,128)(2,1)}, bf16[4,1024,512]{2,1,0:T(8,128)(2,1)S(1)}, u32[]{:S(2)}) %copy-start.8) | copy-done | bytes 4194328
  130.3 2.7 %collective-permute-done.26 = f32[2,4,2,2,128]{4,3,2,1,0:T(2,128)S(1)} collective-permute-done((f32[2,4,2,2,128]{4,3,2,1,0:T(2,128)S(1)}, f32[2,4,2,2,128]{4,3,2,1,0:T(2,128)S(1)}, u32[]{:S(2)}, u32[]{:S(2)}) %collective-permute-start.26) | collective-permute-done | bytes 16416 | tf_op jit(solution)/shard_map/ppermute | solution.py:82
  133.1 1.2 collective-permute-start.27
  135.0 2.1 %collective-permute-start.29 = (f32[2,2,4,2,2,128]{5,4,3,2,1,0:T(2,128)S(1)}, f32[2,2,4,2,2,128]{5,4,3,2,1,0:T(2,128)S(1)}, u32[]{:S(2)}, u32[]{:S(2)}) collective-permute-start(f32[2,2,4,2,2,128]{5,4,3,2,1,0:T(2,128)S(1)} %pad_maximum_fusion.2), channel_id=1, source_target_pairs={{0,12},{1,13},{2,14},{3,15},{4,0},{5,1},{6,2},{7,3},{8,4},{9,5},{1... | collective-permute-start | bytes 98312 | tf_op jit(solution)/shard_map/ppermute | solution.py:82
  137.1 3.5 %copy-done.1 = bf16[8,1088,512]{2,1,0:T(8,128)(2,1)S(1)} copy-done((bf16[8,1088,512]{2,1,0:T(8,128)(2,1)S(1)}, bf16[8,1088,512]{2,1,0:T(8,128)(2,1)}, u32[]{:S(2)}) %copy-start.1) | copy-done | bytes 8912920
  140.6 1.6 copy-done.5
  142.2 3.2 %shard_map.81.value_ref = f32[1088,512]{1,0:T(8,128)S(1)} custom-call(bf16[8,1088,512]{2,1,0:T(8,128)(2,1)S(1)} %copy-done.1, bf16[640,256]{1,0:T(8,128)(2,1)S(1)} %collective-permute-done.5.refs_1_.refs_0_, bf16[640,256]{1,0:T(8,128)(2,1)} %collective-permute-done.22.refs_1_, bf16[640,256]{1,0:T(8,128)(2,1)S(1)} %collective-permute-done.9.refs_2_, ...), custom_call_target="tpu_custom_call" | custom-call | flops 1 | bytes 1 | tf_op jit(solution)/shard_map/pallas_call | solution.py:269
  145.5 2.5 %shard_map.82 = bf16[4,512,128]{2,1,0:T(8,128)(2,1)S(1)} custom-call(s32[4]{0:T(128)S(1)} %and_select_fusion.1.place_ref, bf16[4,1024,512]{2,1,0:T(8,128)(2,1)S(1)} %copy-done.9, f32[1088,512]{1,0:T(8,128)S(1)} %shard_map.81.value_ref), custom_call_target="tpu_custom_call" | custom-call | flops 1 | bytes 1 | tf_op jit(solution)/shard_map/pallas_call | solution.py:370
  150.8 5.2 %collective-permute-done.32 = bf16[4,128,128]{2,1,0:T(8,128)(2,1)S(1)} collective-permute-done((bf16[4,128,128]{2,1,0:T(8,128)(2,1)S(1)}, bf16[4,128,128]{2,1,0:T(8,128)(2,1)S(1)}, u32[]{:S(2)}, u32[]{:S(2)}) %collective-permute-start.32) | collective-permute-done | bytes 131104 | tf_op jit(solution)/shard_map/ppermute | solution.py:82
  156.6 1.7 collective-permute-start.34
  158.3 2.7 %collective-permute-start.35 = (bf16[128,128]{1,0:T(8,128)(2,1)S(1)}, bf16[128,128]{1,0:T(8,128)(2,1)S(1)}, u32[]{:S(2)}, u32[]{:S(2)}) collective-permute-start(bf16[128,128]{1,0:T(8,128)(2,1)S(1)} %get-tuple-element.92), channel_id=1, source_target_pairs={{0,12},{1,13},{2,14},{3,15},{4,0},{5,1},{6,2},{7,3},{8,4},{9,5},{1... | collective-permute-start | bytes 98312 | tf_op jit(solution)/shard_map/ppermute | solution.py:82
  161.0 0.9 collective-permute-done.33
  162.8 2.2 %copy-done.7 = bf16[256,8192]{1,0:T(8,128)(2,1)S(1)} copy-done((bf16[256,8192]{1,0:T(8,128)(2,1)S(1)}, bf16[256,8192]{1,0:T(8,128)(2,1)}, u32[]{:S(2)}) %copy-start.7) | copy-done | bytes 4194328
  165.0 1.4 shard_map.83
  166.5 1.9 %collective-permute-done.37 = bf16[64,4096]{1,0:T(8,128)(2,1)S(1)} collective-permute-done((bf16[64,4096]{1,0:T(8,128)(2,1)S(1)}, bf16[64,4096]{1,0:T(8,128)(2,1)S(1)}, u32[]{:S(2)}, u32[]{:S(2)}) %collective-permute-start.37) | collective-permute-done | bytes 524320 | tf_op jit(solution)/shard_map/ppermute | solution.py:82
  169.2 7.8 %collective-permute-done.38 = bf16[64,2048]{1,0:T(8,128)(2,1)S(1)} collective-permute-done((bf16[64,2048]{1,0:T(8,128)(2,1)S(1)}, bf16[64,2048]{1,0:T(8,128)(2,1)S(1)}, u32[]{:S(2)}, u32[]{:S(2)}) %collective-permute-start.38) | collective-permute-done | bytes 262176 | tf_op jit(solution)/shard_map/ppermute | solution.py:82
  177.1 1.9 %collective-permute-start.39 = (bf16[64,512]{1,0:T(8,128)(2,1)S(1)}, bf16[64,512]{1,0:T(8,128)(2,1)S(1)}, u32[]{:S(2)}, u32[]{:S(2)}) collective-permute-start(bf16[64,512]{1,0:T(8,128)(2,1)S(1)} %get-tuple-element.88), channel_id=1, source_target_pairs={{0,4},{1,5},{2,6},{3,7},{4,8},{5,9},{6,10},{7,11},{8,12},{9,13},{1... | collective-permute-start | bytes 196616 | tf_op jit(solution)/shard_map/ppermute | solution.py:82
  179.0 2.8 %collective-permute-start.40 = (bf16[64,512]{1,0:T(8,128)(2,1)S(1)}, bf16[64,512]{1,0:T(8,128)(2,1)S(1)}, u32[]{:S(2)}, u32[]{:S(2)}) collective-permute-start(bf16[64,512]{1,0:T(8,128)(2,1)S(1)} %get-tuple-element.90), channel_id=1, source_target_pairs={{0,8},{1,9},{2,10},{3,11},{4,12},{5,13},{6,14},{7,15},{8,0},{9,1},... | collective-permute-start | bytes 196616 | tf_op jit(solution)/shard_map/ppermute | solution.py:82
  181.8 2.4 %collective-permute-done.39 = bf16[64,512]{1,0:T(8,128)(2,1)S(1)} collective-permute-done((bf16[64,512]{1,0:T(8,128)(2,1)S(1)}, bf16[64,512]{1,0:T(8,128)(2,1)S(1)}, u32[]{:S(2)}, u32[]{:S(2)}) %collective-permute-start.39) | collective-permute-done | bytes 65568 | tf_op jit(solution)/shard_map/ppermute | solution.py:82
  184.3 1.7 collective-permute-done.40
  (193 shorter events, 22.4 us)
Async XLA Ops:
  0.0 8.8 %copy-start.10 = (bf16[2,32,8192]{2,1,0:T(8,128)(2,1)S(1)}, bf16[2,32,8192]{2,1,0:T(8,128)(2,1)}, u32[]{:S(2)}) copy-start(bf16[2,32,8192]{2,1,0:T(8,128)(2,1)} %param.10) | copy-start | bytes 3145732
  1.2 11.9 %collective-permute-start.1 = (bf16[512,256]{1,0:T(8,128)(2,1)S(1)}, bf16[512,256]{1,0:T(8,128)(2,1)S(1)}, u32[]{:S(2)}, u32[]{:S(2)}) collective-permute-start(bf16[512,256]{1,0:T(8,128)(2,1)S(1)} %get-tuple-element.86), channel_id=1, source_target_pairs={{0,8},{1,9},{2,10},{3,11},{4,0},{5,1},{6,2},{7,3},{8,12},{9,13},{1... | collective-permute-start | bytes 786440 | tf_op jit(solution)/shard_map/ppermute | solution.py:82
  7.0 21.8 %copy-start.14 = (bf16[512,256]{1,0:T(8,128)(2,1)}, bf16[512,256]{1,0:T(8,128)(2,1)S(1)}, u32[]{:S(2)}) copy-start(bf16[512,256]{1,0:T(8,128)(2,1)S(1)} %get-tuple-element.85.refs_0_) | copy-start | bytes 786436
  7.0 10.5 %collective-permute-start.6 = (bf16[512,256]{1,0:T(8,128)(2,1)S(1)}, bf16[512,256]{1,0:T(8,128)(2,1)S(1)}, u32[]{:S(2)}, u32[]{:S(2)}) collective-permute-start(bf16[512,256]{1,0:T(8,128)(2,1)S(1)} %get-tuple-element.85.refs_0_), channel_id=1, source_target_pairs={{0,8},{1,9},{2,10},{3,11},{4,0},{5,1},{6,2},{7,3},{8,12},{9,13},{1... | collective-permute-start | bytes 786440 | tf_op jit(solution)/shard_map/ppermute | solution.py:82
  13.0 47.4 %copy-start.22 = (bf16[64,256]{1,0:T(8,128)(2,1)}, bf16[64,256]{1,0:T(8,128)(2,1)S(1)}, u32[]{:S(2)}) copy-start(bf16[64,256]{1,0:T(8,128)(2,1)S(1)} %shard_map.73) | copy-start | bytes 98308
  13.1 7.6 %collective-permute-start.12 = (bf16[512,256]{1,0:T(8,128)(2,1)S(1)}, bf16[512,256]{1,0:T(8,128)(2,1)S(1)}, u32[]{:S(2)}, u32[]{:S(2)}) collective-permute-start(bf16[512,256]{1,0:T(8,128)(2,1)S(1)} %collective-permute-done.1), channel_id=1, source_target_pairs={{0,16},{1,17},{2,18},{3,19},{4,20},{5,21},{6,22},{7,23},{8,24},{9,... | collective-permute-start | bytes 786440 | tf_op jit(solution)/shard_map/ppermute | solution.py:82
  14.6 7.4 %collective-permute-start.3 = (bf16[512,256]{1,0:T(8,128)(2,1)S(1)}, bf16[512,256]{1,0:T(8,128)(2,1)}, u32[]{:S(2)}, u32[]{:S(2)}) collective-permute-start(bf16[512,256]{1,0:T(8,128)(2,1)S(1)} %collective-permute-done.1), channel_id=1, source_target_pairs={{0,8},{1,9},{2,10},{3,11},{4,0},{5,1},{6,2},{7,3},{8,12},{9,13},{1... | collective-permute-start | bytes 786440 | tf_op jit(solution)/shard_map/ppermute | solution.py:82
  17.6 25.0 %copy-start.23 = (bf16[512,256]{1,0:T(8,128)(2,1)}, bf16[512,256]{1,0:T(8,128)(2,1)S(1)}, u32[]{:S(2)}) copy-start(bf16[512,256]{1,0:T(8,128)(2,1)S(1)} %collective-permute-done.6.refs_2_) | copy-start | bytes 786436
  22.1 3.4 %copy-start.2 = (bf16[512,8192]{1,0:T(8,128)(2,1)S(1)}, bf16[512,8192]{1,0:T(8,128)(2,1)}, u32[]{:S(2)}) copy-start(bf16[512,8192]{1,0:T(8,128)(2,1)} %prompt_ref.1) | copy-start | bytes 25165828
  28.8 65.3 %collective-permute-start.14 = (bf16[512,4096]{1,0:T(8,128)(2,1)}, bf16[512,4096]{1,0:T(8,128)(2,1)}, u32[]{:S(2)}, u32[]{:S(2)}) collective-permute-start(bf16[512,4096]{1,0:T(8,128)(2,1)} %shard_map.75), channel_id=1, source_target_pairs={{0,1},{1,0},{2,3},{3,2},{4,5},{5,4},{6,7},{7,6},{8,9},{9,8},{10,11... | collective-permute-start | bytes 12582920 | tf_op jit(solution)/shard_map/ppermute | solution.py:82
  28.8 8.7 %collective-permute-start = (bf16[512,256]{1,0:T(8,128)(2,1)S(1)}, bf16[512,256]{1,0:T(8,128)(2,1)S(1)}, u32[]{:S(2)}, u32[]{:S(2)}) collective-permute-start(bf16[512,256]{1,0:T(8,128)(2,1)S(1)} %get-tuple-element.85.refs_0_), channel_id=1, source_target_pairs={{0,2},{1,3},{2,0},{3,1},{4,6},{5,7},{6,4},{7,5},{8,10},{9,11},{10,... | collective-permute-start | bytes 786440 | tf_op jit(solution)/shard_map/ppermute | solution.py:82
  37.6 14.2 %collective-permute-start.2 = (bf16[1088,256]{1,0:T(8,128)(2,1)S(1)}, bf16[1088,256]{1,0:T(8,128)(2,1)S(1)}, u32[]{:S(2)}, u32[]{:S(2)}) collective-permute-start(bf16[1088,256]{1,0:T(8,128)(2,1)S(1)} %pad_maximum_fusion.refs_0_), channel_id=1, source_target_pairs={{0,2},{1,3},{2,0},{3,1},{4,6},{5,7},{6,4},{7,5},{8,10},{9,11},{10,... | collective-permute-start | bytes 1671176 | tf_op jit(solution)/shard_map/ppermute | solution.py:82
  39.1 19.9 %collective-permute-start.7 = (bf16[512,256]{1,0:T(8,128)(2,1)S(1)}, bf16[512,256]{1,0:T(8,128)(2,1)S(1)}, u32[]{:S(2)}, u32[]{:S(2)}) collective-permute-start(bf16[512,256]{1,0:T(8,128)(2,1)S(1)} %collective-permute-done.6.refs_2_), channel_id=1, source_target_pairs={{0,8},{1,9},{2,10},{3,11},{4,0},{5,1},{6,2},{7,3},{8,12},{9,13},{1... | collective-permute-start | bytes 786440 | tf_op jit(solution)/shard_map/ppermute | solution.py:82
  42.6 14.1 %collective-permute-start.18 = (bf16[512,256]{1,0:T(8,128)(2,1)S(1)}, bf16[512,256]{1,0:T(8,128)(2,1)S(1)}, u32[]{:S(2)}, u32[]{:S(2)}) collective-permute-start(bf16[512,256]{1,0:T(8,128)(2,1)S(1)} %collective-permute-done.6.refs_2_), channel_id=1, source_target_pairs={{0,16},{1,17},{2,18},{3,19},{4,20},{5,21},{6,22},{7,23},{8,24},{9,... | collective-permute-start | bytes 786440 | tf_op jit(solution)/shard_map/ppermute | solution.py:82
  44.2 47.1 %copy-start.11 = (bf16[1024,256]{1,0:T(8,128)(2,1)}, bf16[1024,256]{1,0:T(8,128)(2,1)S(1)}, u32[]{:S(2)}) copy-start(bf16[1024,256]{1,0:T(8,128)(2,1)S(1)} %constant_dynamic-update-slice_fusion.refs_2_) | copy-start | bytes 1572868
  51.7 15.8 %collective-permute-start.13 = (bf16[1024,256]{1,0:T(8,128)(2,1)S(1)}, bf16[1024,256]{1,0:T(8,128)(2,1)S(1)}, u32[]{:S(2)}, u32[]{:S(2)}) collective-permute-start(bf16[1024,256]{1,0:T(8,128)(2,1)S(1)} %constant_dynamic-update-slice_fusion.refs_2_), channel_id=1, source_target_pairs={{0,2},{1,3},{2,0},{3,1},{4,6},{5,7},{6,4},{7,5},{8,10},{9,11},{10,... | collective-permute-start | bytes 1572872 | tf_op jit(solution)/shard_map/ppermute | solution.py:82
  53.2 8.1 %collective-permute-start.4 = (bf16[512,256]{1,0:T(8,128)(2,1)}, bf16[512,256]{1,0:T(8,128)(2,1)S(1)}, u32[]{:S(2)}, u32[]{:S(2)}) collective-permute-start(bf16[512,256]{1,0:T(8,128)(2,1)} %collective-permute-done.3), channel_id=1, source_target_pairs={{0,8},{1,9},{2,10},{3,11},{4,0},{5,1},{6,2},{7,3},{8,12},{9,13},{1... | collective-permute-start | bytes 786440 | tf_op jit(solution)/shard_map/ppermute | solution.py:82
  57.4 9.4 %collective-permute-start.19 = (bf16[512,256]{1,0:T(8,128)(2,1)}, bf16[512,256]{1,0:T(8,128)(2,1)S(1)}, u32[]{:S(2)}, u32[]{:S(2)}) collective-permute-start(bf16[512,256]{1,0:T(8,128)(2,1)} %collective-permute-done.3), channel_id=1, source_target_pairs={{0,16},{1,17},{2,18},{3,19},{4,20},{5,21},{6,22},{7,23},{8,24},{9,... | collective-permute-start | bytes 786440 | tf_op jit(solution)/shard_map/ppermute | solution.py:82
  58.9 10.7 %collective-permute-start.15 = (bf16[512,256]{1,0:T(8,128)(2,1)S(1)}, bf16[512,256]{1,0:T(8,128)(2,1)S(1)}, u32[]{:S(2)}, u32[]{:S(2)}) collective-permute-start(bf16[512,256]{1,0:T(8,128)(2,1)S(1)} %collective-permute-done), channel_id=1, source_target_pairs={{0,16},{1,17},{2,18},{3,19},{4,20},{5,21},{6,22},{7,23},{8,24},{9,... | collective-permute-start | bytes 786440 | tf_op jit(solution)/shard_map/ppermute | solution.py:82
  61.3 11.2 %collective-permute-start.8 = (bf16[512,256]{1,0:T(8,128)(2,1)S(1)}, bf16[512,256]{1,0:T(8,128)(2,1)S(1)}, u32[]{:S(2)}, u32[]{:S(2)}) collective-permute-start(bf16[512,256]{1,0:T(8,128)(2,1)S(1)} %collective-permute-done.7.refs_4_), channel_id=1, source_target_pairs={{0,8},{1,9},{2,10},{3,11},{4,0},{5,1},{6,2},{7,3},{8,12},{9,13},{1... | collective-permute-start | bytes 786440 | tf_op jit(solution)/shard_map/ppermute | solution.py:82
  66.8 8.0 %collective-permute-start.5 = (bf16[640,256]{1,0:T(8,128)(2,1)S(1)}, bf16[640,256]{1,0:T(8,128)(2,1)S(1)}, u32[]{:S(2)}, u32[]{:S(2)}) collective-permute-start(bf16[640,256]{1,0:T(8,128)(2,1)S(1)} %pad_maximum_fusion.1.refs_0_.refs_8_), channel_id=1, source_target_pairs={{0,8},{1,9},{2,10},{3,11},{4,0},{5,1},{6,2},{7,3},{8,12},{9,13},{1... | collective-permute-start | bytes 983048 | tf_op jit(solution)/shard_map/ppermute | solution.py:82
  67.6 25.2 %copy-start.18 = (bf16[1024,256]{1,0:T(8,128)(2,1)}, bf16[1024,256]{1,0:T(8,128)(2,1)S(1)}, u32[]{:S(2)}) copy-start(bf16[1024,256]{1,0:T(8,128)(2,1)S(1)} %collective-permute-done.13.refs_3_) | copy-start | bytes 1572868
  67.6 18.1 %collective-permute-start.20 = (bf16[1024,256]{1,0:T(8,128)(2,1)S(1)}, bf16[1024,256]{1,0:T(8,128)(2,1)S(1)}, u32[]{:S(2)}, u32[]{:S(2)}) collective-permute-start(bf16[1024,256]{1,0:T(8,128)(2,1)S(1)} %constant_dynamic-update-slice_fusion.2.refs_4_), channel_id=1, source_target_pairs={{0,2},{1,3},{2,0},{3,1},{4,6},{5,7},{6,4},{7,5},{8,10},{9,11},{10,... | collective-permute-start | bytes 1572872 | tf_op jit(solution)/shard_map/ppermute | solution.py:82
  70.3 9.0 %collective-permute-start.16 = (bf16[512,256]{1,0:T(8,128)(2,1)S(1)}, bf16[512,256]{1,0:T(8,128)(2,1)S(1)}, u32[]{:S(2)}, u32[]{:S(2)}) collective-permute-start(bf16[512,256]{1,0:T(8,128)(2,1)S(1)} %collective-permute-done.7.refs_4_), channel_id=1, source_target_pairs={{0,16},{1,17},{2,18},{3,19},{4,20},{5,21},{6,22},{7,23},{8,24},{9,... | collective-permute-start | bytes 786440 | tf_op jit(solution)/shard_map/ppermute | solution.py:82
  72.6 20.2 %copy-start.31 = (bf16[512,256]{1,0:T(8,128)(2,1)}, bf16[512,256]{1,0:T(8,128)(2,1)S(1)}, u32[]{:S(2)}) copy-start(bf16[512,256]{1,0:T(8,128)(2,1)S(1)} %collective-permute-done.8.refs_6_) | copy-start | bytes 786436
  72.6 12.4 %collective-permute-start.21 = (bf16[512,256]{1,0:T(8,128)(2,1)S(1)}, bf16[512,256]{1,0:T(8,128)(2,1)S(1)}, u32[]{:S(2)}, u32[]{:S(2)}) collective-permute-start(bf16[512,256]{1,0:T(8,128)(2,1)S(1)} %collective-permute-done.4), channel_id=1, source_target_pairs={{0,16},{1,17},{2,18},{3,19},{4,20},{5,21},{6,22},{7,23},{8,24},{9,... | collective-permute-start | bytes 786440 | tf_op jit(solution)/shard_map/ppermute | solution.py:82
  74.8 16.5 %collective-permute-start.9 = (bf16[640,256]{1,0:T(8,128)(2,1)S(1)}, bf16[640,256]{1,0:T(8,128)(2,1)S(1)}, u32[]{:S(2)}, u32[]{:S(2)}) collective-permute-start(bf16[640,256]{1,0:T(8,128)(2,1)S(1)} %collective-permute-done.5.refs_1_.refs_0_), channel_id=1, source_target_pairs={{0,8},{1,9},{2,10},{3,11},{4,0},{5,1},{6,2},{7,3},{8,12},{9,13},{1... | collective-permute-start | bytes 983048 | tf_op jit(solution)/shard_map/ppermute | solution.py:82
  79.3 13.5 %copy-start.33 = (bf16[512,256]{1,0:T(8,128)(2,1)}, bf16[512,256]{1,0:T(8,128)(2,1)S(1)}, u32[]{:S(2)}) copy-start(bf16[512,256]{1,0:T(8,128)(2,1)S(1)} %collective-permute-done.16.refs_5_) | copy-start | bytes 786436
  79.3 11.2 %collective-permute-start.17 = (bf16[512,256]{1,0:T(8,128)(2,1)S(1)}, bf16[512,256]{1,0:T(8,128)(2,1)S(1)}, u32[]{:S(2)}, u32[]{:S(2)}) collective-permute-start(bf16[512,256]{1,0:T(8,128)(2,1)S(1)} %collective-permute-done.8.refs_6_), channel_id=1, source_target_pairs={{0,16},{1,17},{2,18},{3,19},{4,20},{5,21},{6,22},{7,23},{8,24},{9,... | collective-permute-start | bytes 786440 | tf_op jit(solution)/shard_map/ppermute | solution.py:82
  86.5 22.4 %collective-permute-start.24 = (bf16[1024,256]{1,0:T(8,128)(2,1)}, bf16[1024,256]{1,0:T(8,128)(2,1)}, u32[]{:S(2)}, u32[]{:S(2)}) collective-permute-start(bf16[1024,256]{1,0:T(8,128)(2,1)} %constant_dynamic-update-slice_fusion.4.refs_0_), channel_id=1, source_target_pairs={{0,2},{1,3},{2,0},{3,1},{4,6},{5,7},{6,4},{7,5},{8,10},{9,11},{10,... | collective-permute-start | bytes 1572872 | tf_op jit(solution)/shard_map/ppermute | solution.py:82
  87.0 17.4 %collective-permute-start.22 = (bf16[640,256]{1,0:T(8,128)(2,1)S(1)}, bf16[640,256]{1,0:T(8,128)(2,1)}, u32[]{:S(2)}, u32[]{:S(2)}) collective-permute-start(bf16[640,256]{1,0:T(8,128)(2,1)S(1)} %collective-permute-done.5.refs_1_.refs_0_), channel_id=1, source_target_pairs={{0,16},{1,17},{2,18},{3,19},{4,20},{5,21},{6,22},{7,23},{8,24},{9,... | collective-permute-start | bytes 983048 | tf_op jit(solution)/shard_map/ppermute | solution.py:82
  91.3 17.6 %collective-permute-start.23 = (bf16[640,256]{1,0:T(8,128)(2,1)S(1)}, bf16[640,256]{1,0:T(8,128)(2,1)}, u32[]{:S(2)}, u32[]{:S(2)}) collective-permute-start(bf16[640,256]{1,0:T(8,128)(2,1)S(1)} %collective-permute-done.9.refs_2_), channel_id=1, source_target_pairs={{0,16},{1,17},{2,18},{3,19},{4,20},{5,21},{6,22},{7,23},{8,24},{9,... | collective-permute-start | bytes 983048 | tf_op jit(solution)/shard_map/ppermute | solution.py:82
  92.8 16.1 %collective-permute-start.10 = (bf16[640,256]{1,0:T(8,128)(2,1)S(1)}, bf16[640,256]{1,0:T(8,128)(2,1)S(1)}, u32[]{:S(2)}, u32[]{:S(2)}) collective-permute-start(bf16[640,256]{1,0:T(8,128)(2,1)S(1)} %collective-permute-done.9.refs_2_), channel_id=1, source_target_pairs={{0,8},{1,9},{2,10},{3,11},{4,0},{5,1},{6,2},{7,3},{8,12},{9,13},{1... | collective-permute-start | bytes 983048 | tf_op jit(solution)/shard_map/ppermute | solution.py:82
  94.0 3.4 %copy-start.3 = (bf16[512,8192]{1,0:T(8,128)(2,1)S(1)}, bf16[512,8192]{1,0:T(8,128)(2,1)}, u32[]{:S(2)}) copy-start(bf16[512,8192]{1,0:T(8,128)(2,1)} %prompt_ref.1) | copy-start | bytes 25165828
  100.7 8.3 %copy-start = (bf16[8,1088,512]{2,1,0:T(8,128)(2,1)}, bf16[8,1088,512]{2,1,0:T(8,128)(2,1)S(1)}, u32[]{:S(2)}) copy-start(bf16[8,1088,512]{2,1,0:T(8,128)(2,1)S(1)} %shard_map.76.left_ref) | copy-start | bytes 26738692
  100.7 3.7 %copy-start.13 = (bf16[512,256]{1,0:T(8,128)(2,1)S(1)}, bf16[512,256]{1,0:T(8,128)(2,1)}, u32[]{:S(2)}) copy-start(bf16[512,256]{1,0:T(8,128)(2,1)} %get-tuple-element.84.refs_1_) | copy-start | bytes 786436
  100.7 3.7 %copy-start.15 = (bf16[512,256]{1,0:T(8,128)(2,1)S(1)}, bf16[512,256]{1,0:T(8,128)(2,1)}, u32[]{:S(2)}) copy-start(bf16[512,256]{1,0:T(8,128)(2,1)} %copy-done.14) | copy-start | bytes 786436
  100.7 3.7 %copy-start.24 = (bf16[512,256]{1,0:T(8,128)(2,1)S(1)}, bf16[512,256]{1,0:T(8,128)(2,1)}, u32[]{:S(2)}) copy-start(bf16[512,256]{1,0:T(8,128)(2,1)} %copy-done.23) | copy-start | bytes 786436
  100.7 3.7 %copy-start.26 = (bf16[512,256]{1,0:T(8,128)(2,1)S(1)}, bf16[512,256]{1,0:T(8,128)(2,1)}, u32[]{:S(2)}) copy-start(bf16[512,256]{1,0:T(8,128)(2,1)} %copy-done.25) | copy-start | bytes 786436
  100.7 3.7 %copy-start.28 = (bf16[512,256]{1,0:T(8,128)(2,1)S(1)}, bf16[512,256]{1,0:T(8,128)(2,1)}, u32[]{:S(2)}) copy-start(bf16[512,256]{1,0:T(8,128)(2,1)} %copy-done.27) | copy-start | bytes 786436
  100.7 3.7 %copy-start.30 = (bf16[512,256]{1,0:T(8,128)(2,1)S(1)}, bf16[512,256]{1,0:T(8,128)(2,1)}, u32[]{:S(2)}) copy-start(bf16[512,256]{1,0:T(8,128)(2,1)} %copy-done.29) | copy-start | bytes 786436
  100.7 3.7 %copy-start.32 = (bf16[512,256]{1,0:T(8,128)(2,1)S(1)}, bf16[512,256]{1,0:T(8,128)(2,1)}, u32[]{:S(2)}) copy-start(bf16[512,256]{1,0:T(8,128)(2,1)} %copy-done.31) | copy-start | bytes 786436
  100.8 3.7 %copy-start.34 = (bf16[512,256]{1,0:T(8,128)(2,1)S(1)}, bf16[512,256]{1,0:T(8,128)(2,1)}, u32[]{:S(2)}) copy-start(bf16[512,256]{1,0:T(8,128)(2,1)} %copy-done.33) | copy-start | bytes 786436
  100.8 3.7 %copy-start.36 = (bf16[512,256]{1,0:T(8,128)(2,1)S(1)}, bf16[512,256]{1,0:T(8,128)(2,1)}, u32[]{:S(2)}) copy-start(bf16[512,256]{1,0:T(8,128)(2,1)} %copy-done.35) | copy-start | bytes 786436
  111.5 7.6 %collective-permute-start.25 = (f32[1088,512]{1,0:T(8,128)S(1)}, f32[1088,512]{1,0:T(8,128)}, u32[]{:S(2)}, u32[]{:S(2)}) collective-permute-start(f32[1088,512]{1,0:T(8,128)S(1)} %shard_map.79.refs_2_), channel_id=1, source_target_pairs={{0,1},{1,0},{2,3},{3,2},{4,5},{5,4},{6,7},{7,6},{8,9},{9,8},{10,11... | collective-permute-start | bytes 6684680 | tf_op jit(solution)/shard_map/ppermute | solution.py:82
  114.5 5.7 %copy-start.37 = (f32[2,32,2,128]{3,2,1,0:T(2,128)S(1)}, f32[2,32,2,128]{3,2,1,0:T(2,128)}, u32[]{:S(2)}) copy-start(f32[2,32,2,128]{3,2,1,0:T(2,128)} %reshape.412) | copy-start | bytes 196612
  118.0 2.4 %collective-permute-start.11 = (bf16[4,128,256]{2,1,0:T(8,128)(2,1)S(1)}, bf16[4,128,256]{2,1,0:T(8,128)(2,1)S(1)}, u32[]{:S(2)}, u32[]{:S(2)}) collective-permute-start(bf16[4,128,256]{2,1,0:T(8,128)(2,1)S(1)} %shard_map.74.refs_0_), channel_id=1, source_target_pairs={{0,1},{1,0},{2,3},{3,2},{4,5},{5,4},{6,7},{7,6},{8,9},{9,8},{10,11... | collective-permute-start | bytes 786440 | tf_op jit(solution)/shard_map/ppermute | solution.py:82
  118.5 18.6 %collective-permute-start.30 = (bf16[640,256]{1,0:T(8,128)(2,1)S(1)}, bf16[640,256]{1,0:T(8,128)(2,1)}, u32[]{:S(2)}, u32[]{:S(2)}) collective-permute-start(bf16[640,256]{1,0:T(8,128)(2,1)S(1)} %collective-permute-done.10.refs_3_.refs_4_), channel_id=1, source_target_pairs={{0,16},{1,17},{2,18},{3,19},{4,20},{5,21},{6,22},{7,23},{8,24},{9,... | collective-permute-start | bytes 983048 | tf_op jit(solution)/shard_map/ppermute | solution.py:82
  129.2 3.8 %collective-permute-start.26 = (f32[2,4,2,2,128]{4,3,2,1,0:T(2,128)S(1)}, f32[2,4,2,2,128]{4,3,2,1,0:T(2,128)S(1)}, u32[]{:S(2)}, u32[]{:S(2)}) collective-permute-start(f32[2,4,2,2,128]{4,3,2,1,0:T(2,128)S(1)} %get-tuple-element.103), channel_id=1, source_target_pairs={{0,2},{1,3},{2,0},{3,1},{4,6},{5,7},{6,4},{7,5},{8,10},{9,11},{10,... | collective-permute-start | bytes 49160 | tf_op jit(solution)/shard_map/ppermute | solution.py:82
  133.1 15.7 %collective-permute-start.27 = (f32[2,2,4,2,2,128]{5,4,3,2,1,0:T(2,128)S(1)}, f32[2,2,4,2,2,128]{5,4,3,2,1,0:T(2,128)S(1)}, u32[]{:S(2)}, u32[]{:S(2)}) collective-permute-start(f32[2,2,4,2,2,128]{5,4,3,2,1,0:T(2,128)S(1)} %pad_maximum_fusion.2), channel_id=1, source_target_pairs={{0,4},{1,5},{2,6},{3,7},{4,8},{5,9},{6,10},{7,11},{8,12},{9,13},{1... | collective-permute-start | bytes 98312 | tf_op jit(solution)/shard_map/ppermute | solution.py:82
  134.3 14.5 %collective-permute-start.28 = (f32[2,2,4,2,2,128]{5,4,3,2,1,0:T(2,128)S(1)}, f32[2,2,4,2,2,128]{5,4,3,2,1,0:T(2,128)S(1)}, u32[]{:S(2)}, u32[]{:S(2)}) collective-permute-start(f32[2,2,4,2,2,128]{5,4,3,2,1,0:T(2,128)S(1)} %pad_maximum_fusion.2), channel_id=1, source_target_pairs={{0,8},{1,9},{2,10},{3,11},{4,12},{5,13},{6,14},{7,15},{8,0},{9,1},... | collective-permute-start | bytes 98312 | tf_op jit(solution)/shard_map/ppermute | solution.py:82
  135.0 13.8 %collective-permute-start.29 = (f32[2,2,4,2,2,128]{5,4,3,2,1,0:T(2,128)S(1)}, f32[2,2,4,2,2,128]{5,4,3,2,1,0:T(2,128)S(1)}, u32[]{:S(2)}, u32[]{:S(2)}) collective-permute-start(f32[2,2,4,2,2,128]{5,4,3,2,1,0:T(2,128)S(1)} %pad_maximum_fusion.2), channel_id=1, source_target_pairs={{0,12},{1,13},{2,14},{3,15},{4,0},{5,1},{6,2},{7,3},{8,4},{9,5},{1... | collective-permute-start | bytes 98312 | tf_op jit(solution)/shard_map/ppermute | solution.py:82
  137.1 3.5 %copy-start.1 = (bf16[8,1088,512]{2,1,0:T(8,128)(2,1)S(1)}, bf16[8,1088,512]{2,1,0:T(8,128)(2,1)}, u32[]{:S(2)}) copy-start(bf16[8,1088,512]{2,1,0:T(8,128)(2,1)} %copy-done) | copy-start | bytes 26738692
  148.1 2.7 %collective-permute-start.36 = (f32[64,512]{1,0:T(8,128)S(1)}, f32[64,512]{1,0:T(8,128)S(1)}, u32[]{:S(2)}, u32[]{:S(2)}) collective-permute-start(f32[64,512]{1,0:T(8,128)S(1)} %slice.182), channel_id=1, source_target_pairs={{0,1},{1,0},{2,3},{3,2},{4,5},{5,4},{6,7},{7,6},{8,9},{9,8},{10,11... | collective-permute-start | bytes 393224 | tf_op jit(solution)/shard_map/ppermute | solution.py:82
  148.2 1.7 collective-permute-start.31
  150.2 5.8 %collective-permute-start.32 = (bf16[4,128,128]{2,1,0:T(8,128)(2,1)S(1)}, bf16[4,128,128]{2,1,0:T(8,128)(2,1)S(1)}, u32[]{:S(2)}, u32[]{:S(2)}) collective-permute-start(bf16[4,128,128]{2,1,0:T(8,128)(2,1)S(1)} %slice_bitcast_fusion), channel_id=1, source_target_pairs={{0,2},{1,3},{2,0},{3,1},{4,6},{5,7},{6,4},{7,5},{8,10},{9,11},{10,... | collective-permute-start | bytes 393224 | tf_op jit(solution)/shard_map/ppermute | solution.py:82
  156.1 5.8 %collective-permute-start.33 = (bf16[128,128]{1,0:T(8,128)(2,1)S(1)}, bf16[128,128]{1,0:T(8,128)(2,1)S(1)}, u32[]{:S(2)}, u32[]{:S(2)}) collective-permute-start(bf16[128,128]{1,0:T(8,128)(2,1)S(1)} %get-tuple-element.91), channel_id=1, source_target_pairs={{0,4},{1,5},{2,6},{3,7},{4,8},{5,9},{6,10},{7,11},{8,12},{9,13},{1... | collective-permute-start | bytes 98312 | tf_op jit(solution)/shard_map/ppermute | solution.py:82
  156.6 5.3 %collective-permute-start.34 = (bf16[128,128]{1,0:T(8,128)(2,1)S(1)}, bf16[128,128]{1,0:T(8,128)(2,1)S(1)}, u32[]{:S(2)}, u32[]{:S(2)}) collective-permute-start(bf16[128,128]{1,0:T(8,128)(2,1)S(1)} %get-tuple-element.93), channel_id=1, source_target_pairs={{0,8},{1,9},{2,10},{3,11},{4,12},{5,13},{6,14},{7,15},{8,0},{9,1},... | collective-permute-start | bytes 98312 | tf_op jit(solution)/shard_map/ppermute | solution.py:82
  158.3 4.3 %collective-permute-start.35 = (bf16[128,128]{1,0:T(8,128)(2,1)S(1)}, bf16[128,128]{1,0:T(8,128)(2,1)S(1)}, u32[]{:S(2)}, u32[]{:S(2)}) collective-permute-start(bf16[128,128]{1,0:T(8,128)(2,1)S(1)} %get-tuple-element.92), channel_id=1, source_target_pairs={{0,12},{1,13},{2,14},{3,15},{4,0},{5,1},{6,2},{7,3},{8,4},{9,5},{1... | collective-permute-start | bytes 98312 | tf_op jit(solution)/shard_map/ppermute | solution.py:82
  166.5 2.0 %collective-permute-start.37 = (bf16[64,4096]{1,0:T(8,128)(2,1)S(1)}, bf16[64,4096]{1,0:T(8,128)(2,1)S(1)}, u32[]{:S(2)}, u32[]{:S(2)}) collective-permute-start(bf16[64,4096]{1,0:T(8,128)(2,1)S(1)} %slice.194), channel_id=1, source_target_pairs={{0,1},{1,0},{2,3},{3,2},{4,5},{5,4},{6,7},{7,6},{8,9},{9,8},{10,11... | collective-permute-start | bytes 1572872 | tf_op jit(solution)/shard_map/ppermute | solution.py:82
  168.6 8.4 %collective-permute-start.38 = (bf16[64,2048]{1,0:T(8,128)(2,1)S(1)}, bf16[64,2048]{1,0:T(8,128)(2,1)S(1)}, u32[]{:S(2)}, u32[]{:S(2)}) collective-permute-start(bf16[64,2048]{1,0:T(8,128)(2,1)S(1)} %slice.196), channel_id=1, source_target_pairs={{0,2},{1,3},{2,0},{3,1},{4,6},{5,7},{6,4},{7,5},{8,10},{9,11},{10,... | collective-permute-start | bytes 786440 | tf_op jit(solution)/shard_map/ppermute | solution.py:82
  177.1 7.2 %collective-permute-start.39 = (bf16[64,512]{1,0:T(8,128)(2,1)S(1)}, bf16[64,512]{1,0:T(8,128)(2,1)S(1)}, u32[]{:S(2)}, u32[]{:S(2)}) collective-permute-start(bf16[64,512]{1,0:T(8,128)(2,1)S(1)} %get-tuple-element.88), channel_id=1, source_target_pairs={{0,4},{1,5},{2,6},{3,7},{4,8},{5,9},{6,10},{7,11},{8,12},{9,13},{1... | collective-permute-start | bytes 196616 | tf_op jit(solution)/shard_map/ppermute | solution.py:82
  179.0 6.9 %collective-permute-start.40 = (bf16[64,512]{1,0:T(8,128)(2,1)S(1)}, bf16[64,512]{1,0:T(8,128)(2,1)S(1)}, u32[]{:S(2)}, u32[]{:S(2)}) collective-permute-start(bf16[64,512]{1,0:T(8,128)(2,1)S(1)} %get-tuple-element.90), channel_id=1, source_target_pairs={{0,8},{1,9},{2,10},{3,11},{4,12},{5,13},{6,14},{7,15},{8,0},{9,1},... | collective-permute-start | bytes 196616 | tf_op jit(solution)/shard_map/ppermute | solution.py:82
  181.8 4.5 %collective-permute-start.41 = (bf16[64,512]{1,0:T(8,128)(2,1)S(1)}, bf16[64,512]{1,0:T(8,128)(2,1)S(1)}, u32[]{:S(2)}, u32[]{:S(2)}) collective-permute-start(bf16[64,512]{1,0:T(8,128)(2,1)S(1)} %get-tuple-element.89), channel_id=1, source_target_pairs={{0,12},{1,13},{2,14},{3,15},{4,0},{5,1},{6,2},{7,3},{8,4},{9,5},{1... | collective-permute-start | bytes 196616 | tf_op jit(solution)/shard_map/ppermute | solution.py:82
  (16 other events, 30.0 us)

commit v8 on v7

--- a/solution.py
+++ b/solution.py
@@ -98,36 +98,6 @@
 
 MIB = 1024 * 1024
 LIGHT = pl.CostEstimate(flops=1, bytes_accessed=1, transcendentals=0)
-
-
-def pick(source, blocks, width):
-    count = blocks.shape[0]
-    rows = source.shape[0]
-
-    def body(block_ref, source_ref, out_ref, sems):
-        copies = []
-        for i in range(count):
-            start = pl.multiple_of(block_ref[i] * width, width)
-            copies.append(
-                pltpu.make_async_copy(
-                    source_ref.at[:, pl.ds(start, width)],
-                    out_ref.at[:, pl.ds(i * width, width)],
-                    sems.at[i],
-                )
-            )
-            copies[-1].start()
-        for copy in copies:
-            copy.wait()
-
-    return pl.pallas_call(
-        body,
-        in_specs=[pl.BlockSpec(memory_space=pltpu.SMEM), pl.BlockSpec(memory_space=pltpu.HBM)],
-        out_specs=pl.BlockSpec(memory_space=pltpu.VMEM),
-        out_shape=jax.ShapeDtypeStruct((rows, count * width), source.dtype),
-        scratch_shapes=[pltpu.SemaphoreType.DMA((count,))],
-        compiler_params=pltpu.CompilerParams(vmem_limit_bytes=12 * MIB),
-        cost_estimate=LIGHT,
-    )(blocks, source)
 
 
 def project_queries(steps, weight, cosine, sine):
@@ -198,7 +168,7 @@
     )(*arrays)
 
 
-def assemble(prompt, steps, got, blocks, width):
+def assemble(prompt, got, steps, blocks, width):
     count = blocks.shape[0]
     row_count, step_count = prompt.shape[0], steps.shape[0]
     height = 2 * row_count + step_count
@@ -210,7 +180,7 @@
             for j, (source, start, rows) in enumerate(
                 (
                     (prompt_ref.at[:, column], 0, row_count),
-                    (got_ref.at[:, pl.ds(i * width, width)], row_count, row_count),
+                    (got_ref.at[:, column], row_count, row_count),
                     (step_ref.at[:, column], 2 * row_count, step_count),
                 )
             ):
@@ -235,7 +205,7 @@
     )(blocks, prompt, got, steps)
 
 
-def project(left, which, pieces, acc):
+def project(left, which, pieces, acc, kind=jnp.float32):
     arrays = []
     for piece in pieces:
         for array, _ in piece:
@@ -247,6 +217,7 @@
 
     def body(left_ref, *refs):
         out_ref = refs[-1]
+        total = {}
         for i, piece in enumerate(pieces):
             side = 0
             for array, first in piece:
@@ -258,11 +229,12 @@
                     preferred_element_type=jnp.float32,
                 )
                 if i:
-                    out_ref[:, place] += product
+                    product += total[place.start]
                 elif extra:
-                    out_ref[:, place] = refs[len(arrays)][:, place] + product
-                else:
-                    out_ref[:, place] = product
+                    product += refs[len(arrays)][:, place]
+                total[place.start] = product
+                if i == len(pieces) - 1:
+                    out_ref[:, place] = product.astype(kind)
                 side += array.shape[1]
 
     whole = pl.BlockSpec(memory_space=pltpu.VMEM)
@@ -270,8 +242,8 @@
         body,
         in_specs=[whole] * (1 + len(arrays) + len(extra)),
         out_specs=whole,
-        out_shape=jax.ShapeDtypeStruct((height, columns), jnp.float32),
-        compiler_params=pltpu.CompilerParams(vmem_limit_bytes=28 * MIB),
+        out_shape=jax.ShapeDtypeStruct((height, columns), kind),
+        compiler_params=pltpu.CompilerParams(vmem_limit_bytes=24 * MIB),
         cost_estimate=LIGHT,
     )(left, *arrays, *extra)
 
@@ -293,8 +265,8 @@
         weight_ref, top_ref, total_ref = refs[-3:]
         keys = jnp.concatenate(
             [
-                own_ref[:half, :] + other_ref[half:tokens, :],
-                own_ref[half:tokens, :] + other_ref[:half, :],
+                own_ref[:half, :].astype(jnp.float32) + other_ref[half:tokens, :],
+                own_ref[half:tokens, :].astype(jnp.float32) + other_ref[:half, :],
             ],
             axis=0,
         )
@@ -350,7 +322,7 @@
             row,
             row,
         ],
-        compiler_params=pltpu.CompilerParams(vmem_limit_bytes=20 * MIB),
+        compiler_params=pltpu.CompilerParams(vmem_limit_bytes=14 * MIB),
         cost_estimate=LIGHT,
     )(places, turns, *([*queries] * share), own, other, cosine, sine, *masks)
 
@@ -360,7 +332,7 @@
 
     def body(place_ref, weight_ref, value_ref, out_ref):
         summed = lax.dot_general(
-            value_ref[:tokens, :].astype(jnp.bfloat16),
+            value_ref[:tokens, :],
             weight_ref[0],
             (((0,), (0,)), ((), ())),
             preferred_element_type=jnp.float32,
@@ -379,7 +351,7 @@
             out_specs=pl.BlockSpec((1, count, HEAD_DIM), lambda j, ref: (j, 0, 0)),
         ),
         out_shape=jax.ShapeDtypeStruct((kv_heads, count, HEAD_DIM), jnp.bfloat16),
-        compiler_params=pltpu.CompilerParams(vmem_limit_bytes=20 * MIB),
+        compiler_params=pltpu.CompilerParams(vmem_limit_bytes=8 * MIB),
         cost_estimate=LIGHT,
     )(places, weights, values)
 
@@ -399,7 +371,7 @@
         in_specs=[pl.BlockSpec(memory_space=pltpu.SMEM), whole, whole],
         out_specs=whole,
         out_shape=jax.ShapeDtypeStruct(shape, jnp.bfloat16),
-        compiler_params=pltpu.CompilerParams(vmem_limit_bytes=20 * MIB),
+        compiler_params=pltpu.CompilerParams(vmem_limit_bytes=10 * MIB),
         cost_estimate=LIGHT,
     )(blocks, heads, weight)
 
@@ -480,6 +452,7 @@
         moved.append(move(after(value, moved[-2]) if len(moved) > 1 else value))
         return moved[-1]
 
+    got = in_chip(prompt_states)
     key_z, mine, theirs = {0: key_mine}, {0: value_mine}, {}
     key_z[1] = send(along_ring, key_z[0])
     mine[1] = send(along_ring, mine[0])
@@ -497,15 +470,14 @@
             key_z[k + 1] = send(along_ring, key_z[k])
             mine[k + 1] = send(along_ring, mine[k])
         key_full[k] = jnp.concatenate([key_z[k], swapped])
-        key_y[k] = send(along_y, after(key_full[k], key_y[k - 1]))
-        if k == 1:
-            sent_blocks = jnp.stack([block(behind(j), flip, 1 - own_c) for j, flip in places])
-            sent = pick(prompt_states, after(sent_blocks, (key_z[2], swapped, mine[1])), width)
-            got = in_chip(sent)
+        if k == deep - 1:
+            left = assemble(
+                prompt_states, got, wide_states, after(own_blocks, (key_y[1], mine[2])), width
+            )
+        key_y[k] = send(along_y, after(key_full[k], (key_y[k - 1], left) if k == deep - 1 else key_y[k - 1]))
     for k in range(1, deep):
         theirs[k] = send(along_ring, theirs[k - 1])
         theirs_x[k] = send(along_x, theirs[k])
-    left = assemble(prompt_states, wide_states, got, after(own_blocks, (key_y[1], mine[2])), width)
 
     ring_queries = collect([theirs[k] for k in range(deep)], width, 2 * packed)
     ring_queries = [ring_queries, in_chip(ring_queries)]
@@ -537,8 +509,8 @@
         for k, flip in places
     ]
 
-    def project_blocks(pieces, which, acc, ready):
-        return project(after(left, ready), which, [pieces[i] for i in which], acc)
+    def project_blocks(pieces, which, acc, ready, kind=jnp.float32):
+        return project(after(left, ready), which, [pieces[i] for i in which], acc, kind)
 
     last = 2 * deep - 2
     key_early = project_blocks(
@@ -547,13 +519,14 @@
     early = [*range(0, 2 * deep, 2), 1]
     value_early = project_blocks(value_pieces, early, None, (key_early, theirs_x[1]))
     key_sum = project_blocks(
-        key_pieces, [last, last + 1], key_early, (value_early, theirs[deep - 1], theirs_x[deep - 2])
+        key_pieces, [last, last + 1], key_early, (value_early, theirs[deep - 1], theirs_x[deep - 2]), jnp.bfloat16
     )
     key_back = in_chip(key_sum)
     own_place = lax.dynamic_index_in_dim(kv_places, own_kv, 0, False) * HEAD_DIM
 
     def own_head(sums):
-        return lax.dynamic_slice_in_dim(sums, own_place, HEAD_DIM, 1).reshape(2, samples, HEAD_DIM)
+        sums = lax.dynamic_slice_in_dim(sums, own_place, HEAD_DIM, 1)
+        return sums.reshape(2, samples, HEAD_DIM).astype(jnp.float32)
 
     new_keys = own_head(key_sum[chip_rows:]) + own_head(key_back[chip_rows:])
     new_keys = turn(new_keys, step_tables).astype(jnp.bfloat16)
@@ -577,11 +550,9 @@
     prefix_total = lax.dynamic_index_in_dim(prefix_total, own_a, 0, False)[0, 0]
 
     late = [i for i in range(2 * deep) if i not in early]
-    value_sum = project_blocks(value_pieces, late, value_early, weights)
+    value_sum = project_blocks(value_pieces, late, value_early, weights, jnp.bfloat16)
     step_values = own_head(value_sum[chip_rows:])
-    step_back = lax.dynamic_slice_in_dim(
-        in_chip(value_sum[chip_rows:]), own_place, HEAD_DIM, 1
-    ).reshape(step_values.shape)
+    step_back = own_head(in_chip(value_sum[chip_rows:]))
     new_values = (step_values + step_back).astype(jnp.bfloat16)
     partial = apply_weights(kv_places, weights, value_sum)
     partial = partial.reshape(by_owner + (HEAD_DIM,))

time: 188 us -> 178 us (0.947)
  waiting for transfers between devices: 56.5 us -> 37 us
  local copies, waits for them, and re-layouts: 30.7 us -> 40 us
  Pallas kernels: 32 us -> 30 us
    ppermute x42, waiting for transfers between devices: 56.5 us -> 37 us  [move(): return lax.ppermute(value, ('groups', 'sample'), pairs)]
    unnamed x84, local copies, waits for them, and re-layouts: 26 us -> 30.5 us
    pallas_call x1 -> x0, Pallas kernels: 3.31 us -> none  [pick(): pl.pallas_call(body, in_specs=[pl.BlockSpec(memory_space=pltpu.SMEM), pl....]
    pallas_call x4, Pallas kernels: 12.5 us -> 14.6 us  [project(): pl.pallas_call(body, in_specs=[whole] * (1 + len(arrays) + len(extra)), o...]
  transfers between devices with their start and end apart: 42 -> 42, of which waited for: 21 -> 18; matrix products, arithmetic and copies ran while one was open for 7% -> 11% of each run, Pallas kernels for 13% -> 15%
where the time goes in v8:
time: 178 us; the launch traced here: 177 us
  starting transfers between devices  58.8 us (33%)
  local copies, waits for them, and re-layouts  40 us (22%)
  waiting for transfers between devices  37 us (21%)
  Pallas kernels  30 us (17%)
  other arithmetic  10 us (6%)
    ppermute x42, starting transfers between devices, move(): return lax.ppermute(value, ('groups', 'sample'), pairs)  58.8 us
    ppermute x42, waiting for transfers between devices, move(): return lax.ppermute(value, ('groups', 'sample'), pairs)  37 us
    unnamed x84, local copies, waits for them, and re-layouts  30.5 us
    pallas_call x4, Pallas kernels, project(): pl.pallas_call(body, in_specs=[whole] * (1 + len(arrays) + len(extra)), o...  14.6 us
    pallas_call x1, Pallas kernels, attend(): pl.pallas_call(body, grid_spec=pltpu.PrefetchScalarGridSpec(num_scalar_pr...  6.08 us
  transfers between devices with their start and end apart: 42, of which 18 were waited for; matrix products, arithmetic and copies ran while one was open for 11% of the time, Pallas kernels for 15%

profile of v8, /device:TPU:0, one launch (start us, length us, event | category | flops | bytes accessed | tf_op | source)
XLA Modules:
  0.0 177.2 jit_solution(4358634630596793410)
XLA Ops:
  0.5 1.8 broadcast_select_fusion
  2.2 2.6 %collective-permute-start = (bf16[512,256]{1,0:T(8,128)(2,1)S(1)}, bf16[512,256]{1,0:T(8,128)(2,1)S(1)}, u32[]{:S(2)}, u32[]{:S(2)}) collective-permute-start(bf16[512,256]{1,0:T(8,128)(2,1)S(1)} %get-tuple-element.83.refs_0_), channel_id=1, source_target_pairs={{0,2},{1,3},{2,0},{3,1},{4,6},{5,7},{6,4},{7,5},{8,10},{9,11},{10,... | collective-permute-start | bytes 786440 | tf_op jit(solution)/shard_map/ppermute | solution.py:82
  4.8 1.1 broadcast_select_fusion.2
  5.9 2.6 %collective-permute-start.1 = (bf16[512,256]{1,0:T(8,128)(2,1)S(1)}, bf16[512,256]{1,0:T(8,128)(2,1)S(1)}, u32[]{:S(2)}, u32[]{:S(2)}) collective-permute-start(bf16[512,256]{1,0:T(8,128)(2,1)S(1)} %get-tuple-element.84), channel_id=1, source_target_pairs={{0,8},{1,9},{2,10},{3,11},{4,0},{5,1},{6,2},{7,3},{8,12},{9,13},{1... | collective-permute-start | bytes 786440 | tf_op jit(solution)/shard_map/ppermute | solution.py:82
  8.8 2.2 %copy-done.5 = bf16[8192,256]{1,0:T(8,128)(2,1)S(1)} copy-done((bf16[8192,256]{1,0:T(8,128)(2,1)S(1)}, bf16[8192,256]{1,0:T(8,128)(2,1)}, u32[]{:S(2)}) %copy-start.5) | copy-done | bytes 4194328
  11.0 2.0 %shard_map.73 = bf16[64,256]{1,0:T(8,128)(2,1)S(1)} custom-call(bf16[64,8192]{1,0:T(8,128)(2,1)S(1)} %bitcast.146, bf16[8192,256]{1,0:T(8,128)(2,1)S(1)} %copy-done.5, f32[64,128]{1,0:T(8,128)S(1)} %bitcast.149, f32[64,128]{1,0:T(8,128)S(1)} %bitcast.150), custom_call_target="tpu_custom_call" | custom-call | flops 1 | bytes 1 | tf_op jit(solution)/shard_map/pallas_call | solution.py:132
  13.0 1.4 collective-permute-done.1
  14.9 3.4 %collective-permute-start.6 = (bf16[512,256]{1,0:T(8,128)(2,1)S(1)}, bf16[512,256]{1,0:T(8,128)(2,1)S(1)}, u32[]{:S(2)}, u32[]{:S(2)}) collective-permute-start(bf16[512,256]{1,0:T(8,128)(2,1)S(1)} %get-tuple-element.83.refs_0_), channel_id=1, source_target_pairs={{0,8},{1,9},{2,10},{3,11},{4,0},{5,1},{6,2},{7,3},{8,12},{9,13},{1... | collective-permute-start | bytes 786440 | tf_op jit(solution)/shard_map/ppermute | solution.py:82
  18.3 1.5 collective-permute-start.12
  19.8 3.3 %collective-permute-done.6.refs_2_ = bf16[512,256]{1,0:T(8,128)(2,1)S(1)} collective-permute-done((bf16[512,256]{1,0:T(8,128)(2,1)S(1)}, bf16[512,256]{1,0:T(8,128)(2,1)S(1)}, u32[]{:S(2)}, u32[]{:S(2)}) %collective-permute-start.6) | collective-permute-done | bytes 262176 | tf_op jit(solution)/shard_map/ppermute | solution.py:82
  23.1 3.4 %collective-permute-start.7 = (bf16[512,256]{1,0:T(8,128)(2,1)S(1)}, bf16[512,256]{1,0:T(8,128)(2,1)S(1)}, u32[]{:S(2)}, u32[]{:S(2)}) collective-permute-start(bf16[512,256]{1,0:T(8,128)(2,1)S(1)} %collective-permute-done.6.refs_2_), channel_id=1, source_target_pairs={{0,8},{1,9},{2,10},{3,11},{4,0},{5,1},{6,2},{7,3},{8,12},{9,13},{1... | collective-permute-start | bytes 786440 | tf_op jit(solution)/shard_map/ppermute | solution.py:82
  26.5 1.6 collective-permute-start.18
  28.3 1.4 collective-permute-start.13
  29.7 6.2 %collective-permute-done.3 = bf16[512,256]{1,0:T(8,128)(2,1)S(1)} collective-permute-done((bf16[512,256]{1,0:T(8,128)(2,1)S(1)}, bf16[512,256]{1,0:T(8,128)(2,1)S(1)}, u32[]{:S(2)}, u32[]{:S(2)}) %collective-permute-start.3) | collective-permute-done | bytes 262176 | tf_op jit(solution)/shard_map/ppermute | solution.py:82
  36.0 3.4 %collective-permute-start.4 = (bf16[512,256]{1,0:T(8,128)(2,1)S(1)}, bf16[512,256]{1,0:T(8,128)(2,1)}, u32[]{:S(2)}, u32[]{:S(2)}) collective-permute-start(bf16[512,256]{1,0:T(8,128)(2,1)S(1)} %collective-permute-done.3), channel_id=1, source_target_pairs={{0,8},{1,9},{2,10},{3,11},{4,0},{5,1},{6,2},{7,3},{8,12},{9,13},{1... | collective-permute-start | bytes 786440 | tf_op jit(solution)/shard_map/ppermute | solution.py:82
  40.0 1.5 collective-permute-start.19
  43.5 3.5 %collective-permute-start.8 = (bf16[512,256]{1,0:T(8,128)(2,1)S(1)}, bf16[512,256]{1,0:T(8,128)(2,1)}, u32[]{:S(2)}, u32[]{:S(2)}) collective-permute-start(bf16[512,256]{1,0:T(8,128)(2,1)S(1)} %collective-permute-done.7.refs_4_), channel_id=1, source_target_pairs={{0,8},{1,9},{2,10},{3,11},{4,0},{5,1},{6,2},{7,3},{8,12},{9,13},{1... | collective-permute-start | bytes 786440 | tf_op jit(solution)/shard_map/ppermute | solution.py:82
  49.1 1.5 collective-permute-start.20
  52.1 1.5 collective-permute-start.16
  54.9 2.1 %collective-permute-done.5.refs_1_.refs_0_ = bf16[640,256]{1,0:T(8,128)(2,1)S(1)} collective-permute-done((bf16[640,256]{1,0:T(8,128)(2,1)S(1)}, bf16[640,256]{1,0:T(8,128)(2,1)S(1)}, u32[]{:S(2)}, u32[]{:S(2)}) %collective-permute-start.5) | collective-permute-done | bytes 327712 | tf_op jit(solution)/shard_map/ppermute | solution.py:82
  57.0 3.4 %collective-permute-start.9 = (bf16[640,256]{1,0:T(8,128)(2,1)S(1)}, bf16[640,256]{1,0:T(8,128)(2,1)S(1)}, u32[]{:S(2)}, u32[]{:S(2)}) collective-permute-start(bf16[640,256]{1,0:T(8,128)(2,1)S(1)} %collective-permute-done.5.refs_1_.refs_0_), channel_id=1, source_target_pairs={{0,8},{1,9},{2,10},{3,11},{4,0},{5,1},{6,2},{7,3},{8,12},{9,13},{1... | collective-permute-start | bytes 983048 | tf_op jit(solution)/shard_map/ppermute | solution.py:82
  60.4 1.7 constant_dynamic-update-slice_fusion.5
  62.1 1.5 collective-permute-start.17
  63.6 1.4 collective-permute-done.21
  64.9 1.7 constant_dynamic-update-slice_fusion.4.refs_0_
  66.6 3.4 %copy-done.4 = bf16[512,8192]{1,0:T(8,128)(2,1)S(1)} copy-done((bf16[512,8192]{1,0:T(8,128)(2,1)S(1)}, bf16[512,8192]{1,0:T(8,128)(2,1)}, u32[]{:S(2)}) %copy-start.4) | copy-done | bytes 8388632
  70.0 3.2 %shard_map.75.left_ref = bf16[8,1088,512]{2,1,0:T(8,128)(2,1)S(1)} custom-call(s32[8]{0:T(128)S(1)} %stack.141.block_ref, bf16[512,8192]{1,0:T(8,128)(2,1)S(1)} %copy-done.4, bf16[512,8192]{1,0:T(8,128)(2,1)} %collective-permute-done.14.got_ref, bf16[64,8192]{1,0:T(8,128)(2,1)S(1)} %bitcast.147), custom_call_target="tpu_custom_call" | custom-call | flops 1 | bytes 1 | tf_op jit(solution)/shard_map/pallas_call | solution.py:197
  73.2 3.5 %copy-done = bf16[8,1088,512]{2,1,0:T(8,128)(2,1)} copy-done((bf16[8,1088,512]{2,1,0:T(8,128)(2,1)}, bf16[8,1088,512]{2,1,0:T(8,128)(2,1)S(1)}, u32[]{:S(2)}) %copy-start) | copy-done | bytes 8912920
  76.7 1.5 collective-permute-start.24
  78.9 1.5 collective-permute-start.22
  83.3 3.5 %copy-done.1 = bf16[8,1088,512]{2,1,0:T(8,128)(2,1)S(1)} copy-done((bf16[8,1088,512]{2,1,0:T(8,128)(2,1)S(1)}, bf16[8,1088,512]{2,1,0:T(8,128)(2,1)}, u32[]{:S(2)}) %copy-start.1) | copy-done | bytes 8912920
  86.8 1.0 copy-done.11
  87.9 1.1 copy-done.16
  90.0 4.8 %shard_map.76.refs_2_ = f32[1088,512]{1,0:T(8,128)S(1)} custom-call(bf16[8,1088,512]{2,1,0:T(8,128)(2,1)S(1)} %copy-done.1, bf16[1088,256]{1,0:T(8,128)(2,1)S(1)} %pad_maximum_fusion.refs_0_, bf16[1088,256]{1,0:T(8,128)(2,1)S(1)} %copy-done.16, bf16[1024,256]{1,0:T(8,128)(2,1)S(1)} %copy-done.11, bf16[1024,256]{1,0:T(8,128)(2,1)S(1)} %copy-done.18, ...), custom_call_target="tpu_custom_call" | custom-call | flops 1 | bytes 1 | tf_op jit(solution)/shard_map/pallas_call | solution.py:241
  95.7 4.1 %shard_map.77.refs_6_ = f32[1088,512]{1,0:T(8,128)S(1)} custom-call(bf16[8,1088,512]{2,1,0:T(8,128)(2,1)S(1)} %copy-done.2, bf16[512,256]{1,0:T(8,128)(2,1)S(1)} %copy-done.14, bf16[512,256]{1,0:T(8,128)(2,1)S(1)} %copy-done.12, bf16[512,256]{1,0:T(8,128)(2,1)S(1)} %copy-done.22, bf16[512,256]{1,0:T(8,128)(2,1)S(1)} %copy-done.26, ...), custom_call_target="tpu_custom_call" | custom-call | flops 1 | bytes 1 | tf_op jit(solution)/shard_map/pallas_call | solution.py:241
  99.8 2.5 %shard_map.78.refs_2_ = bf16[1088,512]{1,0:T(8,128)(2,1)S(1)} custom-call(bf16[8,1088,512]{2,1,0:T(8,128)(2,1)S(1)} %copy-done.2, bf16[1024,256]{1,0:T(8,128)(2,1)} %constant_dynamic-update-slice_fusion.4.refs_0_, bf16[1024,256]{1,0:T(8,128)(2,1)} %collective-permute-done.24.refs_1_, f32[1088,512]{1,0:T(8,128)S(1)} %shard_map.76.refs_2_), custom_call_target="tpu_custom_call" | custom-call | flops 1 | bytes 1 | tf_op jit(solution)/shard_map/pallas_call | solution.py:241
  102.9 1.9 %multiply_sine_fusion = (f32[1024,64]{1,0:T(8,128)S(1)}, f32[1024,64]{1,0:T(8,128)S(1)}) fusion(f32[64]{0:T(128)S(1)} %multiply_power_fusion, f32[1024]{0:T(1024)S(1)} %convert_bitcast_fusion), kind=kLoop, calls=%fused_computation.1 | loop fusion | flops 65536 | bytes 528640 | tf_op jit(solution)/shard_map/sin | solution.py:23
  105.7 1.5 collective-permute-start.30
  108.2 6.1 %shard_map.79 = (bf16[4,1024,512]{2,1,0:T(8,128)(2,1)S(1)}, f32[4,1,512]{2,1,0:T(1,128)S(1)}, f32[4,1,512]{2,1,0:T(1,128)S(1)}) custom-call(s32[4]{0:T(128)S(1)} %and_select_fusion.1.place_ref, s32[4]{0:T(128)S(1)} %pad_add_fusion.turn_ref, bf16[4,128,256]{2,1,0:T(8,128)(2,1)S(1)} %shard_map.74.refs_0_, ...), custom_call_target="tpu_custom_call" | custom-call | flops 1 | bytes 1 | tf_op jit(solution)/shard_map/pallas_call | solution.py:305
  114.3 2.1 %copy-done.7 = bf16[4,1024,512]{2,1,0:T(8,128)(2,1)} copy-done((bf16[4,1024,512]{2,1,0:T(8,128)(2,1)}, bf16[4,1024,512]{2,1,0:T(8,128)(2,1)S(1)}, u32[]{:S(2)}) %copy-start.7) | copy-done | bytes 4194328
  118.9 1.3 copy.61
  120.2 1.3 copy.60
  121.5 1.3 copy.56
  122.8 1.3 rev.3
  124.9 1.8 %collective-permute-start.27 = (f32[2,2,4,2,2,128]{5,4,3,2,1,0:T(2,128)S(1)}, f32[2,2,4,2,2,128]{5,4,3,2,1,0:T(2,128)S(1)}, u32[]{:S(2)}, u32[]{:S(2)}) collective-permute-start(f32[2,2,4,2,2,128]{5,4,3,2,1,0:T(2,128)S(1)} %pad_maximum_fusion.2), channel_id=1, source_target_pairs={{0,4},{1,5},{2,6},{3,7},{4,8},{5,9},{6,10},{7,11},{8,12},{9,13},{1... | collective-permute-start | bytes 98312 | tf_op jit(solution)/shard_map/ppermute | solution.py:82
  126.7 1.1 collective-permute-start.28
  127.9 1.7 collective-permute-start.29
  129.5 3.5 %copy-done.3 = bf16[8,1088,512]{2,1,0:T(8,128)(2,1)S(1)} copy-done((bf16[8,1088,512]{2,1,0:T(8,128)(2,1)S(1)}, bf16[8,1088,512]{2,1,0:T(8,128)(2,1)}, u32[]{:S(2)}) %copy-start.3) | copy-done | bytes 8912920
  133.1 3.1 %shard_map.80.value_ref = bf16[1088,512]{1,0:T(8,128)(2,1)S(1)} custom-call(bf16[8,1088,512]{2,1,0:T(8,128)(2,1)S(1)} %copy-done.3, bf16[640,256]{1,0:T(8,128)(2,1)S(1)} %collective-permute-done.5.refs_1_.refs_0_, bf16[640,256]{1,0:T(8,128)(2,1)S(1)} %copy-done.20, bf16[640,256]{1,0:T(8,128)(2,1)S(1)} %collective-permute-done.9.refs_2_, ...), custom_call_target="tpu_custom_call" | custom-call | flops 1 | bytes 1 | tf_op jit(solution)/shard_map/pallas_call | solution.py:241
  136.3 2.4 %shard_map.81 = bf16[4,512,128]{2,1,0:T(8,128)(2,1)S(1)} custom-call(s32[4]{0:T(128)S(1)} %and_select_fusion.1.place_ref, bf16[4,1024,512]{2,1,0:T(8,128)(2,1)S(1)} %copy-done.8, bf16[1088,512]{1,0:T(8,128)(2,1)S(1)} %shard_map.80.value_ref), custom_call_target="tpu_custom_call" | custom-call | flops 1 | bytes 1 | tf_op jit(solution)/shard_map/pallas_call | solution.py:342
  140.8 1.6 collective-permute-start.32
  142.5 4.2 %collective-permute-done.32 = bf16[4,128,128]{2,1,0:T(8,128)(2,1)S(1)} collective-permute-done((bf16[4,128,128]{2,1,0:T(8,128)(2,1)S(1)}, bf16[4,128,128]{2,1,0:T(8,128)(2,1)S(1)}, u32[]{:S(2)}, u32[]{:S(2)}) %collective-permute-start.32) | collective-permute-done | bytes 131104 | tf_op jit(solution)/shard_map/ppermute | solution.py:82
  147.1 1.8 %collective-permute-start.34 = (bf16[128,128]{1,0:T(8,128)(2,1)S(1)}, bf16[128,128]{1,0:T(8,128)(2,1)S(1)}, u32[]{:S(2)}, u32[]{:S(2)}) collective-permute-start(bf16[128,128]{1,0:T(8,128)(2,1)S(1)} %get-tuple-element.91), channel_id=1, source_target_pairs={{0,8},{1,9},{2,10},{3,11},{4,12},{5,13},{6,14},{7,15},{8,0},{9,1},... | collective-permute-start | bytes 98312 | tf_op jit(solution)/shard_map/ppermute | solution.py:82
  149.0 2.1 %collective-permute-start.35 = (bf16[128,128]{1,0:T(8,128)(2,1)S(1)}, bf16[128,128]{1,0:T(8,128)(2,1)S(1)}, u32[]{:S(2)}, u32[]{:S(2)}) collective-permute-start(bf16[128,128]{1,0:T(8,128)(2,1)S(1)} %get-tuple-element.90), channel_id=1, source_target_pairs={{0,12},{1,13},{2,14},{3,15},{4,0},{5,1},{6,2},{7,3},{8,4},{9,5},{1... | collective-permute-start | bytes 98312 | tf_op jit(solution)/shard_map/ppermute | solution.py:82
  151.0 1.5 collective-permute-done.33
  153.3 2.2 %copy-done.6 = bf16[256,8192]{1,0:T(8,128)(2,1)S(1)} copy-done((bf16[256,8192]{1,0:T(8,128)(2,1)S(1)}, bf16[256,8192]{1,0:T(8,128)(2,1)}, u32[]{:S(2)}) %copy-start.6) | copy-done | bytes 4194328
  155.5 1.4 shard_map.82
  157.0 1.9 %collective-permute-done.37 = bf16[64,4096]{1,0:T(8,128)(2,1)S(1)} collective-permute-done((bf16[64,4096]{1,0:T(8,128)(2,1)S(1)}, bf16[64,4096]{1,0:T(8,128)(2,1)S(1)}, u32[]{:S(2)}, u32[]{:S(2)}) %collective-permute-start.37) | collective-permute-done | bytes 524320 | tf_op jit(solution)/shard_map/ppermute | solution.py:82
  159.1 1.6 collective-permute-start.38
  160.6 6.9 %collective-permute-done.38 = bf16[64,2048]{1,0:T(8,128)(2,1)S(1)} collective-permute-done((bf16[64,2048]{1,0:T(8,128)(2,1)S(1)}, bf16[64,2048]{1,0:T(8,128)(2,1)S(1)}, u32[]{:S(2)}, u32[]{:S(2)}) %collective-permute-start.38) | collective-permute-done | bytes 262176 | tf_op jit(solution)/shard_map/ppermute | solution.py:82
  167.6 2.1 %collective-permute-start.39 = (bf16[64,512]{1,0:T(8,128)(2,1)S(1)}, bf16[64,512]{1,0:T(8,128)(2,1)S(1)}, u32[]{:S(2)}, u32[]{:S(2)}) collective-permute-start(bf16[64,512]{1,0:T(8,128)(2,1)S(1)} %get-tuple-element.86), channel_id=1, source_target_pairs={{0,4},{1,5},{2,6},{3,7},{4,8},{5,9},{6,10},{7,11},{8,12},{9,13},{1... | collective-permute-start | bytes 196616 | tf_op jit(solution)/shard_map/ppermute | solution.py:82
  169.7 2.2 %collective-permute-start.40 = (bf16[64,512]{1,0:T(8,128)(2,1)S(1)}, bf16[64,512]{1,0:T(8,128)(2,1)S(1)}, u32[]{:S(2)}, u32[]{:S(2)}) collective-permute-start(bf16[64,512]{1,0:T(8,128)(2,1)S(1)} %get-tuple-element.88), channel_id=1, source_target_pairs={{0,8},{1,9},{2,10},{3,11},{4,12},{5,13},{6,14},{7,15},{8,0},{9,1},... | collective-permute-start | bytes 196616 | tf_op jit(solution)/shard_map/ppermute | solution.py:82
  172.1 2.1 %collective-permute-done.39 = bf16[64,512]{1,0:T(8,128)(2,1)S(1)} collective-permute-done((bf16[64,512]{1,0:T(8,128)(2,1)S(1)}, bf16[64,512]{1,0:T(8,128)(2,1)S(1)}, u32[]{:S(2)}, u32[]{:S(2)}) %collective-permute-start.39) | collective-permute-done | bytes 65568 | tf_op jit(solution)/shard_map/ppermute | solution.py:82
  174.2 2.1 %collective-permute-done.40 = bf16[64,512]{1,0:T(8,128)(2,1)S(1)} collective-permute-done((bf16[64,512]{1,0:T(8,128)(2,1)S(1)}, bf16[64,512]{1,0:T(8,128)(2,1)S(1)}, u32[]{:S(2)}, u32[]{:S(2)}) %collective-permute-start.40) | collective-permute-done | bytes 65568 | tf_op jit(solution)/shard_map/ppermute | solution.py:82
  (191 shorter events, 24.2 us)
Async XLA Ops:
  0.0 8.8 %copy-start.9 = (bf16[2,32,8192]{2,1,0:T(8,128)(2,1)S(1)}, bf16[2,32,8192]{2,1,0:T(8,128)(2,1)}, u32[]{:S(2)}) copy-start(bf16[2,32,8192]{2,1,0:T(8,128)(2,1)} %param.10) | copy-start | bytes 3145732
  0.0 66.6 %collective-permute-start.14 = (bf16[512,8192]{1,0:T(8,128)(2,1)}, bf16[512,8192]{1,0:T(8,128)(2,1)}, u32[]{:S(2)}, u32[]{:S(2)}) collective-permute-start(bf16[512,8192]{1,0:T(8,128)(2,1)} %prompt_ref.1), channel_id=1, source_target_pairs={{0,1},{1,0},{2,3},{3,2},{4,5},{5,4},{6,7},{7,6},{8,9},{9,8},{10,11... | collective-permute-start | bytes 25165832 | tf_op jit(solution)/shard_map/ppermute | solution.py:82
  2.2 12.7 %copy-start.13 = (bf16[512,256]{1,0:T(8,128)(2,1)}, bf16[512,256]{1,0:T(8,128)(2,1)S(1)}, u32[]{:S(2)}) copy-start(bf16[512,256]{1,0:T(8,128)(2,1)S(1)} %get-tuple-element.83.refs_0_) | copy-start | bytes 786436
  2.2 10.8 %collective-permute-start = (bf16[512,256]{1,0:T(8,128)(2,1)S(1)}, bf16[512,256]{1,0:T(8,128)(2,1)S(1)}, u32[]{:S(2)}, u32[]{:S(2)}) collective-permute-start(bf16[512,256]{1,0:T(8,128)(2,1)S(1)} %get-tuple-element.83.refs_0_), channel_id=1, source_target_pairs={{0,2},{1,3},{2,0},{3,1},{4,6},{5,7},{6,4},{7,5},{8,10},{9,11},{10,... | collective-permute-start | bytes 786440 | tf_op jit(solution)/shard_map/ppermute | solution.py:82
  5.9 8.5 %collective-permute-start.1 = (bf16[512,256]{1,0:T(8,128)(2,1)S(1)}, bf16[512,256]{1,0:T(8,128)(2,1)S(1)}, u32[]{:S(2)}, u32[]{:S(2)}) collective-permute-start(bf16[512,256]{1,0:T(8,128)(2,1)S(1)} %get-tuple-element.84), channel_id=1, source_target_pairs={{0,8},{1,9},{2,10},{3,11},{4,0},{5,1},{6,2},{7,3},{8,12},{9,13},{1... | collective-permute-start | bytes 786440 | tf_op jit(solution)/shard_map/ppermute | solution.py:82
  14.4 13.9 %collective-permute-start.2 = (bf16[1088,256]{1,0:T(8,128)(2,1)S(1)}, bf16[1088,256]{1,0:T(8,128)(2,1)S(1)}, u32[]{:S(2)}, u32[]{:S(2)}) collective-permute-start(bf16[1088,256]{1,0:T(8,128)(2,1)S(1)} %pad_maximum_fusion.refs_0_), channel_id=1, source_target_pairs={{0,2},{1,3},{2,0},{3,1},{4,6},{5,7},{6,4},{7,5},{8,10},{9,11},{10,... | collective-permute-start | bytes 1671176 | tf_op jit(solution)/shard_map/ppermute | solution.py:82
  14.9 8.2 %collective-permute-start.6 = (bf16[512,256]{1,0:T(8,128)(2,1)S(1)}, bf16[512,256]{1,0:T(8,128)(2,1)S(1)}, u32[]{:S(2)}, u32[]{:S(2)}) collective-permute-start(bf16[512,256]{1,0:T(8,128)(2,1)S(1)} %get-tuple-element.83.refs_0_), channel_id=1, source_target_pairs={{0,8},{1,9},{2,10},{3,11},{4,0},{5,1},{6,2},{7,3},{8,12},{9,13},{1... | collective-permute-start | bytes 786440 | tf_op jit(solution)/shard_map/ppermute | solution.py:82
  18.3 8.2 %collective-permute-start.12 = (bf16[512,256]{1,0:T(8,128)(2,1)S(1)}, bf16[512,256]{1,0:T(8,128)(2,1)S(1)}, u32[]{:S(2)}, u32[]{:S(2)}) collective-permute-start(bf16[512,256]{1,0:T(8,128)(2,1)S(1)} %collective-permute-done.1), channel_id=1, source_target_pairs={{0,16},{1,17},{2,18},{3,19},{4,20},{5,21},{6,22},{7,23},{8,24},{9,... | collective-permute-start | bytes 786440 | tf_op jit(solution)/shard_map/ppermute | solution.py:82
  23.1 18.4 %copy-start.21 = (bf16[512,256]{1,0:T(8,128)(2,1)}, bf16[512,256]{1,0:T(8,128)(2,1)S(1)}, u32[]{:S(2)}) copy-start(bf16[512,256]{1,0:T(8,128)(2,1)S(1)} %collective-permute-done.6.refs_2_) | copy-start | bytes 786436
  23.1 18.4 %collective-permute-start.7 = (bf16[512,256]{1,0:T(8,128)(2,1)S(1)}, bf16[512,256]{1,0:T(8,128)(2,1)S(1)}, u32[]{:S(2)}, u32[]{:S(2)}) collective-permute-start(bf16[512,256]{1,0:T(8,128)(2,1)S(1)} %collective-permute-done.6.refs_2_), channel_id=1, source_target_pairs={{0,8},{1,9},{2,10},{3,11},{4,0},{5,1},{6,2},{7,3},{8,12},{9,13},{1... | collective-permute-start | bytes 786440 | tf_op jit(solution)/shard_map/ppermute | solution.py:82
  26.5 9.5 %collective-permute-start.3 = (bf16[512,256]{1,0:T(8,128)(2,1)S(1)}, bf16[512,256]{1,0:T(8,128)(2,1)S(1)}, u32[]{:S(2)}, u32[]{:S(2)}) collective-permute-start(bf16[512,256]{1,0:T(8,128)(2,1)S(1)} %collective-permute-done.1), channel_id=1, source_target_pairs={{0,8},{1,9},{2,10},{3,11},{4,0},{5,1},{6,2},{7,3},{8,12},{9,13},{1... | collective-permute-start | bytes 786440 | tf_op jit(solution)/shard_map/ppermute | solution.py:82
  26.5 12.8 %collective-permute-start.18 = (bf16[512,256]{1,0:T(8,128)(2,1)S(1)}, bf16[512,256]{1,0:T(8,128)(2,1)S(1)}, u32[]{:S(2)}, u32[]{:S(2)}) collective-permute-start(bf16[512,256]{1,0:T(8,128)(2,1)S(1)} %collective-permute-done.6.refs_2_), channel_id=1, source_target_pairs={{0,16},{1,17},{2,18},{3,19},{4,20},{5,21},{6,22},{7,23},{8,24},{9,... | collective-permute-start | bytes 786440 | tf_op jit(solution)/shard_map/ppermute | solution.py:82
  28.1 20.2 %copy-start.10 = (bf16[1024,256]{1,0:T(8,128)(2,1)}, bf16[1024,256]{1,0:T(8,128)(2,1)S(1)}, u32[]{:S(2)}) copy-start(bf16[1024,256]{1,0:T(8,128)(2,1)S(1)} %constant_dynamic-update-slice_fusion.refs_2_) | copy-start | bytes 1572868
  28.3 20.0 %collective-permute-start.13 = (bf16[1024,256]{1,0:T(8,128)(2,1)S(1)}, bf16[1024,256]{1,0:T(8,128)(2,1)S(1)}, u32[]{:S(2)}, u32[]{:S(2)}) collective-permute-start(bf16[1024,256]{1,0:T(8,128)(2,1)S(1)} %constant_dynamic-update-slice_fusion.refs_2_), channel_id=1, source_target_pairs={{0,2},{1,3},{2,0},{3,1},{4,6},{5,7},{6,4},{7,5},{8,10},{9,11},{10,... | collective-permute-start | bytes 1572872 | tf_op jit(solution)/shard_map/ppermute | solution.py:82
  36.0 7.6 %collective-permute-start.4 = (bf16[512,256]{1,0:T(8,128)(2,1)S(1)}, bf16[512,256]{1,0:T(8,128)(2,1)}, u32[]{:S(2)}, u32[]{:S(2)}) collective-permute-start(bf16[512,256]{1,0:T(8,128)(2,1)S(1)} %collective-permute-done.3), channel_id=1, source_target_pairs={{0,8},{1,9},{2,10},{3,11},{4,0},{5,1},{6,2},{7,3},{8,12},{9,13},{1... | collective-permute-start | bytes 786440 | tf_op jit(solution)/shard_map/ppermute | solution.py:82
  40.0 7.9 %collective-permute-start.19 = (bf16[512,256]{1,0:T(8,128)(2,1)S(1)}, bf16[512,256]{1,0:T(8,128)(2,1)S(1)}, u32[]{:S(2)}, u32[]{:S(2)}) collective-permute-start(bf16[512,256]{1,0:T(8,128)(2,1)S(1)} %collective-permute-done.3), channel_id=1, source_target_pairs={{0,16},{1,17},{2,18},{3,19},{4,20},{5,21},{6,22},{7,23},{8,24},{9,... | collective-permute-start | bytes 786440 | tf_op jit(solution)/shard_map/ppermute | solution.py:82
  41.5 9.9 %collective-permute-start.15 = (bf16[512,256]{1,0:T(8,128)(2,1)S(1)}, bf16[512,256]{1,0:T(8,128)(2,1)S(1)}, u32[]{:S(2)}, u32[]{:S(2)}) collective-permute-start(bf16[512,256]{1,0:T(8,128)(2,1)S(1)} %collective-permute-done), channel_id=1, source_target_pairs={{0,16},{1,17},{2,18},{3,19},{4,20},{5,21},{6,22},{7,23},{8,24},{9,... | collective-permute-start | bytes 786440 | tf_op jit(solution)/shard_map/ppermute | solution.py:82
  43.5 10.8 %collective-permute-start.8 = (bf16[512,256]{1,0:T(8,128)(2,1)S(1)}, bf16[512,256]{1,0:T(8,128)(2,1)}, u32[]{:S(2)}, u32[]{:S(2)}) collective-permute-start(bf16[512,256]{1,0:T(8,128)(2,1)S(1)} %collective-permute-done.7.refs_4_), channel_id=1, source_target_pairs={{0,8},{1,9},{2,10},{3,11},{4,0},{5,1},{6,2},{7,3},{8,12},{9,13},{1... | collective-permute-start | bytes 786440 | tf_op jit(solution)/shard_map/ppermute | solution.py:82
  48.0 9.0 %collective-permute-start.5 = (bf16[640,256]{1,0:T(8,128)(2,1)S(1)}, bf16[640,256]{1,0:T(8,128)(2,1)S(1)}, u32[]{:S(2)}, u32[]{:S(2)}) collective-permute-start(bf16[640,256]{1,0:T(8,128)(2,1)S(1)} %pad_maximum_fusion.1.refs_0_.refs_8_), channel_id=1, source_target_pairs={{0,8},{1,9},{2,10},{3,11},{4,0},{5,1},{6,2},{7,3},{8,12},{9,13},{1... | collective-permute-start | bytes 983048 | tf_op jit(solution)/shard_map/ppermute | solution.py:82
  49.1 27.6 %collective-permute-start.20 = (bf16[1024,256]{1,0:T(8,128)(2,1)S(1)}, bf16[1024,256]{1,0:T(8,128)(2,1)}, u32[]{:S(2)}, u32[]{:S(2)}) collective-permute-start(bf16[1024,256]{1,0:T(8,128)(2,1)S(1)} %constant_dynamic-update-slice_fusion.2.refs_4_), channel_id=1, source_target_pairs={{0,2},{1,3},{2,0},{3,1},{4,6},{5,7},{6,4},{7,5},{8,10},{9,11},{10,... | collective-permute-start | bytes 1572872 | tf_op jit(solution)/shard_map/ppermute | solution.py:82
  52.1 9.9 %collective-permute-start.16 = (bf16[512,256]{1,0:T(8,128)(2,1)S(1)}, bf16[512,256]{1,0:T(8,128)(2,1)}, u32[]{:S(2)}, u32[]{:S(2)}) collective-permute-start(bf16[512,256]{1,0:T(8,128)(2,1)S(1)} %collective-permute-done.7.refs_4_), channel_id=1, source_target_pairs={{0,16},{1,17},{2,18},{3,19},{4,20},{5,21},{6,22},{7,23},{8,24},{9,... | collective-permute-start | bytes 786440 | tf_op jit(solution)/shard_map/ppermute | solution.py:82
  54.3 10.6 %collective-permute-start.21 = (bf16[512,256]{1,0:T(8,128)(2,1)}, bf16[512,256]{1,0:T(8,128)(2,1)}, u32[]{:S(2)}, u32[]{:S(2)}) collective-permute-start(bf16[512,256]{1,0:T(8,128)(2,1)} %collective-permute-done.4), channel_id=1, source_target_pairs={{0,16},{1,17},{2,18},{3,19},{4,20},{5,21},{6,22},{7,23},{8,24},{9,... | collective-permute-start | bytes 786440 | tf_op jit(solution)/shard_map/ppermute | solution.py:82
  57.0 24.0 %collective-permute-start.9 = (bf16[640,256]{1,0:T(8,128)(2,1)S(1)}, bf16[640,256]{1,0:T(8,128)(2,1)S(1)}, u32[]{:S(2)}, u32[]{:S(2)}) collective-permute-start(bf16[640,256]{1,0:T(8,128)(2,1)S(1)} %collective-permute-done.5.refs_1_.refs_0_), channel_id=1, source_target_pairs={{0,8},{1,9},{2,10},{3,11},{4,0},{5,1},{6,2},{7,3},{8,12},{9,13},{1... | collective-permute-start | bytes 983048 | tf_op jit(solution)/shard_map/ppermute | solution.py:82
  62.1 18.3 %collective-permute-start.17 = (bf16[512,256]{1,0:T(8,128)(2,1)}, bf16[512,256]{1,0:T(8,128)(2,1)S(1)}, u32[]{:S(2)}, u32[]{:S(2)}) collective-permute-start(bf16[512,256]{1,0:T(8,128)(2,1)} %collective-permute-done.8.refs_6_), channel_id=1, source_target_pairs={{0,16},{1,17},{2,18},{3,19},{4,20},{5,21},{6,22},{7,23},{8,24},{9,... | collective-permute-start | bytes 786440 | tf_op jit(solution)/shard_map/ppermute | solution.py:82
  66.6 3.4 %copy-start.4 = (bf16[512,8192]{1,0:T(8,128)(2,1)S(1)}, bf16[512,8192]{1,0:T(8,128)(2,1)}, u32[]{:S(2)}) copy-start(bf16[512,8192]{1,0:T(8,128)(2,1)} %prompt_ref.1) | copy-start | bytes 25165828
  73.2 3.5 %copy-start = (bf16[8,1088,512]{2,1,0:T(8,128)(2,1)}, bf16[8,1088,512]{2,1,0:T(8,128)(2,1)S(1)}, u32[]{:S(2)}) copy-start(bf16[8,1088,512]{2,1,0:T(8,128)(2,1)S(1)} %shard_map.75.left_ref) | copy-start | bytes 26738692
  76.7 23.1 %collective-permute-start.24 = (bf16[1024,256]{1,0:T(8,128)(2,1)}, bf16[1024,256]{1,0:T(8,128)(2,1)}, u32[]{:S(2)}, u32[]{:S(2)}) collective-permute-start(bf16[1024,256]{1,0:T(8,128)(2,1)} %constant_dynamic-update-slice_fusion.4.refs_0_), channel_id=1, source_target_pairs={{0,2},{1,3},{2,0},{3,1},{4,6},{5,7},{6,4},{7,5},{8,10},{9,11},{10,... | collective-permute-start | bytes 1572872 | tf_op jit(solution)/shard_map/ppermute | solution.py:82
  78.9 16.0 %collective-permute-start.22 = (bf16[640,256]{1,0:T(8,128)(2,1)S(1)}, bf16[640,256]{1,0:T(8,128)(2,1)S(1)}, u32[]{:S(2)}, u32[]{:S(2)}) collective-permute-start(bf16[640,256]{1,0:T(8,128)(2,1)S(1)} %collective-permute-done.5.refs_1_.refs_0_), channel_id=1, source_target_pairs={{0,16},{1,17},{2,18},{3,19},{4,20},{5,21},{6,22},{7,23},{8,24},{9,... | collective-permute-start | bytes 983048 | tf_op jit(solution)/shard_map/ppermute | solution.py:82
  81.0 18.7 %collective-permute-start.23 = (bf16[640,256]{1,0:T(8,128)(2,1)S(1)}, bf16[640,256]{1,0:T(8,128)(2,1)}, u32[]{:S(2)}, u32[]{:S(2)}) collective-permute-start(bf16[640,256]{1,0:T(8,128)(2,1)S(1)} %collective-permute-done.9.refs_2_), channel_id=1, source_target_pairs={{0,16},{1,17},{2,18},{3,19},{4,20},{5,21},{6,22},{7,23},{8,24},{9,... | collective-permute-start | bytes 983048 | tf_op jit(solution)/shard_map/ppermute | solution.py:82
  81.6 18.2 %collective-permute-start.10 = (bf16[640,256]{1,0:T(8,128)(2,1)S(1)}, bf16[640,256]{1,0:T(8,128)(2,1)S(1)}, u32[]{:S(2)}, u32[]{:S(2)}) collective-permute-start(bf16[640,256]{1,0:T(8,128)(2,1)S(1)} %collective-permute-done.9.refs_2_), channel_id=1, source_target_pairs={{0,8},{1,9},{2,10},{3,11},{4,0},{5,1},{6,2},{7,3},{8,12},{9,13},{1... | collective-permute-start | bytes 983048 | tf_op jit(solution)/shard_map/ppermute | solution.py:82
  83.3 3.5 %copy-start.1 = (bf16[8,1088,512]{2,1,0:T(8,128)(2,1)S(1)}, bf16[8,1088,512]{2,1,0:T(8,128)(2,1)}, u32[]{:S(2)}) copy-start(bf16[8,1088,512]{2,1,0:T(8,128)(2,1)} %copy-done) | copy-start | bytes 26738692
  90.0 5.7 %copy-start.2 = (bf16[8,1088,512]{2,1,0:T(8,128)(2,1)S(1)}, bf16[8,1088,512]{2,1,0:T(8,128)(2,1)}, u32[]{:S(2)}) copy-start(bf16[8,1088,512]{2,1,0:T(8,128)(2,1)} %copy-done) | copy-start | bytes 26738692
  90.0 5.7 %copy-start.12 = (bf16[512,256]{1,0:T(8,128)(2,1)S(1)}, bf16[512,256]{1,0:T(8,128)(2,1)}, u32[]{:S(2)}) copy-start(bf16[512,256]{1,0:T(8,128)(2,1)} %get-tuple-element.82.refs_1_) | copy-start | bytes 786436
  90.0 5.7 %copy-start.14 = (bf16[512,256]{1,0:T(8,128)(2,1)S(1)}, bf16[512,256]{1,0:T(8,128)(2,1)}, u32[]{:S(2)}) copy-start(bf16[512,256]{1,0:T(8,128)(2,1)} %copy-done.13) | copy-start | bytes 786436
  90.0 5.7 %copy-start.22 = (bf16[512,256]{1,0:T(8,128)(2,1)S(1)}, bf16[512,256]{1,0:T(8,128)(2,1)}, u32[]{:S(2)}) copy-start(bf16[512,256]{1,0:T(8,128)(2,1)} %copy-done.21) | copy-start | bytes 786436
  90.0 5.7 %copy-start.24 = (bf16[512,256]{1,0:T(8,128)(2,1)S(1)}, bf16[512,256]{1,0:T(8,128)(2,1)}, u32[]{:S(2)}) copy-start(bf16[512,256]{1,0:T(8,128)(2,1)} %copy-done.23) | copy-start | bytes 786436
  90.0 5.7 %copy-start.26 = (bf16[512,256]{1,0:T(8,128)(2,1)S(1)}, bf16[512,256]{1,0:T(8,128)(2,1)}, u32[]{:S(2)}) copy-start(bf16[512,256]{1,0:T(8,128)(2,1)} %copy-done.25) | copy-start | bytes 786436
  90.0 5.7 %copy-start.28 = (bf16[512,256]{1,0:T(8,128)(2,1)S(1)}, bf16[512,256]{1,0:T(8,128)(2,1)}, u32[]{:S(2)}) copy-start(bf16[512,256]{1,0:T(8,128)(2,1)} %copy-done.27) | copy-start | bytes 786436
  90.0 5.7 %copy-start.30 = (bf16[512,256]{1,0:T(8,128)(2,1)S(1)}, bf16[512,256]{1,0:T(8,128)(2,1)}, u32[]{:S(2)}) copy-start(bf16[512,256]{1,0:T(8,128)(2,1)} %copy-done.29) | copy-start | bytes 786436
  102.3 5.1 %copy-start.31 = (f32[2,32,2,128]{3,2,1,0:T(2,128)S(1)}, f32[2,32,2,128]{3,2,1,0:T(2,128)}, u32[]{:S(2)}) copy-start(f32[2,32,2,128]{3,2,1,0:T(2,128)} %reshape.422) | copy-start | bytes 196612
  102.3 4.9 %collective-permute-start.25 = (bf16[1088,512]{1,0:T(8,128)(2,1)S(1)}, bf16[1088,512]{1,0:T(8,128)(2,1)S(1)}, u32[]{:S(2)}, u32[]{:S(2)}) collective-permute-start(bf16[1088,512]{1,0:T(8,128)(2,1)S(1)} %shard_map.78.refs_2_), channel_id=1, source_target_pairs={{0,1},{1,0},{2,3},{3,2},{4,5},{5,4},{6,7},{7,6},{8,9},{9,8},{10,11... | collective-permute-start | bytes 3342344 | tf_op jit(solution)/shard_map/ppermute | solution.py:82
  105.2 3.1 %collective-permute-start.11 = (bf16[4,128,256]{2,1,0:T(8,128)(2,1)S(1)}, bf16[4,128,256]{2,1,0:T(8,128)(2,1)S(1)}, u32[]{:S(2)}, u32[]{:S(2)}) collective-permute-start(bf16[4,128,256]{2,1,0:T(8,128)(2,1)S(1)} %shard_map.74.refs_0_), channel_id=1, source_target_pairs={{0,1},{1,0},{2,3},{3,2},{4,5},{5,4},{6,7},{7,6},{8,9},{9,8},{10,11... | collective-permute-start | bytes 786440 | tf_op jit(solution)/shard_map/ppermute | solution.py:82
  105.7 23.8 %collective-permute-start.30 = (bf16[640,256]{1,0:T(8,128)(2,1)S(1)}, bf16[640,256]{1,0:T(8,128)(2,1)}, u32[]{:S(2)}, u32[]{:S(2)}) collective-permute-start(bf16[640,256]{1,0:T(8,128)(2,1)S(1)} %collective-permute-done.10.refs_3_.refs_4_), channel_id=1, source_target_pairs={{0,16},{1,17},{2,18},{3,19},{4,20},{5,21},{6,22},{7,23},{8,24},{9,... | collective-permute-start | bytes 983048 | tf_op jit(solution)/shard_map/ppermute | solution.py:82
  107.4 22.1 %copy-start.20 = (bf16[640,256]{1,0:T(8,128)(2,1)S(1)}, bf16[640,256]{1,0:T(8,128)(2,1)}, u32[]{:S(2)}) copy-start(bf16[640,256]{1,0:T(8,128)(2,1)} %copy-done.19) | copy-start | bytes 983044
  117.0 5.8 %collective-permute-start.26 = (f32[2,4,2,2,128]{4,3,2,1,0:T(2,128)}, f32[2,4,2,2,128]{4,3,2,1,0:T(2,128)}, u32[]{:S(2)}, u32[]{:S(2)}) collective-permute-start(f32[2,4,2,2,128]{4,3,2,1,0:T(2,128)} %get-tuple-element.101), channel_id=1, source_target_pairs={{0,2},{1,3},{2,0},{3,1},{4,6},{5,7},{6,4},{7,5},{8,10},{9,11},{10,... | collective-permute-start | bytes 49160 | tf_op jit(solution)/shard_map/ppermute | solution.py:82
  124.9 14.5 %collective-permute-start.27 = (f32[2,2,4,2,2,128]{5,4,3,2,1,0:T(2,128)S(1)}, f32[2,2,4,2,2,128]{5,4,3,2,1,0:T(2,128)S(1)}, u32[]{:S(2)}, u32[]{:S(2)}) collective-permute-start(f32[2,2,4,2,2,128]{5,4,3,2,1,0:T(2,128)S(1)} %pad_maximum_fusion.2), channel_id=1, source_target_pairs={{0,4},{1,5},{2,6},{3,7},{4,8},{5,9},{6,10},{7,11},{8,12},{9,13},{1... | collective-permute-start | bytes 98312 | tf_op jit(solution)/shard_map/ppermute | solution.py:82
  126.7 12.7 %collective-permute-start.28 = (f32[2,2,4,2,2,128]{5,4,3,2,1,0:T(2,128)S(1)}, f32[2,2,4,2,2,128]{5,4,3,2,1,0:T(2,128)S(1)}, u32[]{:S(2)}, u32[]{:S(2)}) collective-permute-start(f32[2,2,4,2,2,128]{5,4,3,2,1,0:T(2,128)S(1)} %pad_maximum_fusion.2), channel_id=1, source_target_pairs={{0,8},{1,9},{2,10},{3,11},{4,12},{5,13},{6,14},{7,15},{8,0},{9,1},... | collective-permute-start | bytes 98312 | tf_op jit(solution)/shard_map/ppermute | solution.py:82
  127.9 11.6 %collective-permute-start.29 = (f32[2,2,4,2,2,128]{5,4,3,2,1,0:T(2,128)S(1)}, f32[2,2,4,2,2,128]{5,4,3,2,1,0:T(2,128)S(1)}, u32[]{:S(2)}, u32[]{:S(2)}) collective-permute-start(f32[2,2,4,2,2,128]{5,4,3,2,1,0:T(2,128)S(1)} %pad_maximum_fusion.2), channel_id=1, source_target_pairs={{0,12},{1,13},{2,14},{3,15},{4,0},{5,1},{6,2},{7,3},{8,4},{9,5},{1... | collective-permute-start | bytes 98312 | tf_op jit(solution)/shard_map/ppermute | solution.py:82
  129.5 3.5 %copy-start.3 = (bf16[8,1088,512]{2,1,0:T(8,128)(2,1)S(1)}, bf16[8,1088,512]{2,1,0:T(8,128)(2,1)}, u32[]{:S(2)}) copy-start(bf16[8,1088,512]{2,1,0:T(8,128)(2,1)} %copy-done) | copy-start | bytes 26738692
  133.1 3.1 %copy-start.8 = (bf16[4,1024,512]{2,1,0:T(8,128)(2,1)S(1)}, bf16[4,1024,512]{2,1,0:T(8,128)(2,1)}, u32[]{:S(2)}) copy-start(bf16[4,1024,512]{2,1,0:T(8,128)(2,1)} %copy-done.7) | copy-start | bytes 12582916
  136.2 3.7 %copy-start.35 = (f32[2,32]{1,0:T(2,128)S(1)}, f32[2,32]{1,0:T(2,128)}, u32[]{:S(2)}) copy-start(f32[2,32]{1,0:T(2,128)} %copy.61) | copy-start | bytes 772
  136.2 3.7 %copy-start.36 = (f32[1,2,32]{2,1,0:T(2,128)S(1)}, f32[1,2,32]{2,1,0:T(2,128)}, u32[]{:S(2)}) copy-start(f32[1,2,32]{2,1,0:T(2,128)} %copy.60) | copy-start | bytes 772
  138.7 3.7 %copy-start.34 = (f32[1,2,32]{2,1,0:T(2,128)S(1)}, f32[1,2,32]{2,1,0:T(2,128)}, u32[]{:S(2)}) copy-start(f32[1,2,32]{2,1,0:T(2,128)} %copy.56) | copy-start | bytes 772
  138.7 3.7 %collective-permute-start.36 = (bf16[64,512]{1,0:T(8,128)(2,1)S(1)}, bf16[64,512]{1,0:T(8,128)(2,1)S(1)}, u32[]{:S(2)}, u32[]{:S(2)}) collective-permute-start(bf16[64,512]{1,0:T(8,128)(2,1)S(1)} %slice.182), channel_id=1, source_target_pairs={{0,1},{1,0},{2,3},{3,2},{4,5},{5,4},{6,7},{7,6},{8,9},{9,8},{10,11... | collective-permute-start | bytes 196616 | tf_op jit(solution)/shard_map/ppermute | solution.py:82
  138.9 1.7 collective-permute-start.31
  140.8 5.8 %collective-permute-start.32 = (bf16[4,128,128]{2,1,0:T(8,128)(2,1)S(1)}, bf16[4,128,128]{2,1,0:T(8,128)(2,1)S(1)}, u32[]{:S(2)}, u32[]{:S(2)}) collective-permute-start(bf16[4,128,128]{2,1,0:T(8,128)(2,1)S(1)} %slice_bitcast_fusion), channel_id=1, source_target_pairs={{0,2},{1,3},{2,0},{3,1},{4,6},{5,7},{6,4},{7,5},{8,10},{9,11},{10,... | collective-permute-start | bytes 393224 | tf_op jit(solution)/shard_map/ppermute | solution.py:82
  146.8 5.8 %collective-permute-start.33 = (bf16[128,128]{1,0:T(8,128)(2,1)S(1)}, bf16[128,128]{1,0:T(8,128)(2,1)S(1)}, u32[]{:S(2)}, u32[]{:S(2)}) collective-permute-start(bf16[128,128]{1,0:T(8,128)(2,1)S(1)} %get-tuple-element.89), channel_id=1, source_target_pairs={{0,4},{1,5},{2,6},{3,7},{4,8},{5,9},{6,10},{7,11},{8,12},{9,13},{1... | collective-permute-start | bytes 98312 | tf_op jit(solution)/shard_map/ppermute | solution.py:82
  147.1 5.4 %collective-permute-start.34 = (bf16[128,128]{1,0:T(8,128)(2,1)S(1)}, bf16[128,128]{1,0:T(8,128)(2,1)S(1)}, u32[]{:S(2)}, u32[]{:S(2)}) collective-permute-start(bf16[128,128]{1,0:T(8,128)(2,1)S(1)} %get-tuple-element.91), channel_id=1, source_target_pairs={{0,8},{1,9},{2,10},{3,11},{4,12},{5,13},{6,14},{7,15},{8,0},{9,1},... | collective-permute-start | bytes 98312 | tf_op jit(solution)/shard_map/ppermute | solution.py:82
  149.0 4.1 %collective-permute-start.35 = (bf16[128,128]{1,0:T(8,128)(2,1)S(1)}, bf16[128,128]{1,0:T(8,128)(2,1)S(1)}, u32[]{:S(2)}, u32[]{:S(2)}) collective-permute-start(bf16[128,128]{1,0:T(8,128)(2,1)S(1)} %get-tuple-element.90), channel_id=1, source_target_pairs={{0,12},{1,13},{2,14},{3,15},{4,0},{5,1},{6,2},{7,3},{8,4},{9,5},{1... | collective-permute-start | bytes 98312 | tf_op jit(solution)/shard_map/ppermute | solution.py:82
  157.0 2.0 %collective-permute-start.37 = (bf16[64,4096]{1,0:T(8,128)(2,1)S(1)}, bf16[64,4096]{1,0:T(8,128)(2,1)S(1)}, u32[]{:S(2)}, u32[]{:S(2)}) collective-permute-start(bf16[64,4096]{1,0:T(8,128)(2,1)S(1)} %slice.194), channel_id=1, source_target_pairs={{0,1},{1,0},{2,3},{3,2},{4,5},{5,4},{6,7},{7,6},{8,9},{9,8},{10,11... | collective-permute-start | bytes 1572872 | tf_op jit(solution)/shard_map/ppermute | solution.py:82
  159.1 8.4 %collective-permute-start.38 = (bf16[64,2048]{1,0:T(8,128)(2,1)S(1)}, bf16[64,2048]{1,0:T(8,128)(2,1)S(1)}, u32[]{:S(2)}, u32[]{:S(2)}) collective-permute-start(bf16[64,2048]{1,0:T(8,128)(2,1)S(1)} %slice.196), channel_id=1, source_target_pairs={{0,2},{1,3},{2,0},{3,1},{4,6},{5,7},{6,4},{7,5},{8,10},{9,11},{10,... | collective-permute-start | bytes 786440 | tf_op jit(solution)/shard_map/ppermute | solution.py:82
  167.6 6.7 %collective-permute-start.39 = (bf16[64,512]{1,0:T(8,128)(2,1)S(1)}, bf16[64,512]{1,0:T(8,128)(2,1)S(1)}, u32[]{:S(2)}, u32[]{:S(2)}) collective-permute-start(bf16[64,512]{1,0:T(8,128)(2,1)S(1)} %get-tuple-element.86), channel_id=1, source_target_pairs={{0,4},{1,5},{2,6},{3,7},{4,8},{5,9},{6,10},{7,11},{8,12},{9,13},{1... | collective-permute-start | bytes 196616 | tf_op jit(solution)/shard_map/ppermute | solution.py:82
  169.7 6.6 %collective-permute-start.40 = (bf16[64,512]{1,0:T(8,128)(2,1)S(1)}, bf16[64,512]{1,0:T(8,128)(2,1)S(1)}, u32[]{:S(2)}, u32[]{:S(2)}) collective-permute-start(bf16[64,512]{1,0:T(8,128)(2,1)S(1)} %get-tuple-element.88), channel_id=1, source_target_pairs={{0,8},{1,9},{2,10},{3,11},{4,12},{5,13},{6,14},{7,15},{8,0},{9,1},... | collective-permute-start | bytes 196616 | tf_op jit(solution)/shard_map/ppermute | solution.py:82
  171.9 4.7 %collective-permute-start.41 = (bf16[64,512]{1,0:T(8,128)(2,1)S(1)}, bf16[64,512]{1,0:T(8,128)(2,1)S(1)}, u32[]{:S(2)}, u32[]{:S(2)}) collective-permute-start(bf16[64,512]{1,0:T(8,128)(2,1)S(1)} %get-tuple-element.87), channel_id=1, source_target_pairs={{0,12},{1,13},{2,14},{3,15},{4,0},{5,1},{6,2},{7,3},{8,4},{9,5},{1... | collective-permute-start | bytes 196616 | tf_op jit(solution)/shard_map/ppermute | solution.py:82
  (16 other events, 22.5 us)

commit v9 on v8

--- a/solution.py
+++ b/solution.py
@@ -200,7 +200,7 @@
         out_specs=pl.BlockSpec(memory_space=pltpu.VMEM),
         out_shape=jax.ShapeDtypeStruct((count, height, width), prompt.dtype),
         scratch_shapes=[pltpu.SemaphoreType.DMA((count, 3))],
-        compiler_params=pltpu.CompilerParams(vmem_limit_bytes=16 * MIB),
+        compiler_params=pltpu.CompilerParams(vmem_limit_bytes=57 * MIB),
         cost_estimate=LIGHT,
     )(blocks, prompt, got, steps)
 
@@ -212,38 +212,56 @@
             if not any(array is held for held in arrays):
                 arrays.append(array)
     _, height, width = left.shape
+    count = len(pieces)
     columns = sum(array.shape[1] for array, _ in pieces[0])
     extra = [] if acc is None else [acc]
 
     def body(left_ref, *refs):
-        out_ref = refs[-1]
-        total = {}
+        out_ref, blocks, weights, held, sems = refs[-5:]
+        groups = []
         for i, piece in enumerate(pieces):
+            group = [pltpu.make_async_copy(left_ref.at[which[i]], blocks.at[i], sems.at[i, 0])]
             side = 0
-            for array, first in piece:
+            for j, (array, first) in enumerate(piece):
                 ref = refs[[array is other for other in arrays].index(True)]
-                place = slice(side, side + array.shape[1])
-                product = jnp.dot(
-                    left_ref[which[i]],
-                    ref[first : first + width, :],
-                    preferred_element_type=jnp.float32,
+                group.append(
+                    pltpu.make_async_copy(
+                        ref.at[pl.ds(first, width), :],
+                        weights.at[i, :, pl.ds(side, array.shape[1])],
+                        sems.at[i, 1 + j],
+                    )
                 )
-                if i:
-                    product += total[place.start]
-                elif extra:
-                    product += refs[len(arrays)][:, place]
-                total[place.start] = product
-                if i == len(pieces) - 1:
-                    out_ref[:, place] = product.astype(kind)
                 side += array.shape[1]
-
-    whole = pl.BlockSpec(memory_space=pltpu.VMEM)
+            for copy in group:
+                copy.start()
+            groups.append(group)
+        if extra:
+            before = pltpu.make_async_copy(refs[len(arrays)], held, sems.at[count, 0])
+            before.start()
+        total = None
+        for i, group in enumerate(groups):
+            for copy in group:
+                copy.wait()
+            product = jnp.dot(blocks[i], weights[i], preferred_element_type=jnp.float32)
+            total = product if total is None else total + product
+        if extra:
+            before.wait()
+            total = total + held[...]
+        out_ref[...] = total.astype(kind)
+
+    anywhere = pl.BlockSpec(memory_space=pl.ANY)
     return pl.pallas_call(
         body,
-        in_specs=[whole] * (1 + len(arrays) + len(extra)),
-        out_specs=whole,
+        in_specs=[anywhere] * (1 + len(arrays) + len(extra)),
+        out_specs=pl.BlockSpec(memory_space=pltpu.VMEM),
         out_shape=jax.ShapeDtypeStruct((height, columns), kind),
-        compiler_params=pltpu.CompilerParams(vmem_limit_bytes=24 * MIB),
+        scratch_shapes=[
+            pltpu.VMEM((count, height, width), left.dtype),
+            pltpu.VMEM((count, width, columns), left.dtype),
+            pltpu.VMEM((height, columns) if extra else (8, 128), jnp.float32),
+            pltpu.SemaphoreType.DMA((count + 1, 3)),
+        ],
+        compiler_params=pltpu.CompilerParams(vmem_limit_bytes=57 * MIB),
         cost_estimate=LIGHT,
     )(left, *arrays, *extra)
 
@@ -322,7 +340,7 @@
             row,
             row,
         ],
-        compiler_params=pltpu.CompilerParams(vmem_limit_bytes=14 * MIB),
+        compiler_params=pltpu.CompilerParams(vmem_limit_bytes=57 * MIB),
         cost_estimate=LIGHT,
     )(places, turns, *([*queries] * share), own, other, cosine, sine, *masks)
 
@@ -351,27 +369,46 @@
             out_specs=pl.BlockSpec((1, count, HEAD_DIM), lambda j, ref: (j, 0, 0)),
         ),
         out_shape=jax.ShapeDtypeStruct((kv_heads, count, HEAD_DIM), jnp.bfloat16),
-        compiler_params=pltpu.CompilerParams(vmem_limit_bytes=8 * MIB),
+        compiler_params=pltpu.CompilerParams(vmem_limit_bytes=57 * MIB),
         cost_estimate=LIGHT,
     )(places, weights, values)
 
 
 def out_project(blocks, heads, weight, width):
-    def body(block_ref, head_ref, weight_ref, out_ref):
-        for i in range(blocks.shape[0]):
+    count = blocks.shape[0]
+    depth = weight.shape[0]
+
+    def body(block_ref, head_ref, weight_ref, out_ref, held, sems):
+        copies = []
+        for i in range(count):
             start = pl.multiple_of(block_ref[i] * width, width)
+            copies.append(
+                pltpu.make_async_copy(
+                    weight_ref.at[:, pl.ds(start, width)], held.at[i], sems.at[i]
+                )
+            )
+            copies[-1].start()
+        for i, copy in enumerate(copies):
+            copy.wait()
             out_ref[:, i * width : (i + 1) * width] = jnp.dot(
-                head_ref[...], weight_ref[:, pl.ds(start, width)], preferred_element_type=jnp.float32
+                head_ref[...], held[i], preferred_element_type=jnp.float32
             ).astype(jnp.bfloat16)
 
     whole = pl.BlockSpec(memory_space=pltpu.VMEM)
-    shape = (heads.shape[0], weight.shape[1])
     return pl.pallas_call(
         body,
-        in_specs=[pl.BlockSpec(memory_space=pltpu.SMEM), whole, whole],
+        in_specs=[
+            pl.BlockSpec(memory_space=pltpu.SMEM),
+            whole,
+            pl.BlockSpec(memory_space=pl.ANY),
+        ],
         out_specs=whole,
-        out_shape=jax.ShapeDtypeStruct(shape, jnp.bfloat16),
-        compiler_params=pltpu.CompilerParams(vmem_limit_bytes=10 * MIB),
+        out_shape=jax.ShapeDtypeStruct((heads.shape[0], weight.shape[1]), jnp.bfloat16),
+        scratch_shapes=[
+            pltpu.VMEM((count, depth, width), weight.dtype),
+            pltpu.SemaphoreType.DMA((count,)),
+        ],
+        compiler_params=pltpu.CompilerParams(vmem_limit_bytes=60 * MIB),
         cost_estimate=LIGHT,
     )(blocks, heads, weight)
 
@@ -443,8 +480,28 @@
     packed = packed_queries.shape[0]
     queries = queries.reshape(2, samples, heads_here, HEAD_DIM)
 
+    own_pages = jnp.concatenate(
+        [
+            holder * pages_here + jnp.arange(pages_here, dtype=jnp.int32)
+            for holder in (own_index, own_index ^ 1)
+        ]
+    )
+    slots = jnp.sum(
+        jnp.where(
+            page_table[None, :] == own_pages[:, None],
+            jnp.arange(total_pages, dtype=jnp.int32)[None, :],
+            0,
+        ),
+        axis=1,
+    )
+    positions = (slots % PROMPT_PAGES * PAGE)[:, None] + jnp.arange(PAGE, dtype=jnp.int32)[None, :]
+    cosine, sine_part = rope_tables(positions.reshape(chip_rows))
+
     places = [(k, flip) for k in range(deep) for flip in (0, 1)]
     own_blocks = jnp.stack([block(behind(k), flip, own_c) for k, flip in places])
+    query_turns = jnp.stack([(own_turn + deep - order.index(a)) % deep for a in range(deep)])
+    own_place = (own_kv + jnp.where(first, 0, KV_HEADS // 2)) % KV_HEADS * HEAD_DIM
+    prepared = (cosine, sine_part, kv_places, query_turns)
     done = {}
 
     def send(move, value):
@@ -470,36 +527,18 @@
             key_z[k + 1] = send(along_ring, key_z[k])
             mine[k + 1] = send(along_ring, mine[k])
         key_full[k] = jnp.concatenate([key_z[k], swapped])
-        if k == deep - 1:
-            left = assemble(
-                prompt_states, got, wide_states, after(own_blocks, (key_y[1], mine[2])), width
-            )
-        key_y[k] = send(along_y, after(key_full[k], (key_y[k - 1], left) if k == deep - 1 else key_y[k - 1]))
+        ready = [key_y[k - 1]]
+        if k == 2:
+            left = assemble(prompt_states, got, wide_states, after(own_blocks, prepared), width)
+            ready.append(left)
+        key_y[k] = send(along_y, after(key_full[k], ready))
     for k in range(1, deep):
         theirs[k] = send(along_ring, theirs[k - 1])
         theirs_x[k] = send(along_x, theirs[k])
 
     ring_queries = collect([theirs[k] for k in range(deep)], width, 2 * packed)
     ring_queries = [ring_queries, in_chip(ring_queries)]
-    query_turns = jnp.stack([(own_turn + deep - order.index(a)) % deep for a in range(deep)])
     by_owner = (deep, 2, 2, rows)
-
-    own_pages = jnp.concatenate(
-        [
-            holder * pages_here + jnp.arange(pages_here, dtype=jnp.int32)
-            for holder in (own_index, own_index ^ 1)
-        ]
-    )
-    slots = jnp.sum(
-        jnp.where(
-            page_table[None, :] == own_pages[:, None],
-            jnp.arange(total_pages, dtype=jnp.int32)[None, :],
-            0,
-        ),
-        axis=1,
-    )
-    positions = (slots % PROMPT_PAGES * PAGE)[:, None] + jnp.arange(PAGE, dtype=jnp.int32)[None, :]
-    cosine, sine_part = rope_tables(positions.reshape(chip_rows))
 
     key_pieces = [
         [((key_y if flip else key_full)[k], start) for start in (0, width)] for k, flip in places
@@ -522,7 +561,6 @@
         key_pieces, [last, last + 1], key_early, (value_early, theirs[deep - 1], theirs_x[deep - 2]), jnp.bfloat16
     )
     key_back = in_chip(key_sum)
-    own_place = lax.dynamic_index_in_dim(kv_places, own_kv, 0, False) * HEAD_DIM
 
     def own_head(sums):
         sums = lax.dynamic_slice_in_dim(sums, own_place, HEAD_DIM, 1)

time: 178 us -> 185 us (1.039)
  local copies, waits for them, and re-layouts: 40 us -> 15.7 us
  Pallas kernels: 30 us -> 53.6 us
  waiting for transfers between devices: 37 us -> 46.4 us
  starting transfers between devices: 58.8 us -> 54 us
  other arithmetic: 10 us -> 12.8 us
    unnamed x84 -> x70, local copies, waits for them, and re-layouts: 30.5 us -> 8.93 us
    ppermute x42, waiting for transfers between devices: 37 us -> 46.4 us  [move(): return lax.ppermute(value, ('groups', 'sample'), pairs)]
    pallas_call x4, Pallas kernels: 14.6 us -> 23.9 us  [project(): pl.pallas_call(body, in_specs=[anywhere] * (1 + len(arrays) + len(extra))...]
    pallas_call x1, Pallas kernels: 3.16 us -> 7.94 us  [assemble(): pl.pallas_call(body, in_specs=[pl.BlockSpec(memory_space=pltpu.SMEM)] + [...]
    ppermute x42, starting transfers between devices: 58.8 us -> 54 us  [move(): return lax.ppermute(value, ('groups', 'sample'), pairs)]
    pallas_call x1, Pallas kernels: 1.39 us -> 5.58 us  [out_project(): pl.pallas_call(body, in_specs=[pl.BlockSpec(memory_space=pltpu.SMEM), who...]
    pallas_call x1, Pallas kernels: 2.43 us -> 5.55 us  [apply_weights(): pl.pallas_call(body, grid_spec=pltpu.PrefetchScalarGridSpec(num_scalar_pr...]
    pallas_call x1, Pallas kernels: 6.08 us -> 8.35 us  [attend(): pl.pallas_call(body, grid_spec=pltpu.PrefetchScalarGridSpec(num_scalar_pr...]
  transfers between devices with their start and end apart: 42 -> 42, of which waited for: 18 -> 18; matrix products, arithmetic and copies ran while one was open for 11% -> 10% of each run, Pallas kernels for 15% -> 24%
where the time goes in v9:
time: 185 us; the launch traced here: 184 us
  starting transfers between devices  54 us (29%)
  Pallas kernels  53.6 us (29%)
  waiting for transfers between devices  46.4 us (25%)
  local copies, waits for them, and re-layouts  15.7 us (8%)
  other arithmetic  12.8 us (7%)
    ppermute x42, starting transfers between devices, move(): return lax.ppermute(value, ('groups', 'sample'), pairs)  54 us
    ppermute x42, waiting for transfers between devices, move(): return lax.ppermute(value, ('groups', 'sample'), pairs)  46.4 us
    pallas_call x4, Pallas kernels, project(): pl.pallas_call(body, in_specs=[anywhere] * (1 + len(arrays) + len(extra))...  23.9 us
    unnamed x70, local copies, waits for them, and re-layouts  8.93 us
    pallas_call x1, Pallas kernels, attend(): pl.pallas_call(body, grid_spec=pltpu.PrefetchScalarGridSpec(num_scalar_pr...  8.35 us
    pallas_call x1, Pallas kernels, assemble(): pl.pallas_call(body, in_specs=[pl.BlockSpec(memory_space=pltpu.SMEM)] + [...  7.94 us
    pallas_call x1, Pallas kernels, out_project(): pl.pallas_call(body, in_specs=[pl.BlockSpec(memory_space=pltpu.SMEM), who...  5.58 us
    pallas_call x1, Pallas kernels, apply_weights(): pl.pallas_call(body, grid_spec=pltpu.PrefetchScalarGridSpec(num_scalar_pr...  5.55 us
  transfers between devices with their start and end apart: 42, of which 18 were waited for; matrix products, arithmetic and copies ran while one was open for 10% of the time, Pallas kernels for 24%

profile of v9, /device:TPU:0, one launch (start us, length us, event | category | flops | bytes accessed | tf_op | source)
XLA Modules:
  0.0 183.6 jit_solution(2691120330111173983)
XLA Ops:
  0.5 1.8 broadcast_select_fusion
  2.2 2.6 %collective-permute-start = (bf16[512,256]{1,0:T(8,128)(2,1)S(1)}, bf16[512,256]{1,0:T(8,128)(2,1)S(1)}, u32[]{:S(2)}, u32[]{:S(2)}) collective-permute-start(bf16[512,256]{1,0:T(8,128)(2,1)S(1)} %get-tuple-element.83.refs_0_), channel_id=1, source_target_pairs={{0,2},{1,3},{2,0},{3,1},{4,6},{5,7},{6,4},{7,5},{8,10},{9,11},{10,... | collective-permute-start | bytes 786440 | tf_op jit(solution)/shard_map/ppermute | solution.py:82
  4.8 2.6 %collective-permute-start.6 = (bf16[512,256]{1,0:T(8,128)(2,1)S(1)}, bf16[512,256]{1,0:T(8,128)(2,1)}, u32[]{:S(2)}, u32[]{:S(2)}) collective-permute-start(bf16[512,256]{1,0:T(8,128)(2,1)S(1)} %get-tuple-element.83.refs_0_), channel_id=1, source_target_pairs={{0,8},{1,9},{2,10},{3,11},{4,0},{5,1},{6,2},{7,3},{8,12},{9,13},{1... | collective-permute-start | bytes 786440 | tf_op jit(solution)/shard_map/ppermute | solution.py:82
  7.4 1.1 broadcast_select_fusion.2
  8.5 1.6 collective-permute-start.1
  10.2 0.8 select_reduce_fusion
  11.3 2.2 %copy-done = bf16[8192,256]{1,0:T(8,128)(2,1)S(1)} copy-done((bf16[8192,256]{1,0:T(8,128)(2,1)S(1)}, bf16[8192,256]{1,0:T(8,128)(2,1)}, u32[]{:S(2)}) %copy-start) | copy-done | bytes 4194328
  13.5 2.0 %shard_map.73 = bf16[64,256]{1,0:T(8,128)(2,1)S(1)} custom-call(bf16[64,8192]{1,0:T(8,128)(2,1)S(1)} %bitcast.146, bf16[8192,256]{1,0:T(8,128)(2,1)S(1)} %copy-done, f32[64,128]{1,0:T(8,128)S(1)} %bitcast.147, f32[64,128]{1,0:T(8,128)S(1)} %bitcast.148), custom_call_target="tpu_custom_call" | custom-call | flops 1 | bytes 1 | tf_op jit(solution)/shard_map/pallas_call | solution.py:132
  15.5 0.7 copy-done.22
  16.3 2.6 %collective-permute-done.1 = bf16[512,256]{1,0:T(8,128)(2,1)} collective-permute-done((bf16[512,256]{1,0:T(8,128)(2,1)S(1)}, bf16[512,256]{1,0:T(8,128)(2,1)}, u32[]{:S(2)}, u32[]{:S(2)}) %collective-permute-start.1) | collective-permute-done | bytes 262176 | tf_op jit(solution)/shard_map/ppermute | solution.py:82
  19.5 1.5 collective-permute-start.13
  21.0 3.1 %multiply_sine_fusion = (f32[1024,64]{1,0:T(8,128)}, f32[1024,64]{1,0:T(8,128)}) fusion(f32[64]{0:T(128)S(1)} %multiply_power_fusion, f32[1024]{0:T(1024)S(1)} %convert_bitcast_fusion), kind=kLoop, calls=%fused_computation.1 | loop fusion | flops 65536 | bytes 528640 | tf_op jit(solution)/shard_map/sin | solution.py:23
  24.1 3.5 %collective-permute-start.3 = (bf16[512,256]{1,0:T(8,128)(2,1)}, bf16[512,256]{1,0:T(8,128)(2,1)S(1)}, u32[]{:S(2)}, u32[]{:S(2)}) collective-permute-start(bf16[512,256]{1,0:T(8,128)(2,1)} %collective-permute-done.1), channel_id=1, source_target_pairs={{0,8},{1,9},{2,10},{3,11},{4,0},{5,1},{6,2},{7,3},{8,12},{9,13},{1... | collective-permute-start | bytes 786440 | tf_op jit(solution)/shard_map/ppermute | solution.py:82
  28.1 1.0 constant_dynamic-update-slice_fusion.3
  29.1 3.7 %collective-permute-done.2.refs_1_ = bf16[1088,256]{1,0:T(8,128)(2,1)S(1)} collective-permute-done((bf16[1088,256]{1,0:T(8,128)(2,1)S(1)}, bf16[1088,256]{1,0:T(8,128)(2,1)S(1)}, u32[]{:S(2)}, u32[]{:S(2)}) %collective-permute-start.2) | collective-permute-done | bytes 557088 | tf_op jit(solution)/shard_map/ppermute | solution.py:82
  35.2 0.9 collective-permute-start.18
  36.0 3.5 %collective-permute-start.4 = (bf16[512,256]{1,0:T(8,128)(2,1)S(1)}, bf16[512,256]{1,0:T(8,128)(2,1)S(1)}, u32[]{:S(2)}, u32[]{:S(2)}) collective-permute-start(bf16[512,256]{1,0:T(8,128)(2,1)S(1)} %collective-permute-done.3), channel_id=1, source_target_pairs={{0,8},{1,9},{2,10},{3,11},{4,0},{5,1},{6,2},{7,3},{8,12},{9,13},{1... | collective-permute-start | bytes 786440 | tf_op jit(solution)/shard_map/ppermute | solution.py:82
  41.5 4.8 %collective-permute-done.4 = bf16[512,256]{1,0:T(8,128)(2,1)S(1)} collective-permute-done((bf16[512,256]{1,0:T(8,128)(2,1)S(1)}, bf16[512,256]{1,0:T(8,128)(2,1)S(1)}, u32[]{:S(2)}, u32[]{:S(2)}) %collective-permute-start.4) | collective-permute-done | bytes 262176 | tf_op jit(solution)/shard_map/ppermute | solution.py:82
  46.8 3.4 %collective-permute-start.5 = (bf16[640,256]{1,0:T(8,128)(2,1)S(1)}, bf16[640,256]{1,0:T(8,128)(2,1)S(1)}, u32[]{:S(2)}, u32[]{:S(2)}) collective-permute-start(bf16[640,256]{1,0:T(8,128)(2,1)S(1)} %pad_maximum_fusion.1.refs_0_.refs_8_), channel_id=1, source_target_pairs={{0,8},{1,9},{2,10},{3,11},{4,0},{5,1},{6,2},{7,3},{8,12},{9,13},{1... | collective-permute-start | bytes 983048 | tf_op jit(solution)/shard_map/ppermute | solution.py:82
  50.2 1.0 constant_dynamic-update-slice_fusion.refs_4_
  51.2 7.9 %shard_map.75.left_ref = bf16[8,1088,512]{2,1,0:T(8,128)(2,1)} custom-call(s32[8]{0:T(128)} %stack.141.block_ref, bf16[512,8192]{1,0:T(8,128)(2,1)} %prompt_ref.1, bf16[512,8192]{1,0:T(8,128)(2,1)} %collective-permute-done.12.got_ref, bf16[64,8192]{1,0:T(8,128)(2,1)} %bitcast.145), custom_call_target="tpu_custom_call" | custom-call | flops 1 | bytes 1 | tf_op jit(solution)/shard_map/pallas_call | solution.py:197
  59.2 1.6 collective-permute-start.20
  60.8 1.6 collective-permute-start.15
  62.9 5.1 %collective-permute-done.8.refs_6_ = bf16[512,256]{1,0:T(8,128)(2,1)S(1)} collective-permute-done((bf16[512,256]{1,0:T(8,128)(2,1)S(1)}, bf16[512,256]{1,0:T(8,128)(2,1)S(1)}, u32[]{:S(2)}, u32[]{:S(2)}) %collective-permute-start.8) | collective-permute-done | bytes 262176 | tf_op jit(solution)/shard_map/ppermute | solution.py:82
  68.0 2.9 %collective-permute-start.9 = (bf16[640,256]{1,0:T(8,128)(2,1)S(1)}, bf16[640,256]{1,0:T(8,128)(2,1)S(1)}, u32[]{:S(2)}, u32[]{:S(2)}) collective-permute-start(bf16[640,256]{1,0:T(8,128)(2,1)S(1)} %collective-permute-done.5.refs_1_.refs_0_), channel_id=1, source_target_pairs={{0,8},{1,9},{2,10},{3,11},{4,0},{5,1},{6,2},{7,3},{8,12},{9,13},{1... | collective-permute-start | bytes 983048 | tf_op jit(solution)/shard_map/ppermute | solution.py:82
  70.9 1.4 collective-permute-start.16
  72.3 3.4 %collective-permute-done.21 = bf16[512,256]{1,0:T(8,128)(2,1)S(1)} collective-permute-done((bf16[512,256]{1,0:T(8,128)(2,1)S(1)}, bf16[512,256]{1,0:T(8,128)(2,1)S(1)}, u32[]{:S(2)}, u32[]{:S(2)}) %collective-permute-start.21) | collective-permute-done | bytes 262176 | tf_op jit(solution)/shard_map/ppermute | solution.py:82
  75.8 2.0 %collective-permute-start.22 = (bf16[640,256]{1,0:T(8,128)(2,1)S(1)}, bf16[640,256]{1,0:T(8,128)(2,1)S(1)}, u32[]{:S(2)}, u32[]{:S(2)}) collective-permute-start(bf16[640,256]{1,0:T(8,128)(2,1)S(1)} %collective-permute-done.5.refs_1_.refs_0_), channel_id=1, source_target_pairs={{0,16},{1,17},{2,18},{3,19},{4,20},{5,21},{6,22},{7,23},{8,24},{9,... | collective-permute-start | bytes 983048 | tf_op jit(solution)/shard_map/ppermute | solution.py:82
  77.8 3.5 %collective-permute-done.16.refs_7_ = bf16[512,256]{1,0:T(8,128)(2,1)S(1)} collective-permute-done((bf16[512,256]{1,0:T(8,128)(2,1)S(1)}, bf16[512,256]{1,0:T(8,128)(2,1)S(1)}, u32[]{:S(2)}, u32[]{:S(2)}) %collective-permute-start.16) | collective-permute-done | bytes 262176 | tf_op jit(solution)/shard_map/ppermute | solution.py:82
  81.3 1.6 collective-permute-start.23
  82.9 0.8 collective-permute-start.10
  83.7 7.4 %shard_map.76.refs_2_ = f32[1088,512]{1,0:T(8,128)} custom-call(bf16[8,1088,512]{2,1,0:T(8,128)(2,1)} %shard_map.75.left_ref, bf16[1088,256]{1,0:T(8,128)(2,1)} %copy-done.8, bf16[1088,256]{1,0:T(8,128)(2,1)} %copy-done.14, bf16[1024,256]{1,0:T(8,128)(2,1)} %copy-done.11, bf16[1024,256]{1,0:T(8,128)(2,1)} %copy-done.15, bf16[1024,256]{1,0:T(8,128)(2,1)} %copy-done.10, ...), custom_call_target="tpu_custom_call" | custom-call | flops 1 | bytes 1 | tf_op jit(solution)/shard_map/pallas_call | solution.py:253
  91.2 6.9 %shard_map.77.refs_6_ = f32[1088,512]{1,0:T(8,128)} custom-call(bf16[8,1088,512]{2,1,0:T(8,128)(2,1)} %shard_map.75.left_ref, bf16[512,256]{1,0:T(8,128)(2,1)} %copy-done.13, bf16[512,256]{1,0:T(8,128)(2,1)} %get-tuple-element.82.refs_1_, bf16[512,256]{1,0:T(8,128)(2,1)} %collective-permute-done.6.refs_2_, bf16[512,256]{1,0:T(8,128)(2,1)} %copy-done.24, ...), custom_call_target="tpu_custom_call" | custom-call | flops 1 | bytes 1 | tf_op jit(solution)/shard_map/pallas_call | solution.py:253
  98.8 0.8 copy-done.17
  99.6 4.5 %shard_map.78.refs_2_ = bf16[1088,512]{1,0:T(8,128)(2,1)} custom-call(bf16[8,1088,512]{2,1,0:T(8,128)(2,1)} %shard_map.75.left_ref, bf16[1024,256]{1,0:T(8,128)(2,1)} %copy-done.12, bf16[1024,256]{1,0:T(8,128)(2,1)} %copy-done.17, f32[1088,512]{1,0:T(8,128)} %shard_map.76.refs_2_), custom_call_target="tpu_custom_call" | custom-call | flops 1 | bytes 1 | tf_op jit(solution)/shard_map/pallas_call | solution.py:253
  106.1 1.2 collective-permute-start.30
  107.3 0.8 slice.170
  109.9 8.3 %shard_map.79 = (bf16[4,1024,512]{2,1,0:T(8,128)(2,1)}, f32[4,1,512]{2,1,0:T(1,128)}, f32[4,1,512]{2,1,0:T(1,128)}) custom-call(s32[4]{0:T(128)} %and_select_fusion.1.place_ref, s32[4]{0:T(128)} %pad_add_fusion.turn_ref, bf16[4,128,256]{2,1,0:T(8,128)(2,1)} %copy-done.7, bf16[4,128,256]{2,1,0:T(8,128)(2,1)} %copy-done.21, ...), custom_call_target="tpu_custom_call" | custom-call | flops 1 | bytes 1 | tf_op jit(solution)/shard_map/pallas_call | solution.py:323
  118.2 0.7 fusion.31
  119.0 0.9 collective-permute-start.26
  120.0 0.7 constant_dynamic-update-slice_fusion.10
  121.0 1.8 collective-permute-done.26
  123.4 1.6 collective-permute-start.28
  125.0 1.7 collective-permute-start.29
  126.7 0.7 copy-done.20
  127.4 5.1 %shard_map.80.value_ref = bf16[1088,512]{1,0:T(8,128)(2,1)} custom-call(bf16[8,1088,512]{2,1,0:T(8,128)(2,1)} %shard_map.75.left_ref, bf16[640,256]{1,0:T(8,128)(2,1)} %copy-done.4, bf16[640,256]{1,0:T(8,128)(2,1)} %copy-done.18, bf16[640,256]{1,0:T(8,128)(2,1)} %copy-done.5, bf16[640,256]{1,0:T(8,128)(2,1)} %copy-done.19, bf16[640,256]{1,0:T(8,128)(2,1)} %copy-done.6, ...), custom_call_target="tpu_custom_call" | custom-call | flops 1 | bytes 1 | tf_op jit(solution)/shard_map/pallas_call | solution.py:253
  132.6 0.8 slice.182
  133.4 5.5 %shard_map.81 = bf16[4,512,128]{2,1,0:T(8,128)(2,1)} custom-call(s32[4]{0:T(128)} %and_select_fusion.1.place_ref, bf16[4,1024,512]{2,1,0:T(8,128)(2,1)} %get-tuple-element.70.weight_ref, bf16[1088,512]{1,0:T(8,128)(2,1)} %shard_map.80.value_ref), custom_call_target="tpu_custom_call" | custom-call | flops 1 | bytes 1 | tf_op jit(solution)/shard_map/pallas_call | solution.py:360
  139.0 1.1 fusion.35
  142.0 0.9 collective-permute-start.32
  143.0 4.9 %collective-permute-done.32 = bf16[4,128,128]{2,1,0:T(8,128)(2,1)S(1)} collective-permute-done((bf16[4,128,128]{2,1,0:T(8,128)(2,1)S(1)}, bf16[4,128,128]{2,1,0:T(8,128)(2,1)S(1)}, u32[]{:S(2)}, u32[]{:S(2)}) %collective-permute-start.32) | collective-permute-done | bytes 131104 | tf_op jit(solution)/shard_map/ppermute | solution.py:82
  148.6 1.5 collective-permute-start.34
  150.1 2.8 %collective-permute-start.35 = (bf16[128,128]{1,0:T(8,128)(2,1)S(1)}, bf16[128,128]{1,0:T(8,128)(2,1)S(1)}, u32[]{:S(2)}, u32[]{:S(2)}) collective-permute-start(bf16[128,128]{1,0:T(8,128)(2,1)S(1)} %get-tuple-element.90), channel_id=1, source_target_pairs={{0,12},{1,13},{2,14},{3,15},{4,0},{5,1},{6,2},{7,3},{8,4},{9,5},{1... | collective-permute-start | bytes 98312 | tf_op jit(solution)/shard_map/ppermute | solution.py:82
  152.9 0.9 collective-permute-done.33
  155.4 5.6 %shard_map.82 = bf16[64,8192]{1,0:T(8,128)(2,1)} custom-call(s32[16]{0:T(128)} %stack.127.block_ref, bf16[64,256]{1,0:T(8,128)(2,1)} %bitcast.157, bf16[256,8192]{1,0:T(8,128)(2,1)} %weight_ref.3), custom_call_target="tpu_custom_call" | custom-call | flops 1 | bytes 1 | tf_op jit(solution)/shard_map/pallas_call | solution.py:398
  161.0 1.1 slice.194
  162.1 1.9 %collective-permute-done.37 = bf16[64,4096]{1,0:T(8,128)(2,1)S(1)} collective-permute-done((bf16[64,4096]{1,0:T(8,128)(2,1)S(1)}, bf16[64,4096]{1,0:T(8,128)(2,1)S(1)}, u32[]{:S(2)}, u32[]{:S(2)}) %collective-permute-start.37) | collective-permute-done | bytes 524320 | tf_op jit(solution)/shard_map/ppermute | solution.py:82
  164.0 1.2 add_convert_fusion
  165.2 0.9 collective-permute-start.38
  166.1 7.5 %collective-permute-done.38 = bf16[64,2048]{1,0:T(8,128)(2,1)S(1)} collective-permute-done((bf16[64,2048]{1,0:T(8,128)(2,1)S(1)}, bf16[64,2048]{1,0:T(8,128)(2,1)S(1)}, u32[]{:S(2)}, u32[]{:S(2)}) %collective-permute-start.38) | collective-permute-done | bytes 262176 | tf_op jit(solution)/shard_map/ppermute | solution.py:82
  173.7 1.8 collective-permute-start.39
  175.5 2.9 %collective-permute-start.40 = (bf16[64,512]{1,0:T(8,128)(2,1)S(1)}, bf16[64,512]{1,0:T(8,128)(2,1)S(1)}, u32[]{:S(2)}, u32[]{:S(2)}) collective-permute-start(bf16[64,512]{1,0:T(8,128)(2,1)S(1)} %get-tuple-element.88), channel_id=1, source_target_pairs={{0,8},{1,9},{2,10},{3,11},{4,12},{5,13},{6,14},{7,15},{8,0},{9,1},... | collective-permute-start | bytes 196616 | tf_op jit(solution)/shard_map/ppermute | solution.py:82
  178.5 2.4 %collective-permute-done.39 = bf16[64,512]{1,0:T(8,128)(2,1)S(1)} collective-permute-done((bf16[64,512]{1,0:T(8,128)(2,1)S(1)}, bf16[64,512]{1,0:T(8,128)(2,1)S(1)}, u32[]{:S(2)}, u32[]{:S(2)}) %collective-permute-start.39) | collective-permute-done | bytes 65568 | tf_op jit(solution)/shard_map/ppermute | solution.py:82
  180.9 1.6 collective-permute-done.40
  (176 shorter events, 18.2 us)
Async XLA Ops:
  0.0 11.3 %copy-start.1 = (bf16[2,32,8192]{2,1,0:T(8,128)(2,1)S(1)}, bf16[2,32,8192]{2,1,0:T(8,128)(2,1)}, u32[]{:S(2)}) copy-start(bf16[2,32,8192]{2,1,0:T(8,128)(2,1)} %param.10) | copy-start | bytes 3145732
  0.0 51.2 %collective-permute-start.12 = (bf16[512,8192]{1,0:T(8,128)(2,1)}, bf16[512,8192]{1,0:T(8,128)(2,1)}, u32[]{:S(2)}, u32[]{:S(2)}) collective-permute-start(bf16[512,8192]{1,0:T(8,128)(2,1)} %prompt_ref.1), channel_id=1, source_target_pairs={{0,1},{1,0},{2,3},{3,2},{4,5},{5,4},{6,7},{7,6},{8,9},{9,8},{10,11... | collective-permute-start | bytes 25165832 | tf_op jit(solution)/shard_map/ppermute | solution.py:82
  2.2 13.2 %copy-start.13 = (bf16[512,256]{1,0:T(8,128)(2,1)}, bf16[512,256]{1,0:T(8,128)(2,1)S(1)}, u32[]{:S(2)}) copy-start(bf16[512,256]{1,0:T(8,128)(2,1)S(1)} %get-tuple-element.83.refs_0_) | copy-start | bytes 786436
  2.2 13.3 %collective-permute-start = (bf16[512,256]{1,0:T(8,128)(2,1)S(1)}, bf16[512,256]{1,0:T(8,128)(2,1)S(1)}, u32[]{:S(2)}, u32[]{:S(2)}) collective-permute-start(bf16[512,256]{1,0:T(8,128)(2,1)S(1)} %get-tuple-element.83.refs_0_), channel_id=1, source_target_pairs={{0,2},{1,3},{2,0},{3,1},{4,6},{5,7},{6,4},{7,5},{8,10},{9,11},{10,... | collective-permute-start | bytes 786440 | tf_op jit(solution)/shard_map/ppermute | solution.py:82
  4.8 22.7 %collective-permute-start.6 = (bf16[512,256]{1,0:T(8,128)(2,1)S(1)}, bf16[512,256]{1,0:T(8,128)(2,1)}, u32[]{:S(2)}, u32[]{:S(2)}) collective-permute-start(bf16[512,256]{1,0:T(8,128)(2,1)S(1)} %get-tuple-element.83.refs_0_), channel_id=1, source_target_pairs={{0,8},{1,9},{2,10},{3,11},{4,0},{5,1},{6,2},{7,3},{8,12},{9,13},{1... | collective-permute-start | bytes 786440 | tf_op jit(solution)/shard_map/ppermute | solution.py:82
  8.5 10.4 %collective-permute-start.1 = (bf16[512,256]{1,0:T(8,128)(2,1)S(1)}, bf16[512,256]{1,0:T(8,128)(2,1)}, u32[]{:S(2)}, u32[]{:S(2)}) collective-permute-start(bf16[512,256]{1,0:T(8,128)(2,1)S(1)} %get-tuple-element.84), channel_id=1, source_target_pairs={{0,8},{1,9},{2,10},{3,11},{4,0},{5,1},{6,2},{7,3},{8,12},{9,13},{1... | collective-permute-start | bytes 786440 | tf_op jit(solution)/shard_map/ppermute | solution.py:82
  15.5 43.6 %copy-start.8 = (bf16[1088,256]{1,0:T(8,128)(2,1)}, bf16[1088,256]{1,0:T(8,128)(2,1)S(1)}, u32[]{:S(2)}) copy-start(bf16[1088,256]{1,0:T(8,128)(2,1)S(1)} %pad_maximum_fusion.refs_0_) | copy-start | bytes 1671172
  18.9 22.5 %copy-start.23 = (bf16[512,256]{1,0:T(8,128)(2,1)S(1)}, bf16[512,256]{1,0:T(8,128)(2,1)}, u32[]{:S(2)}) copy-start(bf16[512,256]{1,0:T(8,128)(2,1)} %copy-done.22) | copy-start | bytes 786436
  18.9 13.9 %collective-permute-start.2 = (bf16[1088,256]{1,0:T(8,128)(2,1)S(1)}, bf16[1088,256]{1,0:T(8,128)(2,1)S(1)}, u32[]{:S(2)}, u32[]{:S(2)}) collective-permute-start(bf16[1088,256]{1,0:T(8,128)(2,1)S(1)} %pad_maximum_fusion.refs_0_), channel_id=1, source_target_pairs={{0,2},{1,3},{2,0},{3,1},{4,6},{5,7},{6,4},{7,5},{8,10},{9,11},{10,... | collective-permute-start | bytes 1671176 | tf_op jit(solution)/shard_map/ppermute | solution.py:82
  19.5 9.6 %collective-permute-start.13 = (bf16[512,256]{1,0:T(8,128)(2,1)}, bf16[512,256]{1,0:T(8,128)(2,1)S(1)}, u32[]{:S(2)}, u32[]{:S(2)}) collective-permute-start(bf16[512,256]{1,0:T(8,128)(2,1)} %collective-permute-done.1), channel_id=1, source_target_pairs={{0,16},{1,17},{2,18},{3,19},{4,20},{5,21},{6,22},{7,23},{8,24},{9,... | collective-permute-start | bytes 786440 | tf_op jit(solution)/shard_map/ppermute | solution.py:82
  24.1 9.9 %collective-permute-start.3 = (bf16[512,256]{1,0:T(8,128)(2,1)}, bf16[512,256]{1,0:T(8,128)(2,1)S(1)}, u32[]{:S(2)}, u32[]{:S(2)}) collective-permute-start(bf16[512,256]{1,0:T(8,128)(2,1)} %collective-permute-done.1), channel_id=1, source_target_pairs={{0,8},{1,9},{2,10},{3,11},{4,0},{5,1},{6,2},{7,3},{8,12},{9,13},{1... | collective-permute-start | bytes 786440 | tf_op jit(solution)/shard_map/ppermute | solution.py:82
  27.5 6.9 %collective-permute-start.17 = (bf16[512,256]{1,0:T(8,128)(2,1)}, bf16[512,256]{1,0:T(8,128)(2,1)S(1)}, u32[]{:S(2)}, u32[]{:S(2)}) collective-permute-start(bf16[512,256]{1,0:T(8,128)(2,1)} %collective-permute-done.6.refs_2_), channel_id=1, source_target_pairs={{0,16},{1,17},{2,18},{3,19},{4,20},{5,21},{6,22},{7,23},{8,24},{9,... | collective-permute-start | bytes 786440 | tf_op jit(solution)/shard_map/ppermute | solution.py:82
  29.1 30.1 %copy-start.11 = (bf16[1024,256]{1,0:T(8,128)(2,1)}, bf16[1024,256]{1,0:T(8,128)(2,1)S(1)}, u32[]{:S(2)}) copy-start(bf16[1024,256]{1,0:T(8,128)(2,1)S(1)} %constant_dynamic-update-slice_fusion.2.refs_2_) | copy-start | bytes 1572868
  32.8 26.4 %copy-start.14 = (bf16[1088,256]{1,0:T(8,128)(2,1)}, bf16[1088,256]{1,0:T(8,128)(2,1)S(1)}, u32[]{:S(2)}) copy-start(bf16[1088,256]{1,0:T(8,128)(2,1)S(1)} %collective-permute-done.2.refs_1_) | copy-start | bytes 1671172
  32.8 26.4 %collective-permute-start.19 = (bf16[1024,256]{1,0:T(8,128)(2,1)S(1)}, bf16[1024,256]{1,0:T(8,128)(2,1)S(1)}, u32[]{:S(2)}, u32[]{:S(2)}) collective-permute-start(bf16[1024,256]{1,0:T(8,128)(2,1)S(1)} %constant_dynamic-update-slice_fusion.2.refs_2_), channel_id=1, source_target_pairs={{0,2},{1,3},{2,0},{3,1},{4,6},{5,7},{6,4},{7,5},{8,10},{9,11},{10,... | collective-permute-start | bytes 1572872 | tf_op jit(solution)/shard_map/ppermute | solution.py:82
  35.2 11.7 %collective-permute-start.18 = (bf16[512,256]{1,0:T(8,128)(2,1)S(1)}, bf16[512,256]{1,0:T(8,128)(2,1)}, u32[]{:S(2)}, u32[]{:S(2)}) collective-permute-start(bf16[512,256]{1,0:T(8,128)(2,1)S(1)} %collective-permute-done.3), channel_id=1, source_target_pairs={{0,16},{1,17},{2,18},{3,19},{4,20},{5,21},{6,22},{7,23},{8,24},{9,... | collective-permute-start | bytes 786440 | tf_op jit(solution)/shard_map/ppermute | solution.py:82
  36.0 10.2 %collective-permute-start.4 = (bf16[512,256]{1,0:T(8,128)(2,1)S(1)}, bf16[512,256]{1,0:T(8,128)(2,1)S(1)}, u32[]{:S(2)}, u32[]{:S(2)}) collective-permute-start(bf16[512,256]{1,0:T(8,128)(2,1)S(1)} %collective-permute-done.3), channel_id=1, source_target_pairs={{0,8},{1,9},{2,10},{3,11},{4,0},{5,1},{6,2},{7,3},{8,12},{9,13},{1... | collective-permute-start | bytes 786440 | tf_op jit(solution)/shard_map/ppermute | solution.py:82
  40.7 20.0 %collective-permute-start.7 = (bf16[512,256]{1,0:T(8,128)(2,1)}, bf16[512,256]{1,0:T(8,128)(2,1)S(1)}, u32[]{:S(2)}, u32[]{:S(2)}) collective-permute-start(bf16[512,256]{1,0:T(8,128)(2,1)} %collective-permute-done.6.refs_2_), channel_id=1, source_target_pairs={{0,8},{1,9},{2,10},{3,11},{4,0},{5,1},{6,2},{7,3},{8,12},{9,13},{1... | collective-permute-start | bytes 786440 | tf_op jit(solution)/shard_map/ppermute | solution.py:82
  41.5 17.7 %copy-start.2 = (bf16[640,256]{1,0:T(8,128)(2,1)}, bf16[640,256]{1,0:T(8,128)(2,1)S(1)}, u32[]{:S(2)}) copy-start(bf16[640,256]{1,0:T(8,128)(2,1)S(1)} %pad_maximum_fusion.1.refs_0_.refs_8_) | copy-start | bytes 983044
  46.3 14.5 %collective-permute-start.14 = (bf16[512,256]{1,0:T(8,128)(2,1)S(1)}, bf16[512,256]{1,0:T(8,128)(2,1)S(1)}, u32[]{:S(2)}, u32[]{:S(2)}) collective-permute-start(bf16[512,256]{1,0:T(8,128)(2,1)S(1)} %copy-done.23), channel_id=1, source_target_pairs={{0,16},{1,17},{2,18},{3,19},{4,20},{5,21},{6,22},{7,23},{8,24},{9,... | collective-permute-start | bytes 786440 | tf_op jit(solution)/shard_map/ppermute | solution.py:82
  46.8 21.2 %collective-permute-start.5 = (bf16[640,256]{1,0:T(8,128)(2,1)S(1)}, bf16[640,256]{1,0:T(8,128)(2,1)S(1)}, u32[]{:S(2)}, u32[]{:S(2)}) collective-permute-start(bf16[640,256]{1,0:T(8,128)(2,1)S(1)} %pad_maximum_fusion.1.refs_0_.refs_8_), channel_id=1, source_target_pairs={{0,8},{1,9},{2,10},{3,11},{4,0},{5,1},{6,2},{7,3},{8,12},{9,13},{1... | collective-permute-start | bytes 983048 | tf_op jit(solution)/shard_map/ppermute | solution.py:82
  51.2 8.0 %copy-start.10 = (bf16[1024,256]{1,0:T(8,128)(2,1)}, bf16[1024,256]{1,0:T(8,128)(2,1)S(1)}, u32[]{:S(2)}) copy-start(bf16[1024,256]{1,0:T(8,128)(2,1)S(1)} %constant_dynamic-update-slice_fusion.refs_4_) | copy-start | bytes 1572868
  59.2 24.5 %copy-start.15 = (bf16[1024,256]{1,0:T(8,128)(2,1)}, bf16[1024,256]{1,0:T(8,128)(2,1)S(1)}, u32[]{:S(2)}) copy-start(bf16[1024,256]{1,0:T(8,128)(2,1)S(1)} %collective-permute-done.19.refs_3_) | copy-start | bytes 1572868
  59.2 16.5 %collective-permute-start.20 = (bf16[1024,256]{1,0:T(8,128)(2,1)S(1)}, bf16[1024,256]{1,0:T(8,128)(2,1)S(1)}, u32[]{:S(2)}, u32[]{:S(2)}) collective-permute-start(bf16[1024,256]{1,0:T(8,128)(2,1)S(1)} %constant_dynamic-update-slice_fusion.refs_4_), channel_id=1, source_target_pairs={{0,2},{1,3},{2,0},{3,1},{4,6},{5,7},{6,4},{7,5},{8,10},{9,11},{10,... | collective-permute-start | bytes 1572872 | tf_op jit(solution)/shard_map/ppermute | solution.py:82
  60.8 30.3 %copy-start.25 = (bf16[512,256]{1,0:T(8,128)(2,1)}, bf16[512,256]{1,0:T(8,128)(2,1)S(1)}, u32[]{:S(2)}) copy-start(bf16[512,256]{1,0:T(8,128)(2,1)S(1)} %collective-permute-done.7.refs_4_) | copy-start | bytes 786436
  60.8 7.2 %collective-permute-start.8 = (bf16[512,256]{1,0:T(8,128)(2,1)S(1)}, bf16[512,256]{1,0:T(8,128)(2,1)S(1)}, u32[]{:S(2)}, u32[]{:S(2)}) collective-permute-start(bf16[512,256]{1,0:T(8,128)(2,1)S(1)} %collective-permute-done.7.refs_4_), channel_id=1, source_target_pairs={{0,8},{1,9},{2,10},{3,11},{4,0},{5,1},{6,2},{7,3},{8,12},{9,13},{1... | collective-permute-start | bytes 786440 | tf_op jit(solution)/shard_map/ppermute | solution.py:82
  60.8 30.3 %copy-start.26 = (bf16[512,256]{1,0:T(8,128)(2,1)}, bf16[512,256]{1,0:T(8,128)(2,1)S(1)}, u32[]{:S(2)}) copy-start(bf16[512,256]{1,0:T(8,128)(2,1)S(1)} %collective-permute-done.14.refs_9_) | copy-start | bytes 786436
  60.8 10.1 %collective-permute-start.15 = (bf16[512,256]{1,0:T(8,128)(2,1)S(1)}, bf16[512,256]{1,0:T(8,128)(2,1)S(1)}, u32[]{:S(2)}, u32[]{:S(2)}) collective-permute-start(bf16[512,256]{1,0:T(8,128)(2,1)S(1)} %collective-permute-done.7.refs_4_), channel_id=1, source_target_pairs={{0,16},{1,17},{2,18},{3,19},{4,20},{5,21},{6,22},{7,23},{8,24},{9,... | collective-permute-start | bytes 786440 | tf_op jit(solution)/shard_map/ppermute | solution.py:82
  62.4 13.3 %collective-permute-start.21 = (bf16[512,256]{1,0:T(8,128)(2,1)S(1)}, bf16[512,256]{1,0:T(8,128)(2,1)S(1)}, u32[]{:S(2)}, u32[]{:S(2)}) collective-permute-start(bf16[512,256]{1,0:T(8,128)(2,1)S(1)} %collective-permute-done.4), channel_id=1, source_target_pairs={{0,16},{1,17},{2,18},{3,19},{4,20},{5,21},{6,22},{7,23},{8,24},{9,... | collective-permute-start | bytes 786440 | tf_op jit(solution)/shard_map/ppermute | solution.py:82
  68.0 23.1 %copy-start.27 = (bf16[512,256]{1,0:T(8,128)(2,1)}, bf16[512,256]{1,0:T(8,128)(2,1)S(1)}, u32[]{:S(2)}) copy-start(bf16[512,256]{1,0:T(8,128)(2,1)S(1)} %collective-permute-done.8.refs_6_) | copy-start | bytes 786436
  68.0 37.2 %copy-start.4 = (bf16[640,256]{1,0:T(8,128)(2,1)}, bf16[640,256]{1,0:T(8,128)(2,1)S(1)}, u32[]{:S(2)}) copy-start(bf16[640,256]{1,0:T(8,128)(2,1)S(1)} %collective-permute-done.5.refs_1_.refs_0_) | copy-start | bytes 983044
  68.0 13.3 %collective-permute-start.9 = (bf16[640,256]{1,0:T(8,128)(2,1)S(1)}, bf16[640,256]{1,0:T(8,128)(2,1)S(1)}, u32[]{:S(2)}, u32[]{:S(2)}) collective-permute-start(bf16[640,256]{1,0:T(8,128)(2,1)S(1)} %collective-permute-done.5.refs_1_.refs_0_), channel_id=1, source_target_pairs={{0,8},{1,9},{2,10},{3,11},{4,0},{5,1},{6,2},{7,3},{8,12},{9,13},{1... | collective-permute-start | bytes 983048 | tf_op jit(solution)/shard_map/ppermute | solution.py:82
  70.9 20.2 %copy-start.28 = (bf16[512,256]{1,0:T(8,128)(2,1)}, bf16[512,256]{1,0:T(8,128)(2,1)S(1)}, u32[]{:S(2)}) copy-start(bf16[512,256]{1,0:T(8,128)(2,1)S(1)} %collective-permute-done.15.refs_5_) | copy-start | bytes 786436
  70.9 10.3 %collective-permute-start.16 = (bf16[512,256]{1,0:T(8,128)(2,1)S(1)}, bf16[512,256]{1,0:T(8,128)(2,1)S(1)}, u32[]{:S(2)}, u32[]{:S(2)}) collective-permute-start(bf16[512,256]{1,0:T(8,128)(2,1)S(1)} %collective-permute-done.8.refs_6_), channel_id=1, source_target_pairs={{0,16},{1,17},{2,18},{3,19},{4,20},{5,21},{6,22},{7,23},{8,24},{9,... | collective-permute-start | bytes 786440 | tf_op jit(solution)/shard_map/ppermute | solution.py:82
  75.7 15.4 %copy-start.12 = (bf16[1024,256]{1,0:T(8,128)(2,1)}, bf16[1024,256]{1,0:T(8,128)(2,1)S(1)}, u32[]{:S(2)}) copy-start(bf16[1024,256]{1,0:T(8,128)(2,1)S(1)} %constant_dynamic-update-slice_fusion.4.refs_0_) | copy-start | bytes 1572868
  75.7 7.9 %copy-start.16 = (bf16[1024,256]{1,0:T(8,128)(2,1)}, bf16[1024,256]{1,0:T(8,128)(2,1)S(1)}, u32[]{:S(2)}) copy-start(bf16[1024,256]{1,0:T(8,128)(2,1)S(1)} %collective-permute-done.20.refs_5_) | copy-start | bytes 1572868
  75.7 22.4 %collective-permute-start.24 = (bf16[1024,256]{1,0:T(8,128)(2,1)S(1)}, bf16[1024,256]{1,0:T(8,128)(2,1)S(1)}, u32[]{:S(2)}, u32[]{:S(2)}) collective-permute-start(bf16[1024,256]{1,0:T(8,128)(2,1)S(1)} %constant_dynamic-update-slice_fusion.4.refs_0_), channel_id=1, source_target_pairs={{0,2},{1,3},{2,0},{3,1},{4,6},{5,7},{6,4},{7,5},{8,10},{9,11},{10,... | collective-permute-start | bytes 1572872 | tf_op jit(solution)/shard_map/ppermute | solution.py:82
  75.8 15.3 %collective-permute-start.22 = (bf16[640,256]{1,0:T(8,128)(2,1)S(1)}, bf16[640,256]{1,0:T(8,128)(2,1)S(1)}, u32[]{:S(2)}, u32[]{:S(2)}) collective-permute-start(bf16[640,256]{1,0:T(8,128)(2,1)S(1)} %collective-permute-done.5.refs_1_.refs_0_), channel_id=1, source_target_pairs={{0,16},{1,17},{2,18},{3,19},{4,20},{5,21},{6,22},{7,23},{8,24},{9,... | collective-permute-start | bytes 983048 | tf_op jit(solution)/shard_map/ppermute | solution.py:82
  81.3 9.8 %copy-start.29 = (bf16[512,256]{1,0:T(8,128)(2,1)}, bf16[512,256]{1,0:T(8,128)(2,1)S(1)}, u32[]{:S(2)}) copy-start(bf16[512,256]{1,0:T(8,128)(2,1)S(1)} %collective-permute-done.16.refs_7_) | copy-start | bytes 786436
  81.3 23.9 %copy-start.5 = (bf16[640,256]{1,0:T(8,128)(2,1)}, bf16[640,256]{1,0:T(8,128)(2,1)S(1)}, u32[]{:S(2)}) copy-start(bf16[640,256]{1,0:T(8,128)(2,1)S(1)} %collective-permute-done.9.refs_2_) | copy-start | bytes 983044
  81.3 16.8 %collective-permute-start.23 = (bf16[640,256]{1,0:T(8,128)(2,1)S(1)}, bf16[640,256]{1,0:T(8,128)(2,1)S(1)}, u32[]{:S(2)}, u32[]{:S(2)}) collective-permute-start(bf16[640,256]{1,0:T(8,128)(2,1)S(1)} %collective-permute-done.9.refs_2_), channel_id=1, source_target_pairs={{0,16},{1,17},{2,18},{3,19},{4,20},{5,21},{6,22},{7,23},{8,24},{9,... | collective-permute-start | bytes 983048 | tf_op jit(solution)/shard_map/ppermute | solution.py:82
  82.9 15.2 %collective-permute-start.10 = (bf16[640,256]{1,0:T(8,128)(2,1)S(1)}, bf16[640,256]{1,0:T(8,128)(2,1)S(1)}, u32[]{:S(2)}, u32[]{:S(2)}) collective-permute-start(bf16[640,256]{1,0:T(8,128)(2,1)S(1)} %collective-permute-done.9.refs_2_), channel_id=1, source_target_pairs={{0,8},{1,9},{2,10},{3,11},{4,0},{5,1},{6,2},{7,3},{8,12},{9,13},{1... | collective-permute-start | bytes 983048 | tf_op jit(solution)/shard_map/ppermute | solution.py:82
  91.2 6.9 %copy-start.18 = (bf16[640,256]{1,0:T(8,128)(2,1)}, bf16[640,256]{1,0:T(8,128)(2,1)S(1)}, u32[]{:S(2)}) copy-start(bf16[640,256]{1,0:T(8,128)(2,1)S(1)} %collective-permute-done.22.refs_1_) | copy-start | bytes 983044
  98.1 7.1 %copy-start.3 = (bf16[640,256]{1,0:T(8,128)(2,1)S(1)}, bf16[640,256]{1,0:T(8,128)(2,1)}, u32[]{:S(2)}) copy-start(bf16[640,256]{1,0:T(8,128)(2,1)} %copy-done.2) | copy-start | bytes 983044
  98.1 8.0 %copy-start.6 = (bf16[640,256]{1,0:T(8,128)(2,1)}, bf16[640,256]{1,0:T(8,128)(2,1)S(1)}, u32[]{:S(2)}) copy-start(bf16[640,256]{1,0:T(8,128)(2,1)S(1)} %collective-permute-done.10.refs_3_.refs_4_) | copy-start | bytes 983044
  104.1 4.1 %collective-permute-start.25 = (bf16[1088,512]{1,0:T(8,128)(2,1)}, bf16[1088,512]{1,0:T(8,128)(2,1)S(1)}, u32[]{:S(2)}, u32[]{:S(2)}) collective-permute-start(bf16[1088,512]{1,0:T(8,128)(2,1)} %shard_map.78.refs_2_), channel_id=1, source_target_pairs={{0,1},{1,0},{2,3},{3,2},{4,5},{5,4},{6,7},{7,6},{8,9},{9,8},{10,11... | collective-permute-start | bytes 3342344 | tf_op jit(solution)/shard_map/ppermute | solution.py:82
  105.6 3.0 %collective-permute-start.11 = (bf16[4,128,256]{2,1,0:T(8,128)(2,1)S(1)}, bf16[4,128,256]{2,1,0:T(8,128)(2,1)S(1)}, u32[]{:S(2)}, u32[]{:S(2)}) collective-permute-start(bf16[4,128,256]{2,1,0:T(8,128)(2,1)S(1)} %shard_map.74.refs_0_), channel_id=1, source_target_pairs={{0,1},{1,0},{2,3},{3,2},{4,5},{5,4},{6,7},{7,6},{8,9},{9,8},{10,11... | collective-permute-start | bytes 786440 | tf_op jit(solution)/shard_map/ppermute | solution.py:82
  106.1 20.6 %collective-permute-start.30 = (bf16[640,256]{1,0:T(8,128)(2,1)S(1)}, bf16[640,256]{1,0:T(8,128)(2,1)S(1)}, u32[]{:S(2)}, u32[]{:S(2)}) collective-permute-start(bf16[640,256]{1,0:T(8,128)(2,1)S(1)} %collective-permute-done.10.refs_3_.refs_4_), channel_id=1, source_target_pairs={{0,16},{1,17},{2,18},{3,19},{4,20},{5,21},{6,22},{7,23},{8,24},{9,... | collective-permute-start | bytes 983048 | tf_op jit(solution)/shard_map/ppermute | solution.py:82
  119.0 3.8 %collective-permute-start.26 = (f32[2,4,2,2,128]{4,3,2,1,0:T(2,128)S(1)}, f32[2,4,2,2,128]{4,3,2,1,0:T(2,128)S(1)}, u32[]{:S(2)}, u32[]{:S(2)}) collective-permute-start(f32[2,4,2,2,128]{4,3,2,1,0:T(2,128)S(1)} %get-tuple-element.101), channel_id=1, source_target_pairs={{0,2},{1,3},{2,0},{3,1},{4,6},{5,7},{6,4},{7,5},{8,10},{9,11},{10,... | collective-permute-start | bytes 49160 | tf_op jit(solution)/shard_map/ppermute | solution.py:82
  122.8 17.8 %collective-permute-start.27 = (f32[2,2,4,2,2,128]{5,4,3,2,1,0:T(2,128)S(1)}, f32[2,2,4,2,2,128]{5,4,3,2,1,0:T(2,128)S(1)}, u32[]{:S(2)}, u32[]{:S(2)}) collective-permute-start(f32[2,2,4,2,2,128]{5,4,3,2,1,0:T(2,128)S(1)} %pad_maximum_fusion.2), channel_id=1, source_target_pairs={{0,4},{1,5},{2,6},{3,7},{4,8},{5,9},{6,10},{7,11},{8,12},{9,13},{1... | collective-permute-start | bytes 98312 | tf_op jit(solution)/shard_map/ppermute | solution.py:82
  123.4 17.2 %collective-permute-start.28 = (f32[2,2,4,2,2,128]{5,4,3,2,1,0:T(2,128)S(1)}, f32[2,2,4,2,2,128]{5,4,3,2,1,0:T(2,128)S(1)}, u32[]{:S(2)}, u32[]{:S(2)}) collective-permute-start(f32[2,2,4,2,2,128]{5,4,3,2,1,0:T(2,128)S(1)} %pad_maximum_fusion.2), channel_id=1, source_target_pairs={{0,8},{1,9},{2,10},{3,11},{4,12},{5,13},{6,14},{7,15},{8,0},{9,1},... | collective-permute-start | bytes 98312 | tf_op jit(solution)/shard_map/ppermute | solution.py:82
  125.0 15.7 %collective-permute-start.29 = (f32[2,2,4,2,2,128]{5,4,3,2,1,0:T(2,128)S(1)}, f32[2,2,4,2,2,128]{5,4,3,2,1,0:T(2,128)S(1)}, u32[]{:S(2)}, u32[]{:S(2)}) collective-permute-start(f32[2,2,4,2,2,128]{5,4,3,2,1,0:T(2,128)S(1)} %pad_maximum_fusion.2), channel_id=1, source_target_pairs={{0,12},{1,13},{2,14},{3,15},{4,0},{5,1},{6,2},{7,3},{8,4},{9,5},{1... | collective-permute-start | bytes 98312 | tf_op jit(solution)/shard_map/ppermute | solution.py:82
  133.4 7.7 %copy-start.30 = (f32[4,1,512]{2,1,0:T(1,128)S(1)}, f32[4,1,512]{2,1,0:T(1,128)}, u32[]{:S(2)}) copy-start(f32[4,1,512]{2,1,0:T(1,128)} %get-tuple-element.67) | copy-start | bytes 24580
  139.0 4.0 %collective-permute-start.36 = (bf16[64,512]{1,0:T(8,128)(2,1)S(1)}, bf16[64,512]{1,0:T(8,128)(2,1)S(1)}, u32[]{:S(2)}, u32[]{:S(2)}) collective-permute-start(bf16[64,512]{1,0:T(8,128)(2,1)S(1)} %slice.182), channel_id=1, source_target_pairs={{0,1},{1,0},{2,3},{3,2},{4,5},{5,4},{6,7},{7,6},{8,9},{9,8},{10,11... | collective-permute-start | bytes 196616 | tf_op jit(solution)/shard_map/ppermute | solution.py:82
  140.1 1.7 collective-permute-start.31
  142.0 5.8 %collective-permute-start.32 = (bf16[4,128,128]{2,1,0:T(8,128)(2,1)S(1)}, bf16[4,128,128]{2,1,0:T(8,128)(2,1)S(1)}, u32[]{:S(2)}, u32[]{:S(2)}) collective-permute-start(bf16[4,128,128]{2,1,0:T(8,128)(2,1)S(1)} %slice_bitcast_fusion), channel_id=1, source_target_pairs={{0,2},{1,3},{2,0},{3,1},{4,6},{5,7},{6,4},{7,5},{8,10},{9,11},{10,... | collective-permute-start | bytes 393224 | tf_op jit(solution)/shard_map/ppermute | solution.py:82
  148.0 5.9 %collective-permute-start.33 = (bf16[128,128]{1,0:T(8,128)(2,1)S(1)}, bf16[128,128]{1,0:T(8,128)(2,1)S(1)}, u32[]{:S(2)}, u32[]{:S(2)}) collective-permute-start(bf16[128,128]{1,0:T(8,128)(2,1)S(1)} %get-tuple-element.89), channel_id=1, source_target_pairs={{0,4},{1,5},{2,6},{3,7},{4,8},{5,9},{6,10},{7,11},{8,12},{9,13},{1... | collective-permute-start | bytes 98312 | tf_op jit(solution)/shard_map/ppermute | solution.py:82
  148.6 5.4 %collective-permute-start.34 = (bf16[128,128]{1,0:T(8,128)(2,1)S(1)}, bf16[128,128]{1,0:T(8,128)(2,1)S(1)}, u32[]{:S(2)}, u32[]{:S(2)}) collective-permute-start(bf16[128,128]{1,0:T(8,128)(2,1)S(1)} %get-tuple-element.91), channel_id=1, source_target_pairs={{0,8},{1,9},{2,10},{3,11},{4,12},{5,13},{6,14},{7,15},{8,0},{9,1},... | collective-permute-start | bytes 98312 | tf_op jit(solution)/shard_map/ppermute | solution.py:82
  150.1 4.4 %collective-permute-start.35 = (bf16[128,128]{1,0:T(8,128)(2,1)S(1)}, bf16[128,128]{1,0:T(8,128)(2,1)S(1)}, u32[]{:S(2)}, u32[]{:S(2)}) collective-permute-start(bf16[128,128]{1,0:T(8,128)(2,1)S(1)} %get-tuple-element.90), channel_id=1, source_target_pairs={{0,12},{1,13},{2,14},{3,15},{4,0},{5,1},{6,2},{7,3},{8,4},{9,5},{1... | collective-permute-start | bytes 98312 | tf_op jit(solution)/shard_map/ppermute | solution.py:82
  162.1 2.0 %collective-permute-start.37 = (bf16[64,4096]{1,0:T(8,128)(2,1)S(1)}, bf16[64,4096]{1,0:T(8,128)(2,1)S(1)}, u32[]{:S(2)}, u32[]{:S(2)}) collective-permute-start(bf16[64,4096]{1,0:T(8,128)(2,1)S(1)} %slice.194), channel_id=1, source_target_pairs={{0,1},{1,0},{2,3},{3,2},{4,5},{5,4},{6,7},{7,6},{8,9},{9,8},{10,11... | collective-permute-start | bytes 1572872 | tf_op jit(solution)/shard_map/ppermute | solution.py:82
  165.2 8.4 %collective-permute-start.38 = (bf16[64,2048]{1,0:T(8,128)(2,1)S(1)}, bf16[64,2048]{1,0:T(8,128)(2,1)S(1)}, u32[]{:S(2)}, u32[]{:S(2)}) collective-permute-start(bf16[64,2048]{1,0:T(8,128)(2,1)S(1)} %slice.196), channel_id=1, source_target_pairs={{0,2},{1,3},{2,0},{3,1},{4,6},{5,7},{6,4},{7,5},{8,10},{9,11},{10,... | collective-permute-start | bytes 786440 | tf_op jit(solution)/shard_map/ppermute | solution.py:82
  173.7 7.2 %collective-permute-start.39 = (bf16[64,512]{1,0:T(8,128)(2,1)S(1)}, bf16[64,512]{1,0:T(8,128)(2,1)S(1)}, u32[]{:S(2)}, u32[]{:S(2)}) collective-permute-start(bf16[64,512]{1,0:T(8,128)(2,1)S(1)} %get-tuple-element.86), channel_id=1, source_target_pairs={{0,4},{1,5},{2,6},{3,7},{4,8},{5,9},{6,10},{7,11},{8,12},{9,13},{1... | collective-permute-start | bytes 196616 | tf_op jit(solution)/shard_map/ppermute | solution.py:82
  175.5 7.0 %collective-permute-start.40 = (bf16[64,512]{1,0:T(8,128)(2,1)S(1)}, bf16[64,512]{1,0:T(8,128)(2,1)S(1)}, u32[]{:S(2)}, u32[]{:S(2)}) collective-permute-start(bf16[64,512]{1,0:T(8,128)(2,1)S(1)} %get-tuple-element.88), channel_id=1, source_target_pairs={{0,8},{1,9},{2,10},{3,11},{4,12},{5,13},{6,14},{7,15},{8,0},{9,1},... | collective-permute-start | bytes 196616 | tf_op jit(solution)/shard_map/ppermute | solution.py:82
  178.5 4.5 %collective-permute-start.41 = (bf16[64,512]{1,0:T(8,128)(2,1)S(1)}, bf16[64,512]{1,0:T(8,128)(2,1)S(1)}, u32[]{:S(2)}, u32[]{:S(2)}) collective-permute-start(bf16[64,512]{1,0:T(8,128)(2,1)S(1)} %get-tuple-element.87), channel_id=1, source_target_pairs={{0,12},{1,13},{2,14},{3,15},{4,0},{5,1},{6,2},{7,3},{8,4},{9,5},{1... | collective-permute-start | bytes 196616 | tf_op jit(solution)/shard_map/ppermute | solution.py:82
  (9 other events, 10.6 us)

commit v10 on v9

--- a/solution.py
+++ b/solution.py
@@ -168,247 +168,228 @@
     )(*arrays)
 
 
-def assemble(prompt, got, steps, blocks, width):
-    count = blocks.shape[0]
-    row_count, step_count = prompt.shape[0], steps.shape[0]
-    height = 2 * row_count + step_count
-
-    def body(block_ref, prompt_ref, got_ref, step_ref, out_ref, sems):
-        copies = []
-        for i in range(count):
-            column = pl.ds(pl.multiple_of(block_ref[i] * width, width), width)
-            for j, (source, start, rows) in enumerate(
-                (
-                    (prompt_ref.at[:, column], 0, row_count),
-                    (got_ref.at[:, column], row_count, row_count),
-                    (step_ref.at[:, column], 2 * row_count, step_count),
+class Blocks:
+    def __init__(self, prompt, steps, width, pieces):
+        self.arrays = []
+        for piece in pieces:
+            for array, _ in piece:
+                if not any(array is held for held in self.arrays):
+                    self.arrays.append(array)
+        self.pieces, self.width, self.count = pieces, width, len(pieces)
+        self.row_count, self.step_count = prompt.shape[0], steps.shape[0]
+        self.height = 2 * self.row_count + self.step_count
+        self.columns = sum(array.shape[1] for array, _ in pieces[0])
+        self.scratch = [
+            pltpu.VMEM((self.count, self.height, width), prompt.dtype),
+            pltpu.VMEM((self.count, width, self.columns), prompt.dtype),
+            pltpu.SemaphoreType.DMA((self.count, 5)),
+        ]
+
+    def copies(self, i, block_ref, sources, weight_refs, scratch):
+        left, weights, sems = scratch
+        column = pl.ds(pl.multiple_of(block_ref[i] * self.width, self.width), self.width)
+        group = []
+        start = 0
+        for j, (source, rows) in enumerate(
+            zip(sources, (self.row_count, self.row_count, self.step_count))
+        ):
+            group.append(
+                pltpu.make_async_copy(
+                    source.at[:, column], left.at[i, pl.ds(start, rows), :], sems.at[i, j]
                 )
-            ):
-                copies.append(
-                    pltpu.make_async_copy(
-                        source, out_ref.at[i, pl.ds(start, rows), :], sems.at[i, j]
-                    )
+            )
+            start += rows
+        side = 0
+        for j, (array, first) in enumerate(self.pieces[i]):
+            ref = weight_refs[[array is other for other in self.arrays].index(True)]
+            group.append(
+                pltpu.make_async_copy(
+                    ref.at[pl.ds(first, self.width), :],
+                    weights.at[i, :, pl.ds(side, array.shape[1])],
+                    sems.at[i, 3 + j],
                 )
-                copies[-1].start()
-        for copy in copies:
-            copy.wait()
-
-    anywhere = pl.BlockSpec(memory_space=pl.ANY)
-    return pl.pallas_call(
-        body,
-        in_specs=[pl.BlockSpec(memory_space=pltpu.SMEM)] + [anywhere] * 3,
-        out_specs=pl.BlockSpec(memory_space=pltpu.VMEM),
-        out_shape=jax.ShapeDtypeStruct((count, height, width), prompt.dtype),
-        scratch_shapes=[pltpu.SemaphoreType.DMA((count, 3))],
-        compiler_params=pltpu.CompilerParams(vmem_limit_bytes=57 * MIB),
-        cost_estimate=LIGHT,
-    )(blocks, prompt, got, steps)
-
-
-def project(left, which, pieces, acc, kind=jnp.float32):
-    arrays = []
-    for piece in pieces:
-        for array, _ in piece:
-            if not any(array is held for held in arrays):
-                arrays.append(array)
-    _, height, width = left.shape
-    count = len(pieces)
-    columns = sum(array.shape[1] for array, _ in pieces[0])
-    extra = [] if acc is None else [acc]
-
-    def body(left_ref, *refs):
-        out_ref, blocks, weights, held, sems = refs[-5:]
-        groups = []
-        for i, piece in enumerate(pieces):
-            group = [pltpu.make_async_copy(left_ref.at[which[i]], blocks.at[i], sems.at[i, 0])]
-            side = 0
-            for j, (array, first) in enumerate(piece):
-                ref = refs[[array is other for other in arrays].index(True)]
-                group.append(
-                    pltpu.make_async_copy(
-                        ref.at[pl.ds(first, width), :],
-                        weights.at[i, :, pl.ds(side, array.shape[1])],
-                        sems.at[i, 1 + j],
-                    )
-                )
-                side += array.shape[1]
+            )
+            side += array.shape[1]
+        return group
+
+
+AHEAD = 3
+
+
+def project(prompt, got, steps, blocks, width, pieces, kind):
+    held = Blocks(prompt, steps, width, pieces)
+
+    def body(block_ref, prompt_ref, got_ref, step_ref, *refs):
+        weight_refs = refs[: len(held.arrays)]
+        out_ref, *scratch = refs[len(held.arrays) :]
+        left, weights, _ = scratch
+        sources = (prompt_ref, got_ref, step_ref)
+        groups = [
+            held.copies(i, block_ref, sources, weight_refs, scratch) for i in range(held.count)
+        ]
+        for group in groups[:AHEAD]:
             for copy in group:
                 copy.start()
-            groups.append(group)
-        if extra:
-            before = pltpu.make_async_copy(refs[len(arrays)], held, sems.at[count, 0])
-            before.start()
         total = None
         for i, group in enumerate(groups):
             for copy in group:
                 copy.wait()
-            product = jnp.dot(blocks[i], weights[i], preferred_element_type=jnp.float32)
+            if i + AHEAD < held.count:
+                for copy in groups[i + AHEAD]:
+                    copy.start()
+            product = jnp.dot(left[i], weights[i], preferred_element_type=jnp.float32)
             total = product if total is None else total + product
-        if extra:
-            before.wait()
-            total = total + held[...]
         out_ref[...] = total.astype(kind)
 
     anywhere = pl.BlockSpec(memory_space=pl.ANY)
     return pl.pallas_call(
         body,
-        in_specs=[anywhere] * (1 + len(arrays) + len(extra)),
+        in_specs=[pl.BlockSpec(memory_space=pltpu.SMEM)] + [anywhere] * (3 + len(held.arrays)),
         out_specs=pl.BlockSpec(memory_space=pltpu.VMEM),
-        out_shape=jax.ShapeDtypeStruct((height, columns), kind),
-        scratch_shapes=[
-            pltpu.VMEM((count, height, width), left.dtype),
-            pltpu.VMEM((count, width, columns), left.dtype),
-            pltpu.VMEM((height, columns) if extra else (8, 128), jnp.float32),
-            pltpu.SemaphoreType.DMA((count + 1, 3)),
-        ],
+        out_shape=jax.ShapeDtypeStruct((held.height, held.columns), kind),
+        scratch_shapes=held.scratch,
         compiler_params=pltpu.CompilerParams(vmem_limit_bytes=57 * MIB),
         cost_estimate=LIGHT,
-    )(left, *arrays, *extra)
-
-
-def attend(places, turns, queries, own, other, cosine, sine, token_prompt, row_prompt):
+    )(blocks, prompt, got, steps, *held.arrays)
+
+
+def attend(
+    places, turns, queries, own, other, cosine, sine, masks, prompt, got, steps, blocks, width,
+    pieces, early,
+):
     kv_heads = places.shape[0]
     deep, packed, lanes = queries[0].shape
     share = deep // kv_heads
     count = 2 * share * packed * lanes // HEAD_DIM
     tokens = cosine.shape[0]
     half = tokens // 2
-    height = own.shape[0]
-    masks = [] if token_prompt is None else [token_prompt, row_prompt]
-
-    def body(place_ref, turn_ref, *refs):
-        query_refs = refs[: 2 * share]
-        own_ref, other_ref, cosine_ref, sine_ref = refs[2 * share : 2 * share + 4]
-        mask_refs = refs[2 * share + 4 : -3]
-        weight_ref, top_ref, total_ref = refs[-3:]
-        keys = jnp.concatenate(
-            [
-                own_ref[:half, :].astype(jnp.float32) + other_ref[half:tokens, :],
-                own_ref[half:tokens, :].astype(jnp.float32) + other_ref[:half, :],
-            ],
-            axis=0,
-        )
-        swapped = pltpu.roll(keys, HEAD_DIM // 2, 1)
+    held = Blocks(prompt, steps, width, pieces)
+    inputs = [*queries, own, other, cosine, sine, *masks]
+
+    def body(place_ref, turn_ref, block_ref, *refs):
+        query_refs = refs[:2]
+        own_ref, other_ref, cosine_ref, sine_ref = refs[2:6]
+        mask_refs = refs[6 : len(inputs)]
+        prompt_ref, got_ref, step_ref, early_ref = refs[len(inputs) : len(inputs) + 4]
+        rest = refs[len(inputs) + 4 :]
+        weight_refs, rest = rest[: len(held.arrays)], rest[len(held.arrays) :]
+        out_ref, top_ref, total_ref, step_out_ref = rest[:4]
+        early_held, weight_held, value_held, early_sem, *scratch = rest[4:]
+        left, weight_rows, _ = scratch
+        sources = (prompt_ref, got_ref, step_ref)
+        groups = [
+            held.copies(i, block_ref, sources, weight_refs, scratch) for i in range(held.count)
+        ]
+        before = pltpu.make_async_copy(early_ref, early_held, early_sem.at[0])
+        before.start()
+        for group in groups:
+            for copy in group:
+                copy.start()
         wide_cosine = jnp.concatenate([cosine_ref[...], cosine_ref[...]], axis=1)
         wide_sine = jnp.concatenate([-sine_ref[...], sine_ref[...]], axis=1)
-        keys = (keys * wide_cosine + swapped * wide_sine).astype(jnp.bfloat16)
-        unpacked = []
-        for ref in query_refs:
-            for low in range(0, packed, packed // 2):
-                for left in range(0, lanes, HEAD_DIM):
-                    unpacked.append(ref[0, low : low + packed // 2, left : left + HEAD_DIM])
-        scores = lax.dot_general(
-            keys,
-            jnp.concatenate(unpacked, axis=0),
-            (((1,), (1,)), ((), ())),
-            preferred_element_type=jnp.float32,
-        ) * (HEAD_DIM**-0.5)
-        if masks:
-            scores = jnp.where(mask_refs[0][...] == mask_refs[1][...], scores, -1e30)
-        top = jnp.max(scores, axis=0, keepdims=True)
-        weights = jnp.exp(scores - top)
-        top_ref[0] = top
-        total_ref[0] = jnp.sum(weights, axis=0, keepdims=True)
-        weight_ref[0] = weights.astype(jnp.bfloat16)
-
-    def query_spec(part):
-        return pl.BlockSpec(
-            (1, packed, lanes), lambda j, place, turn: (turn[j * share + part], 0, 0)
-        )
-
+
+        def one_head(j, _):
+            column = pl.ds(pl.multiple_of(place_ref[j] * HEAD_DIM, HEAD_DIM), HEAD_DIM)
+            keys = jnp.concatenate(
+                [
+                    own_ref[:half, column].astype(jnp.float32)
+                    + other_ref[half:tokens, column].astype(jnp.float32),
+                    own_ref[half:tokens, column].astype(jnp.float32)
+                    + other_ref[:half, column].astype(jnp.float32),
+                ],
+                axis=0,
+            )
+            swapped = pltpu.roll(keys, HEAD_DIM // 2, 1)
+            keys = (keys * wide_cosine + swapped * wide_sine).astype(jnp.bfloat16)
+            unpacked = []
+            for part in range(share):
+                for ref in query_refs:
+                    both = ref[turn_ref[j * share + part]]
+                    for low in range(0, packed, packed // 2):
+                        for left_lane in range(0, lanes, HEAD_DIM):
+                            unpacked.append(
+                                both[low : low + packed // 2, left_lane : left_lane + HEAD_DIM]
+                            )
+            scores = lax.dot_general(
+                keys,
+                jnp.concatenate(unpacked, axis=0),
+                (((1,), (1,)), ((), ())),
+                preferred_element_type=jnp.float32,
+            ) * (HEAD_DIM**-0.5)
+            if masks:
+                scores = jnp.where(mask_refs[0][...] == mask_refs[1][...], scores, -1e30)
+            top = jnp.max(scores, axis=0, keepdims=True)
+            weights = jnp.exp(scores - top)
+            top_ref[j] = top
+            total_ref[j] = jnp.sum(weights, axis=0, keepdims=True)
+            weight_held[j] = weights.astype(jnp.bfloat16)
+            return 0
+
+        lax.fori_loop(0, kv_heads, one_head, 0)
+        before.wait()
+        total = early_held[...]
+        for i, group in enumerate(groups):
+            for copy in group:
+                copy.wait()
+            total += jnp.dot(left[i], weight_rows[i], preferred_element_type=jnp.float32)
+        value_held[...] = total[:tokens].astype(jnp.bfloat16)
+        step_out_ref[...] = total[tokens:]
+
+        def one_sum(j, _):
+            column = pl.ds(pl.multiple_of(place_ref[j] * HEAD_DIM, HEAD_DIM), HEAD_DIM)
+            summed = lax.dot_general(
+                value_held[:, column],
+                weight_held[j],
+                (((0,), (0,)), ((), ())),
+                preferred_element_type=jnp.float32,
+            )
+            out_ref[j] = summed.T.astype(jnp.bfloat16)
+            return 0
+
+        lax.fori_loop(0, kv_heads, one_sum, 0)
+
+    anywhere = pl.BlockSpec(memory_space=pl.ANY)
+    whole = pl.BlockSpec(memory_space=pltpu.VMEM)
     row = jax.ShapeDtypeStruct((kv_heads, 1, count), jnp.float32)
-    row_spec = pl.BlockSpec((1, 1, count), lambda j, place, turn: (j, 0, 0))
-    fixed = lambda j, place, turn: (0, 0)
-    column = pl.BlockSpec((height, HEAD_DIM), lambda j, place, turn: (0, place[j]))
     return pl.pallas_call(
         body,
-        grid_spec=pltpu.PrefetchScalarGridSpec(
-            num_scalar_prefetch=2,
-            grid=(kv_heads,),
-            in_specs=[query_spec(part) for part in range(share) for _ in queries]
-            + [column, column]
-            + [pl.BlockSpec(cosine.shape, fixed)] * 2
-            + [pl.BlockSpec(mask.shape, fixed) for mask in masks],
-            out_specs=[
-                pl.BlockSpec((1, tokens, count), lambda j, place, turn: (j, 0, 0)),
-                row_spec,
-                row_spec,
-            ],
-        ),
+        in_specs=[pl.BlockSpec(memory_space=pltpu.SMEM)] * 3
+        + [whole] * len(inputs)
+        + [anywhere] * (4 + len(held.arrays)),
+        out_specs=[whole] * 4,
         out_shape=[
-            jax.ShapeDtypeStruct((kv_heads, tokens, count), jnp.bfloat16),
+            jax.ShapeDtypeStruct((kv_heads, count, HEAD_DIM), jnp.bfloat16),
             row,
             row,
+            jax.ShapeDtypeStruct((held.step_count, held.columns), jnp.float32),
+        ],
+        scratch_shapes=[
+            pltpu.VMEM((held.height, held.columns), jnp.float32),
+            pltpu.VMEM((kv_heads, tokens, count), jnp.bfloat16),
+            pltpu.VMEM((tokens, held.columns), jnp.bfloat16),
+            pltpu.SemaphoreType.DMA((1,)),
+            *held.scratch,
         ],
         compiler_params=pltpu.CompilerParams(vmem_limit_bytes=57 * MIB),
         cost_estimate=LIGHT,
-    )(places, turns, *([*queries] * share), own, other, cosine, sine, *masks)
-
-
-def apply_weights(places, weights, values):
-    kv_heads, tokens, count = weights.shape
-
-    def body(place_ref, weight_ref, value_ref, out_ref):
-        summed = lax.dot_general(
-            value_ref[:tokens, :],
-            weight_ref[0],
-            (((0,), (0,)), ((), ())),
-            preferred_element_type=jnp.float32,
-        )
-        out_ref[0] = summed.T.astype(jnp.bfloat16)
-
-    return pl.pallas_call(
-        body,
-        grid_spec=pltpu.PrefetchScalarGridSpec(
-            num_scalar_prefetch=1,
-            grid=(kv_heads,),
-            in_specs=[
-                pl.BlockSpec((1, tokens, count), lambda j, ref: (j, 0, 0)),
-                pl.BlockSpec((values.shape[0], HEAD_DIM), lambda j, ref: (0, ref[j])),
-            ],
-            out_specs=pl.BlockSpec((1, count, HEAD_DIM), lambda j, ref: (j, 0, 0)),
-        ),
-        out_shape=jax.ShapeDtypeStruct((kv_heads, count, HEAD_DIM), jnp.bfloat16),
-        compiler_params=pltpu.CompilerParams(vmem_limit_bytes=57 * MIB),
-        cost_estimate=LIGHT,
-    )(places, weights, values)
+    )(places, turns, blocks, *inputs, prompt, got, steps, early, *held.arrays)
 
 
 def out_project(blocks, heads, weight, width):
-    count = blocks.shape[0]
-    depth = weight.shape[0]
-
-    def body(block_ref, head_ref, weight_ref, out_ref, held, sems):
-        copies = []
-        for i in range(count):
+    def body(block_ref, head_ref, weight_ref, out_ref):
+        for i in range(blocks.shape[0]):
             start = pl.multiple_of(block_ref[i] * width, width)
-            copies.append(
-                pltpu.make_async_copy(
-                    weight_ref.at[:, pl.ds(start, width)], held.at[i], sems.at[i]
-                )
-            )
-            copies[-1].start()
-        for i, copy in enumerate(copies):
-            copy.wait()
             out_ref[:, i * width : (i + 1) * width] = jnp.dot(
-                head_ref[...], held[i], preferred_element_type=jnp.float32
+                head_ref[...], weight_ref[:, pl.ds(start, width)], preferred_element_type=jnp.float32
             ).astype(jnp.bfloat16)
 
     whole = pl.BlockSpec(memory_space=pltpu.VMEM)
     return pl.pallas_call(
         body,
-        in_specs=[
-            pl.BlockSpec(memory_space=pltpu.SMEM),
-            whole,
-            pl.BlockSpec(memory_space=pl.ANY),
-        ],
+        in_specs=[pl.BlockSpec(memory_space=pltpu.SMEM), whole, whole],
         out_specs=whole,
         out_shape=jax.ShapeDtypeStruct((heads.shape[0], weight.shape[1]), jnp.bfloat16),
-        scratch_shapes=[
-            pltpu.VMEM((count, depth, width), weight.dtype),
-            pltpu.SemaphoreType.DMA((count,)),
-        ],
-        compiler_params=pltpu.CompilerParams(vmem_limit_bytes=60 * MIB),
+        compiler_params=pltpu.CompilerParams(vmem_limit_bytes=10 * MIB),
         cost_estimate=LIGHT,
     )(blocks, heads, weight)
 
@@ -527,11 +508,7 @@
             key_z[k + 1] = send(along_ring, key_z[k])
             mine[k + 1] = send(along_ring, mine[k])
         key_full[k] = jnp.concatenate([key_z[k], swapped])
-        ready = [key_y[k - 1]]
-        if k == 2:
-            left = assemble(prompt_states, got, wide_states, after(own_blocks, prepared), width)
-            ready.append(left)
-        key_y[k] = send(along_y, after(key_full[k], ready))
+        key_y[k] = send(along_y, after(key_full[k], (key_y[k - 1], prepared if k == 2 else ())))
     for k in range(1, deep):
         theirs[k] = send(along_ring, theirs[k - 1])
         theirs_x[k] = send(along_x, theirs[k])
@@ -548,18 +525,18 @@
         for k, flip in places
     ]
 
-    def project_blocks(pieces, which, acc, ready, kind=jnp.float32):
-        return project(after(left, ready), which, [pieces[i] for i in which], acc, kind)
-
-    last = 2 * deep - 2
-    key_early = project_blocks(
-        key_pieces, range(last), None, (theirs[1], mine_x[deep - 1], key_y[deep - 2])
+    def project_blocks(pieces, which, ready, kind):
+        taken = after(jnp.stack([own_blocks[i] for i in which]), ready)
+        return project(
+            prompt_states, got, wide_states, taken, width, [pieces[i] for i in which], kind
+        )
+
+    key_sum = project_blocks(
+        key_pieces, range(2 * deep), (theirs[deep - 1], [theirs_x[k] for k in range(1, deep - 1)]), jnp.bfloat16
     )
     early = [*range(0, 2 * deep, 2), 1]
-    value_early = project_blocks(value_pieces, early, None, (key_early, theirs_x[1]))
-    key_sum = project_blocks(
-        key_pieces, [last, last + 1], key_early, (value_early, theirs[deep - 1], theirs_x[deep - 2]), jnp.bfloat16
-    )
+    late = [i for i in range(2 * deep) if i not in early]
+    value_early = project_blocks(value_pieces, early, key_sum, jnp.float32)
     key_back = in_chip(key_sum)
 
     def own_head(sums):
@@ -568,32 +545,18 @@
 
     new_keys = own_head(key_sum[chip_rows:]) + own_head(key_back[chip_rows:])
     new_keys = turn(new_keys, step_tables).astype(jnp.bfloat16)
-    masks = (None, None)
+    masks = []
     if prompts > 1:
         token_prompt = jnp.repeat(slots // PROMPT_PAGES, PAGE)
         row_prompt = jnp.tile(sample_order // group_size, devices // KV_HEADS * rows // samples)
-        masks = (token_prompt[:, None], row_prompt[None, :])
-    weights, top, total = attend(
-        kv_places, query_turns, ring_queries, key_sum, key_back, cosine, sine_part, *masks
-    )
-
-    stats = jnp.stack([top.reshape(by_owner), total.reshape(by_owner)])
-    stats = jnp.stack([stats, along_y(stats)[:, :, :, ::-1]])
-    weights = after(weights, stats)
-    stats = jnp.concatenate([stats] + [along_z(stats, k) for k in range(1, deep)])
-    prefix_top = jnp.max(stats[:, 0], axis=0)
-    prefix_total = jnp.sum(jnp.exp(stats[:, 0] - prefix_top) * stats[:, 1], axis=0)
-    factor = jnp.exp(top.reshape(by_owner) - prefix_top)[:, 0]
-    prefix_top = lax.dynamic_index_in_dim(prefix_top, own_a, 0, False)[0, 0]
-    prefix_total = lax.dynamic_index_in_dim(prefix_total, own_a, 0, False)[0, 0]
-
-    late = [i for i in range(2 * deep) if i not in early]
-    value_sum = project_blocks(value_pieces, late, value_early, weights, jnp.bfloat16)
-    step_values = own_head(value_sum[chip_rows:])
-    step_back = own_head(in_chip(value_sum[chip_rows:]))
-    new_values = (step_values + step_back).astype(jnp.bfloat16)
-    partial = apply_weights(kv_places, weights, value_sum)
-    partial = partial.reshape(by_owner + (HEAD_DIM,))
+        masks = [token_prompt[:, None], row_prompt[None, :]]
+    partial, top, total, step_values = attend(
+        kv_places, query_turns, ring_queries, key_sum, key_back, cosine, sine_part, masks,
+        prompt_states, got, wide_states, jnp.stack([own_blocks[i] for i in late]), width,
+        [value_pieces[i] for i in late], value_early,
+    )
+    new_values = own_head(step_values) + own_head(in_chip(step_values))
+    new_values = new_values.astype(jnp.bfloat16)
 
     def narrow(value):
         return value.astype(jnp.bfloat16)
@@ -601,13 +564,29 @@
     def wide(value):
         return value.astype(jnp.float32)
 
-    partial = wide(partial[:, 0]) + wide(in_chip(partial[:, 1]))
-    partial = narrow(partial * factor[..., None])
-    partial = narrow(wide(partial[:, 0]) + wide(along_y(partial[:, 1])))
-    prefix_sum = wide(lax.dynamic_index_in_dim(partial, own_a, 0, False))
+    def to_z(value, k):
+        return lax.dynamic_index_in_dim(value, (own_a + k) % deep, 0, False)
+
+    stats = jnp.stack([top.reshape(by_owner)[:, 0], total.reshape(by_owner)[:, 0]], axis=2)
+    partial = partial.reshape(by_owner + (HEAD_DIM,))
+    near = stats[:, 0]
+    far = along_y(stats[:, 1])
+    top = jnp.maximum(near[:, 0], far[:, 0])
+    near_factor, far_factor = jnp.exp(near[:, 0] - top), jnp.exp(far[:, 0] - top)
+    stats = jnp.stack([top, near[:, 1] * near_factor + far[:, 1] * far_factor], axis=1)
+    stats = jnp.stack([to_z(stats, 0)] + [along_z(to_z(stats, k), k) for k in range(1, deep)])
+    prefix_top = jnp.max(stats[:, 0], axis=0)
+    factors = jnp.exp(stats[:, 0] - prefix_top)
+    prefix_total = jnp.sum(stats[:, 1] * factors, axis=0)
+
+    partial = narrow(wide(partial[:, 0]) + wide(in_chip(partial[:, 1])))
+    partial = narrow(
+        wide(partial[:, 0]) * near_factor[..., None]
+        + wide(along_y(partial[:, 1])) * far_factor[..., None]
+    )
+    prefix_sum = wide(to_z(partial, 0)) * factors[0][:, None]
     for k in range(1, deep):
-        piece = lax.dynamic_index_in_dim(partial, (own_a + k) % deep, 0, False)
-        prefix_sum = prefix_sum + wide(along_z(piece, k))
+        prefix_sum = prefix_sum + wide(along_z(to_z(partial, k), k)) * factors[k][:, None]
 
     by_head = (heads_here, 2, samples)
     head_out = finish_heads(

time: 185 us -> 171 us (0.924)
  Pallas kernels: 53.6 us -> 32.3 us
  starting transfers between devices: 54 us -> 67.6 us
  other arithmetic: 12.8 us -> 9.47 us
    pallas_call x7 -> x3, Pallas kernels: 45.7 us -> 28.5 us  [the longest x2 16.8 us: project(): pl.pallas_call(body, in_specs=[pl.BlockSpec(memory_space=pltpu.SMEM)] + [...]
    ppermute x42, starting transfers between devices: 54 us -> 67.6 us  [move(): return lax.ppermute(value, ('groups', 'sample'), pairs)]
    pallas_call x1, Pallas kernels: 5.58 us -> 1.39 us  [out_project(): pl.pallas_call(body, in_specs=[pl.BlockSpec(memory_space=pltpu.SMEM), who...]
    unnamed x70 -> x69, local copies, waits for them, and re-layouts: 8.93 us -> 8.72 us
  transfers between devices with their start and end apart: 42 -> 42, of which waited for: 18 -> 20; matrix products, arithmetic and copies ran while one was open for 10% -> 8% of each run, Pallas kernels for 24% -> 6%
where the time goes in v10:
time: 171 us
  starting transfers between devices  67.6 us (40%)
  waiting for transfers between devices  46.5 us (27%)
  Pallas kernels  32.3 us (19%)
  local copies, waits for them, and re-layouts  14.1 us (8%)
  other arithmetic  9.47 us (6%)
    ppermute x42, starting transfers between devices, move(): return lax.ppermute(value, ('groups', 'sample'), pairs)  67.6 us
    ppermute x42, waiting for transfers between devices, move(): return lax.ppermute(value, ('groups', 'sample'), pairs)  46.5 us
    pallas_call x2, Pallas kernels, project(): pl.pallas_call(body, in_specs=[pl.BlockSpec(memory_space=pltpu.SMEM)] + [...  16.8 us
    pallas_call x1, Pallas kernels, attend(): pl.pallas_call(body, in_specs=[pl.BlockSpec(memory_space=pltpu.SMEM)] * 3...  11.7 us
    unnamed x69, local copies, waits for them, and re-layouts  8.72 us
  transfers between devices with their start and end apart: 42, of which 20 were waited for; matrix products, arithmetic and copies ran while one was open for 8% of the time, Pallas kernels for 6%

profile of v10, /device:TPU:0, one launch (start us, length us, event | category | flops | bytes accessed | tf_op | source)
XLA Modules:
  0.0 170.7 jit_solution(17487211968970556888)
XLA Ops:
  0.5 1.9 %broadcast_select_fusion = (bf16[512,256]{1,0:T(8,128)(2,1)}, bf16[512,256]{1,0:T(8,128)(2,1)S(1)}) fusion(pred[]{:T(512)S(6)} %eq.98, bf16[512,512]{1,0:T(8,128)(2,1)} %param.12), kind=kLoop, calls=%fused_computation.13 | loop fusion | flops 262144 | bytes 1048577 | tf_op jit(solution)/shard_map/jit(_where)/select_n | solution.py:446
  2.3 2.6 %collective-permute-start = (bf16[512,256]{1,0:T(8,128)(2,1)S(1)}, bf16[512,256]{1,0:T(8,128)(2,1)S(1)}, u32[]{:S(2)}, u32[]{:S(2)}) collective-permute-start(bf16[512,256]{1,0:T(8,128)(2,1)S(1)} %get-tuple-element.81.refs_0_), channel_id=1, source_target_pairs={{0,2},{1,3},{2,0},{3,1},{4,6},{5,7},{6,4},{7,5},{8,10},{9,11},{10,... | collective-permute-start | bytes 786440 | tf_op jit(solution)/shard_map/ppermute | solution.py:82
  4.9 2.6 %collective-permute-start.6 = (bf16[512,256]{1,0:T(8,128)(2,1)S(1)}, bf16[512,256]{1,0:T(8,128)(2,1)S(1)}, u32[]{:S(2)}, u32[]{:S(2)}) collective-permute-start(bf16[512,256]{1,0:T(8,128)(2,1)S(1)} %get-tuple-element.81.refs_0_), channel_id=1, source_target_pairs={{0,8},{1,9},{2,10},{3,11},{4,0},{5,1},{6,2},{7,3},{8,12},{9,13},{1... | collective-permute-start | bytes 786440 | tf_op jit(solution)/shard_map/ppermute | solution.py:82
  7.5 1.6 collective-permute-start.1
  9.7 2.2 %copy-done.1 = bf16[8192,256]{1,0:T(8,128)(2,1)S(1)} copy-done((bf16[8192,256]{1,0:T(8,128)(2,1)S(1)}, bf16[8192,256]{1,0:T(8,128)(2,1)}, u32[]{:S(2)}) %copy-start.1) | copy-done | bytes 4194328
  11.9 2.0 %shard_map.73 = bf16[64,256]{1,0:T(8,128)(2,1)S(1)} custom-call(bf16[64,8192]{1,0:T(8,128)(2,1)S(1)} %bitcast.162, bf16[8192,256]{1,0:T(8,128)(2,1)S(1)} %copy-done.1, f32[64,128]{1,0:T(8,128)S(1)} %bitcast.163, f32[64,128]{1,0:T(8,128)S(1)} %bitcast.164), custom_call_target="tpu_custom_call" | custom-call | flops 1 | bytes 1 | tf_op jit(solution)/shard_map/pallas_call | solution.py:132
  13.9 5.1 %collective-permute-done.1 = bf16[512,256]{1,0:T(8,128)(2,1)} collective-permute-done((bf16[512,256]{1,0:T(8,128)(2,1)S(1)}, bf16[512,256]{1,0:T(8,128)(2,1)}, u32[]{:S(2)}, u32[]{:S(2)}) %collective-permute-start.1) | collective-permute-done | bytes 262176 | tf_op jit(solution)/shard_map/ppermute | solution.py:82
  19.6 1.5 collective-permute-start.16
  21.1 3.1 %multiply_sine_fusion = (f32[1024,64]{1,0:T(8,128)}, f32[1024,64]{1,0:T(8,128)}) fusion(f32[64]{0:T(128)S(1)} %multiply_power_fusion, f32[1024]{0:T(1024)S(1)} %convert_bitcast_fusion), kind=kLoop, calls=%fused_computation.1 | loop fusion | flops 65536 | bytes 528640 | tf_op jit(solution)/shard_map/sin | solution.py:23
  24.1 3.5 %collective-permute-start.3 = (bf16[512,256]{1,0:T(8,128)(2,1)}, bf16[512,256]{1,0:T(8,128)(2,1)}, u32[]{:S(2)}, u32[]{:S(2)}) collective-permute-start(bf16[512,256]{1,0:T(8,128)(2,1)} %collective-permute-done.1), channel_id=1, source_target_pairs={{0,8},{1,9},{2,10},{3,11},{4,0},{5,1},{6,2},{7,3},{8,12},{9,13},{1... | collective-permute-start | bytes 786440 | tf_op jit(solution)/shard_map/ppermute | solution.py:82
  28.2 1.0 constant_dynamic-update-slice_fusion.1
  29.3 2.4 %collective-permute-start.7 = (bf16[512,256]{1,0:T(8,128)(2,1)S(1)}, bf16[512,256]{1,0:T(8,128)(2,1)}, u32[]{:S(2)}, u32[]{:S(2)}) collective-permute-start(bf16[512,256]{1,0:T(8,128)(2,1)S(1)} %collective-permute-done.6.refs_2_), channel_id=1, source_target_pairs={{0,8},{1,9},{2,10},{3,11},{4,0},{5,1},{6,2},{7,3},{8,12},{9,13},{1... | collective-permute-start | bytes 786440 | tf_op jit(solution)/shard_map/ppermute | solution.py:82
  31.7 1.2 collective-permute-done.2.refs_1_
  34.7 1.5 collective-permute-start.13
  36.3 2.7 %collective-permute-start.4 = (bf16[512,256]{1,0:T(8,128)(2,1)}, bf16[512,256]{1,0:T(8,128)(2,1)S(1)}, u32[]{:S(2)}, u32[]{:S(2)}) collective-permute-start(bf16[512,256]{1,0:T(8,128)(2,1)} %collective-permute-done.3), channel_id=1, source_target_pairs={{0,8},{1,9},{2,10},{3,11},{4,0},{5,1},{6,2},{7,3},{8,12},{9,13},{1... | collective-permute-start | bytes 786440 | tf_op jit(solution)/shard_map/ppermute | solution.py:82
  39.6 2.5 %collective-permute-start.8 = (bf16[512,256]{1,0:T(8,128)(2,1)}, bf16[512,256]{1,0:T(8,128)(2,1)S(1)}, u32[]{:S(2)}, u32[]{:S(2)}) collective-permute-start(bf16[512,256]{1,0:T(8,128)(2,1)} %collective-permute-done.7.refs_4_), channel_id=1, source_target_pairs={{0,8},{1,9},{2,10},{3,11},{4,0},{5,1},{6,2},{7,3},{8,12},{9,13},{1... | collective-permute-start | bytes 786440 | tf_op jit(solution)/shard_map/ppermute | solution.py:82
  42.1 1.0 constant_dynamic-update-slice_fusion.3
  43.1 2.9 %collective-permute-done.4 = bf16[512,256]{1,0:T(8,128)(2,1)S(1)} collective-permute-done((bf16[512,256]{1,0:T(8,128)(2,1)}, bf16[512,256]{1,0:T(8,128)(2,1)S(1)}, u32[]{:S(2)}, u32[]{:S(2)}) %collective-permute-start.4) | collective-permute-done | bytes 262176 | tf_op jit(solution)/shard_map/ppermute | solution.py:82
  46.0 1.2 collective-permute-start.17
  47.2 3.3 %collective-permute-start.5 = (bf16[640,256]{1,0:T(8,128)(2,1)S(1)}, bf16[640,256]{1,0:T(8,128)(2,1)S(1)}, u32[]{:S(2)}, u32[]{:S(2)}) collective-permute-start(bf16[640,256]{1,0:T(8,128)(2,1)S(1)} %pad_maximum_fusion.1.refs_0_.refs_8_), channel_id=1, source_target_pairs={{0,8},{1,9},{2,10},{3,11},{4,0},{5,1},{6,2},{7,3},{8,12},{9,13},{1... | collective-permute-start | bytes 983048 | tf_op jit(solution)/shard_map/ppermute | solution.py:82
  50.5 1.6 collective-permute-start.23
  52.1 3.0 %collective-permute-done.17.refs_9_ = bf16[512,256]{1,0:T(8,128)(2,1)S(1)} collective-permute-done((bf16[512,256]{1,0:T(8,128)(2,1)S(1)}, bf16[512,256]{1,0:T(8,128)(2,1)S(1)}, u32[]{:S(2)}, u32[]{:S(2)}) %collective-permute-start.17) | collective-permute-done | bytes 262176 | tf_op jit(solution)/shard_map/ppermute | solution.py:82
  55.1 1.2 collective-permute-start.18
  56.3 0.8 collective-permute-start.14
  57.1 3.3 %collective-permute-start.9 = (bf16[640,256]{1,0:T(8,128)(2,1)S(1)}, bf16[640,256]{1,0:T(8,128)(2,1)S(1)}, u32[]{:S(2)}, u32[]{:S(2)}) collective-permute-start(bf16[640,256]{1,0:T(8,128)(2,1)S(1)} %collective-permute-done.5.refs_1_.refs_10_), channel_id=1, source_target_pairs={{0,8},{1,9},{2,10},{3,11},{4,0},{5,1},{6,2},{7,3},{8,12},{9,13},{1... | collective-permute-start | bytes 983048 | tf_op jit(solution)/shard_map/ppermute | solution.py:82
  60.5 3.1 %collective-permute-done.18.refs_5_ = bf16[512,256]{1,0:T(8,128)(2,1)S(1)} collective-permute-done((bf16[512,256]{1,0:T(8,128)(2,1)}, bf16[512,256]{1,0:T(8,128)(2,1)S(1)}, u32[]{:S(2)}, u32[]{:S(2)}) %collective-permute-start.18) | collective-permute-done | bytes 262176 | tf_op jit(solution)/shard_map/ppermute | solution.py:82
  63.5 2.2 %collective-permute-start.19 = (bf16[512,256]{1,0:T(8,128)(2,1)S(1)}, bf16[512,256]{1,0:T(8,128)(2,1)S(1)}, u32[]{:S(2)}, u32[]{:S(2)}) collective-permute-start(bf16[512,256]{1,0:T(8,128)(2,1)S(1)} %collective-permute-done.8.refs_6_), channel_id=1, source_target_pairs={{0,16},{1,17},{2,18},{3,19},{4,20},{5,21},{6,22},{7,23},{8,24},{9,... | collective-permute-start | bytes 786440 | tf_op jit(solution)/shard_map/ppermute | solution.py:82
  65.7 3.5 %collective-permute-done.14 = bf16[512,256]{1,0:T(8,128)(2,1)S(1)} collective-permute-done((bf16[512,256]{1,0:T(8,128)(2,1)S(1)}, bf16[512,256]{1,0:T(8,128)(2,1)S(1)}, u32[]{:S(2)}, u32[]{:S(2)}) %collective-permute-start.14) | collective-permute-done | bytes 262176 | tf_op jit(solution)/shard_map/ppermute | solution.py:82
  69.2 1.6 collective-permute-start.24
  70.8 2.2 %collective-permute-start.15 = (bf16[640,256]{1,0:T(8,128)(2,1)S(1)}, bf16[640,256]{1,0:T(8,128)(2,1)}, u32[]{:S(2)}, u32[]{:S(2)}) collective-permute-start(bf16[640,256]{1,0:T(8,128)(2,1)S(1)} %collective-permute-done.5.refs_1_.refs_10_), channel_id=1, source_target_pairs={{0,16},{1,17},{2,18},{3,19},{4,20},{5,21},{6,22},{7,23},{8,24},{9,... | collective-permute-start | bytes 983048 | tf_op jit(solution)/shard_map/ppermute | solution.py:82
  73.0 1.8 %collective-permute-done.19.refs_7_ = bf16[512,256]{1,0:T(8,128)(2,1)S(1)} collective-permute-done((bf16[512,256]{1,0:T(8,128)(2,1)S(1)}, bf16[512,256]{1,0:T(8,128)(2,1)S(1)}, u32[]{:S(2)}, u32[]{:S(2)}) %collective-permute-start.19) | collective-permute-done | bytes 262176 | tf_op jit(solution)/shard_map/ppermute | solution.py:82
  74.8 2.2 %collective-permute-start.20 = (bf16[640,256]{1,0:T(8,128)(2,1)S(1)}, bf16[640,256]{1,0:T(8,128)(2,1)}, u32[]{:S(2)}, u32[]{:S(2)}) collective-permute-start(bf16[640,256]{1,0:T(8,128)(2,1)S(1)} %collective-permute-done.9.refs_2_.refs_12_), channel_id=1, source_target_pairs={{0,16},{1,17},{2,18},{3,19},{4,20},{5,21},{6,22},{7,23},{8,24},{9,... | collective-permute-start | bytes 983048 | tf_op jit(solution)/shard_map/ppermute | solution.py:82
  77.0 3.3 %collective-permute-start.10 = (bf16[640,256]{1,0:T(8,128)(2,1)S(1)}, bf16[640,256]{1,0:T(8,128)(2,1)S(1)}, u32[]{:S(2)}, u32[]{:S(2)}) collective-permute-start(bf16[640,256]{1,0:T(8,128)(2,1)S(1)} %collective-permute-done.9.refs_2_.refs_12_), channel_id=1, source_target_pairs={{0,8},{1,9},{2,10},{3,11},{4,0},{5,1},{6,2},{7,3},{8,12},{9,13},{1... | collective-permute-start | bytes 983048 | tf_op jit(solution)/shard_map/ppermute | solution.py:82
  81.0 3.2 %collective-permute-done.20.refs_13_ = bf16[640,256]{1,0:T(8,128)(2,1)} collective-permute-done((bf16[640,256]{1,0:T(8,128)(2,1)S(1)}, bf16[640,256]{1,0:T(8,128)(2,1)}, u32[]{:S(2)}, u32[]{:S(2)}) %collective-permute-start.20) | collective-permute-done | bytes 327712 | tf_op jit(solution)/shard_map/ppermute | solution.py:82
  84.2 0.7 collective-permute-done.10.refs_3_.refs_14_
  85.0 0.8 copy-done.17
  85.8 9.3 %shard_map.75.refs_2_ = bf16[1088,512]{1,0:T(8,128)(2,1)} custom-call(s32[8]{0:T(128)} %stack.157.block_ref, bf16[512,8192]{1,0:T(8,128)(2,1)} %refs_6_.1, bf16[512,8192]{1,0:T(8,128)(2,1)} %collective-permute-done.21.got_ref.refs_7_, bf16[64,8192]{1,0:T(8,128)(2,1)} %bitcast.159, bf16[1088,256]{1,0:T(8,128)(2,1)} %copy-done.8, ...), custom_call_target="tpu_custom_call" | custom-call | flops 1 | bytes 1 | tf_op jit(solution)/shard_map/pallas_call | solution.py:245
  96.7 1.1 collective-permute-start.26
  98.5 7.5 %shard_map.76.refs_9_ = f32[1088,512]{1,0:T(8,128)} custom-call(s32[5]{0:T(128)} %stack.158.block_ref, bf16[512,8192]{1,0:T(8,128)(2,1)} %refs_6_.1, bf16[512,8192]{1,0:T(8,128)(2,1)} %collective-permute-done.21.got_ref.refs_7_, bf16[64,8192]{1,0:T(8,128)(2,1)} %bitcast.160, bf16[512,256]{1,0:T(8,128)(2,1)} %copy-done.13, ...), custom_call_target="tpu_custom_call" | custom-call | flops 1 | bytes 1 | tf_op jit(solution)/shard_map/pallas_call | solution.py:245
  106.1 0.8 slice.210
  108.0 0.7 copy-done.19
  108.8 11.7 %shard_map.77 = (bf16[4,512,128]{2,1,0:T(8,128)(2,1)}, f32[4,1,512]{2,1,0:T(1,128)}, f32[4,1,512]{2,1,0:T(1,128)}, f32[64,512]{1,0:T(8,128)}) custom-call(s32[4]{0:T(128)} %and_select_fusion.1.place_ref, s32[4]{0:T(128)} %pad_add_fusion.turn_ref, s32[3]{0:T(128)} %pad_add_fusion.1.block_ref, bf16[4,128,256]{2,1,0:T(8,128)(2,1)} %copy-done.7, ...), custom_call_target="tpu_custom_call" | custom-call | flops 1 | bytes 1 | tf_op jit(solution)/shard_map/pallas_call | solution.py:354
  120.5 0.7 slice.201
  121.9 1.5 collective-permute-start.27
  123.4 1.1 fusion.42
  125.6 2.4 %collective-permute-start.28 = (f32[2,128]{1,0:T(2,128)S(1)}, f32[2,128]{1,0:T(2,128)S(1)}, u32[]{:S(2)}, u32[]{:S(2)}) collective-permute-start(f32[2,128]{1,0:T(2,128)S(1)} %bitcast.186), channel_id=1, source_target_pairs={{0,4},{1,5},{2,6},{3,7},{4,8},{5,9},{6,10},{7,11},{8,12},{9,13},{1... | collective-permute-start | bytes 3080 | tf_op jit(solution)/shard_map/ppermute | solution.py:82
  128.0 1.1 collective-permute-start.29
  129.1 2.8 %collective-permute-start.30 = (f32[2,128]{1,0:T(2,128)S(1)}, f32[2,128]{1,0:T(2,128)S(1)}, u32[]{:S(2)}, u32[]{:S(2)}) collective-permute-start(f32[2,128]{1,0:T(2,128)S(1)} %bitcast.184), channel_id=1, source_target_pairs={{0,12},{1,13},{2,14},{3,15},{4,0},{5,1},{6,2},{7,3},{8,4},{9,5},{1... | collective-permute-start | bytes 3080 | tf_op jit(solution)/shard_map/ppermute | solution.py:82
  132.4 0.8 collective-permute-done.30
  133.6 1.6 collective-permute-start.32
  135.2 3.5 %collective-permute-done.32 = bf16[4,128,128]{2,1,0:T(8,128)(2,1)S(1)} collective-permute-done((bf16[4,128,128]{2,1,0:T(8,128)(2,1)S(1)}, bf16[4,128,128]{2,1,0:T(8,128)(2,1)S(1)}, u32[]{:S(2)}, u32[]{:S(2)}) %collective-permute-start.32) | collective-permute-done | bytes 131104 | tf_op jit(solution)/shard_map/ppermute | solution.py:82
  138.9 0.9 collective-permute-start.33
  139.7 3.8 %collective-permute-start.34 = (bf16[128,128]{1,0:T(8,128)(2,1)S(1)}, bf16[128,128]{1,0:T(8,128)(2,1)S(1)}, u32[]{:S(2)}, u32[]{:S(2)}) collective-permute-start(bf16[128,128]{1,0:T(8,128)(2,1)S(1)} %get-tuple-element.89), channel_id=1, source_target_pairs={{0,8},{1,9},{2,10},{3,11},{4,12},{5,13},{6,14},{7,15},{8,0},{9,1},... | collective-permute-start | bytes 98312 | tf_op jit(solution)/shard_map/ppermute | solution.py:82
  143.6 1.3 collective-permute-done.33
  145.6 1.9 %collective-permute-done.35 = bf16[128,128]{1,0:T(8,128)(2,1)S(1)} collective-permute-done((bf16[128,128]{1,0:T(8,128)(2,1)S(1)}, bf16[128,128]{1,0:T(8,128)(2,1)S(1)}, u32[]{:S(2)}, u32[]{:S(2)}) %collective-permute-start.35) | collective-permute-done | bytes 32800 | tf_op jit(solution)/shard_map/ppermute | solution.py:82
  147.8 2.2 %copy-done.2 = bf16[256,8192]{1,0:T(8,128)(2,1)S(1)} copy-done((bf16[256,8192]{1,0:T(8,128)(2,1)S(1)}, bf16[256,8192]{1,0:T(8,128)(2,1)}, u32[]{:S(2)}) %copy-start.2) | copy-done | bytes 4194328
  150.0 1.4 shard_map.78
  151.5 1.9 %collective-permute-done.37 = bf16[64,4096]{1,0:T(8,128)(2,1)S(1)} collective-permute-done((bf16[64,4096]{1,0:T(8,128)(2,1)S(1)}, bf16[64,4096]{1,0:T(8,128)(2,1)S(1)}, u32[]{:S(2)}, u32[]{:S(2)}) %collective-permute-start.37) | collective-permute-done | bytes 524320 | tf_op jit(solution)/shard_map/ppermute | solution.py:82
  153.6 1.6 collective-permute-start.38
  155.1 6.9 %collective-permute-done.38 = bf16[64,2048]{1,0:T(8,128)(2,1)S(1)} collective-permute-done((bf16[64,2048]{1,0:T(8,128)(2,1)S(1)}, bf16[64,2048]{1,0:T(8,128)(2,1)S(1)}, u32[]{:S(2)}, u32[]{:S(2)}) %collective-permute-start.38) | collective-permute-done | bytes 262176 | tf_op jit(solution)/shard_map/ppermute | solution.py:82
  162.2 2.6 %collective-permute-start.40 = (bf16[64,512]{1,0:T(8,128)(2,1)S(1)}, bf16[64,512]{1,0:T(8,128)(2,1)S(1)}, u32[]{:S(2)}, u32[]{:S(2)}) collective-permute-start(bf16[64,512]{1,0:T(8,128)(2,1)S(1)} %get-tuple-element.86), channel_id=1, source_target_pairs={{0,8},{1,9},{2,10},{3,11},{4,12},{5,13},{6,14},{7,15},{8,0},{9,1},... | collective-permute-start | bytes 196616 | tf_op jit(solution)/shard_map/ppermute | solution.py:82
  164.9 1.1 collective-permute-start.41
  166.0 2.7 %collective-permute-done.39 = bf16[64,512]{1,0:T(8,128)(2,1)S(1)} collective-permute-done((bf16[64,512]{1,0:T(8,128)(2,1)S(1)}, bf16[64,512]{1,0:T(8,128)(2,1)S(1)}, u32[]{:S(2)}, u32[]{:S(2)}) %collective-permute-start.39) | collective-permute-done | bytes 65568 | tf_op jit(solution)/shard_map/ppermute | solution.py:82
  168.7 1.3 collective-permute-done.40
  (169 shorter events, 13.8 us)
Async XLA Ops:
  0.0 7.5 %copy-start.18 = (bf16[512,512]{1,0:T(8,128)(2,1)S(1)}, bf16[512,512]{1,0:T(8,128)(2,1)}, u32[]{:S(2)}) copy-start(bf16[512,512]{1,0:T(8,128)(2,1)} %param.11) | copy-start | bytes 1572868
  0.0 9.3 %copy-start.30 = (s32[64]{0:T(128)S(1)}, s32[64]{0:T(128)}, u32[]{:S(2)}) copy-start(s32[64]{0:T(128)} %param.9) | copy-start | bytes 772
  0.0 84.9 %collective-permute-start.21 = (bf16[512,8192]{1,0:T(8,128)(2,1)}, bf16[512,8192]{1,0:T(8,128)(2,1)}, u32[]{:S(2)}, u32[]{:S(2)}) collective-permute-start(bf16[512,8192]{1,0:T(8,128)(2,1)} %refs_6_.1), channel_id=1, source_target_pairs={{0,1},{1,0},{2,3},{3,2},{4,5},{5,4},{6,7},{7,6},{8,9},{9,8},{10,11... | collective-permute-start | bytes 25165832 | tf_op jit(solution)/shard_map/ppermute | solution.py:82
  0.5 9.2 %copy-start = (bf16[2,32,8192]{2,1,0:T(8,128)(2,1)S(1)}, bf16[2,32,8192]{2,1,0:T(8,128)(2,1)}, u32[]{:S(2)}) copy-start(bf16[2,32,8192]{2,1,0:T(8,128)(2,1)} %param.10) | copy-start | bytes 3145732
  2.3 11.5 %copy-start.13 = (bf16[512,256]{1,0:T(8,128)(2,1)}, bf16[512,256]{1,0:T(8,128)(2,1)S(1)}, u32[]{:S(2)}) copy-start(bf16[512,256]{1,0:T(8,128)(2,1)S(1)} %get-tuple-element.81.refs_0_) | copy-start | bytes 786436
  2.3 11.6 %collective-permute-start = (bf16[512,256]{1,0:T(8,128)(2,1)S(1)}, bf16[512,256]{1,0:T(8,128)(2,1)S(1)}, u32[]{:S(2)}, u32[]{:S(2)}) collective-permute-start(bf16[512,256]{1,0:T(8,128)(2,1)S(1)} %get-tuple-element.81.refs_0_), channel_id=1, source_target_pairs={{0,2},{1,3},{2,0},{3,1},{4,6},{5,7},{6,4},{7,5},{8,10},{9,11},{10,... | collective-permute-start | bytes 786440 | tf_op jit(solution)/shard_map/ppermute | solution.py:82
  4.9 22.7 %collective-permute-start.6 = (bf16[512,256]{1,0:T(8,128)(2,1)S(1)}, bf16[512,256]{1,0:T(8,128)(2,1)S(1)}, u32[]{:S(2)}, u32[]{:S(2)}) collective-permute-start(bf16[512,256]{1,0:T(8,128)(2,1)S(1)} %get-tuple-element.81.refs_0_), channel_id=1, source_target_pairs={{0,8},{1,9},{2,10},{3,11},{4,0},{5,1},{6,2},{7,3},{8,12},{9,13},{1... | collective-permute-start | bytes 786440 | tf_op jit(solution)/shard_map/ppermute | solution.py:82
  7.5 11.5 %collective-permute-start.1 = (bf16[512,256]{1,0:T(8,128)(2,1)S(1)}, bf16[512,256]{1,0:T(8,128)(2,1)}, u32[]{:S(2)}, u32[]{:S(2)}) collective-permute-start(bf16[512,256]{1,0:T(8,128)(2,1)S(1)} %get-tuple-element.82), channel_id=1, source_target_pairs={{0,8},{1,9},{2,10},{3,11},{4,0},{5,1},{6,2},{7,3},{8,12},{9,13},{1... | collective-permute-start | bytes 786440 | tf_op jit(solution)/shard_map/ppermute | solution.py:82
  13.9 20.1 %copy-start.8 = (bf16[1088,256]{1,0:T(8,128)(2,1)}, bf16[1088,256]{1,0:T(8,128)(2,1)S(1)}, u32[]{:S(2)}) copy-start(bf16[1088,256]{1,0:T(8,128)(2,1)S(1)} %pad_maximum_fusion.refs_0_) | copy-start | bytes 1671172
  13.9 13.7 %copy-start.27 = (bf16[512,256]{1,0:T(8,128)(2,1)}, bf16[512,256]{1,0:T(8,128)(2,1)S(1)}, u32[]{:S(2)}) copy-start(bf16[512,256]{1,0:T(8,128)(2,1)S(1)} %collective-permute-done) | copy-start | bytes 786436
  19.0 13.9 %collective-permute-start.2 = (bf16[1088,256]{1,0:T(8,128)(2,1)S(1)}, bf16[1088,256]{1,0:T(8,128)(2,1)S(1)}, u32[]{:S(2)}, u32[]{:S(2)}) collective-permute-start(bf16[1088,256]{1,0:T(8,128)(2,1)S(1)} %pad_maximum_fusion.refs_0_), channel_id=1, source_target_pairs={{0,2},{1,3},{2,0},{3,1},{4,6},{5,7},{6,4},{7,5},{8,10},{9,11},{10,... | collective-permute-start | bytes 1671176 | tf_op jit(solution)/shard_map/ppermute | solution.py:82
  19.6 9.7 %collective-permute-start.16 = (bf16[512,256]{1,0:T(8,128)(2,1)}, bf16[512,256]{1,0:T(8,128)(2,1)S(1)}, u32[]{:S(2)}, u32[]{:S(2)}) collective-permute-start(bf16[512,256]{1,0:T(8,128)(2,1)} %collective-permute-done.1), channel_id=1, source_target_pairs={{0,16},{1,17},{2,18},{3,19},{4,20},{5,21},{6,22},{7,23},{8,24},{9,... | collective-permute-start | bytes 786440 | tf_op jit(solution)/shard_map/ppermute | solution.py:82
  24.1 10.6 %collective-permute-start.3 = (bf16[512,256]{1,0:T(8,128)(2,1)}, bf16[512,256]{1,0:T(8,128)(2,1)}, u32[]{:S(2)}, u32[]{:S(2)}) collective-permute-start(bf16[512,256]{1,0:T(8,128)(2,1)} %collective-permute-done.1), channel_id=1, source_target_pairs={{0,8},{1,9},{2,10},{3,11},{4,0},{5,1},{6,2},{7,3},{8,12},{9,13},{1... | collective-permute-start | bytes 786440 | tf_op jit(solution)/shard_map/ppermute | solution.py:82
  27.6 15.5 %copy-start.20 = (bf16[512,256]{1,0:T(8,128)(2,1)}, bf16[512,256]{1,0:T(8,128)(2,1)S(1)}, u32[]{:S(2)}) copy-start(bf16[512,256]{1,0:T(8,128)(2,1)S(1)} %collective-permute-done.6.refs_2_) | copy-start | bytes 786436
  27.6 7.1 %collective-permute-start.12 = (bf16[512,256]{1,0:T(8,128)(2,1)S(1)}, bf16[512,256]{1,0:T(8,128)(2,1)S(1)}, u32[]{:S(2)}, u32[]{:S(2)}) collective-permute-start(bf16[512,256]{1,0:T(8,128)(2,1)S(1)} %collective-permute-done.6.refs_2_), channel_id=1, source_target_pairs={{0,16},{1,17},{2,18},{3,19},{4,20},{5,21},{6,22},{7,23},{8,24},{9,... | collective-permute-start | bytes 786440 | tf_op jit(solution)/shard_map/ppermute | solution.py:82
  28.2 14.9 %copy-start.28 = (bf16[512,256]{1,0:T(8,128)(2,1)S(1)}, bf16[512,256]{1,0:T(8,128)(2,1)}, u32[]{:S(2)}) copy-start(bf16[512,256]{1,0:T(8,128)(2,1)} %copy-done.27) | copy-start | bytes 786436
  29.3 10.3 %collective-permute-start.7 = (bf16[512,256]{1,0:T(8,128)(2,1)S(1)}, bf16[512,256]{1,0:T(8,128)(2,1)}, u32[]{:S(2)}, u32[]{:S(2)}) collective-permute-start(bf16[512,256]{1,0:T(8,128)(2,1)S(1)} %collective-permute-done.6.refs_2_), channel_id=1, source_target_pairs={{0,8},{1,9},{2,10},{3,11},{4,0},{5,1},{6,2},{7,3},{8,12},{9,13},{1... | collective-permute-start | bytes 786440 | tf_op jit(solution)/shard_map/ppermute | solution.py:82
  31.7 28.8 %copy-start.12 = (bf16[1024,256]{1,0:T(8,128)(2,1)}, bf16[1024,256]{1,0:T(8,128)(2,1)S(1)}, u32[]{:S(2)}) copy-start(bf16[1024,256]{1,0:T(8,128)(2,1)S(1)} %constant_dynamic-update-slice_fusion.refs_2_) | copy-start | bytes 1572868
  32.9 10.2 %copy-start.14 = (bf16[1088,256]{1,0:T(8,128)(2,1)}, bf16[1088,256]{1,0:T(8,128)(2,1)S(1)}, u32[]{:S(2)}) copy-start(bf16[1088,256]{1,0:T(8,128)(2,1)S(1)} %collective-permute-done.2.refs_1_) | copy-start | bytes 1671172
  32.9 17.6 %collective-permute-start.22 = (bf16[1024,256]{1,0:T(8,128)(2,1)S(1)}, bf16[1024,256]{1,0:T(8,128)(2,1)S(1)}, u32[]{:S(2)}, u32[]{:S(2)}) collective-permute-start(bf16[1024,256]{1,0:T(8,128)(2,1)S(1)} %constant_dynamic-update-slice_fusion.refs_2_), channel_id=1, source_target_pairs={{0,2},{1,3},{2,0},{3,1},{4,6},{5,7},{6,4},{7,5},{8,10},{9,11},{10,... | collective-permute-start | bytes 1572872 | tf_op jit(solution)/shard_map/ppermute | solution.py:82
  34.7 22.4 %copy-start.21 = (bf16[512,256]{1,0:T(8,128)(2,1)}, bf16[512,256]{1,0:T(8,128)(2,1)S(1)}, u32[]{:S(2)}) copy-start(bf16[512,256]{1,0:T(8,128)(2,1)S(1)} %collective-permute-done.12.refs_3_) | copy-start | bytes 786436
  34.7 12.5 %collective-permute-start.13 = (bf16[512,256]{1,0:T(8,128)(2,1)}, bf16[512,256]{1,0:T(8,128)(2,1)S(1)}, u32[]{:S(2)}, u32[]{:S(2)}) collective-permute-start(bf16[512,256]{1,0:T(8,128)(2,1)} %collective-permute-done.3), channel_id=1, source_target_pairs={{0,16},{1,17},{2,18},{3,19},{4,20},{5,21},{6,22},{7,23},{8,24},{9,... | collective-permute-start | bytes 786440 | tf_op jit(solution)/shard_map/ppermute | solution.py:82
  36.3 9.8 %collective-permute-start.4 = (bf16[512,256]{1,0:T(8,128)(2,1)}, bf16[512,256]{1,0:T(8,128)(2,1)S(1)}, u32[]{:S(2)}, u32[]{:S(2)}) collective-permute-start(bf16[512,256]{1,0:T(8,128)(2,1)} %collective-permute-done.3), channel_id=1, source_target_pairs={{0,8},{1,9},{2,10},{3,11},{4,0},{5,1},{6,2},{7,3},{8,12},{9,13},{1... | collective-permute-start | bytes 786440 | tf_op jit(solution)/shard_map/ppermute | solution.py:82
  39.6 16.7 %collective-permute-start.8 = (bf16[512,256]{1,0:T(8,128)(2,1)}, bf16[512,256]{1,0:T(8,128)(2,1)S(1)}, u32[]{:S(2)}, u32[]{:S(2)}) collective-permute-start(bf16[512,256]{1,0:T(8,128)(2,1)} %collective-permute-done.7.refs_4_), channel_id=1, source_target_pairs={{0,8},{1,9},{2,10},{3,11},{4,0},{5,1},{6,2},{7,3},{8,12},{9,13},{1... | collective-permute-start | bytes 786440 | tf_op jit(solution)/shard_map/ppermute | solution.py:82
  43.1 54.7 %copy-start.3 = (bf16[640,256]{1,0:T(8,128)(2,1)}, bf16[640,256]{1,0:T(8,128)(2,1)S(1)}, u32[]{:S(2)}) copy-start(bf16[640,256]{1,0:T(8,128)(2,1)S(1)} %pad_maximum_fusion.1.refs_0_.refs_8_) | copy-start | bytes 983044
  46.0 9.0 %collective-permute-start.17 = (bf16[512,256]{1,0:T(8,128)(2,1)S(1)}, bf16[512,256]{1,0:T(8,128)(2,1)S(1)}, u32[]{:S(2)}, u32[]{:S(2)}) collective-permute-start(bf16[512,256]{1,0:T(8,128)(2,1)S(1)} %copy-done.28), channel_id=1, source_target_pairs={{0,16},{1,17},{2,18},{3,19},{4,20},{5,21},{6,22},{7,23},{8,24},{9,... | collective-permute-start | bytes 786440 | tf_op jit(solution)/shard_map/ppermute | solution.py:82
  47.2 9.9 %collective-permute-start.5 = (bf16[640,256]{1,0:T(8,128)(2,1)S(1)}, bf16[640,256]{1,0:T(8,128)(2,1)S(1)}, u32[]{:S(2)}, u32[]{:S(2)}) collective-permute-start(bf16[640,256]{1,0:T(8,128)(2,1)S(1)} %pad_maximum_fusion.1.refs_0_.refs_8_), channel_id=1, source_target_pairs={{0,8},{1,9},{2,10},{3,11},{4,0},{5,1},{6,2},{7,3},{8,12},{9,13},{1... | collective-permute-start | bytes 983048 | tf_op jit(solution)/shard_map/ppermute | solution.py:82
  50.5 34.5 %copy-start.10 = (bf16[1024,256]{1,0:T(8,128)(2,1)}, bf16[1024,256]{1,0:T(8,128)(2,1)S(1)}, u32[]{:S(2)}) copy-start(bf16[1024,256]{1,0:T(8,128)(2,1)S(1)} %constant_dynamic-update-slice_fusion.2.refs_4_) | copy-start | bytes 1572868
  50.5 34.4 %copy-start.15 = (bf16[1024,256]{1,0:T(8,128)(2,1)}, bf16[1024,256]{1,0:T(8,128)(2,1)S(1)}, u32[]{:S(2)}) copy-start(bf16[1024,256]{1,0:T(8,128)(2,1)S(1)} %collective-permute-done.22.refs_3_) | copy-start | bytes 1572868
  50.5 18.7 %collective-permute-start.23 = (bf16[1024,256]{1,0:T(8,128)(2,1)S(1)}, bf16[1024,256]{1,0:T(8,128)(2,1)S(1)}, u32[]{:S(2)}, u32[]{:S(2)}) collective-permute-start(bf16[1024,256]{1,0:T(8,128)(2,1)S(1)} %constant_dynamic-update-slice_fusion.2.refs_4_), channel_id=1, source_target_pairs={{0,2},{1,3},{2,0},{3,1},{4,6},{5,7},{6,4},{7,5},{8,10},{9,11},{10,... | collective-permute-start | bytes 1572872 | tf_op jit(solution)/shard_map/ppermute | solution.py:82
  55.1 19.7 %copy-start.23 = (bf16[512,256]{1,0:T(8,128)(2,1)}, bf16[512,256]{1,0:T(8,128)(2,1)S(1)}, u32[]{:S(2)}) copy-start(bf16[512,256]{1,0:T(8,128)(2,1)S(1)} %collective-permute-done.17.refs_9_) | copy-start | bytes 786436
  55.1 8.5 %collective-permute-start.18 = (bf16[512,256]{1,0:T(8,128)(2,1)}, bf16[512,256]{1,0:T(8,128)(2,1)S(1)}, u32[]{:S(2)}, u32[]{:S(2)}) collective-permute-start(bf16[512,256]{1,0:T(8,128)(2,1)} %collective-permute-done.7.refs_4_), channel_id=1, source_target_pairs={{0,16},{1,17},{2,18},{3,19},{4,20},{5,21},{6,22},{7,23},{8,24},{9,... | collective-permute-start | bytes 786440 | tf_op jit(solution)/shard_map/ppermute | solution.py:82
  56.3 20.7 %copy-start.22 = (bf16[512,256]{1,0:T(8,128)(2,1)}, bf16[512,256]{1,0:T(8,128)(2,1)S(1)}, u32[]{:S(2)}) copy-start(bf16[512,256]{1,0:T(8,128)(2,1)S(1)} %collective-permute-done.8.refs_6_) | copy-start | bytes 786436
  56.3 12.8 %collective-permute-start.14 = (bf16[512,256]{1,0:T(8,128)(2,1)S(1)}, bf16[512,256]{1,0:T(8,128)(2,1)S(1)}, u32[]{:S(2)}, u32[]{:S(2)}) collective-permute-start(bf16[512,256]{1,0:T(8,128)(2,1)S(1)} %collective-permute-done.4), channel_id=1, source_target_pairs={{0,16},{1,17},{2,18},{3,19},{4,20},{5,21},{6,22},{7,23},{8,24},{9,... | collective-permute-start | bytes 786440 | tf_op jit(solution)/shard_map/ppermute | solution.py:82
  57.1 40.8 %copy-start.4 = (bf16[640,256]{1,0:T(8,128)(2,1)}, bf16[640,256]{1,0:T(8,128)(2,1)S(1)}, u32[]{:S(2)}) copy-start(bf16[640,256]{1,0:T(8,128)(2,1)S(1)} %collective-permute-done.5.refs_1_.refs_10_) | copy-start | bytes 983044
  57.1 17.7 %collective-permute-start.9 = (bf16[640,256]{1,0:T(8,128)(2,1)S(1)}, bf16[640,256]{1,0:T(8,128)(2,1)S(1)}, u32[]{:S(2)}, u32[]{:S(2)}) collective-permute-start(bf16[640,256]{1,0:T(8,128)(2,1)S(1)} %collective-permute-done.5.refs_1_.refs_10_), channel_id=1, source_target_pairs={{0,8},{1,9},{2,10},{3,11},{4,0},{5,1},{6,2},{7,3},{8,12},{9,13},{1... | collective-permute-start | bytes 983048 | tf_op jit(solution)/shard_map/ppermute | solution.py:82
  63.5 13.5 %copy-start.24 = (bf16[512,256]{1,0:T(8,128)(2,1)}, bf16[512,256]{1,0:T(8,128)(2,1)S(1)}, u32[]{:S(2)}) copy-start(bf16[512,256]{1,0:T(8,128)(2,1)S(1)} %collective-permute-done.18.refs_5_) | copy-start | bytes 786436
  63.5 11.2 %collective-permute-start.19 = (bf16[512,256]{1,0:T(8,128)(2,1)S(1)}, bf16[512,256]{1,0:T(8,128)(2,1)S(1)}, u32[]{:S(2)}, u32[]{:S(2)}) collective-permute-start(bf16[512,256]{1,0:T(8,128)(2,1)S(1)} %collective-permute-done.8.refs_6_), channel_id=1, source_target_pairs={{0,16},{1,17},{2,18},{3,19},{4,20},{5,21},{6,22},{7,23},{8,24},{9,... | collective-permute-start | bytes 786440 | tf_op jit(solution)/shard_map/ppermute | solution.py:82
  69.2 15.8 %copy-start.11 = (bf16[1024,256]{1,0:T(8,128)(2,1)}, bf16[1024,256]{1,0:T(8,128)(2,1)S(1)}, u32[]{:S(2)}) copy-start(bf16[1024,256]{1,0:T(8,128)(2,1)S(1)} %constant_dynamic-update-slice_fusion.4.refs_6_) | copy-start | bytes 1572868
  69.2 15.7 %collective-permute-start.24 = (bf16[1024,256]{1,0:T(8,128)(2,1)S(1)}, bf16[1024,256]{1,0:T(8,128)(2,1)S(1)}, u32[]{:S(2)}, u32[]{:S(2)}) collective-permute-start(bf16[1024,256]{1,0:T(8,128)(2,1)S(1)} %constant_dynamic-update-slice_fusion.4.refs_6_), channel_id=1, source_target_pairs={{0,2},{1,3},{2,0},{3,1},{4,6},{5,7},{6,4},{7,5},{8,10},{9,11},{10,... | collective-permute-start | bytes 1572872 | tf_op jit(solution)/shard_map/ppermute | solution.py:82
  70.8 10.2 %collective-permute-start.15 = (bf16[640,256]{1,0:T(8,128)(2,1)S(1)}, bf16[640,256]{1,0:T(8,128)(2,1)}, u32[]{:S(2)}, u32[]{:S(2)}) collective-permute-start(bf16[640,256]{1,0:T(8,128)(2,1)S(1)} %collective-permute-done.5.refs_1_.refs_10_), channel_id=1, source_target_pairs={{0,16},{1,17},{2,18},{3,19},{4,20},{5,21},{6,22},{7,23},{8,24},{9,... | collective-permute-start | bytes 983048 | tf_op jit(solution)/shard_map/ppermute | solution.py:82
  74.8 23.1 %copy-start.5 = (bf16[640,256]{1,0:T(8,128)(2,1)}, bf16[640,256]{1,0:T(8,128)(2,1)S(1)}, u32[]{:S(2)}) copy-start(bf16[640,256]{1,0:T(8,128)(2,1)S(1)} %collective-permute-done.9.refs_2_.refs_12_) | copy-start | bytes 983044
  74.8 9.4 %collective-permute-start.20 = (bf16[640,256]{1,0:T(8,128)(2,1)S(1)}, bf16[640,256]{1,0:T(8,128)(2,1)}, u32[]{:S(2)}, u32[]{:S(2)}) collective-permute-start(bf16[640,256]{1,0:T(8,128)(2,1)S(1)} %collective-permute-done.9.refs_2_.refs_12_), channel_id=1, source_target_pairs={{0,16},{1,17},{2,18},{3,19},{4,20},{5,21},{6,22},{7,23},{8,24},{9,... | collective-permute-start | bytes 983048 | tf_op jit(solution)/shard_map/ppermute | solution.py:82
  77.0 7.9 %collective-permute-start.10 = (bf16[640,256]{1,0:T(8,128)(2,1)S(1)}, bf16[640,256]{1,0:T(8,128)(2,1)S(1)}, u32[]{:S(2)}, u32[]{:S(2)}) collective-permute-start(bf16[640,256]{1,0:T(8,128)(2,1)S(1)} %collective-permute-done.9.refs_2_.refs_12_), channel_id=1, source_target_pairs={{0,8},{1,9},{2,10},{3,11},{4,0},{5,1},{6,2},{7,3},{8,12},{9,13},{1... | collective-permute-start | bytes 983048 | tf_op jit(solution)/shard_map/ppermute | solution.py:82
  84.9 13.0 %copy-start.6 = (bf16[640,256]{1,0:T(8,128)(2,1)}, bf16[640,256]{1,0:T(8,128)(2,1)S(1)}, u32[]{:S(2)}) copy-start(bf16[640,256]{1,0:T(8,128)(2,1)S(1)} %collective-permute-done.10.refs_3_.refs_14_) | copy-start | bytes 983044
  95.1 11.8 %collective-permute-start.25 = (bf16[1088,512]{1,0:T(8,128)(2,1)}, bf16[1088,512]{1,0:T(8,128)(2,1)S(1)}, u32[]{:S(2)}, u32[]{:S(2)}) collective-permute-start(bf16[1088,512]{1,0:T(8,128)(2,1)} %shard_map.75.refs_2_), channel_id=1, source_target_pairs={{0,1},{1,0},{2,3},{3,2},{4,5},{5,4},{6,7},{7,6},{8,9},{9,8},{10,11... | collective-permute-start | bytes 3342344 | tf_op jit(solution)/shard_map/ppermute | solution.py:82
  96.7 10.6 %collective-permute-start.26 = (bf16[640,256]{1,0:T(8,128)(2,1)S(1)}, bf16[640,256]{1,0:T(8,128)(2,1)S(1)}, u32[]{:S(2)}, u32[]{:S(2)}) collective-permute-start(bf16[640,256]{1,0:T(8,128)(2,1)S(1)} %collective-permute-done.10.refs_3_.refs_14_), channel_id=1, source_target_pairs={{0,16},{1,17},{2,18},{3,19},{4,20},{5,21},{6,22},{7,23},{8,24},{9,... | collective-permute-start | bytes 983048 | tf_op jit(solution)/shard_map/ppermute | solution.py:82
  98.3 7.8 %copy-start.7 = (bf16[4,128,256]{2,1,0:T(8,128)(2,1)}, bf16[4,128,256]{2,1,0:T(8,128)(2,1)S(1)}, u32[]{:S(2)}) copy-start(bf16[4,128,256]{2,1,0:T(8,128)(2,1)S(1)} %shard_map.74.refs_0_) | copy-start | bytes 786436
  98.3 9.0 %collective-permute-start.11 = (bf16[4,128,256]{2,1,0:T(8,128)(2,1)S(1)}, bf16[4,128,256]{2,1,0:T(8,128)(2,1)S(1)}, u32[]{:S(2)}, u32[]{:S(2)}) collective-permute-start(bf16[4,128,256]{2,1,0:T(8,128)(2,1)S(1)} %shard_map.74.refs_0_), channel_id=1, source_target_pairs={{0,1},{1,0},{2,3},{3,2},{4,5},{5,4},{6,7},{7,6},{8,9},{9,8},{10,11... | collective-permute-start | bytes 786440 | tf_op jit(solution)/shard_map/ppermute | solution.py:82
  121.9 3.6 %collective-permute-start.27 = (f32[4,2,128]{2,0,1:T(4,128)S(1)}, f32[4,2,128]{2,0,1:T(4,128)S(1)}, u32[]{:S(2)}, u32[]{:S(2)}) collective-permute-start(f32[4,2,128]{2,0,1:T(4,128)S(1)} %get-tuple-element.101), channel_id=1, source_target_pairs={{0,2},{1,3},{2,0},{3,1},{4,6},{5,7},{6,4},{7,5},{8,10},{9,11},{10,... | collective-permute-start | bytes 12296 | tf_op jit(solution)/shard_map/ppermute | solution.py:82
  124.8 10.3 %collective-permute-start.36 = (f32[64,512]{1,0:T(8,128)S(1)}, f32[64,512]{1,0:T(8,128)S(1)}, u32[]{:S(2)}, u32[]{:S(2)}) collective-permute-start(f32[64,512]{1,0:T(8,128)S(1)} %copy-done.29), channel_id=1, source_target_pairs={{0,1},{1,0},{2,3},{3,2},{4,5},{5,4},{6,7},{7,6},{8,9},{9,8},{10,11... | collective-permute-start | bytes 393224 | tf_op jit(solution)/shard_map/ppermute | solution.py:82
  125.0 8.5 %collective-permute-start.31 = (bf16[4,2,128,128]{3,2,0,1:T(8,128)(2,1)S(1)}, bf16[4,2,128,128]{3,2,0,1:T(8,128)(2,1)S(1)}, u32[]{:S(2)}, u32[]{:S(2)}) collective-permute-start(bf16[4,2,128,128]{3,2,0,1:T(8,128)(2,1)S(1)} %bitcast.170), channel_id=1, source_target_pairs={{0,1},{1,0},{2,3},{3,2},{4,5},{5,4},{6,7},{7,6},{8,9},{9,8},{10,11... | collective-permute-start | bytes 786440 | tf_op jit(solution)/shard_map/ppermute | solution.py:82
  125.6 6.4 %collective-permute-start.28 = (f32[2,128]{1,0:T(2,128)S(1)}, f32[2,128]{1,0:T(2,128)S(1)}, u32[]{:S(2)}, u32[]{:S(2)}) collective-permute-start(f32[2,128]{1,0:T(2,128)S(1)} %bitcast.186), channel_id=1, source_target_pairs={{0,4},{1,5},{2,6},{3,7},{4,8},{5,9},{6,10},{7,11},{8,12},{9,13},{1... | collective-permute-start | bytes 3080 | tf_op jit(solution)/shard_map/ppermute | solution.py:82
  128.0 4.5 %collective-permute-start.29 = (f32[2,128]{1,0:T(2,128)S(1)}, f32[2,128]{1,0:T(2,128)S(1)}, u32[]{:S(2)}, u32[]{:S(2)}) collective-permute-start(f32[2,128]{1,0:T(2,128)S(1)} %bitcast.185), channel_id=1, source_target_pairs={{0,8},{1,9},{2,10},{3,11},{4,12},{5,13},{6,14},{7,15},{8,0},{9,1},... | collective-permute-start | bytes 3080 | tf_op jit(solution)/shard_map/ppermute | solution.py:82
  129.1 4.1 %collective-permute-start.30 = (f32[2,128]{1,0:T(2,128)S(1)}, f32[2,128]{1,0:T(2,128)S(1)}, u32[]{:S(2)}, u32[]{:S(2)}) collective-permute-start(f32[2,128]{1,0:T(2,128)S(1)} %bitcast.184), channel_id=1, source_target_pairs={{0,12},{1,13},{2,14},{3,15},{4,0},{5,1},{6,2},{7,3},{8,4},{9,5},{1... | collective-permute-start | bytes 3080 | tf_op jit(solution)/shard_map/ppermute | solution.py:82
  133.6 5.0 %collective-permute-start.32 = (bf16[4,128,128]{2,1,0:T(8,128)(2,1)S(1)}, bf16[4,128,128]{2,1,0:T(8,128)(2,1)S(1)}, u32[]{:S(2)}, u32[]{:S(2)}) collective-permute-start(bf16[4,128,128]{2,1,0:T(8,128)(2,1)S(1)} %slice_bitcast_fusion), channel_id=1, source_target_pairs={{0,2},{1,3},{2,0},{3,1},{4,6},{5,7},{6,4},{7,5},{8,10},{9,11},{10,... | collective-permute-start | bytes 393224 | tf_op jit(solution)/shard_map/ppermute | solution.py:82
  138.9 6.0 %collective-permute-start.33 = (bf16[128,128]{1,0:T(8,128)(2,1)S(1)}, bf16[128,128]{1,0:T(8,128)(2,1)S(1)}, u32[]{:S(2)}, u32[]{:S(2)}) collective-permute-start(bf16[128,128]{1,0:T(8,128)(2,1)S(1)} %get-tuple-element.87), channel_id=1, source_target_pairs={{0,4},{1,5},{2,6},{3,7},{4,8},{5,9},{6,10},{7,11},{8,12},{9,13},{1... | collective-permute-start | bytes 98312 | tf_op jit(solution)/shard_map/ppermute | solution.py:82
  139.7 5.9 %collective-permute-start.34 = (bf16[128,128]{1,0:T(8,128)(2,1)S(1)}, bf16[128,128]{1,0:T(8,128)(2,1)S(1)}, u32[]{:S(2)}, u32[]{:S(2)}) collective-permute-start(bf16[128,128]{1,0:T(8,128)(2,1)S(1)} %get-tuple-element.89), channel_id=1, source_target_pairs={{0,8},{1,9},{2,10},{3,11},{4,12},{5,13},{6,14},{7,15},{8,0},{9,1},... | collective-permute-start | bytes 98312 | tf_op jit(solution)/shard_map/ppermute | solution.py:82
  143.6 3.9 %collective-permute-start.35 = (bf16[128,128]{1,0:T(8,128)(2,1)S(1)}, bf16[128,128]{1,0:T(8,128)(2,1)S(1)}, u32[]{:S(2)}, u32[]{:S(2)}) collective-permute-start(bf16[128,128]{1,0:T(8,128)(2,1)S(1)} %get-tuple-element.88), channel_id=1, source_target_pairs={{0,12},{1,13},{2,14},{3,15},{4,0},{5,1},{6,2},{7,3},{8,4},{9,5},{1... | collective-permute-start | bytes 98312 | tf_op jit(solution)/shard_map/ppermute | solution.py:82
  151.5 2.0 %collective-permute-start.37 = (bf16[64,4096]{1,0:T(8,128)(2,1)S(1)}, bf16[64,4096]{1,0:T(8,128)(2,1)S(1)}, u32[]{:S(2)}, u32[]{:S(2)}) collective-permute-start(bf16[64,4096]{1,0:T(8,128)(2,1)S(1)} %slice.230), channel_id=1, source_target_pairs={{0,1},{1,0},{2,3},{3,2},{4,5},{5,4},{6,7},{7,6},{8,9},{9,8},{10,11... | collective-permute-start | bytes 1572872 | tf_op jit(solution)/shard_map/ppermute | solution.py:82
  153.6 8.4 %collective-permute-start.38 = (bf16[64,2048]{1,0:T(8,128)(2,1)S(1)}, bf16[64,2048]{1,0:T(8,128)(2,1)S(1)}, u32[]{:S(2)}, u32[]{:S(2)}) collective-permute-start(bf16[64,2048]{1,0:T(8,128)(2,1)S(1)} %slice.232), channel_id=1, source_target_pairs={{0,2},{1,3},{2,0},{3,1},{4,6},{5,7},{6,4},{7,5},{8,10},{9,11},{10,... | collective-permute-start | bytes 786440 | tf_op jit(solution)/shard_map/ppermute | solution.py:82
  162.1 6.6 %collective-permute-start.39 = (bf16[64,512]{1,0:T(8,128)(2,1)S(1)}, bf16[64,512]{1,0:T(8,128)(2,1)S(1)}, u32[]{:S(2)}, u32[]{:S(2)}) collective-permute-start(bf16[64,512]{1,0:T(8,128)(2,1)S(1)} %get-tuple-element.84), channel_id=1, source_target_pairs={{0,4},{1,5},{2,6},{3,7},{4,8},{5,9},{6,10},{7,11},{8,12},{9,13},{1... | collective-permute-start | bytes 196616 | tf_op jit(solution)/shard_map/ppermute | solution.py:82
  162.2 7.8 %collective-permute-start.40 = (bf16[64,512]{1,0:T(8,128)(2,1)S(1)}, bf16[64,512]{1,0:T(8,128)(2,1)S(1)}, u32[]{:S(2)}, u32[]{:S(2)}) collective-permute-start(bf16[64,512]{1,0:T(8,128)(2,1)S(1)} %get-tuple-element.86), channel_id=1, source_target_pairs={{0,8},{1,9},{2,10},{3,11},{4,12},{5,13},{6,14},{7,15},{8,0},{9,1},... | collective-permute-start | bytes 196616 | tf_op jit(solution)/shard_map/ppermute | solution.py:82
  164.9 5.1 %collective-permute-start.41 = (bf16[64,512]{1,0:T(8,128)(2,1)S(1)}, bf16[64,512]{1,0:T(8,128)(2,1)S(1)}, u32[]{:S(2)}, u32[]{:S(2)}) collective-permute-start(bf16[64,512]{1,0:T(8,128)(2,1)S(1)} %get-tuple-element.85), channel_id=1, source_target_pairs={{0,12},{1,13},{2,14},{3,15},{4,0},{5,1},{6,2},{7,3},{8,4},{9,5},{1... | collective-permute-start | bytes 196616 | tf_op jit(solution)/shard_map/ppermute | solution.py:82
  (9 other events, 19.9 us)

commit v11 on v10

--- a/solution.py
+++ b/solution.py
@@ -35,32 +35,6 @@
         ],
         axis=-1,
     )
-
-
-def finish_heads(prefix_top, prefix_total, prefix_sum, queries, new_keys, new_values):
-    score_scale = queries.shape[-1] ** (-0.5)
-    query_wide = queries.astype(jnp.float32)
-    key_wide = new_keys.astype(jnp.float32)
-    value_wide = new_values.astype(jnp.float32)
-    own_score = jnp.sum(query_wide * key_wide, axis=-1) * score_scale
-    back_score = jnp.sum(query_wide[1] * key_wide[0], axis=-1) * score_scale
-    first_high = jnp.maximum(prefix_top[0], own_score[0])
-    first_old = jnp.exp(prefix_top[0] - first_high)
-    first_own = jnp.exp(own_score[0] - first_high)
-    first_out = (first_old[..., None] * prefix_sum[0] + first_own[..., None] * value_wide[0]) / (
-        first_old * prefix_total[0] + first_own
-    )[..., None]
-    second_high = jnp.maximum(jnp.maximum(prefix_top[1], own_score[1]), back_score)
-    second_old = jnp.exp(prefix_top[1] - second_high)
-    second_back = jnp.exp(back_score - second_high)
-    second_own = jnp.exp(own_score[1] - second_high)
-    second_num = (
-        second_old[..., None] * prefix_sum[1]
-        + second_back[..., None] * value_wide[0]
-        + second_own[..., None] * value_wide[1]
-    )
-    second_out = second_num / (second_old * prefix_total[1] + second_back + second_own)[..., None]
-    return jnp.stack([first_out, second_out]).astype(jnp.bfloat16)
 
 
 def ring_order(deep):
@@ -253,6 +227,77 @@
     )(blocks, prompt, got, steps, *held.arrays)
 
 
+NOTES = 16
+
+
+def thirds(value):
+    parts = []
+    for _ in range(3):
+        parts.append(value.astype(jnp.bfloat16))
+        value = value - parts[-1].astype(jnp.float32)
+    return parts
+
+
+def note_rows(top, total):
+    parts = [part.astype(jnp.float32) for part in thirds(top) + thirds(total)]
+    rows = jnp.concatenate(parts + [jnp.zeros((NOTES - 6, top.shape[1]), jnp.float32)], axis=0)
+    return rows.astype(jnp.bfloat16)
+
+
+def read_notes(rows):
+    rows = rows.astype(jnp.float32)
+    return rows[0:1] + rows[1:2] + rows[2:3], rows[3:4] + rows[4:5] + rows[5:6]
+
+
+def small_call(body, out_shapes, scalars, arrays):
+    whole = pl.BlockSpec(memory_space=pltpu.VMEM)
+    return pl.pallas_call(
+        body,
+        in_specs=[pl.BlockSpec(memory_space=pltpu.SMEM)] * len(scalars) + [whole] * len(arrays),
+        out_specs=[whole] * len(out_shapes),
+        out_shape=[jax.ShapeDtypeStruct(shape, jnp.bfloat16) for shape in out_shapes],
+        compiler_params=pltpu.CompilerParams(vmem_limit_bytes=12 * MIB),
+        cost_estimate=LIGHT,
+    )(*scalars, *arrays)
+
+
+def merge_cores(own, other):
+    deep, _, _, height, lanes = own.shape
+
+    def body(own_ref, other_ref, near_ref, far_ref):
+        for z in range(deep):
+            for y, out_ref in enumerate((near_ref, far_ref)):
+                both = own_ref[z, 0, y, :HEAD_DIM, :].astype(jnp.float32) + other_ref[
+                    z, y, :HEAD_DIM, :
+                ].astype(jnp.float32)
+                out_ref[z, :HEAD_DIM, :] = both.astype(jnp.bfloat16)
+                out_ref[z, HEAD_DIM:, :] = own_ref[z, 0, y, HEAD_DIM:, :]
+
+    return small_call(body, [(deep, height, lanes)] * 2, [], [own, other])
+
+
+def merge_chips(own_place, near, far):
+    deep, height, lanes = near.shape
+
+    def body(place_ref, near_ref, far_ref, *out_refs):
+        for k, out_ref in enumerate(out_refs):
+            z = lax.rem(place_ref[0] + k, deep)
+            first, second = near_ref[z], far_ref[z]
+            first_top, first_total = read_notes(first[HEAD_DIM:, :])
+            second_top, second_total = read_notes(second[HEAD_DIM:, :])
+            top = jnp.maximum(first_top, second_top)
+            first_factor, second_factor = jnp.exp(first_top - top), jnp.exp(second_top - top)
+            out_ref[:HEAD_DIM, :] = (
+                first[:HEAD_DIM, :].astype(jnp.float32) * first_factor
+                + second[:HEAD_DIM, :].astype(jnp.float32) * second_factor
+            ).astype(jnp.bfloat16)
+            out_ref[HEAD_DIM:, :] = note_rows(
+                top, first_total * first_factor + second_total * second_factor
+            )
+
+    return small_call(body, [(height, lanes)] * deep, [own_place], [near, far])
+
+
 def attend(
     places, turns, queries, own, other, cosine, sine, masks, prompt, got, steps, blocks, width,
     pieces, early,
@@ -261,6 +306,7 @@
     deep, packed, lanes = queries[0].shape
     share = deep // kv_heads
     count = 2 * share * packed * lanes // HEAD_DIM
+    owners = count // HEAD_DIM
     tokens = cosine.shape[0]
     half = tokens // 2
     held = Blocks(prompt, steps, width, pieces)
@@ -273,8 +319,8 @@
         prompt_ref, got_ref, step_ref, early_ref = refs[len(inputs) : len(inputs) + 4]
         rest = refs[len(inputs) + 4 :]
         weight_refs, rest = rest[: len(held.arrays)], rest[len(held.arrays) :]
-        out_ref, top_ref, total_ref, step_out_ref = rest[:4]
-        early_held, weight_held, value_held, early_sem, *scratch = rest[4:]
+        out_ref, step_out_ref = rest[:2]
+        early_held, weight_held, value_held, early_sem, *scratch = rest[2:]
         left, weight_rows, _ = scratch
         sources = (prompt_ref, got_ref, step_ref)
         groups = [
@@ -320,8 +366,10 @@
                 scores = jnp.where(mask_refs[0][...] == mask_refs[1][...], scores, -1e30)
             top = jnp.max(scores, axis=0, keepdims=True)
             weights = jnp.exp(scores - top)
-            top_ref[j] = top
-            total_ref[j] = jnp.sum(weights, axis=0, keepdims=True)
+            total = jnp.sum(weights, axis=0, keepdims=True)
+            for i in range(owners):
+                lane = slice(i * HEAD_DIM, (i + 1) * HEAD_DIM)
+                out_ref[j, i, HEAD_DIM:, :] = note_rows(top[:, lane], total[:, lane])
             weight_held[j] = weights.astype(jnp.bfloat16)
             return 0
 
@@ -343,24 +391,23 @@
                 (((0,), (0,)), ((), ())),
                 preferred_element_type=jnp.float32,
             )
-            out_ref[j] = summed.T.astype(jnp.bfloat16)
+            for i in range(owners):
+                lane = slice(i * HEAD_DIM, (i + 1) * HEAD_DIM)
+                out_ref[j, i, :HEAD_DIM, :] = summed[:, lane].astype(jnp.bfloat16)
             return 0
 
         lax.fori_loop(0, kv_heads, one_sum, 0)
 
     anywhere = pl.BlockSpec(memory_space=pl.ANY)
     whole = pl.BlockSpec(memory_space=pltpu.VMEM)
-    row = jax.ShapeDtypeStruct((kv_heads, 1, count), jnp.float32)
     return pl.pallas_call(
         body,
         in_specs=[pl.BlockSpec(memory_space=pltpu.SMEM)] * 3
         + [whole] * len(inputs)
         + [anywhere] * (4 + len(held.arrays)),
-        out_specs=[whole] * 4,
+        out_specs=[whole] * 2,
         out_shape=[
-            jax.ShapeDtypeStruct((kv_heads, count, HEAD_DIM), jnp.bfloat16),
-            row,
-            row,
+            jax.ShapeDtypeStruct((kv_heads, owners, HEAD_DIM + NOTES, HEAD_DIM), jnp.bfloat16),
             jax.ShapeDtypeStruct((held.step_count, held.columns), jnp.float32),
         ],
         scratch_shapes=[
@@ -375,23 +422,61 @@
     )(places, turns, blocks, *inputs, prompt, got, steps, early, *held.arrays)
 
 
-def out_project(blocks, heads, weight, width):
-    def body(block_ref, head_ref, weight_ref, out_ref):
+def out_project(blocks, parts, queries, new_keys, new_values, weight, width):
+    count = len(parts)
+    steps = queries.shape[0]
+    samples = steps // 2
+
+    def body(block_ref, *refs):
+        part_refs = refs[:count]
+        query_ref, key_ref, value_ref, weight_ref, out_ref = refs[count:]
+        notes = [read_notes(ref[HEAD_DIM:, :]) for ref in part_refs]
+        top = notes[0][0]
+        for other, _ in notes[1:]:
+            top = jnp.maximum(top, other)
+        sums = total = 0.0
+        for ref, (part_top, part_total) in zip(part_refs, notes):
+            factor = jnp.exp(part_top - top)
+            sums = sums + ref[:HEAD_DIM, :].astype(jnp.float32) * factor
+            total = total + part_total * factor
+        sums = sums.T
+        both = jnp.concatenate([top, total, jnp.zeros((6, HEAD_DIM), jnp.float32)], axis=0).T
+        keys, values = key_ref[...], value_ref[...]
+        heads = []
+        for h in range(queries.shape[1] // HEAD_DIM):
+            query = query_ref[:, h * HEAD_DIM : (h + 1) * HEAD_DIM].astype(jnp.float32)
+            own_score = jnp.sum(query * keys, axis=1, keepdims=True) * (HEAD_DIM**-0.5)
+            back_score = jnp.sum(
+                query[samples:] * keys[:samples], axis=1, keepdims=True
+            ) * (HEAD_DIM**-0.5)
+            ends = []
+            for step in (0, 1):
+                place = slice((2 * h + step) * samples, (2 * h + step + 1) * samples)
+                here = slice(step * samples, (step + 1) * samples)
+                old_top, old_total = both[place, 0:1], both[place, 1:2]
+                scores = [(own_score[here], values[here])]
+                if step:
+                    scores.append((back_score, values[:samples]))
+                high = old_top
+                for score, _ in scores:
+                    high = jnp.maximum(high, score)
+                old = jnp.exp(old_top - high)
+                numerator, denominator = old * sums[place], old * old_total
+                for score, value in scores:
+                    new = jnp.exp(score - high)
+                    numerator, denominator = numerator + new * value, denominator + new
+                ends.append(numerator / denominator)
+            heads.append(jnp.concatenate(ends, axis=0).astype(jnp.bfloat16))
+        heads = jnp.concatenate(heads, axis=1)
         for i in range(blocks.shape[0]):
             start = pl.multiple_of(block_ref[i] * width, width)
             out_ref[:, i * width : (i + 1) * width] = jnp.dot(
-                head_ref[...], weight_ref[:, pl.ds(start, width)], preferred_element_type=jnp.float32
+                heads, weight_ref[:, pl.ds(start, width)], preferred_element_type=jnp.float32
             ).astype(jnp.bfloat16)
 
-    whole = pl.BlockSpec(memory_space=pltpu.VMEM)
-    return pl.pallas_call(
-        body,
-        in_specs=[pl.BlockSpec(memory_space=pltpu.SMEM), whole, whole],
-        out_specs=whole,
-        out_shape=jax.ShapeDtypeStruct((heads.shape[0], weight.shape[1]), jnp.bfloat16),
-        compiler_params=pltpu.CompilerParams(vmem_limit_bytes=10 * MIB),
-        cost_estimate=LIGHT,
-    )(blocks, heads, weight)
+    return small_call(
+        body, [(steps, weight.shape[1])], [blocks], [*parts, queries, new_keys, new_values, weight]
+    )[0]
 
 
 def on_device(
@@ -459,7 +544,6 @@
         jnp.split(queries, half // queries.shape[1], axis=0), axis=1
     )
     packed = packed_queries.shape[0]
-    queries = queries.reshape(2, samples, heads_here, HEAD_DIM)
 
     own_pages = jnp.concatenate(
         [
@@ -531,12 +615,11 @@
             prompt_states, got, wide_states, taken, width, [pieces[i] for i in which], kind
         )
 
-    key_sum = project_blocks(
-        key_pieces, range(2 * deep), (theirs[deep - 1], [theirs_x[k] for k in range(1, deep - 1)]), jnp.bfloat16
-    )
     early = [*range(0, 2 * deep, 2), 1]
     late = [i for i in range(2 * deep) if i not in early]
-    value_early = project_blocks(value_pieces, early, key_sum, jnp.float32)
+    value_early = project_blocks(value_pieces, early, (theirs_x[1], theirs[deep - 2]), jnp.float32)
+    awaited = (value_early, theirs[deep - 1], [theirs_x[k] for k in range(1, deep - 1)])
+    key_sum = project_blocks(key_pieces, range(2 * deep), awaited, jnp.bfloat16)
     key_back = in_chip(key_sum)
 
     def own_head(sums):
@@ -544,60 +627,25 @@
         return sums.reshape(2, samples, HEAD_DIM).astype(jnp.float32)
 
     new_keys = own_head(key_sum[chip_rows:]) + own_head(key_back[chip_rows:])
-    new_keys = turn(new_keys, step_tables).astype(jnp.bfloat16)
+    new_keys = turn(new_keys, step_tables).astype(jnp.bfloat16).astype(jnp.float32)
+    new_keys = new_keys.reshape(steps, HEAD_DIM)
     masks = []
     if prompts > 1:
         token_prompt = jnp.repeat(slots // PROMPT_PAGES, PAGE)
         row_prompt = jnp.tile(sample_order // group_size, devices // KV_HEADS * rows // samples)
         masks = [token_prompt[:, None], row_prompt[None, :]]
-    partial, top, total, step_values = attend(
+    partial, step_values = attend(
         kv_places, query_turns, ring_queries, key_sum, key_back, cosine, sine_part, masks,
         prompt_states, got, wide_states, jnp.stack([own_blocks[i] for i in late]), width,
         [value_pieces[i] for i in late], value_early,
     )
     new_values = own_head(step_values) + own_head(in_chip(step_values))
-    new_values = new_values.astype(jnp.bfloat16)
-
-    def narrow(value):
-        return value.astype(jnp.bfloat16)
-
-    def wide(value):
-        return value.astype(jnp.float32)
-
-    def to_z(value, k):
-        return lax.dynamic_index_in_dim(value, (own_a + k) % deep, 0, False)
-
-    stats = jnp.stack([top.reshape(by_owner)[:, 0], total.reshape(by_owner)[:, 0]], axis=2)
-    partial = partial.reshape(by_owner + (HEAD_DIM,))
-    near = stats[:, 0]
-    far = along_y(stats[:, 1])
-    top = jnp.maximum(near[:, 0], far[:, 0])
-    near_factor, far_factor = jnp.exp(near[:, 0] - top), jnp.exp(far[:, 0] - top)
-    stats = jnp.stack([top, near[:, 1] * near_factor + far[:, 1] * far_factor], axis=1)
-    stats = jnp.stack([to_z(stats, 0)] + [along_z(to_z(stats, k), k) for k in range(1, deep)])
-    prefix_top = jnp.max(stats[:, 0], axis=0)
-    factors = jnp.exp(stats[:, 0] - prefix_top)
-    prefix_total = jnp.sum(stats[:, 1] * factors, axis=0)
-
-    partial = narrow(wide(partial[:, 0]) + wide(in_chip(partial[:, 1])))
-    partial = narrow(
-        wide(partial[:, 0]) * near_factor[..., None]
-        + wide(along_y(partial[:, 1])) * far_factor[..., None]
-    )
-    prefix_sum = wide(to_z(partial, 0)) * factors[0][:, None]
-    for k in range(1, deep):
-        prefix_sum = prefix_sum + wide(along_z(to_z(partial, k), k)) * factors[k][:, None]
-
-    by_head = (heads_here, 2, samples)
-    head_out = finish_heads(
-        prefix_top.reshape(by_head).swapaxes(0, 1),
-        prefix_total.reshape(by_head).swapaxes(0, 1),
-        prefix_sum.reshape(by_head + (HEAD_DIM,)).swapaxes(0, 1),
-        queries.transpose(0, 2, 1, 3),
-        new_keys[:, None],
-        new_values[:, None],
-    )
-    flat_heads = head_out.transpose(0, 2, 1, 3).reshape(steps, heads_here * HEAD_DIM)
+    new_values = new_values.astype(jnp.bfloat16).astype(jnp.float32).reshape(steps, HEAD_DIM)
+
+    partial = partial.reshape(by_owner[:3] + partial.shape[2:])
+    near, far = merge_cores(partial, in_chip(partial[:, 1]))
+    merged = merge_chips(own_a[None], near, along_y(far))
+    parts = [merged[0]] + [along_z(merged[k], k) for k in range(1, deep)]
 
     out_width = out_weight.shape[1] // devices
     out_blocks = jnp.stack(
@@ -608,7 +656,14 @@
             for k in range(deep)
         ]
     )
-    terms = out_project(out_blocks, flat_heads, out_weight, out_width)
+    terms = out_project(out_blocks, parts, queries, new_keys, new_values, out_weight, out_width)
+
+    def narrow(value):
+        return value.astype(jnp.bfloat16)
+
+    def wide(value):
+        return value.astype(jnp.float32)
+
     for move in (in_chip, along_y):
         share = terms.shape[1] // 2
         terms = narrow(wide(terms[:, :share]) + wide(move(terms[:, share:])))

time: 171 us -> 161 us (0.942)
  starting transfers between devices: 67.6 us -> 61.8 us
  local copies, waits for them, and re-layouts: 14.1 us -> 10.1 us
    ppermute x42 -> x38, starting transfers between devices: 67.6 us -> 61.8 us  [move(): return lax.ppermute(value, ('groups', 'sample'), pairs)]
    unnamed x69 -> x63, local copies, waits for them, and re-layouts: 8.72 us -> 5.79 us
    slice x9 -> x0, local copies, waits for them, and re-layouts: 2.64 us -> none  [the longest x1 1.06 us: on_device(): partial = narrow(wide(partial[:, 0]) + wide(in_chip(partial[:, 1])))]
    ppermute x42 -> x38, waiting for transfers between devices: 46.5 us -> 46.1 us  [move(): return lax.ppermute(value, ('groups', 'sample'), pairs)]
  transfers between devices with their start and end apart: 42 -> 38, of which waited for: 20 -> 20; matrix products, arithmetic and copies ran while one was open for 8% -> 8% of each run, Pallas kernels for 6% -> 6%
where the time goes in v11:
time: 161 us
  starting transfers between devices  61.8 us (38%)
  waiting for transfers between devices  46.1 us (29%)
  Pallas kernels  32.8 us (20%)
  local copies, waits for them, and re-layouts  10.1 us (6%)
  other arithmetic  9.19 us (6%)
    ppermute x38, starting transfers between devices, move(): return lax.ppermute(value, ('groups', 'sample'), pairs)  61.8 us
    ppermute x38, waiting for transfers between devices, move(): return lax.ppermute(value, ('groups', 'sample'), pairs)  46.1 us
    pallas_call x2, Pallas kernels, project(): pl.pallas_call(body, in_specs=[pl.BlockSpec(memory_space=pltpu.SMEM)] + [...  16.8 us
    pallas_call x1, Pallas kernels, attend(): pl.pallas_call(body, in_specs=[pl.BlockSpec(memory_space=pltpu.SMEM)] * 3...  11.8 us
    unnamed x63, local copies, waits for them, and re-layouts  5.79 us
  transfers between devices with their start and end apart: 38, of which 20 were waited for; matrix products, arithmetic and copies ran while one was open for 8% of the time, Pallas kernels for 6%

profile of v11, /device:TPU:0, one launch (start us, length us, event | category | flops | bytes accessed | tf_op | source)
XLA Modules:
  0.0 160.5 jit_solution(10808892785220477947)
XLA Ops:
  0.5 1.9 %broadcast_select_fusion = (bf16[512,256]{1,0:T(8,128)(2,1)}, bf16[512,256]{1,0:T(8,128)(2,1)S(1)}) fusion(pred[]{:T(512)S(6)} %eq.45, bf16[512,512]{1,0:T(8,128)(2,1)} %param.12), kind=kLoop, calls=%fused_computation.7 | loop fusion | flops 262144 | bytes 1048577 | tf_op jit(solution)/shard_map/jit(_where)/select_n | solution.py:531
  2.3 2.6 %collective-permute-start = (bf16[512,256]{1,0:T(8,128)(2,1)S(1)}, bf16[512,256]{1,0:T(8,128)(2,1)S(1)}, u32[]{:S(2)}, u32[]{:S(2)}) collective-permute-start(bf16[512,256]{1,0:T(8,128)(2,1)S(1)} %get-tuple-element.76.refs_0_), channel_id=1, source_target_pairs={{0,2},{1,3},{2,0},{3,1},{4,6},{5,7},{6,4},{7,5},{8,10},{9,11},{10,... | collective-permute-start | bytes 786440 | tf_op jit(solution)/shard_map/ppermute | solution.py:56
  4.9 2.6 %collective-permute-start.6 = (bf16[512,256]{1,0:T(8,128)(2,1)S(1)}, bf16[512,256]{1,0:T(8,128)(2,1)}, u32[]{:S(2)}, u32[]{:S(2)}) collective-permute-start(bf16[512,256]{1,0:T(8,128)(2,1)S(1)} %get-tuple-element.76.refs_0_), channel_id=1, source_target_pairs={{0,8},{1,9},{2,10},{3,11},{4,0},{5,1},{6,2},{7,3},{8,12},{9,13},{1... | collective-permute-start | bytes 786440 | tf_op jit(solution)/shard_map/ppermute | solution.py:56
  7.6 1.6 %collective-permute-start.1 = (bf16[512,256]{1,0:T(8,128)(2,1)S(1)}, bf16[512,256]{1,0:T(8,128)(2,1)}, u32[]{:S(2)}, u32[]{:S(2)}) collective-permute-start(bf16[512,256]{1,0:T(8,128)(2,1)S(1)} %get-tuple-element.77), channel_id=1, source_target_pairs={{0,8},{1,9},{2,10},{3,11},{4,0},{5,1},{6,2},{7,3},{8,12},{9,13},{1... | collective-permute-start | bytes 786440 | tf_op jit(solution)/shard_map/ppermute | solution.py:56
  9.7 2.2 %copy-done.1 = bf16[8192,256]{1,0:T(8,128)(2,1)S(1)} copy-done((bf16[8192,256]{1,0:T(8,128)(2,1)S(1)}, bf16[8192,256]{1,0:T(8,128)(2,1)}, u32[]{:S(2)}) %copy-start.1) | copy-done | bytes 4194328
  11.9 2.0 %shard_map.73.refs_4_ = bf16[64,256]{1,0:T(8,128)(2,1)S(1)} custom-call(bf16[64,8192]{1,0:T(8,128)(2,1)S(1)} %bitcast.50, bf16[8192,256]{1,0:T(8,128)(2,1)S(1)} %copy-done.1, f32[64,128]{1,0:T(8,128)S(1)} %bitcast.53, f32[64,128]{1,0:T(8,128)S(1)} %bitcast.54), custom_call_target="tpu_custom_call" | custom-call | flops 1 | bytes 1 | tf_op jit(solution)/shard_map/pallas_call | solution.py:106
  14.0 5.1 %collective-permute-done.1 = bf16[512,256]{1,0:T(8,128)(2,1)} collective-permute-done((bf16[512,256]{1,0:T(8,128)(2,1)S(1)}, bf16[512,256]{1,0:T(8,128)(2,1)}, u32[]{:S(2)}, u32[]{:S(2)}) %collective-permute-start.1) | collective-permute-done | bytes 262176 | tf_op jit(solution)/shard_map/ppermute | solution.py:56
  19.6 1.5 collective-permute-start.17
  21.1 3.0 %multiply_sine_fusion = (f32[1024,64]{1,0:T(8,128)}, f32[1024,64]{1,0:T(8,128)}) fusion(f32[64]{0:T(128)S(1)} %multiply_power_fusion, f32[1024]{0:T(1024)S(1)} %convert_bitcast_fusion), kind=kLoop, calls=%fused_computation.1 | loop fusion | flops 65536 | bytes 528640 | tf_op jit(solution)/shard_map/sin | solution.py:23
  24.1 3.5 %collective-permute-start.3 = (bf16[512,256]{1,0:T(8,128)(2,1)}, bf16[512,256]{1,0:T(8,128)(2,1)}, u32[]{:S(2)}, u32[]{:S(2)}) collective-permute-start(bf16[512,256]{1,0:T(8,128)(2,1)} %collective-permute-done.1), channel_id=1, source_target_pairs={{0,8},{1,9},{2,10},{3,11},{4,0},{5,1},{6,2},{7,3},{8,12},{9,13},{1... | collective-permute-start | bytes 786440 | tf_op jit(solution)/shard_map/ppermute | solution.py:56
  28.2 1.0 constant_dynamic-update-slice_fusion.1
  29.2 2.3 %collective-permute-start.7 = (bf16[512,256]{1,0:T(8,128)(2,1)}, bf16[512,256]{1,0:T(8,128)(2,1)}, u32[]{:S(2)}, u32[]{:S(2)}) collective-permute-start(bf16[512,256]{1,0:T(8,128)(2,1)} %collective-permute-done.6.refs_2_), channel_id=1, source_target_pairs={{0,8},{1,9},{2,10},{3,11},{4,0},{5,1},{6,2},{7,3},{8,12},{9,13},{1... | collective-permute-start | bytes 786440 | tf_op jit(solution)/shard_map/ppermute | solution.py:56
  31.6 1.3 collective-permute-done.2.refs_1_
  32.9 0.7 collective-permute-start.22
  34.7 3.4 %collective-permute-start.4 = (bf16[512,256]{1,0:T(8,128)(2,1)}, bf16[512,256]{1,0:T(8,128)(2,1)S(1)}, u32[]{:S(2)}, u32[]{:S(2)}) collective-permute-start(bf16[512,256]{1,0:T(8,128)(2,1)} %collective-permute-done.3), channel_id=1, source_target_pairs={{0,8},{1,9},{2,10},{3,11},{4,0},{5,1},{6,2},{7,3},{8,12},{9,13},{1... | collective-permute-start | bytes 786440 | tf_op jit(solution)/shard_map/ppermute | solution.py:56
  38.1 0.9 collective-permute-start.13
  39.9 3.4 %collective-permute-start.8 = (bf16[512,256]{1,0:T(8,128)(2,1)}, bf16[512,256]{1,0:T(8,128)(2,1)S(1)}, u32[]{:S(2)}, u32[]{:S(2)}) collective-permute-start(bf16[512,256]{1,0:T(8,128)(2,1)} %collective-permute-done.7.refs_4_), channel_id=1, source_target_pairs={{0,8},{1,9},{2,10},{3,11},{4,0},{5,1},{6,2},{7,3},{8,12},{9,13},{1... | collective-permute-start | bytes 786440 | tf_op jit(solution)/shard_map/ppermute | solution.py:56
  43.3 1.0 constant_dynamic-update-slice_fusion.3
  44.3 1.2 collective-permute-done.4
  46.1 3.3 %collective-permute-start.5 = (bf16[640,256]{1,0:T(8,128)(2,1)S(1)}, bf16[640,256]{1,0:T(8,128)(2,1)S(1)}, u32[]{:S(2)}, u32[]{:S(2)}) collective-permute-start(bf16[640,256]{1,0:T(8,128)(2,1)S(1)} %pad_maximum_fusion.1.refs_0_.refs_8_), channel_id=1, source_target_pairs={{0,8},{1,9},{2,10},{3,11},{4,0},{5,1},{6,2},{7,3},{8,12},{9,13},{1... | collective-permute-start | bytes 983048 | tf_op jit(solution)/shard_map/ppermute | solution.py:56
  49.4 1.6 collective-permute-start.23
  51.0 2.4 %collective-permute-done.18.refs_9_ = bf16[512,256]{1,0:T(8,128)(2,1)S(1)} collective-permute-done((bf16[512,256]{1,0:T(8,128)(2,1)S(1)}, bf16[512,256]{1,0:T(8,128)(2,1)S(1)}, u32[]{:S(2)}, u32[]{:S(2)}) %collective-permute-start.18) | collective-permute-done | bytes 262176 | tf_op jit(solution)/shard_map/ppermute | solution.py:56
  53.5 1.9 %collective-permute-start.14 = (bf16[512,256]{1,0:T(8,128)(2,1)S(1)}, bf16[512,256]{1,0:T(8,128)(2,1)S(1)}, u32[]{:S(2)}, u32[]{:S(2)}) collective-permute-start(bf16[512,256]{1,0:T(8,128)(2,1)S(1)} %collective-permute-done.4), channel_id=1, source_target_pairs={{0,16},{1,17},{2,18},{3,19},{4,20},{5,21},{6,22},{7,23},{8,24},{9,... | collective-permute-start | bytes 786440 | tf_op jit(solution)/shard_map/ppermute | solution.py:56
  55.4 0.8 collective-permute-done.5.refs_1_.refs_10_
  56.2 3.4 %collective-permute-start.9 = (bf16[640,256]{1,0:T(8,128)(2,1)S(1)}, bf16[640,256]{1,0:T(8,128)(2,1)S(1)}, u32[]{:S(2)}, u32[]{:S(2)}) collective-permute-start(bf16[640,256]{1,0:T(8,128)(2,1)S(1)} %collective-permute-done.5.refs_1_.refs_10_), channel_id=1, source_target_pairs={{0,8},{1,9},{2,10},{3,11},{4,0},{5,1},{6,2},{7,3},{8,12},{9,13},{1... | collective-permute-start | bytes 983048 | tf_op jit(solution)/shard_map/ppermute | solution.py:56
  59.7 0.7 collective-permute-done.19.refs_5_
  60.3 0.7 collective-permute-start.20
  61.0 4.9 %collective-permute-done.14 = bf16[512,256]{1,0:T(8,128)(2,1)S(1)} collective-permute-done((bf16[512,256]{1,0:T(8,128)(2,1)S(1)}, bf16[512,256]{1,0:T(8,128)(2,1)S(1)}, u32[]{:S(2)}, u32[]{:S(2)}) %collective-permute-start.14) | collective-permute-done | bytes 262176 | tf_op jit(solution)/shard_map/ppermute | solution.py:56
  66.0 1.6 collective-permute-start.24
  67.5 0.8 collective-permute-start.15
  68.3 5.7 %collective-permute-start.10 = (bf16[640,256]{1,0:T(8,128)(2,1)S(1)}, bf16[640,256]{1,0:T(8,128)(2,1)S(1)}, u32[]{:S(2)}, u32[]{:S(2)}) collective-permute-start(bf16[640,256]{1,0:T(8,128)(2,1)S(1)} %collective-permute-done.9.refs_2_.refs_12_), channel_id=1, source_target_pairs={{0,8},{1,9},{2,10},{3,11},{4,0},{5,1},{6,2},{7,3},{8,12},{9,13},{1... | collective-permute-start | bytes 983048 | tf_op jit(solution)/shard_map/ppermute | solution.py:56
  74.0 1.6 %collective-permute-start.21 = (bf16[640,256]{1,0:T(8,128)(2,1)S(1)}, bf16[640,256]{1,0:T(8,128)(2,1)}, u32[]{:S(2)}, u32[]{:S(2)}) collective-permute-start(bf16[640,256]{1,0:T(8,128)(2,1)S(1)} %collective-permute-done.9.refs_2_.refs_12_), channel_id=1, source_target_pairs={{0,16},{1,17},{2,18},{3,19},{4,20},{5,21},{6,22},{7,23},{8,24},{9,... | collective-permute-start | bytes 983048 | tf_op jit(solution)/shard_map/ppermute | solution.py:56
  75.6 0.6 stack.131.block_ref
  76.2 0.7 stack.130.block_ref
  76.9 1.7 %collective-permute-done.15.refs_11_ = bf16[640,256]{1,0:T(8,128)(2,1)} collective-permute-done((bf16[640,256]{1,0:T(8,128)(2,1)S(1)}, bf16[640,256]{1,0:T(8,128)(2,1)}, u32[]{:S(2)}, u32[]{:S(2)}) %collective-permute-start.15) | collective-permute-done | bytes 327712 | tf_op jit(solution)/shard_map/ppermute | solution.py:56
  78.7 7.5 %shard_map.75.refs_9_ = f32[1088,512]{1,0:T(8,128)} custom-call(s32[5]{0:T(128)} %stack.131.block_ref, bf16[512,8192]{1,0:T(8,128)(2,1)} %refs_6_.1, bf16[512,8192]{1,0:T(8,128)(2,1)} %collective-permute-done.16.got_ref.refs_7_, bf16[64,8192]{1,0:T(8,128)(2,1)} %bitcast.47, bf16[512,256]{1,0:T(8,128)(2,1)} %copy-done.14, ...), custom_call_target="tpu_custom_call" | custom-call | flops 1 | bytes 1 | tf_op jit(solution)/shard_map/pallas_call | solution.py:219
  86.3 0.8 copy-done.18
  87.1 9.3 %shard_map.76.refs_2_ = bf16[1088,512]{1,0:T(8,128)(2,1)} custom-call(s32[8]{0:T(128)} %stack.130.block_ref, bf16[512,8192]{1,0:T(8,128)(2,1)} %refs_6_.1, bf16[512,8192]{1,0:T(8,128)(2,1)} %collective-permute-done.16.got_ref.refs_7_, bf16[64,8192]{1,0:T(8,128)(2,1)} %bitcast.48, bf16[1088,256]{1,0:T(8,128)(2,1)} %copy-done.10, ...), custom_call_target="tpu_custom_call" | custom-call | flops 1 | bytes 1 | tf_op jit(solution)/shard_map/pallas_call | solution.py:219
  96.5 0.8 collective-permute-start.26
  98.0 0.6 pad_add_fusion.1.block_ref
  98.6 1.0 collective-permute-done.11.refs_1_
  99.6 7.0 %collective-permute-done.26.refs_15_ = bf16[640,256]{1,0:T(8,128)(2,1)S(1)} collective-permute-done((bf16[640,256]{1,0:T(8,128)(2,1)S(1)}, bf16[640,256]{1,0:T(8,128)(2,1)S(1)}, u32[]{:S(2)}, u32[]{:S(2)}) %collective-permute-start.26) | collective-permute-done | bytes 327712 | tf_op jit(solution)/shard_map/ppermute | solution.py:56
  106.6 0.7 copy-done.20
  107.3 11.8 %shard_map.77 = (bf16[4,4,144,128]{3,2,1,0:T(8,128)(2,1)}, f32[64,512]{1,0:T(8,128)}) custom-call(s32[4]{0:T(128)} %and_select_fusion.1.place_ref, s32[4]{0:T(128)} %pad_add_fusion.turn_ref, s32[3]{0:T(128)} %pad_add_fusion.1.block_ref, bf16[4,128,256]{2,1,0:T(8,128)(2,1)} %copy-done.9, bf16[4,128,256]{2,1,0:T(8,128)(2,1)} %copy-done.22, ...), custom_call_target="tpu_custom_call" | custom-call | flops 1 | bytes 1 | tf_op jit(solution)/shard_map/pallas_call | solution.py:403
  119.1 1.0 slice_bitcast_fusion
  120.4 0.8 slice.74
  121.7 0.8 slice.75
  122.7 1.6 collective-permute-start.28
  124.4 4.1 %collective-permute-done.28.far_ref = bf16[4,144,128]{2,1,0:T(8,128)(2,1)S(1)} collective-permute-done((bf16[4,144,128]{2,1,0:T(8,128)(2,1)S(1)}, bf16[4,144,128]{2,1,0:T(8,128)(2,1)S(1)}, u32[]{:S(2)}, u32[]{:S(2)}) %collective-permute-start.28) | collective-permute-done | bytes 147488 | tf_op jit(solution)/shard_map/ppermute | solution.py:56
  128.6 3.1 %collective-permute-start.29 = (bf16[144,128]{1,0:T(8,128)(2,1)S(1)}, bf16[144,128]{1,0:T(8,128)(2,1)S(1)}, u32[]{:S(2)}, u32[]{:S(2)}) collective-permute-start(bf16[144,128]{1,0:T(8,128)(2,1)S(1)} %get-tuple-element.71), channel_id=1, source_target_pairs={{0,4},{1,5},{2,6},{3,7},{4,8},{5,9},{6,10},{7,11},{8,12},{9,13},{1... | collective-permute-start | bytes 110600 | tf_op jit(solution)/shard_map/ppermute | solution.py:56
  131.7 1.1 collective-permute-start.30
  132.8 2.8 %collective-permute-start.31 = (bf16[144,128]{1,0:T(8,128)(2,1)S(1)}, bf16[144,128]{1,0:T(8,128)(2,1)S(1)}, u32[]{:S(2)}, u32[]{:S(2)}) collective-permute-start(bf16[144,128]{1,0:T(8,128)(2,1)S(1)} %get-tuple-element.73), channel_id=1, source_target_pairs={{0,12},{1,13},{2,14},{3,15},{4,0},{5,1},{6,2},{7,3},{8,4},{9,5},{1... | collective-permute-start | bytes 110600 | tf_op jit(solution)/shard_map/ppermute | solution.py:56
  135.6 0.8 fusion.refs_6_
  136.6 0.7 collective-permute-done.31.refs_3_
  137.2 1.7 %shard_map.80 = bf16[64,8192]{1,0:T(8,128)(2,1)S(1)} custom-call(s32[16]{0:T(128)S(1)} %stack.115.block_ref, bf16[144,128]{1,0:T(8,128)(2,1)S(1)} %get-tuple-element.70.refs_0_, bf16[144,128]{1,0:T(8,128)(2,1)S(1)} %collective-permute-done.29.refs_1_, bf16[144,128]{1,0:T(8,128)(2,1)S(1)} %collective-permute-done.30.refs_2_, ...), custom_call_target="tpu_custom_call" | custom-call | flops 1 | bytes 1 | tf_op jit(solution)/shard_map/pallas_call | solution.py:254
  139.1 1.9 %collective-permute-done.33 = bf16[64,4096]{1,0:T(8,128)(2,1)S(1)} collective-permute-done((bf16[64,4096]{1,0:T(8,128)(2,1)S(1)}, bf16[64,4096]{1,0:T(8,128)(2,1)S(1)}, u32[]{:S(2)}, u32[]{:S(2)}) %collective-permute-start.33) | collective-permute-done | bytes 524320 | tf_op jit(solution)/shard_map/ppermute | solution.py:56
  141.1 1.6 collective-permute-start.34
  142.7 6.8 %collective-permute-done.34 = bf16[64,2048]{1,0:T(8,128)(2,1)S(1)} collective-permute-done((bf16[64,2048]{1,0:T(8,128)(2,1)S(1)}, bf16[64,2048]{1,0:T(8,128)(2,1)S(1)}, u32[]{:S(2)}, u32[]{:S(2)}) %collective-permute-start.34) | collective-permute-done | bytes 262176 | tf_op jit(solution)/shard_map/ppermute | solution.py:56
  149.6 4.2 %collective-permute-start.37 = (bf16[64,512]{1,0:T(8,128)(2,1)S(1)}, bf16[64,512]{1,0:T(8,128)(2,1)S(1)}, u32[]{:S(2)}, u32[]{:S(2)}) collective-permute-start(bf16[64,512]{1,0:T(8,128)(2,1)S(1)} %get-tuple-element.80), channel_id=1, source_target_pairs={{0,12},{1,13},{2,14},{3,15},{4,0},{5,1},{6,2},{7,3},{8,4},{9,5},{1... | collective-permute-start | bytes 196616 | tf_op jit(solution)/shard_map/ppermute | solution.py:56
  153.8 0.6 collective-permute-start.35
  154.4 1.6 collective-permute-done.37
  156.0 2.9 %collective-permute-done.36 = bf16[64,512]{1,0:T(8,128)(2,1)S(1)} collective-permute-done((bf16[64,512]{1,0:T(8,128)(2,1)S(1)}, bf16[64,512]{1,0:T(8,128)(2,1)S(1)}, u32[]{:S(2)}, u32[]{:S(2)}) %collective-permute-start.36) | collective-permute-done | bytes 65568 | tf_op jit(solution)/shard_map/ppermute | solution.py:56
  159.0 0.9 collective-permute-done.35
  159.9 0.7 add_convert_fusion.2
  (123 shorter events, 7.4 us)
Async XLA Ops:
  0.0 7.5 %copy-start.19 = (bf16[512,512]{1,0:T(8,128)(2,1)S(1)}, bf16[512,512]{1,0:T(8,128)(2,1)}, u32[]{:S(2)}) copy-start(bf16[512,512]{1,0:T(8,128)(2,1)} %param.11) | copy-start | bytes 1572868
  0.0 9.3 %copy-start.29 = (s32[64]{0:T(128)S(1)}, s32[64]{0:T(128)}, u32[]{:S(2)}) copy-start(s32[64]{0:T(128)} %param.9) | copy-start | bytes 772
  0.0 78.6 %collective-permute-start.16 = (bf16[512,8192]{1,0:T(8,128)(2,1)}, bf16[512,8192]{1,0:T(8,128)(2,1)}, u32[]{:S(2)}, u32[]{:S(2)}) collective-permute-start(bf16[512,8192]{1,0:T(8,128)(2,1)} %refs_6_.1), channel_id=1, source_target_pairs={{0,1},{1,0},{2,3},{3,2},{4,5},{5,4},{6,7},{7,6},{8,9},{9,8},{10,11... | collective-permute-start | bytes 25165832 | tf_op jit(solution)/shard_map/ppermute | solution.py:56
  0.5 9.2 %copy-start = (bf16[2,32,8192]{2,1,0:T(8,128)(2,1)S(1)}, bf16[2,32,8192]{2,1,0:T(8,128)(2,1)}, u32[]{:S(2)}) copy-start(bf16[2,32,8192]{2,1,0:T(8,128)(2,1)} %param.10) | copy-start | bytes 3145732
  2.3 11.5 %copy-start.14 = (bf16[512,256]{1,0:T(8,128)(2,1)}, bf16[512,256]{1,0:T(8,128)(2,1)S(1)}, u32[]{:S(2)}) copy-start(bf16[512,256]{1,0:T(8,128)(2,1)S(1)} %get-tuple-element.76.refs_0_) | copy-start | bytes 786436
  2.3 11.6 %collective-permute-start = (bf16[512,256]{1,0:T(8,128)(2,1)S(1)}, bf16[512,256]{1,0:T(8,128)(2,1)S(1)}, u32[]{:S(2)}, u32[]{:S(2)}) collective-permute-start(bf16[512,256]{1,0:T(8,128)(2,1)S(1)} %get-tuple-element.76.refs_0_), channel_id=1, source_target_pairs={{0,2},{1,3},{2,0},{3,1},{4,6},{5,7},{6,4},{7,5},{8,10},{9,11},{10,... | collective-permute-start | bytes 786440 | tf_op jit(solution)/shard_map/ppermute | solution.py:56
  4.9 22.7 %collective-permute-start.6 = (bf16[512,256]{1,0:T(8,128)(2,1)S(1)}, bf16[512,256]{1,0:T(8,128)(2,1)}, u32[]{:S(2)}, u32[]{:S(2)}) collective-permute-start(bf16[512,256]{1,0:T(8,128)(2,1)S(1)} %get-tuple-element.76.refs_0_), channel_id=1, source_target_pairs={{0,8},{1,9},{2,10},{3,11},{4,0},{5,1},{6,2},{7,3},{8,12},{9,13},{1... | collective-permute-start | bytes 786440 | tf_op jit(solution)/shard_map/ppermute | solution.py:56
  7.6 11.5 %collective-permute-start.1 = (bf16[512,256]{1,0:T(8,128)(2,1)S(1)}, bf16[512,256]{1,0:T(8,128)(2,1)}, u32[]{:S(2)}, u32[]{:S(2)}) collective-permute-start(bf16[512,256]{1,0:T(8,128)(2,1)S(1)} %get-tuple-element.77), channel_id=1, source_target_pairs={{0,8},{1,9},{2,10},{3,11},{4,0},{5,1},{6,2},{7,3},{8,12},{9,13},{1... | collective-permute-start | bytes 786440 | tf_op jit(solution)/shard_map/ppermute | solution.py:56
  13.9 20.2 %copy-start.10 = (bf16[1088,256]{1,0:T(8,128)(2,1)}, bf16[1088,256]{1,0:T(8,128)(2,1)S(1)}, u32[]{:S(2)}) copy-start(bf16[1088,256]{1,0:T(8,128)(2,1)S(1)} %pad_maximum_fusion.refs_0_) | copy-start | bytes 1671172
  14.0 13.7 %copy-start.27 = (bf16[512,256]{1,0:T(8,128)(2,1)}, bf16[512,256]{1,0:T(8,128)(2,1)S(1)}, u32[]{:S(2)}) copy-start(bf16[512,256]{1,0:T(8,128)(2,1)S(1)} %collective-permute-done) | copy-start | bytes 786436
  19.0 13.9 %collective-permute-start.2 = (bf16[1088,256]{1,0:T(8,128)(2,1)S(1)}, bf16[1088,256]{1,0:T(8,128)(2,1)S(1)}, u32[]{:S(2)}, u32[]{:S(2)}) collective-permute-start(bf16[1088,256]{1,0:T(8,128)(2,1)S(1)} %pad_maximum_fusion.refs_0_), channel_id=1, source_target_pairs={{0,2},{1,3},{2,0},{3,1},{4,6},{5,7},{6,4},{7,5},{8,10},{9,11},{10,... | collective-permute-start | bytes 1671176 | tf_op jit(solution)/shard_map/ppermute | solution.py:56
  19.6 9.6 %collective-permute-start.17 = (bf16[512,256]{1,0:T(8,128)(2,1)}, bf16[512,256]{1,0:T(8,128)(2,1)S(1)}, u32[]{:S(2)}, u32[]{:S(2)}) collective-permute-start(bf16[512,256]{1,0:T(8,128)(2,1)} %collective-permute-done.1), channel_id=1, source_target_pairs={{0,16},{1,17},{2,18},{3,19},{4,20},{5,21},{6,22},{7,23},{8,24},{9,... | collective-permute-start | bytes 786440 | tf_op jit(solution)/shard_map/ppermute | solution.py:56
  24.1 10.6 %collective-permute-start.3 = (bf16[512,256]{1,0:T(8,128)(2,1)}, bf16[512,256]{1,0:T(8,128)(2,1)}, u32[]{:S(2)}, u32[]{:S(2)}) collective-permute-start(bf16[512,256]{1,0:T(8,128)(2,1)} %collective-permute-done.1), channel_id=1, source_target_pairs={{0,8},{1,9},{2,10},{3,11},{4,0},{5,1},{6,2},{7,3},{8,12},{9,13},{1... | collective-permute-start | bytes 786440 | tf_op jit(solution)/shard_map/ppermute | solution.py:56
  27.6 10.5 %collective-permute-start.12 = (bf16[512,256]{1,0:T(8,128)(2,1)}, bf16[512,256]{1,0:T(8,128)(2,1)S(1)}, u32[]{:S(2)}, u32[]{:S(2)}) collective-permute-start(bf16[512,256]{1,0:T(8,128)(2,1)} %collective-permute-done.6.refs_2_), channel_id=1, source_target_pairs={{0,16},{1,17},{2,18},{3,19},{4,20},{5,21},{6,22},{7,23},{8,24},{9,... | collective-permute-start | bytes 786440 | tf_op jit(solution)/shard_map/ppermute | solution.py:56
  28.2 16.1 %copy-start.28 = (bf16[512,256]{1,0:T(8,128)(2,1)S(1)}, bf16[512,256]{1,0:T(8,128)(2,1)}, u32[]{:S(2)}) copy-start(bf16[512,256]{1,0:T(8,128)(2,1)} %copy-done.27) | copy-start | bytes 786436
  29.2 10.7 %collective-permute-start.7 = (bf16[512,256]{1,0:T(8,128)(2,1)}, bf16[512,256]{1,0:T(8,128)(2,1)}, u32[]{:S(2)}, u32[]{:S(2)}) collective-permute-start(bf16[512,256]{1,0:T(8,128)(2,1)} %collective-permute-done.6.refs_2_), channel_id=1, source_target_pairs={{0,8},{1,9},{2,10},{3,11},{4,0},{5,1},{6,2},{7,3},{8,12},{9,13},{1... | collective-permute-start | bytes 786440 | tf_op jit(solution)/shard_map/ppermute | solution.py:56
  31.6 28.1 %copy-start.13 = (bf16[1024,256]{1,0:T(8,128)(2,1)}, bf16[1024,256]{1,0:T(8,128)(2,1)S(1)}, u32[]{:S(2)}) copy-start(bf16[1024,256]{1,0:T(8,128)(2,1)S(1)} %constant_dynamic-update-slice_fusion.refs_2_) | copy-start | bytes 1572868
  32.9 11.4 %copy-start.15 = (bf16[1088,256]{1,0:T(8,128)(2,1)}, bf16[1088,256]{1,0:T(8,128)(2,1)S(1)}, u32[]{:S(2)}) copy-start(bf16[1088,256]{1,0:T(8,128)(2,1)S(1)} %collective-permute-done.2.refs_1_) | copy-start | bytes 1671172
  32.9 16.5 %collective-permute-start.22 = (bf16[1024,256]{1,0:T(8,128)(2,1)S(1)}, bf16[1024,256]{1,0:T(8,128)(2,1)S(1)}, u32[]{:S(2)}, u32[]{:S(2)}) collective-permute-start(bf16[1024,256]{1,0:T(8,128)(2,1)S(1)} %constant_dynamic-update-slice_fusion.refs_2_), channel_id=1, source_target_pairs={{0,2},{1,3},{2,0},{3,1},{4,6},{5,7},{6,4},{7,5},{8,10},{9,11},{10,... | collective-permute-start | bytes 1572872 | tf_op jit(solution)/shard_map/ppermute | solution.py:56
  34.7 10.8 %collective-permute-start.4 = (bf16[512,256]{1,0:T(8,128)(2,1)}, bf16[512,256]{1,0:T(8,128)(2,1)S(1)}, u32[]{:S(2)}, u32[]{:S(2)}) collective-permute-start(bf16[512,256]{1,0:T(8,128)(2,1)} %collective-permute-done.3), channel_id=1, source_target_pairs={{0,8},{1,9},{2,10},{3,11},{4,0},{5,1},{6,2},{7,3},{8,12},{9,13},{1... | collective-permute-start | bytes 786440 | tf_op jit(solution)/shard_map/ppermute | solution.py:56
  38.1 21.6 %copy-start.21 = (bf16[512,256]{1,0:T(8,128)(2,1)}, bf16[512,256]{1,0:T(8,128)(2,1)S(1)}, u32[]{:S(2)}) copy-start(bf16[512,256]{1,0:T(8,128)(2,1)S(1)} %collective-permute-done.12.refs_3_) | copy-start | bytes 786436
  38.1 8.0 %collective-permute-start.13 = (bf16[512,256]{1,0:T(8,128)(2,1)}, bf16[512,256]{1,0:T(8,128)(2,1)S(1)}, u32[]{:S(2)}, u32[]{:S(2)}) collective-permute-start(bf16[512,256]{1,0:T(8,128)(2,1)} %collective-permute-done.3), channel_id=1, source_target_pairs={{0,16},{1,17},{2,18},{3,19},{4,20},{5,21},{6,22},{7,23},{8,24},{9,... | collective-permute-start | bytes 786440 | tf_op jit(solution)/shard_map/ppermute | solution.py:56
  39.9 13.6 %collective-permute-start.8 = (bf16[512,256]{1,0:T(8,128)(2,1)}, bf16[512,256]{1,0:T(8,128)(2,1)S(1)}, u32[]{:S(2)}, u32[]{:S(2)}) collective-permute-start(bf16[512,256]{1,0:T(8,128)(2,1)} %collective-permute-done.7.refs_4_), channel_id=1, source_target_pairs={{0,8},{1,9},{2,10},{3,11},{4,0},{5,1},{6,2},{7,3},{8,12},{9,13},{1... | collective-permute-start | bytes 786440 | tf_op jit(solution)/shard_map/ppermute | solution.py:56
  44.3 34.3 %copy-start.3 = (bf16[640,256]{1,0:T(8,128)(2,1)}, bf16[640,256]{1,0:T(8,128)(2,1)S(1)}, u32[]{:S(2)}) copy-start(bf16[640,256]{1,0:T(8,128)(2,1)S(1)} %pad_maximum_fusion.1.refs_0_.refs_8_) | copy-start | bytes 983044
  45.5 7.8 %collective-permute-start.18 = (bf16[512,256]{1,0:T(8,128)(2,1)S(1)}, bf16[512,256]{1,0:T(8,128)(2,1)S(1)}, u32[]{:S(2)}, u32[]{:S(2)}) collective-permute-start(bf16[512,256]{1,0:T(8,128)(2,1)S(1)} %copy-done.28), channel_id=1, source_target_pairs={{0,16},{1,17},{2,18},{3,19},{4,20},{5,21},{6,22},{7,23},{8,24},{9,... | collective-permute-start | bytes 786440 | tf_op jit(solution)/shard_map/ppermute | solution.py:56
  46.1 10.2 %collective-permute-start.5 = (bf16[640,256]{1,0:T(8,128)(2,1)S(1)}, bf16[640,256]{1,0:T(8,128)(2,1)S(1)}, u32[]{:S(2)}, u32[]{:S(2)}) collective-permute-start(bf16[640,256]{1,0:T(8,128)(2,1)S(1)} %pad_maximum_fusion.1.refs_0_.refs_8_), channel_id=1, source_target_pairs={{0,8},{1,9},{2,10},{3,11},{4,0},{5,1},{6,2},{7,3},{8,12},{9,13},{1... | collective-permute-start | bytes 983048 | tf_op jit(solution)/shard_map/ppermute | solution.py:56
  49.4 36.8 %copy-start.11 = (bf16[1024,256]{1,0:T(8,128)(2,1)}, bf16[1024,256]{1,0:T(8,128)(2,1)S(1)}, u32[]{:S(2)}) copy-start(bf16[1024,256]{1,0:T(8,128)(2,1)S(1)} %constant_dynamic-update-slice_fusion.2.refs_4_) | copy-start | bytes 1572868
  49.4 6.0 %copy-start.16 = (bf16[1024,256]{1,0:T(8,128)(2,1)}, bf16[1024,256]{1,0:T(8,128)(2,1)S(1)}, u32[]{:S(2)}) copy-start(bf16[1024,256]{1,0:T(8,128)(2,1)S(1)} %collective-permute-done.22.refs_3_) | copy-start | bytes 1572868
  49.4 16.5 %collective-permute-start.23 = (bf16[1024,256]{1,0:T(8,128)(2,1)S(1)}, bf16[1024,256]{1,0:T(8,128)(2,1)S(1)}, u32[]{:S(2)}, u32[]{:S(2)}) collective-permute-start(bf16[1024,256]{1,0:T(8,128)(2,1)S(1)} %constant_dynamic-update-slice_fusion.2.refs_4_), channel_id=1, source_target_pairs={{0,2},{1,3},{2,0},{3,1},{4,6},{5,7},{6,4},{7,5},{8,10},{9,11},{10,... | collective-permute-start | bytes 1572872 | tf_op jit(solution)/shard_map/ppermute | solution.py:56
  53.4 7.0 %collective-permute-start.19 = (bf16[512,256]{1,0:T(8,128)(2,1)}, bf16[512,256]{1,0:T(8,128)(2,1)S(1)}, u32[]{:S(2)}, u32[]{:S(2)}) collective-permute-start(bf16[512,256]{1,0:T(8,128)(2,1)} %collective-permute-done.7.refs_4_), channel_id=1, source_target_pairs={{0,16},{1,17},{2,18},{3,19},{4,20},{5,21},{6,22},{7,23},{8,24},{9,... | collective-permute-start | bytes 786440 | tf_op jit(solution)/shard_map/ppermute | solution.py:56
  53.5 20.5 %copy-start.23 = (bf16[512,256]{1,0:T(8,128)(2,1)}, bf16[512,256]{1,0:T(8,128)(2,1)S(1)}, u32[]{:S(2)}) copy-start(bf16[512,256]{1,0:T(8,128)(2,1)S(1)} %collective-permute-done.8.refs_6_) | copy-start | bytes 786436
  53.5 12.4 %collective-permute-start.14 = (bf16[512,256]{1,0:T(8,128)(2,1)S(1)}, bf16[512,256]{1,0:T(8,128)(2,1)S(1)}, u32[]{:S(2)}, u32[]{:S(2)}) collective-permute-start(bf16[512,256]{1,0:T(8,128)(2,1)S(1)} %collective-permute-done.4), channel_id=1, source_target_pairs={{0,16},{1,17},{2,18},{3,19},{4,20},{5,21},{6,22},{7,23},{8,24},{9,... | collective-permute-start | bytes 786440 | tf_op jit(solution)/shard_map/ppermute | solution.py:56
  56.2 41.1 %copy-start.6 = (bf16[640,256]{1,0:T(8,128)(2,1)}, bf16[640,256]{1,0:T(8,128)(2,1)S(1)}, u32[]{:S(2)}) copy-start(bf16[640,256]{1,0:T(8,128)(2,1)S(1)} %collective-permute-done.5.refs_1_.refs_10_) | copy-start | bytes 983044
  56.2 12.1 %collective-permute-start.9 = (bf16[640,256]{1,0:T(8,128)(2,1)S(1)}, bf16[640,256]{1,0:T(8,128)(2,1)S(1)}, u32[]{:S(2)}, u32[]{:S(2)}) collective-permute-start(bf16[640,256]{1,0:T(8,128)(2,1)S(1)} %collective-permute-done.5.refs_1_.refs_10_), channel_id=1, source_target_pairs={{0,8},{1,9},{2,10},{3,11},{4,0},{5,1},{6,2},{7,3},{8,12},{9,13},{1... | collective-permute-start | bytes 983048 | tf_op jit(solution)/shard_map/ppermute | solution.py:56
  60.3 13.7 %copy-start.25 = (bf16[512,256]{1,0:T(8,128)(2,1)}, bf16[512,256]{1,0:T(8,128)(2,1)S(1)}, u32[]{:S(2)}) copy-start(bf16[512,256]{1,0:T(8,128)(2,1)S(1)} %collective-permute-done.19.refs_5_) | copy-start | bytes 786436
  60.3 13.7 %collective-permute-start.20 = (bf16[512,256]{1,0:T(8,128)(2,1)S(1)}, bf16[512,256]{1,0:T(8,128)(2,1)S(1)}, u32[]{:S(2)}, u32[]{:S(2)}) collective-permute-start(bf16[512,256]{1,0:T(8,128)(2,1)S(1)} %collective-permute-done.8.refs_6_), channel_id=1, source_target_pairs={{0,16},{1,17},{2,18},{3,19},{4,20},{5,21},{6,22},{7,23},{8,24},{9,... | collective-permute-start | bytes 786440 | tf_op jit(solution)/shard_map/ppermute | solution.py:56
  65.9 20.3 %copy-start.12 = (bf16[1024,256]{1,0:T(8,128)(2,1)}, bf16[1024,256]{1,0:T(8,128)(2,1)S(1)}, u32[]{:S(2)}) copy-start(bf16[1024,256]{1,0:T(8,128)(2,1)S(1)} %constant_dynamic-update-slice_fusion.4.refs_6_) | copy-start | bytes 1572868
  65.9 8.0 %copy-start.17 = (bf16[1024,256]{1,0:T(8,128)(2,1)}, bf16[1024,256]{1,0:T(8,128)(2,1)S(1)}, u32[]{:S(2)}) copy-start(bf16[1024,256]{1,0:T(8,128)(2,1)S(1)} %collective-permute-done.23.refs_5_) | copy-start | bytes 1572868
  66.0 20.3 %collective-permute-start.24 = (bf16[1024,256]{1,0:T(8,128)(2,1)S(1)}, bf16[1024,256]{1,0:T(8,128)(2,1)S(1)}, u32[]{:S(2)}, u32[]{:S(2)}) collective-permute-start(bf16[1024,256]{1,0:T(8,128)(2,1)S(1)} %constant_dynamic-update-slice_fusion.4.refs_6_), channel_id=1, source_target_pairs={{0,2},{1,3},{2,0},{3,1},{4,6},{5,7},{6,4},{7,5},{8,10},{9,11},{10,... | collective-permute-start | bytes 1572872 | tf_op jit(solution)/shard_map/ppermute | solution.py:56
  67.5 11.1 %collective-permute-start.15 = (bf16[640,256]{1,0:T(8,128)(2,1)S(1)}, bf16[640,256]{1,0:T(8,128)(2,1)}, u32[]{:S(2)}, u32[]{:S(2)}) collective-permute-start(bf16[640,256]{1,0:T(8,128)(2,1)S(1)} %collective-permute-done.5.refs_1_.refs_10_), channel_id=1, source_target_pairs={{0,16},{1,17},{2,18},{3,19},{4,20},{5,21},{6,22},{7,23},{8,24},{9,... | collective-permute-start | bytes 983048 | tf_op jit(solution)/shard_map/ppermute | solution.py:56
  68.3 29.0 %copy-start.7 = (bf16[640,256]{1,0:T(8,128)(2,1)}, bf16[640,256]{1,0:T(8,128)(2,1)S(1)}, u32[]{:S(2)}) copy-start(bf16[640,256]{1,0:T(8,128)(2,1)S(1)} %collective-permute-done.9.refs_2_.refs_12_) | copy-start | bytes 983044
  68.3 17.9 %collective-permute-start.10 = (bf16[640,256]{1,0:T(8,128)(2,1)S(1)}, bf16[640,256]{1,0:T(8,128)(2,1)S(1)}, u32[]{:S(2)}, u32[]{:S(2)}) collective-permute-start(bf16[640,256]{1,0:T(8,128)(2,1)S(1)} %collective-permute-done.9.refs_2_.refs_12_), channel_id=1, source_target_pairs={{0,8},{1,9},{2,10},{3,11},{4,0},{5,1},{6,2},{7,3},{8,12},{9,13},{1... | collective-permute-start | bytes 983048 | tf_op jit(solution)/shard_map/ppermute | solution.py:56
  74.0 4.6 %copy-start.26 = (bf16[512,256]{1,0:T(8,128)(2,1)}, bf16[512,256]{1,0:T(8,128)(2,1)S(1)}, u32[]{:S(2)}) copy-start(bf16[512,256]{1,0:T(8,128)(2,1)S(1)} %collective-permute-done.20.refs_7_) | copy-start | bytes 786436
  74.0 12.2 %collective-permute-start.21 = (bf16[640,256]{1,0:T(8,128)(2,1)S(1)}, bf16[640,256]{1,0:T(8,128)(2,1)}, u32[]{:S(2)}, u32[]{:S(2)}) collective-permute-start(bf16[640,256]{1,0:T(8,128)(2,1)S(1)} %collective-permute-done.9.refs_2_.refs_12_), channel_id=1, source_target_pairs={{0,16},{1,17},{2,18},{3,19},{4,20},{5,21},{6,22},{7,23},{8,24},{9,... | collective-permute-start | bytes 983048 | tf_op jit(solution)/shard_map/ppermute | solution.py:56
  86.2 11.1 %copy-start.4 = (bf16[640,256]{1,0:T(8,128)(2,1)S(1)}, bf16[640,256]{1,0:T(8,128)(2,1)}, u32[]{:S(2)}) copy-start(bf16[640,256]{1,0:T(8,128)(2,1)} %copy-done.3) | copy-start | bytes 983044
  86.2 11.1 %copy-start.8 = (bf16[640,256]{1,0:T(8,128)(2,1)}, bf16[640,256]{1,0:T(8,128)(2,1)S(1)}, u32[]{:S(2)}) copy-start(bf16[640,256]{1,0:T(8,128)(2,1)S(1)} %collective-permute-done.10.refs_3_.refs_14_) | copy-start | bytes 983044
  96.4 10.2 %collective-permute-start.25 = (bf16[1088,512]{1,0:T(8,128)(2,1)}, bf16[1088,512]{1,0:T(8,128)(2,1)}, u32[]{:S(2)}, u32[]{:S(2)}) collective-permute-start(bf16[1088,512]{1,0:T(8,128)(2,1)} %shard_map.76.refs_2_), channel_id=1, source_target_pairs={{0,1},{1,0},{2,3},{3,2},{4,5},{5,4},{6,7},{7,6},{8,9},{9,8},{10,11... | collective-permute-start | bytes 3342344 | tf_op jit(solution)/shard_map/ppermute | solution.py:56
  96.5 10.1 %collective-permute-start.26 = (bf16[640,256]{1,0:T(8,128)(2,1)S(1)}, bf16[640,256]{1,0:T(8,128)(2,1)S(1)}, u32[]{:S(2)}, u32[]{:S(2)}) collective-permute-start(bf16[640,256]{1,0:T(8,128)(2,1)S(1)} %collective-permute-done.10.refs_3_.refs_14_), channel_id=1, source_target_pairs={{0,16},{1,17},{2,18},{3,19},{4,20},{5,21},{6,22},{7,23},{8,24},{9,... | collective-permute-start | bytes 983048 | tf_op jit(solution)/shard_map/ppermute | solution.py:56
  97.7 8.9 %copy-start.9 = (bf16[4,128,256]{2,1,0:T(8,128)(2,1)}, bf16[4,128,256]{2,1,0:T(8,128)(2,1)S(1)}, u32[]{:S(2)}) copy-start(bf16[4,128,256]{2,1,0:T(8,128)(2,1)S(1)} %shard_map.74.refs_0_) | copy-start | bytes 786436
  97.7 1.9 %collective-permute-start.11 = (bf16[4,128,256]{2,1,0:T(8,128)(2,1)S(1)}, bf16[4,128,256]{2,1,0:T(8,128)(2,1)S(1)}, u32[]{:S(2)}, u32[]{:S(2)}) collective-permute-start(bf16[4,128,256]{2,1,0:T(8,128)(2,1)S(1)} %shard_map.74.refs_0_), channel_id=1, source_target_pairs={{0,1},{1,0},{2,3},{3,2},{4,5},{5,4},{6,7},{7,6},{8,9},{9,8},{10,11... | collective-permute-start | bytes 786440 | tf_op jit(solution)/shard_map/ppermute | solution.py:56
  99.6 7.0 %copy-start.22 = (bf16[4,128,256]{2,1,0:T(8,128)(2,1)}, bf16[4,128,256]{2,1,0:T(8,128)(2,1)S(1)}, u32[]{:S(2)}) copy-start(bf16[4,128,256]{2,1,0:T(8,128)(2,1)S(1)} %collective-permute-done.11.refs_1_) | copy-start | bytes 786436
  107.3 29.9 %copy-start.2 = (bf16[256,8192]{1,0:T(8,128)(2,1)S(1)}, bf16[256,8192]{1,0:T(8,128)(2,1)}, u32[]{:S(2)}) copy-start(bf16[256,8192]{1,0:T(8,128)(2,1)} %refs_7_.1) | copy-start | bytes 12582916
  119.1 3.5 %copy-start.5 = (bf16[4,4,144,128]{3,2,1,0:T(8,128)(2,1)S(1)}, bf16[4,4,144,128]{3,2,1,0:T(8,128)(2,1)}, u32[]{:S(2)}) copy-start(bf16[4,4,144,128]{3,2,1,0:T(8,128)(2,1)} %get-tuple-element.67) | copy-start | bytes 1769476
  120.2 2.4 %collective-permute-start.27 = (bf16[4,2,144,128]{3,2,1,0:T(8,128)(2,1)S(1)}, bf16[4,2,144,128]{3,2,1,0:T(8,128)(2,1)S(1)}, u32[]{:S(2)}, u32[]{:S(2)}) collective-permute-start(bf16[4,2,144,128]{3,2,1,0:T(8,128)(2,1)S(1)} %slice_bitcast_fusion), channel_id=1, source_target_pairs={{0,1},{1,0},{2,3},{3,2},{4,5},{5,4},{6,7},{7,6},{8,9},{9,8},{10,11... | collective-permute-start | bytes 884744 | tf_op jit(solution)/shard_map/ppermute | solution.py:56
  121.2 14.4 %collective-permute-start.32 = (f32[64,512]{1,0:T(8,128)}, f32[64,512]{1,0:T(8,128)S(1)}, u32[]{:S(2)}, u32[]{:S(2)}) collective-permute-start(f32[64,512]{1,0:T(8,128)} %get-tuple-element.74), channel_id=1, source_target_pairs={{0,1},{1,0},{2,3},{3,2},{4,5},{5,4},{6,7},{7,6},{8,9},{9,8},{10,11... | collective-permute-start | bytes 393224 | tf_op jit(solution)/shard_map/ppermute | solution.py:56
  122.7 5.8 %collective-permute-start.28 = (bf16[4,144,128]{2,1,0:T(8,128)(2,1)S(1)}, bf16[4,144,128]{2,1,0:T(8,128)(2,1)S(1)}, u32[]{:S(2)}, u32[]{:S(2)}) collective-permute-start(bf16[4,144,128]{2,1,0:T(8,128)(2,1)S(1)} %get-tuple-element.69), channel_id=1, source_target_pairs={{0,2},{1,3},{2,0},{3,1},{4,6},{5,7},{6,4},{7,5},{8,10},{9,11},{10,... | collective-permute-start | bytes 442376 | tf_op jit(solution)/shard_map/ppermute | solution.py:56
  128.6 7.8 %collective-permute-start.29 = (bf16[144,128]{1,0:T(8,128)(2,1)S(1)}, bf16[144,128]{1,0:T(8,128)(2,1)S(1)}, u32[]{:S(2)}, u32[]{:S(2)}) collective-permute-start(bf16[144,128]{1,0:T(8,128)(2,1)S(1)} %get-tuple-element.71), channel_id=1, source_target_pairs={{0,4},{1,5},{2,6},{3,7},{4,8},{5,9},{6,10},{7,11},{8,12},{9,13},{1... | collective-permute-start | bytes 110600 | tf_op jit(solution)/shard_map/ppermute | solution.py:56
  131.7 4.9 %collective-permute-start.30 = (bf16[144,128]{1,0:T(8,128)(2,1)S(1)}, bf16[144,128]{1,0:T(8,128)(2,1)S(1)}, u32[]{:S(2)}, u32[]{:S(2)}) collective-permute-start(bf16[144,128]{1,0:T(8,128)(2,1)S(1)} %get-tuple-element.72), channel_id=1, source_target_pairs={{0,8},{1,9},{2,10},{3,11},{4,12},{5,13},{6,14},{7,15},{8,0},{9,1},... | collective-permute-start | bytes 110600 | tf_op jit(solution)/shard_map/ppermute | solution.py:56
  132.8 4.5 %collective-permute-start.31 = (bf16[144,128]{1,0:T(8,128)(2,1)S(1)}, bf16[144,128]{1,0:T(8,128)(2,1)S(1)}, u32[]{:S(2)}, u32[]{:S(2)}) collective-permute-start(bf16[144,128]{1,0:T(8,128)(2,1)S(1)} %get-tuple-element.73), channel_id=1, source_target_pairs={{0,12},{1,13},{2,14},{3,15},{4,0},{5,1},{6,2},{7,3},{8,4},{9,5},{1... | collective-permute-start | bytes 110600 | tf_op jit(solution)/shard_map/ppermute | solution.py:56
  139.0 2.0 %collective-permute-start.33 = (bf16[64,4096]{1,0:T(8,128)(2,1)S(1)}, bf16[64,4096]{1,0:T(8,128)(2,1)S(1)}, u32[]{:S(2)}, u32[]{:S(2)}) collective-permute-start(bf16[64,4096]{1,0:T(8,128)(2,1)S(1)} %slice.79), channel_id=1, source_target_pairs={{0,1},{1,0},{2,3},{3,2},{4,5},{5,4},{6,7},{7,6},{8,9},{9,8},{10,11... | collective-permute-start | bytes 1572872 | tf_op jit(solution)/shard_map/ppermute | solution.py:56
  141.1 8.4 %collective-permute-start.34 = (bf16[64,2048]{1,0:T(8,128)(2,1)S(1)}, bf16[64,2048]{1,0:T(8,128)(2,1)S(1)}, u32[]{:S(2)}, u32[]{:S(2)}) collective-permute-start(bf16[64,2048]{1,0:T(8,128)(2,1)S(1)} %slice.81), channel_id=1, source_target_pairs={{0,2},{1,3},{2,0},{3,1},{4,6},{5,7},{6,4},{7,5},{8,10},{9,11},{10,... | collective-permute-start | bytes 786440 | tf_op jit(solution)/shard_map/ppermute | solution.py:56
  149.6 6.4 %collective-permute-start.37 = (bf16[64,512]{1,0:T(8,128)(2,1)S(1)}, bf16[64,512]{1,0:T(8,128)(2,1)S(1)}, u32[]{:S(2)}, u32[]{:S(2)}) collective-permute-start(bf16[64,512]{1,0:T(8,128)(2,1)S(1)} %get-tuple-element.80), channel_id=1, source_target_pairs={{0,12},{1,13},{2,14},{3,15},{4,0},{5,1},{6,2},{7,3},{8,4},{9,5},{1... | collective-permute-start | bytes 196616 | tf_op jit(solution)/shard_map/ppermute | solution.py:56
  153.8 5.2 %collective-permute-start.36 = (bf16[64,512]{1,0:T(8,128)(2,1)S(1)}, bf16[64,512]{1,0:T(8,128)(2,1)S(1)}, u32[]{:S(2)}, u32[]{:S(2)}) collective-permute-start(bf16[64,512]{1,0:T(8,128)(2,1)S(1)} %get-tuple-element.81), channel_id=1, source_target_pairs={{0,8},{1,9},{2,10},{3,11},{4,12},{5,13},{6,14},{7,15},{8,0},{9,1},... | collective-permute-start | bytes 196616 | tf_op jit(solution)/shard_map/ppermute | solution.py:56
  153.8 6.1 %collective-permute-start.35 = (bf16[64,512]{1,0:T(8,128)(2,1)S(1)}, bf16[64,512]{1,0:T(8,128)(2,1)S(1)}, u32[]{:S(2)}, u32[]{:S(2)}) collective-permute-start(bf16[64,512]{1,0:T(8,128)(2,1)S(1)} %get-tuple-element.79), channel_id=1, source_target_pairs={{0,4},{1,5},{2,6},{3,7},{4,8},{5,9},{6,10},{7,11},{8,12},{9,13},{1... | collective-permute-start | bytes 196616 | tf_op jit(solution)/shard_map/ppermute | solution.py:56
  (4 other events, 6.6 us)

commit v12 on v11

--- a/solution.py
+++ b/solution.py
@@ -190,12 +190,13 @@
 AHEAD = 3
 
 
-def project(prompt, got, steps, blocks, width, pieces, kind):
+def project(prompt, got, steps, blocks, width, pieces, acc, kind):
     held = Blocks(prompt, steps, width, pieces)
+    extra = [] if acc is None else [acc]
 
     def body(block_ref, prompt_ref, got_ref, step_ref, *refs):
         weight_refs = refs[: len(held.arrays)]
-        out_ref, *scratch = refs[len(held.arrays) :]
+        out_ref, acc_held, acc_sem, *scratch = refs[len(held.arrays) + len(extra) :]
         left, weights, _ = scratch
         sources = (prompt_ref, got_ref, step_ref)
         groups = [
@@ -204,6 +205,9 @@
         for group in groups[:AHEAD]:
             for copy in group:
                 copy.start()
+        if extra:
+            before = pltpu.make_async_copy(refs[len(held.arrays)], acc_held, acc_sem.at[0])
+            before.start()
         total = None
         for i, group in enumerate(groups):
             for copy in group:
@@ -213,18 +217,25 @@
                     copy.start()
             product = jnp.dot(left[i], weights[i], preferred_element_type=jnp.float32)
             total = product if total is None else total + product
+        if extra:
+            before.wait()
+            total = total + acc_held[...]
         out_ref[...] = total.astype(kind)
 
     anywhere = pl.BlockSpec(memory_space=pl.ANY)
     return pl.pallas_call(
         body,
-        in_specs=[pl.BlockSpec(memory_space=pltpu.SMEM)] + [anywhere] * (3 + len(held.arrays)),
+        in_specs=[pl.BlockSpec(memory_space=pltpu.SMEM)] + [anywhere] * (3 + len(held.arrays) + len(extra)),
         out_specs=pl.BlockSpec(memory_space=pltpu.VMEM),
         out_shape=jax.ShapeDtypeStruct((held.height, held.columns), kind),
-        scratch_shapes=held.scratch,
+        scratch_shapes=[
+            pltpu.VMEM((held.height, held.columns) if extra else (8, HEAD_DIM), jnp.float32),
+            pltpu.SemaphoreType.DMA((1,)),
+            *held.scratch,
+        ],
         compiler_params=pltpu.CompilerParams(vmem_limit_bytes=57 * MIB),
         cost_estimate=LIGHT,
-    )(blocks, prompt, got, steps, *held.arrays)
+    )(blocks, prompt, got, steps, *held.arrays, *extra)
 
 
 NOTES = 16
@@ -526,24 +537,9 @@
     def behind(k):
         return by_place([order[(order.index(a) - k) % deep] for a in range(deep)])
 
-    def halves(weight):
-        low, high = weight[:, :half], weight[:, half:]
-        return jnp.where(first, low, high), jnp.where(first, high, low)
-
-    key_mine, key_other = halves(key_weight)
-    value_mine, value_other = halves(value_weight)
-
-    step_place = PROMPT_PAGES * PAGE + jnp.arange(2, dtype=jnp.int32)
-    step_tables = tuple(t[:, None, :] for t in rope_tables(step_place))
-    flat_tables = [
-        jnp.repeat(jnp.concatenate([sign * table, table], axis=-1)[:, 0], samples, axis=0)
-        for sign, table in zip((1, -1), step_tables)
-    ]
-    queries = project_queries(wide_states, query_weight, *flat_tables)
-    packed_queries = jnp.concatenate(
-        jnp.split(queries, half // queries.shape[1], axis=0), axis=1
-    )
-    packed = packed_queries.shape[0]
+    low = jnp.concatenate([key_weight[:, :half], value_weight[:, :half]])
+    high = jnp.concatenate([key_weight[:, half:], value_weight[:, half:]])
+    both_mine, both_other = jnp.where(first, low, high), jnp.where(first, high, low)
 
     own_pages = jnp.concatenate(
         [
@@ -562,11 +558,24 @@
     positions = (slots % PROMPT_PAGES * PAGE)[:, None] + jnp.arange(PAGE, dtype=jnp.int32)[None, :]
     cosine, sine_part = rope_tables(positions.reshape(chip_rows))
 
+    step_place = PROMPT_PAGES * PAGE + jnp.arange(2, dtype=jnp.int32)
+    step_tables = tuple(t[:, None, :] for t in rope_tables(step_place))
+    flat_tables = [
+        jnp.repeat(jnp.concatenate([sign * table, table], axis=-1)[:, 0], samples, axis=0)
+        for sign, table in zip((1, -1), step_tables)
+    ]
+    queries = project_queries(
+        after(wide_states, (cosine, sine_part)), query_weight, *flat_tables
+    )
+    packed_queries = jnp.concatenate(
+        jnp.split(queries, half // queries.shape[1], axis=0), axis=1
+    )
+    packed = packed_queries.shape[0]
+
     places = [(k, flip) for k in range(deep) for flip in (0, 1)]
     own_blocks = jnp.stack([block(behind(k), flip, own_c) for k, flip in places])
     query_turns = jnp.stack([(own_turn + deep - order.index(a)) % deep for a in range(deep)])
     own_place = (own_kv + jnp.where(first, 0, KV_HEADS // 2)) % KV_HEADS * HEAD_DIM
-    prepared = (cosine, sine_part, kv_places, query_turns)
     done = {}
 
     def send(move, value):
@@ -575,24 +584,20 @@
         return moved[-1]
 
     got = in_chip(prompt_states)
-    key_z, mine, theirs = {0: key_mine}, {0: value_mine}, {}
-    key_z[1] = send(along_ring, key_z[0])
-    mine[1] = send(along_ring, mine[0])
-    value_y = send(along_y, value_mine)
-    key_full = {0: jnp.concatenate([key_mine, key_other, packed_queries])}
-    key_y = {0: send(along_y, after(key_full[0], (value_y, key_z[1])))}
+    both_z, both_x, theirs, theirs_x = {0: both_mine}, {0: both_other}, {}, {}
+    both_z[1] = send(along_ring, both_mine)
+    value_y = send(along_y, both_mine[width:])
+    key_full = {0: jnp.concatenate([both_mine[:width], both_other[:width], packed_queries])}
+    key_y = {0: send(along_y, after(key_full[0], value_y))}
     theirs[0] = jnp.concatenate([value_y, packed_queries, key_y[0][2 * width :]])
-    mine_x, theirs_x = {0: value_other}, {}
     for k in range(1, deep):
-        swapped = send(along_x, after(key_z[k], packed_queries))
-        mine_x[k] = send(along_x, mine[k])
+        if k + 1 < deep:
+            both_z[k + 1] = send(along_ring, both_z[k])
+        both_x[k] = send(along_x, both_z[k])
         if k == 1:
             theirs_x[0] = send(along_x, value_y)
-        if k + 1 < deep:
-            key_z[k + 1] = send(along_ring, key_z[k])
-            mine[k + 1] = send(along_ring, mine[k])
-        key_full[k] = jnp.concatenate([key_z[k], swapped])
-        key_y[k] = send(along_y, after(key_full[k], (key_y[k - 1], prepared if k == 2 else ())))
+        key_full[k] = jnp.concatenate([both_z[k][:width], both_x[k][:width]])
+        key_y[k] = send(along_y, after(key_full[k], key_y[k - 1]))
     for k in range(1, deep):
         theirs[k] = send(along_ring, theirs[k - 1])
         theirs_x[k] = send(along_x, theirs[k])
@@ -605,21 +610,25 @@
         [((key_y if flip else key_full)[k], start) for start in (0, width)] for k, flip in places
     ]
     value_pieces = [
-        [((theirs if flip else mine)[k], 0), ((theirs_x if flip else mine_x)[k], 0)]
+        [(theirs[k], 0), (theirs_x[k], 0)] if flip else [(both_z[k], width), (both_x[k], width)]
         for k, flip in places
     ]
 
-    def project_blocks(pieces, which, ready, kind):
+    def project_blocks(pieces, which, acc, ready, kind):
         taken = after(jnp.stack([own_blocks[i] for i in which]), ready)
         return project(
-            prompt_states, got, wide_states, taken, width, [pieces[i] for i in which], kind
+            prompt_states, got, wide_states, taken, width, [pieces[i] for i in which], acc, kind
         )
 
+    last = 2 * deep - 2
+    key_early = project_blocks(
+        key_pieces, range(last), None, (theirs_x[1], theirs[deep - 2]), jnp.float32
+    )
+    awaited = [theirs_x[k] for k in range(1, deep)]
+    key_sum = project_blocks(key_pieces, [last, last + 1], key_early, awaited, jnp.bfloat16)
     early = [*range(0, 2 * deep, 2), 1]
     late = [i for i in range(2 * deep) if i not in early]
-    value_early = project_blocks(value_pieces, early, (theirs_x[1], theirs[deep - 2]), jnp.float32)
-    awaited = (value_early, theirs[deep - 1], [theirs_x[k] for k in range(1, deep - 1)])
-    key_sum = project_blocks(key_pieces, range(2 * deep), awaited, jnp.bfloat16)
+    value_early = project_blocks(value_pieces, early, None, key_sum, jnp.float32)
     key_back = in_chip(key_sum)
 
     def own_head(sums):

time: 161 us -> 157 us (0.975)
  starting transfers between devices: 61.8 us -> 50.6 us
  waiting for transfers between devices: 46.1 us -> 50.4 us
  Pallas kernels: 32.8 us -> 36.9 us
    ppermute x38 -> x32, starting transfers between devices: 61.8 us -> 50.6 us  [move(): return lax.ppermute(value, ('groups', 'sample'), pairs)]
    ppermute x38 -> x32, waiting for transfers between devices: 46.1 us -> 50.4 us  [move(): return lax.ppermute(value, ('groups', 'sample'), pairs)]
    pallas_call x2 -> x3, Pallas kernels: 16.8 us -> 20.9 us  [project(): pl.pallas_call(body, in_specs=[pl.BlockSpec(memory_space=pltpu.SMEM)] + [...]
    unnamed x63 -> x58, local copies, waits for them, and re-layouts: 5.79 us -> 3.43 us
    slice x0 -> x9, local copies, waits for them, and re-layouts: none -> 2.22 us  [the longest x1 1.25 us: on_device(): low = jnp.concatenate([key_weight[:, :half], value_weight[:, :half]])]
    select_n x2 -> x1, other arithmetic: 1.92 us -> 0.19 us  [on_device(): jnp.where(first, low, high)]
  transfers between devices with their start and end apart: 38 -> 32, of which waited for: 20 -> 17; matrix products, arithmetic and copies ran while one was open for 8% -> 8% of each run, Pallas kernels for 6% -> 12%
where the time goes in v12:
time: 157 us
  starting transfers between devices  50.6 us (32%)
  waiting for transfers between devices  50.4 us (32%)
  Pallas kernels  36.9 us (24%)
  local copies, waits for them, and re-layouts  9.8 us (6%)
  other arithmetic  8.74 us (6%)
    ppermute x32, starting transfers between devices, move(): return lax.ppermute(value, ('groups', 'sample'), pairs)  50.6 us
    ppermute x32, waiting for transfers between devices, move(): return lax.ppermute(value, ('groups', 'sample'), pairs)  50.4 us
    pallas_call x3, Pallas kernels, project(): pl.pallas_call(body, in_specs=[pl.BlockSpec(memory_space=pltpu.SMEM)] + [...  20.9 us
    pallas_call x1, Pallas kernels, attend(): pl.pallas_call(body, in_specs=[pl.BlockSpec(memory_space=pltpu.SMEM)] * 3...  11.8 us
    unnamed x58, local copies, waits for them, and re-layouts  3.43 us
  transfers between devices with their start and end apart: 32, of which 17 were waited for; matrix products, arithmetic and copies ran while one was open for 8% of the time, Pallas kernels for 12%

profile of v12, /device:TPU:0, one launch (start us, length us, event | category | flops | bytes accessed | tf_op | source)
XLA Modules:
  0.0 157.1 jit_solution(2506977468219731033)
XLA Ops:
  0.5 1.3 fusion.5
  2.0 3.6 %collective-permute-start.2 = (bf16[1024,256]{1,0:T(8,128)(2,1)S(1)}, bf16[1024,256]{1,0:T(8,128)(2,1)S(1)}, u32[]{:S(2)}, u32[]{:S(2)}) collective-permute-start(bf16[1024,256]{1,0:T(8,128)(2,1)S(1)} %get-tuple-element.61.refs_0_), channel_id=1, source_target_pairs={{0,8},{1,9},{2,10},{3,11},{4,0},{5,1},{6,2},{7,3},{8,12},{9,13},{1... | collective-permute-start | bytes 1572872 | tf_op jit(solution)/shard_map/ppermute | solution.py:56
  5.6 0.8 fusion.4
  6.4 1.5 collective-permute-start
  8.4 3.1 %multiply_sine_fusion = (f32[1024,64]{1,0:T(8,128)}, f32[1024,64]{1,0:T(8,128)}) fusion(f32[64]{0:T(128)S(1)} %multiply_power_fusion, f32[1024]{0:T(1024)S(1)} %convert_bitcast_fusion), kind=kLoop, calls=%fused_computation.1 | loop fusion | flops 65536 | bytes 528640 | tf_op jit(solution)/shard_map/sin | solution.py:23
  11.7 2.2 %copy-done.1 = bf16[8192,256]{1,0:T(8,128)(2,1)S(1)} copy-done((bf16[8192,256]{1,0:T(8,128)(2,1)S(1)}, bf16[8192,256]{1,0:T(8,128)(2,1)}, u32[]{:S(2)}) %copy-start.1) | copy-done | bytes 4194328
  13.9 2.0 %shard_map.73.refs_4_ = bf16[64,256]{1,0:T(8,128)(2,1)S(1)} custom-call(bf16[64,8192]{1,0:T(8,128)(2,1)S(1)} %bitcast.51, bf16[8192,256]{1,0:T(8,128)(2,1)S(1)} %copy-done.1, f32[64,128]{1,0:T(8,128)S(1)} %bitcast.54, f32[64,128]{1,0:T(8,128)S(1)} %bitcast.55), custom_call_target="tpu_custom_call" | custom-call | flops 1 | bytes 1 | tf_op jit(solution)/shard_map/pallas_call | solution.py:106
  15.9 1.6 collective-permute-done.2.refs_2_
  17.4 1.5 collective-permute-start.9
  18.9 3.4 %collective-permute-start.3 = (bf16[1024,256]{1,0:T(8,128)(2,1)S(1)}, bf16[1024,256]{1,0:T(8,128)(2,1)S(1)}, u32[]{:S(2)}, u32[]{:S(2)}) collective-permute-start(bf16[1024,256]{1,0:T(8,128)(2,1)S(1)} %collective-permute-done.2.refs_2_), channel_id=1, source_target_pairs={{0,8},{1,9},{2,10},{3,11},{4,0},{5,1},{6,2},{7,3},{8,12},{9,13},{1... | collective-permute-start | bytes 1572872 | tf_op jit(solution)/shard_map/ppermute | solution.py:56
  22.4 1.6 %collective-permute-start.1 = (bf16[1088,256]{1,0:T(8,128)(2,1)S(1)}, bf16[1088,256]{1,0:T(8,128)(2,1)S(1)}, u32[]{:S(2)}, u32[]{:S(2)}) collective-permute-start(bf16[1088,256]{1,0:T(8,128)(2,1)S(1)} %pad_maximum_fusion.refs_0_), channel_id=1, source_target_pairs={{0,2},{1,3},{2,0},{3,1},{4,6},{5,7},{6,4},{7,5},{8,10},{9,11},{10,... | collective-permute-start | bytes 1671176 | tf_op jit(solution)/shard_map/ppermute | solution.py:56
  24.0 0.5 collective-permute-start.12
  24.5 7.8 %collective-permute-done.9.refs_3_ = bf16[1024,256]{1,0:T(8,128)(2,1)S(1)} collective-permute-done((bf16[1024,256]{1,0:T(8,128)(2,1)S(1)}, bf16[1024,256]{1,0:T(8,128)(2,1)S(1)}, u32[]{:S(2)}, u32[]{:S(2)}) %collective-permute-start.9) | collective-permute-done | bytes 524320 | tf_op jit(solution)/shard_map/ppermute | solution.py:56
  32.3 0.8 collective-permute-done.3.refs_4_
  33.1 0.7 collective-permute-start.10
  33.8 3.4 %collective-permute-start.5 = (bf16[1024,256]{1,0:T(8,128)(2,1)S(1)}, bf16[1024,256]{1,0:T(8,128)(2,1)S(1)}, u32[]{:S(2)}, u32[]{:S(2)}) collective-permute-start(bf16[1024,256]{1,0:T(8,128)(2,1)S(1)} %collective-permute-done.3.refs_4_), channel_id=1, source_target_pairs={{0,8},{1,9},{2,10},{3,11},{4,0},{5,1},{6,2},{7,3},{8,12},{9,13},{1... | collective-permute-start | bytes 1572872 | tf_op jit(solution)/shard_map/ppermute | solution.py:56
  37.3 1.6 %collective-permute-start.17 = (bf16[1024,256]{1,0:T(8,128)(2,1)S(1)}, bf16[1024,256]{1,0:T(8,128)(2,1)S(1)}, u32[]{:S(2)}, u32[]{:S(2)}) collective-permute-start(bf16[1024,256]{1,0:T(8,128)(2,1)S(1)} %pad_maximum_fusion.5.refs_2_), channel_id=1, source_target_pairs={{0,2},{1,3},{2,0},{3,1},{4,6},{5,7},{6,4},{7,5},{8,10},{9,11},{10,... | collective-permute-start | bytes 1572872 | tf_op jit(solution)/shard_map/ppermute | solution.py:56
  38.9 1.0 pad_maximum_fusion.6.refs_0_.refs_8_
  39.9 1.5 collective-permute-start.4
  41.4 8.2 %collective-permute-done.5.refs_6_ = bf16[1024,256]{1,0:T(8,128)(2,1)S(1)} collective-permute-done((bf16[1024,256]{1,0:T(8,128)(2,1)S(1)}, bf16[1024,256]{1,0:T(8,128)(2,1)S(1)}, u32[]{:S(2)}, u32[]{:S(2)}) %collective-permute-start.5) | collective-permute-done | bytes 524320 | tf_op jit(solution)/shard_map/ppermute | solution.py:56
  49.6 1.3 collective-permute-start.13
  51.0 1.6 %collective-permute-start.18 = (bf16[1024,256]{1,0:T(8,128)(2,1)S(1)}, bf16[1024,256]{1,0:T(8,128)(2,1)S(1)}, u32[]{:S(2)}, u32[]{:S(2)}) collective-permute-start(bf16[1024,256]{1,0:T(8,128)(2,1)S(1)} %pad_maximum_fusion.4.refs_4_), channel_id=1, source_target_pairs={{0,2},{1,3},{2,0},{3,1},{4,6},{5,7},{6,4},{7,5},{8,10},{9,11},{10,... | collective-permute-start | bytes 1572872 | tf_op jit(solution)/shard_map/ppermute | solution.py:56
  52.6 1.0 collective-permute-done.4.refs_1_.refs_10_
  53.6 3.4 %collective-permute-start.6 = (bf16[640,256]{1,0:T(8,128)(2,1)S(1)}, bf16[640,256]{1,0:T(8,128)(2,1)S(1)}, u32[]{:S(2)}, u32[]{:S(2)}) collective-permute-start(bf16[640,256]{1,0:T(8,128)(2,1)S(1)} %collective-permute-done.4.refs_1_.refs_10_), channel_id=1, source_target_pairs={{0,8},{1,9},{2,10},{3,11},{4,0},{5,1},{6,2},{7,3},{8,12},{9,13},{1... | collective-permute-start | bytes 983048 | tf_op jit(solution)/shard_map/ppermute | solution.py:56
  57.0 1.5 collective-permute-start.11
  58.5 3.6 %collective-permute-done.6.refs_2_.refs_12_ = bf16[640,256]{1,0:T(8,128)(2,1)S(1)} collective-permute-done((bf16[640,256]{1,0:T(8,128)(2,1)S(1)}, bf16[640,256]{1,0:T(8,128)(2,1)S(1)}, u32[]{:S(2)}, u32[]{:S(2)}) %collective-permute-start.6) | collective-permute-done | bytes 327712 | tf_op jit(solution)/shard_map/ppermute | solution.py:56
  62.1 3.4 %collective-permute-start.7 = (bf16[640,256]{1,0:T(8,128)(2,1)S(1)}, bf16[640,256]{1,0:T(8,128)(2,1)S(1)}, u32[]{:S(2)}, u32[]{:S(2)}) collective-permute-start(bf16[640,256]{1,0:T(8,128)(2,1)S(1)} %collective-permute-done.6.refs_2_.refs_12_), channel_id=1, source_target_pairs={{0,8},{1,9},{2,10},{3,11},{4,0},{5,1},{6,2},{7,3},{8,12},{9,13},{1... | collective-permute-start | bytes 983048 | tf_op jit(solution)/shard_map/ppermute | solution.py:56
  65.6 1.6 %collective-permute-start.19 = (bf16[1024,256]{1,0:T(8,128)(2,1)S(1)}, bf16[1024,256]{1,0:T(8,128)(2,1)}, u32[]{:S(2)}, u32[]{:S(2)}) collective-permute-start(bf16[1024,256]{1,0:T(8,128)(2,1)S(1)} %pad_maximum_fusion.3.refs_0_), channel_id=1, source_target_pairs={{0,2},{1,3},{2,0},{3,1},{4,6},{5,7},{6,4},{7,5},{8,10},{9,11},{10,... | collective-permute-start | bytes 1572872 | tf_op jit(solution)/shard_map/ppermute | solution.py:56
  67.2 1.3 collective-permute-start.14
  68.5 1.5 collective-permute-done.7.refs_3_.refs_14_
  70.1 1.4 collective-permute-start.15
  71.4 0.6 stack.134.block_ref
  72.0 0.6 pad_add_fusion.3.block_ref
  72.7 4.1 %collective-permute-done.14.refs_13_ = bf16[640,256]{1,0:T(8,128)(2,1)} collective-permute-done((bf16[640,256]{1,0:T(8,128)(2,1)S(1)}, bf16[640,256]{1,0:T(8,128)(2,1)}, u32[]{:S(2)}, u32[]{:S(2)}) %collective-permute-start.14) | collective-permute-done | bytes 327712 | tf_op jit(solution)/shard_map/ppermute | solution.py:56
  76.8 3.5 %collective-permute-done.15.refs_15_ = bf16[640,256]{1,0:T(8,128)(2,1)} collective-permute-done((bf16[640,256]{1,0:T(8,128)(2,1)S(1)}, bf16[640,256]{1,0:T(8,128)(2,1)}, u32[]{:S(2)}, u32[]{:S(2)}) %collective-permute-start.15) | collective-permute-done | bytes 327712 | tf_op jit(solution)/shard_map/ppermute | solution.py:56
  80.3 8.2 %shard_map.75.refs_2_ = f32[1088,512]{1,0:T(8,128)} custom-call(s32[6]{0:T(128)} %stack.134.block_ref, bf16[512,8192]{1,0:T(8,128)(2,1)} %refs_6_.1, bf16[512,8192]{1,0:T(8,128)(2,1)} %collective-permute-done.16.got_ref.refs_7_, bf16[64,8192]{1,0:T(8,128)(2,1)} %bitcast.47, bf16[1088,256]{1,0:T(8,128)(2,1)} %copy-done.11, bf16[1088,256]{1,0:T(8,128)(2,1)} %copy-done.23, ...), custom_call_target="tpu_custom_call" | custom-call | flops 1 | bytes 1 | tf_op jit(solution)/shard_map/pallas_call | solution.py:226
  88.5 5.2 %shard_map.76.refs_2_ = bf16[1088,512]{1,0:T(8,128)(2,1)} custom-call(s32[2]{0:T(128)} %pad_add_fusion.3.block_ref, bf16[512,8192]{1,0:T(8,128)(2,1)} %refs_6_.1, bf16[512,8192]{1,0:T(8,128)(2,1)} %collective-permute-done.16.got_ref.refs_7_, bf16[64,8192]{1,0:T(8,128)(2,1)} %bitcast.48, bf16[1024,256]{1,0:T(8,128)(2,1)} %copy-done.14, ...), custom_call_target="tpu_custom_call" | custom-call | flops 1 | bytes 1 | tf_op jit(solution)/shard_map/pallas_call | solution.py:226
  94.2 0.5 collective-permute-start.8
  94.8 0.6 stack.135.block_ref
  95.5 0.6 pad_add_fusion.1.block_ref
  96.1 0.7 and_select_fusion.1
  96.8 7.5 %shard_map.77.refs_9_ = f32[1088,512]{1,0:T(8,128)} custom-call(s32[5]{0:T(128)} %stack.135.block_ref, bf16[512,8192]{1,0:T(8,128)(2,1)} %refs_6_.1, bf16[512,8192]{1,0:T(8,128)(2,1)} %collective-permute-done.16.got_ref.refs_7_, bf16[64,8192]{1,0:T(8,128)(2,1)} %bitcast.49, bf16[1024,256]{1,0:T(8,128)(2,1)} %copy-done.9, bf16[1024,256]{1,0:T(8,128)(2,1)} %copy-done.10, ...), custom_call_target="tpu_custom_call" | custom-call | flops 1 | bytes 1 | tf_op jit(solution)/shard_map/pallas_call | solution.py:226
  104.3 0.7 copy-done.27
  105.5 11.8 %shard_map.78 = (bf16[4,4,144,128]{3,2,1,0:T(8,128)(2,1)}, f32[64,512]{1,0:T(8,128)}) custom-call(s32[4]{0:T(128)} %get-tuple-element.81.place_ref, s32[4]{0:T(128)} %get-tuple-element.82.turn_ref, s32[3]{0:T(128)} %pad_add_fusion.1.block_ref, bf16[4,128,256]{2,1,0:T(8,128)(2,1)} %copy-done.8, bf16[4,128,256]{2,1,0:T(8,128)(2,1)} %copy-done.27, ...), custom_call_target="tpu_custom_call" | custom-call | flops 1 | bytes 1 | tf_op jit(solution)/shard_map/pallas_call | solution.py:414
  117.3 1.0 slice_bitcast_fusion
  118.6 0.8 slice.119
  119.4 0.5 collective-permute-start.26
  119.9 0.8 slice.120
  120.8 1.6 %collective-permute-start.22 = (bf16[4,144,128]{2,1,0:T(8,128)(2,1)S(1)}, bf16[4,144,128]{2,1,0:T(8,128)(2,1)S(1)}, u32[]{:S(2)}, u32[]{:S(2)}) collective-permute-start(bf16[4,144,128]{2,1,0:T(8,128)(2,1)S(1)} %get-tuple-element.55), channel_id=1, source_target_pairs={{0,2},{1,3},{2,0},{3,1},{4,6},{5,7},{6,4},{7,5},{8,10},{9,11},{10,... | collective-permute-start | bytes 442376 | tf_op jit(solution)/shard_map/ppermute | solution.py:56
  122.6 4.1 %collective-permute-done.22.far_ref = bf16[4,144,128]{2,1,0:T(8,128)(2,1)S(1)} collective-permute-done((bf16[4,144,128]{2,1,0:T(8,128)(2,1)S(1)}, bf16[4,144,128]{2,1,0:T(8,128)(2,1)S(1)}, u32[]{:S(2)}, u32[]{:S(2)}) %collective-permute-start.22) | collective-permute-done | bytes 147488 | tf_op jit(solution)/shard_map/ppermute | solution.py:56
  126.8 2.4 %collective-permute-start.23 = (bf16[144,128]{1,0:T(8,128)(2,1)S(1)}, bf16[144,128]{1,0:T(8,128)(2,1)S(1)}, u32[]{:S(2)}, u32[]{:S(2)}) collective-permute-start(bf16[144,128]{1,0:T(8,128)(2,1)S(1)} %get-tuple-element.57), channel_id=1, source_target_pairs={{0,4},{1,5},{2,6},{3,7},{4,8},{5,9},{6,10},{7,11},{8,12},{9,13},{1... | collective-permute-start | bytes 110600 | tf_op jit(solution)/shard_map/ppermute | solution.py:56
  129.2 1.7 %collective-permute-start.24 = (bf16[144,128]{1,0:T(8,128)(2,1)S(1)}, bf16[144,128]{1,0:T(8,128)(2,1)S(1)}, u32[]{:S(2)}, u32[]{:S(2)}) collective-permute-start(bf16[144,128]{1,0:T(8,128)(2,1)S(1)} %get-tuple-element.58), channel_id=1, source_target_pairs={{0,8},{1,9},{2,10},{3,11},{4,12},{5,13},{6,14},{7,15},{8,0},{9,1},... | collective-permute-start | bytes 110600 | tf_op jit(solution)/shard_map/ppermute | solution.py:56
  130.9 2.2 %collective-permute-start.25 = (bf16[144,128]{1,0:T(8,128)(2,1)S(1)}, bf16[144,128]{1,0:T(8,128)(2,1)S(1)}, u32[]{:S(2)}, u32[]{:S(2)}) collective-permute-start(bf16[144,128]{1,0:T(8,128)(2,1)S(1)} %get-tuple-element.59), channel_id=1, source_target_pairs={{0,12},{1,13},{2,14},{3,15},{4,0},{5,1},{6,2},{7,3},{8,4},{9,5},{1... | collective-permute-start | bytes 110600 | tf_op jit(solution)/shard_map/ppermute | solution.py:56
  133.1 0.8 fusion.refs_6_
  134.1 0.8 collective-permute-done.25.refs_3_
  134.9 1.7 %shard_map.81 = bf16[64,8192]{1,0:T(8,128)(2,1)S(1)} custom-call(s32[16]{0:T(128)S(1)} %stack.118.block_ref, bf16[144,128]{1,0:T(8,128)(2,1)S(1)} %get-tuple-element.56.refs_0_, bf16[144,128]{1,0:T(8,128)(2,1)S(1)} %collective-permute-done.23.refs_1_, bf16[144,128]{1,0:T(8,128)(2,1)S(1)} %collective-permute-done.24.refs_2_, ...), custom_call_target="tpu_custom_call" | custom-call | flops 1 | bytes 1 | tf_op jit(solution)/shard_map/pallas_call | solution.py:265
  136.7 1.9 %collective-permute-done.27 = bf16[64,4096]{1,0:T(8,128)(2,1)S(1)} collective-permute-done((bf16[64,4096]{1,0:T(8,128)(2,1)S(1)}, bf16[64,4096]{1,0:T(8,128)(2,1)S(1)}, u32[]{:S(2)}, u32[]{:S(2)}) %collective-permute-start.27) | collective-permute-done | bytes 524320 | tf_op jit(solution)/shard_map/ppermute | solution.py:56
  138.7 1.6 %collective-permute-start.28 = (bf16[64,2048]{1,0:T(8,128)(2,1)S(1)}, bf16[64,2048]{1,0:T(8,128)(2,1)S(1)}, u32[]{:S(2)}, u32[]{:S(2)}) collective-permute-start(bf16[64,2048]{1,0:T(8,128)(2,1)S(1)} %slice.126), channel_id=1, source_target_pairs={{0,2},{1,3},{2,0},{3,1},{4,6},{5,7},{6,4},{7,5},{8,10},{9,11},{10,... | collective-permute-start | bytes 786440 | tf_op jit(solution)/shard_map/ppermute | solution.py:56
  140.3 6.8 %collective-permute-done.28 = bf16[64,2048]{1,0:T(8,128)(2,1)S(1)} collective-permute-done((bf16[64,2048]{1,0:T(8,128)(2,1)S(1)}, bf16[64,2048]{1,0:T(8,128)(2,1)S(1)}, u32[]{:S(2)}, u32[]{:S(2)}) %collective-permute-start.28) | collective-permute-done | bytes 262176 | tf_op jit(solution)/shard_map/ppermute | solution.py:56
  147.2 0.8 collective-permute-start.29
  148.1 3.8 %collective-permute-start.30 = (bf16[64,512]{1,0:T(8,128)(2,1)S(1)}, bf16[64,512]{1,0:T(8,128)(2,1)S(1)}, u32[]{:S(2)}, u32[]{:S(2)}) collective-permute-start(bf16[64,512]{1,0:T(8,128)(2,1)S(1)} %get-tuple-element.71), channel_id=1, source_target_pairs={{0,8},{1,9},{2,10},{3,11},{4,12},{5,13},{6,14},{7,15},{8,0},{9,1},... | collective-permute-start | bytes 196616 | tf_op jit(solution)/shard_map/ppermute | solution.py:56
  151.9 2.4 %collective-permute-done.29 = bf16[64,512]{1,0:T(8,128)(2,1)S(1)} collective-permute-done((bf16[64,512]{1,0:T(8,128)(2,1)S(1)}, bf16[64,512]{1,0:T(8,128)(2,1)S(1)}, u32[]{:S(2)}, u32[]{:S(2)}) %collective-permute-start.29) | collective-permute-done | bytes 65568 | tf_op jit(solution)/shard_map/ppermute | solution.py:56
  154.3 1.6 %collective-permute-done.30 = bf16[64,512]{1,0:T(8,128)(2,1)S(1)} collective-permute-done((bf16[64,512]{1,0:T(8,128)(2,1)S(1)}, bf16[64,512]{1,0:T(8,128)(2,1)S(1)}, u32[]{:S(2)}, u32[]{:S(2)}) %collective-permute-start.30) | collective-permute-done | bytes 65568 | tf_op jit(solution)/shard_map/ppermute | solution.py:56
  156.4 0.7 add_convert_fusion.2
  (115 shorter events, 4.1 us)
Async XLA Ops:
  0.0 80.3 %collective-permute-start.16 = (bf16[512,8192]{1,0:T(8,128)(2,1)}, bf16[512,8192]{1,0:T(8,128)(2,1)}, u32[]{:S(2)}, u32[]{:S(2)}) collective-permute-start(bf16[512,8192]{1,0:T(8,128)(2,1)} %refs_6_.1), channel_id=1, source_target_pairs={{0,1},{1,0},{2,3},{3,2},{4,5},{5,4},{6,7},{7,6},{8,9},{9,8},{10,11... | collective-permute-start | bytes 25165832 | tf_op jit(solution)/shard_map/ppermute | solution.py:56
  1.7 6.3 %copy-start.28 = (s32[64]{0:T(128)S(1)}, s32[64]{0:T(128)}, u32[]{:S(2)}) copy-start(s32[64]{0:T(128)} %param.9) | copy-start | bytes 772
  1.9 9.7 %copy-start.9 = (bf16[1024,256]{1,0:T(8,128)(2,1)}, bf16[1024,256]{1,0:T(8,128)(2,1)S(1)}, u32[]{:S(2)}) copy-start(bf16[1024,256]{1,0:T(8,128)(2,1)S(1)} %get-tuple-element.61.refs_0_) | copy-start | bytes 1572868
  1.9 13.9 %copy-start.10 = (bf16[1024,256]{1,0:T(8,128)(2,1)}, bf16[1024,256]{1,0:T(8,128)(2,1)S(1)}, u32[]{:S(2)}) copy-start(bf16[1024,256]{1,0:T(8,128)(2,1)S(1)} %get-tuple-element.62.refs_1_) | copy-start | bytes 1572868
  1.9 9.7 %copy-start = (bf16[2,32,8192]{2,1,0:T(8,128)(2,1)S(1)}, bf16[2,32,8192]{2,1,0:T(8,128)(2,1)}, u32[]{:S(2)}) copy-start(bf16[2,32,8192]{2,1,0:T(8,128)(2,1)} %param.10) | copy-start | bytes 3145732
  2.0 15.5 %collective-permute-start.2 = (bf16[1024,256]{1,0:T(8,128)(2,1)S(1)}, bf16[1024,256]{1,0:T(8,128)(2,1)S(1)}, u32[]{:S(2)}, u32[]{:S(2)}) collective-permute-start(bf16[1024,256]{1,0:T(8,128)(2,1)S(1)} %get-tuple-element.61.refs_0_), channel_id=1, source_target_pairs={{0,8},{1,9},{2,10},{3,11},{4,0},{5,1},{6,2},{7,3},{8,12},{9,13},{1... | collective-permute-start | bytes 1572872 | tf_op jit(solution)/shard_map/ppermute | solution.py:56
  6.4 15.9 %collective-permute-start = (bf16[512,256]{1,0:T(8,128)(2,1)}, bf16[512,256]{1,0:T(8,128)(2,1)}, u32[]{:S(2)}, u32[]{:S(2)}) collective-permute-start(bf16[512,256]{1,0:T(8,128)(2,1)} %get-tuple-element.63), channel_id=1, source_target_pairs={{0,2},{1,3},{2,0},{3,1},{4,6},{5,7},{6,4},{7,5},{8,10},{9,11},{10,... | collective-permute-start | bytes 786440 | tf_op jit(solution)/shard_map/ppermute | solution.py:56
  11.7 2.2 %copy-start.1 = (bf16[8192,256]{1,0:T(8,128)(2,1)S(1)}, bf16[8192,256]{1,0:T(8,128)(2,1)}, u32[]{:S(2)}) copy-start(bf16[8192,256]{1,0:T(8,128)(2,1)} %weight_ref.1) | copy-start | bytes 12582916
  13.9 8.5 %copy-start.22 = (bf16[512,256]{1,0:T(8,128)(2,1)S(1)}, bf16[512,256]{1,0:T(8,128)(2,1)}, u32[]{:S(2)}) copy-start(bf16[512,256]{1,0:T(8,128)(2,1)} %get-tuple-element.64) | copy-start | bytes 786436
  17.4 19.8 %copy-start.16 = (bf16[1024,256]{1,0:T(8,128)(2,1)}, bf16[1024,256]{1,0:T(8,128)(2,1)S(1)}, u32[]{:S(2)}) copy-start(bf16[1024,256]{1,0:T(8,128)(2,1)S(1)} %collective-permute-done.2.refs_2_) | copy-start | bytes 1572868
  17.4 14.8 %collective-permute-start.9 = (bf16[1024,256]{1,0:T(8,128)(2,1)S(1)}, bf16[1024,256]{1,0:T(8,128)(2,1)S(1)}, u32[]{:S(2)}, u32[]{:S(2)}) collective-permute-start(bf16[1024,256]{1,0:T(8,128)(2,1)S(1)} %collective-permute-done.2.refs_2_), channel_id=1, source_target_pairs={{0,16},{1,17},{2,18},{3,19},{4,20},{5,21},{6,22},{7,23},{8,24},{9,... | collective-permute-start | bytes 1572872 | tf_op jit(solution)/shard_map/ppermute | solution.py:56
  18.9 14.2 %collective-permute-start.3 = (bf16[1024,256]{1,0:T(8,128)(2,1)S(1)}, bf16[1024,256]{1,0:T(8,128)(2,1)S(1)}, u32[]{:S(2)}, u32[]{:S(2)}) collective-permute-start(bf16[1024,256]{1,0:T(8,128)(2,1)S(1)} %collective-permute-done.2.refs_2_), channel_id=1, source_target_pairs={{0,8},{1,9},{2,10},{3,11},{4,0},{5,1},{6,2},{7,3},{8,12},{9,13},{1... | collective-permute-start | bytes 1572872 | tf_op jit(solution)/shard_map/ppermute | solution.py:56
  22.4 17.5 %copy-start.11 = (bf16[1088,256]{1,0:T(8,128)(2,1)}, bf16[1088,256]{1,0:T(8,128)(2,1)S(1)}, u32[]{:S(2)}) copy-start(bf16[1088,256]{1,0:T(8,128)(2,1)S(1)} %pad_maximum_fusion.refs_0_) | copy-start | bytes 1671172
  22.4 14.9 %collective-permute-start.1 = (bf16[1088,256]{1,0:T(8,128)(2,1)S(1)}, bf16[1088,256]{1,0:T(8,128)(2,1)S(1)}, u32[]{:S(2)}, u32[]{:S(2)}) collective-permute-start(bf16[1088,256]{1,0:T(8,128)(2,1)S(1)} %pad_maximum_fusion.refs_0_), channel_id=1, source_target_pairs={{0,2},{1,3},{2,0},{3,1},{4,6},{5,7},{6,4},{7,5},{8,10},{9,11},{10,... | collective-permute-start | bytes 1671176 | tf_op jit(solution)/shard_map/ppermute | solution.py:56
  24.0 15.9 %collective-permute-start.12 = (bf16[512,256]{1,0:T(8,128)(2,1)}, bf16[512,256]{1,0:T(8,128)(2,1)}, u32[]{:S(2)}, u32[]{:S(2)}) collective-permute-start(bf16[512,256]{1,0:T(8,128)(2,1)} %collective-permute-done), channel_id=1, source_target_pairs={{0,16},{1,17},{2,18},{3,19},{4,20},{5,21},{6,22},{7,23},{8,24},{9,... | collective-permute-start | bytes 786440 | tf_op jit(solution)/shard_map/ppermute | solution.py:56
  32.3 4.9 %copy-start.17 = (bf16[1024,256]{1,0:T(8,128)(2,1)}, bf16[1024,256]{1,0:T(8,128)(2,1)S(1)}, u32[]{:S(2)}) copy-start(bf16[1024,256]{1,0:T(8,128)(2,1)S(1)} %collective-permute-done.9.refs_3_) | copy-start | bytes 1572868
  33.1 8.3 %copy-start.18 = (bf16[1024,256]{1,0:T(8,128)(2,1)}, bf16[1024,256]{1,0:T(8,128)(2,1)S(1)}, u32[]{:S(2)}) copy-start(bf16[1024,256]{1,0:T(8,128)(2,1)S(1)} %collective-permute-done.3.refs_4_) | copy-start | bytes 1572868
  33.1 17.8 %collective-permute-start.10 = (bf16[1024,256]{1,0:T(8,128)(2,1)S(1)}, bf16[1024,256]{1,0:T(8,128)(2,1)S(1)}, u32[]{:S(2)}, u32[]{:S(2)}) collective-permute-start(bf16[1024,256]{1,0:T(8,128)(2,1)S(1)} %collective-permute-done.3.refs_4_), channel_id=1, source_target_pairs={{0,16},{1,17},{2,18},{3,19},{4,20},{5,21},{6,22},{7,23},{8,24},{9,... | collective-permute-start | bytes 1572872 | tf_op jit(solution)/shard_map/ppermute | solution.py:56
  33.8 15.8 %collective-permute-start.5 = (bf16[1024,256]{1,0:T(8,128)(2,1)S(1)}, bf16[1024,256]{1,0:T(8,128)(2,1)S(1)}, u32[]{:S(2)}, u32[]{:S(2)}) collective-permute-start(bf16[1024,256]{1,0:T(8,128)(2,1)S(1)} %collective-permute-done.3.refs_4_), channel_id=1, source_target_pairs={{0,8},{1,9},{2,10},{3,11},{4,0},{5,1},{6,2},{7,3},{8,12},{9,13},{1... | collective-permute-start | bytes 1572872 | tf_op jit(solution)/shard_map/ppermute | solution.py:56
  37.3 13.7 %copy-start.12 = (bf16[1024,256]{1,0:T(8,128)(2,1)}, bf16[1024,256]{1,0:T(8,128)(2,1)S(1)}, u32[]{:S(2)}) copy-start(bf16[1024,256]{1,0:T(8,128)(2,1)S(1)} %pad_maximum_fusion.5.refs_2_) | copy-start | bytes 1572868
  37.3 13.7 %copy-start.23 = (bf16[1088,256]{1,0:T(8,128)(2,1)}, bf16[1088,256]{1,0:T(8,128)(2,1)S(1)}, u32[]{:S(2)}) copy-start(bf16[1088,256]{1,0:T(8,128)(2,1)S(1)} %collective-permute-done.1.refs_1_) | copy-start | bytes 1671172
  37.3 13.7 %collective-permute-start.17 = (bf16[1024,256]{1,0:T(8,128)(2,1)S(1)}, bf16[1024,256]{1,0:T(8,128)(2,1)S(1)}, u32[]{:S(2)}, u32[]{:S(2)}) collective-permute-start(bf16[1024,256]{1,0:T(8,128)(2,1)S(1)} %pad_maximum_fusion.5.refs_2_), channel_id=1, source_target_pairs={{0,2},{1,3},{2,0},{3,1},{4,6},{5,7},{6,4},{7,5},{8,10},{9,11},{10,... | collective-permute-start | bytes 1572872 | tf_op jit(solution)/shard_map/ppermute | solution.py:56
  39.9 53.9 %copy-start.3 = (bf16[640,256]{1,0:T(8,128)(2,1)}, bf16[640,256]{1,0:T(8,128)(2,1)S(1)}, u32[]{:S(2)}) copy-start(bf16[640,256]{1,0:T(8,128)(2,1)S(1)} %pad_maximum_fusion.6.refs_0_.refs_8_) | copy-start | bytes 983044
  39.9 13.7 %collective-permute-start.4 = (bf16[640,256]{1,0:T(8,128)(2,1)S(1)}, bf16[640,256]{1,0:T(8,128)(2,1)S(1)}, u32[]{:S(2)}, u32[]{:S(2)}) collective-permute-start(bf16[640,256]{1,0:T(8,128)(2,1)S(1)} %pad_maximum_fusion.6.refs_0_.refs_8_), channel_id=1, source_target_pairs={{0,8},{1,9},{2,10},{3,11},{4,0},{5,1},{6,2},{7,3},{8,12},{9,13},{1... | collective-permute-start | bytes 983048 | tf_op jit(solution)/shard_map/ppermute | solution.py:56
  49.6 15.9 %copy-start.20 = (bf16[1024,256]{1,0:T(8,128)(2,1)}, bf16[1024,256]{1,0:T(8,128)(2,1)S(1)}, u32[]{:S(2)}) copy-start(bf16[1024,256]{1,0:T(8,128)(2,1)S(1)} %collective-permute-done.5.refs_6_) | copy-start | bytes 1572868
  49.6 15.9 %collective-permute-start.13 = (bf16[1024,256]{1,0:T(8,128)(2,1)S(1)}, bf16[1024,256]{1,0:T(8,128)(2,1)S(1)}, u32[]{:S(2)}, u32[]{:S(2)}) collective-permute-start(bf16[1024,256]{1,0:T(8,128)(2,1)S(1)} %collective-permute-done.5.refs_6_), channel_id=1, source_target_pairs={{0,16},{1,17},{2,18},{3,19},{4,20},{5,21},{6,22},{7,23},{8,24},{9,... | collective-permute-start | bytes 1572872 | tf_op jit(solution)/shard_map/ppermute | solution.py:56
  50.9 14.6 %copy-start.19 = (bf16[1024,256]{1,0:T(8,128)(2,1)}, bf16[1024,256]{1,0:T(8,128)(2,1)S(1)}, u32[]{:S(2)}) copy-start(bf16[1024,256]{1,0:T(8,128)(2,1)S(1)} %collective-permute-done.10.refs_5_) | copy-start | bytes 1572868
  51.0 20.4 %copy-start.13 = (bf16[1024,256]{1,0:T(8,128)(2,1)}, bf16[1024,256]{1,0:T(8,128)(2,1)S(1)}, u32[]{:S(2)}) copy-start(bf16[1024,256]{1,0:T(8,128)(2,1)S(1)} %pad_maximum_fusion.4.refs_4_) | copy-start | bytes 1572868
  51.0 19.0 %copy-start.24 = (bf16[1024,256]{1,0:T(8,128)(2,1)}, bf16[1024,256]{1,0:T(8,128)(2,1)S(1)}, u32[]{:S(2)}) copy-start(bf16[1024,256]{1,0:T(8,128)(2,1)S(1)} %collective-permute-done.17.refs_3_) | copy-start | bytes 1572868
  51.0 14.6 %collective-permute-start.18 = (bf16[1024,256]{1,0:T(8,128)(2,1)S(1)}, bf16[1024,256]{1,0:T(8,128)(2,1)S(1)}, u32[]{:S(2)}, u32[]{:S(2)}) collective-permute-start(bf16[1024,256]{1,0:T(8,128)(2,1)S(1)} %pad_maximum_fusion.4.refs_4_), channel_id=1, source_target_pairs={{0,2},{1,3},{2,0},{3,1},{4,6},{5,7},{6,4},{7,5},{8,10},{9,11},{10,... | collective-permute-start | bytes 1572872 | tf_op jit(solution)/shard_map/ppermute | solution.py:56
  53.6 40.2 %copy-start.5 = (bf16[640,256]{1,0:T(8,128)(2,1)}, bf16[640,256]{1,0:T(8,128)(2,1)S(1)}, u32[]{:S(2)}) copy-start(bf16[640,256]{1,0:T(8,128)(2,1)S(1)} %collective-permute-done.4.refs_1_.refs_10_) | copy-start | bytes 983044
  53.6 8.4 %collective-permute-start.6 = (bf16[640,256]{1,0:T(8,128)(2,1)S(1)}, bf16[640,256]{1,0:T(8,128)(2,1)S(1)}, u32[]{:S(2)}, u32[]{:S(2)}) collective-permute-start(bf16[640,256]{1,0:T(8,128)(2,1)S(1)} %collective-permute-done.4.refs_1_.refs_10_), channel_id=1, source_target_pairs={{0,8},{1,9},{2,10},{3,11},{4,0},{5,1},{6,2},{7,3},{8,12},{9,13},{1... | collective-permute-start | bytes 983048 | tf_op jit(solution)/shard_map/ppermute | solution.py:56
  57.0 11.5 %collective-permute-start.11 = (bf16[640,256]{1,0:T(8,128)(2,1)S(1)}, bf16[640,256]{1,0:T(8,128)(2,1)S(1)}, u32[]{:S(2)}, u32[]{:S(2)}) collective-permute-start(bf16[640,256]{1,0:T(8,128)(2,1)S(1)} %collective-permute-done.4.refs_1_.refs_10_), channel_id=1, source_target_pairs={{0,16},{1,17},{2,18},{3,19},{4,20},{5,21},{6,22},{7,23},{8,24},{9,... | collective-permute-start | bytes 983048 | tf_op jit(solution)/shard_map/ppermute | solution.py:56
  62.1 31.7 %copy-start.6 = (bf16[640,256]{1,0:T(8,128)(2,1)}, bf16[640,256]{1,0:T(8,128)(2,1)S(1)}, u32[]{:S(2)}) copy-start(bf16[640,256]{1,0:T(8,128)(2,1)S(1)} %collective-permute-done.6.refs_2_.refs_12_) | copy-start | bytes 983044
  62.1 8.0 %collective-permute-start.7 = (bf16[640,256]{1,0:T(8,128)(2,1)S(1)}, bf16[640,256]{1,0:T(8,128)(2,1)S(1)}, u32[]{:S(2)}, u32[]{:S(2)}) collective-permute-start(bf16[640,256]{1,0:T(8,128)(2,1)S(1)} %collective-permute-done.6.refs_2_.refs_12_), channel_id=1, source_target_pairs={{0,8},{1,9},{2,10},{3,11},{4,0},{5,1},{6,2},{7,3},{8,12},{9,13},{1... | collective-permute-start | bytes 983048 | tf_op jit(solution)/shard_map/ppermute | solution.py:56
  65.5 23.0 %copy-start.21 = (bf16[1024,256]{1,0:T(8,128)(2,1)}, bf16[1024,256]{1,0:T(8,128)(2,1)S(1)}, u32[]{:S(2)}) copy-start(bf16[1024,256]{1,0:T(8,128)(2,1)S(1)} %collective-permute-done.13.refs_7_) | copy-start | bytes 1572868
  65.6 22.9 %copy-start.14 = (bf16[1024,256]{1,0:T(8,128)(2,1)}, bf16[1024,256]{1,0:T(8,128)(2,1)S(1)}, u32[]{:S(2)}) copy-start(bf16[1024,256]{1,0:T(8,128)(2,1)S(1)} %pad_maximum_fusion.3.refs_0_) | copy-start | bytes 1572868
  65.6 4.4 %copy-start.25 = (bf16[1024,256]{1,0:T(8,128)(2,1)}, bf16[1024,256]{1,0:T(8,128)(2,1)S(1)}, u32[]{:S(2)}) copy-start(bf16[1024,256]{1,0:T(8,128)(2,1)S(1)} %collective-permute-done.18.refs_5_) | copy-start | bytes 1572868
  65.6 22.9 %collective-permute-start.19 = (bf16[1024,256]{1,0:T(8,128)(2,1)S(1)}, bf16[1024,256]{1,0:T(8,128)(2,1)}, u32[]{:S(2)}, u32[]{:S(2)}) collective-permute-start(bf16[1024,256]{1,0:T(8,128)(2,1)S(1)} %pad_maximum_fusion.3.refs_0_), channel_id=1, source_target_pairs={{0,2},{1,3},{2,0},{3,1},{4,6},{5,7},{6,4},{7,5},{8,10},{9,11},{10,... | collective-permute-start | bytes 1572872 | tf_op jit(solution)/shard_map/ppermute | solution.py:56
  67.2 9.5 %collective-permute-start.14 = (bf16[640,256]{1,0:T(8,128)(2,1)S(1)}, bf16[640,256]{1,0:T(8,128)(2,1)}, u32[]{:S(2)}, u32[]{:S(2)}) collective-permute-start(bf16[640,256]{1,0:T(8,128)(2,1)S(1)} %collective-permute-done.6.refs_2_.refs_12_), channel_id=1, source_target_pairs={{0,16},{1,17},{2,18},{3,19},{4,20},{5,21},{6,22},{7,23},{8,24},{9,... | collective-permute-start | bytes 983048 | tf_op jit(solution)/shard_map/ppermute | solution.py:56
  68.5 1.5 copy-start.26
  70.1 23.8 %copy-start.7 = (bf16[640,256]{1,0:T(8,128)(2,1)}, bf16[640,256]{1,0:T(8,128)(2,1)S(1)}, u32[]{:S(2)}) copy-start(bf16[640,256]{1,0:T(8,128)(2,1)S(1)} %collective-permute-done.7.refs_3_.refs_14_) | copy-start | bytes 983044
  70.1 10.2 %collective-permute-start.15 = (bf16[640,256]{1,0:T(8,128)(2,1)S(1)}, bf16[640,256]{1,0:T(8,128)(2,1)}, u32[]{:S(2)}, u32[]{:S(2)}) collective-permute-start(bf16[640,256]{1,0:T(8,128)(2,1)S(1)} %collective-permute-done.7.refs_3_.refs_14_), channel_id=1, source_target_pairs={{0,16},{1,17},{2,18},{3,19},{4,20},{5,21},{6,22},{7,23},{8,24},{9,... | collective-permute-start | bytes 983048 | tf_op jit(solution)/shard_map/ppermute | solution.py:56
  93.7 10.6 %collective-permute-start.20 = (bf16[1088,512]{1,0:T(8,128)(2,1)}, bf16[1088,512]{1,0:T(8,128)(2,1)S(1)}, u32[]{:S(2)}, u32[]{:S(2)}) collective-permute-start(bf16[1088,512]{1,0:T(8,128)(2,1)} %shard_map.76.refs_2_), channel_id=1, source_target_pairs={{0,1},{1,0},{2,3},{3,2},{4,5},{5,4},{6,7},{7,6},{8,9},{9,8},{10,11... | collective-permute-start | bytes 3342344 | tf_op jit(solution)/shard_map/ppermute | solution.py:56
  94.2 10.1 %copy-start.8 = (bf16[4,128,256]{2,1,0:T(8,128)(2,1)}, bf16[4,128,256]{2,1,0:T(8,128)(2,1)S(1)}, u32[]{:S(2)}) copy-start(bf16[4,128,256]{2,1,0:T(8,128)(2,1)S(1)} %shard_map.74.refs_0_) | copy-start | bytes 786436
  94.2 10.1 %collective-permute-start.8 = (bf16[4,128,256]{2,1,0:T(8,128)(2,1)S(1)}, bf16[4,128,256]{2,1,0:T(8,128)(2,1)S(1)}, u32[]{:S(2)}, u32[]{:S(2)}) collective-permute-start(bf16[4,128,256]{2,1,0:T(8,128)(2,1)S(1)} %shard_map.74.refs_0_), channel_id=1, source_target_pairs={{0,1},{1,0},{2,3},{3,2},{4,5},{5,4},{6,7},{7,6},{8,9},{9,8},{10,11... | collective-permute-start | bytes 786440 | tf_op jit(solution)/shard_map/ppermute | solution.py:56
  104.3 0.7 copy-start.27
  104.3 1.1 copy-start.15
  105.5 29.4 %copy-start.2 = (bf16[256,8192]{1,0:T(8,128)(2,1)S(1)}, bf16[256,8192]{1,0:T(8,128)(2,1)}, u32[]{:S(2)}) copy-start(bf16[256,8192]{1,0:T(8,128)(2,1)} %refs_7_.1) | copy-start | bytes 12582916
  117.3 3.5 %copy-start.4 = (bf16[4,4,144,128]{3,2,1,0:T(8,128)(2,1)S(1)}, bf16[4,4,144,128]{3,2,1,0:T(8,128)(2,1)}, u32[]{:S(2)}) copy-start(bf16[4,4,144,128]{3,2,1,0:T(8,128)(2,1)} %get-tuple-element.53) | copy-start | bytes 1769476
  118.4 2.4 %collective-permute-start.21 = (bf16[4,2,144,128]{3,2,1,0:T(8,128)(2,1)S(1)}, bf16[4,2,144,128]{3,2,1,0:T(8,128)(2,1)S(1)}, u32[]{:S(2)}, u32[]{:S(2)}) collective-permute-start(bf16[4,2,144,128]{3,2,1,0:T(8,128)(2,1)S(1)} %slice_bitcast_fusion), channel_id=1, source_target_pairs={{0,1},{1,0},{2,3},{3,2},{4,5},{5,4},{6,7},{7,6},{8,9},{9,8},{10,11... | collective-permute-start | bytes 884744 | tf_op jit(solution)/shard_map/ppermute | solution.py:56
  119.4 13.7 %collective-permute-start.26 = (f32[64,512]{1,0:T(8,128)}, f32[64,512]{1,0:T(8,128)S(1)}, u32[]{:S(2)}, u32[]{:S(2)}) collective-permute-start(f32[64,512]{1,0:T(8,128)} %get-tuple-element.60), channel_id=1, source_target_pairs={{0,1},{1,0},{2,3},{3,2},{4,5},{5,4},{6,7},{7,6},{8,9},{9,8},{10,11... | collective-permute-start | bytes 393224 | tf_op jit(solution)/shard_map/ppermute | solution.py:56
  120.8 5.9 %collective-permute-start.22 = (bf16[4,144,128]{2,1,0:T(8,128)(2,1)S(1)}, bf16[4,144,128]{2,1,0:T(8,128)(2,1)S(1)}, u32[]{:S(2)}, u32[]{:S(2)}) collective-permute-start(bf16[4,144,128]{2,1,0:T(8,128)(2,1)S(1)} %get-tuple-element.55), channel_id=1, source_target_pairs={{0,2},{1,3},{2,0},{3,1},{4,6},{5,7},{6,4},{7,5},{8,10},{9,11},{10,... | collective-permute-start | bytes 442376 | tf_op jit(solution)/shard_map/ppermute | solution.py:56
  126.8 7.1 %collective-permute-start.23 = (bf16[144,128]{1,0:T(8,128)(2,1)S(1)}, bf16[144,128]{1,0:T(8,128)(2,1)S(1)}, u32[]{:S(2)}, u32[]{:S(2)}) collective-permute-start(bf16[144,128]{1,0:T(8,128)(2,1)S(1)} %get-tuple-element.57), channel_id=1, source_target_pairs={{0,4},{1,5},{2,6},{3,7},{4,8},{5,9},{6,10},{7,11},{8,12},{9,13},{1... | collective-permute-start | bytes 110600 | tf_op jit(solution)/shard_map/ppermute | solution.py:56
  129.2 4.9 %collective-permute-start.24 = (bf16[144,128]{1,0:T(8,128)(2,1)S(1)}, bf16[144,128]{1,0:T(8,128)(2,1)S(1)}, u32[]{:S(2)}, u32[]{:S(2)}) collective-permute-start(bf16[144,128]{1,0:T(8,128)(2,1)S(1)} %get-tuple-element.58), channel_id=1, source_target_pairs={{0,8},{1,9},{2,10},{3,11},{4,12},{5,13},{6,14},{7,15},{8,0},{9,1},... | collective-permute-start | bytes 110600 | tf_op jit(solution)/shard_map/ppermute | solution.py:56
  130.9 4.0 %collective-permute-start.25 = (bf16[144,128]{1,0:T(8,128)(2,1)S(1)}, bf16[144,128]{1,0:T(8,128)(2,1)S(1)}, u32[]{:S(2)}, u32[]{:S(2)}) collective-permute-start(bf16[144,128]{1,0:T(8,128)(2,1)S(1)} %get-tuple-element.59), channel_id=1, source_target_pairs={{0,12},{1,13},{2,14},{3,15},{4,0},{5,1},{6,2},{7,3},{8,4},{9,5},{1... | collective-permute-start | bytes 110600 | tf_op jit(solution)/shard_map/ppermute | solution.py:56
  136.6 2.0 %collective-permute-start.27 = (bf16[64,4096]{1,0:T(8,128)(2,1)S(1)}, bf16[64,4096]{1,0:T(8,128)(2,1)S(1)}, u32[]{:S(2)}, u32[]{:S(2)}) collective-permute-start(bf16[64,4096]{1,0:T(8,128)(2,1)S(1)} %slice.124), channel_id=1, source_target_pairs={{0,1},{1,0},{2,3},{3,2},{4,5},{5,4},{6,7},{7,6},{8,9},{9,8},{10,11... | collective-permute-start | bytes 1572872 | tf_op jit(solution)/shard_map/ppermute | solution.py:56
  138.7 8.4 %collective-permute-start.28 = (bf16[64,2048]{1,0:T(8,128)(2,1)S(1)}, bf16[64,2048]{1,0:T(8,128)(2,1)S(1)}, u32[]{:S(2)}, u32[]{:S(2)}) collective-permute-start(bf16[64,2048]{1,0:T(8,128)(2,1)S(1)} %slice.126), channel_id=1, source_target_pairs={{0,2},{1,3},{2,0},{3,1},{4,6},{5,7},{6,4},{7,5},{8,10},{9,11},{10,... | collective-permute-start | bytes 786440 | tf_op jit(solution)/shard_map/ppermute | solution.py:56
  147.2 7.1 %collective-permute-start.29 = (bf16[64,512]{1,0:T(8,128)(2,1)S(1)}, bf16[64,512]{1,0:T(8,128)(2,1)S(1)}, u32[]{:S(2)}, u32[]{:S(2)}) collective-permute-start(bf16[64,512]{1,0:T(8,128)(2,1)S(1)} %get-tuple-element.69), channel_id=1, source_target_pairs={{0,4},{1,5},{2,6},{3,7},{4,8},{5,9},{6,10},{7,11},{8,12},{9,13},{1... | collective-permute-start | bytes 196616 | tf_op jit(solution)/shard_map/ppermute | solution.py:56
  148.1 7.9 %collective-permute-start.30 = (bf16[64,512]{1,0:T(8,128)(2,1)S(1)}, bf16[64,512]{1,0:T(8,128)(2,1)S(1)}, u32[]{:S(2)}, u32[]{:S(2)}) collective-permute-start(bf16[64,512]{1,0:T(8,128)(2,1)S(1)} %get-tuple-element.71), channel_id=1, source_target_pairs={{0,8},{1,9},{2,10},{3,11},{4,12},{5,13},{6,14},{7,15},{8,0},{9,1},... | collective-permute-start | bytes 196616 | tf_op jit(solution)/shard_map/ppermute | solution.py:56
  151.9 4.5 %collective-permute-start.31 = (bf16[64,512]{1,0:T(8,128)(2,1)S(1)}, bf16[64,512]{1,0:T(8,128)(2,1)S(1)}, u32[]{:S(2)}, u32[]{:S(2)}) collective-permute-start(bf16[64,512]{1,0:T(8,128)(2,1)S(1)} %get-tuple-element.70), channel_id=1, source_target_pairs={{0,12},{1,13},{2,14},{3,15},{4,0},{5,1},{6,2},{7,3},{8,4},{9,5},{1... | collective-permute-start | bytes 196616 | tf_op jit(solution)/shard_map/ppermute | solution.py:56

commit v13 on v12

--- a/solution.py
+++ b/solution.py
@@ -273,16 +273,16 @@
 
 
 def merge_cores(own, other):
-    deep, _, _, height, lanes = own.shape
+    deep, _, height, lanes = own.shape
 
     def body(own_ref, other_ref, near_ref, far_ref):
         for z in range(deep):
             for y, out_ref in enumerate((near_ref, far_ref)):
-                both = own_ref[z, 0, y, :HEAD_DIM, :].astype(jnp.float32) + other_ref[
+                both = own_ref[z, y, :HEAD_DIM, :].astype(jnp.float32) + other_ref[
                     z, y, :HEAD_DIM, :
                 ].astype(jnp.float32)
                 out_ref[z, :HEAD_DIM, :] = both.astype(jnp.bfloat16)
-                out_ref[z, HEAD_DIM:, :] = own_ref[z, 0, y, HEAD_DIM:, :]
+                out_ref[z, HEAD_DIM:, :] = own_ref[z, y, HEAD_DIM:, :]
 
     return small_call(body, [(deep, height, lanes)] * 2, [], [own, other])
 
@@ -330,8 +330,8 @@
         prompt_ref, got_ref, step_ref, early_ref = refs[len(inputs) : len(inputs) + 4]
         rest = refs[len(inputs) + 4 :]
         weight_refs, rest = rest[: len(held.arrays)], rest[len(held.arrays) :]
-        out_ref, step_out_ref = rest[:2]
-        early_held, weight_held, value_held, early_sem, *scratch = rest[2:]
+        *out_refs, step_out_ref = rest[:3]
+        early_held, weight_held, value_held, early_sem, *scratch = rest[3:]
         left, weight_rows, _ = scratch
         sources = (prompt_ref, got_ref, step_ref)
         groups = [
@@ -380,7 +380,10 @@
             total = jnp.sum(weights, axis=0, keepdims=True)
             for i in range(owners):
                 lane = slice(i * HEAD_DIM, (i + 1) * HEAD_DIM)
-                out_ref[j, i, HEAD_DIM:, :] = note_rows(top[:, lane], total[:, lane])
+                out_ref = out_refs[i // 2 % 2]
+                out_ref[j, i // 4 * 2 + i % 2, HEAD_DIM:, :] = note_rows(
+                    top[:, lane], total[:, lane]
+                )
             weight_held[j] = weights.astype(jnp.bfloat16)
             return 0
 
@@ -404,7 +407,8 @@
             )
             for i in range(owners):
                 lane = slice(i * HEAD_DIM, (i + 1) * HEAD_DIM)
-                out_ref[j, i, :HEAD_DIM, :] = summed[:, lane].astype(jnp.bfloat16)
+                out_ref = out_refs[i // 2 % 2]
+                out_ref[j, i // 4 * 2 + i % 2, :HEAD_DIM, :] = summed[:, lane].astype(jnp.bfloat16)
             return 0
 
         lax.fori_loop(0, kv_heads, one_sum, 0)
@@ -416,9 +420,14 @@
         in_specs=[pl.BlockSpec(memory_space=pltpu.SMEM)] * 3
         + [whole] * len(inputs)
         + [anywhere] * (4 + len(held.arrays)),
-        out_specs=[whole] * 2,
+        out_specs=[whole] * 3,
         out_shape=[
-            jax.ShapeDtypeStruct((kv_heads, owners, HEAD_DIM + NOTES, HEAD_DIM), jnp.bfloat16),
+            *[
+                jax.ShapeDtypeStruct(
+                    (kv_heads, owners // 2, HEAD_DIM + NOTES, HEAD_DIM), jnp.bfloat16
+                )
+            ]
+            * 2,
             jax.ShapeDtypeStruct((held.step_count, held.columns), jnp.float32),
         ],
         scratch_shapes=[
@@ -593,18 +602,17 @@
     for k in range(1, deep):
         if k + 1 < deep:
             both_z[k + 1] = send(along_ring, both_z[k])
-        both_x[k] = send(along_x, both_z[k])
         if k == 1:
             theirs_x[0] = send(along_x, value_y)
+        both_x[k] = send(along_x, after(both_z[k], theirs_x[0]))
         key_full[k] = jnp.concatenate([both_z[k][:width], both_x[k][:width]])
         key_y[k] = send(along_y, after(key_full[k], key_y[k - 1]))
     for k in range(1, deep):
         theirs[k] = send(along_ring, theirs[k - 1])
-        theirs_x[k] = send(along_x, theirs[k])
+        theirs_x[k] = send(along_x, theirs[k][:width])
 
     ring_queries = collect([theirs[k] for k in range(deep)], width, 2 * packed)
     ring_queries = [ring_queries, in_chip(ring_queries)]
-    by_owner = (deep, 2, 2, rows)
 
     key_pieces = [
         [((key_y if flip else key_full)[k], start) for start in (0, width)] for k, flip in places
@@ -620,15 +628,13 @@
             prompt_states, got, wide_states, taken, width, [pieces[i] for i in which], acc, kind
         )
 
-    last = 2 * deep - 2
-    key_early = project_blocks(
-        key_pieces, range(last), None, (theirs_x[1], theirs[deep - 2]), jnp.float32
-    )
-    awaited = [theirs_x[k] for k in range(1, deep)]
-    key_sum = project_blocks(key_pieces, [last, last + 1], key_early, awaited, jnp.bfloat16)
     early = [*range(0, 2 * deep, 2), 1]
     late = [i for i in range(2 * deep) if i not in early]
-    value_early = project_blocks(value_pieces, early, None, key_sum, jnp.float32)
+    value_early = project_blocks(
+        value_pieces, early, None, (theirs_x[1], theirs[deep - 1]), jnp.float32
+    )
+    awaited = (value_early, [theirs_x[k] for k in range(1, deep)])
+    key_sum = project_blocks(key_pieces, range(2 * deep), None, awaited, jnp.bfloat16)
     key_back = in_chip(key_sum)
 
     def own_head(sums):
@@ -643,7 +649,7 @@
         token_prompt = jnp.repeat(slots // PROMPT_PAGES, PAGE)
         row_prompt = jnp.tile(sample_order // group_size, devices // KV_HEADS * rows // samples)
         masks = [token_prompt[:, None], row_prompt[None, :]]
-    partial, step_values = attend(
+    kept, sent, step_values = attend(
         kv_places, query_turns, ring_queries, key_sum, key_back, cosine, sine_part, masks,
         prompt_states, got, wide_states, jnp.stack([own_blocks[i] for i in late]), width,
         [value_pieces[i] for i in late], value_early,
@@ -651,8 +657,8 @@
     new_values = own_head(step_values) + own_head(in_chip(step_values))
     new_values = new_values.astype(jnp.bfloat16).astype(jnp.float32).reshape(steps, HEAD_DIM)
 
-    partial = partial.reshape(by_owner[:3] + partial.shape[2:])
-    near, far = merge_cores(partial, in_chip(partial[:, 1]))
+    by_owner = (deep, 2, *kept.shape[2:])
+    near, far = merge_cores(kept.reshape(by_owner), in_chip(sent.reshape(by_owner)))
     merged = merge_chips(own_a[None], near, along_y(far))
     parts = [merged[0]] + [along_z(merged[k], k) for k in range(1, deep)]
 

time: 157 us -> 150 us (0.955)
  starting transfers between devices: 50.6 us -> 42.6 us
  Pallas kernels: 36.9 us -> 32.9 us
  local copies, waits for them, and re-layouts: 9.8 us -> 12.3 us
  waiting for transfers between devices: 50.4 us -> 52.7 us
    ppermute x32, starting transfers between devices: 50.6 us -> 42.6 us  [move(): return lax.ppermute(value, ('groups', 'sample'), pairs)]
    pallas_call x3 -> x2, Pallas kernels: 20.9 us -> 16.9 us  [project(): pl.pallas_call(body, in_specs=[pl.BlockSpec(memory_space=pltpu.SMEM)] + [...]
    unnamed x58 -> x66, local copies, waits for them, and re-layouts: 3.43 us -> 6.28 us
    ppermute x32, waiting for transfers between devices: 50.4 us -> 52.7 us  [move(): return lax.ppermute(value, ('groups', 'sample'), pairs)]
  transfers between devices with their start and end apart: 32 -> 32, of which waited for: 17 -> 16; matrix products, arithmetic and copies ran while one was open for 8% -> 9% of each run, Pallas kernels for 12% -> 7%
where the time goes in v13:
time: 150 us; the launch traced here: 149 us
  waiting for transfers between devices  52.7 us (35%)
  starting transfers between devices  42.6 us (28%)
  Pallas kernels  32.9 us (22%)
  local copies, waits for them, and re-layouts  12.3 us (8%)
  other arithmetic  8.03 us (5%)
    ppermute x32, waiting for transfers between devices, move(): return lax.ppermute(value, ('groups', 'sample'), pairs)  52.7 us
    ppermute x32, starting transfers between devices, move(): return lax.ppermute(value, ('groups', 'sample'), pairs)  42.6 us
    pallas_call x2, Pallas kernels, project(): pl.pallas_call(body, in_specs=[pl.BlockSpec(memory_space=pltpu.SMEM)] + [...  16.9 us
    pallas_call x1, Pallas kernels, attend(): pl.pallas_call(body, in_specs=[pl.BlockSpec(memory_space=pltpu.SMEM)] * 3...  11.8 us
    unnamed x66, local copies, waits for them, and re-layouts  6.28 us
    sin x1, other arithmetic, rope_tables(): return (jnp.cos(angles), jnp.sin(angles))  3.08 us
  transfers between devices with their start and end apart: 32, of which 16 were waited for; matrix products, arithmetic and copies ran while one was open for 9% of the time, Pallas kernels for 7%

profile of v13, /device:TPU:0, one launch (start us, length us, event | category | flops | bytes accessed | tf_op | source)
XLA Modules:
  0.0 149.2 jit_solution(7608913454121674534)
XLA Ops:
  0.5 1.3 fusion.5
  2.0 3.6 %collective-permute-start.2 = (bf16[1024,256]{1,0:T(8,128)(2,1)S(1)}, bf16[1024,256]{1,0:T(8,128)(2,1)S(1)}, u32[]{:S(2)}, u32[]{:S(2)}) collective-permute-start(bf16[1024,256]{1,0:T(8,128)(2,1)S(1)} %get-tuple-element.67.refs_0_), channel_id=1, source_target_pairs={{0,8},{1,9},{2,10},{3,11},{4,0},{5,1},{6,2},{7,3},{8,12},{9,13},{1... | collective-permute-start | bytes 1572872 | tf_op jit(solution)/shard_map/ppermute | solution.py:56
  5.6 0.7 fusion.4
  6.3 1.5 %collective-permute-start = (bf16[512,256]{1,0:T(8,128)(2,1)S(1)}, bf16[512,256]{1,0:T(8,128)(2,1)}, u32[]{:S(2)}, u32[]{:S(2)}) collective-permute-start(bf16[512,256]{1,0:T(8,128)(2,1)S(1)} %get-tuple-element.69), channel_id=1, source_target_pairs={{0,2},{1,3},{2,0},{3,1},{4,6},{5,7},{6,4},{7,5},{8,10},{9,11},{10,... | collective-permute-start | bytes 786440 | tf_op jit(solution)/shard_map/ppermute | solution.py:56
  8.2 3.1 %multiply_sine_fusion = (f32[1024,64]{1,0:T(8,128)}, f32[1024,64]{1,0:T(8,128)}) fusion(f32[64]{0:T(128)S(1)} %multiply_power_fusion, f32[1024]{0:T(1024)S(1)} %convert_bitcast_fusion), kind=kLoop, calls=%fused_computation.1 | loop fusion | flops 65536 | bytes 528640 | tf_op jit(solution)/shard_map/sin | solution.py:23
  11.3 3.6 %collective-permute-done = bf16[512,256]{1,0:T(8,128)(2,1)} collective-permute-done((bf16[512,256]{1,0:T(8,128)(2,1)S(1)}, bf16[512,256]{1,0:T(8,128)(2,1)}, u32[]{:S(2)}, u32[]{:S(2)}) %collective-permute-start) | collective-permute-done | bytes 262176 | tf_op jit(solution)/shard_map/ppermute | solution.py:56
  14.9 1.5 collective-permute-start.9
  16.6 2.2 %copy-done.1 = bf16[8192,256]{1,0:T(8,128)(2,1)S(1)} copy-done((bf16[8192,256]{1,0:T(8,128)(2,1)S(1)}, bf16[8192,256]{1,0:T(8,128)(2,1)}, u32[]{:S(2)}) %copy-start.1) | copy-done | bytes 4194328
  18.8 2.0 %shard_map.73.refs_4_ = bf16[64,256]{1,0:T(8,128)(2,1)S(1)} custom-call(bf16[64,8192]{1,0:T(8,128)(2,1)S(1)} %bitcast.45, bf16[8192,256]{1,0:T(8,128)(2,1)S(1)} %copy-done.1, f32[64,128]{1,0:T(8,128)S(1)} %bitcast.46, f32[64,128]{1,0:T(8,128)S(1)} %bitcast.47), custom_call_target="tpu_custom_call" | custom-call | flops 1 | bytes 1 | tf_op jit(solution)/shard_map/pallas_call | solution.py:106
  20.8 1.9 %collective-permute-done.9.refs_9_ = bf16[512,256]{1,0:T(8,128)(2,1)S(1)} collective-permute-done((bf16[512,256]{1,0:T(8,128)(2,1)}, bf16[512,256]{1,0:T(8,128)(2,1)S(1)}, u32[]{:S(2)}, u32[]{:S(2)}) %collective-permute-start.9) | collective-permute-done | bytes 262176 | tf_op jit(solution)/shard_map/ppermute | solution.py:56
  22.7 1.5 collective-permute-start.13
  24.2 1.6 %collective-permute-start.3 = (bf16[1024,256]{1,0:T(8,128)(2,1)S(1)}, bf16[1024,256]{1,0:T(8,128)(2,1)S(1)}, u32[]{:S(2)}, u32[]{:S(2)}) collective-permute-start(bf16[1024,256]{1,0:T(8,128)(2,1)S(1)} %collective-permute-done.2.refs_2_), channel_id=1, source_target_pairs={{0,8},{1,9},{2,10},{3,11},{4,0},{5,1},{6,2},{7,3},{8,12},{9,13},{1... | collective-permute-start | bytes 1572872 | tf_op jit(solution)/shard_map/ppermute | solution.py:56
  25.8 1.6 %collective-permute-start.1 = (bf16[1088,256]{1,0:T(8,128)(2,1)S(1)}, bf16[1088,256]{1,0:T(8,128)(2,1)S(1)}, u32[]{:S(2)}, u32[]{:S(2)}) collective-permute-start(bf16[1088,256]{1,0:T(8,128)(2,1)S(1)} %pad_maximum_fusion.refs_0_), channel_id=1, source_target_pairs={{0,2},{1,3},{2,0},{3,1},{4,6},{5,7},{6,4},{7,5},{8,10},{9,11},{10,... | collective-permute-start | bytes 1671176 | tf_op jit(solution)/shard_map/ppermute | solution.py:56
  27.4 8.8 %collective-permute-done.3.refs_4_ = bf16[1024,256]{1,0:T(8,128)(2,1)S(1)} collective-permute-done((bf16[1024,256]{1,0:T(8,128)(2,1)S(1)}, bf16[1024,256]{1,0:T(8,128)(2,1)S(1)}, u32[]{:S(2)}, u32[]{:S(2)}) %collective-permute-start.3) | collective-permute-done | bytes 524320 | tf_op jit(solution)/shard_map/ppermute | solution.py:56
  36.3 2.4 %collective-permute-start.5 = (bf16[1024,256]{1,0:T(8,128)(2,1)S(1)}, bf16[1024,256]{1,0:T(8,128)(2,1)S(1)}, u32[]{:S(2)}, u32[]{:S(2)}) collective-permute-start(bf16[1024,256]{1,0:T(8,128)(2,1)S(1)} %collective-permute-done.3.refs_4_), channel_id=1, source_target_pairs={{0,8},{1,9},{2,10},{3,11},{4,0},{5,1},{6,2},{7,3},{8,12},{9,13},{1... | collective-permute-start | bytes 1572872 | tf_op jit(solution)/shard_map/ppermute | solution.py:56
  38.7 0.5 collective-permute-start.10
  39.2 0.8 copy-done.17
  40.2 1.6 %collective-permute-start.17 = (bf16[1024,256]{1,0:T(8,128)(2,1)S(1)}, bf16[1024,256]{1,0:T(8,128)(2,1)S(1)}, u32[]{:S(2)}, u32[]{:S(2)}) collective-permute-start(bf16[1024,256]{1,0:T(8,128)(2,1)S(1)} %pad_maximum_fusion.3.refs_2_), channel_id=1, source_target_pairs={{0,2},{1,3},{2,0},{3,1},{4,6},{5,7},{6,4},{7,5},{8,10},{9,11},{10,... | collective-permute-start | bytes 1572872 | tf_op jit(solution)/shard_map/ppermute | solution.py:56
  41.7 1.0 pad_maximum_fusion.6.refs_0_.refs_8_
  42.8 8.1 %collective-permute-done.5.refs_6_ = bf16[1024,256]{1,0:T(8,128)(2,1)S(1)} collective-permute-done((bf16[1024,256]{1,0:T(8,128)(2,1)S(1)}, bf16[1024,256]{1,0:T(8,128)(2,1)S(1)}, u32[]{:S(2)}, u32[]{:S(2)}) %collective-permute-start.5) | collective-permute-done | bytes 524320 | tf_op jit(solution)/shard_map/ppermute | solution.py:56
  51.0 0.5 collective-permute-start.14
  51.5 1.0 collective-permute-done.10.refs_5_
  52.6 1.6 %collective-permute-start.18 = (bf16[1024,256]{1,0:T(8,128)(2,1)S(1)}, bf16[1024,256]{1,0:T(8,128)(2,1)S(1)}, u32[]{:S(2)}, u32[]{:S(2)}) collective-permute-start(bf16[1024,256]{1,0:T(8,128)(2,1)S(1)} %pad_maximum_fusion.4.refs_4_), channel_id=1, source_target_pairs={{0,2},{1,3},{2,0},{3,1},{4,6},{5,7},{6,4},{7,5},{8,10},{9,11},{10,... | collective-permute-start | bytes 1572872 | tf_op jit(solution)/shard_map/ppermute | solution.py:56
  54.2 1.2 collective-permute-done.4.refs_1_.refs_10_
  55.4 2.4 %collective-permute-start.6 = (bf16[640,256]{1,0:T(8,128)(2,1)S(1)}, bf16[640,256]{1,0:T(8,128)(2,1)S(1)}, u32[]{:S(2)}, u32[]{:S(2)}) collective-permute-start(bf16[640,256]{1,0:T(8,128)(2,1)S(1)} %collective-permute-done.4.refs_1_.refs_10_), channel_id=1, source_target_pairs={{0,8},{1,9},{2,10},{3,11},{4,0},{5,1},{6,2},{7,3},{8,12},{9,13},{1... | collective-permute-start | bytes 983048 | tf_op jit(solution)/shard_map/ppermute | solution.py:56
  57.8 0.6 collective-permute-start.11
  58.5 5.7 %collective-permute-done.6.refs_2_.refs_12_ = bf16[640,256]{1,0:T(8,128)(2,1)S(1)} collective-permute-done((bf16[640,256]{1,0:T(8,128)(2,1)S(1)}, bf16[640,256]{1,0:T(8,128)(2,1)S(1)}, u32[]{:S(2)}, u32[]{:S(2)}) %collective-permute-start.6) | collective-permute-done | bytes 327712 | tf_op jit(solution)/shard_map/ppermute | solution.py:56
  64.2 2.8 %collective-permute-start.7 = (bf16[640,256]{1,0:T(8,128)(2,1)S(1)}, bf16[640,256]{1,0:T(8,128)(2,1)S(1)}, u32[]{:S(2)}, u32[]{:S(2)}) collective-permute-start(bf16[640,256]{1,0:T(8,128)(2,1)S(1)} %collective-permute-done.6.refs_2_.refs_12_), channel_id=1, source_target_pairs={{0,8},{1,9},{2,10},{3,11},{4,0},{5,1},{6,2},{7,3},{8,12},{9,13},{1... | collective-permute-start | bytes 983048 | tf_op jit(solution)/shard_map/ppermute | solution.py:56
  67.1 1.6 %collective-permute-start.19 = (bf16[1024,256]{1,0:T(8,128)(2,1)S(1)}, bf16[1024,256]{1,0:T(8,128)(2,1)S(1)}, u32[]{:S(2)}, u32[]{:S(2)}) collective-permute-start(bf16[1024,256]{1,0:T(8,128)(2,1)S(1)} %pad_maximum_fusion.5.refs_6_), channel_id=1, source_target_pairs={{0,2},{1,3},{2,0},{3,1},{4,6},{5,7},{6,4},{7,5},{8,10},{9,11},{10,... | collective-permute-start | bytes 1572872 | tf_op jit(solution)/shard_map/ppermute | solution.py:56
  68.7 0.6 collective-permute-start.15
  69.3 2.3 %collective-permute-done.7.refs_3_.refs_14_ = bf16[640,256]{1,0:T(8,128)(2,1)S(1)} collective-permute-done((bf16[640,256]{1,0:T(8,128)(2,1)S(1)}, bf16[640,256]{1,0:T(8,128)(2,1)S(1)}, u32[]{:S(2)}, u32[]{:S(2)}) %collective-permute-start.7) | collective-permute-done | bytes 327712 | tf_op jit(solution)/shard_map/ppermute | solution.py:56
  71.5 0.8 slice.122
  72.3 0.7 copy-done.27
  73.0 0.5 collective-permute-start.16
  73.6 0.6 stack.131.block_ref
  74.2 0.6 stack.130.block_ref
  74.8 7.5 %shard_map.75.refs_9_ = f32[1088,512]{1,0:T(8,128)} custom-call(s32[5]{0:T(128)} %stack.131.block_ref, bf16[512,8192]{1,0:T(8,128)(2,1)} %refs_6_.1, bf16[512,8192]{1,0:T(8,128)(2,1)} %collective-permute-done.12.got_ref.refs_7_, bf16[64,8192]{1,0:T(8,128)(2,1)} %bitcast.42, bf16[1024,256]{1,0:T(8,128)(2,1)} %copy-done.10, bf16[1024,256]{1,0:T(8,128)(2,1)} %copy-done.11, ...), custom_call_target="tpu_custom_call" | custom-call | flops 1 | bytes 1 | tf_op jit(solution)/shard_map/pallas_call | solution.py:226
  82.4 0.8 copy-done.26
  83.2 9.3 %shard_map.76.refs_2_ = bf16[1088,512]{1,0:T(8,128)(2,1)} custom-call(s32[8]{0:T(128)} %stack.130.block_ref, bf16[512,8192]{1,0:T(8,128)(2,1)} %refs_6_.1, bf16[512,8192]{1,0:T(8,128)(2,1)} %collective-permute-done.12.got_ref.refs_7_, bf16[64,8192]{1,0:T(8,128)(2,1)} %bitcast.43, bf16[1088,256]{1,0:T(8,128)(2,1)} %copy-done.12, ...), custom_call_target="tpu_custom_call" | custom-call | flops 1 | bytes 1 | tf_op jit(solution)/shard_map/pallas_call | solution.py:226
  93.7 0.6 pad_add_fusion.1.block_ref
  94.3 0.6 and_select_fusion.1
  94.9 0.8 collective-permute-done.8.refs_1_
  95.8 0.7 copy-done.30
  96.5 11.8 %shard_map.77 = (bf16[4,2,144,128]{3,2,1,0:T(8,128)(2,1)}, bf16[4,2,144,128]{3,2,1,0:T(8,128)(2,1)}, f32[64,512]{1,0:T(8,128)}) custom-call(s32[4]{0:T(128)} %get-tuple-element.87.place_ref, s32[4]{0:T(128)} %get-tuple-element.88.turn_ref, s32[3]{0:T(128)} %pad_add_fusion.1.block_ref, bf16[4,128,256]{2,1,0:T(8,128)(2,1)} %copy-done.8, ...), custom_call_target="tpu_custom_call" | custom-call | flops 1 | bytes 1 | tf_op jit(solution)/shard_map/pallas_call | solution.py:418
  108.7 0.8 slice.129
  109.9 0.8 slice.130
  110.8 1.0 copy-done.9
  111.8 1.6 %collective-permute-start.22 = (bf16[4,144,128]{2,1,0:T(8,128)(2,1)S(1)}, bf16[4,144,128]{2,1,0:T(8,128)(2,1)S(1)}, u32[]{:S(2)}, u32[]{:S(2)}) collective-permute-start(bf16[4,144,128]{2,1,0:T(8,128)(2,1)S(1)} %get-tuple-element.61), channel_id=1, source_target_pairs={{0,2},{1,3},{2,0},{3,1},{4,6},{5,7},{6,4},{7,5},{8,10},{9,11},{10,... | collective-permute-start | bytes 442376 | tf_op jit(solution)/shard_map/ppermute | solution.py:56
  113.5 4.2 %collective-permute-done.22.far_ref = bf16[4,144,128]{2,1,0:T(8,128)(2,1)S(1)} collective-permute-done((bf16[4,144,128]{2,1,0:T(8,128)(2,1)S(1)}, bf16[4,144,128]{2,1,0:T(8,128)(2,1)S(1)}, u32[]{:S(2)}, u32[]{:S(2)}) %collective-permute-start.22) | collective-permute-done | bytes 147488 | tf_op jit(solution)/shard_map/ppermute | solution.py:56
  117.8 1.8 %collective-permute-start.23 = (bf16[144,128]{1,0:T(8,128)(2,1)S(1)}, bf16[144,128]{1,0:T(8,128)(2,1)S(1)}, u32[]{:S(2)}, u32[]{:S(2)}) collective-permute-start(bf16[144,128]{1,0:T(8,128)(2,1)S(1)} %get-tuple-element.63), channel_id=1, source_target_pairs={{0,4},{1,5},{2,6},{3,7},{4,8},{5,9},{6,10},{7,11},{8,12},{9,13},{1... | collective-permute-start | bytes 110600 | tf_op jit(solution)/shard_map/ppermute | solution.py:56
  119.6 1.8 %collective-permute-start.24 = (bf16[144,128]{1,0:T(8,128)(2,1)S(1)}, bf16[144,128]{1,0:T(8,128)(2,1)S(1)}, u32[]{:S(2)}, u32[]{:S(2)}) collective-permute-start(bf16[144,128]{1,0:T(8,128)(2,1)S(1)} %get-tuple-element.64), channel_id=1, source_target_pairs={{0,8},{1,9},{2,10},{3,11},{4,12},{5,13},{6,14},{7,15},{8,0},{9,1},... | collective-permute-start | bytes 110600 | tf_op jit(solution)/shard_map/ppermute | solution.py:56
  121.4 2.8 %collective-permute-start.25 = (bf16[144,128]{1,0:T(8,128)(2,1)S(1)}, bf16[144,128]{1,0:T(8,128)(2,1)S(1)}, u32[]{:S(2)}, u32[]{:S(2)}) collective-permute-start(bf16[144,128]{1,0:T(8,128)(2,1)S(1)} %get-tuple-element.65), channel_id=1, source_target_pairs={{0,12},{1,13},{2,14},{3,15},{4,0},{5,1},{6,2},{7,3},{8,4},{9,5},{1... | collective-permute-start | bytes 110600 | tf_op jit(solution)/shard_map/ppermute | solution.py:56
  124.3 0.8 fusion.refs_6_
  125.0 0.9 collective-permute-done.25.refs_3_
  125.9 1.7 %shard_map.80 = bf16[64,8192]{1,0:T(8,128)(2,1)S(1)} custom-call(s32[16]{0:T(128)S(1)} %stack.115.block_ref, bf16[144,128]{1,0:T(8,128)(2,1)S(1)} %get-tuple-element.62.refs_0_, bf16[144,128]{1,0:T(8,128)(2,1)S(1)} %collective-permute-done.23.refs_1_, bf16[144,128]{1,0:T(8,128)(2,1)S(1)} %collective-permute-done.24.refs_2_, ...), custom_call_target="tpu_custom_call" | custom-call | flops 1 | bytes 1 | tf_op jit(solution)/shard_map/pallas_call | solution.py:265
  127.7 1.9 %collective-permute-done.27 = bf16[64,4096]{1,0:T(8,128)(2,1)S(1)} collective-permute-done((bf16[64,4096]{1,0:T(8,128)(2,1)S(1)}, bf16[64,4096]{1,0:T(8,128)(2,1)S(1)}, u32[]{:S(2)}, u32[]{:S(2)}) %collective-permute-start.27) | collective-permute-done | bytes 524320 | tf_op jit(solution)/shard_map/ppermute | solution.py:56
  129.8 1.5 %collective-permute-start.28 = (bf16[64,2048]{1,0:T(8,128)(2,1)S(1)}, bf16[64,2048]{1,0:T(8,128)(2,1)S(1)}, u32[]{:S(2)}, u32[]{:S(2)}) collective-permute-start(bf16[64,2048]{1,0:T(8,128)(2,1)S(1)} %slice.136), channel_id=1, source_target_pairs={{0,2},{1,3},{2,0},{3,1},{4,6},{5,7},{6,4},{7,5},{8,10},{9,11},{10,... | collective-permute-start | bytes 786440 | tf_op jit(solution)/shard_map/ppermute | solution.py:56
  131.3 6.9 %collective-permute-done.28 = bf16[64,2048]{1,0:T(8,128)(2,1)S(1)} collective-permute-done((bf16[64,2048]{1,0:T(8,128)(2,1)S(1)}, bf16[64,2048]{1,0:T(8,128)(2,1)S(1)}, u32[]{:S(2)}, u32[]{:S(2)}) %collective-permute-start.28) | collective-permute-done | bytes 262176 | tf_op jit(solution)/shard_map/ppermute | solution.py:56
  138.3 4.2 %collective-permute-start.31 = (bf16[64,512]{1,0:T(8,128)(2,1)S(1)}, bf16[64,512]{1,0:T(8,128)(2,1)S(1)}, u32[]{:S(2)}, u32[]{:S(2)}) collective-permute-start(bf16[64,512]{1,0:T(8,128)(2,1)S(1)} %get-tuple-element.76), channel_id=1, source_target_pairs={{0,12},{1,13},{2,14},{3,15},{4,0},{5,1},{6,2},{7,3},{8,4},{9,5},{1... | collective-permute-start | bytes 196616 | tf_op jit(solution)/shard_map/ppermute | solution.py:56
  142.4 0.6 collective-permute-start.29
  143.1 1.6 %collective-permute-done.31 = bf16[64,512]{1,0:T(8,128)(2,1)S(1)} collective-permute-done((bf16[64,512]{1,0:T(8,128)(2,1)S(1)}, bf16[64,512]{1,0:T(8,128)(2,1)S(1)}, u32[]{:S(2)}, u32[]{:S(2)}) %collective-permute-start.31) | collective-permute-done | bytes 65568 | tf_op jit(solution)/shard_map/ppermute | solution.py:56
  144.7 2.9 %collective-permute-done.30 = bf16[64,512]{1,0:T(8,128)(2,1)S(1)} collective-permute-done((bf16[64,512]{1,0:T(8,128)(2,1)S(1)}, bf16[64,512]{1,0:T(8,128)(2,1)S(1)}, u32[]{:S(2)}, u32[]{:S(2)}) %collective-permute-start.30) | collective-permute-done | bytes 65568 | tf_op jit(solution)/shard_map/ppermute | solution.py:56
  147.6 0.9 collective-permute-done.29
  148.5 0.7 add_convert_fusion.2
  (123 shorter events, 4.2 us)
Async XLA Ops:
  0.0 74.8 %collective-permute-start.12 = (bf16[512,8192]{1,0:T(8,128)(2,1)}, bf16[512,8192]{1,0:T(8,128)(2,1)}, u32[]{:S(2)}, u32[]{:S(2)}) collective-permute-start(bf16[512,8192]{1,0:T(8,128)(2,1)} %refs_6_.1), channel_id=1, source_target_pairs={{0,1},{1,0},{2,3},{3,2},{4,5},{5,4},{6,7},{7,6},{8,9},{9,8},{10,11... | collective-permute-start | bytes 25165832 | tf_op jit(solution)/shard_map/ppermute | solution.py:56
  1.7 6.2 %copy-start.32 = (s32[64]{0:T(128)S(1)}, s32[64]{0:T(128)}, u32[]{:S(2)}) copy-start(s32[64]{0:T(128)} %param.9) | copy-start | bytes 772
  1.9 14.6 %copy-start.10 = (bf16[1024,256]{1,0:T(8,128)(2,1)}, bf16[1024,256]{1,0:T(8,128)(2,1)S(1)}, u32[]{:S(2)}) copy-start(bf16[1024,256]{1,0:T(8,128)(2,1)S(1)} %get-tuple-element.67.refs_0_) | copy-start | bytes 1572868
  1.9 18.8 %copy-start.11 = (bf16[1024,256]{1,0:T(8,128)(2,1)}, bf16[1024,256]{1,0:T(8,128)(2,1)S(1)}, u32[]{:S(2)}) copy-start(bf16[1024,256]{1,0:T(8,128)(2,1)S(1)} %get-tuple-element.68.refs_1_) | copy-start | bytes 1572868
  1.9 14.6 %copy-start = (bf16[2,32,8192]{2,1,0:T(8,128)(2,1)S(1)}, bf16[2,32,8192]{2,1,0:T(8,128)(2,1)}, u32[]{:S(2)}) copy-start(bf16[2,32,8192]{2,1,0:T(8,128)(2,1)} %param.10) | copy-start | bytes 3145732
  2.0 18.9 %collective-permute-start.2 = (bf16[1024,256]{1,0:T(8,128)(2,1)S(1)}, bf16[1024,256]{1,0:T(8,128)(2,1)S(1)}, u32[]{:S(2)}, u32[]{:S(2)}) collective-permute-start(bf16[1024,256]{1,0:T(8,128)(2,1)S(1)} %get-tuple-element.67.refs_0_), channel_id=1, source_target_pairs={{0,8},{1,9},{2,10},{3,11},{4,0},{5,1},{6,2},{7,3},{8,12},{9,13},{1... | collective-permute-start | bytes 1572872 | tf_op jit(solution)/shard_map/ppermute | solution.py:56
  6.3 8.5 %collective-permute-start = (bf16[512,256]{1,0:T(8,128)(2,1)S(1)}, bf16[512,256]{1,0:T(8,128)(2,1)}, u32[]{:S(2)}, u32[]{:S(2)}) collective-permute-start(bf16[512,256]{1,0:T(8,128)(2,1)S(1)} %get-tuple-element.69), channel_id=1, source_target_pairs={{0,2},{1,3},{2,0},{3,1},{4,6},{5,7},{6,4},{7,5},{8,10},{9,11},{10,... | collective-permute-start | bytes 786440 | tf_op jit(solution)/shard_map/ppermute | solution.py:56
  14.9 7.8 %collective-permute-start.9 = (bf16[512,256]{1,0:T(8,128)(2,1)}, bf16[512,256]{1,0:T(8,128)(2,1)S(1)}, u32[]{:S(2)}, u32[]{:S(2)}) collective-permute-start(bf16[512,256]{1,0:T(8,128)(2,1)} %collective-permute-done), channel_id=1, source_target_pairs={{0,16},{1,17},{2,18},{3,19},{4,20},{5,21},{6,22},{7,23},{8,24},{9,... | collective-permute-start | bytes 786440 | tf_op jit(solution)/shard_map/ppermute | solution.py:56
  16.6 2.2 %copy-start.1 = (bf16[8192,256]{1,0:T(8,128)(2,1)S(1)}, bf16[8192,256]{1,0:T(8,128)(2,1)}, u32[]{:S(2)}) copy-start(bf16[8192,256]{1,0:T(8,128)(2,1)} %weight_ref.1) | copy-start | bytes 12582916
  18.8 7.0 %copy-start.22 = (bf16[512,256]{1,0:T(8,128)(2,1)S(1)}, bf16[512,256]{1,0:T(8,128)(2,1)}, u32[]{:S(2)}) copy-start(bf16[512,256]{1,0:T(8,128)(2,1)} %get-tuple-element.70) | copy-start | bytes 786436
  20.8 19.3 %copy-start.16 = (bf16[1024,256]{1,0:T(8,128)(2,1)}, bf16[1024,256]{1,0:T(8,128)(2,1)S(1)}, u32[]{:S(2)}) copy-start(bf16[1024,256]{1,0:T(8,128)(2,1)S(1)} %collective-permute-done.2.refs_2_) | copy-start | bytes 1572868
  22.7 3.1 %copy-start.31 = (bf16[512,256]{1,0:T(8,128)(2,1)}, bf16[512,256]{1,0:T(8,128)(2,1)S(1)}, u32[]{:S(2)}) copy-start(bf16[512,256]{1,0:T(8,128)(2,1)S(1)} %collective-permute-done.9.refs_9_) | copy-start | bytes 786436
  22.7 16.5 %collective-permute-start.13 = (bf16[1024,256]{1,0:T(8,128)(2,1)S(1)}, bf16[1024,256]{1,0:T(8,128)(2,1)S(1)}, u32[]{:S(2)}, u32[]{:S(2)}) collective-permute-start(bf16[1024,256]{1,0:T(8,128)(2,1)S(1)} %collective-permute-done.2.refs_2_), channel_id=1, source_target_pairs={{0,16},{1,17},{2,18},{3,19},{4,20},{5,21},{6,22},{7,23},{8,24},{9,... | collective-permute-start | bytes 1572872 | tf_op jit(solution)/shard_map/ppermute | solution.py:56
  24.2 12.1 %collective-permute-start.3 = (bf16[1024,256]{1,0:T(8,128)(2,1)S(1)}, bf16[1024,256]{1,0:T(8,128)(2,1)S(1)}, u32[]{:S(2)}, u32[]{:S(2)}) collective-permute-start(bf16[1024,256]{1,0:T(8,128)(2,1)S(1)} %collective-permute-done.2.refs_2_), channel_id=1, source_target_pairs={{0,8},{1,9},{2,10},{3,11},{4,0},{5,1},{6,2},{7,3},{8,12},{9,13},{1... | collective-permute-start | bytes 1572872 | tf_op jit(solution)/shard_map/ppermute | solution.py:56
  25.8 16.9 %copy-start.12 = (bf16[1088,256]{1,0:T(8,128)(2,1)}, bf16[1088,256]{1,0:T(8,128)(2,1)S(1)}, u32[]{:S(2)}) copy-start(bf16[1088,256]{1,0:T(8,128)(2,1)S(1)} %pad_maximum_fusion.refs_0_) | copy-start | bytes 1671172
  25.8 14.3 %collective-permute-start.1 = (bf16[1088,256]{1,0:T(8,128)(2,1)S(1)}, bf16[1088,256]{1,0:T(8,128)(2,1)S(1)}, u32[]{:S(2)}, u32[]{:S(2)}) collective-permute-start(bf16[1088,256]{1,0:T(8,128)(2,1)S(1)} %pad_maximum_fusion.refs_0_), channel_id=1, source_target_pairs={{0,2},{1,3},{2,0},{3,1},{4,6},{5,7},{6,4},{7,5},{8,10},{9,11},{10,... | collective-permute-start | bytes 1671176 | tf_op jit(solution)/shard_map/ppermute | solution.py:56
  36.3 18.0 %copy-start.18 = (bf16[1024,256]{1,0:T(8,128)(2,1)}, bf16[1024,256]{1,0:T(8,128)(2,1)S(1)}, u32[]{:S(2)}) copy-start(bf16[1024,256]{1,0:T(8,128)(2,1)S(1)} %collective-permute-done.3.refs_4_) | copy-start | bytes 1572868
  36.3 14.7 %collective-permute-start.5 = (bf16[1024,256]{1,0:T(8,128)(2,1)S(1)}, bf16[1024,256]{1,0:T(8,128)(2,1)S(1)}, u32[]{:S(2)}, u32[]{:S(2)}) collective-permute-start(bf16[1024,256]{1,0:T(8,128)(2,1)S(1)} %collective-permute-done.3.refs_4_), channel_id=1, source_target_pairs={{0,8},{1,9},{2,10},{3,11},{4,0},{5,1},{6,2},{7,3},{8,12},{9,13},{1... | collective-permute-start | bytes 1572872 | tf_op jit(solution)/shard_map/ppermute | solution.py:56
  38.7 13.8 %collective-permute-start.10 = (bf16[1024,256]{1,0:T(8,128)(2,1)S(1)}, bf16[1024,256]{1,0:T(8,128)(2,1)S(1)}, u32[]{:S(2)}, u32[]{:S(2)}) collective-permute-start(bf16[1024,256]{1,0:T(8,128)(2,1)S(1)} %collective-permute-done.3.refs_4_), channel_id=1, source_target_pairs={{0,16},{1,17},{2,18},{3,19},{4,20},{5,21},{6,22},{7,23},{8,24},{9,... | collective-permute-start | bytes 1572872 | tf_op jit(solution)/shard_map/ppermute | solution.py:56
  39.2 0.8 copy-start.17
  40.1 12.5 %copy-start.13 = (bf16[1024,256]{1,0:T(8,128)(2,1)}, bf16[1024,256]{1,0:T(8,128)(2,1)S(1)}, u32[]{:S(2)}) copy-start(bf16[1024,256]{1,0:T(8,128)(2,1)S(1)} %pad_maximum_fusion.3.refs_2_) | copy-start | bytes 1572868
  40.1 12.5 %copy-start.23 = (bf16[1088,256]{1,0:T(8,128)(2,1)}, bf16[1088,256]{1,0:T(8,128)(2,1)S(1)}, u32[]{:S(2)}) copy-start(bf16[1088,256]{1,0:T(8,128)(2,1)S(1)} %collective-permute-done.1.refs_1_) | copy-start | bytes 1671172
  40.2 12.5 %collective-permute-start.17 = (bf16[1024,256]{1,0:T(8,128)(2,1)S(1)}, bf16[1024,256]{1,0:T(8,128)(2,1)S(1)}, u32[]{:S(2)}, u32[]{:S(2)}) collective-permute-start(bf16[1024,256]{1,0:T(8,128)(2,1)S(1)} %pad_maximum_fusion.3.refs_2_), channel_id=1, source_target_pairs={{0,2},{1,3},{2,0},{3,1},{4,6},{5,7},{6,4},{7,5},{8,10},{9,11},{10,... | collective-permute-start | bytes 1572872 | tf_op jit(solution)/shard_map/ppermute | solution.py:56
  42.7 15.1 %copy-start.3 = (bf16[640,256]{1,0:T(8,128)(2,1)}, bf16[640,256]{1,0:T(8,128)(2,1)S(1)}, u32[]{:S(2)}) copy-start(bf16[640,256]{1,0:T(8,128)(2,1)S(1)} %pad_maximum_fusion.6.refs_0_.refs_8_) | copy-start | bytes 983044
  42.7 12.7 %collective-permute-start.4 = (bf16[640,256]{1,0:T(8,128)(2,1)S(1)}, bf16[640,256]{1,0:T(8,128)(2,1)S(1)}, u32[]{:S(2)}, u32[]{:S(2)}) collective-permute-start(bf16[640,256]{1,0:T(8,128)(2,1)S(1)} %pad_maximum_fusion.6.refs_0_.refs_8_), channel_id=1, source_target_pairs={{0,8},{1,9},{2,10},{3,11},{4,0},{5,1},{6,2},{7,3},{8,12},{9,13},{1... | collective-permute-start | bytes 983048 | tf_op jit(solution)/shard_map/ppermute | solution.py:56
  51.0 7.5 %copy-start.19 = (bf16[1024,256]{1,0:T(8,128)(2,1)}, bf16[1024,256]{1,0:T(8,128)(2,1)S(1)}, u32[]{:S(2)}) copy-start(bf16[1024,256]{1,0:T(8,128)(2,1)S(1)} %collective-permute-done.5.refs_6_) | copy-start | bytes 1572868
  51.0 16.0 %collective-permute-start.14 = (bf16[1024,256]{1,0:T(8,128)(2,1)S(1)}, bf16[1024,256]{1,0:T(8,128)(2,1)S(1)}, u32[]{:S(2)}, u32[]{:S(2)}) collective-permute-start(bf16[1024,256]{1,0:T(8,128)(2,1)S(1)} %collective-permute-done.5.refs_6_), channel_id=1, source_target_pairs={{0,16},{1,17},{2,18},{3,19},{4,20},{5,21},{6,22},{7,23},{8,24},{9,... | collective-permute-start | bytes 1572872 | tf_op jit(solution)/shard_map/ppermute | solution.py:56
  52.5 6.0 %copy-start.20 = (bf16[1024,256]{1,0:T(8,128)(2,1)}, bf16[1024,256]{1,0:T(8,128)(2,1)S(1)}, u32[]{:S(2)}) copy-start(bf16[1024,256]{1,0:T(8,128)(2,1)S(1)} %collective-permute-done.10.refs_5_) | copy-start | bytes 1572868
  52.6 14.4 %copy-start.14 = (bf16[1024,256]{1,0:T(8,128)(2,1)}, bf16[1024,256]{1,0:T(8,128)(2,1)S(1)}, u32[]{:S(2)}) copy-start(bf16[1024,256]{1,0:T(8,128)(2,1)S(1)} %pad_maximum_fusion.4.refs_4_) | copy-start | bytes 1572868
  52.6 14.4 %copy-start.24 = (bf16[1024,256]{1,0:T(8,128)(2,1)}, bf16[1024,256]{1,0:T(8,128)(2,1)S(1)}, u32[]{:S(2)}) copy-start(bf16[1024,256]{1,0:T(8,128)(2,1)S(1)} %collective-permute-done.17.refs_3_) | copy-start | bytes 1572868
  52.6 14.4 %collective-permute-start.18 = (bf16[1024,256]{1,0:T(8,128)(2,1)S(1)}, bf16[1024,256]{1,0:T(8,128)(2,1)S(1)}, u32[]{:S(2)}, u32[]{:S(2)}) collective-permute-start(bf16[1024,256]{1,0:T(8,128)(2,1)S(1)} %pad_maximum_fusion.4.refs_4_), channel_id=1, source_target_pairs={{0,2},{1,3},{2,0},{3,1},{4,6},{5,7},{6,4},{7,5},{8,10},{9,11},{10,... | collective-permute-start | bytes 1572872 | tf_op jit(solution)/shard_map/ppermute | solution.py:56
  55.4 37.3 %copy-start.5 = (bf16[640,256]{1,0:T(8,128)(2,1)}, bf16[640,256]{1,0:T(8,128)(2,1)S(1)}, u32[]{:S(2)}) copy-start(bf16[640,256]{1,0:T(8,128)(2,1)S(1)} %collective-permute-done.4.refs_1_.refs_10_) | copy-start | bytes 983044
  55.4 8.8 %collective-permute-start.6 = (bf16[640,256]{1,0:T(8,128)(2,1)S(1)}, bf16[640,256]{1,0:T(8,128)(2,1)S(1)}, u32[]{:S(2)}, u32[]{:S(2)}) collective-permute-start(bf16[640,256]{1,0:T(8,128)(2,1)S(1)} %collective-permute-done.4.refs_1_.refs_10_), channel_id=1, source_target_pairs={{0,8},{1,9},{2,10},{3,11},{4,0},{5,1},{6,2},{7,3},{8,12},{9,13},{1... | collective-permute-start | bytes 983048 | tf_op jit(solution)/shard_map/ppermute | solution.py:56
  57.8 14.5 %collective-permute-start.11 = (bf16[512,256]{1,0:T(8,128)(2,1)S(1)}, bf16[512,256]{1,0:T(8,128)(2,1)S(1)}, u32[]{:S(2)}, u32[]{:S(2)}) collective-permute-start(bf16[512,256]{1,0:T(8,128)(2,1)S(1)} %slice.120), channel_id=1, source_target_pairs={{0,16},{1,17},{2,18},{3,19},{4,20},{5,21},{6,22},{7,23},{8,24},{9,... | collective-permute-start | bytes 786440 | tf_op jit(solution)/shard_map/ppermute | solution.py:56
  64.2 28.5 %copy-start.6 = (bf16[640,256]{1,0:T(8,128)(2,1)}, bf16[640,256]{1,0:T(8,128)(2,1)S(1)}, u32[]{:S(2)}) copy-start(bf16[640,256]{1,0:T(8,128)(2,1)S(1)} %collective-permute-done.6.refs_2_.refs_12_) | copy-start | bytes 983044
  64.2 7.4 %collective-permute-start.7 = (bf16[640,256]{1,0:T(8,128)(2,1)S(1)}, bf16[640,256]{1,0:T(8,128)(2,1)S(1)}, u32[]{:S(2)}, u32[]{:S(2)}) collective-permute-start(bf16[640,256]{1,0:T(8,128)(2,1)S(1)} %collective-permute-done.6.refs_2_.refs_12_), channel_id=1, source_target_pairs={{0,8},{1,9},{2,10},{3,11},{4,0},{5,1},{6,2},{7,3},{8,12},{9,13},{1... | collective-permute-start | bytes 983048 | tf_op jit(solution)/shard_map/ppermute | solution.py:56
  66.9 5.3 %copy-start.21 = (bf16[1024,256]{1,0:T(8,128)(2,1)}, bf16[1024,256]{1,0:T(8,128)(2,1)S(1)}, u32[]{:S(2)}) copy-start(bf16[1024,256]{1,0:T(8,128)(2,1)S(1)} %collective-permute-done.14.refs_7_) | copy-start | bytes 1572868
  67.0 15.3 %copy-start.15 = (bf16[1024,256]{1,0:T(8,128)(2,1)}, bf16[1024,256]{1,0:T(8,128)(2,1)S(1)}, u32[]{:S(2)}) copy-start(bf16[1024,256]{1,0:T(8,128)(2,1)S(1)} %pad_maximum_fusion.5.refs_6_) | copy-start | bytes 1572868
  67.1 5.2 %copy-start.25 = (bf16[1024,256]{1,0:T(8,128)(2,1)}, bf16[1024,256]{1,0:T(8,128)(2,1)S(1)}, u32[]{:S(2)}) copy-start(bf16[1024,256]{1,0:T(8,128)(2,1)S(1)} %collective-permute-done.18.refs_5_) | copy-start | bytes 1572868
  67.1 15.3 %collective-permute-start.19 = (bf16[1024,256]{1,0:T(8,128)(2,1)S(1)}, bf16[1024,256]{1,0:T(8,128)(2,1)S(1)}, u32[]{:S(2)}, u32[]{:S(2)}) collective-permute-start(bf16[1024,256]{1,0:T(8,128)(2,1)S(1)} %pad_maximum_fusion.5.refs_6_), channel_id=1, source_target_pairs={{0,2},{1,3},{2,0},{3,1},{4,6},{5,7},{6,4},{7,5},{8,10},{9,11},{10,... | collective-permute-start | bytes 1572872 | tf_op jit(solution)/shard_map/ppermute | solution.py:56
  68.7 13.7 %collective-permute-start.15 = (bf16[512,256]{1,0:T(8,128)(2,1)S(1)}, bf16[512,256]{1,0:T(8,128)(2,1)S(1)}, u32[]{:S(2)}, u32[]{:S(2)}) collective-permute-start(bf16[512,256]{1,0:T(8,128)(2,1)S(1)} %slice.121), channel_id=1, source_target_pairs={{0,16},{1,17},{2,18},{3,19},{4,20},{5,21},{6,22},{7,23},{8,24},{9,... | collective-permute-start | bytes 786440 | tf_op jit(solution)/shard_map/ppermute | solution.py:56
  71.5 21.2 %copy-start.7 = (bf16[640,256]{1,0:T(8,128)(2,1)}, bf16[640,256]{1,0:T(8,128)(2,1)S(1)}, u32[]{:S(2)}) copy-start(bf16[640,256]{1,0:T(8,128)(2,1)S(1)} %collective-permute-done.7.refs_3_.refs_14_) | copy-start | bytes 983044
  73.0 9.4 %collective-permute-start.16 = (bf16[512,256]{1,0:T(8,128)(2,1)}, bf16[512,256]{1,0:T(8,128)(2,1)S(1)}, u32[]{:S(2)}, u32[]{:S(2)}) collective-permute-start(bf16[512,256]{1,0:T(8,128)(2,1)} %slice.122), channel_id=1, source_target_pairs={{0,16},{1,17},{2,18},{3,19},{4,20},{5,21},{6,22},{7,23},{8,24},{9,... | collective-permute-start | bytes 786440 | tf_op jit(solution)/shard_map/ppermute | solution.py:56
  82.3 10.4 %copy-start.4 = (bf16[640,256]{1,0:T(8,128)(2,1)S(1)}, bf16[640,256]{1,0:T(8,128)(2,1)}, u32[]{:S(2)}) copy-start(bf16[640,256]{1,0:T(8,128)(2,1)} %copy-done.3) | copy-start | bytes 983044
  82.4 10.2 %copy-start.28 = (bf16[512,256]{1,0:T(8,128)(2,1)}, bf16[512,256]{1,0:T(8,128)(2,1)S(1)}, u32[]{:S(2)}) copy-start(bf16[512,256]{1,0:T(8,128)(2,1)S(1)} %collective-permute-done.15.refs_13_) | copy-start | bytes 786436
  82.4 10.2 %copy-start.29 = (bf16[512,256]{1,0:T(8,128)(2,1)}, bf16[512,256]{1,0:T(8,128)(2,1)S(1)}, u32[]{:S(2)}) copy-start(bf16[512,256]{1,0:T(8,128)(2,1)S(1)} %collective-permute-done.16.refs_15_) | copy-start | bytes 786436
  82.4 0.8 copy-start.26
  92.6 3.2 %collective-permute-start.20 = (bf16[1088,512]{1,0:T(8,128)(2,1)}, bf16[1088,512]{1,0:T(8,128)(2,1)}, u32[]{:S(2)}, u32[]{:S(2)}) collective-permute-start(bf16[1088,512]{1,0:T(8,128)(2,1)} %shard_map.76.refs_2_), channel_id=1, source_target_pairs={{0,1},{1,0},{2,3},{3,2},{4,5},{5,4},{6,7},{7,6},{8,9},{9,8},{10,11... | collective-permute-start | bytes 3342344 | tf_op jit(solution)/shard_map/ppermute | solution.py:56
  93.1 2.7 %copy-start.8 = (bf16[4,128,256]{2,1,0:T(8,128)(2,1)}, bf16[4,128,256]{2,1,0:T(8,128)(2,1)S(1)}, u32[]{:S(2)}) copy-start(bf16[4,128,256]{2,1,0:T(8,128)(2,1)S(1)} %shard_map.74.refs_0_) | copy-start | bytes 786436
  93.1 2.7 %collective-permute-start.8 = (bf16[4,128,256]{2,1,0:T(8,128)(2,1)S(1)}, bf16[4,128,256]{2,1,0:T(8,128)(2,1)S(1)}, u32[]{:S(2)}, u32[]{:S(2)}) collective-permute-start(bf16[4,128,256]{2,1,0:T(8,128)(2,1)S(1)} %shard_map.74.refs_0_), channel_id=1, source_target_pairs={{0,1},{1,0},{2,3},{3,2},{4,5},{5,4},{6,7},{7,6},{8,9},{9,8},{10,11... | collective-permute-start | bytes 786440 | tf_op jit(solution)/shard_map/ppermute | solution.py:56
  95.8 0.7 copy-start.30
  96.5 29.4 %copy-start.2 = (bf16[256,8192]{1,0:T(8,128)(2,1)S(1)}, bf16[256,8192]{1,0:T(8,128)(2,1)}, u32[]{:S(2)}) copy-start(bf16[256,8192]{1,0:T(8,128)(2,1)} %refs_7_.1) | copy-start | bytes 12582916
  108.4 2.4 %collective-permute-start.21 = (bf16[4,2,144,128]{3,2,1,0:T(8,128)(2,1)}, bf16[4,2,144,128]{3,2,1,0:T(8,128)(2,1)S(1)}, u32[]{:S(2)}, u32[]{:S(2)}) collective-permute-start(bf16[4,2,144,128]{3,2,1,0:T(8,128)(2,1)} %get-tuple-element.59), channel_id=1, source_target_pairs={{0,1},{1,0},{2,3},{3,2},{4,5},{5,4},{6,7},{7,6},{8,9},{9,8},{10,11... | collective-permute-start | bytes 884744 | tf_op jit(solution)/shard_map/ppermute | solution.py:56
  109.5 14.7 %collective-permute-start.26 = (f32[64,512]{1,0:T(8,128)}, f32[64,512]{1,0:T(8,128)S(1)}, u32[]{:S(2)}, u32[]{:S(2)}) collective-permute-start(f32[64,512]{1,0:T(8,128)} %get-tuple-element.66), channel_id=1, source_target_pairs={{0,1},{1,0},{2,3},{3,2},{4,5},{5,4},{6,7},{7,6},{8,9},{9,8},{10,11... | collective-permute-start | bytes 393224 | tf_op jit(solution)/shard_map/ppermute | solution.py:56
  110.8 1.0 copy-start.9
  111.8 6.0 %collective-permute-start.22 = (bf16[4,144,128]{2,1,0:T(8,128)(2,1)S(1)}, bf16[4,144,128]{2,1,0:T(8,128)(2,1)S(1)}, u32[]{:S(2)}, u32[]{:S(2)}) collective-permute-start(bf16[4,144,128]{2,1,0:T(8,128)(2,1)S(1)} %get-tuple-element.61), channel_id=1, source_target_pairs={{0,2},{1,3},{2,0},{3,1},{4,6},{5,7},{6,4},{7,5},{8,10},{9,11},{10,... | collective-permute-start | bytes 442376 | tf_op jit(solution)/shard_map/ppermute | solution.py:56
  117.8 7.2 %collective-permute-start.23 = (bf16[144,128]{1,0:T(8,128)(2,1)S(1)}, bf16[144,128]{1,0:T(8,128)(2,1)S(1)}, u32[]{:S(2)}, u32[]{:S(2)}) collective-permute-start(bf16[144,128]{1,0:T(8,128)(2,1)S(1)} %get-tuple-element.63), channel_id=1, source_target_pairs={{0,4},{1,5},{2,6},{3,7},{4,8},{5,9},{6,10},{7,11},{8,12},{9,13},{1... | collective-permute-start | bytes 110600 | tf_op jit(solution)/shard_map/ppermute | solution.py:56
  119.6 5.4 %collective-permute-start.24 = (bf16[144,128]{1,0:T(8,128)(2,1)S(1)}, bf16[144,128]{1,0:T(8,128)(2,1)S(1)}, u32[]{:S(2)}, u32[]{:S(2)}) collective-permute-start(bf16[144,128]{1,0:T(8,128)(2,1)S(1)} %get-tuple-element.64), channel_id=1, source_target_pairs={{0,8},{1,9},{2,10},{3,11},{4,12},{5,13},{6,14},{7,15},{8,0},{9,1},... | collective-permute-start | bytes 110600 | tf_op jit(solution)/shard_map/ppermute | solution.py:56
  121.4 4.5 %collective-permute-start.25 = (bf16[144,128]{1,0:T(8,128)(2,1)S(1)}, bf16[144,128]{1,0:T(8,128)(2,1)S(1)}, u32[]{:S(2)}, u32[]{:S(2)}) collective-permute-start(bf16[144,128]{1,0:T(8,128)(2,1)S(1)} %get-tuple-element.65), channel_id=1, source_target_pairs={{0,12},{1,13},{2,14},{3,15},{4,0},{5,1},{6,2},{7,3},{8,4},{9,5},{1... | collective-permute-start | bytes 110600 | tf_op jit(solution)/shard_map/ppermute | solution.py:56
  127.6 2.0 %collective-permute-start.27 = (bf16[64,4096]{1,0:T(8,128)(2,1)S(1)}, bf16[64,4096]{1,0:T(8,128)(2,1)S(1)}, u32[]{:S(2)}, u32[]{:S(2)}) collective-permute-start(bf16[64,4096]{1,0:T(8,128)(2,1)S(1)} %slice.134), channel_id=1, source_target_pairs={{0,1},{1,0},{2,3},{3,2},{4,5},{5,4},{6,7},{7,6},{8,9},{9,8},{10,11... | collective-permute-start | bytes 1572872 | tf_op jit(solution)/shard_map/ppermute | solution.py:56
  129.8 8.4 %collective-permute-start.28 = (bf16[64,2048]{1,0:T(8,128)(2,1)S(1)}, bf16[64,2048]{1,0:T(8,128)(2,1)S(1)}, u32[]{:S(2)}, u32[]{:S(2)}) collective-permute-start(bf16[64,2048]{1,0:T(8,128)(2,1)S(1)} %slice.136), channel_id=1, source_target_pairs={{0,2},{1,3},{2,0},{3,1},{4,6},{5,7},{6,4},{7,5},{8,10},{9,11},{10,... | collective-permute-start | bytes 786440 | tf_op jit(solution)/shard_map/ppermute | solution.py:56
  138.3 6.4 %collective-permute-start.31 = (bf16[64,512]{1,0:T(8,128)(2,1)S(1)}, bf16[64,512]{1,0:T(8,128)(2,1)S(1)}, u32[]{:S(2)}, u32[]{:S(2)}) collective-permute-start(bf16[64,512]{1,0:T(8,128)(2,1)S(1)} %get-tuple-element.76), channel_id=1, source_target_pairs={{0,12},{1,13},{2,14},{3,15},{4,0},{5,1},{6,2},{7,3},{8,4},{9,5},{1... | collective-permute-start | bytes 196616 | tf_op jit(solution)/shard_map/ppermute | solution.py:56
  142.4 5.2 %collective-permute-start.30 = (bf16[64,512]{1,0:T(8,128)(2,1)S(1)}, bf16[64,512]{1,0:T(8,128)(2,1)S(1)}, u32[]{:S(2)}, u32[]{:S(2)}) collective-permute-start(bf16[64,512]{1,0:T(8,128)(2,1)S(1)} %get-tuple-element.77), channel_id=1, source_target_pairs={{0,8},{1,9},{2,10},{3,11},{4,12},{5,13},{6,14},{7,15},{8,0},{9,1},... | collective-permute-start | bytes 196616 | tf_op jit(solution)/shard_map/ppermute | solution.py:56
  142.4 6.1 %collective-permute-start.29 = (bf16[64,512]{1,0:T(8,128)(2,1)S(1)}, bf16[64,512]{1,0:T(8,128)(2,1)S(1)}, u32[]{:S(2)}, u32[]{:S(2)}) collective-permute-start(bf16[64,512]{1,0:T(8,128)(2,1)S(1)} %get-tuple-element.75), channel_id=1, source_target_pairs={{0,4},{1,5},{2,6},{3,7},{4,8},{5,9},{6,10},{7,11},{8,12},{9,13},{1... | collective-permute-start | bytes 196616 | tf_op jit(solution)/shard_map/ppermute | solution.py:56
  (1 other events, 0.7 us)

commit v14 on v13

--- a/solution.py
+++ b/solution.py
@@ -59,7 +59,7 @@
         return order[(order.index(a) + 1) % deep]
 
     along_ring = lambda v: move(v, lambda g, a, b, c: (g, next_on_ring(a), b, c))
-    along_z = lambda v, k: move(v, lambda g, a, b, c: (g, a + k, b, c))
+    along_z = lambda v, k: move(v, lambda g, a, b, c: (g, a ^ k, b, c))
     along_y = lambda v: move(v, lambda g, a, b, c: (g, a, 1 - b, c))
     along_x = lambda v: move(v, lambda g, a, b, c: (g ^ 1, a, b, c))
     in_chip = lambda v: move(v, lambda g, a, b, c: (g, a, b, 1 - c))
@@ -112,7 +112,7 @@
             pltpu.VMEM((parts, piece, weight.shape[1]), weight.dtype),
             pltpu.SemaphoreType.DMA((parts,)),
         ],
-        compiler_params=pltpu.CompilerParams(vmem_limit_bytes=10 * MIB),
+        compiler_params=pltpu.CompilerParams(vmem_limit_bytes=61 * MIB),
         cost_estimate=LIGHT,
     )(steps, weight, cosine, sine)
 
@@ -292,7 +292,7 @@
 
     def body(place_ref, near_ref, far_ref, *out_refs):
         for k, out_ref in enumerate(out_refs):
-            z = lax.rem(place_ref[0] + k, deep)
+            z = place_ref[0] ^ k
             first, second = near_ref[z], far_ref[z]
             first_top, first_total = read_notes(first[HEAD_DIM:, :])
             second_top, second_total = read_notes(second[HEAD_DIM:, :])
@@ -604,7 +604,7 @@
             both_z[k + 1] = send(along_ring, both_z[k])
         if k == 1:
             theirs_x[0] = send(along_x, value_y)
-        both_x[k] = send(along_x, after(both_z[k], theirs_x[0]))
+        both_x[k] = send(along_x, both_z[k])
         key_full[k] = jnp.concatenate([both_z[k][:width], both_x[k][:width]])
         key_y[k] = send(along_y, after(key_full[k], key_y[k - 1]))
     for k in range(1, deep):
@@ -665,7 +665,7 @@
     out_width = out_weight.shape[1] // devices
     out_blocks = jnp.stack(
         [
-            block((own_a + k) % deep, flip, own_c ^ turned)
+            block(own_a ^ k, flip, own_c ^ turned)
             for turned in (0, 1)
             for flip in (0, 1)
             for k in range(deep)

time: 150 us -> 150 us (level)
  Pallas kernels: 32.9 us -> 35.6 us
    pallas_call x1, Pallas kernels: 1.98 us -> 4.71 us  [project_queries(): pl.pallas_call(body, in_specs=[whole, pl.BlockSpec(memory_space=pltpu.HBM...]
    unnamed x66 -> x60, local copies, waits for them, and re-layouts: 6.28 us -> 4.06 us
  transfers between devices with their start and end apart: 32 -> 32, of which waited for: 16 -> 17; matrix products, arithmetic and copies ran while one was open for 9% -> 10% of each run, Pallas kernels for 7% -> 9%
where the time goes in v14:
time: 150 us; the launch traced here: 149 us
  waiting for transfers between devices  51.8 us (35%)
  starting transfers between devices  41.2 us (27%)
  Pallas kernels  35.6 us (24%)
  local copies, waits for them, and re-layouts  11.3 us (8%)
  other arithmetic  8.83 us (6%)
    ppermute x32, waiting for transfers between devices, move(): return lax.ppermute(value, ('groups', 'sample'), pairs)  51.8 us
    ppermute x32, starting transfers between devices, move(): return lax.ppermute(value, ('groups', 'sample'), pairs)  41.2 us
    pallas_call x2, Pallas kernels, project(): pl.pallas_call(body, in_specs=[pl.BlockSpec(memory_space=pltpu.SMEM)] + [...  16.9 us
    pallas_call x1, Pallas kernels, attend(): pl.pallas_call(body, in_specs=[pl.BlockSpec(memory_space=pltpu.SMEM)] * 3...  11.8 us
    pallas_call x1, Pallas kernels, project_queries(): pl.pallas_call(body, in_specs=[whole, pl.BlockSpec(memory_space=pltpu.HBM...  4.71 us
    unnamed x60, local copies, waits for them, and re-layouts  4.06 us
    sin x1, other arithmetic, rope_tables(): return (jnp.cos(angles), jnp.sin(angles))  3.05 us
  transfers between devices with their start and end apart: 32, of which 17 were waited for; matrix products, arithmetic and copies ran while one was open for 10% of the time, Pallas kernels for 9%

profile of v14, /device:TPU:0, one launch (start us, length us, event | category | flops | bytes accessed | tf_op | source)
XLA Modules:
  0.0 149.4 jit_solution(15255899878018786808)
XLA Ops:
  0.0 0.5 collective-permute-start.12
  0.5 1.3 fusion.5
  1.9 3.6 %collective-permute-start.2 = (bf16[1024,256]{1,0:T(8,128)(2,1)S(1)}, bf16[1024,256]{1,0:T(8,128)(2,1)S(1)}, u32[]{:S(2)}, u32[]{:S(2)}) collective-permute-start(bf16[1024,256]{1,0:T(8,128)(2,1)S(1)} %get-tuple-element.61.refs_0_), channel_id=1, source_target_pairs={{0,8},{1,9},{2,10},{3,11},{4,0},{5,1},{6,2},{7,3},{8,12},{9,13},{1... | collective-permute-start | bytes 1572872 | tf_op jit(solution)/shard_map/ppermute | solution.py:56
  5.6 0.7 fusion.4
  6.3 1.5 %collective-permute-start = (bf16[512,256]{1,0:T(8,128)(2,1)}, bf16[512,256]{1,0:T(8,128)(2,1)}, u32[]{:S(2)}, u32[]{:S(2)}) collective-permute-start(bf16[512,256]{1,0:T(8,128)(2,1)} %get-tuple-element.63), channel_id=1, source_target_pairs={{0,2},{1,3},{2,0},{3,1},{4,6},{5,7},{6,4},{7,5},{8,10},{9,11},{10,... | collective-permute-start | bytes 786440 | tf_op jit(solution)/shard_map/ppermute | solution.py:56
  8.3 3.1 %multiply_sine_fusion = (f32[1024,64]{1,0:T(8,128)}, f32[1024,64]{1,0:T(8,128)}) fusion(f32[64]{0:T(128)S(1)} %multiply_power_fusion, f32[1024]{0:T(1024)S(1)} %convert_bitcast_fusion), kind=kLoop, calls=%fused_computation.1 | loop fusion | flops 65536 | bytes 528640 | tf_op jit(solution)/shard_map/sin | solution.py:23
  11.4 0.6 broadcast_in_dim.21
  12.1 0.6 broadcast_in_dim.36
  12.7 4.7 %shard_map.73.refs_4_ = bf16[64,256]{1,0:T(8,128)(2,1)} custom-call(bf16[64,8192]{1,0:T(8,128)(2,1)} %bitcast.42, bf16[8192,256]{1,0:T(8,128)(2,1)} %weight_ref.1, f32[64,128]{1,0:T(8,128)} %bitcast.47, f32[64,128]{1,0:T(8,128)} %bitcast.48), custom_call_target="tpu_custom_call" | custom-call | flops 1 | bytes 1 | tf_op jit(solution)/shard_map/pallas_call | solution.py:106
  17.4 3.4 %collective-permute-start.3 = (bf16[1024,256]{1,0:T(8,128)(2,1)S(1)}, bf16[1024,256]{1,0:T(8,128)(2,1)S(1)}, u32[]{:S(2)}, u32[]{:S(2)}) collective-permute-start(bf16[1024,256]{1,0:T(8,128)(2,1)S(1)} %collective-permute-done.2.refs_2_), channel_id=1, source_target_pairs={{0,8},{1,9},{2,10},{3,11},{4,0},{5,1},{6,2},{7,3},{8,12},{9,13},{1... | collective-permute-start | bytes 1572872 | tf_op jit(solution)/shard_map/ppermute | solution.py:56
  20.8 1.5 collective-permute-start.13
  22.3 0.8 pad_maximum_fusion.refs_0_
  23.1 1.6 %collective-permute-start.1 = (bf16[1088,256]{1,0:T(8,128)(2,1)S(1)}, bf16[1088,256]{1,0:T(8,128)(2,1)S(1)}, u32[]{:S(2)}, u32[]{:S(2)}) collective-permute-start(bf16[1088,256]{1,0:T(8,128)(2,1)S(1)} %pad_maximum_fusion.refs_0_), channel_id=1, source_target_pairs={{0,2},{1,3},{2,0},{3,1},{4,6},{5,7},{6,4},{7,5},{8,10},{9,11},{10,... | collective-permute-start | bytes 1671176 | tf_op jit(solution)/shard_map/ppermute | solution.py:56
  24.7 0.5 collective-permute-start.9
  25.3 6.6 %collective-permute-done.3.refs_4_ = bf16[1024,256]{1,0:T(8,128)(2,1)S(1)} collective-permute-done((bf16[1024,256]{1,0:T(8,128)(2,1)S(1)}, bf16[1024,256]{1,0:T(8,128)(2,1)S(1)}, u32[]{:S(2)}, u32[]{:S(2)}) %collective-permute-start.3) | collective-permute-done | bytes 524320 | tf_op jit(solution)/shard_map/ppermute | solution.py:56
  31.9 3.4 %collective-permute-start.5 = (bf16[1024,256]{1,0:T(8,128)(2,1)S(1)}, bf16[1024,256]{1,0:T(8,128)(2,1)S(1)}, u32[]{:S(2)}, u32[]{:S(2)}) collective-permute-start(bf16[1024,256]{1,0:T(8,128)(2,1)S(1)} %collective-permute-done.3.refs_4_), channel_id=1, source_target_pairs={{0,8},{1,9},{2,10},{3,11},{4,0},{5,1},{6,2},{7,3},{8,12},{9,13},{1... | collective-permute-start | bytes 1572872 | tf_op jit(solution)/shard_map/ppermute | solution.py:56
  35.3 4.5 %collective-permute-done.9.refs_9_ = bf16[512,256]{1,0:T(8,128)(2,1)} collective-permute-done((bf16[512,256]{1,0:T(8,128)(2,1)}, bf16[512,256]{1,0:T(8,128)(2,1)}, u32[]{:S(2)}, u32[]{:S(2)}) %collective-permute-start.9) | collective-permute-done | bytes 262176 | tf_op jit(solution)/shard_map/ppermute | solution.py:56
  39.8 1.5 collective-permute-start.10
  41.3 0.8 copy-done.17
  42.2 1.6 %collective-permute-start.17 = (bf16[1024,256]{1,0:T(8,128)(2,1)S(1)}, bf16[1024,256]{1,0:T(8,128)(2,1)S(1)}, u32[]{:S(2)}, u32[]{:S(2)}) collective-permute-start(bf16[1024,256]{1,0:T(8,128)(2,1)S(1)} %pad_maximum_fusion.3.refs_2_), channel_id=1, source_target_pairs={{0,2},{1,3},{2,0},{3,1},{4,6},{5,7},{6,4},{7,5},{8,10},{9,11},{10,... | collective-permute-start | bytes 1572872 | tf_op jit(solution)/shard_map/ppermute | solution.py:56
  43.8 1.0 pad_maximum_fusion.6.refs_0_.refs_8_
  44.8 0.7 collective-permute-start.4
  45.6 1.7 %collective-permute-done.5.refs_6_ = bf16[1024,256]{1,0:T(8,128)(2,1)S(1)} collective-permute-done((bf16[1024,256]{1,0:T(8,128)(2,1)S(1)}, bf16[1024,256]{1,0:T(8,128)(2,1)S(1)}, u32[]{:S(2)}, u32[]{:S(2)}) %collective-permute-start.5) | collective-permute-done | bytes 524320 | tf_op jit(solution)/shard_map/ppermute | solution.py:56
  47.2 1.9 %collective-permute-start.14 = (bf16[1024,256]{1,0:T(8,128)(2,1)S(1)}, bf16[1024,256]{1,0:T(8,128)(2,1)S(1)}, u32[]{:S(2)}, u32[]{:S(2)}) collective-permute-start(bf16[1024,256]{1,0:T(8,128)(2,1)S(1)} %collective-permute-done.5.refs_6_), channel_id=1, source_target_pairs={{0,16},{1,17},{2,18},{3,19},{4,20},{5,21},{6,22},{7,23},{8,24},{9,... | collective-permute-start | bytes 1572872 | tf_op jit(solution)/shard_map/ppermute | solution.py:56
  49.1 5.5 %collective-permute-done.10.refs_5_ = bf16[1024,256]{1,0:T(8,128)(2,1)S(1)} collective-permute-done((bf16[1024,256]{1,0:T(8,128)(2,1)S(1)}, bf16[1024,256]{1,0:T(8,128)(2,1)S(1)}, u32[]{:S(2)}, u32[]{:S(2)}) %collective-permute-start.10) | collective-permute-done | bytes 524320 | tf_op jit(solution)/shard_map/ppermute | solution.py:56
  54.8 1.6 %collective-permute-start.18 = (bf16[1024,256]{1,0:T(8,128)(2,1)S(1)}, bf16[1024,256]{1,0:T(8,128)(2,1)S(1)}, u32[]{:S(2)}, u32[]{:S(2)}) collective-permute-start(bf16[1024,256]{1,0:T(8,128)(2,1)S(1)} %pad_maximum_fusion.4.refs_4_), channel_id=1, source_target_pairs={{0,2},{1,3},{2,0},{3,1},{4,6},{5,7},{6,4},{7,5},{8,10},{9,11},{10,... | collective-permute-start | bytes 1572872 | tf_op jit(solution)/shard_map/ppermute | solution.py:56
  56.4 0.7 collective-permute-start.6
  57.1 1.6 %collective-permute-start.11 = (bf16[512,256]{1,0:T(8,128)(2,1)S(1)}, bf16[512,256]{1,0:T(8,128)(2,1)S(1)}, u32[]{:S(2)}, u32[]{:S(2)}) collective-permute-start(bf16[512,256]{1,0:T(8,128)(2,1)S(1)} %slice.120), channel_id=1, source_target_pairs={{0,16},{1,17},{2,18},{3,19},{4,20},{5,21},{6,22},{7,23},{8,24},{9,... | collective-permute-start | bytes 786440 | tf_op jit(solution)/shard_map/ppermute | solution.py:56
  58.7 6.4 %collective-permute-done.6.refs_2_.refs_12_ = bf16[640,256]{1,0:T(8,128)(2,1)S(1)} collective-permute-done((bf16[640,256]{1,0:T(8,128)(2,1)S(1)}, bf16[640,256]{1,0:T(8,128)(2,1)S(1)}, u32[]{:S(2)}, u32[]{:S(2)}) %collective-permute-start.6) | collective-permute-done | bytes 327712 | tf_op jit(solution)/shard_map/ppermute | solution.py:56
  66.0 0.9 collective-permute-done.18.refs_5_
  66.9 1.5 %collective-permute-start.19 = (bf16[1024,256]{1,0:T(8,128)(2,1)S(1)}, bf16[1024,256]{1,0:T(8,128)(2,1)S(1)}, u32[]{:S(2)}, u32[]{:S(2)}) collective-permute-start(bf16[1024,256]{1,0:T(8,128)(2,1)S(1)} %pad_maximum_fusion.5.refs_6_), channel_id=1, source_target_pairs={{0,2},{1,3},{2,0},{3,1},{4,6},{5,7},{6,4},{7,5},{8,10},{9,11},{10,... | collective-permute-start | bytes 1572872 | tf_op jit(solution)/shard_map/ppermute | solution.py:56
  68.5 0.7 collective-permute-start.15
  69.2 3.0 %collective-permute-done.7.refs_3_.refs_14_ = bf16[640,256]{1,0:T(8,128)(2,1)S(1)} collective-permute-done((bf16[640,256]{1,0:T(8,128)(2,1)S(1)}, bf16[640,256]{1,0:T(8,128)(2,1)S(1)}, u32[]{:S(2)}, u32[]{:S(2)}) %collective-permute-start.7) | collective-permute-done | bytes 327712 | tf_op jit(solution)/shard_map/ppermute | solution.py:56
  72.2 0.7 slice.122
  72.9 0.7 copy-done.25
  73.7 2.5 %collective-permute-start.16 = (bf16[512,256]{1,0:T(8,128)(2,1)}, bf16[512,256]{1,0:T(8,128)(2,1)S(1)}, u32[]{:S(2)}, u32[]{:S(2)}) collective-permute-start(bf16[512,256]{1,0:T(8,128)(2,1)} %slice.122), channel_id=1, source_target_pairs={{0,16},{1,17},{2,18},{3,19},{4,20},{5,21},{6,22},{7,23},{8,24},{9,... | collective-permute-start | bytes 786440 | tf_op jit(solution)/shard_map/ppermute | solution.py:56
  76.2 0.7 stack.131.block_ref
  76.9 0.6 stack.130.block_ref
  77.5 7.5 %shard_map.75.refs_9_ = f32[1088,512]{1,0:T(8,128)} custom-call(s32[5]{0:T(128)} %stack.131.block_ref, bf16[512,8192]{1,0:T(8,128)(2,1)} %refs_6_.1, bf16[512,8192]{1,0:T(8,128)(2,1)} %collective-permute-done.12.got_ref.refs_7_, bf16[64,8192]{1,0:T(8,128)(2,1)} %bitcast.43, bf16[1024,256]{1,0:T(8,128)(2,1)} %copy-done.9, bf16[1024,256]{1,0:T(8,128)(2,1)} %copy-done.10, ...), custom_call_target="tpu_custom_call" | custom-call | flops 1 | bytes 1 | tf_op jit(solution)/shard_map/pallas_call | solution.py:226
  85.1 0.8 copy-done.24
  85.9 9.3 %shard_map.76.refs_2_ = bf16[1088,512]{1,0:T(8,128)(2,1)} custom-call(s32[8]{0:T(128)} %stack.130.block_ref, bf16[512,8192]{1,0:T(8,128)(2,1)} %refs_6_.1, bf16[512,8192]{1,0:T(8,128)(2,1)} %collective-permute-done.12.got_ref.refs_7_, bf16[64,8192]{1,0:T(8,128)(2,1)} %bitcast.44, bf16[1088,256]{1,0:T(8,128)(2,1)} %copy-done.11, ...), custom_call_target="tpu_custom_call" | custom-call | flops 1 | bytes 1 | tf_op jit(solution)/shard_map/pallas_call | solution.py:226
  95.8 0.5 collective-permute-start.8
  96.4 0.6 pad_add_fusion.1.block_ref
  97.0 0.7 and_select_fusion.1
  97.7 0.8 collective-permute-done.8.refs_1_
  98.5 0.7 copy-done.28
  99.2 11.8 %shard_map.77 = (bf16[4,2,144,128]{3,2,1,0:T(8,128)(2,1)}, bf16[4,2,144,128]{3,2,1,0:T(8,128)(2,1)}, f32[64,512]{1,0:T(8,128)}) custom-call(s32[4]{0:T(128)} %get-tuple-element.81.place_ref, s32[4]{0:T(128)} %get-tuple-element.82.turn_ref, s32[3]{0:T(128)} %pad_add_fusion.1.block_ref, bf16[4,128,256]{2,1,0:T(8,128)(2,1)} %copy-done.6, ...), custom_call_target="tpu_custom_call" | custom-call | flops 1 | bytes 1 | tf_op jit(solution)/shard_map/pallas_call | solution.py:418
  111.3 0.8 slice.129
  112.5 0.8 slice.130
  113.4 1.0 copy-done.8
  114.7 5.7 %collective-permute-done.22.far_ref = bf16[4,144,128]{2,1,0:T(8,128)(2,1)S(1)} collective-permute-done((bf16[4,144,128]{2,1,0:T(8,128)(2,1)S(1)}, bf16[4,144,128]{2,1,0:T(8,128)(2,1)S(1)}, u32[]{:S(2)}, u32[]{:S(2)}) %collective-permute-start.22) | collective-permute-done | bytes 147488 | tf_op jit(solution)/shard_map/ppermute | solution.py:56
  120.5 0.5 collective-permute-start.23
  121.0 0.6 collective-permute-start.24
  121.6 3.3 %collective-permute-start.25 = (bf16[144,128]{1,0:T(8,128)(2,1)S(1)}, bf16[144,128]{1,0:T(8,128)(2,1)S(1)}, u32[]{:S(2)}, u32[]{:S(2)}) collective-permute-start(bf16[144,128]{1,0:T(8,128)(2,1)S(1)} %get-tuple-element.59), channel_id=1, source_target_pairs={{0,12},{1,13},{2,14},{3,15},{4,8},{5,9},{6,10},{7,11},{8,4},{9,5},... | collective-permute-start | bytes 110600 | tf_op jit(solution)/shard_map/ppermute | solution.py:56
  124.9 0.8 fusion.refs_6_
  126.0 1.4 collective-permute-done.25.refs_3_
  127.4 1.7 %shard_map.80 = bf16[64,8192]{1,0:T(8,128)(2,1)S(1)} custom-call(s32[16]{0:T(128)S(1)} %stack.115.block_ref, bf16[144,128]{1,0:T(8,128)(2,1)S(1)} %get-tuple-element.56.refs_0_, bf16[144,128]{1,0:T(8,128)(2,1)S(1)} %collective-permute-done.23.refs_1_, bf16[144,128]{1,0:T(8,128)(2,1)S(1)} %collective-permute-done.24.refs_2_, ...), custom_call_target="tpu_custom_call" | custom-call | flops 1 | bytes 1 | tf_op jit(solution)/shard_map/pallas_call | solution.py:265
  129.2 1.9 %collective-permute-done.27 = bf16[64,4096]{1,0:T(8,128)(2,1)S(1)} collective-permute-done((bf16[64,4096]{1,0:T(8,128)(2,1)S(1)}, bf16[64,4096]{1,0:T(8,128)(2,1)S(1)}, u32[]{:S(2)}, u32[]{:S(2)}) %collective-permute-start.27) | collective-permute-done | bytes 524320 | tf_op jit(solution)/shard_map/ppermute | solution.py:56
  131.6 8.1 %collective-permute-done.28 = bf16[64,2048]{1,0:T(8,128)(2,1)S(1)} collective-permute-done((bf16[64,2048]{1,0:T(8,128)(2,1)S(1)}, bf16[64,2048]{1,0:T(8,128)(2,1)S(1)}, u32[]{:S(2)}, u32[]{:S(2)}) %collective-permute-start.28) | collective-permute-done | bytes 262176 | tf_op jit(solution)/shard_map/ppermute | solution.py:56
  139.8 3.4 %collective-permute-start.31 = (bf16[64,512]{1,0:T(8,128)(2,1)S(1)}, bf16[64,512]{1,0:T(8,128)(2,1)S(1)}, u32[]{:S(2)}, u32[]{:S(2)}) collective-permute-start(bf16[64,512]{1,0:T(8,128)(2,1)S(1)} %get-tuple-element.70), channel_id=1, source_target_pairs={{0,12},{1,13},{2,14},{3,15},{4,8},{5,9},{6,10},{7,11},{8,4},{9,5},... | collective-permute-start | bytes 196616 | tf_op jit(solution)/shard_map/ppermute | solution.py:56
  143.1 1.1 collective-permute-start.29
  144.2 1.8 %collective-permute-done.31 = bf16[64,512]{1,0:T(8,128)(2,1)S(1)} collective-permute-done((bf16[64,512]{1,0:T(8,128)(2,1)S(1)}, bf16[64,512]{1,0:T(8,128)(2,1)S(1)}, u32[]{:S(2)}, u32[]{:S(2)}) %collective-permute-start.31) | collective-permute-done | bytes 65568 | tf_op jit(solution)/shard_map/ppermute | solution.py:56
  146.0 2.5 %collective-permute-done.30 = bf16[64,512]{1,0:T(8,128)(2,1)S(1)} collective-permute-done((bf16[64,512]{1,0:T(8,128)(2,1)S(1)}, bf16[64,512]{1,0:T(8,128)(2,1)S(1)}, u32[]{:S(2)}, u32[]{:S(2)}) %collective-permute-start.30) | collective-permute-done | bytes 65568 | tf_op jit(solution)/shard_map/ppermute | solution.py:56
  148.8 0.7 add_convert_fusion.2
  (117 shorter events, 4.8 us)
Async XLA Ops:
  0.0 77.5 %collective-permute-start.12 = (bf16[512,8192]{1,0:T(8,128)(2,1)}, bf16[512,8192]{1,0:T(8,128)(2,1)}, u32[]{:S(2)}, u32[]{:S(2)}) collective-permute-start(bf16[512,8192]{1,0:T(8,128)(2,1)} %refs_6_.1), channel_id=1, source_target_pairs={{0,1},{1,0},{2,3},{3,2},{4,5},{5,4},{6,7},{7,6},{8,9},{9,8},{10,11... | collective-permute-start | bytes 25165832 | tf_op jit(solution)/shard_map/ppermute | solution.py:56
  1.7 6.2 %copy-start.29 = (s32[64]{0:T(128)S(1)}, s32[64]{0:T(128)}, u32[]{:S(2)}) copy-start(s32[64]{0:T(128)} %param.9) | copy-start | bytes 772
  1.9 10.8 %copy-start.9 = (bf16[1024,256]{1,0:T(8,128)(2,1)}, bf16[1024,256]{1,0:T(8,128)(2,1)S(1)}, u32[]{:S(2)}) copy-start(bf16[1024,256]{1,0:T(8,128)(2,1)S(1)} %get-tuple-element.61.refs_0_) | copy-start | bytes 1572868
  1.9 15.5 %copy-start.10 = (bf16[1024,256]{1,0:T(8,128)(2,1)}, bf16[1024,256]{1,0:T(8,128)(2,1)S(1)}, u32[]{:S(2)}) copy-start(bf16[1024,256]{1,0:T(8,128)(2,1)S(1)} %get-tuple-element.62.refs_1_) | copy-start | bytes 1572868
  1.9 15.5 %collective-permute-start.2 = (bf16[1024,256]{1,0:T(8,128)(2,1)S(1)}, bf16[1024,256]{1,0:T(8,128)(2,1)S(1)}, u32[]{:S(2)}, u32[]{:S(2)}) collective-permute-start(bf16[1024,256]{1,0:T(8,128)(2,1)S(1)} %get-tuple-element.61.refs_0_), channel_id=1, source_target_pairs={{0,8},{1,9},{2,10},{3,11},{4,0},{5,1},{6,2},{7,3},{8,12},{9,13},{1... | collective-permute-start | bytes 1572872 | tf_op jit(solution)/shard_map/ppermute | solution.py:56
  6.3 16.8 %collective-permute-start = (bf16[512,256]{1,0:T(8,128)(2,1)}, bf16[512,256]{1,0:T(8,128)(2,1)}, u32[]{:S(2)}, u32[]{:S(2)}) collective-permute-start(bf16[512,256]{1,0:T(8,128)(2,1)} %get-tuple-element.63), channel_id=1, source_target_pairs={{0,2},{1,3},{2,0},{3,1},{4,6},{5,7},{6,4},{7,5},{8,10},{9,11},{10,... | collective-permute-start | bytes 786440 | tf_op jit(solution)/shard_map/ppermute | solution.py:56
  17.4 24.8 %copy-start.15 = (bf16[1024,256]{1,0:T(8,128)(2,1)}, bf16[1024,256]{1,0:T(8,128)(2,1)S(1)}, u32[]{:S(2)}) copy-start(bf16[1024,256]{1,0:T(8,128)(2,1)S(1)} %collective-permute-done.2.refs_2_) | copy-start | bytes 1572868
  17.4 14.4 %collective-permute-start.3 = (bf16[1024,256]{1,0:T(8,128)(2,1)S(1)}, bf16[1024,256]{1,0:T(8,128)(2,1)S(1)}, u32[]{:S(2)}, u32[]{:S(2)}) collective-permute-start(bf16[1024,256]{1,0:T(8,128)(2,1)S(1)} %collective-permute-done.2.refs_2_), channel_id=1, source_target_pairs={{0,8},{1,9},{2,10},{3,11},{4,0},{5,1},{6,2},{7,3},{8,12},{9,13},{1... | collective-permute-start | bytes 1572872 | tf_op jit(solution)/shard_map/ppermute | solution.py:56
  20.8 20.5 %collective-permute-start.13 = (bf16[1024,256]{1,0:T(8,128)(2,1)S(1)}, bf16[1024,256]{1,0:T(8,128)(2,1)S(1)}, u32[]{:S(2)}, u32[]{:S(2)}) collective-permute-start(bf16[1024,256]{1,0:T(8,128)(2,1)S(1)} %collective-permute-done.2.refs_2_), channel_id=1, source_target_pairs={{0,16},{1,17},{2,18},{3,19},{4,20},{5,21},{6,22},{7,23},{8,24},{9,... | collective-permute-start | bytes 1572872 | tf_op jit(solution)/shard_map/ppermute | solution.py:56
  23.1 21.7 %copy-start.11 = (bf16[1088,256]{1,0:T(8,128)(2,1)}, bf16[1088,256]{1,0:T(8,128)(2,1)S(1)}, u32[]{:S(2)}) copy-start(bf16[1088,256]{1,0:T(8,128)(2,1)S(1)} %pad_maximum_fusion.refs_0_) | copy-start | bytes 1671172
  23.1 20.7 %copy-start.7 = (bf16[64,256]{1,0:T(8,128)(2,1)S(1)}, bf16[64,256]{1,0:T(8,128)(2,1)}, u32[]{:S(2)}) copy-start(bf16[64,256]{1,0:T(8,128)(2,1)} %shard_map.73.refs_4_) | copy-start | bytes 98308
  23.1 19.1 %collective-permute-start.1 = (bf16[1088,256]{1,0:T(8,128)(2,1)S(1)}, bf16[1088,256]{1,0:T(8,128)(2,1)S(1)}, u32[]{:S(2)}, u32[]{:S(2)}) collective-permute-start(bf16[1088,256]{1,0:T(8,128)(2,1)S(1)} %pad_maximum_fusion.refs_0_), channel_id=1, source_target_pairs={{0,2},{1,3},{2,0},{3,1},{4,6},{5,7},{6,4},{7,5},{8,10},{9,11},{10,... | collective-permute-start | bytes 1671176 | tf_op jit(solution)/shard_map/ppermute | solution.py:56
  24.7 15.1 %collective-permute-start.9 = (bf16[512,256]{1,0:T(8,128)(2,1)}, bf16[512,256]{1,0:T(8,128)(2,1)}, u32[]{:S(2)}, u32[]{:S(2)}) collective-permute-start(bf16[512,256]{1,0:T(8,128)(2,1)} %collective-permute-done), channel_id=1, source_target_pairs={{0,16},{1,17},{2,18},{3,19},{4,20},{5,21},{6,22},{7,23},{8,24},{9,... | collective-permute-start | bytes 786440 | tf_op jit(solution)/shard_map/ppermute | solution.py:56
  31.9 13.7 %copy-start.16 = (bf16[1024,256]{1,0:T(8,128)(2,1)}, bf16[1024,256]{1,0:T(8,128)(2,1)S(1)}, u32[]{:S(2)}) copy-start(bf16[1024,256]{1,0:T(8,128)(2,1)S(1)} %collective-permute-done.3.refs_4_) | copy-start | bytes 1572868
  31.9 15.3 %collective-permute-start.5 = (bf16[1024,256]{1,0:T(8,128)(2,1)S(1)}, bf16[1024,256]{1,0:T(8,128)(2,1)S(1)}, u32[]{:S(2)}, u32[]{:S(2)}) collective-permute-start(bf16[1024,256]{1,0:T(8,128)(2,1)S(1)} %collective-permute-done.3.refs_4_), channel_id=1, source_target_pairs={{0,8},{1,9},{2,10},{3,11},{4,0},{5,1},{6,2},{7,3},{8,12},{9,13},{1... | collective-permute-start | bytes 1572872 | tf_op jit(solution)/shard_map/ppermute | solution.py:56
  39.8 14.9 %collective-permute-start.10 = (bf16[1024,256]{1,0:T(8,128)(2,1)S(1)}, bf16[1024,256]{1,0:T(8,128)(2,1)S(1)}, u32[]{:S(2)}, u32[]{:S(2)}) collective-permute-start(bf16[1024,256]{1,0:T(8,128)(2,1)S(1)} %collective-permute-done.3.refs_4_), channel_id=1, source_target_pairs={{0,16},{1,17},{2,18},{3,19},{4,20},{5,21},{6,22},{7,23},{8,24},{9,... | collective-permute-start | bytes 1572872 | tf_op jit(solution)/shard_map/ppermute | solution.py:56
  41.3 0.8 copy-start.17
  42.2 12.5 %copy-start.12 = (bf16[1024,256]{1,0:T(8,128)(2,1)}, bf16[1024,256]{1,0:T(8,128)(2,1)S(1)}, u32[]{:S(2)}) copy-start(bf16[1024,256]{1,0:T(8,128)(2,1)S(1)} %pad_maximum_fusion.3.refs_2_) | copy-start | bytes 1572868
  42.2 12.5 %copy-start.21 = (bf16[1088,256]{1,0:T(8,128)(2,1)}, bf16[1088,256]{1,0:T(8,128)(2,1)S(1)}, u32[]{:S(2)}) copy-start(bf16[1088,256]{1,0:T(8,128)(2,1)S(1)} %collective-permute-done.1.refs_1_) | copy-start | bytes 1671172
  42.2 12.5 %collective-permute-start.17 = (bf16[1024,256]{1,0:T(8,128)(2,1)S(1)}, bf16[1024,256]{1,0:T(8,128)(2,1)S(1)}, u32[]{:S(2)}, u32[]{:S(2)}) collective-permute-start(bf16[1024,256]{1,0:T(8,128)(2,1)S(1)} %pad_maximum_fusion.3.refs_2_), channel_id=1, source_target_pairs={{0,2},{1,3},{2,0},{3,1},{4,6},{5,7},{6,4},{7,5},{8,10},{9,11},{10,... | collective-permute-start | bytes 1572872 | tf_op jit(solution)/shard_map/ppermute | solution.py:56
  44.8 12.3 %copy-start.1 = (bf16[640,256]{1,0:T(8,128)(2,1)}, bf16[640,256]{1,0:T(8,128)(2,1)S(1)}, u32[]{:S(2)}) copy-start(bf16[640,256]{1,0:T(8,128)(2,1)S(1)} %pad_maximum_fusion.6.refs_0_.refs_8_) | copy-start | bytes 983044
  44.8 11.6 %collective-permute-start.4 = (bf16[640,256]{1,0:T(8,128)(2,1)S(1)}, bf16[640,256]{1,0:T(8,128)(2,1)S(1)}, u32[]{:S(2)}, u32[]{:S(2)}) collective-permute-start(bf16[640,256]{1,0:T(8,128)(2,1)S(1)} %pad_maximum_fusion.6.refs_0_.refs_8_), channel_id=1, source_target_pairs={{0,8},{1,9},{2,10},{3,11},{4,0},{5,1},{6,2},{7,3},{8,12},{9,13},{1... | collective-permute-start | bytes 983048 | tf_op jit(solution)/shard_map/ppermute | solution.py:56
  47.2 11.4 %copy-start.18 = (bf16[1024,256]{1,0:T(8,128)(2,1)}, bf16[1024,256]{1,0:T(8,128)(2,1)S(1)}, u32[]{:S(2)}) copy-start(bf16[1024,256]{1,0:T(8,128)(2,1)S(1)} %collective-permute-done.5.refs_6_) | copy-start | bytes 1572868
  47.2 18.7 %collective-permute-start.14 = (bf16[1024,256]{1,0:T(8,128)(2,1)S(1)}, bf16[1024,256]{1,0:T(8,128)(2,1)S(1)}, u32[]{:S(2)}, u32[]{:S(2)}) collective-permute-start(bf16[1024,256]{1,0:T(8,128)(2,1)S(1)} %collective-permute-done.5.refs_6_), channel_id=1, source_target_pairs={{0,16},{1,17},{2,18},{3,19},{4,20},{5,21},{6,22},{7,23},{8,24},{9,... | collective-permute-start | bytes 1572872 | tf_op jit(solution)/shard_map/ppermute | solution.py:56
  54.7 4.0 %copy-start.19 = (bf16[1024,256]{1,0:T(8,128)(2,1)}, bf16[1024,256]{1,0:T(8,128)(2,1)S(1)}, u32[]{:S(2)}) copy-start(bf16[1024,256]{1,0:T(8,128)(2,1)S(1)} %collective-permute-done.10.refs_5_) | copy-start | bytes 1572868
  54.8 11.2 %copy-start.13 = (bf16[1024,256]{1,0:T(8,128)(2,1)}, bf16[1024,256]{1,0:T(8,128)(2,1)S(1)}, u32[]{:S(2)}) copy-start(bf16[1024,256]{1,0:T(8,128)(2,1)S(1)} %pad_maximum_fusion.4.refs_4_) | copy-start | bytes 1572868
  54.8 11.2 %copy-start.22 = (bf16[1024,256]{1,0:T(8,128)(2,1)}, bf16[1024,256]{1,0:T(8,128)(2,1)S(1)}, u32[]{:S(2)}) copy-start(bf16[1024,256]{1,0:T(8,128)(2,1)S(1)} %collective-permute-done.17.refs_3_) | copy-start | bytes 1572868
  54.8 12.2 %collective-permute-start.18 = (bf16[1024,256]{1,0:T(8,128)(2,1)S(1)}, bf16[1024,256]{1,0:T(8,128)(2,1)S(1)}, u32[]{:S(2)}, u32[]{:S(2)}) collective-permute-start(bf16[1024,256]{1,0:T(8,128)(2,1)S(1)} %pad_maximum_fusion.4.refs_4_), channel_id=1, source_target_pairs={{0,2},{1,3},{2,0},{3,1},{4,6},{5,7},{6,4},{7,5},{8,10},{9,11},{10,... | collective-permute-start | bytes 1572872 | tf_op jit(solution)/shard_map/ppermute | solution.py:56
  56.4 39.0 %copy-start.3 = (bf16[640,256]{1,0:T(8,128)(2,1)}, bf16[640,256]{1,0:T(8,128)(2,1)S(1)}, u32[]{:S(2)}) copy-start(bf16[640,256]{1,0:T(8,128)(2,1)S(1)} %collective-permute-done.4.refs_1_.refs_10_) | copy-start | bytes 983044
  56.4 8.7 %collective-permute-start.6 = (bf16[640,256]{1,0:T(8,128)(2,1)S(1)}, bf16[640,256]{1,0:T(8,128)(2,1)S(1)}, u32[]{:S(2)}, u32[]{:S(2)}) collective-permute-start(bf16[640,256]{1,0:T(8,128)(2,1)S(1)} %collective-permute-done.4.refs_1_.refs_10_), channel_id=1, source_target_pairs={{0,8},{1,9},{2,10},{3,11},{4,0},{5,1},{6,2},{7,3},{8,12},{9,13},{1... | collective-permute-start | bytes 983048 | tf_op jit(solution)/shard_map/ppermute | solution.py:56
  57.1 15.8 %collective-permute-start.11 = (bf16[512,256]{1,0:T(8,128)(2,1)S(1)}, bf16[512,256]{1,0:T(8,128)(2,1)S(1)}, u32[]{:S(2)}, u32[]{:S(2)}) collective-permute-start(bf16[512,256]{1,0:T(8,128)(2,1)S(1)} %slice.120), channel_id=1, source_target_pairs={{0,16},{1,17},{2,18},{3,19},{4,20},{5,21},{6,22},{7,23},{8,24},{9,... | collective-permute-start | bytes 786440 | tf_op jit(solution)/shard_map/ppermute | solution.py:56
  65.1 30.3 %copy-start.4 = (bf16[640,256]{1,0:T(8,128)(2,1)}, bf16[640,256]{1,0:T(8,128)(2,1)S(1)}, u32[]{:S(2)}) copy-start(bf16[640,256]{1,0:T(8,128)(2,1)S(1)} %collective-permute-done.6.refs_2_.refs_12_) | copy-start | bytes 983044
  65.1 7.1 %collective-permute-start.7 = (bf16[640,256]{1,0:T(8,128)(2,1)S(1)}, bf16[640,256]{1,0:T(8,128)(2,1)S(1)}, u32[]{:S(2)}, u32[]{:S(2)}) collective-permute-start(bf16[640,256]{1,0:T(8,128)(2,1)S(1)} %collective-permute-done.6.refs_2_.refs_12_), channel_id=1, source_target_pairs={{0,8},{1,9},{2,10},{3,11},{4,0},{5,1},{6,2},{7,3},{8,12},{9,13},{1... | collective-permute-start | bytes 983048 | tf_op jit(solution)/shard_map/ppermute | solution.py:56
  65.9 7.0 %copy-start.20 = (bf16[1024,256]{1,0:T(8,128)(2,1)}, bf16[1024,256]{1,0:T(8,128)(2,1)S(1)}, u32[]{:S(2)}) copy-start(bf16[1024,256]{1,0:T(8,128)(2,1)S(1)} %collective-permute-done.14.refs_7_) | copy-start | bytes 1572868
  66.0 19.0 %copy-start.14 = (bf16[1024,256]{1,0:T(8,128)(2,1)}, bf16[1024,256]{1,0:T(8,128)(2,1)S(1)}, u32[]{:S(2)}) copy-start(bf16[1024,256]{1,0:T(8,128)(2,1)S(1)} %pad_maximum_fusion.5.refs_6_) | copy-start | bytes 1572868
  66.9 6.0 %copy-start.23 = (bf16[1024,256]{1,0:T(8,128)(2,1)}, bf16[1024,256]{1,0:T(8,128)(2,1)S(1)}, u32[]{:S(2)}) copy-start(bf16[1024,256]{1,0:T(8,128)(2,1)S(1)} %collective-permute-done.18.refs_5_) | copy-start | bytes 1572868
  66.9 18.1 %collective-permute-start.19 = (bf16[1024,256]{1,0:T(8,128)(2,1)S(1)}, bf16[1024,256]{1,0:T(8,128)(2,1)S(1)}, u32[]{:S(2)}, u32[]{:S(2)}) collective-permute-start(bf16[1024,256]{1,0:T(8,128)(2,1)S(1)} %pad_maximum_fusion.5.refs_6_), channel_id=1, source_target_pairs={{0,2},{1,3},{2,0},{3,1},{4,6},{5,7},{6,4},{7,5},{8,10},{9,11},{10,... | collective-permute-start | bytes 1572872 | tf_op jit(solution)/shard_map/ppermute | solution.py:56
  68.5 16.6 %collective-permute-start.15 = (bf16[512,256]{1,0:T(8,128)(2,1)S(1)}, bf16[512,256]{1,0:T(8,128)(2,1)S(1)}, u32[]{:S(2)}, u32[]{:S(2)}) collective-permute-start(bf16[512,256]{1,0:T(8,128)(2,1)S(1)} %slice.121), channel_id=1, source_target_pairs={{0,16},{1,17},{2,18},{3,19},{4,20},{5,21},{6,22},{7,23},{8,24},{9,... | collective-permute-start | bytes 786440 | tf_op jit(solution)/shard_map/ppermute | solution.py:56
  72.2 23.2 %copy-start.5 = (bf16[640,256]{1,0:T(8,128)(2,1)}, bf16[640,256]{1,0:T(8,128)(2,1)S(1)}, u32[]{:S(2)}) copy-start(bf16[640,256]{1,0:T(8,128)(2,1)S(1)} %collective-permute-done.7.refs_3_.refs_14_) | copy-start | bytes 983044
  72.9 0.7 copy-start.25
  73.7 11.4 %collective-permute-start.16 = (bf16[512,256]{1,0:T(8,128)(2,1)}, bf16[512,256]{1,0:T(8,128)(2,1)S(1)}, u32[]{:S(2)}, u32[]{:S(2)}) collective-permute-start(bf16[512,256]{1,0:T(8,128)(2,1)} %slice.122), channel_id=1, source_target_pairs={{0,16},{1,17},{2,18},{3,19},{4,20},{5,21},{6,22},{7,23},{8,24},{9,... | collective-permute-start | bytes 786440 | tf_op jit(solution)/shard_map/ppermute | solution.py:56
  85.0 10.3 %copy-start.2 = (bf16[640,256]{1,0:T(8,128)(2,1)S(1)}, bf16[640,256]{1,0:T(8,128)(2,1)}, u32[]{:S(2)}) copy-start(bf16[640,256]{1,0:T(8,128)(2,1)} %copy-done.1) | copy-start | bytes 983044
  85.1 10.2 %copy-start.26 = (bf16[512,256]{1,0:T(8,128)(2,1)}, bf16[512,256]{1,0:T(8,128)(2,1)S(1)}, u32[]{:S(2)}) copy-start(bf16[512,256]{1,0:T(8,128)(2,1)S(1)} %collective-permute-done.15.refs_13_) | copy-start | bytes 786436
  85.1 10.2 %copy-start.27 = (bf16[512,256]{1,0:T(8,128)(2,1)}, bf16[512,256]{1,0:T(8,128)(2,1)S(1)}, u32[]{:S(2)}) copy-start(bf16[512,256]{1,0:T(8,128)(2,1)S(1)} %collective-permute-done.16.refs_15_) | copy-start | bytes 786436
  85.1 0.8 copy-start.24
  95.3 3.2 %collective-permute-start.20 = (bf16[1088,512]{1,0:T(8,128)(2,1)}, bf16[1088,512]{1,0:T(8,128)(2,1)}, u32[]{:S(2)}, u32[]{:S(2)}) collective-permute-start(bf16[1088,512]{1,0:T(8,128)(2,1)} %shard_map.76.refs_2_), channel_id=1, source_target_pairs={{0,1},{1,0},{2,3},{3,2},{4,5},{5,4},{6,7},{7,6},{8,9},{9,8},{10,11... | collective-permute-start | bytes 3342344 | tf_op jit(solution)/shard_map/ppermute | solution.py:56
  95.8 2.7 %copy-start.6 = (bf16[4,128,256]{2,1,0:T(8,128)(2,1)}, bf16[4,128,256]{2,1,0:T(8,128)(2,1)S(1)}, u32[]{:S(2)}) copy-start(bf16[4,128,256]{2,1,0:T(8,128)(2,1)S(1)} %shard_map.74.refs_0_) | copy-start | bytes 786436
  95.8 2.7 %collective-permute-start.8 = (bf16[4,128,256]{2,1,0:T(8,128)(2,1)S(1)}, bf16[4,128,256]{2,1,0:T(8,128)(2,1)S(1)}, u32[]{:S(2)}, u32[]{:S(2)}) collective-permute-start(bf16[4,128,256]{2,1,0:T(8,128)(2,1)S(1)} %shard_map.74.refs_0_), channel_id=1, source_target_pairs={{0,1},{1,0},{2,3},{3,2},{4,5},{5,4},{6,7},{7,6},{8,9},{9,8},{10,11... | collective-permute-start | bytes 786440 | tf_op jit(solution)/shard_map/ppermute | solution.py:56
  98.5 0.7 copy-start.28
  99.2 28.2 %copy-start = (bf16[256,8192]{1,0:T(8,128)(2,1)S(1)}, bf16[256,8192]{1,0:T(8,128)(2,1)}, u32[]{:S(2)}) copy-start(bf16[256,8192]{1,0:T(8,128)(2,1)} %refs_7_.1) | copy-start | bytes 12582916
  111.0 2.4 %collective-permute-start.21 = (bf16[4,2,144,128]{3,2,1,0:T(8,128)(2,1)}, bf16[4,2,144,128]{3,2,1,0:T(8,128)(2,1)S(1)}, u32[]{:S(2)}, u32[]{:S(2)}) collective-permute-start(bf16[4,2,144,128]{3,2,1,0:T(8,128)(2,1)} %get-tuple-element.53), channel_id=1, source_target_pairs={{0,1},{1,0},{2,3},{3,2},{4,5},{5,4},{6,7},{7,6},{8,9},{9,8},{10,11... | collective-permute-start | bytes 884744 | tf_op jit(solution)/shard_map/ppermute | solution.py:56
  112.2 12.8 %collective-permute-start.26 = (f32[64,512]{1,0:T(8,128)}, f32[64,512]{1,0:T(8,128)S(1)}, u32[]{:S(2)}, u32[]{:S(2)}) collective-permute-start(f32[64,512]{1,0:T(8,128)} %get-tuple-element.60), channel_id=1, source_target_pairs={{0,1},{1,0},{2,3},{3,2},{4,5},{5,4},{6,7},{7,6},{8,9},{9,8},{10,11... | collective-permute-start | bytes 393224 | tf_op jit(solution)/shard_map/ppermute | solution.py:56
  113.4 1.0 copy-start.8
  114.4 6.0 %collective-permute-start.22 = (bf16[4,144,128]{2,1,0:T(8,128)(2,1)S(1)}, bf16[4,144,128]{2,1,0:T(8,128)(2,1)S(1)}, u32[]{:S(2)}, u32[]{:S(2)}) collective-permute-start(bf16[4,144,128]{2,1,0:T(8,128)(2,1)S(1)} %get-tuple-element.55), channel_id=1, source_target_pairs={{0,2},{1,3},{2,0},{3,1},{4,6},{5,7},{6,4},{7,5},{8,10},{9,11},{10,... | collective-permute-start | bytes 442376 | tf_op jit(solution)/shard_map/ppermute | solution.py:56
  120.5 5.2 %collective-permute-start.23 = (bf16[144,128]{1,0:T(8,128)(2,1)S(1)}, bf16[144,128]{1,0:T(8,128)(2,1)S(1)}, u32[]{:S(2)}, u32[]{:S(2)}) collective-permute-start(bf16[144,128]{1,0:T(8,128)(2,1)S(1)} %get-tuple-element.57), channel_id=1, source_target_pairs={{0,4},{1,5},{2,6},{3,7},{4,0},{5,1},{6,2},{7,3},{8,12},{9,13},{10,... | collective-permute-start | bytes 110600 | tf_op jit(solution)/shard_map/ppermute | solution.py:56
  121.0 5.0 %collective-permute-start.24 = (bf16[144,128]{1,0:T(8,128)(2,1)S(1)}, bf16[144,128]{1,0:T(8,128)(2,1)S(1)}, u32[]{:S(2)}, u32[]{:S(2)}) collective-permute-start(bf16[144,128]{1,0:T(8,128)(2,1)S(1)} %get-tuple-element.58), channel_id=1, source_target_pairs={{0,8},{1,9},{2,10},{3,11},{4,12},{5,13},{6,14},{7,15},{8,0},{9,1},... | collective-permute-start | bytes 110600 | tf_op jit(solution)/shard_map/ppermute | solution.py:56
  121.6 5.8 %collective-permute-start.25 = (bf16[144,128]{1,0:T(8,128)(2,1)S(1)}, bf16[144,128]{1,0:T(8,128)(2,1)S(1)}, u32[]{:S(2)}, u32[]{:S(2)}) collective-permute-start(bf16[144,128]{1,0:T(8,128)(2,1)S(1)} %get-tuple-element.59), channel_id=1, source_target_pairs={{0,12},{1,13},{2,14},{3,15},{4,8},{5,9},{6,10},{7,11},{8,4},{9,5},... | collective-permute-start | bytes 110600 | tf_op jit(solution)/shard_map/ppermute | solution.py:56
  129.1 2.0 %collective-permute-start.27 = (bf16[64,4096]{1,0:T(8,128)(2,1)S(1)}, bf16[64,4096]{1,0:T(8,128)(2,1)S(1)}, u32[]{:S(2)}, u32[]{:S(2)}) collective-permute-start(bf16[64,4096]{1,0:T(8,128)(2,1)S(1)} %slice.134), channel_id=1, source_target_pairs={{0,1},{1,0},{2,3},{3,2},{4,5},{5,4},{6,7},{7,6},{8,9},{9,8},{10,11... | collective-permute-start | bytes 1572872 | tf_op jit(solution)/shard_map/ppermute | solution.py:56
  131.3 8.4 %collective-permute-start.28 = (bf16[64,2048]{1,0:T(8,128)(2,1)S(1)}, bf16[64,2048]{1,0:T(8,128)(2,1)S(1)}, u32[]{:S(2)}, u32[]{:S(2)}) collective-permute-start(bf16[64,2048]{1,0:T(8,128)(2,1)S(1)} %slice.136), channel_id=1, source_target_pairs={{0,2},{1,3},{2,0},{3,1},{4,6},{5,7},{6,4},{7,5},{8,10},{9,11},{10,... | collective-permute-start | bytes 786440 | tf_op jit(solution)/shard_map/ppermute | solution.py:56
  139.8 6.2 %collective-permute-start.31 = (bf16[64,512]{1,0:T(8,128)(2,1)S(1)}, bf16[64,512]{1,0:T(8,128)(2,1)S(1)}, u32[]{:S(2)}, u32[]{:S(2)}) collective-permute-start(bf16[64,512]{1,0:T(8,128)(2,1)S(1)} %get-tuple-element.70), channel_id=1, source_target_pairs={{0,12},{1,13},{2,14},{3,15},{4,8},{5,9},{6,10},{7,11},{8,4},{9,5},... | collective-permute-start | bytes 196616 | tf_op jit(solution)/shard_map/ppermute | solution.py:56
  143.1 5.4 %collective-permute-start.30 = (bf16[64,512]{1,0:T(8,128)(2,1)S(1)}, bf16[64,512]{1,0:T(8,128)(2,1)S(1)}, u32[]{:S(2)}, u32[]{:S(2)}) collective-permute-start(bf16[64,512]{1,0:T(8,128)(2,1)S(1)} %get-tuple-element.71), channel_id=1, source_target_pairs={{0,8},{1,9},{2,10},{3,11},{4,12},{5,13},{6,14},{7,15},{8,0},{9,1},... | collective-permute-start | bytes 196616 | tf_op jit(solution)/shard_map/ppermute | solution.py:56
  143.1 5.6 %collective-permute-start.29 = (bf16[64,512]{1,0:T(8,128)(2,1)S(1)}, bf16[64,512]{1,0:T(8,128)(2,1)S(1)}, u32[]{:S(2)}, u32[]{:S(2)}) collective-permute-start(bf16[64,512]{1,0:T(8,128)(2,1)S(1)} %get-tuple-element.69), channel_id=1, source_target_pairs={{0,4},{1,5},{2,6},{3,7},{4,0},{5,1},{6,2},{7,3},{8,12},{9,13},{10,... | collective-permute-start | bytes 196616 | tf_op jit(solution)/shard_map/ppermute | solution.py:56

commit v15 on v14

--- a/solution.py
+++ b/solution.py
@@ -594,16 +594,16 @@
 
     got = in_chip(prompt_states)
     both_z, both_x, theirs, theirs_x = {0: both_mine}, {0: both_other}, {}, {}
+    value_y = send(along_y, value_weight)
     both_z[1] = send(along_ring, both_mine)
-    value_y = send(along_y, both_mine[width:])
+    theirs_x[0] = jnp.where(first, value_y[:, half:], value_y[:, :half])
+    value_y = jnp.where(first, value_y[:, :half], value_y[:, half:])
     key_full = {0: jnp.concatenate([both_mine[:width], both_other[:width], packed_queries])}
     key_y = {0: send(along_y, after(key_full[0], value_y))}
     theirs[0] = jnp.concatenate([value_y, packed_queries, key_y[0][2 * width :]])
     for k in range(1, deep):
         if k + 1 < deep:
             both_z[k + 1] = send(along_ring, both_z[k])
-        if k == 1:
-            theirs_x[0] = send(along_x, value_y)
         both_x[k] = send(along_x, both_z[k])
         key_full[k] = jnp.concatenate([both_z[k][:width], both_x[k][:width]])
         key_y[k] = send(along_y, after(key_full[k], key_y[k - 1]))

time: 150 us -> 147 us (0.980)
  waiting for transfers between devices: 51.8 us -> 47.4 us
  starting transfers between devices: 41.2 us -> 42.9 us
    ppermute x32 -> x31, waiting for transfers between devices: 51.8 us -> 47.4 us  [move(): return lax.ppermute(value, ('groups', 'sample'), pairs)]
    select_n x0 -> x1, other arithmetic: none -> 1.78 us  [on_device(): theirs_x[0] = jnp.where(first, value_y[:, half:], value_y[:, :half])]
    ppermute x32 -> x31, starting transfers between devices: 41.2 us -> 42.9 us  [move(): return lax.ppermute(value, ('groups', 'sample'), pairs)]
    unnamed x60 -> x62, local copies, waits for them, and re-layouts: 4.06 us -> 4.1 us
  transfers between devices with their start and end apart: 32 -> 31, of which waited for: 17 -> 17; matrix products, arithmetic and copies ran while one was open for 10% -> 10% of each run, Pallas kernels for 9% -> 9%
where the time goes in v15:
time: 147 us
  waiting for transfers between devices  47.4 us (32%)
  starting transfers between devices  42.9 us (29%)
  Pallas kernels  35.6 us (24%)
  local copies, waits for them, and re-layouts  10.5 us (7%)
  other arithmetic  9.67 us (7%)
    ppermute x31, waiting for transfers between devices, move(): return lax.ppermute(value, ('groups', 'sample'), pairs)  47.4 us
    ppermute x31, starting transfers between devices, move(): return lax.ppermute(value, ('groups', 'sample'), pairs)  42.9 us
    pallas_call x2, Pallas kernels, project(): pl.pallas_call(body, in_specs=[pl.BlockSpec(memory_space=pltpu.SMEM)] + [...  16.9 us
    pallas_call x1, Pallas kernels, attend(): pl.pallas_call(body, in_specs=[pl.BlockSpec(memory_space=pltpu.SMEM)] * 3...  11.9 us
    pallas_call x1, Pallas kernels, project_queries(): pl.pallas_call(body, in_specs=[whole, pl.BlockSpec(memory_space=pltpu.HBM...  4.71 us
    unnamed x62, local copies, waits for them, and re-layouts  4.1 us
    sin x1, other arithmetic, rope_tables(): return (jnp.cos(angles), jnp.sin(angles))  3.06 us
  transfers between devices with their start and end apart: 31, of which 17 were waited for; matrix products, arithmetic and copies ran while one was open for 10% of the time, Pallas kernels for 9%

profile of v15, /device:TPU:0, one launch (start us, length us, event | category | flops | bytes accessed | tf_op | source)
XLA Modules:
  0.0 146.7 jit_solution(9009551638014698839)
XLA Ops:
  0.5 2.6 %collective-permute-start = (bf16[512,512]{1,0:T(8,128)(2,1)}, bf16[512,512]{1,0:T(8,128)(2,1)}, u32[]{:S(2)}, u32[]{:S(2)}) collective-permute-start(bf16[512,512]{1,0:T(8,128)(2,1)} %param.12), channel_id=1, source_target_pairs={{0,2},{1,3},{2,0},{3,1},{4,6},{5,7},{6,4},{7,5},{8,10},{9,11},{10,... | collective-permute-start | bytes 1572872 | tf_op jit(solution)/shard_map/ppermute | solution.py:56
  3.0 1.1 fusion.5
  4.4 2.6 %collective-permute-start.2 = (bf16[1024,256]{1,0:T(8,128)(2,1)S(1)}, bf16[1024,256]{1,0:T(8,128)(2,1)S(1)}, u32[]{:S(2)}, u32[]{:S(2)}) collective-permute-start(bf16[1024,256]{1,0:T(8,128)(2,1)S(1)} %get-tuple-element.59.refs_0_), channel_id=1, source_target_pairs={{0,8},{1,9},{2,10},{3,11},{4,0},{5,1},{6,2},{7,3},{8,12},{9,13},{1... | collective-permute-start | bytes 1572872 | tf_op jit(solution)/shard_map/ppermute | solution.py:56
  7.4 3.1 %multiply_sine_fusion = (f32[1024,64]{1,0:T(8,128)}, f32[1024,64]{1,0:T(8,128)}) fusion(f32[64]{0:T(128)S(1)} %multiply_power_fusion, f32[1024]{0:T(1024)S(1)} %convert_bitcast_fusion), kind=kLoop, calls=%fused_computation.1 | loop fusion | flops 65536 | bytes 528640 | tf_op jit(solution)/shard_map/sin | solution.py:23
  10.6 0.6 broadcast_in_dim.21
  11.3 0.6 broadcast_in_dim.36
  11.9 4.7 %shard_map.73.refs_4_ = bf16[64,256]{1,0:T(8,128)(2,1)} custom-call(bf16[64,8192]{1,0:T(8,128)(2,1)} %bitcast.42, bf16[8192,256]{1,0:T(8,128)(2,1)} %weight_ref.1, f32[64,128]{1,0:T(8,128)} %bitcast.47, f32[64,128]{1,0:T(8,128)} %bitcast.48), custom_call_target="tpu_custom_call" | custom-call | flops 1 | bytes 1 | tf_op jit(solution)/shard_map/pallas_call | solution.py:106
  16.7 0.8 pad_maximum_fusion.refs_0_
  17.5 1.1 collective-permute-done.2.refs_2_
  18.5 3.4 %collective-permute-start.3 = (bf16[1024,256]{1,0:T(8,128)(2,1)S(1)}, bf16[1024,256]{1,0:T(8,128)(2,1)S(1)}, u32[]{:S(2)}, u32[]{:S(2)}) collective-permute-start(bf16[1024,256]{1,0:T(8,128)(2,1)S(1)} %collective-permute-done.2.refs_2_), channel_id=1, source_target_pairs={{0,8},{1,9},{2,10},{3,11},{4,0},{5,1},{6,2},{7,3},{8,12},{9,13},{1... | collective-permute-start | bytes 1572872 | tf_op jit(solution)/shard_map/ppermute | solution.py:56
  21.9 1.5 %collective-permute-start.12 = (bf16[1024,256]{1,0:T(8,128)(2,1)S(1)}, bf16[1024,256]{1,0:T(8,128)(2,1)S(1)}, u32[]{:S(2)}, u32[]{:S(2)}) collective-permute-start(bf16[1024,256]{1,0:T(8,128)(2,1)S(1)} %collective-permute-done.2.refs_2_), channel_id=1, source_target_pairs={{0,16},{1,17},{2,18},{3,19},{4,20},{5,21},{6,22},{7,23},{8,24},{9,... | collective-permute-start | bytes 1572872 | tf_op jit(solution)/shard_map/ppermute | solution.py:56
  23.4 1.8 %broadcast_select_fusion.2 = (bf16[512,256]{1,0:T(8,128)(2,1)}, bf16[512,256]{1,0:T(8,128)(2,1)S(1)}) fusion(pred[]{:T(512)S(6)} %eq.29, bf16[512,512]{1,0:T(8,128)(2,1)} %collective-permute-done), kind=kLoop, calls=%fused_computation.13 | loop fusion | flops 262144 | bytes 1048577 | tf_op jit(solution)/shard_map/jit(_where)/select_n | solution.py:599
  25.2 0.5 collective-permute-start.1
  25.7 6.9 %collective-permute-done.3.refs_4_ = bf16[1024,256]{1,0:T(8,128)(2,1)S(1)} collective-permute-done((bf16[1024,256]{1,0:T(8,128)(2,1)S(1)}, bf16[1024,256]{1,0:T(8,128)(2,1)S(1)}, u32[]{:S(2)}, u32[]{:S(2)}) %collective-permute-start.3) | collective-permute-done | bytes 524320 | tf_op jit(solution)/shard_map/ppermute | solution.py:56
  32.6 3.4 %collective-permute-start.5 = (bf16[1024,256]{1,0:T(8,128)(2,1)S(1)}, bf16[1024,256]{1,0:T(8,128)(2,1)S(1)}, u32[]{:S(2)}, u32[]{:S(2)}) collective-permute-start(bf16[1024,256]{1,0:T(8,128)(2,1)S(1)} %collective-permute-done.3.refs_4_), channel_id=1, source_target_pairs={{0,8},{1,9},{2,10},{3,11},{4,0},{5,1},{6,2},{7,3},{8,12},{9,13},{1... | collective-permute-start | bytes 1572872 | tf_op jit(solution)/shard_map/ppermute | solution.py:56
  36.0 1.5 %collective-permute-start.9 = (bf16[1024,256]{1,0:T(8,128)(2,1)S(1)}, bf16[1024,256]{1,0:T(8,128)(2,1)S(1)}, u32[]{:S(2)}, u32[]{:S(2)}) collective-permute-start(bf16[1024,256]{1,0:T(8,128)(2,1)S(1)} %collective-permute-done.3.refs_4_), channel_id=1, source_target_pairs={{0,16},{1,17},{2,18},{3,19},{4,20},{5,21},{6,22},{7,23},{8,24},{9,... | collective-permute-start | bytes 1572872 | tf_op jit(solution)/shard_map/ppermute | solution.py:56
  37.5 0.8 copy-done.17
  38.5 0.5 collective-permute-start.16
  39.1 0.7 collective-permute-start.4
  39.8 8.6 %collective-permute-done.5.refs_6_ = bf16[1024,256]{1,0:T(8,128)(2,1)S(1)} collective-permute-done((bf16[1024,256]{1,0:T(8,128)(2,1)S(1)}, bf16[1024,256]{1,0:T(8,128)(2,1)S(1)}, u32[]{:S(2)}, u32[]{:S(2)}) %collective-permute-start.5) | collective-permute-done | bytes 524320 | tf_op jit(solution)/shard_map/ppermute | solution.py:56
  48.4 1.5 %collective-permute-start.13 = (bf16[1024,256]{1,0:T(8,128)(2,1)S(1)}, bf16[1024,256]{1,0:T(8,128)(2,1)S(1)}, u32[]{:S(2)}, u32[]{:S(2)}) collective-permute-start(bf16[1024,256]{1,0:T(8,128)(2,1)S(1)} %collective-permute-done.5.refs_6_), channel_id=1, source_target_pairs={{0,16},{1,17},{2,18},{3,19},{4,20},{5,21},{6,22},{7,23},{8,24},{9,... | collective-permute-start | bytes 1572872 | tf_op jit(solution)/shard_map/ppermute | solution.py:56
  50.6 0.5 collective-permute-start.17
  51.1 1.7 %collective-permute-done.4.refs_1_.refs_10_ = bf16[640,256]{1,0:T(8,128)(2,1)S(1)} collective-permute-done((bf16[640,256]{1,0:T(8,128)(2,1)S(1)}, bf16[640,256]{1,0:T(8,128)(2,1)S(1)}, u32[]{:S(2)}, u32[]{:S(2)}) %collective-permute-start.4) | collective-permute-done | bytes 327712 | tf_op jit(solution)/shard_map/ppermute | solution.py:56
  52.8 3.4 %collective-permute-start.6 = (bf16[640,256]{1,0:T(8,128)(2,1)S(1)}, bf16[640,256]{1,0:T(8,128)(2,1)S(1)}, u32[]{:S(2)}, u32[]{:S(2)}) collective-permute-start(bf16[640,256]{1,0:T(8,128)(2,1)S(1)} %collective-permute-done.4.refs_1_.refs_10_), channel_id=1, source_target_pairs={{0,8},{1,9},{2,10},{3,11},{4,0},{5,1},{6,2},{7,3},{8,12},{9,13},{1... | collective-permute-start | bytes 983048 | tf_op jit(solution)/shard_map/ppermute | solution.py:56
  56.2 1.6 %collective-permute-start.10 = (bf16[512,256]{1,0:T(8,128)(2,1)S(1)}, bf16[512,256]{1,0:T(8,128)(2,1)S(1)}, u32[]{:S(2)}, u32[]{:S(2)}) collective-permute-start(bf16[512,256]{1,0:T(8,128)(2,1)S(1)} %slice.127), channel_id=1, source_target_pairs={{0,16},{1,17},{2,18},{3,19},{4,20},{5,21},{6,22},{7,23},{8,24},{9,... | collective-permute-start | bytes 786440 | tf_op jit(solution)/shard_map/ppermute | solution.py:56
  57.8 3.1 %collective-permute-done.6.refs_2_.refs_12_ = bf16[640,256]{1,0:T(8,128)(2,1)S(1)} collective-permute-done((bf16[640,256]{1,0:T(8,128)(2,1)S(1)}, bf16[640,256]{1,0:T(8,128)(2,1)S(1)}, u32[]{:S(2)}, u32[]{:S(2)}) %collective-permute-start.6) | collective-permute-done | bytes 327712 | tf_op jit(solution)/shard_map/ppermute | solution.py:56
  60.9 3.4 %collective-permute-start.7 = (bf16[640,256]{1,0:T(8,128)(2,1)S(1)}, bf16[640,256]{1,0:T(8,128)(2,1)S(1)}, u32[]{:S(2)}, u32[]{:S(2)}) collective-permute-start(bf16[640,256]{1,0:T(8,128)(2,1)S(1)} %collective-permute-done.6.refs_2_.refs_12_), channel_id=1, source_target_pairs={{0,8},{1,9},{2,10},{3,11},{4,0},{5,1},{6,2},{7,3},{8,12},{9,13},{1... | collective-permute-start | bytes 983048 | tf_op jit(solution)/shard_map/ppermute | solution.py:56
  64.4 0.6 collective-permute-start.18
  65.0 1.6 %collective-permute-start.14 = (bf16[512,256]{1,0:T(8,128)(2,1)S(1)}, bf16[512,256]{1,0:T(8,128)(2,1)S(1)}, u32[]{:S(2)}, u32[]{:S(2)}) collective-permute-start(bf16[512,256]{1,0:T(8,128)(2,1)S(1)} %slice.128), channel_id=1, source_target_pairs={{0,16},{1,17},{2,18},{3,19},{4,20},{5,21},{6,22},{7,23},{8,24},{9,... | collective-permute-start | bytes 786440 | tf_op jit(solution)/shard_map/ppermute | solution.py:56
  66.6 2.3 %collective-permute-done.7.refs_3_.refs_14_ = bf16[640,256]{1,0:T(8,128)(2,1)S(1)} collective-permute-done((bf16[640,256]{1,0:T(8,128)(2,1)S(1)}, bf16[640,256]{1,0:T(8,128)(2,1)S(1)}, u32[]{:S(2)}, u32[]{:S(2)}) %collective-permute-start.7) | collective-permute-done | bytes 327712 | tf_op jit(solution)/shard_map/ppermute | solution.py:56
  68.9 0.8 slice.129
  69.7 0.7 copy-done.26
  70.4 1.5 %collective-permute-start.15 = (bf16[512,256]{1,0:T(8,128)(2,1)}, bf16[512,256]{1,0:T(8,128)(2,1)S(1)}, u32[]{:S(2)}, u32[]{:S(2)}) collective-permute-start(bf16[512,256]{1,0:T(8,128)(2,1)} %slice.129), channel_id=1, source_target_pairs={{0,16},{1,17},{2,18},{3,19},{4,20},{5,21},{6,22},{7,23},{8,24},{9,... | collective-permute-start | bytes 786440 | tf_op jit(solution)/shard_map/ppermute | solution.py:56
  71.9 0.7 stack.131.block_ref
  72.5 0.7 stack.130.block_ref
  73.2 7.5 %shard_map.75.refs_9_ = f32[1088,512]{1,0:T(8,128)} custom-call(s32[5]{0:T(128)} %stack.131.block_ref, bf16[512,8192]{1,0:T(8,128)(2,1)} %refs_6_.1, bf16[512,8192]{1,0:T(8,128)(2,1)} %collective-permute-done.11.got_ref.refs_7_, bf16[64,8192]{1,0:T(8,128)(2,1)} %bitcast.43, bf16[1024,256]{1,0:T(8,128)(2,1)} %copy-done.9, bf16[1024,256]{1,0:T(8,128)(2,1)} %copy-done.10, ...), custom_call_target="tpu_custom_call" | custom-call | flops 1 | bytes 1 | tf_op jit(solution)/shard_map/pallas_call | solution.py:226
  80.8 0.8 copy-done.24
  81.6 9.3 %shard_map.76.refs_2_ = bf16[1088,512]{1,0:T(8,128)(2,1)} custom-call(s32[8]{0:T(128)} %stack.130.block_ref, bf16[512,8192]{1,0:T(8,128)(2,1)} %refs_6_.1, bf16[512,8192]{1,0:T(8,128)(2,1)} %collective-permute-done.11.got_ref.refs_7_, bf16[64,8192]{1,0:T(8,128)(2,1)} %bitcast.44, bf16[1088,256]{1,0:T(8,128)(2,1)} %copy-done.11, ...), custom_call_target="tpu_custom_call" | custom-call | flops 1 | bytes 1 | tf_op jit(solution)/shard_map/pallas_call | solution.py:226
  91.5 0.5 collective-permute-start.8
  92.1 0.7 pad_add_fusion.1.block_ref
  92.8 0.6 and_select_fusion.1
  93.4 0.8 collective-permute-done.8.refs_1_
  94.1 0.7 copy-done.29
  94.8 11.9 %shard_map.77 = (bf16[4,2,144,128]{3,2,1,0:T(8,128)(2,1)}, bf16[4,2,144,128]{3,2,1,0:T(8,128)(2,1)}, f32[64,512]{1,0:T(8,128)}) custom-call(s32[4]{0:T(128)} %get-tuple-element.79.place_ref, s32[4]{0:T(128)} %get-tuple-element.80.turn_ref, s32[3]{0:T(128)} %pad_add_fusion.1.block_ref, bf16[4,128,256]{2,1,0:T(8,128)(2,1)} %copy-done.6, ...), custom_call_target="tpu_custom_call" | custom-call | flops 1 | bytes 1 | tf_op jit(solution)/shard_map/pallas_call | solution.py:418
  107.0 0.8 slice.136
  108.2 0.8 slice.137
  109.1 1.0 copy-done.8
  110.1 0.6 collective-permute-start.21
  110.9 5.2 %collective-permute-done.21.far_ref = bf16[4,144,128]{2,1,0:T(8,128)(2,1)S(1)} collective-permute-done((bf16[4,144,128]{2,1,0:T(8,128)(2,1)S(1)}, bf16[4,144,128]{2,1,0:T(8,128)(2,1)S(1)}, u32[]{:S(2)}, u32[]{:S(2)}) %collective-permute-start.21) | collective-permute-done | bytes 147488 | tf_op jit(solution)/shard_map/ppermute | solution.py:56
  116.2 2.4 %collective-permute-start.22 = (bf16[144,128]{1,0:T(8,128)(2,1)S(1)}, bf16[144,128]{1,0:T(8,128)(2,1)S(1)}, u32[]{:S(2)}, u32[]{:S(2)}) collective-permute-start(bf16[144,128]{1,0:T(8,128)(2,1)S(1)} %get-tuple-element.55), channel_id=1, source_target_pairs={{0,4},{1,5},{2,6},{3,7},{4,0},{5,1},{6,2},{7,3},{8,12},{9,13},{10,... | collective-permute-start | bytes 110600 | tf_op jit(solution)/shard_map/ppermute | solution.py:56
  118.6 1.1 collective-permute-start.23
  119.7 1.4 collective-permute-start.24
  121.1 0.8 fusion.refs_6_
  121.9 2.3 %collective-permute-done.23.refs_2_ = bf16[144,128]{1,0:T(8,128)(2,1)S(1)} collective-permute-done((bf16[144,128]{1,0:T(8,128)(2,1)S(1)}, bf16[144,128]{1,0:T(8,128)(2,1)S(1)}, u32[]{:S(2)}, u32[]{:S(2)}) %collective-permute-start.23) | collective-permute-done | bytes 36896 | tf_op jit(solution)/shard_map/ppermute | solution.py:56
  124.2 1.3 collective-permute-done.24.refs_3_
  125.5 1.7 %shard_map.80 = bf16[64,8192]{1,0:T(8,128)(2,1)S(1)} custom-call(s32[16]{0:T(128)S(1)} %stack.115.block_ref, bf16[144,128]{1,0:T(8,128)(2,1)S(1)} %get-tuple-element.54.refs_0_, bf16[144,128]{1,0:T(8,128)(2,1)S(1)} %collective-permute-done.22.refs_1_, bf16[144,128]{1,0:T(8,128)(2,1)S(1)} %collective-permute-done.23.refs_2_, ...), custom_call_target="tpu_custom_call" | custom-call | flops 1 | bytes 1 | tf_op jit(solution)/shard_map/pallas_call | solution.py:265
  127.3 1.9 %collective-permute-done.26 = bf16[64,4096]{1,0:T(8,128)(2,1)S(1)} collective-permute-done((bf16[64,4096]{1,0:T(8,128)(2,1)S(1)}, bf16[64,4096]{1,0:T(8,128)(2,1)S(1)}, u32[]{:S(2)}, u32[]{:S(2)}) %collective-permute-start.26) | collective-permute-done | bytes 524320 | tf_op jit(solution)/shard_map/ppermute | solution.py:56
  129.4 0.6 collective-permute-start.27
  129.9 7.8 %collective-permute-done.27 = bf16[64,2048]{1,0:T(8,128)(2,1)S(1)} collective-permute-done((bf16[64,2048]{1,0:T(8,128)(2,1)S(1)}, bf16[64,2048]{1,0:T(8,128)(2,1)S(1)}, u32[]{:S(2)}, u32[]{:S(2)}) %collective-permute-start.27) | collective-permute-done | bytes 262176 | tf_op jit(solution)/shard_map/ppermute | solution.py:56
  137.9 1.4 collective-permute-start.30
  139.5 2.8 %collective-permute-start.28 = (bf16[64,512]{1,0:T(8,128)(2,1)S(1)}, bf16[64,512]{1,0:T(8,128)(2,1)S(1)}, u32[]{:S(2)}, u32[]{:S(2)}) collective-permute-start(bf16[64,512]{1,0:T(8,128)(2,1)S(1)} %get-tuple-element.67), channel_id=1, source_target_pairs={{0,4},{1,5},{2,6},{3,7},{4,0},{5,1},{6,2},{7,3},{8,12},{9,13},{10,... | collective-permute-start | bytes 196616 | tf_op jit(solution)/shard_map/ppermute | solution.py:56
  142.3 2.2 %collective-permute-done.30 = bf16[64,512]{1,0:T(8,128)(2,1)S(1)} collective-permute-done((bf16[64,512]{1,0:T(8,128)(2,1)S(1)}, bf16[64,512]{1,0:T(8,128)(2,1)S(1)}, u32[]{:S(2)}, u32[]{:S(2)}) %collective-permute-start.30) | collective-permute-done | bytes 65568 | tf_op jit(solution)/shard_map/ppermute | solution.py:56
  144.6 1.4 collective-permute-done.29
  146.0 0.7 add_convert_fusion.2
  (119 shorter events, 4.6 us)
Async XLA Ops:
  0.0 4.1 %copy-start.25 = (bf16[512,512]{1,0:T(8,128)(2,1)S(1)}, bf16[512,512]{1,0:T(8,128)(2,1)}, u32[]{:S(2)}) copy-start(bf16[512,512]{1,0:T(8,128)(2,1)} %param.11) | copy-start | bytes 1572868
  0.0 73.2 %collective-permute-start.11 = (bf16[512,8192]{1,0:T(8,128)(2,1)}, bf16[512,8192]{1,0:T(8,128)(2,1)}, u32[]{:S(2)}, u32[]{:S(2)}) collective-permute-start(bf16[512,8192]{1,0:T(8,128)(2,1)} %refs_6_.1), channel_id=1, source_target_pairs={{0,1},{1,0},{2,3},{3,2},{4,5},{5,4},{6,7},{7,6},{8,9},{9,8},{10,11... | collective-permute-start | bytes 25165832 | tf_op jit(solution)/shard_map/ppermute | solution.py:56
  0.5 23.0 %collective-permute-start = (bf16[512,512]{1,0:T(8,128)(2,1)}, bf16[512,512]{1,0:T(8,128)(2,1)}, u32[]{:S(2)}, u32[]{:S(2)}) collective-permute-start(bf16[512,512]{1,0:T(8,128)(2,1)} %param.12), channel_id=1, source_target_pairs={{0,2},{1,3},{2,0},{3,1},{4,6},{5,7},{6,4},{7,5},{8,10},{9,11},{10,... | collective-permute-start | bytes 1572872 | tf_op jit(solution)/shard_map/ppermute | solution.py:56
  4.2 3.0 %copy-start.30 = (s32[64]{0:T(128)S(1)}, s32[64]{0:T(128)}, u32[]{:S(2)}) copy-start(s32[64]{0:T(128)} %param.9) | copy-start | bytes 772
  4.4 12.2 %copy-start.9 = (bf16[1024,256]{1,0:T(8,128)(2,1)}, bf16[1024,256]{1,0:T(8,128)(2,1)S(1)}, u32[]{:S(2)}) copy-start(bf16[1024,256]{1,0:T(8,128)(2,1)S(1)} %get-tuple-element.59.refs_0_) | copy-start | bytes 1572868
  4.4 12.3 %copy-start.10 = (bf16[1024,256]{1,0:T(8,128)(2,1)}, bf16[1024,256]{1,0:T(8,128)(2,1)S(1)}, u32[]{:S(2)}) copy-start(bf16[1024,256]{1,0:T(8,128)(2,1)S(1)} %get-tuple-element.60.refs_1_) | copy-start | bytes 1572868
  4.4 14.2 %collective-permute-start.2 = (bf16[1024,256]{1,0:T(8,128)(2,1)S(1)}, bf16[1024,256]{1,0:T(8,128)(2,1)S(1)}, u32[]{:S(2)}, u32[]{:S(2)}) collective-permute-start(bf16[1024,256]{1,0:T(8,128)(2,1)S(1)} %get-tuple-element.59.refs_0_), channel_id=1, source_target_pairs={{0,8},{1,9},{2,10},{3,11},{4,0},{5,1},{6,2},{7,3},{8,12},{9,13},{1... | collective-permute-start | bytes 1572872 | tf_op jit(solution)/shard_map/ppermute | solution.py:56
  17.5 20.9 %copy-start.11 = (bf16[1088,256]{1,0:T(8,128)(2,1)}, bf16[1088,256]{1,0:T(8,128)(2,1)S(1)}, u32[]{:S(2)}) copy-start(bf16[1088,256]{1,0:T(8,128)(2,1)S(1)} %pad_maximum_fusion.refs_0_) | copy-start | bytes 1671172
  18.5 19.8 %copy-start.15 = (bf16[1024,256]{1,0:T(8,128)(2,1)}, bf16[1024,256]{1,0:T(8,128)(2,1)S(1)}, u32[]{:S(2)}) copy-start(bf16[1024,256]{1,0:T(8,128)(2,1)S(1)} %collective-permute-done.2.refs_2_) | copy-start | bytes 1572868
  18.5 14.1 %collective-permute-start.3 = (bf16[1024,256]{1,0:T(8,128)(2,1)S(1)}, bf16[1024,256]{1,0:T(8,128)(2,1)S(1)}, u32[]{:S(2)}, u32[]{:S(2)}) collective-permute-start(bf16[1024,256]{1,0:T(8,128)(2,1)S(1)} %collective-permute-done.2.refs_2_), channel_id=1, source_target_pairs={{0,8},{1,9},{2,10},{3,11},{4,0},{5,1},{6,2},{7,3},{8,12},{9,13},{1... | collective-permute-start | bytes 1572872 | tf_op jit(solution)/shard_map/ppermute | solution.py:56
  21.9 15.6 %collective-permute-start.12 = (bf16[1024,256]{1,0:T(8,128)(2,1)S(1)}, bf16[1024,256]{1,0:T(8,128)(2,1)S(1)}, u32[]{:S(2)}, u32[]{:S(2)}) collective-permute-start(bf16[1024,256]{1,0:T(8,128)(2,1)S(1)} %collective-permute-done.2.refs_2_), channel_id=1, source_target_pairs={{0,16},{1,17},{2,18},{3,19},{4,20},{5,21},{6,22},{7,23},{8,24},{9,... | collective-permute-start | bytes 1572872 | tf_op jit(solution)/shard_map/ppermute | solution.py:56
  25.2 13.8 %copy-start.7 = (bf16[64,256]{1,0:T(8,128)(2,1)S(1)}, bf16[64,256]{1,0:T(8,128)(2,1)}, u32[]{:S(2)}) copy-start(bf16[64,256]{1,0:T(8,128)(2,1)} %shard_map.73.refs_4_) | copy-start | bytes 98308
  25.2 13.3 %collective-permute-start.1 = (bf16[1088,256]{1,0:T(8,128)(2,1)S(1)}, bf16[1088,256]{1,0:T(8,128)(2,1)S(1)}, u32[]{:S(2)}, u32[]{:S(2)}) collective-permute-start(bf16[1088,256]{1,0:T(8,128)(2,1)S(1)} %pad_maximum_fusion.refs_0_), channel_id=1, source_target_pairs={{0,2},{1,3},{2,0},{3,1},{4,6},{5,7},{6,4},{7,5},{8,10},{9,11},{10,... | collective-permute-start | bytes 1671176 | tf_op jit(solution)/shard_map/ppermute | solution.py:56
  32.6 7.2 %copy-start.16 = (bf16[1024,256]{1,0:T(8,128)(2,1)}, bf16[1024,256]{1,0:T(8,128)(2,1)S(1)}, u32[]{:S(2)}) copy-start(bf16[1024,256]{1,0:T(8,128)(2,1)S(1)} %collective-permute-done.3.refs_4_) | copy-start | bytes 1572868
  32.6 15.8 %collective-permute-start.5 = (bf16[1024,256]{1,0:T(8,128)(2,1)S(1)}, bf16[1024,256]{1,0:T(8,128)(2,1)S(1)}, u32[]{:S(2)}, u32[]{:S(2)}) collective-permute-start(bf16[1024,256]{1,0:T(8,128)(2,1)S(1)} %collective-permute-done.3.refs_4_), channel_id=1, source_target_pairs={{0,8},{1,9},{2,10},{3,11},{4,0},{5,1},{6,2},{7,3},{8,12},{9,13},{1... | collective-permute-start | bytes 1572872 | tf_op jit(solution)/shard_map/ppermute | solution.py:56
  36.0 14.0 %collective-permute-start.9 = (bf16[1024,256]{1,0:T(8,128)(2,1)S(1)}, bf16[1024,256]{1,0:T(8,128)(2,1)S(1)}, u32[]{:S(2)}, u32[]{:S(2)}) collective-permute-start(bf16[1024,256]{1,0:T(8,128)(2,1)S(1)} %collective-permute-done.3.refs_4_), channel_id=1, source_target_pairs={{0,16},{1,17},{2,18},{3,19},{4,20},{5,21},{6,22},{7,23},{8,24},{9,... | collective-permute-start | bytes 1572872 | tf_op jit(solution)/shard_map/ppermute | solution.py:56
  37.5 0.8 copy-start.17
  38.4 11.7 %copy-start.12 = (bf16[1024,256]{1,0:T(8,128)(2,1)}, bf16[1024,256]{1,0:T(8,128)(2,1)S(1)}, u32[]{:S(2)}) copy-start(bf16[1024,256]{1,0:T(8,128)(2,1)S(1)} %pad_maximum_fusion.3.refs_2_) | copy-start | bytes 1572868
  38.5 11.6 %copy-start.21 = (bf16[1088,256]{1,0:T(8,128)(2,1)}, bf16[1088,256]{1,0:T(8,128)(2,1)S(1)}, u32[]{:S(2)}) copy-start(bf16[1088,256]{1,0:T(8,128)(2,1)S(1)} %collective-permute-done.1.refs_1_) | copy-start | bytes 1671172
  38.5 12.1 %collective-permute-start.16 = (bf16[1024,256]{1,0:T(8,128)(2,1)S(1)}, bf16[1024,256]{1,0:T(8,128)(2,1)S(1)}, u32[]{:S(2)}, u32[]{:S(2)}) collective-permute-start(bf16[1024,256]{1,0:T(8,128)(2,1)S(1)} %pad_maximum_fusion.3.refs_2_), channel_id=1, source_target_pairs={{0,2},{1,3},{2,0},{3,1},{4,6},{5,7},{6,4},{7,5},{8,10},{9,11},{10,... | collective-permute-start | bytes 1572872 | tf_op jit(solution)/shard_map/ppermute | solution.py:56
  39.0 17.1 %copy-start.1 = (bf16[640,256]{1,0:T(8,128)(2,1)}, bf16[640,256]{1,0:T(8,128)(2,1)S(1)}, u32[]{:S(2)}) copy-start(bf16[640,256]{1,0:T(8,128)(2,1)S(1)} %pad_maximum_fusion.6.refs_0_.refs_8_) | copy-start | bytes 983044
  39.1 13.7 %collective-permute-start.4 = (bf16[640,256]{1,0:T(8,128)(2,1)S(1)}, bf16[640,256]{1,0:T(8,128)(2,1)S(1)}, u32[]{:S(2)}, u32[]{:S(2)}) collective-permute-start(bf16[640,256]{1,0:T(8,128)(2,1)S(1)} %pad_maximum_fusion.6.refs_0_.refs_8_), channel_id=1, source_target_pairs={{0,8},{1,9},{2,10},{3,11},{4,0},{5,1},{6,2},{7,3},{8,12},{9,13},{1... | collective-permute-start | bytes 983048 | tf_op jit(solution)/shard_map/ppermute | solution.py:56
  48.4 9.4 %copy-start.18 = (bf16[1024,256]{1,0:T(8,128)(2,1)}, bf16[1024,256]{1,0:T(8,128)(2,1)S(1)}, u32[]{:S(2)}) copy-start(bf16[1024,256]{1,0:T(8,128)(2,1)S(1)} %collective-permute-done.5.refs_6_) | copy-start | bytes 1572868
  48.4 15.9 %collective-permute-start.13 = (bf16[1024,256]{1,0:T(8,128)(2,1)S(1)}, bf16[1024,256]{1,0:T(8,128)(2,1)S(1)}, u32[]{:S(2)}, u32[]{:S(2)}) collective-permute-start(bf16[1024,256]{1,0:T(8,128)(2,1)S(1)} %collective-permute-done.5.refs_6_), channel_id=1, source_target_pairs={{0,16},{1,17},{2,18},{3,19},{4,20},{5,21},{6,22},{7,23},{8,24},{9,... | collective-permute-start | bytes 1572872 | tf_op jit(solution)/shard_map/ppermute | solution.py:56
  50.0 7.8 %copy-start.19 = (bf16[1024,256]{1,0:T(8,128)(2,1)}, bf16[1024,256]{1,0:T(8,128)(2,1)S(1)}, u32[]{:S(2)}) copy-start(bf16[1024,256]{1,0:T(8,128)(2,1)S(1)} %collective-permute-done.9.refs_5_) | copy-start | bytes 1572868
  50.1 14.3 %copy-start.13 = (bf16[1024,256]{1,0:T(8,128)(2,1)}, bf16[1024,256]{1,0:T(8,128)(2,1)S(1)}, u32[]{:S(2)}) copy-start(bf16[1024,256]{1,0:T(8,128)(2,1)S(1)} %pad_maximum_fusion.4.refs_4_) | copy-start | bytes 1572868
  50.6 13.8 %copy-start.22 = (bf16[1024,256]{1,0:T(8,128)(2,1)}, bf16[1024,256]{1,0:T(8,128)(2,1)S(1)}, u32[]{:S(2)}) copy-start(bf16[1024,256]{1,0:T(8,128)(2,1)S(1)} %collective-permute-done.16.refs_3_) | copy-start | bytes 1572868
  50.6 13.8 %collective-permute-start.17 = (bf16[1024,256]{1,0:T(8,128)(2,1)S(1)}, bf16[1024,256]{1,0:T(8,128)(2,1)S(1)}, u32[]{:S(2)}, u32[]{:S(2)}) collective-permute-start(bf16[1024,256]{1,0:T(8,128)(2,1)S(1)} %pad_maximum_fusion.4.refs_4_), channel_id=1, source_target_pairs={{0,2},{1,3},{2,0},{3,1},{4,6},{5,7},{6,4},{7,5},{8,10},{9,11},{10,... | collective-permute-start | bytes 1572872 | tf_op jit(solution)/shard_map/ppermute | solution.py:56
  52.8 38.2 %copy-start.3 = (bf16[640,256]{1,0:T(8,128)(2,1)}, bf16[640,256]{1,0:T(8,128)(2,1)S(1)}, u32[]{:S(2)}) copy-start(bf16[640,256]{1,0:T(8,128)(2,1)S(1)} %collective-permute-done.4.refs_1_.refs_10_) | copy-start | bytes 983044
  52.8 8.1 %collective-permute-start.6 = (bf16[640,256]{1,0:T(8,128)(2,1)S(1)}, bf16[640,256]{1,0:T(8,128)(2,1)S(1)}, u32[]{:S(2)}, u32[]{:S(2)}) collective-permute-start(bf16[640,256]{1,0:T(8,128)(2,1)S(1)} %collective-permute-done.4.refs_1_.refs_10_), channel_id=1, source_target_pairs={{0,8},{1,9},{2,10},{3,11},{4,0},{5,1},{6,2},{7,3},{8,12},{9,13},{1... | collective-permute-start | bytes 983048 | tf_op jit(solution)/shard_map/ppermute | solution.py:56
  56.2 13.5 %collective-permute-start.10 = (bf16[512,256]{1,0:T(8,128)(2,1)S(1)}, bf16[512,256]{1,0:T(8,128)(2,1)S(1)}, u32[]{:S(2)}, u32[]{:S(2)}) collective-permute-start(bf16[512,256]{1,0:T(8,128)(2,1)S(1)} %slice.127), channel_id=1, source_target_pairs={{0,16},{1,17},{2,18},{3,19},{4,20},{5,21},{6,22},{7,23},{8,24},{9,... | collective-permute-start | bytes 786440 | tf_op jit(solution)/shard_map/ppermute | solution.py:56
  60.9 30.1 %copy-start.4 = (bf16[640,256]{1,0:T(8,128)(2,1)}, bf16[640,256]{1,0:T(8,128)(2,1)S(1)}, u32[]{:S(2)}) copy-start(bf16[640,256]{1,0:T(8,128)(2,1)S(1)} %collective-permute-done.6.refs_2_.refs_12_) | copy-start | bytes 983044
  60.9 8.0 %collective-permute-start.7 = (bf16[640,256]{1,0:T(8,128)(2,1)S(1)}, bf16[640,256]{1,0:T(8,128)(2,1)S(1)}, u32[]{:S(2)}, u32[]{:S(2)}) collective-permute-start(bf16[640,256]{1,0:T(8,128)(2,1)S(1)} %collective-permute-done.6.refs_2_.refs_12_), channel_id=1, source_target_pairs={{0,8},{1,9},{2,10},{3,11},{4,0},{5,1},{6,2},{7,3},{8,12},{9,13},{1... | collective-permute-start | bytes 983048 | tf_op jit(solution)/shard_map/ppermute | solution.py:56
  64.3 5.3 %copy-start.20 = (bf16[1024,256]{1,0:T(8,128)(2,1)}, bf16[1024,256]{1,0:T(8,128)(2,1)S(1)}, u32[]{:S(2)}) copy-start(bf16[1024,256]{1,0:T(8,128)(2,1)S(1)} %collective-permute-done.13.refs_7_) | copy-start | bytes 1572868
  64.4 16.3 %copy-start.14 = (bf16[1024,256]{1,0:T(8,128)(2,1)}, bf16[1024,256]{1,0:T(8,128)(2,1)S(1)}, u32[]{:S(2)}) copy-start(bf16[1024,256]{1,0:T(8,128)(2,1)S(1)} %pad_maximum_fusion.5.refs_6_) | copy-start | bytes 1572868
  64.4 5.2 %copy-start.23 = (bf16[1024,256]{1,0:T(8,128)(2,1)}, bf16[1024,256]{1,0:T(8,128)(2,1)S(1)}, u32[]{:S(2)}) copy-start(bf16[1024,256]{1,0:T(8,128)(2,1)S(1)} %collective-permute-done.17.refs_5_) | copy-start | bytes 1572868
  64.4 16.4 %collective-permute-start.18 = (bf16[1024,256]{1,0:T(8,128)(2,1)S(1)}, bf16[1024,256]{1,0:T(8,128)(2,1)S(1)}, u32[]{:S(2)}, u32[]{:S(2)}) collective-permute-start(bf16[1024,256]{1,0:T(8,128)(2,1)S(1)} %pad_maximum_fusion.5.refs_6_), channel_id=1, source_target_pairs={{0,2},{1,3},{2,0},{3,1},{4,6},{5,7},{6,4},{7,5},{8,10},{9,11},{10,... | collective-permute-start | bytes 1572872 | tf_op jit(solution)/shard_map/ppermute | solution.py:56
  65.0 15.7 %collective-permute-start.14 = (bf16[512,256]{1,0:T(8,128)(2,1)S(1)}, bf16[512,256]{1,0:T(8,128)(2,1)S(1)}, u32[]{:S(2)}, u32[]{:S(2)}) collective-permute-start(bf16[512,256]{1,0:T(8,128)(2,1)S(1)} %slice.128), channel_id=1, source_target_pairs={{0,16},{1,17},{2,18},{3,19},{4,20},{5,21},{6,22},{7,23},{8,24},{9,... | collective-permute-start | bytes 786440 | tf_op jit(solution)/shard_map/ppermute | solution.py:56
  68.9 22.2 %copy-start.5 = (bf16[640,256]{1,0:T(8,128)(2,1)}, bf16[640,256]{1,0:T(8,128)(2,1)S(1)}, u32[]{:S(2)}) copy-start(bf16[640,256]{1,0:T(8,128)(2,1)S(1)} %collective-permute-done.7.refs_3_.refs_14_) | copy-start | bytes 983044
  69.6 0.7 copy-start.26
  70.4 10.4 %collective-permute-start.15 = (bf16[512,256]{1,0:T(8,128)(2,1)}, bf16[512,256]{1,0:T(8,128)(2,1)S(1)}, u32[]{:S(2)}, u32[]{:S(2)}) collective-permute-start(bf16[512,256]{1,0:T(8,128)(2,1)} %slice.129), channel_id=1, source_target_pairs={{0,16},{1,17},{2,18},{3,19},{4,20},{5,21},{6,22},{7,23},{8,24},{9,... | collective-permute-start | bytes 786440 | tf_op jit(solution)/shard_map/ppermute | solution.py:56
  80.7 10.3 %copy-start.2 = (bf16[640,256]{1,0:T(8,128)(2,1)S(1)}, bf16[640,256]{1,0:T(8,128)(2,1)}, u32[]{:S(2)}) copy-start(bf16[640,256]{1,0:T(8,128)(2,1)} %copy-done.1) | copy-start | bytes 983044
  80.7 10.2 %copy-start.27 = (bf16[512,256]{1,0:T(8,128)(2,1)}, bf16[512,256]{1,0:T(8,128)(2,1)S(1)}, u32[]{:S(2)}) copy-start(bf16[512,256]{1,0:T(8,128)(2,1)S(1)} %collective-permute-done.14.refs_13_) | copy-start | bytes 786436
  80.8 10.2 %copy-start.28 = (bf16[512,256]{1,0:T(8,128)(2,1)}, bf16[512,256]{1,0:T(8,128)(2,1)S(1)}, u32[]{:S(2)}) copy-start(bf16[512,256]{1,0:T(8,128)(2,1)S(1)} %collective-permute-done.15.refs_15_) | copy-start | bytes 786436
  80.8 0.8 copy-start.24
  90.9 3.2 %collective-permute-start.19 = (bf16[1088,512]{1,0:T(8,128)(2,1)}, bf16[1088,512]{1,0:T(8,128)(2,1)}, u32[]{:S(2)}, u32[]{:S(2)}) collective-permute-start(bf16[1088,512]{1,0:T(8,128)(2,1)} %shard_map.76.refs_2_), channel_id=1, source_target_pairs={{0,1},{1,0},{2,3},{3,2},{4,5},{5,4},{6,7},{7,6},{8,9},{9,8},{10,11... | collective-permute-start | bytes 3342344 | tf_op jit(solution)/shard_map/ppermute | solution.py:56
  91.5 2.7 %copy-start.6 = (bf16[4,128,256]{2,1,0:T(8,128)(2,1)}, bf16[4,128,256]{2,1,0:T(8,128)(2,1)S(1)}, u32[]{:S(2)}) copy-start(bf16[4,128,256]{2,1,0:T(8,128)(2,1)S(1)} %shard_map.74.refs_0_) | copy-start | bytes 786436
  91.5 2.7 %collective-permute-start.8 = (bf16[4,128,256]{2,1,0:T(8,128)(2,1)S(1)}, bf16[4,128,256]{2,1,0:T(8,128)(2,1)S(1)}, u32[]{:S(2)}, u32[]{:S(2)}) collective-permute-start(bf16[4,128,256]{2,1,0:T(8,128)(2,1)S(1)} %shard_map.74.refs_0_), channel_id=1, source_target_pairs={{0,1},{1,0},{2,3},{3,2},{4,5},{5,4},{6,7},{7,6},{8,9},{9,8},{10,11... | collective-permute-start | bytes 786440 | tf_op jit(solution)/shard_map/ppermute | solution.py:56
  94.1 0.7 copy-start.29
  94.8 30.6 %copy-start = (bf16[256,8192]{1,0:T(8,128)(2,1)S(1)}, bf16[256,8192]{1,0:T(8,128)(2,1)}, u32[]{:S(2)}) copy-start(bf16[256,8192]{1,0:T(8,128)(2,1)} %refs_7_.1) | copy-start | bytes 12582916
  106.7 2.4 %collective-permute-start.20 = (bf16[4,2,144,128]{3,2,1,0:T(8,128)(2,1)}, bf16[4,2,144,128]{3,2,1,0:T(8,128)(2,1)S(1)}, u32[]{:S(2)}, u32[]{:S(2)}) collective-permute-start(bf16[4,2,144,128]{3,2,1,0:T(8,128)(2,1)} %get-tuple-element.51), channel_id=1, source_target_pairs={{0,1},{1,0},{2,3},{3,2},{4,5},{5,4},{6,7},{7,6},{8,9},{9,8},{10,11... | collective-permute-start | bytes 884744 | tf_op jit(solution)/shard_map/ppermute | solution.py:56
  107.9 13.2 %collective-permute-start.25 = (f32[64,512]{1,0:T(8,128)}, f32[64,512]{1,0:T(8,128)S(1)}, u32[]{:S(2)}, u32[]{:S(2)}) collective-permute-start(f32[64,512]{1,0:T(8,128)} %get-tuple-element.58), channel_id=1, source_target_pairs={{0,1},{1,0},{2,3},{3,2},{4,5},{5,4},{6,7},{7,6},{8,9},{9,8},{10,11... | collective-permute-start | bytes 393224 | tf_op jit(solution)/shard_map/ppermute | solution.py:56
  109.1 1.0 copy-start.8
  110.1 6.0 %collective-permute-start.21 = (bf16[4,144,128]{2,1,0:T(8,128)(2,1)S(1)}, bf16[4,144,128]{2,1,0:T(8,128)(2,1)S(1)}, u32[]{:S(2)}, u32[]{:S(2)}) collective-permute-start(bf16[4,144,128]{2,1,0:T(8,128)(2,1)S(1)} %get-tuple-element.53), channel_id=1, source_target_pairs={{0,2},{1,3},{2,0},{3,1},{4,6},{5,7},{6,4},{7,5},{8,10},{9,11},{10,... | collective-permute-start | bytes 442376 | tf_op jit(solution)/shard_map/ppermute | solution.py:56
  116.2 5.7 %collective-permute-start.22 = (bf16[144,128]{1,0:T(8,128)(2,1)S(1)}, bf16[144,128]{1,0:T(8,128)(2,1)S(1)}, u32[]{:S(2)}, u32[]{:S(2)}) collective-permute-start(bf16[144,128]{1,0:T(8,128)(2,1)S(1)} %get-tuple-element.55), channel_id=1, source_target_pairs={{0,4},{1,5},{2,6},{3,7},{4,0},{5,1},{6,2},{7,3},{8,12},{9,13},{10,... | collective-permute-start | bytes 110600 | tf_op jit(solution)/shard_map/ppermute | solution.py:56
  118.6 5.6 %collective-permute-start.23 = (bf16[144,128]{1,0:T(8,128)(2,1)S(1)}, bf16[144,128]{1,0:T(8,128)(2,1)S(1)}, u32[]{:S(2)}, u32[]{:S(2)}) collective-permute-start(bf16[144,128]{1,0:T(8,128)(2,1)S(1)} %get-tuple-element.56), channel_id=1, source_target_pairs={{0,8},{1,9},{2,10},{3,11},{4,12},{5,13},{6,14},{7,15},{8,0},{9,1},... | collective-permute-start | bytes 110600 | tf_op jit(solution)/shard_map/ppermute | solution.py:56
  119.7 5.8 %collective-permute-start.24 = (bf16[144,128]{1,0:T(8,128)(2,1)S(1)}, bf16[144,128]{1,0:T(8,128)(2,1)S(1)}, u32[]{:S(2)}, u32[]{:S(2)}) collective-permute-start(bf16[144,128]{1,0:T(8,128)(2,1)S(1)} %get-tuple-element.57), channel_id=1, source_target_pairs={{0,12},{1,13},{2,14},{3,15},{4,8},{5,9},{6,10},{7,11},{8,4},{9,5},... | collective-permute-start | bytes 110600 | tf_op jit(solution)/shard_map/ppermute | solution.py:56
  127.2 2.0 %collective-permute-start.26 = (bf16[64,4096]{1,0:T(8,128)(2,1)S(1)}, bf16[64,4096]{1,0:T(8,128)(2,1)S(1)}, u32[]{:S(2)}, u32[]{:S(2)}) collective-permute-start(bf16[64,4096]{1,0:T(8,128)(2,1)S(1)} %slice.141), channel_id=1, source_target_pairs={{0,1},{1,0},{2,3},{3,2},{4,5},{5,4},{6,7},{7,6},{8,9},{9,8},{10,11... | collective-permute-start | bytes 1572872 | tf_op jit(solution)/shard_map/ppermute | solution.py:56
  129.4 8.4 %collective-permute-start.27 = (bf16[64,2048]{1,0:T(8,128)(2,1)S(1)}, bf16[64,2048]{1,0:T(8,128)(2,1)S(1)}, u32[]{:S(2)}, u32[]{:S(2)}) collective-permute-start(bf16[64,2048]{1,0:T(8,128)(2,1)S(1)} %slice.143), channel_id=1, source_target_pairs={{0,2},{1,3},{2,0},{3,1},{4,6},{5,7},{6,4},{7,5},{8,10},{9,11},{10,... | collective-permute-start | bytes 786440 | tf_op jit(solution)/shard_map/ppermute | solution.py:56
  137.9 6.7 %collective-permute-start.30 = (bf16[64,512]{1,0:T(8,128)(2,1)S(1)}, bf16[64,512]{1,0:T(8,128)(2,1)S(1)}, u32[]{:S(2)}, u32[]{:S(2)}) collective-permute-start(bf16[64,512]{1,0:T(8,128)(2,1)S(1)} %get-tuple-element.68), channel_id=1, source_target_pairs={{0,12},{1,13},{2,14},{3,15},{4,8},{5,9},{6,10},{7,11},{8,4},{9,5},... | collective-permute-start | bytes 196616 | tf_op jit(solution)/shard_map/ppermute | solution.py:56
  139.3 6.7 %collective-permute-start.29 = (bf16[64,512]{1,0:T(8,128)(2,1)S(1)}, bf16[64,512]{1,0:T(8,128)(2,1)S(1)}, u32[]{:S(2)}, u32[]{:S(2)}) collective-permute-start(bf16[64,512]{1,0:T(8,128)(2,1)S(1)} %get-tuple-element.69), channel_id=1, source_target_pairs={{0,8},{1,9},{2,10},{3,11},{4,12},{5,13},{6,14},{7,15},{8,0},{9,1},... | collective-permute-start | bytes 196616 | tf_op jit(solution)/shard_map/ppermute | solution.py:56
  139.5 6.5 %collective-permute-start.28 = (bf16[64,512]{1,0:T(8,128)(2,1)S(1)}, bf16[64,512]{1,0:T(8,128)(2,1)S(1)}, u32[]{:S(2)}, u32[]{:S(2)}) collective-permute-start(bf16[64,512]{1,0:T(8,128)(2,1)S(1)} %get-tuple-element.67), channel_id=1, source_target_pairs={{0,4},{1,5},{2,6},{3,7},{4,0},{5,1},{6,2},{7,3},{8,12},{9,13},{10,... | collective-permute-start | bytes 196616 | tf_op jit(solution)/shard_map/ppermute | solution.py:56

commit v16 on v15

--- a/solution.py
+++ b/solution.py
@@ -327,8 +327,9 @@
         query_refs = refs[:2]
         own_ref, other_ref, cosine_ref, sine_ref = refs[2:6]
         mask_refs = refs[6 : len(inputs)]
-        prompt_ref, got_ref, step_ref, early_ref = refs[len(inputs) : len(inputs) + 4]
-        rest = refs[len(inputs) + 4 :]
+        prompt_ref, got_ref, step_ref = refs[len(inputs) : len(inputs) + 3]
+        early_refs = refs[len(inputs) + 3 : len(inputs) + 3 + len(early)]
+        rest = refs[len(inputs) + 3 + len(early) :]
         weight_refs, rest = rest[: len(held.arrays)], rest[len(held.arrays) :]
         *out_refs, step_out_ref = rest[:3]
         early_held, weight_held, value_held, early_sem, *scratch = rest[3:]
@@ -337,8 +338,12 @@
         groups = [
             held.copies(i, block_ref, sources, weight_refs, scratch) for i in range(held.count)
         ]
-        before = pltpu.make_async_copy(early_ref, early_held, early_sem.at[0])
-        before.start()
+        before = [
+            pltpu.make_async_copy(ref, early_held.at[i], early_sem.at[i])
+            for i, ref in enumerate(early_refs)
+        ]
+        for copy in before:
+            copy.start()
         for group in groups:
             for copy in group:
                 copy.start()
@@ -388,8 +393,9 @@
             return 0
 
         lax.fori_loop(0, kv_heads, one_head, 0)
-        before.wait()
-        total = early_held[...]
+        for copy in before:
+            copy.wait()
+        total = sum(early_held[i] for i in range(len(early)))
         for i, group in enumerate(groups):
             for copy in group:
                 copy.wait()
@@ -419,7 +425,7 @@
         body,
         in_specs=[pl.BlockSpec(memory_space=pltpu.SMEM)] * 3
         + [whole] * len(inputs)
-        + [anywhere] * (4 + len(held.arrays)),
+        + [anywhere] * (3 + len(early) + len(held.arrays)),
         out_specs=[whole] * 3,
         out_shape=[
             *[
@@ -431,15 +437,15 @@
             jax.ShapeDtypeStruct((held.step_count, held.columns), jnp.float32),
         ],
         scratch_shapes=[
-            pltpu.VMEM((held.height, held.columns), jnp.float32),
+            pltpu.VMEM((len(early), held.height, held.columns), jnp.float32),
             pltpu.VMEM((kv_heads, tokens, count), jnp.bfloat16),
             pltpu.VMEM((tokens, held.columns), jnp.bfloat16),
-            pltpu.SemaphoreType.DMA((1,)),
+            pltpu.SemaphoreType.DMA((len(early),)),
             *held.scratch,
         ],
         compiler_params=pltpu.CompilerParams(vmem_limit_bytes=57 * MIB),
         cost_estimate=LIGHT,
-    )(places, turns, blocks, *inputs, prompt, got, steps, early, *held.arrays)
+    )(places, turns, blocks, *inputs, prompt, got, steps, *early, *held.arrays)
 
 
 def out_project(blocks, parts, queries, new_keys, new_values, weight, width):
@@ -582,7 +588,15 @@
     packed = packed_queries.shape[0]
 
     places = [(k, flip) for k in range(deep) for flip in (0, 1)]
-    own_blocks = jnp.stack([block(behind(k), flip, own_c) for k, flip in places])
+    parts_of = [
+        tuple(range(0, 2 * deep, 2)),
+        tuple(range(1, 2 * deep - 4, 2)),
+        tuple(range(2 * deep - 3, 2 * deep, 2)),
+    ]
+    taken_blocks = {
+        which: jnp.stack([block(behind(places[i][0]), places[i][1], own_c) for i in which])
+        for which in (tuple(range(2 * deep)), *parts_of)
+    }
     query_turns = jnp.stack([(own_turn + deep - order.index(a)) % deep for a in range(deep)])
     own_place = (own_kv + jnp.where(first, 0, KV_HEADS // 2)) % KV_HEADS * HEAD_DIM
     done = {}
@@ -606,7 +620,8 @@
             both_z[k + 1] = send(along_ring, both_z[k])
         both_x[k] = send(along_x, both_z[k])
         key_full[k] = jnp.concatenate([both_z[k][:width], both_x[k][:width]])
-        key_y[k] = send(along_y, after(key_full[k], key_y[k - 1]))
+        early_work = (taken_blocks, kv_places, query_turns) if k == 2 else ()
+        key_y[k] = send(along_y, after(key_full[k], (key_y[k - 1], early_work)))
     for k in range(1, deep):
         theirs[k] = send(along_ring, theirs[k - 1])
         theirs_x[k] = send(along_x, theirs[k][:width])
@@ -623,18 +638,17 @@
     ]
 
     def project_blocks(pieces, which, acc, ready, kind):
-        taken = after(jnp.stack([own_blocks[i] for i in which]), ready)
+        taken = after(taken_blocks[tuple(which)], ready)
         return project(
             prompt_states, got, wide_states, taken, width, [pieces[i] for i in which], acc, kind
         )
 
-    early = [*range(0, 2 * deep, 2), 1]
-    late = [i for i in range(2 * deep) if i not in early]
     value_early = project_blocks(
-        value_pieces, early, None, (theirs_x[1], theirs[deep - 1]), jnp.float32
+        value_pieces, parts_of[0], None, (theirs_x[1], theirs[deep - 1]), jnp.float32
     )
     awaited = (value_early, [theirs_x[k] for k in range(1, deep)])
     key_sum = project_blocks(key_pieces, range(2 * deep), None, awaited, jnp.bfloat16)
+    value_next = project_blocks(value_pieces, parts_of[1], None, key_sum, jnp.float32)
     key_back = in_chip(key_sum)
 
     def own_head(sums):
@@ -651,8 +665,8 @@
         masks = [token_prompt[:, None], row_prompt[None, :]]
     kept, sent, step_values = attend(
         kv_places, query_turns, ring_queries, key_sum, key_back, cosine, sine_part, masks,
-        prompt_states, got, wide_states, jnp.stack([own_blocks[i] for i in late]), width,
-        [value_pieces[i] for i in late], value_early,
+        prompt_states, got, wide_states, taken_blocks[parts_of[2]], width,
+        [value_pieces[i] for i in parts_of[2]], [value_early, value_next],
     )
     new_values = own_head(step_values) + own_head(in_chip(step_values))
     new_values = new_values.astype(jnp.bfloat16).astype(jnp.float32).reshape(steps, HEAD_DIM)

time: 147 us -> 147 us (level)
  waiting for transfers between devices: 47.4 us -> 41 us
  Pallas kernels: 35.6 us -> 39.7 us
    ppermute x31, waiting for transfers between devices: 47.4 us -> 41 us  [move(): return lax.ppermute(value, ('groups', 'sample'), pairs)]
    pallas_call x2 -> x3, Pallas kernels: 16.9 us -> 21.5 us  [project(): pl.pallas_call(body, in_specs=[pl.BlockSpec(memory_space=pltpu.SMEM)] + [...]
    slice x6, local copies, waits for them, and re-layouts: 0.11 us -> 2.01 us  [on_device(): key_full[k] = jnp.concatenate([both_z[k][:width], both_x[k][:width]])]
    unnamed x62 -> x54, local copies, waits for them, and re-layouts: 4.1 us -> 3.42 us
  transfers between devices with their start and end apart: 31 -> 31, of which waited for: 17 -> 14; matrix products, arithmetic and copies ran while one was open for 10% -> 12% of each run, Pallas kernels for 9% -> 12%
where the time goes in v16:
time: 147 us; the launch traced here: 146 us
  starting transfers between devices  43 us (29%)
  waiting for transfers between devices  41 us (28%)
  Pallas kernels  39.7 us (27%)
  local copies, waits for them, and re-layouts  11.1 us (8%)
  other arithmetic  10.8 us (7%)
    ppermute x31, starting transfers between devices, move(): return lax.ppermute(value, ('groups', 'sample'), pairs)  43 us
    ppermute x31, waiting for transfers between devices, move(): return lax.ppermute(value, ('groups', 'sample'), pairs)  41 us
    pallas_call x3, Pallas kernels, project(): pl.pallas_call(body, in_specs=[pl.BlockSpec(memory_space=pltpu.SMEM)] + [...  21.5 us
    pallas_call x1, Pallas kernels, attend(): pl.pallas_call(body, in_specs=[pl.BlockSpec(memory_space=pltpu.SMEM)] * 3...  11.2 us
    pallas_call x1, Pallas kernels, project_queries(): pl.pallas_call(body, in_specs=[whole, pl.BlockSpec(memory_space=pltpu.HBM...  4.71 us
    unnamed x54, local copies, waits for them, and re-layouts  3.42 us
    sin x1, other arithmetic, rope_tables(): return (jnp.cos(angles), jnp.sin(angles))  3.05 us
  transfers between devices with their start and end apart: 31, of which 14 were waited for; matrix products, arithmetic and copies ran while one was open for 12% of the time, Pallas kernels for 12%

profile of v16, /device:TPU:0, one launch (start us, length us, event | category | flops | bytes accessed | tf_op | source)
XLA Modules:
  0.0 146.1 jit_solution(14652375054428895202)
XLA Ops:
  0.5 2.6 %collective-permute-start = (bf16[512,512]{1,0:T(8,128)(2,1)}, bf16[512,512]{1,0:T(8,128)(2,1)}, u32[]{:S(2)}, u32[]{:S(2)}) collective-permute-start(bf16[512,512]{1,0:T(8,128)(2,1)} %param.12), channel_id=1, source_target_pairs={{0,2},{1,3},{2,0},{3,1},{4,6},{5,7},{6,4},{7,5},{8,10},{9,11},{10,... | collective-permute-start | bytes 1572872 | tf_op jit(solution)/shard_map/ppermute | solution.py:56
  3.0 1.1 fusion.5
  4.4 2.6 %collective-permute-start.2 = (bf16[1024,256]{1,0:T(8,128)(2,1)S(1)}, bf16[1024,256]{1,0:T(8,128)(2,1)S(1)}, u32[]{:S(2)}, u32[]{:S(2)}) collective-permute-start(bf16[1024,256]{1,0:T(8,128)(2,1)S(1)} %get-tuple-element.61.refs_0_), channel_id=1, source_target_pairs={{0,8},{1,9},{2,10},{3,11},{4,0},{5,1},{6,2},{7,3},{8,12},{9,13},{1... | collective-permute-start | bytes 1572872 | tf_op jit(solution)/shard_map/ppermute | solution.py:56
  7.4 3.0 %multiply_sine_fusion = (f32[1024,64]{1,0:T(8,128)}, f32[1024,64]{1,0:T(8,128)}) fusion(f32[64]{0:T(128)S(1)} %multiply_power_fusion, f32[1024]{0:T(1024)S(1)} %convert_bitcast_fusion), kind=kLoop, calls=%fused_computation.1 | loop fusion | flops 65536 | bytes 528640 | tf_op jit(solution)/shard_map/sin | solution.py:23
  10.6 0.6 broadcast_in_dim.21
  11.3 0.6 broadcast_in_dim.36
  11.9 4.7 %shard_map.73.refs_4_ = bf16[64,256]{1,0:T(8,128)(2,1)} custom-call(bf16[64,8192]{1,0:T(8,128)(2,1)} %bitcast.42, bf16[8192,256]{1,0:T(8,128)(2,1)} %weight_ref.1, f32[64,128]{1,0:T(8,128)} %bitcast.48, f32[64,128]{1,0:T(8,128)} %bitcast.49), custom_call_target="tpu_custom_call" | custom-call | flops 1 | bytes 1 | tf_op jit(solution)/shard_map/pallas_call | solution.py:106
  16.7 0.8 pad_maximum_fusion.refs_0_
  17.5 1.1 collective-permute-done.2.refs_2_
  18.5 3.4 %collective-permute-start.3 = (bf16[1024,256]{1,0:T(8,128)(2,1)S(1)}, bf16[1024,256]{1,0:T(8,128)(2,1)S(1)}, u32[]{:S(2)}, u32[]{:S(2)}) collective-permute-start(bf16[1024,256]{1,0:T(8,128)(2,1)S(1)} %collective-permute-done.2.refs_2_), channel_id=1, source_target_pairs={{0,8},{1,9},{2,10},{3,11},{4,0},{5,1},{6,2},{7,3},{8,12},{9,13},{1... | collective-permute-start | bytes 1572872 | tf_op jit(solution)/shard_map/ppermute | solution.py:56
  21.9 1.5 %collective-permute-start.12 = (bf16[1024,256]{1,0:T(8,128)(2,1)S(1)}, bf16[1024,256]{1,0:T(8,128)(2,1)S(1)}, u32[]{:S(2)}, u32[]{:S(2)}) collective-permute-start(bf16[1024,256]{1,0:T(8,128)(2,1)S(1)} %collective-permute-done.2.refs_2_), channel_id=1, source_target_pairs={{0,16},{1,17},{2,18},{3,19},{4,20},{5,21},{6,22},{7,23},{8,24},{9,... | collective-permute-start | bytes 1572872 | tf_op jit(solution)/shard_map/ppermute | solution.py:56
  23.4 1.8 %broadcast_select_fusion.2 = (bf16[512,256]{1,0:T(8,128)(2,1)}, bf16[512,256]{1,0:T(8,128)(2,1)S(1)}) fusion(pred[]{:T(512)S(6)} %eq.29, bf16[512,512]{1,0:T(8,128)(2,1)} %collective-permute-done), kind=kLoop, calls=%fused_computation.13 | loop fusion | flops 262144 | bytes 1048577 | tf_op jit(solution)/shard_map/jit(_where)/select_n | solution.py:613
  25.2 0.5 collective-permute-start.1
  25.7 0.6 pad_add_fusion.1.block_ref
  26.3 6.3 %collective-permute-done.3.refs_4_ = bf16[1024,256]{1,0:T(8,128)(2,1)S(1)} collective-permute-done((bf16[1024,256]{1,0:T(8,128)(2,1)S(1)}, bf16[1024,256]{1,0:T(8,128)(2,1)S(1)}, u32[]{:S(2)}, u32[]{:S(2)}) %collective-permute-start.3) | collective-permute-done | bytes 524320 | tf_op jit(solution)/shard_map/ppermute | solution.py:56
  32.6 3.4 %collective-permute-start.5 = (bf16[1024,256]{1,0:T(8,128)(2,1)S(1)}, bf16[1024,256]{1,0:T(8,128)(2,1)}, u32[]{:S(2)}, u32[]{:S(2)}) collective-permute-start(bf16[1024,256]{1,0:T(8,128)(2,1)S(1)} %collective-permute-done.3.refs_4_), channel_id=1, source_target_pairs={{0,8},{1,9},{2,10},{3,11},{4,0},{5,1},{6,2},{7,3},{8,12},{9,13},{1... | collective-permute-start | bytes 1572872 | tf_op jit(solution)/shard_map/ppermute | solution.py:56
  36.0 1.5 %collective-permute-start.9 = (bf16[1024,256]{1,0:T(8,128)(2,1)S(1)}, bf16[1024,256]{1,0:T(8,128)(2,1)}, u32[]{:S(2)}, u32[]{:S(2)}) collective-permute-start(bf16[1024,256]{1,0:T(8,128)(2,1)S(1)} %collective-permute-done.3.refs_4_), channel_id=1, source_target_pairs={{0,16},{1,17},{2,18},{3,19},{4,20},{5,21},{6,22},{7,23},{8,24},{9,... | collective-permute-start | bytes 1572872 | tf_op jit(solution)/shard_map/ppermute | solution.py:56
  37.5 0.8 copy-done.16
  39.1 0.6 pad_add_fusion.4.block_ref
  39.7 0.8 slice.126
  40.5 0.7 collective-permute-start.4
  41.2 0.6 pad_add_fusion.3.block_ref
  41.8 0.7 stack.141.block_ref
  42.5 0.6 and_select_fusion.1
  43.1 5.2 %collective-permute-done.5.refs_6_ = bf16[1024,256]{1,0:T(8,128)(2,1)} collective-permute-done((bf16[1024,256]{1,0:T(8,128)(2,1)S(1)}, bf16[1024,256]{1,0:T(8,128)(2,1)}, u32[]{:S(2)}, u32[]{:S(2)}) %collective-permute-start.5) | collective-permute-done | bytes 524320 | tf_op jit(solution)/shard_map/ppermute | solution.py:56
  48.4 1.5 %collective-permute-start.13 = (bf16[1024,256]{1,0:T(8,128)(2,1)}, bf16[1024,256]{1,0:T(8,128)(2,1)S(1)}, u32[]{:S(2)}, u32[]{:S(2)}) collective-permute-start(bf16[1024,256]{1,0:T(8,128)(2,1)} %collective-permute-done.5.refs_6_), channel_id=1, source_target_pairs={{0,16},{1,17},{2,18},{3,19},{4,20},{5,21},{6,22},{7,23},{8,24},{9,... | collective-permute-start | bytes 1572872 | tf_op jit(solution)/shard_map/ppermute | solution.py:56
  49.9 1.0 slice.133
  50.9 0.6 collective-permute-start.17
  51.5 1.3 collective-permute-done.4.refs_1_.refs_2_
  52.8 3.4 %collective-permute-start.6 = (bf16[640,256]{1,0:T(8,128)(2,1)S(1)}, bf16[640,256]{1,0:T(8,128)(2,1)S(1)}, u32[]{:S(2)}, u32[]{:S(2)}) collective-permute-start(bf16[640,256]{1,0:T(8,128)(2,1)S(1)} %collective-permute-done.4.refs_1_.refs_2_), channel_id=1, source_target_pairs={{0,8},{1,9},{2,10},{3,11},{4,0},{5,1},{6,2},{7,3},{8,12},{9,13},{1... | collective-permute-start | bytes 983048 | tf_op jit(solution)/shard_map/ppermute | solution.py:56
  56.2 1.6 %collective-permute-start.10 = (bf16[512,256]{1,0:T(8,128)(2,1)S(1)}, bf16[512,256]{1,0:T(8,128)(2,1)S(1)}, u32[]{:S(2)}, u32[]{:S(2)}) collective-permute-start(bf16[512,256]{1,0:T(8,128)(2,1)S(1)} %slice.127), channel_id=1, source_target_pairs={{0,16},{1,17},{2,18},{3,19},{4,20},{5,21},{6,22},{7,23},{8,24},{9,... | collective-permute-start | bytes 786440 | tf_op jit(solution)/shard_map/ppermute | solution.py:56
  57.7 1.0 slice.134
  58.7 2.2 %collective-permute-done.6.refs_2_.refs_11_ = bf16[640,256]{1,0:T(8,128)(2,1)S(1)} collective-permute-done((bf16[640,256]{1,0:T(8,128)(2,1)S(1)}, bf16[640,256]{1,0:T(8,128)(2,1)S(1)}, u32[]{:S(2)}, u32[]{:S(2)}) %collective-permute-start.6) | collective-permute-done | bytes 327712 | tf_op jit(solution)/shard_map/ppermute | solution.py:56
  60.9 3.4 %collective-permute-start.7 = (bf16[640,256]{1,0:T(8,128)(2,1)S(1)}, bf16[640,256]{1,0:T(8,128)(2,1)S(1)}, u32[]{:S(2)}, u32[]{:S(2)}) collective-permute-start(bf16[640,256]{1,0:T(8,128)(2,1)S(1)} %collective-permute-done.6.refs_2_.refs_11_), channel_id=1, source_target_pairs={{0,8},{1,9},{2,10},{3,11},{4,0},{5,1},{6,2},{7,3},{8,12},{9,13},{1... | collective-permute-start | bytes 983048 | tf_op jit(solution)/shard_map/ppermute | solution.py:56
  64.4 0.6 collective-permute-start.18
  65.0 1.6 %collective-permute-start.14 = (bf16[512,256]{1,0:T(8,128)(2,1)S(1)}, bf16[512,256]{1,0:T(8,128)(2,1)S(1)}, u32[]{:S(2)}, u32[]{:S(2)}) collective-permute-start(bf16[512,256]{1,0:T(8,128)(2,1)S(1)} %slice.128), channel_id=1, source_target_pairs={{0,16},{1,17},{2,18},{3,19},{4,20},{5,21},{6,22},{7,23},{8,24},{9,... | collective-permute-start | bytes 786440 | tf_op jit(solution)/shard_map/ppermute | solution.py:56
  66.6 2.3 %collective-permute-done.7.refs_3_.refs_13_ = bf16[640,256]{1,0:T(8,128)(2,1)S(1)} collective-permute-done((bf16[640,256]{1,0:T(8,128)(2,1)S(1)}, bf16[640,256]{1,0:T(8,128)(2,1)S(1)}, u32[]{:S(2)}, u32[]{:S(2)}) %collective-permute-start.7) | collective-permute-done | bytes 327712 | tf_op jit(solution)/shard_map/ppermute | solution.py:56
  68.9 1.6 %collective-permute-start.15 = (bf16[512,256]{1,0:T(8,128)(2,1)S(1)}, bf16[512,256]{1,0:T(8,128)(2,1)S(1)}, u32[]{:S(2)}, u32[]{:S(2)}) collective-permute-start(bf16[512,256]{1,0:T(8,128)(2,1)S(1)} %slice.129), channel_id=1, source_target_pairs={{0,16},{1,17},{2,18},{3,19},{4,20},{5,21},{6,22},{7,23},{8,24},{9,... | collective-permute-start | bytes 786440 | tf_op jit(solution)/shard_map/ppermute | solution.py:56
  70.5 6.9 %shard_map.75.refs_9_ = f32[1088,512]{1,0:T(8,128)} custom-call(s32[4]{0:T(128)} %pad_add_fusion.3.block_ref, bf16[512,8192]{1,0:T(8,128)(2,1)} %refs_6_.1, bf16[512,8192]{1,0:T(8,128)(2,1)} %collective-permute-done.11.got_ref.refs_7_, bf16[64,8192]{1,0:T(8,128)(2,1)} %bitcast.43, bf16[1024,256]{1,0:T(8,128)(2,1)} %copy-done.8, bf16[1024,256]{1,0:T(8,128)(2,1)} %copy-done.9, ...), custom_call_target="tpu_custom_call" | custom-call | flops 1 | bytes 1 | tf_op jit(solution)/shard_map/pallas_call | solution.py:226
  77.5 0.9 copy-done.20
  78.4 9.3 %shard_map.76.refs_2_ = bf16[1088,512]{1,0:T(8,128)(2,1)} custom-call(s32[8]{0:T(128)} %stack.141.block_ref, bf16[512,8192]{1,0:T(8,128)(2,1)} %refs_6_.1, bf16[512,8192]{1,0:T(8,128)(2,1)} %collective-permute-done.11.got_ref.refs_7_, bf16[64,8192]{1,0:T(8,128)(2,1)} %bitcast.44, bf16[1088,256]{1,0:T(8,128)(2,1)} %copy-done.10, ...), custom_call_target="tpu_custom_call" | custom-call | flops 1 | bytes 1 | tf_op jit(solution)/shard_map/pallas_call | solution.py:226
  88.2 0.5 collective-permute-start.8
  88.9 5.3 %shard_map.77.refs_10_ = f32[1088,512]{1,0:T(8,128)} custom-call(s32[2]{0:T(128)} %pad_add_fusion.4.block_ref, bf16[512,8192]{1,0:T(8,128)(2,1)} %refs_6_.1, bf16[512,8192]{1,0:T(8,128)(2,1)} %collective-permute-done.11.got_ref.refs_7_, bf16[64,8192]{1,0:T(8,128)(2,1)} %bitcast.45, bf16[640,256]{1,0:T(8,128)(2,1)} %copy-done.1, ...), custom_call_target="tpu_custom_call" | custom-call | flops 1 | bytes 1 | tf_op jit(solution)/shard_map/pallas_call | solution.py:226
  94.2 0.7 copy-done.25
  94.9 11.2 %shard_map.78 = (bf16[4,2,144,128]{3,2,1,0:T(8,128)(2,1)}, bf16[4,2,144,128]{3,2,1,0:T(8,128)(2,1)}, f32[64,512]{1,0:T(8,128)}) custom-call(s32[4]{0:T(128)} %get-tuple-element.81.place_ref, s32[4]{0:T(128)} %get-tuple-element.82.turn_ref, s32[2]{0:T(128)} %pad_add_fusion.1.block_ref, bf16[4,128,256]{2,1,0:T(8,128)(2,1)} %copy-done.5, ...), custom_call_target="tpu_custom_call" | custom-call | flops 1 | bytes 1 | tf_op jit(solution)/shard_map/pallas_call | solution.py:424
  106.4 0.8 slice.136
  107.7 0.8 slice.137
  108.6 1.0 copy-done.7
  109.6 0.6 collective-permute-start.21
  110.3 5.2 %collective-permute-done.21.far_ref = bf16[4,144,128]{2,1,0:T(8,128)(2,1)S(1)} collective-permute-done((bf16[4,144,128]{2,1,0:T(8,128)(2,1)S(1)}, bf16[4,144,128]{2,1,0:T(8,128)(2,1)S(1)}, u32[]{:S(2)}, u32[]{:S(2)}) %collective-permute-start.21) | collective-permute-done | bytes 147488 | tf_op jit(solution)/shard_map/ppermute | solution.py:56
  115.6 2.4 %collective-permute-start.22 = (bf16[144,128]{1,0:T(8,128)(2,1)S(1)}, bf16[144,128]{1,0:T(8,128)(2,1)S(1)}, u32[]{:S(2)}, u32[]{:S(2)}) collective-permute-start(bf16[144,128]{1,0:T(8,128)(2,1)S(1)} %get-tuple-element.57), channel_id=1, source_target_pairs={{0,4},{1,5},{2,6},{3,7},{4,0},{5,1},{6,2},{7,3},{8,12},{9,13},{10,... | collective-permute-start | bytes 110600 | tf_op jit(solution)/shard_map/ppermute | solution.py:56
  118.0 1.2 collective-permute-start.23
  119.2 1.4 collective-permute-start.24
  120.6 0.8 fusion.refs_6_
  121.4 2.3 %collective-permute-done.23.refs_2_ = bf16[144,128]{1,0:T(8,128)(2,1)S(1)} collective-permute-done((bf16[144,128]{1,0:T(8,128)(2,1)S(1)}, bf16[144,128]{1,0:T(8,128)(2,1)S(1)}, u32[]{:S(2)}, u32[]{:S(2)}) %collective-permute-start.23) | collective-permute-done | bytes 36896 | tf_op jit(solution)/shard_map/ppermute | solution.py:56
  123.7 1.3 collective-permute-done.24.refs_3_
  125.0 1.7 %shard_map.81 = bf16[64,8192]{1,0:T(8,128)(2,1)S(1)} custom-call(s32[16]{0:T(128)S(1)} %stack.126.block_ref, bf16[144,128]{1,0:T(8,128)(2,1)S(1)} %get-tuple-element.56.refs_0_, bf16[144,128]{1,0:T(8,128)(2,1)S(1)} %collective-permute-done.22.refs_1_, bf16[144,128]{1,0:T(8,128)(2,1)S(1)} %collective-permute-done.23.refs_2_, ...), custom_call_target="tpu_custom_call" | custom-call | flops 1 | bytes 1 | tf_op jit(solution)/shard_map/pallas_call | solution.py:265
  126.8 1.9 %collective-permute-done.26 = bf16[64,4096]{1,0:T(8,128)(2,1)S(1)} collective-permute-done((bf16[64,4096]{1,0:T(8,128)(2,1)S(1)}, bf16[64,4096]{1,0:T(8,128)(2,1)S(1)}, u32[]{:S(2)}, u32[]{:S(2)}) %collective-permute-start.26) | collective-permute-done | bytes 524320 | tf_op jit(solution)/shard_map/ppermute | solution.py:56
  129.3 7.9 %collective-permute-done.27 = bf16[64,2048]{1,0:T(8,128)(2,1)S(1)} collective-permute-done((bf16[64,2048]{1,0:T(8,128)(2,1)S(1)}, bf16[64,2048]{1,0:T(8,128)(2,1)S(1)}, u32[]{:S(2)}, u32[]{:S(2)}) %collective-permute-start.27) | collective-permute-done | bytes 262176 | tf_op jit(solution)/shard_map/ppermute | solution.py:56
  137.3 1.4 collective-permute-start.30
  139.0 2.8 %collective-permute-start.28 = (bf16[64,512]{1,0:T(8,128)(2,1)S(1)}, bf16[64,512]{1,0:T(8,128)(2,1)S(1)}, u32[]{:S(2)}, u32[]{:S(2)}) collective-permute-start(bf16[64,512]{1,0:T(8,128)(2,1)S(1)} %get-tuple-element.69), channel_id=1, source_target_pairs={{0,4},{1,5},{2,6},{3,7},{4,0},{5,1},{6,2},{7,3},{8,12},{9,13},{10,... | collective-permute-start | bytes 196616 | tf_op jit(solution)/shard_map/ppermute | solution.py:56
  141.8 2.2 %collective-permute-done.30 = bf16[64,512]{1,0:T(8,128)(2,1)S(1)} collective-permute-done((bf16[64,512]{1,0:T(8,128)(2,1)S(1)}, bf16[64,512]{1,0:T(8,128)(2,1)S(1)}, u32[]{:S(2)}, u32[]{:S(2)}) %collective-permute-start.30) | collective-permute-done | bytes 65568 | tf_op jit(solution)/shard_map/ppermute | solution.py:56
  144.0 1.4 collective-permute-done.29
  145.5 0.7 add_convert_fusion.2
  (113 shorter events, 5.0 us)
Async XLA Ops:
  0.0 4.1 %copy-start.21 = (bf16[512,512]{1,0:T(8,128)(2,1)S(1)}, bf16[512,512]{1,0:T(8,128)(2,1)}, u32[]{:S(2)}) copy-start(bf16[512,512]{1,0:T(8,128)(2,1)} %param.11) | copy-start | bytes 1572868
  0.0 70.5 %collective-permute-start.11 = (bf16[512,8192]{1,0:T(8,128)(2,1)}, bf16[512,8192]{1,0:T(8,128)(2,1)}, u32[]{:S(2)}, u32[]{:S(2)}) collective-permute-start(bf16[512,8192]{1,0:T(8,128)(2,1)} %refs_6_.1), channel_id=1, source_target_pairs={{0,1},{1,0},{2,3},{3,2},{4,5},{5,4},{6,7},{7,6},{8,9},{9,8},{10,11... | collective-permute-start | bytes 25165832 | tf_op jit(solution)/shard_map/ppermute | solution.py:56
  0.5 23.0 %collective-permute-start = (bf16[512,512]{1,0:T(8,128)(2,1)}, bf16[512,512]{1,0:T(8,128)(2,1)}, u32[]{:S(2)}, u32[]{:S(2)}) collective-permute-start(bf16[512,512]{1,0:T(8,128)(2,1)} %param.12), channel_id=1, source_target_pairs={{0,2},{1,3},{2,0},{3,1},{4,6},{5,7},{6,4},{7,5},{8,10},{9,11},{10,... | collective-permute-start | bytes 1572872 | tf_op jit(solution)/shard_map/ppermute | solution.py:56
  4.2 3.0 %copy-start.26 = (s32[64]{0:T(128)S(1)}, s32[64]{0:T(128)}, u32[]{:S(2)}) copy-start(s32[64]{0:T(128)} %param.9) | copy-start | bytes 772
  4.4 12.2 %copy-start.8 = (bf16[1024,256]{1,0:T(8,128)(2,1)}, bf16[1024,256]{1,0:T(8,128)(2,1)S(1)}, u32[]{:S(2)}) copy-start(bf16[1024,256]{1,0:T(8,128)(2,1)S(1)} %get-tuple-element.61.refs_0_) | copy-start | bytes 1572868
  4.4 12.3 %copy-start.9 = (bf16[1024,256]{1,0:T(8,128)(2,1)}, bf16[1024,256]{1,0:T(8,128)(2,1)S(1)}, u32[]{:S(2)}) copy-start(bf16[1024,256]{1,0:T(8,128)(2,1)S(1)} %get-tuple-element.62.refs_1_) | copy-start | bytes 1572868
  4.4 14.2 %collective-permute-start.2 = (bf16[1024,256]{1,0:T(8,128)(2,1)S(1)}, bf16[1024,256]{1,0:T(8,128)(2,1)S(1)}, u32[]{:S(2)}, u32[]{:S(2)}) collective-permute-start(bf16[1024,256]{1,0:T(8,128)(2,1)S(1)} %get-tuple-element.61.refs_0_), channel_id=1, source_target_pairs={{0,8},{1,9},{2,10},{3,11},{4,0},{5,1},{6,2},{7,3},{8,12},{9,13},{1... | collective-permute-start | bytes 1572872 | tf_op jit(solution)/shard_map/ppermute | solution.py:56
  17.5 20.8 %copy-start.10 = (bf16[1088,256]{1,0:T(8,128)(2,1)}, bf16[1088,256]{1,0:T(8,128)(2,1)S(1)}, u32[]{:S(2)}) copy-start(bf16[1088,256]{1,0:T(8,128)(2,1)S(1)} %pad_maximum_fusion.refs_0_) | copy-start | bytes 1671172
  18.5 19.8 %copy-start.14 = (bf16[1024,256]{1,0:T(8,128)(2,1)}, bf16[1024,256]{1,0:T(8,128)(2,1)S(1)}, u32[]{:S(2)}) copy-start(bf16[1024,256]{1,0:T(8,128)(2,1)S(1)} %collective-permute-done.2.refs_2_) | copy-start | bytes 1572868
  18.5 14.1 %collective-permute-start.3 = (bf16[1024,256]{1,0:T(8,128)(2,1)S(1)}, bf16[1024,256]{1,0:T(8,128)(2,1)S(1)}, u32[]{:S(2)}, u32[]{:S(2)}) collective-permute-start(bf16[1024,256]{1,0:T(8,128)(2,1)S(1)} %collective-permute-done.2.refs_2_), channel_id=1, source_target_pairs={{0,8},{1,9},{2,10},{3,11},{4,0},{5,1},{6,2},{7,3},{8,12},{9,13},{1... | collective-permute-start | bytes 1572872 | tf_op jit(solution)/shard_map/ppermute | solution.py:56
  21.9 15.6 %collective-permute-start.12 = (bf16[1024,256]{1,0:T(8,128)(2,1)S(1)}, bf16[1024,256]{1,0:T(8,128)(2,1)S(1)}, u32[]{:S(2)}, u32[]{:S(2)}) collective-permute-start(bf16[1024,256]{1,0:T(8,128)(2,1)S(1)} %collective-permute-done.2.refs_2_), channel_id=1, source_target_pairs={{0,16},{1,17},{2,18},{3,19},{4,20},{5,21},{6,22},{7,23},{8,24},{9,... | collective-permute-start | bytes 1572872 | tf_op jit(solution)/shard_map/ppermute | solution.py:56
  25.2 13.4 %collective-permute-start.1 = (bf16[1088,256]{1,0:T(8,128)(2,1)S(1)}, bf16[1088,256]{1,0:T(8,128)(2,1)}, u32[]{:S(2)}, u32[]{:S(2)}) collective-permute-start(bf16[1088,256]{1,0:T(8,128)(2,1)S(1)} %pad_maximum_fusion.refs_0_), channel_id=1, source_target_pairs={{0,2},{1,3},{2,0},{3,1},{4,6},{5,7},{6,4},{7,5},{8,10},{9,11},{10,... | collective-permute-start | bytes 1671176 | tf_op jit(solution)/shard_map/ppermute | solution.py:56
  25.7 14.8 %copy-start.6 = (bf16[64,256]{1,0:T(8,128)(2,1)S(1)}, bf16[64,256]{1,0:T(8,128)(2,1)}, u32[]{:S(2)}) copy-start(bf16[64,256]{1,0:T(8,128)(2,1)} %shard_map.73.refs_4_) | copy-start | bytes 98308
  32.6 10.5 %copy-start.15 = (bf16[1024,256]{1,0:T(8,128)(2,1)}, bf16[1024,256]{1,0:T(8,128)(2,1)S(1)}, u32[]{:S(2)}) copy-start(bf16[1024,256]{1,0:T(8,128)(2,1)S(1)} %collective-permute-done.3.refs_4_) | copy-start | bytes 1572868
  32.6 15.8 %collective-permute-start.5 = (bf16[1024,256]{1,0:T(8,128)(2,1)S(1)}, bf16[1024,256]{1,0:T(8,128)(2,1)}, u32[]{:S(2)}, u32[]{:S(2)}) collective-permute-start(bf16[1024,256]{1,0:T(8,128)(2,1)S(1)} %collective-permute-done.3.refs_4_), channel_id=1, source_target_pairs={{0,8},{1,9},{2,10},{3,11},{4,0},{5,1},{6,2},{7,3},{8,12},{9,13},{1... | collective-permute-start | bytes 1572872 | tf_op jit(solution)/shard_map/ppermute | solution.py:56
  36.0 13.9 %collective-permute-start.9 = (bf16[1024,256]{1,0:T(8,128)(2,1)S(1)}, bf16[1024,256]{1,0:T(8,128)(2,1)}, u32[]{:S(2)}, u32[]{:S(2)}) collective-permute-start(bf16[1024,256]{1,0:T(8,128)(2,1)S(1)} %collective-permute-done.3.refs_4_), channel_id=1, source_target_pairs={{0,16},{1,17},{2,18},{3,19},{4,20},{5,21},{6,22},{7,23},{8,24},{9,... | collective-permute-start | bytes 1572872 | tf_op jit(solution)/shard_map/ppermute | solution.py:56
  37.5 0.8 copy-start.16
  38.4 12.5 %copy-start.11 = (bf16[1024,256]{1,0:T(8,128)(2,1)}, bf16[1024,256]{1,0:T(8,128)(2,1)S(1)}, u32[]{:S(2)}) copy-start(bf16[1024,256]{1,0:T(8,128)(2,1)S(1)} %pad_maximum_fusion.3.refs_2_) | copy-start | bytes 1572868
  38.6 12.3 %collective-permute-start.16 = (bf16[1024,256]{1,0:T(8,128)(2,1)S(1)}, bf16[1024,256]{1,0:T(8,128)(2,1)S(1)}, u32[]{:S(2)}, u32[]{:S(2)}) collective-permute-start(bf16[1024,256]{1,0:T(8,128)(2,1)S(1)} %pad_maximum_fusion.3.refs_2_), channel_id=1, source_target_pairs={{0,2},{1,3},{2,0},{3,1},{4,6},{5,7},{6,4},{7,5},{8,10},{9,11},{10,... | collective-permute-start | bytes 1572872 | tf_op jit(solution)/shard_map/ppermute | solution.py:56
  40.5 47.3 %copy-start.1 = (bf16[640,256]{1,0:T(8,128)(2,1)}, bf16[640,256]{1,0:T(8,128)(2,1)S(1)}, u32[]{:S(2)}) copy-start(bf16[640,256]{1,0:T(8,128)(2,1)S(1)} %pad_maximum_fusion.6.refs_0_) | copy-start | bytes 983044
  40.5 12.3 %collective-permute-start.4 = (bf16[640,256]{1,0:T(8,128)(2,1)S(1)}, bf16[640,256]{1,0:T(8,128)(2,1)S(1)}, u32[]{:S(2)}, u32[]{:S(2)}) collective-permute-start(bf16[640,256]{1,0:T(8,128)(2,1)S(1)} %pad_maximum_fusion.6.refs_0_), channel_id=1, source_target_pairs={{0,8},{1,9},{2,10},{3,11},{4,0},{5,1},{6,2},{7,3},{8,12},{9,13},{1... | collective-permute-start | bytes 983048 | tf_op jit(solution)/shard_map/ppermute | solution.py:56
  48.4 15.9 %collective-permute-start.13 = (bf16[1024,256]{1,0:T(8,128)(2,1)}, bf16[1024,256]{1,0:T(8,128)(2,1)S(1)}, u32[]{:S(2)}, u32[]{:S(2)}) collective-permute-start(bf16[1024,256]{1,0:T(8,128)(2,1)} %collective-permute-done.5.refs_6_), channel_id=1, source_target_pairs={{0,16},{1,17},{2,18},{3,19},{4,20},{5,21},{6,22},{7,23},{8,24},{9,... | collective-permute-start | bytes 1572872 | tf_op jit(solution)/shard_map/ppermute | solution.py:56
  50.9 13.5 %copy-start.12 = (bf16[1024,256]{1,0:T(8,128)(2,1)}, bf16[1024,256]{1,0:T(8,128)(2,1)S(1)}, u32[]{:S(2)}) copy-start(bf16[1024,256]{1,0:T(8,128)(2,1)S(1)} %pad_maximum_fusion.4.refs_4_) | copy-start | bytes 1572868
  50.9 13.5 %copy-start.18 = (bf16[1024,256]{1,0:T(8,128)(2,1)}, bf16[1024,256]{1,0:T(8,128)(2,1)S(1)}, u32[]{:S(2)}) copy-start(bf16[1024,256]{1,0:T(8,128)(2,1)S(1)} %collective-permute-done.16.refs_3_) | copy-start | bytes 1572868
  50.9 13.5 %collective-permute-start.17 = (bf16[1024,256]{1,0:T(8,128)(2,1)S(1)}, bf16[1024,256]{1,0:T(8,128)(2,1)S(1)}, u32[]{:S(2)}, u32[]{:S(2)}) collective-permute-start(bf16[1024,256]{1,0:T(8,128)(2,1)S(1)} %pad_maximum_fusion.4.refs_4_), channel_id=1, source_target_pairs={{0,2},{1,3},{2,0},{3,1},{4,6},{5,7},{6,4},{7,5},{8,10},{9,11},{10,... | collective-permute-start | bytes 1572872 | tf_op jit(solution)/shard_map/ppermute | solution.py:56
  52.8 35.0 %copy-start.2 = (bf16[640,256]{1,0:T(8,128)(2,1)}, bf16[640,256]{1,0:T(8,128)(2,1)S(1)}, u32[]{:S(2)}) copy-start(bf16[640,256]{1,0:T(8,128)(2,1)S(1)} %collective-permute-done.4.refs_1_.refs_2_) | copy-start | bytes 983044
  52.8 8.1 %collective-permute-start.6 = (bf16[640,256]{1,0:T(8,128)(2,1)S(1)}, bf16[640,256]{1,0:T(8,128)(2,1)S(1)}, u32[]{:S(2)}, u32[]{:S(2)}) collective-permute-start(bf16[640,256]{1,0:T(8,128)(2,1)S(1)} %collective-permute-done.4.refs_1_.refs_2_), channel_id=1, source_target_pairs={{0,8},{1,9},{2,10},{3,11},{4,0},{5,1},{6,2},{7,3},{8,12},{9,13},{1... | collective-permute-start | bytes 983048 | tf_op jit(solution)/shard_map/ppermute | solution.py:56
  56.2 12.7 %collective-permute-start.10 = (bf16[512,256]{1,0:T(8,128)(2,1)S(1)}, bf16[512,256]{1,0:T(8,128)(2,1)S(1)}, u32[]{:S(2)}, u32[]{:S(2)}) collective-permute-start(bf16[512,256]{1,0:T(8,128)(2,1)S(1)} %slice.127), channel_id=1, source_target_pairs={{0,16},{1,17},{2,18},{3,19},{4,20},{5,21},{6,22},{7,23},{8,24},{9,... | collective-permute-start | bytes 786440 | tf_op jit(solution)/shard_map/ppermute | solution.py:56
  60.9 26.9 %copy-start.3 = (bf16[640,256]{1,0:T(8,128)(2,1)}, bf16[640,256]{1,0:T(8,128)(2,1)S(1)}, u32[]{:S(2)}) copy-start(bf16[640,256]{1,0:T(8,128)(2,1)S(1)} %collective-permute-done.6.refs_2_.refs_11_) | copy-start | bytes 983044
  60.9 8.0 %collective-permute-start.7 = (bf16[640,256]{1,0:T(8,128)(2,1)S(1)}, bf16[640,256]{1,0:T(8,128)(2,1)S(1)}, u32[]{:S(2)}, u32[]{:S(2)}) collective-permute-start(bf16[640,256]{1,0:T(8,128)(2,1)S(1)} %collective-permute-done.6.refs_2_.refs_11_), channel_id=1, source_target_pairs={{0,8},{1,9},{2,10},{3,11},{4,0},{5,1},{6,2},{7,3},{8,12},{9,13},{1... | collective-permute-start | bytes 983048 | tf_op jit(solution)/shard_map/ppermute | solution.py:56
  64.3 4.6 %copy-start.17 = (bf16[1024,256]{1,0:T(8,128)(2,1)}, bf16[1024,256]{1,0:T(8,128)(2,1)S(1)}, u32[]{:S(2)}) copy-start(bf16[1024,256]{1,0:T(8,128)(2,1)S(1)} %collective-permute-done.13.refs_7_) | copy-start | bytes 1572868
  64.4 13.0 %copy-start.13 = (bf16[1024,256]{1,0:T(8,128)(2,1)}, bf16[1024,256]{1,0:T(8,128)(2,1)S(1)}, u32[]{:S(2)}) copy-start(bf16[1024,256]{1,0:T(8,128)(2,1)S(1)} %pad_maximum_fusion.5.refs_6_) | copy-start | bytes 1572868
  64.4 13.0 %copy-start.19 = (bf16[1024,256]{1,0:T(8,128)(2,1)}, bf16[1024,256]{1,0:T(8,128)(2,1)S(1)}, u32[]{:S(2)}) copy-start(bf16[1024,256]{1,0:T(8,128)(2,1)S(1)} %collective-permute-done.17.refs_5_) | copy-start | bytes 1572868
  64.4 13.1 %collective-permute-start.18 = (bf16[1024,256]{1,0:T(8,128)(2,1)S(1)}, bf16[1024,256]{1,0:T(8,128)(2,1)S(1)}, u32[]{:S(2)}, u32[]{:S(2)}) collective-permute-start(bf16[1024,256]{1,0:T(8,128)(2,1)S(1)} %pad_maximum_fusion.5.refs_6_), channel_id=1, source_target_pairs={{0,2},{1,3},{2,0},{3,1},{4,6},{5,7},{6,4},{7,5},{8,10},{9,11},{10,... | collective-permute-start | bytes 1572872 | tf_op jit(solution)/shard_map/ppermute | solution.py:56
  65.0 12.4 %collective-permute-start.14 = (bf16[512,256]{1,0:T(8,128)(2,1)S(1)}, bf16[512,256]{1,0:T(8,128)(2,1)S(1)}, u32[]{:S(2)}, u32[]{:S(2)}) collective-permute-start(bf16[512,256]{1,0:T(8,128)(2,1)S(1)} %slice.128), channel_id=1, source_target_pairs={{0,16},{1,17},{2,18},{3,19},{4,20},{5,21},{6,22},{7,23},{8,24},{9,... | collective-permute-start | bytes 786440 | tf_op jit(solution)/shard_map/ppermute | solution.py:56
  68.9 18.9 %copy-start.4 = (bf16[640,256]{1,0:T(8,128)(2,1)}, bf16[640,256]{1,0:T(8,128)(2,1)S(1)}, u32[]{:S(2)}) copy-start(bf16[640,256]{1,0:T(8,128)(2,1)S(1)} %collective-permute-done.7.refs_3_.refs_13_) | copy-start | bytes 983044
  68.9 8.5 %copy-start.22 = (bf16[512,256]{1,0:T(8,128)(2,1)}, bf16[512,256]{1,0:T(8,128)(2,1)S(1)}, u32[]{:S(2)}) copy-start(bf16[512,256]{1,0:T(8,128)(2,1)S(1)} %collective-permute-done.10.refs_3_) | copy-start | bytes 786436
  68.9 8.5 %collective-permute-start.15 = (bf16[512,256]{1,0:T(8,128)(2,1)S(1)}, bf16[512,256]{1,0:T(8,128)(2,1)S(1)}, u32[]{:S(2)}, u32[]{:S(2)}) collective-permute-start(bf16[512,256]{1,0:T(8,128)(2,1)S(1)} %slice.129), channel_id=1, source_target_pairs={{0,16},{1,17},{2,18},{3,19},{4,20},{5,21},{6,22},{7,23},{8,24},{9,... | collective-permute-start | bytes 786440 | tf_op jit(solution)/shard_map/ppermute | solution.py:56
  77.5 10.2 %copy-start.23 = (bf16[512,256]{1,0:T(8,128)(2,1)}, bf16[512,256]{1,0:T(8,128)(2,1)S(1)}, u32[]{:S(2)}) copy-start(bf16[512,256]{1,0:T(8,128)(2,1)S(1)} %collective-permute-done.14.refs_12_) | copy-start | bytes 786436
  77.5 10.2 %copy-start.24 = (bf16[512,256]{1,0:T(8,128)(2,1)}, bf16[512,256]{1,0:T(8,128)(2,1)S(1)}, u32[]{:S(2)}) copy-start(bf16[512,256]{1,0:T(8,128)(2,1)S(1)} %collective-permute-done.15.refs_14_) | copy-start | bytes 786436
  77.5 0.9 copy-start.20
  87.7 6.5 %collective-permute-start.19 = (bf16[1088,512]{1,0:T(8,128)(2,1)}, bf16[1088,512]{1,0:T(8,128)(2,1)}, u32[]{:S(2)}, u32[]{:S(2)}) collective-permute-start(bf16[1088,512]{1,0:T(8,128)(2,1)} %shard_map.76.refs_2_), channel_id=1, source_target_pairs={{0,1},{1,0},{2,3},{3,2},{4,5},{5,4},{6,7},{7,6},{8,9},{9,8},{10,11... | collective-permute-start | bytes 3342344 | tf_op jit(solution)/shard_map/ppermute | solution.py:56
  88.2 6.0 %copy-start.5 = (bf16[4,128,256]{2,1,0:T(8,128)(2,1)}, bf16[4,128,256]{2,1,0:T(8,128)(2,1)S(1)}, u32[]{:S(2)}) copy-start(bf16[4,128,256]{2,1,0:T(8,128)(2,1)S(1)} %shard_map.74.refs_0_) | copy-start | bytes 786436
  88.2 6.0 %collective-permute-start.8 = (bf16[4,128,256]{2,1,0:T(8,128)(2,1)S(1)}, bf16[4,128,256]{2,1,0:T(8,128)(2,1)S(1)}, u32[]{:S(2)}, u32[]{:S(2)}) collective-permute-start(bf16[4,128,256]{2,1,0:T(8,128)(2,1)S(1)} %shard_map.74.refs_0_), channel_id=1, source_target_pairs={{0,1},{1,0},{2,3},{3,2},{4,5},{5,4},{6,7},{7,6},{8,9},{9,8},{10,11... | collective-permute-start | bytes 786440 | tf_op jit(solution)/shard_map/ppermute | solution.py:56
  94.2 0.7 copy-start.25
  94.9 30.0 %copy-start = (bf16[256,8192]{1,0:T(8,128)(2,1)S(1)}, bf16[256,8192]{1,0:T(8,128)(2,1)}, u32[]{:S(2)}) copy-start(bf16[256,8192]{1,0:T(8,128)(2,1)} %refs_7_.1) | copy-start | bytes 12582916
  106.2 2.4 %collective-permute-start.20 = (bf16[4,2,144,128]{3,2,1,0:T(8,128)(2,1)}, bf16[4,2,144,128]{3,2,1,0:T(8,128)(2,1)S(1)}, u32[]{:S(2)}, u32[]{:S(2)}) collective-permute-start(bf16[4,2,144,128]{3,2,1,0:T(8,128)(2,1)} %get-tuple-element.53), channel_id=1, source_target_pairs={{0,1},{1,0},{2,3},{3,2},{4,5},{5,4},{6,7},{7,6},{8,9},{9,8},{10,11... | collective-permute-start | bytes 884744 | tf_op jit(solution)/shard_map/ppermute | solution.py:56
  107.3 13.3 %collective-permute-start.25 = (f32[64,512]{1,0:T(8,128)}, f32[64,512]{1,0:T(8,128)S(1)}, u32[]{:S(2)}, u32[]{:S(2)}) collective-permute-start(f32[64,512]{1,0:T(8,128)} %get-tuple-element.60), channel_id=1, source_target_pairs={{0,1},{1,0},{2,3},{3,2},{4,5},{5,4},{6,7},{7,6},{8,9},{9,8},{10,11... | collective-permute-start | bytes 393224 | tf_op jit(solution)/shard_map/ppermute | solution.py:56
  108.6 1.0 copy-start.7
  109.6 5.9 %collective-permute-start.21 = (bf16[4,144,128]{2,1,0:T(8,128)(2,1)S(1)}, bf16[4,144,128]{2,1,0:T(8,128)(2,1)S(1)}, u32[]{:S(2)}, u32[]{:S(2)}) collective-permute-start(bf16[4,144,128]{2,1,0:T(8,128)(2,1)S(1)} %get-tuple-element.55), channel_id=1, source_target_pairs={{0,2},{1,3},{2,0},{3,1},{4,6},{5,7},{6,4},{7,5},{8,10},{9,11},{10,... | collective-permute-start | bytes 442376 | tf_op jit(solution)/shard_map/ppermute | solution.py:56
  115.6 5.8 %collective-permute-start.22 = (bf16[144,128]{1,0:T(8,128)(2,1)S(1)}, bf16[144,128]{1,0:T(8,128)(2,1)S(1)}, u32[]{:S(2)}, u32[]{:S(2)}) collective-permute-start(bf16[144,128]{1,0:T(8,128)(2,1)S(1)} %get-tuple-element.57), channel_id=1, source_target_pairs={{0,4},{1,5},{2,6},{3,7},{4,0},{5,1},{6,2},{7,3},{8,12},{9,13},{10,... | collective-permute-start | bytes 110600 | tf_op jit(solution)/shard_map/ppermute | solution.py:56
  118.0 5.6 %collective-permute-start.23 = (bf16[144,128]{1,0:T(8,128)(2,1)S(1)}, bf16[144,128]{1,0:T(8,128)(2,1)S(1)}, u32[]{:S(2)}, u32[]{:S(2)}) collective-permute-start(bf16[144,128]{1,0:T(8,128)(2,1)S(1)} %get-tuple-element.58), channel_id=1, source_target_pairs={{0,8},{1,9},{2,10},{3,11},{4,12},{5,13},{6,14},{7,15},{8,0},{9,1},... | collective-permute-start | bytes 110600 | tf_op jit(solution)/shard_map/ppermute | solution.py:56
  119.2 5.8 %collective-permute-start.24 = (bf16[144,128]{1,0:T(8,128)(2,1)S(1)}, bf16[144,128]{1,0:T(8,128)(2,1)S(1)}, u32[]{:S(2)}, u32[]{:S(2)}) collective-permute-start(bf16[144,128]{1,0:T(8,128)(2,1)S(1)} %get-tuple-element.59), channel_id=1, source_target_pairs={{0,12},{1,13},{2,14},{3,15},{4,8},{5,9},{6,10},{7,11},{8,4},{9,5},... | collective-permute-start | bytes 110600 | tf_op jit(solution)/shard_map/ppermute | solution.py:56
  126.7 2.0 %collective-permute-start.26 = (bf16[64,4096]{1,0:T(8,128)(2,1)S(1)}, bf16[64,4096]{1,0:T(8,128)(2,1)S(1)}, u32[]{:S(2)}, u32[]{:S(2)}) collective-permute-start(bf16[64,4096]{1,0:T(8,128)(2,1)S(1)} %slice.141), channel_id=1, source_target_pairs={{0,1},{1,0},{2,3},{3,2},{4,5},{5,4},{6,7},{7,6},{8,9},{9,8},{10,11... | collective-permute-start | bytes 1572872 | tf_op jit(solution)/shard_map/ppermute | solution.py:56
  128.8 8.4 %collective-permute-start.27 = (bf16[64,2048]{1,0:T(8,128)(2,1)S(1)}, bf16[64,2048]{1,0:T(8,128)(2,1)S(1)}, u32[]{:S(2)}, u32[]{:S(2)}) collective-permute-start(bf16[64,2048]{1,0:T(8,128)(2,1)S(1)} %slice.143), channel_id=1, source_target_pairs={{0,2},{1,3},{2,0},{3,1},{4,6},{5,7},{6,4},{7,5},{8,10},{9,11},{10,... | collective-permute-start | bytes 786440 | tf_op jit(solution)/shard_map/ppermute | solution.py:56
  137.3 6.7 %collective-permute-start.30 = (bf16[64,512]{1,0:T(8,128)(2,1)S(1)}, bf16[64,512]{1,0:T(8,128)(2,1)S(1)}, u32[]{:S(2)}, u32[]{:S(2)}) collective-permute-start(bf16[64,512]{1,0:T(8,128)(2,1)S(1)} %get-tuple-element.70), channel_id=1, source_target_pairs={{0,12},{1,13},{2,14},{3,15},{4,8},{5,9},{6,10},{7,11},{8,4},{9,5},... | collective-permute-start | bytes 196616 | tf_op jit(solution)/shard_map/ppermute | solution.py:56
  138.8 6.7 %collective-permute-start.29 = (bf16[64,512]{1,0:T(8,128)(2,1)S(1)}, bf16[64,512]{1,0:T(8,128)(2,1)S(1)}, u32[]{:S(2)}, u32[]{:S(2)}) collective-permute-start(bf16[64,512]{1,0:T(8,128)(2,1)S(1)} %get-tuple-element.71), channel_id=1, source_target_pairs={{0,8},{1,9},{2,10},{3,11},{4,12},{5,13},{6,14},{7,15},{8,0},{9,1},... | collective-permute-start | bytes 196616 | tf_op jit(solution)/shard_map/ppermute | solution.py:56
  139.0 6.5 %collective-permute-start.28 = (bf16[64,512]{1,0:T(8,128)(2,1)S(1)}, bf16[64,512]{1,0:T(8,128)(2,1)S(1)}, u32[]{:S(2)}, u32[]{:S(2)}) collective-permute-start(bf16[64,512]{1,0:T(8,128)(2,1)S(1)} %get-tuple-element.69), channel_id=1, source_target_pairs={{0,4},{1,5},{2,6},{3,7},{4,0},{5,1},{6,2},{7,3},{8,12},{9,13},{10,... | collective-permute-start | bytes 196616 | tf_op jit(solution)/shard_map/ppermute | solution.py:56

commit v17 on v16

--- a/solution.py
+++ b/solution.py
@@ -377,7 +377,7 @@
                 jnp.concatenate(unpacked, axis=0),
                 (((1,), (1,)), ((), ())),
                 preferred_element_type=jnp.float32,
-            ) * (HEAD_DIM**-0.5)
+            )
             if masks:
                 scores = jnp.where(mask_refs[0][...] == mask_refs[1][...], scores, -1e30)
             top = jnp.max(scores, axis=0, keepdims=True)
@@ -395,7 +395,7 @@
         lax.fori_loop(0, kv_heads, one_head, 0)
         for copy in before:
             copy.wait()
-        total = sum(early_held[i] for i in range(len(early)))
+        total = sum(early_held[i].astype(jnp.float32) for i in range(len(early)))
         for i, group in enumerate(groups):
             for copy in group:
                 copy.wait()
@@ -437,7 +437,7 @@
             jax.ShapeDtypeStruct((held.step_count, held.columns), jnp.float32),
         ],
         scratch_shapes=[
-            pltpu.VMEM((len(early), held.height, held.columns), jnp.float32),
+            pltpu.VMEM((len(early), held.height, held.columns), jnp.bfloat16),
             pltpu.VMEM((kv_heads, tokens, count), jnp.bfloat16),
             pltpu.VMEM((tokens, held.columns), jnp.bfloat16),
             pltpu.SemaphoreType.DMA((len(early),)),
@@ -571,7 +571,9 @@
         axis=1,
     )
     positions = (slots % PROMPT_PAGES * PAGE)[:, None] + jnp.arange(PAGE, dtype=jnp.int32)[None, :]
-    cosine, sine_part = rope_tables(positions.reshape(chip_rows))
+    scaled_tables = tuple(
+        table * HEAD_DIM ** (-0.5) for table in rope_tables(positions.reshape(chip_rows))
+    )
 
     step_place = PROMPT_PAGES * PAGE + jnp.arange(2, dtype=jnp.int32)
     step_tables = tuple(t[:, None, :] for t in rope_tables(step_place))
@@ -580,7 +582,7 @@
         for sign, table in zip((1, -1), step_tables)
     ]
     queries = project_queries(
-        after(wide_states, (cosine, sine_part)), query_weight, *flat_tables
+        after(wide_states, scaled_tables), query_weight, *flat_tables
     )
     packed_queries = jnp.concatenate(
         jnp.split(queries, half // queries.shape[1], axis=0), axis=1
@@ -589,9 +591,8 @@
 
     places = [(k, flip) for k in range(deep) for flip in (0, 1)]
     parts_of = [
-        tuple(range(0, 2 * deep, 2)),
-        tuple(range(1, 2 * deep - 4, 2)),
-        tuple(range(2 * deep - 3, 2 * deep, 2)),
+        (*range(0, 2 * deep, 2), 1),
+        tuple(range(3, 2 * deep, 2)),
     ]
     taken_blocks = {
         which: jnp.stack([block(behind(places[i][0]), places[i][1], own_c) for i in which])
@@ -644,11 +645,10 @@
         )
 
     value_early = project_blocks(
-        value_pieces, parts_of[0], None, (theirs_x[1], theirs[deep - 1]), jnp.float32
+        value_pieces, parts_of[0], None, (theirs_x[1], theirs[deep - 1]), jnp.bfloat16
     )
     awaited = (value_early, [theirs_x[k] for k in range(1, deep)])
     key_sum = project_blocks(key_pieces, range(2 * deep), None, awaited, jnp.bfloat16)
-    value_next = project_blocks(value_pieces, parts_of[1], None, key_sum, jnp.float32)
     key_back = in_chip(key_sum)
 
     def own_head(sums):
@@ -664,9 +664,9 @@
         row_prompt = jnp.tile(sample_order // group_size, devices // KV_HEADS * rows // samples)
         masks = [token_prompt[:, None], row_prompt[None, :]]
     kept, sent, step_values = attend(
-        kv_places, query_turns, ring_queries, key_sum, key_back, cosine, sine_part, masks,
-        prompt_states, got, wide_states, taken_blocks[parts_of[2]], width,
-        [value_pieces[i] for i in parts_of[2]], [value_early, value_next],
+        kv_places, query_turns, ring_queries, key_sum, key_back, *scaled_tables, masks,
+        prompt_states, got, wide_states, taken_blocks[parts_of[1]], width,
+        [value_pieces[i] for i in parts_of[1]], [value_early],
     )
     new_values = own_head(step_values) + own_head(in_chip(step_values))
     new_values = new_values.astype(jnp.bfloat16).astype(jnp.float32).reshape(steps, HEAD_DIM)

time: 147 us -> 144 us (0.980)
  Pallas kernels: 39.7 us -> 34.7 us
  waiting for transfers between devices: 41 us -> 43.8 us
    pallas_call x3 -> x2, Pallas kernels: 21.5 us -> 16.5 us  [project(): pl.pallas_call(body, in_specs=[pl.BlockSpec(memory_space=pltpu.SMEM)] + [...]
    mul x0 -> x1, other arithmetic: none -> 3.11 us  [on_device(): table * HEAD_DIM ** (-0.5)]
    sin x1 -> x0, other arithmetic: 3.05 us -> none  [rope_tables(): return (jnp.cos(angles), jnp.sin(angles))]
    ppermute x31, waiting for transfers between devices: 41 us -> 43.8 us  [move(): return lax.ppermute(value, ('groups', 'sample'), pairs)]
    unnamed x54 -> x58, local copies, waits for them, and re-layouts: 3.42 us -> 3.66 us
  transfers between devices with their start and end apart: 31 -> 31, of which waited for: 14 -> 15; matrix products, arithmetic and copies ran while one was open for 12% -> 11% of each run, Pallas kernels for 12% -> 9%
where the time goes in v17:
time: 144 us; the launch traced here: 143 us
  waiting for transfers between devices  43.8 us (30%)
  starting transfers between devices  43 us (30%)
  Pallas kernels  34.7 us (24%)
  local copies, waits for them, and re-layouts  11.3 us (8%)
  other arithmetic  9.71 us (7%)
    ppermute x31, waiting for transfers between devices, move(): return lax.ppermute(value, ('groups', 'sample'), pairs)  43.8 us
    ppermute x31, starting transfers between devices, move(): return lax.ppermute(value, ('groups', 'sample'), pairs)  43 us
    pallas_call x2, Pallas kernels, project(): pl.pallas_call(body, in_specs=[pl.BlockSpec(memory_space=pltpu.SMEM)] + [...  16.5 us
    pallas_call x1, Pallas kernels, attend(): pl.pallas_call(body, in_specs=[pl.BlockSpec(memory_space=pltpu.SMEM)] * 3...  11.3 us
    pallas_call x1, Pallas kernels, project_queries(): pl.pallas_call(body, in_specs=[whole, pl.BlockSpec(memory_space=pltpu.HBM...  4.7 us
    unnamed x58, local copies, waits for them, and re-layouts  3.66 us
    mul x1, other arithmetic, on_device(): table * HEAD_DIM ** (-0.5)  3.11 us
  transfers between devices with their start and end apart: 31, of which 15 were waited for; matrix products, arithmetic and copies ran while one was open for 11% of the time, Pallas kernels for 9%

profile of v17, /device:TPU:0, one launch (start us, length us, event | category | flops | bytes accessed | tf_op | source)
XLA Modules:
  0.0 143.1 jit_solution(9572002330912527561)
XLA Ops:
  0.5 2.6 %collective-permute-start = (bf16[512,512]{1,0:T(8,128)(2,1)}, bf16[512,512]{1,0:T(8,128)(2,1)}, u32[]{:S(2)}, u32[]{:S(2)}) collective-permute-start(bf16[512,512]{1,0:T(8,128)(2,1)} %param.12), channel_id=1, source_target_pairs={{0,2},{1,3},{2,0},{3,1},{4,6},{5,7},{6,4},{7,5},{8,10},{9,11},{10,... | collective-permute-start | bytes 1572872 | tf_op jit(solution)/shard_map/ppermute | solution.py:56
  3.0 1.1 fusion.7
  4.4 2.6 %collective-permute-start.2 = (bf16[1024,256]{1,0:T(8,128)(2,1)S(1)}, bf16[1024,256]{1,0:T(8,128)(2,1)S(1)}, u32[]{:S(2)}, u32[]{:S(2)}) collective-permute-start(bf16[1024,256]{1,0:T(8,128)(2,1)S(1)} %get-tuple-element.59.refs_0_), channel_id=1, source_target_pairs={{0,8},{1,9},{2,10},{3,11},{4,0},{5,1},{6,2},{7,3},{8,12},{9,13},{1... | collective-permute-start | bytes 1572872 | tf_op jit(solution)/shard_map/ppermute | solution.py:56
  7.4 3.1 %fusion.1 = (f32[1024,64]{1,0:T(8,128)}, f32[1024,64]{1,0:T(8,128)}) fusion(f32[64]{0:T(128)S(1)} %multiply_power_fusion, f32[1024]{0:T(1024)S(1)} %convert_bitcast_fusion), kind=kLoop, calls=%fused_computation.5 | loop fusion | flops 196608 | bytes 528640 | tf_op jit(solution)/shard_map/mul | solution.py:575
  10.7 0.6 broadcast_in_dim.21
  11.3 0.6 broadcast_in_dim.36
  11.9 4.7 %shard_map.73.refs_4_ = bf16[64,256]{1,0:T(8,128)(2,1)} custom-call(bf16[64,8192]{1,0:T(8,128)(2,1)} %bitcast.42, bf16[8192,256]{1,0:T(8,128)(2,1)} %weight_ref.1, f32[64,128]{1,0:T(8,128)} %bitcast.47, f32[64,128]{1,0:T(8,128)} %bitcast.48), custom_call_target="tpu_custom_call" | custom-call | flops 1 | bytes 1 | tf_op jit(solution)/shard_map/pallas_call | solution.py:106
  16.7 0.8 pad_maximum_fusion.refs_0_
  17.5 1.0 collective-permute-done.2.refs_2_
  18.5 3.4 %collective-permute-start.3 = (bf16[1024,256]{1,0:T(8,128)(2,1)S(1)}, bf16[1024,256]{1,0:T(8,128)(2,1)S(1)}, u32[]{:S(2)}, u32[]{:S(2)}) collective-permute-start(bf16[1024,256]{1,0:T(8,128)(2,1)S(1)} %collective-permute-done.2.refs_2_), channel_id=1, source_target_pairs={{0,8},{1,9},{2,10},{3,11},{4,0},{5,1},{6,2},{7,3},{8,12},{9,13},{1... | collective-permute-start | bytes 1572872 | tf_op jit(solution)/shard_map/ppermute | solution.py:56
  21.9 1.5 %collective-permute-start.12 = (bf16[1024,256]{1,0:T(8,128)(2,1)S(1)}, bf16[1024,256]{1,0:T(8,128)(2,1)S(1)}, u32[]{:S(2)}, u32[]{:S(2)}) collective-permute-start(bf16[1024,256]{1,0:T(8,128)(2,1)S(1)} %collective-permute-done.2.refs_2_), channel_id=1, source_target_pairs={{0,16},{1,17},{2,18},{3,19},{4,20},{5,21},{6,22},{7,23},{8,24},{9,... | collective-permute-start | bytes 1572872 | tf_op jit(solution)/shard_map/ppermute | solution.py:56
  23.4 1.8 %broadcast_select_fusion.2 = (bf16[512,256]{1,0:T(8,128)(2,1)}, bf16[512,256]{1,0:T(8,128)(2,1)S(1)}) fusion(pred[]{:T(512)S(6)} %eq.29, bf16[512,512]{1,0:T(8,128)(2,1)} %collective-permute-done), kind=kLoop, calls=%fused_computation.15 | loop fusion | flops 262144 | bytes 1048577 | tf_op jit(solution)/shard_map/jit(_where)/select_n | solution.py:614
  25.2 0.5 collective-permute-start.1
  25.7 6.9 %collective-permute-done.3.refs_4_ = bf16[1024,256]{1,0:T(8,128)(2,1)S(1)} collective-permute-done((bf16[1024,256]{1,0:T(8,128)(2,1)S(1)}, bf16[1024,256]{1,0:T(8,128)(2,1)S(1)}, u32[]{:S(2)}, u32[]{:S(2)}) %collective-permute-start.3) | collective-permute-done | bytes 524320 | tf_op jit(solution)/shard_map/ppermute | solution.py:56
  32.6 3.4 %collective-permute-start.5 = (bf16[1024,256]{1,0:T(8,128)(2,1)S(1)}, bf16[1024,256]{1,0:T(8,128)(2,1)}, u32[]{:S(2)}, u32[]{:S(2)}) collective-permute-start(bf16[1024,256]{1,0:T(8,128)(2,1)S(1)} %collective-permute-done.3.refs_4_), channel_id=1, source_target_pairs={{0,8},{1,9},{2,10},{3,11},{4,0},{5,1},{6,2},{7,3},{8,12},{9,13},{1... | collective-permute-start | bytes 1572872 | tf_op jit(solution)/shard_map/ppermute | solution.py:56
  36.0 1.5 %collective-permute-start.9 = (bf16[1024,256]{1,0:T(8,128)(2,1)S(1)}, bf16[1024,256]{1,0:T(8,128)(2,1)}, u32[]{:S(2)}, u32[]{:S(2)}) collective-permute-start(bf16[1024,256]{1,0:T(8,128)(2,1)S(1)} %collective-permute-done.3.refs_4_), channel_id=1, source_target_pairs={{0,16},{1,17},{2,18},{3,19},{4,20},{5,21},{6,22},{7,23},{8,24},{9,... | collective-permute-start | bytes 1572872 | tf_op jit(solution)/shard_map/ppermute | solution.py:56
  37.5 0.8 copy-done.17
  38.5 0.5 collective-permute-start.16
  39.4 0.7 collective-permute-start.4
  40.1 0.6 pad_add_fusion.1.block_ref
  40.7 0.7 stack.138.block_ref
  41.4 0.7 stack.139.block_ref
  42.1 0.6 and_select_fusion.1
  42.7 5.6 %collective-permute-done.5.refs_6_ = bf16[1024,256]{1,0:T(8,128)(2,1)} collective-permute-done((bf16[1024,256]{1,0:T(8,128)(2,1)S(1)}, bf16[1024,256]{1,0:T(8,128)(2,1)}, u32[]{:S(2)}, u32[]{:S(2)}) %collective-permute-start.5) | collective-permute-done | bytes 524320 | tf_op jit(solution)/shard_map/ppermute | solution.py:56
  48.4 1.5 %collective-permute-start.13 = (bf16[1024,256]{1,0:T(8,128)(2,1)}, bf16[1024,256]{1,0:T(8,128)(2,1)S(1)}, u32[]{:S(2)}, u32[]{:S(2)}) collective-permute-start(bf16[1024,256]{1,0:T(8,128)(2,1)} %collective-permute-done.5.refs_6_), channel_id=1, source_target_pairs={{0,16},{1,17},{2,18},{3,19},{4,20},{5,21},{6,22},{7,23},{8,24},{9,... | collective-permute-start | bytes 1572872 | tf_op jit(solution)/shard_map/ppermute | solution.py:56
  49.9 1.0 slice.133
  50.9 0.6 collective-permute-start.17
  51.5 1.3 collective-permute-done.4.refs_1_.refs_10_
  52.8 3.4 %collective-permute-start.6 = (bf16[640,256]{1,0:T(8,128)(2,1)S(1)}, bf16[640,256]{1,0:T(8,128)(2,1)S(1)}, u32[]{:S(2)}, u32[]{:S(2)}) collective-permute-start(bf16[640,256]{1,0:T(8,128)(2,1)S(1)} %collective-permute-done.4.refs_1_.refs_10_), channel_id=1, source_target_pairs={{0,8},{1,9},{2,10},{3,11},{4,0},{5,1},{6,2},{7,3},{8,12},{9,13},{1... | collective-permute-start | bytes 983048 | tf_op jit(solution)/shard_map/ppermute | solution.py:56
  56.2 1.6 %collective-permute-start.10 = (bf16[512,256]{1,0:T(8,128)(2,1)S(1)}, bf16[512,256]{1,0:T(8,128)(2,1)S(1)}, u32[]{:S(2)}, u32[]{:S(2)}) collective-permute-start(bf16[512,256]{1,0:T(8,128)(2,1)S(1)} %slice.127), channel_id=1, source_target_pairs={{0,16},{1,17},{2,18},{3,19},{4,20},{5,21},{6,22},{7,23},{8,24},{9,... | collective-permute-start | bytes 786440 | tf_op jit(solution)/shard_map/ppermute | solution.py:56
  57.7 1.0 slice.134
  58.7 2.2 %collective-permute-done.6.refs_2_.refs_12_ = bf16[640,256]{1,0:T(8,128)(2,1)S(1)} collective-permute-done((bf16[640,256]{1,0:T(8,128)(2,1)S(1)}, bf16[640,256]{1,0:T(8,128)(2,1)S(1)}, u32[]{:S(2)}, u32[]{:S(2)}) %collective-permute-start.6) | collective-permute-done | bytes 327712 | tf_op jit(solution)/shard_map/ppermute | solution.py:56
  60.9 3.4 %collective-permute-start.7 = (bf16[640,256]{1,0:T(8,128)(2,1)S(1)}, bf16[640,256]{1,0:T(8,128)(2,1)S(1)}, u32[]{:S(2)}, u32[]{:S(2)}) collective-permute-start(bf16[640,256]{1,0:T(8,128)(2,1)S(1)} %collective-permute-done.6.refs_2_.refs_12_), channel_id=1, source_target_pairs={{0,8},{1,9},{2,10},{3,11},{4,0},{5,1},{6,2},{7,3},{8,12},{9,13},{1... | collective-permute-start | bytes 983048 | tf_op jit(solution)/shard_map/ppermute | solution.py:56
  64.4 0.6 collective-permute-start.18
  65.0 1.6 %collective-permute-start.14 = (bf16[512,256]{1,0:T(8,128)(2,1)S(1)}, bf16[512,256]{1,0:T(8,128)(2,1)S(1)}, u32[]{:S(2)}, u32[]{:S(2)}) collective-permute-start(bf16[512,256]{1,0:T(8,128)(2,1)S(1)} %slice.128), channel_id=1, source_target_pairs={{0,16},{1,17},{2,18},{3,19},{4,20},{5,21},{6,22},{7,23},{8,24},{9,... | collective-permute-start | bytes 786440 | tf_op jit(solution)/shard_map/ppermute | solution.py:56
  66.6 2.3 %collective-permute-done.7.refs_3_.refs_14_ = bf16[640,256]{1,0:T(8,128)(2,1)S(1)} collective-permute-done((bf16[640,256]{1,0:T(8,128)(2,1)S(1)}, bf16[640,256]{1,0:T(8,128)(2,1)S(1)}, u32[]{:S(2)}, u32[]{:S(2)}) %collective-permute-start.7) | collective-permute-done | bytes 327712 | tf_op jit(solution)/shard_map/ppermute | solution.py:56
  68.9 1.6 %collective-permute-start.15 = (bf16[512,256]{1,0:T(8,128)(2,1)S(1)}, bf16[512,256]{1,0:T(8,128)(2,1)S(1)}, u32[]{:S(2)}, u32[]{:S(2)}) collective-permute-start(bf16[512,256]{1,0:T(8,128)(2,1)S(1)} %slice.129), channel_id=1, source_target_pairs={{0,16},{1,17},{2,18},{3,19},{4,20},{5,21},{6,22},{7,23},{8,24},{9,... | collective-permute-start | bytes 786440 | tf_op jit(solution)/shard_map/ppermute | solution.py:56
  70.5 7.2 %shard_map.75.refs_9_ = bf16[1088,512]{1,0:T(8,128)(2,1)} custom-call(s32[5]{0:T(128)} %stack.139.block_ref, bf16[512,8192]{1,0:T(8,128)(2,1)} %refs_6_.1, bf16[512,8192]{1,0:T(8,128)(2,1)} %collective-permute-done.11.got_ref.refs_7_, bf16[64,8192]{1,0:T(8,128)(2,1)} %bitcast.43, bf16[1024,256]{1,0:T(8,128)(2,1)} %copy-done.9, bf16[1024,256]{1,0:T(8,128)(2,1)} %copy-done.10, ...), custom_call_target="tpu_custom_call" | custom-call | flops 1 | bytes 1 | tf_op jit(solution)/shard_map/pallas_call | solution.py:226
  77.8 0.8 copy-done.22
  78.6 9.3 %shard_map.76.refs_2_ = bf16[1088,512]{1,0:T(8,128)(2,1)} custom-call(s32[8]{0:T(128)} %stack.138.block_ref, bf16[512,8192]{1,0:T(8,128)(2,1)} %refs_6_.1, bf16[512,8192]{1,0:T(8,128)(2,1)} %collective-permute-done.11.got_ref.refs_7_, bf16[64,8192]{1,0:T(8,128)(2,1)} %bitcast.44, bf16[1088,256]{1,0:T(8,128)(2,1)} %copy-done.11, ...), custom_call_target="tpu_custom_call" | custom-call | flops 1 | bytes 1 | tf_op jit(solution)/shard_map/pallas_call | solution.py:226
  88.5 0.5 collective-permute-start.8
  89.1 2.0 %collective-permute-done.8.refs_1_ = bf16[4,128,256]{2,1,0:T(8,128)(2,1)S(1)} collective-permute-done((bf16[4,128,256]{2,1,0:T(8,128)(2,1)S(1)}, bf16[4,128,256]{2,1,0:T(8,128)(2,1)S(1)}, u32[]{:S(2)}, u32[]{:S(2)}) %collective-permute-start.8) | collective-permute-done | bytes 262176 | tf_op jit(solution)/shard_map/ppermute | solution.py:56
  91.1 0.7 copy-done.27
  91.8 11.3 %shard_map.77 = (bf16[4,2,144,128]{3,2,1,0:T(8,128)(2,1)}, bf16[4,2,144,128]{3,2,1,0:T(8,128)(2,1)}, f32[64,512]{1,0:T(8,128)}) custom-call(s32[4]{0:T(128)} %get-tuple-element.79.place_ref, s32[4]{0:T(128)} %get-tuple-element.80.turn_ref, s32[3]{0:T(128)} %pad_add_fusion.1.block_ref, bf16[4,128,256]{2,1,0:T(8,128)(2,1)} %copy-done.6, ...), custom_call_target="tpu_custom_call" | custom-call | flops 1 | bytes 1 | tf_op jit(solution)/shard_map/pallas_call | solution.py:424
  103.4 0.8 slice.136
  104.6 0.8 slice.137
  105.5 1.0 copy-done.8
  106.5 0.6 collective-permute-start.21
  107.3 5.2 %collective-permute-done.21.far_ref = bf16[4,144,128]{2,1,0:T(8,128)(2,1)S(1)} collective-permute-done((bf16[4,144,128]{2,1,0:T(8,128)(2,1)S(1)}, bf16[4,144,128]{2,1,0:T(8,128)(2,1)S(1)}, u32[]{:S(2)}, u32[]{:S(2)}) %collective-permute-start.21) | collective-permute-done | bytes 147488 | tf_op jit(solution)/shard_map/ppermute | solution.py:56
  112.6 2.4 %collective-permute-start.22 = (bf16[144,128]{1,0:T(8,128)(2,1)S(1)}, bf16[144,128]{1,0:T(8,128)(2,1)S(1)}, u32[]{:S(2)}, u32[]{:S(2)}) collective-permute-start(bf16[144,128]{1,0:T(8,128)(2,1)S(1)} %get-tuple-element.55), channel_id=1, source_target_pairs={{0,4},{1,5},{2,6},{3,7},{4,0},{5,1},{6,2},{7,3},{8,12},{9,13},{10,... | collective-permute-start | bytes 110600 | tf_op jit(solution)/shard_map/ppermute | solution.py:56
  115.0 1.2 collective-permute-start.23
  116.2 1.4 collective-permute-start.24
  117.6 0.8 fusion.2.refs_6_
  118.4 2.3 %collective-permute-done.23.refs_2_ = bf16[144,128]{1,0:T(8,128)(2,1)S(1)} collective-permute-done((bf16[144,128]{1,0:T(8,128)(2,1)S(1)}, bf16[144,128]{1,0:T(8,128)(2,1)S(1)}, u32[]{:S(2)}, u32[]{:S(2)}) %collective-permute-start.23) | collective-permute-done | bytes 36896 | tf_op jit(solution)/shard_map/ppermute | solution.py:56
  120.7 1.3 collective-permute-done.24.refs_3_
  121.9 1.7 %shard_map.80 = bf16[64,8192]{1,0:T(8,128)(2,1)S(1)} custom-call(s32[16]{0:T(128)S(1)} %stack.123.block_ref, bf16[144,128]{1,0:T(8,128)(2,1)S(1)} %get-tuple-element.54.refs_0_, bf16[144,128]{1,0:T(8,128)(2,1)S(1)} %collective-permute-done.22.refs_1_, bf16[144,128]{1,0:T(8,128)(2,1)S(1)} %collective-permute-done.23.refs_2_, ...), custom_call_target="tpu_custom_call" | custom-call | flops 1 | bytes 1 | tf_op jit(solution)/shard_map/pallas_call | solution.py:265
  123.8 1.9 %collective-permute-done.26 = bf16[64,4096]{1,0:T(8,128)(2,1)S(1)} collective-permute-done((bf16[64,4096]{1,0:T(8,128)(2,1)S(1)}, bf16[64,4096]{1,0:T(8,128)(2,1)S(1)}, u32[]{:S(2)}, u32[]{:S(2)}) %collective-permute-start.26) | collective-permute-done | bytes 524320 | tf_op jit(solution)/shard_map/ppermute | solution.py:56
  125.8 0.5 collective-permute-start.27
  126.3 7.9 %collective-permute-done.27 = bf16[64,2048]{1,0:T(8,128)(2,1)S(1)} collective-permute-done((bf16[64,2048]{1,0:T(8,128)(2,1)S(1)}, bf16[64,2048]{1,0:T(8,128)(2,1)S(1)}, u32[]{:S(2)}, u32[]{:S(2)}) %collective-permute-start.27) | collective-permute-done | bytes 262176 | tf_op jit(solution)/shard_map/ppermute | solution.py:56
  134.3 1.5 %collective-permute-start.30 = (bf16[64,512]{1,0:T(8,128)(2,1)S(1)}, bf16[64,512]{1,0:T(8,128)(2,1)S(1)}, u32[]{:S(2)}, u32[]{:S(2)}) collective-permute-start(bf16[64,512]{1,0:T(8,128)(2,1)S(1)} %get-tuple-element.68), channel_id=1, source_target_pairs={{0,12},{1,13},{2,14},{3,15},{4,8},{5,9},{6,10},{7,11},{8,4},{9,5},... | collective-permute-start | bytes 196616 | tf_op jit(solution)/shard_map/ppermute | solution.py:56
  136.0 2.8 %collective-permute-start.28 = (bf16[64,512]{1,0:T(8,128)(2,1)S(1)}, bf16[64,512]{1,0:T(8,128)(2,1)S(1)}, u32[]{:S(2)}, u32[]{:S(2)}) collective-permute-start(bf16[64,512]{1,0:T(8,128)(2,1)S(1)} %get-tuple-element.67), channel_id=1, source_target_pairs={{0,4},{1,5},{2,6},{3,7},{4,0},{5,1},{6,2},{7,3},{8,12},{9,13},{10,... | collective-permute-start | bytes 196616 | tf_op jit(solution)/shard_map/ppermute | solution.py:56
  138.8 2.2 %collective-permute-done.30 = bf16[64,512]{1,0:T(8,128)(2,1)S(1)} collective-permute-done((bf16[64,512]{1,0:T(8,128)(2,1)S(1)}, bf16[64,512]{1,0:T(8,128)(2,1)S(1)}, u32[]{:S(2)}, u32[]{:S(2)}) %collective-permute-start.30) | collective-permute-done | bytes 65568 | tf_op jit(solution)/shard_map/ppermute | solution.py:56
  141.0 1.4 %collective-permute-done.29 = bf16[64,512]{1,0:T(8,128)(2,1)S(1)} collective-permute-done((bf16[64,512]{1,0:T(8,128)(2,1)S(1)}, bf16[64,512]{1,0:T(8,128)(2,1)S(1)}, u32[]{:S(2)}, u32[]{:S(2)}) %collective-permute-start.29) | collective-permute-done | bytes 65568 | tf_op jit(solution)/shard_map/ppermute | solution.py:56
  142.5 0.7 add_convert_fusion.2
  (115 shorter events, 4.3 us)
Async XLA Ops:
  0.0 4.1 %copy-start.23 = (bf16[512,512]{1,0:T(8,128)(2,1)S(1)}, bf16[512,512]{1,0:T(8,128)(2,1)}, u32[]{:S(2)}) copy-start(bf16[512,512]{1,0:T(8,128)(2,1)} %param.11) | copy-start | bytes 1572868
  0.0 70.5 %collective-permute-start.11 = (bf16[512,8192]{1,0:T(8,128)(2,1)}, bf16[512,8192]{1,0:T(8,128)(2,1)}, u32[]{:S(2)}, u32[]{:S(2)}) collective-permute-start(bf16[512,8192]{1,0:T(8,128)(2,1)} %refs_6_.1), channel_id=1, source_target_pairs={{0,1},{1,0},{2,3},{3,2},{4,5},{5,4},{6,7},{7,6},{8,9},{9,8},{10,11... | collective-permute-start | bytes 25165832 | tf_op jit(solution)/shard_map/ppermute | solution.py:56
  0.5 23.0 %collective-permute-start = (bf16[512,512]{1,0:T(8,128)(2,1)}, bf16[512,512]{1,0:T(8,128)(2,1)}, u32[]{:S(2)}, u32[]{:S(2)}) collective-permute-start(bf16[512,512]{1,0:T(8,128)(2,1)} %param.12), channel_id=1, source_target_pairs={{0,2},{1,3},{2,0},{3,1},{4,6},{5,7},{6,4},{7,5},{8,10},{9,11},{10,... | collective-permute-start | bytes 1572872 | tf_op jit(solution)/shard_map/ppermute | solution.py:56
  4.2 3.0 %copy-start.28 = (s32[64]{0:T(128)S(1)}, s32[64]{0:T(128)}, u32[]{:S(2)}) copy-start(s32[64]{0:T(128)} %param.9) | copy-start | bytes 772
  4.4 12.3 %copy-start.9 = (bf16[1024,256]{1,0:T(8,128)(2,1)}, bf16[1024,256]{1,0:T(8,128)(2,1)S(1)}, u32[]{:S(2)}) copy-start(bf16[1024,256]{1,0:T(8,128)(2,1)S(1)} %get-tuple-element.59.refs_0_) | copy-start | bytes 1572868
  4.4 12.3 %copy-start.10 = (bf16[1024,256]{1,0:T(8,128)(2,1)}, bf16[1024,256]{1,0:T(8,128)(2,1)S(1)}, u32[]{:S(2)}) copy-start(bf16[1024,256]{1,0:T(8,128)(2,1)S(1)} %get-tuple-element.60.refs_1_) | copy-start | bytes 1572868
  4.4 14.2 %collective-permute-start.2 = (bf16[1024,256]{1,0:T(8,128)(2,1)S(1)}, bf16[1024,256]{1,0:T(8,128)(2,1)S(1)}, u32[]{:S(2)}, u32[]{:S(2)}) collective-permute-start(bf16[1024,256]{1,0:T(8,128)(2,1)S(1)} %get-tuple-element.59.refs_0_), channel_id=1, source_target_pairs={{0,8},{1,9},{2,10},{3,11},{4,0},{5,1},{6,2},{7,3},{8,12},{9,13},{1... | collective-permute-start | bytes 1572872 | tf_op jit(solution)/shard_map/ppermute | solution.py:56
  17.5 20.8 %copy-start.11 = (bf16[1088,256]{1,0:T(8,128)(2,1)}, bf16[1088,256]{1,0:T(8,128)(2,1)S(1)}, u32[]{:S(2)}) copy-start(bf16[1088,256]{1,0:T(8,128)(2,1)S(1)} %pad_maximum_fusion.refs_0_) | copy-start | bytes 1671172
  18.5 19.8 %copy-start.15 = (bf16[1024,256]{1,0:T(8,128)(2,1)}, bf16[1024,256]{1,0:T(8,128)(2,1)S(1)}, u32[]{:S(2)}) copy-start(bf16[1024,256]{1,0:T(8,128)(2,1)S(1)} %collective-permute-done.2.refs_2_) | copy-start | bytes 1572868
  18.5 14.1 %collective-permute-start.3 = (bf16[1024,256]{1,0:T(8,128)(2,1)S(1)}, bf16[1024,256]{1,0:T(8,128)(2,1)S(1)}, u32[]{:S(2)}, u32[]{:S(2)}) collective-permute-start(bf16[1024,256]{1,0:T(8,128)(2,1)S(1)} %collective-permute-done.2.refs_2_), channel_id=1, source_target_pairs={{0,8},{1,9},{2,10},{3,11},{4,0},{5,1},{6,2},{7,3},{8,12},{9,13},{1... | collective-permute-start | bytes 1572872 | tf_op jit(solution)/shard_map/ppermute | solution.py:56
  21.9 15.6 %collective-permute-start.12 = (bf16[1024,256]{1,0:T(8,128)(2,1)S(1)}, bf16[1024,256]{1,0:T(8,128)(2,1)S(1)}, u32[]{:S(2)}, u32[]{:S(2)}) collective-permute-start(bf16[1024,256]{1,0:T(8,128)(2,1)S(1)} %collective-permute-done.2.refs_2_), channel_id=1, source_target_pairs={{0,16},{1,17},{2,18},{3,19},{4,20},{5,21},{6,22},{7,23},{8,24},{9,... | collective-permute-start | bytes 1572872 | tf_op jit(solution)/shard_map/ppermute | solution.py:56
  25.2 14.2 %copy-start.7 = (bf16[64,256]{1,0:T(8,128)(2,1)S(1)}, bf16[64,256]{1,0:T(8,128)(2,1)}, u32[]{:S(2)}) copy-start(bf16[64,256]{1,0:T(8,128)(2,1)} %shard_map.73.refs_4_) | copy-start | bytes 98308
  25.2 13.3 %collective-permute-start.1 = (bf16[1088,256]{1,0:T(8,128)(2,1)S(1)}, bf16[1088,256]{1,0:T(8,128)(2,1)S(1)}, u32[]{:S(2)}, u32[]{:S(2)}) collective-permute-start(bf16[1088,256]{1,0:T(8,128)(2,1)S(1)} %pad_maximum_fusion.refs_0_), channel_id=1, source_target_pairs={{0,2},{1,3},{2,0},{3,1},{4,6},{5,7},{6,4},{7,5},{8,10},{9,11},{10,... | collective-permute-start | bytes 1671176 | tf_op jit(solution)/shard_map/ppermute | solution.py:56
  32.6 10.1 %copy-start.16 = (bf16[1024,256]{1,0:T(8,128)(2,1)}, bf16[1024,256]{1,0:T(8,128)(2,1)S(1)}, u32[]{:S(2)}) copy-start(bf16[1024,256]{1,0:T(8,128)(2,1)S(1)} %collective-permute-done.3.refs_4_) | copy-start | bytes 1572868
  32.6 15.8 %collective-permute-start.5 = (bf16[1024,256]{1,0:T(8,128)(2,1)S(1)}, bf16[1024,256]{1,0:T(8,128)(2,1)}, u32[]{:S(2)}, u32[]{:S(2)}) collective-permute-start(bf16[1024,256]{1,0:T(8,128)(2,1)S(1)} %collective-permute-done.3.refs_4_), channel_id=1, source_target_pairs={{0,8},{1,9},{2,10},{3,11},{4,0},{5,1},{6,2},{7,3},{8,12},{9,13},{1... | collective-permute-start | bytes 1572872 | tf_op jit(solution)/shard_map/ppermute | solution.py:56
  36.0 13.9 %collective-permute-start.9 = (bf16[1024,256]{1,0:T(8,128)(2,1)S(1)}, bf16[1024,256]{1,0:T(8,128)(2,1)}, u32[]{:S(2)}, u32[]{:S(2)}) collective-permute-start(bf16[1024,256]{1,0:T(8,128)(2,1)S(1)} %collective-permute-done.3.refs_4_), channel_id=1, source_target_pairs={{0,16},{1,17},{2,18},{3,19},{4,20},{5,21},{6,22},{7,23},{8,24},{9,... | collective-permute-start | bytes 1572872 | tf_op jit(solution)/shard_map/ppermute | solution.py:56
  37.5 0.8 copy-start.17
  38.4 12.5 %copy-start.12 = (bf16[1024,256]{1,0:T(8,128)(2,1)}, bf16[1024,256]{1,0:T(8,128)(2,1)S(1)}, u32[]{:S(2)}) copy-start(bf16[1024,256]{1,0:T(8,128)(2,1)S(1)} %pad_maximum_fusion.3.refs_2_) | copy-start | bytes 1572868
  38.5 0.8 copy-start.19
  38.5 12.4 %collective-permute-start.16 = (bf16[1024,256]{1,0:T(8,128)(2,1)S(1)}, bf16[1024,256]{1,0:T(8,128)(2,1)S(1)}, u32[]{:S(2)}, u32[]{:S(2)}) collective-permute-start(bf16[1024,256]{1,0:T(8,128)(2,1)S(1)} %pad_maximum_fusion.3.refs_2_), channel_id=1, source_target_pairs={{0,2},{1,3},{2,0},{3,1},{4,6},{5,7},{6,4},{7,5},{8,10},{9,11},{10,... | collective-permute-start | bytes 1572872 | tf_op jit(solution)/shard_map/ppermute | solution.py:56
  39.4 11.5 %copy-start.1 = (bf16[640,256]{1,0:T(8,128)(2,1)}, bf16[640,256]{1,0:T(8,128)(2,1)S(1)}, u32[]{:S(2)}) copy-start(bf16[640,256]{1,0:T(8,128)(2,1)S(1)} %pad_maximum_fusion.6.refs_0_.refs_8_) | copy-start | bytes 983044
  39.4 13.4 %collective-permute-start.4 = (bf16[640,256]{1,0:T(8,128)(2,1)S(1)}, bf16[640,256]{1,0:T(8,128)(2,1)S(1)}, u32[]{:S(2)}, u32[]{:S(2)}) collective-permute-start(bf16[640,256]{1,0:T(8,128)(2,1)S(1)} %pad_maximum_fusion.6.refs_0_.refs_8_), channel_id=1, source_target_pairs={{0,8},{1,9},{2,10},{3,11},{4,0},{5,1},{6,2},{7,3},{8,12},{9,13},{1... | collective-permute-start | bytes 983048 | tf_op jit(solution)/shard_map/ppermute | solution.py:56
  48.4 15.9 %collective-permute-start.13 = (bf16[1024,256]{1,0:T(8,128)(2,1)}, bf16[1024,256]{1,0:T(8,128)(2,1)S(1)}, u32[]{:S(2)}, u32[]{:S(2)}) collective-permute-start(bf16[1024,256]{1,0:T(8,128)(2,1)} %collective-permute-done.5.refs_6_), channel_id=1, source_target_pairs={{0,16},{1,17},{2,18},{3,19},{4,20},{5,21},{6,22},{7,23},{8,24},{9,... | collective-permute-start | bytes 1572872 | tf_op jit(solution)/shard_map/ppermute | solution.py:56
  50.9 13.5 %copy-start.13 = (bf16[1024,256]{1,0:T(8,128)(2,1)}, bf16[1024,256]{1,0:T(8,128)(2,1)S(1)}, u32[]{:S(2)}) copy-start(bf16[1024,256]{1,0:T(8,128)(2,1)S(1)} %pad_maximum_fusion.4.refs_4_) | copy-start | bytes 1572868
  50.9 13.5 %copy-start.20 = (bf16[1024,256]{1,0:T(8,128)(2,1)}, bf16[1024,256]{1,0:T(8,128)(2,1)S(1)}, u32[]{:S(2)}) copy-start(bf16[1024,256]{1,0:T(8,128)(2,1)S(1)} %collective-permute-done.16.refs_3_) | copy-start | bytes 1572868
  50.9 13.5 %collective-permute-start.17 = (bf16[1024,256]{1,0:T(8,128)(2,1)S(1)}, bf16[1024,256]{1,0:T(8,128)(2,1)S(1)}, u32[]{:S(2)}, u32[]{:S(2)}) collective-permute-start(bf16[1024,256]{1,0:T(8,128)(2,1)S(1)} %pad_maximum_fusion.4.refs_4_), channel_id=1, source_target_pairs={{0,2},{1,3},{2,0},{3,1},{4,6},{5,7},{6,4},{7,5},{8,10},{9,11},{10,... | collective-permute-start | bytes 1572872 | tf_op jit(solution)/shard_map/ppermute | solution.py:56
  52.8 35.2 %copy-start.3 = (bf16[640,256]{1,0:T(8,128)(2,1)}, bf16[640,256]{1,0:T(8,128)(2,1)S(1)}, u32[]{:S(2)}) copy-start(bf16[640,256]{1,0:T(8,128)(2,1)S(1)} %collective-permute-done.4.refs_1_.refs_10_) | copy-start | bytes 983044
  52.8 8.1 %collective-permute-start.6 = (bf16[640,256]{1,0:T(8,128)(2,1)S(1)}, bf16[640,256]{1,0:T(8,128)(2,1)S(1)}, u32[]{:S(2)}, u32[]{:S(2)}) collective-permute-start(bf16[640,256]{1,0:T(8,128)(2,1)S(1)} %collective-permute-done.4.refs_1_.refs_10_), channel_id=1, source_target_pairs={{0,8},{1,9},{2,10},{3,11},{4,0},{5,1},{6,2},{7,3},{8,12},{9,13},{1... | collective-permute-start | bytes 983048 | tf_op jit(solution)/shard_map/ppermute | solution.py:56
  56.2 12.7 %collective-permute-start.10 = (bf16[512,256]{1,0:T(8,128)(2,1)S(1)}, bf16[512,256]{1,0:T(8,128)(2,1)S(1)}, u32[]{:S(2)}, u32[]{:S(2)}) collective-permute-start(bf16[512,256]{1,0:T(8,128)(2,1)S(1)} %slice.127), channel_id=1, source_target_pairs={{0,16},{1,17},{2,18},{3,19},{4,20},{5,21},{6,22},{7,23},{8,24},{9,... | collective-permute-start | bytes 786440 | tf_op jit(solution)/shard_map/ppermute | solution.py:56
  60.9 27.1 %copy-start.4 = (bf16[640,256]{1,0:T(8,128)(2,1)}, bf16[640,256]{1,0:T(8,128)(2,1)S(1)}, u32[]{:S(2)}) copy-start(bf16[640,256]{1,0:T(8,128)(2,1)S(1)} %collective-permute-done.6.refs_2_.refs_12_) | copy-start | bytes 983044
  60.9 8.0 %collective-permute-start.7 = (bf16[640,256]{1,0:T(8,128)(2,1)S(1)}, bf16[640,256]{1,0:T(8,128)(2,1)S(1)}, u32[]{:S(2)}, u32[]{:S(2)}) collective-permute-start(bf16[640,256]{1,0:T(8,128)(2,1)S(1)} %collective-permute-done.6.refs_2_.refs_12_), channel_id=1, source_target_pairs={{0,8},{1,9},{2,10},{3,11},{4,0},{5,1},{6,2},{7,3},{8,12},{9,13},{1... | collective-permute-start | bytes 983048 | tf_op jit(solution)/shard_map/ppermute | solution.py:56
  64.3 4.6 %copy-start.18 = (bf16[1024,256]{1,0:T(8,128)(2,1)}, bf16[1024,256]{1,0:T(8,128)(2,1)S(1)}, u32[]{:S(2)}) copy-start(bf16[1024,256]{1,0:T(8,128)(2,1)S(1)} %collective-permute-done.13.refs_7_) | copy-start | bytes 1572868
  64.4 13.3 %copy-start.14 = (bf16[1024,256]{1,0:T(8,128)(2,1)}, bf16[1024,256]{1,0:T(8,128)(2,1)S(1)}, u32[]{:S(2)}) copy-start(bf16[1024,256]{1,0:T(8,128)(2,1)S(1)} %pad_maximum_fusion.5.refs_6_) | copy-start | bytes 1572868
  64.4 13.3 %copy-start.21 = (bf16[1024,256]{1,0:T(8,128)(2,1)}, bf16[1024,256]{1,0:T(8,128)(2,1)S(1)}, u32[]{:S(2)}) copy-start(bf16[1024,256]{1,0:T(8,128)(2,1)S(1)} %collective-permute-done.17.refs_5_) | copy-start | bytes 1572868
  64.4 13.3 %collective-permute-start.18 = (bf16[1024,256]{1,0:T(8,128)(2,1)S(1)}, bf16[1024,256]{1,0:T(8,128)(2,1)S(1)}, u32[]{:S(2)}, u32[]{:S(2)}) collective-permute-start(bf16[1024,256]{1,0:T(8,128)(2,1)S(1)} %pad_maximum_fusion.5.refs_6_), channel_id=1, source_target_pairs={{0,2},{1,3},{2,0},{3,1},{4,6},{5,7},{6,4},{7,5},{8,10},{9,11},{10,... | collective-permute-start | bytes 1572872 | tf_op jit(solution)/shard_map/ppermute | solution.py:56
  65.0 12.7 %collective-permute-start.14 = (bf16[512,256]{1,0:T(8,128)(2,1)S(1)}, bf16[512,256]{1,0:T(8,128)(2,1)S(1)}, u32[]{:S(2)}, u32[]{:S(2)}) collective-permute-start(bf16[512,256]{1,0:T(8,128)(2,1)S(1)} %slice.128), channel_id=1, source_target_pairs={{0,16},{1,17},{2,18},{3,19},{4,20},{5,21},{6,22},{7,23},{8,24},{9,... | collective-permute-start | bytes 786440 | tf_op jit(solution)/shard_map/ppermute | solution.py:56
  68.9 19.2 %copy-start.5 = (bf16[640,256]{1,0:T(8,128)(2,1)}, bf16[640,256]{1,0:T(8,128)(2,1)S(1)}, u32[]{:S(2)}) copy-start(bf16[640,256]{1,0:T(8,128)(2,1)S(1)} %collective-permute-done.7.refs_3_.refs_14_) | copy-start | bytes 983044
  68.9 8.8 %copy-start.24 = (bf16[512,256]{1,0:T(8,128)(2,1)}, bf16[512,256]{1,0:T(8,128)(2,1)S(1)}, u32[]{:S(2)}) copy-start(bf16[512,256]{1,0:T(8,128)(2,1)S(1)} %collective-permute-done.10.refs_11_) | copy-start | bytes 786436
  68.9 8.8 %collective-permute-start.15 = (bf16[512,256]{1,0:T(8,128)(2,1)S(1)}, bf16[512,256]{1,0:T(8,128)(2,1)S(1)}, u32[]{:S(2)}, u32[]{:S(2)}) collective-permute-start(bf16[512,256]{1,0:T(8,128)(2,1)S(1)} %slice.129), channel_id=1, source_target_pairs={{0,16},{1,17},{2,18},{3,19},{4,20},{5,21},{6,22},{7,23},{8,24},{9,... | collective-permute-start | bytes 786440 | tf_op jit(solution)/shard_map/ppermute | solution.py:56
  77.7 10.4 %copy-start.2 = (bf16[640,256]{1,0:T(8,128)(2,1)S(1)}, bf16[640,256]{1,0:T(8,128)(2,1)}, u32[]{:S(2)}) copy-start(bf16[640,256]{1,0:T(8,128)(2,1)} %copy-done.1) | copy-start | bytes 983044
  77.7 10.2 %copy-start.25 = (bf16[512,256]{1,0:T(8,128)(2,1)}, bf16[512,256]{1,0:T(8,128)(2,1)S(1)}, u32[]{:S(2)}) copy-start(bf16[512,256]{1,0:T(8,128)(2,1)S(1)} %collective-permute-done.14.refs_13_) | copy-start | bytes 786436
  77.7 10.2 %copy-start.26 = (bf16[512,256]{1,0:T(8,128)(2,1)}, bf16[512,256]{1,0:T(8,128)(2,1)S(1)}, u32[]{:S(2)}) copy-start(bf16[512,256]{1,0:T(8,128)(2,1)S(1)} %collective-permute-done.15.refs_15_) | copy-start | bytes 786436
  77.8 0.8 copy-start.22
  87.9 3.2 %collective-permute-start.19 = (bf16[1088,512]{1,0:T(8,128)(2,1)}, bf16[1088,512]{1,0:T(8,128)(2,1)}, u32[]{:S(2)}, u32[]{:S(2)}) collective-permute-start(bf16[1088,512]{1,0:T(8,128)(2,1)} %shard_map.76.refs_2_), channel_id=1, source_target_pairs={{0,1},{1,0},{2,3},{3,2},{4,5},{5,4},{6,7},{7,6},{8,9},{9,8},{10,11... | collective-permute-start | bytes 3342344 | tf_op jit(solution)/shard_map/ppermute | solution.py:56
  88.4 2.7 %copy-start.6 = (bf16[4,128,256]{2,1,0:T(8,128)(2,1)}, bf16[4,128,256]{2,1,0:T(8,128)(2,1)S(1)}, u32[]{:S(2)}) copy-start(bf16[4,128,256]{2,1,0:T(8,128)(2,1)S(1)} %shard_map.74.refs_0_) | copy-start | bytes 786436
  88.5 2.7 %collective-permute-start.8 = (bf16[4,128,256]{2,1,0:T(8,128)(2,1)S(1)}, bf16[4,128,256]{2,1,0:T(8,128)(2,1)S(1)}, u32[]{:S(2)}, u32[]{:S(2)}) collective-permute-start(bf16[4,128,256]{2,1,0:T(8,128)(2,1)S(1)} %shard_map.74.refs_0_), channel_id=1, source_target_pairs={{0,1},{1,0},{2,3},{3,2},{4,5},{5,4},{6,7},{7,6},{8,9},{9,8},{10,11... | collective-permute-start | bytes 786440 | tf_op jit(solution)/shard_map/ppermute | solution.py:56
  91.1 0.7 copy-start.27
  91.8 30.1 %copy-start = (bf16[256,8192]{1,0:T(8,128)(2,1)S(1)}, bf16[256,8192]{1,0:T(8,128)(2,1)}, u32[]{:S(2)}) copy-start(bf16[256,8192]{1,0:T(8,128)(2,1)} %refs_7_.1) | copy-start | bytes 12582916
  103.1 2.4 %collective-permute-start.20 = (bf16[4,2,144,128]{3,2,1,0:T(8,128)(2,1)}, bf16[4,2,144,128]{3,2,1,0:T(8,128)(2,1)S(1)}, u32[]{:S(2)}, u32[]{:S(2)}) collective-permute-start(bf16[4,2,144,128]{3,2,1,0:T(8,128)(2,1)} %get-tuple-element.51), channel_id=1, source_target_pairs={{0,1},{1,0},{2,3},{3,2},{4,5},{5,4},{6,7},{7,6},{8,9},{9,8},{10,11... | collective-permute-start | bytes 884744 | tf_op jit(solution)/shard_map/ppermute | solution.py:56
  104.3 13.3 %collective-permute-start.25 = (f32[64,512]{1,0:T(8,128)}, f32[64,512]{1,0:T(8,128)S(1)}, u32[]{:S(2)}, u32[]{:S(2)}) collective-permute-start(f32[64,512]{1,0:T(8,128)} %get-tuple-element.58), channel_id=1, source_target_pairs={{0,1},{1,0},{2,3},{3,2},{4,5},{5,4},{6,7},{7,6},{8,9},{9,8},{10,11... | collective-permute-start | bytes 393224 | tf_op jit(solution)/shard_map/ppermute | solution.py:56
  105.5 1.0 copy-start.8
  106.5 6.0 %collective-permute-start.21 = (bf16[4,144,128]{2,1,0:T(8,128)(2,1)S(1)}, bf16[4,144,128]{2,1,0:T(8,128)(2,1)S(1)}, u32[]{:S(2)}, u32[]{:S(2)}) collective-permute-start(bf16[4,144,128]{2,1,0:T(8,128)(2,1)S(1)} %get-tuple-element.53), channel_id=1, source_target_pairs={{0,2},{1,3},{2,0},{3,1},{4,6},{5,7},{6,4},{7,5},{8,10},{9,11},{10,... | collective-permute-start | bytes 442376 | tf_op jit(solution)/shard_map/ppermute | solution.py:56
  112.6 5.8 %collective-permute-start.22 = (bf16[144,128]{1,0:T(8,128)(2,1)S(1)}, bf16[144,128]{1,0:T(8,128)(2,1)S(1)}, u32[]{:S(2)}, u32[]{:S(2)}) collective-permute-start(bf16[144,128]{1,0:T(8,128)(2,1)S(1)} %get-tuple-element.55), channel_id=1, source_target_pairs={{0,4},{1,5},{2,6},{3,7},{4,0},{5,1},{6,2},{7,3},{8,12},{9,13},{10,... | collective-permute-start | bytes 110600 | tf_op jit(solution)/shard_map/ppermute | solution.py:56
  115.0 5.6 %collective-permute-start.23 = (bf16[144,128]{1,0:T(8,128)(2,1)S(1)}, bf16[144,128]{1,0:T(8,128)(2,1)S(1)}, u32[]{:S(2)}, u32[]{:S(2)}) collective-permute-start(bf16[144,128]{1,0:T(8,128)(2,1)S(1)} %get-tuple-element.56), channel_id=1, source_target_pairs={{0,8},{1,9},{2,10},{3,11},{4,12},{5,13},{6,14},{7,15},{8,0},{9,1},... | collective-permute-start | bytes 110600 | tf_op jit(solution)/shard_map/ppermute | solution.py:56
  116.2 5.8 %collective-permute-start.24 = (bf16[144,128]{1,0:T(8,128)(2,1)S(1)}, bf16[144,128]{1,0:T(8,128)(2,1)S(1)}, u32[]{:S(2)}, u32[]{:S(2)}) collective-permute-start(bf16[144,128]{1,0:T(8,128)(2,1)S(1)} %get-tuple-element.57), channel_id=1, source_target_pairs={{0,12},{1,13},{2,14},{3,15},{4,8},{5,9},{6,10},{7,11},{8,4},{9,5},... | collective-permute-start | bytes 110600 | tf_op jit(solution)/shard_map/ppermute | solution.py:56
  123.7 2.0 %collective-permute-start.26 = (bf16[64,4096]{1,0:T(8,128)(2,1)S(1)}, bf16[64,4096]{1,0:T(8,128)(2,1)S(1)}, u32[]{:S(2)}, u32[]{:S(2)}) collective-permute-start(bf16[64,4096]{1,0:T(8,128)(2,1)S(1)} %slice.141), channel_id=1, source_target_pairs={{0,1},{1,0},{2,3},{3,2},{4,5},{5,4},{6,7},{7,6},{8,9},{9,8},{10,11... | collective-permute-start | bytes 1572872 | tf_op jit(solution)/shard_map/ppermute | solution.py:56
  125.8 8.4 %collective-permute-start.27 = (bf16[64,2048]{1,0:T(8,128)(2,1)S(1)}, bf16[64,2048]{1,0:T(8,128)(2,1)S(1)}, u32[]{:S(2)}, u32[]{:S(2)}) collective-permute-start(bf16[64,2048]{1,0:T(8,128)(2,1)S(1)} %slice.143), channel_id=1, source_target_pairs={{0,2},{1,3},{2,0},{3,1},{4,6},{5,7},{6,4},{7,5},{8,10},{9,11},{10,... | collective-permute-start | bytes 786440 | tf_op jit(solution)/shard_map/ppermute | solution.py:56
  134.3 6.7 %collective-permute-start.30 = (bf16[64,512]{1,0:T(8,128)(2,1)S(1)}, bf16[64,512]{1,0:T(8,128)(2,1)S(1)}, u32[]{:S(2)}, u32[]{:S(2)}) collective-permute-start(bf16[64,512]{1,0:T(8,128)(2,1)S(1)} %get-tuple-element.68), channel_id=1, source_target_pairs={{0,12},{1,13},{2,14},{3,15},{4,8},{5,9},{6,10},{7,11},{8,4},{9,5},... | collective-permute-start | bytes 196616 | tf_op jit(solution)/shard_map/ppermute | solution.py:56
  135.8 6.7 %collective-permute-start.29 = (bf16[64,512]{1,0:T(8,128)(2,1)S(1)}, bf16[64,512]{1,0:T(8,128)(2,1)S(1)}, u32[]{:S(2)}, u32[]{:S(2)}) collective-permute-start(bf16[64,512]{1,0:T(8,128)(2,1)S(1)} %get-tuple-element.69), channel_id=1, source_target_pairs={{0,8},{1,9},{2,10},{3,11},{4,12},{5,13},{6,14},{7,15},{8,0},{9,1},... | collective-permute-start | bytes 196616 | tf_op jit(solution)/shard_map/ppermute | solution.py:56
  136.0 6.5 %collective-permute-start.28 = (bf16[64,512]{1,0:T(8,128)(2,1)S(1)}, bf16[64,512]{1,0:T(8,128)(2,1)S(1)}, u32[]{:S(2)}, u32[]{:S(2)}) collective-permute-start(bf16[64,512]{1,0:T(8,128)(2,1)S(1)} %get-tuple-element.67), channel_id=1, source_target_pairs={{0,4},{1,5},{2,6},{3,7},{4,0},{5,1},{6,2},{7,3},{8,12},{9,13},{10,... | collective-permute-start | bytes 196616 | tf_op jit(solution)/shard_map/ppermute | solution.py:56

commit v18 on v17

--- a/solution.py
+++ b/solution.py
@@ -97,9 +97,16 @@
                 preferred_element_type=jnp.float32,
             )
             total = product if total is None else total + product
+        tables = [
+            jnp.concatenate(
+                [jnp.broadcast_to(ref[i : i + 1, :], (count // 2, HEAD_DIM)) for i in (0, 1)],
+                axis=0,
+            )
+            for ref in (cosine_ref, sine_ref)
+        ]
         for start in range(0, weight.shape[1], HEAD_DIM):
             head = total[:, start : start + HEAD_DIM]
-            turned = head * cosine_ref[...] + pltpu.roll(head, HEAD_DIM // 2, 1) * sine_ref[...]
+            turned = head * tables[0] + pltpu.roll(head, HEAD_DIM // 2, 1) * tables[1]
             out_ref[:, start : start + HEAD_DIM] = turned.astype(jnp.bfloat16)
 
     whole = pl.BlockSpec(memory_space=pltpu.VMEM)
@@ -578,7 +585,7 @@
     step_place = PROMPT_PAGES * PAGE + jnp.arange(2, dtype=jnp.int32)
     step_tables = tuple(t[:, None, :] for t in rope_tables(step_place))
     flat_tables = [
-        jnp.repeat(jnp.concatenate([sign * table, table], axis=-1)[:, 0], samples, axis=0)
+        jnp.concatenate([sign * table, table], axis=-1)[:, 0]
         for sign, table in zip((1, -1), step_tables)
     ]
     queries = project_queries(
@@ -609,7 +616,7 @@
 
     got = in_chip(prompt_states)
     both_z, both_x, theirs, theirs_x = {0: both_mine}, {0: both_other}, {}, {}
-    value_y = send(along_y, value_weight)
+    value_y = send(along_y, after(value_weight, both_mine))
     both_z[1] = send(along_ring, both_mine)
     theirs_x[0] = jnp.where(first, value_y[:, half:], value_y[:, :half])
     value_y = jnp.where(first, value_y[:, :half], value_y[:, half:])

time: 144 us -> 144 us (level)
  starting transfers between devices: 43 us -> 49.1 us
  waiting for transfers between devices: 43.8 us -> 38.5 us
  local copies, waits for them, and re-layouts: 11.3 us -> 9.85 us
    ppermute x31, starting transfers between devices: 43 us -> 49.1 us  [move(): return lax.ppermute(value, ('groups', 'sample'), pairs)]
    ppermute x31, waiting for transfers between devices: 43.8 us -> 38.5 us  [move(): return lax.ppermute(value, ('groups', 'sample'), pairs)]
    unnamed x58 -> x56, local copies, waits for them, and re-layouts: 3.66 us -> 3.36 us
where the time goes in v18:
time: 144 us; the launch traced here: 143 us
  starting transfers between devices  49.1 us (34%)
  waiting for transfers between devices  38.5 us (27%)
  Pallas kernels  34.7 us (24%)
  other arithmetic  10.3 us (7%)
  local copies, waits for them, and re-layouts  9.85 us (7%)
    ppermute x31, starting transfers between devices, move(): return lax.ppermute(value, ('groups', 'sample'), pairs)  49.1 us
    ppermute x31, waiting for transfers between devices, move(): return lax.ppermute(value, ('groups', 'sample'), pairs)  38.5 us
    pallas_call x2, Pallas kernels, project(): pl.pallas_call(body, in_specs=[pl.BlockSpec(memory_space=pltpu.SMEM)] + [...  16.5 us
    pallas_call x1, Pallas kernels, attend(): pl.pallas_call(body, in_specs=[pl.BlockSpec(memory_space=pltpu.SMEM)] * 3...  11.3 us
    pallas_call x1, Pallas kernels, project_queries(): pl.pallas_call(body, in_specs=[whole, pl.BlockSpec(memory_space=pltpu.HBM...  4.7 us
    unnamed x56, local copies, waits for them, and re-layouts  3.36 us
    mul x1, other arithmetic, on_device(): table * HEAD_DIM ** (-0.5)  3.11 us
  transfers between devices with their start and end apart: 31, of which 15 were waited for; matrix products, arithmetic and copies ran while one was open for 11% of the time, Pallas kernels for 9%

profile of v18, /device:TPU:0, one launch (start us, length us, event | category | flops | bytes accessed | tf_op | source)
XLA Modules:
  0.0 143.0 jit_solution(17113029975994467353)
XLA Ops:
  0.0 0.5 collective-permute-start.11
  0.5 1.3 fusion.6
  1.9 3.6 %collective-permute-start.2 = (bf16[1024,256]{1,0:T(8,128)(2,1)S(1)}, bf16[1024,256]{1,0:T(8,128)(2,1)S(1)}, u32[]{:S(2)}, u32[]{:S(2)}) collective-permute-start(bf16[1024,256]{1,0:T(8,128)(2,1)S(1)} %get-tuple-element.61.refs_0_), channel_id=1, source_target_pairs={{0,8},{1,9},{2,10},{3,11},{4,0},{5,1},{6,2},{7,3},{8,12},{9,13},{1... | collective-permute-start | bytes 1572872 | tf_op jit(solution)/shard_map/ppermute | solution.py:56
  5.6 1.5 %collective-permute-start = (bf16[512,512]{1,0:T(8,128)(2,1)}, bf16[512,512]{1,0:T(8,128)(2,1)}, u32[]{:S(2)}, u32[]{:S(2)}) collective-permute-start(bf16[512,512]{1,0:T(8,128)(2,1)} %param.12), channel_id=1, source_target_pairs={{0,2},{1,3},{2,0},{3,1},{4,6},{5,7},{6,4},{7,5},{8,10},{9,11},{10,... | collective-permute-start | bytes 1572872 | tf_op jit(solution)/shard_map/ppermute | solution.py:56
  7.5 3.1 %fusion.1 = (f32[1024,64]{1,0:T(8,128)}, f32[1024,64]{1,0:T(8,128)}) fusion(f32[64]{0:T(128)S(1)} %multiply_power_fusion, f32[1024]{0:T(1024)S(1)} %convert_bitcast_fusion), kind=kLoop, calls=%fused_computation.5 | loop fusion | flops 196608 | bytes 528640 | tf_op jit(solution)/shard_map/mul | solution.py:582
  10.7 0.7 maximum_bitcast_fusion
  11.4 4.7 %shard_map.73.refs_4_ = bf16[64,256]{1,0:T(8,128)(2,1)} custom-call(bf16[64,8192]{1,0:T(8,128)(2,1)} %bitcast.40, bf16[8192,256]{1,0:T(8,128)(2,1)} %weight_ref.1, f32[2,128]{1,0:T(2,128)} %get-tuple-element.85.cosine_ref, f32[2,128]{1,0:T(2,128)} %get-tuple-element.86.sine_ref), custom_call_target="tpu_custom_call" | custom-call | flops 1 | bytes 1 | tf_op jit(solution)/shard_map/pallas_call | solution.py:113
  16.1 0.8 pad_maximum_fusion.refs_0_
  17.0 0.5 collective-permute-done.2.refs_2_
  17.4 3.4 %collective-permute-start.3 = (bf16[1024,256]{1,0:T(8,128)(2,1)S(1)}, bf16[1024,256]{1,0:T(8,128)(2,1)S(1)}, u32[]{:S(2)}, u32[]{:S(2)}) collective-permute-start(bf16[1024,256]{1,0:T(8,128)(2,1)S(1)} %collective-permute-done.2.refs_2_), channel_id=1, source_target_pairs={{0,8},{1,9},{2,10},{3,11},{4,0},{5,1},{6,2},{7,3},{8,12},{9,13},{1... | collective-permute-start | bytes 1572872 | tf_op jit(solution)/shard_map/ppermute | solution.py:56
  20.8 1.5 %collective-permute-start.12 = (bf16[1024,256]{1,0:T(8,128)(2,1)S(1)}, bf16[1024,256]{1,0:T(8,128)(2,1)S(1)}, u32[]{:S(2)}, u32[]{:S(2)}) collective-permute-start(bf16[1024,256]{1,0:T(8,128)(2,1)S(1)} %collective-permute-done.2.refs_2_), channel_id=1, source_target_pairs={{0,16},{1,17},{2,18},{3,19},{4,20},{5,21},{6,22},{7,23},{8,24},{9,... | collective-permute-start | bytes 1572872 | tf_op jit(solution)/shard_map/ppermute | solution.py:56
  22.3 1.8 %broadcast_select_fusion.2 = (bf16[512,256]{1,0:T(8,128)(2,1)}, bf16[512,256]{1,0:T(8,128)(2,1)S(1)}) fusion(pred[]{:T(512)S(6)} %eq.29, bf16[512,512]{1,0:T(8,128)(2,1)} %collective-permute-done), kind=kLoop, calls=%fused_computation.15 | loop fusion | flops 262144 | bytes 1048577 | tf_op jit(solution)/shard_map/jit(_where)/select_n | solution.py:621
  24.1 1.5 %collective-permute-start.1 = (bf16[1088,256]{1,0:T(8,128)(2,1)S(1)}, bf16[1088,256]{1,0:T(8,128)(2,1)S(1)}, u32[]{:S(2)}, u32[]{:S(2)}) collective-permute-start(bf16[1088,256]{1,0:T(8,128)(2,1)S(1)} %pad_maximum_fusion.refs_0_), channel_id=1, source_target_pairs={{0,2},{1,3},{2,0},{3,1},{4,6},{5,7},{6,4},{7,5},{8,10},{9,11},{10,... | collective-permute-start | bytes 1671176 | tf_op jit(solution)/shard_map/ppermute | solution.py:56
  25.6 6.3 %collective-permute-done.3.refs_4_ = bf16[1024,256]{1,0:T(8,128)(2,1)S(1)} collective-permute-done((bf16[1024,256]{1,0:T(8,128)(2,1)S(1)}, bf16[1024,256]{1,0:T(8,128)(2,1)S(1)}, u32[]{:S(2)}, u32[]{:S(2)}) %collective-permute-start.3) | collective-permute-done | bytes 524320 | tf_op jit(solution)/shard_map/ppermute | solution.py:56
  31.9 3.4 %collective-permute-start.5 = (bf16[1024,256]{1,0:T(8,128)(2,1)S(1)}, bf16[1024,256]{1,0:T(8,128)(2,1)}, u32[]{:S(2)}, u32[]{:S(2)}) collective-permute-start(bf16[1024,256]{1,0:T(8,128)(2,1)S(1)} %collective-permute-done.3.refs_4_), channel_id=1, source_target_pairs={{0,8},{1,9},{2,10},{3,11},{4,0},{5,1},{6,2},{7,3},{8,12},{9,13},{1... | collective-permute-start | bytes 1572872 | tf_op jit(solution)/shard_map/ppermute | solution.py:56
  35.3 1.5 %collective-permute-start.9 = (bf16[1024,256]{1,0:T(8,128)(2,1)S(1)}, bf16[1024,256]{1,0:T(8,128)(2,1)}, u32[]{:S(2)}, u32[]{:S(2)}) collective-permute-start(bf16[1024,256]{1,0:T(8,128)(2,1)S(1)} %collective-permute-done.3.refs_4_), channel_id=1, source_target_pairs={{0,16},{1,17},{2,18},{3,19},{4,20},{5,21},{6,22},{7,23},{8,24},{9,... | collective-permute-start | bytes 1572872 | tf_op jit(solution)/shard_map/ppermute | solution.py:56
  36.8 0.8 copy-done.17
  37.8 1.5 %collective-permute-start.16 = (bf16[1024,256]{1,0:T(8,128)(2,1)S(1)}, bf16[1024,256]{1,0:T(8,128)(2,1)S(1)}, u32[]{:S(2)}, u32[]{:S(2)}) collective-permute-start(bf16[1024,256]{1,0:T(8,128)(2,1)S(1)} %pad_maximum_fusion.3.refs_2_), channel_id=1, source_target_pairs={{0,2},{1,3},{2,0},{3,1},{4,6},{5,7},{6,4},{7,5},{8,10},{9,11},{10,... | collective-permute-start | bytes 1572872 | tf_op jit(solution)/shard_map/ppermute | solution.py:56
  39.4 0.8 collective-permute-start.4
  40.2 0.6 pad_add_fusion.1.block_ref
  40.8 0.6 stack.138.block_ref
  41.4 0.7 stack.139.block_ref
  42.1 0.7 and_select_fusion.1
  42.8 4.9 %collective-permute-done.5.refs_6_ = bf16[1024,256]{1,0:T(8,128)(2,1)} collective-permute-done((bf16[1024,256]{1,0:T(8,128)(2,1)S(1)}, bf16[1024,256]{1,0:T(8,128)(2,1)}, u32[]{:S(2)}, u32[]{:S(2)}) %collective-permute-start.5) | collective-permute-done | bytes 524320 | tf_op jit(solution)/shard_map/ppermute | solution.py:56
  47.7 1.5 %collective-permute-start.13 = (bf16[1024,256]{1,0:T(8,128)(2,1)}, bf16[1024,256]{1,0:T(8,128)(2,1)S(1)}, u32[]{:S(2)}, u32[]{:S(2)}) collective-permute-start(bf16[1024,256]{1,0:T(8,128)(2,1)} %collective-permute-done.5.refs_6_), channel_id=1, source_target_pairs={{0,16},{1,17},{2,18},{3,19},{4,20},{5,21},{6,22},{7,23},{8,24},{9,... | collective-permute-start | bytes 1572872 | tf_op jit(solution)/shard_map/ppermute | solution.py:56
  49.1 1.0 slice.133
  50.2 1.6 %collective-permute-start.17 = (bf16[1024,256]{1,0:T(8,128)(2,1)S(1)}, bf16[1024,256]{1,0:T(8,128)(2,1)S(1)}, u32[]{:S(2)}, u32[]{:S(2)}) collective-permute-start(bf16[1024,256]{1,0:T(8,128)(2,1)S(1)} %pad_maximum_fusion.4.refs_4_), channel_id=1, source_target_pairs={{0,2},{1,3},{2,0},{3,1},{4,6},{5,7},{6,4},{7,5},{8,10},{9,11},{10,... | collective-permute-start | bytes 1572872 | tf_op jit(solution)/shard_map/ppermute | solution.py:56
  51.8 0.7 collective-permute-done.4.refs_1_.refs_10_
  52.5 3.4 %collective-permute-start.6 = (bf16[640,256]{1,0:T(8,128)(2,1)S(1)}, bf16[640,256]{1,0:T(8,128)(2,1)S(1)}, u32[]{:S(2)}, u32[]{:S(2)}) collective-permute-start(bf16[640,256]{1,0:T(8,128)(2,1)S(1)} %collective-permute-done.4.refs_1_.refs_10_), channel_id=1, source_target_pairs={{0,8},{1,9},{2,10},{3,11},{4,0},{5,1},{6,2},{7,3},{8,12},{9,13},{1... | collective-permute-start | bytes 983048 | tf_op jit(solution)/shard_map/ppermute | solution.py:56
  55.9 1.6 %collective-permute-start.10 = (bf16[512,256]{1,0:T(8,128)(2,1)S(1)}, bf16[512,256]{1,0:T(8,128)(2,1)S(1)}, u32[]{:S(2)}, u32[]{:S(2)}) collective-permute-start(bf16[512,256]{1,0:T(8,128)(2,1)S(1)} %slice.127), channel_id=1, source_target_pairs={{0,16},{1,17},{2,18},{3,19},{4,20},{5,21},{6,22},{7,23},{8,24},{9,... | collective-permute-start | bytes 786440 | tf_op jit(solution)/shard_map/ppermute | solution.py:56
  57.4 1.0 slice.134
  58.4 2.5 %collective-permute-done.6.refs_2_.refs_12_ = bf16[640,256]{1,0:T(8,128)(2,1)S(1)} collective-permute-done((bf16[640,256]{1,0:T(8,128)(2,1)S(1)}, bf16[640,256]{1,0:T(8,128)(2,1)S(1)}, u32[]{:S(2)}, u32[]{:S(2)}) %collective-permute-start.6) | collective-permute-done | bytes 327712 | tf_op jit(solution)/shard_map/ppermute | solution.py:56
  60.9 3.4 %collective-permute-start.7 = (bf16[640,256]{1,0:T(8,128)(2,1)S(1)}, bf16[640,256]{1,0:T(8,128)(2,1)S(1)}, u32[]{:S(2)}, u32[]{:S(2)}) collective-permute-start(bf16[640,256]{1,0:T(8,128)(2,1)S(1)} %collective-permute-done.6.refs_2_.refs_12_), channel_id=1, source_target_pairs={{0,8},{1,9},{2,10},{3,11},{4,0},{5,1},{6,2},{7,3},{8,12},{9,13},{1... | collective-permute-start | bytes 983048 | tf_op jit(solution)/shard_map/ppermute | solution.py:56
  64.4 1.6 %collective-permute-start.18 = (bf16[1024,256]{1,0:T(8,128)(2,1)S(1)}, bf16[1024,256]{1,0:T(8,128)(2,1)S(1)}, u32[]{:S(2)}, u32[]{:S(2)}) collective-permute-start(bf16[1024,256]{1,0:T(8,128)(2,1)S(1)} %pad_maximum_fusion.5.refs_6_), channel_id=1, source_target_pairs={{0,2},{1,3},{2,0},{3,1},{4,6},{5,7},{6,4},{7,5},{8,10},{9,11},{10,... | collective-permute-start | bytes 1572872 | tf_op jit(solution)/shard_map/ppermute | solution.py:56
  66.0 1.6 %collective-permute-start.14 = (bf16[512,256]{1,0:T(8,128)(2,1)S(1)}, bf16[512,256]{1,0:T(8,128)(2,1)S(1)}, u32[]{:S(2)}, u32[]{:S(2)}) collective-permute-start(bf16[512,256]{1,0:T(8,128)(2,1)S(1)} %slice.128), channel_id=1, source_target_pairs={{0,16},{1,17},{2,18},{3,19},{4,20},{5,21},{6,22},{7,23},{8,24},{9,... | collective-permute-start | bytes 786440 | tf_op jit(solution)/shard_map/ppermute | solution.py:56
  67.6 1.3 collective-permute-done.7.refs_3_.refs_14_
  68.9 1.6 %collective-permute-start.15 = (bf16[512,256]{1,0:T(8,128)(2,1)S(1)}, bf16[512,256]{1,0:T(8,128)(2,1)S(1)}, u32[]{:S(2)}, u32[]{:S(2)}) collective-permute-start(bf16[512,256]{1,0:T(8,128)(2,1)S(1)} %slice.129), channel_id=1, source_target_pairs={{0,16},{1,17},{2,18},{3,19},{4,20},{5,21},{6,22},{7,23},{8,24},{9,... | collective-permute-start | bytes 786440 | tf_op jit(solution)/shard_map/ppermute | solution.py:56
  70.5 7.2 %shard_map.75.refs_9_ = bf16[1088,512]{1,0:T(8,128)(2,1)} custom-call(s32[5]{0:T(128)} %stack.139.block_ref, bf16[512,8192]{1,0:T(8,128)(2,1)} %refs_6_.1, bf16[512,8192]{1,0:T(8,128)(2,1)} %collective-permute-done.11.got_ref.refs_7_, bf16[64,8192]{1,0:T(8,128)(2,1)} %bitcast.41, bf16[1024,256]{1,0:T(8,128)(2,1)} %copy-done.9, bf16[1024,256]{1,0:T(8,128)(2,1)} %copy-done.10, ...), custom_call_target="tpu_custom_call" | custom-call | flops 1 | bytes 1 | tf_op jit(solution)/shard_map/pallas_call | solution.py:233
  77.8 0.8 copy-done.22
  78.6 9.3 %shard_map.76.refs_2_ = bf16[1088,512]{1,0:T(8,128)(2,1)} custom-call(s32[8]{0:T(128)} %stack.138.block_ref, bf16[512,8192]{1,0:T(8,128)(2,1)} %refs_6_.1, bf16[512,8192]{1,0:T(8,128)(2,1)} %collective-permute-done.11.got_ref.refs_7_, bf16[64,8192]{1,0:T(8,128)(2,1)} %bitcast.42, bf16[1088,256]{1,0:T(8,128)(2,1)} %copy-done.11, ...), custom_call_target="tpu_custom_call" | custom-call | flops 1 | bytes 1 | tf_op jit(solution)/shard_map/pallas_call | solution.py:233
  88.4 0.5 collective-permute-start.8
  89.1 2.0 %collective-permute-done.8.refs_1_ = bf16[4,128,256]{2,1,0:T(8,128)(2,1)S(1)} collective-permute-done((bf16[4,128,256]{2,1,0:T(8,128)(2,1)S(1)}, bf16[4,128,256]{2,1,0:T(8,128)(2,1)S(1)}, u32[]{:S(2)}, u32[]{:S(2)}) %collective-permute-start.8) | collective-permute-done | bytes 262176 | tf_op jit(solution)/shard_map/ppermute | solution.py:56
  91.1 0.7 copy-done.26
  91.8 11.3 %shard_map.77 = (bf16[4,2,144,128]{3,2,1,0:T(8,128)(2,1)}, bf16[4,2,144,128]{3,2,1,0:T(8,128)(2,1)}, f32[64,512]{1,0:T(8,128)}) custom-call(s32[4]{0:T(128)} %get-tuple-element.81.place_ref, s32[4]{0:T(128)} %get-tuple-element.82.turn_ref, s32[3]{0:T(128)} %pad_add_fusion.1.block_ref, bf16[4,128,256]{2,1,0:T(8,128)(2,1)} %copy-done.6, ...), custom_call_target="tpu_custom_call" | custom-call | flops 1 | bytes 1 | tf_op jit(solution)/shard_map/pallas_call | solution.py:431
  103.4 0.8 slice.136
  104.6 0.8 slice.137
  105.5 1.0 copy-done.8
  106.5 1.6 %collective-permute-start.21 = (bf16[4,144,128]{2,1,0:T(8,128)(2,1)S(1)}, bf16[4,144,128]{2,1,0:T(8,128)(2,1)S(1)}, u32[]{:S(2)}, u32[]{:S(2)}) collective-permute-start(bf16[4,144,128]{2,1,0:T(8,128)(2,1)S(1)} %get-tuple-element.55), channel_id=1, source_target_pairs={{0,2},{1,3},{2,0},{3,1},{4,6},{5,7},{6,4},{7,5},{8,10},{9,11},{10,... | collective-permute-start | bytes 442376 | tf_op jit(solution)/shard_map/ppermute | solution.py:56
  108.3 4.2 %collective-permute-done.21.far_ref = bf16[4,144,128]{2,1,0:T(8,128)(2,1)S(1)} collective-permute-done((bf16[4,144,128]{2,1,0:T(8,128)(2,1)S(1)}, bf16[4,144,128]{2,1,0:T(8,128)(2,1)S(1)}, u32[]{:S(2)}, u32[]{:S(2)}) %collective-permute-start.21) | collective-permute-done | bytes 147488 | tf_op jit(solution)/shard_map/ppermute | solution.py:56
  112.6 2.4 %collective-permute-start.22 = (bf16[144,128]{1,0:T(8,128)(2,1)S(1)}, bf16[144,128]{1,0:T(8,128)(2,1)S(1)}, u32[]{:S(2)}, u32[]{:S(2)}) collective-permute-start(bf16[144,128]{1,0:T(8,128)(2,1)S(1)} %get-tuple-element.57), channel_id=1, source_target_pairs={{0,4},{1,5},{2,6},{3,7},{4,0},{5,1},{6,2},{7,3},{8,12},{9,13},{10,... | collective-permute-start | bytes 110600 | tf_op jit(solution)/shard_map/ppermute | solution.py:56
  115.0 1.1 collective-permute-start.23
  116.1 1.4 collective-permute-start.24
  117.5 0.8 fusion.2.refs_6_
  118.3 2.3 %collective-permute-done.23.refs_2_ = bf16[144,128]{1,0:T(8,128)(2,1)S(1)} collective-permute-done((bf16[144,128]{1,0:T(8,128)(2,1)S(1)}, bf16[144,128]{1,0:T(8,128)(2,1)S(1)}, u32[]{:S(2)}, u32[]{:S(2)}) %collective-permute-start.23) | collective-permute-done | bytes 36896 | tf_op jit(solution)/shard_map/ppermute | solution.py:56
  120.6 1.3 collective-permute-done.24.refs_3_
  121.8 1.7 %shard_map.80 = bf16[64,8192]{1,0:T(8,128)(2,1)S(1)} custom-call(s32[16]{0:T(128)S(1)} %stack.123.block_ref, bf16[144,128]{1,0:T(8,128)(2,1)S(1)} %get-tuple-element.56.refs_0_, bf16[144,128]{1,0:T(8,128)(2,1)S(1)} %collective-permute-done.22.refs_1_, bf16[144,128]{1,0:T(8,128)(2,1)S(1)} %collective-permute-done.23.refs_2_, ...), custom_call_target="tpu_custom_call" | custom-call | flops 1 | bytes 1 | tf_op jit(solution)/shard_map/pallas_call | solution.py:272
  123.7 1.9 %collective-permute-done.26 = bf16[64,4096]{1,0:T(8,128)(2,1)S(1)} collective-permute-done((bf16[64,4096]{1,0:T(8,128)(2,1)S(1)}, bf16[64,4096]{1,0:T(8,128)(2,1)S(1)}, u32[]{:S(2)}, u32[]{:S(2)}) %collective-permute-start.26) | collective-permute-done | bytes 524320 | tf_op jit(solution)/shard_map/ppermute | solution.py:56
  125.7 1.6 %collective-permute-start.27 = (bf16[64,2048]{1,0:T(8,128)(2,1)S(1)}, bf16[64,2048]{1,0:T(8,128)(2,1)S(1)}, u32[]{:S(2)}, u32[]{:S(2)}) collective-permute-start(bf16[64,2048]{1,0:T(8,128)(2,1)S(1)} %slice.143), channel_id=1, source_target_pairs={{0,2},{1,3},{2,0},{3,1},{4,6},{5,7},{6,4},{7,5},{8,10},{9,11},{10,... | collective-permute-start | bytes 786440 | tf_op jit(solution)/shard_map/ppermute | solution.py:56
  127.3 6.8 %collective-permute-done.27 = bf16[64,2048]{1,0:T(8,128)(2,1)S(1)} collective-permute-done((bf16[64,2048]{1,0:T(8,128)(2,1)S(1)}, bf16[64,2048]{1,0:T(8,128)(2,1)S(1)}, u32[]{:S(2)}, u32[]{:S(2)}) %collective-permute-start.27) | collective-permute-done | bytes 262176 | tf_op jit(solution)/shard_map/ppermute | solution.py:56
  134.2 1.5 %collective-permute-start.30 = (bf16[64,512]{1,0:T(8,128)(2,1)S(1)}, bf16[64,512]{1,0:T(8,128)(2,1)S(1)}, u32[]{:S(2)}, u32[]{:S(2)}) collective-permute-start(bf16[64,512]{1,0:T(8,128)(2,1)S(1)} %get-tuple-element.70), channel_id=1, source_target_pairs={{0,12},{1,13},{2,14},{3,15},{4,8},{5,9},{6,10},{7,11},{8,4},{9,5},... | collective-permute-start | bytes 196616 | tf_op jit(solution)/shard_map/ppermute | solution.py:56
  135.9 2.8 %collective-permute-start.28 = (bf16[64,512]{1,0:T(8,128)(2,1)S(1)}, bf16[64,512]{1,0:T(8,128)(2,1)S(1)}, u32[]{:S(2)}, u32[]{:S(2)}) collective-permute-start(bf16[64,512]{1,0:T(8,128)(2,1)S(1)} %get-tuple-element.69), channel_id=1, source_target_pairs={{0,4},{1,5},{2,6},{3,7},{4,0},{5,1},{6,2},{7,3},{8,12},{9,13},{10,... | collective-permute-start | bytes 196616 | tf_op jit(solution)/shard_map/ppermute | solution.py:56
  138.7 2.2 %collective-permute-done.30 = bf16[64,512]{1,0:T(8,128)(2,1)S(1)} collective-permute-done((bf16[64,512]{1,0:T(8,128)(2,1)S(1)}, bf16[64,512]{1,0:T(8,128)(2,1)S(1)}, u32[]{:S(2)}, u32[]{:S(2)}) %collective-permute-start.30) | collective-permute-done | bytes 65568 | tf_op jit(solution)/shard_map/ppermute | solution.py:56
  140.9 1.4 %collective-permute-done.29 = bf16[64,512]{1,0:T(8,128)(2,1)S(1)} collective-permute-done((bf16[64,512]{1,0:T(8,128)(2,1)S(1)}, bf16[64,512]{1,0:T(8,128)(2,1)S(1)}, u32[]{:S(2)}, u32[]{:S(2)}) %collective-permute-start.29) | collective-permute-done | bytes 65568 | tf_op jit(solution)/shard_map/ppermute | solution.py:56
  142.4 0.7 add_convert_fusion.2
  (110 shorter events, 3.3 us)
Async XLA Ops:
  0.0 70.5 %collective-permute-start.11 = (bf16[512,8192]{1,0:T(8,128)(2,1)}, bf16[512,8192]{1,0:T(8,128)(2,1)}, u32[]{:S(2)}, u32[]{:S(2)}) collective-permute-start(bf16[512,8192]{1,0:T(8,128)(2,1)} %refs_6_.1), channel_id=1, source_target_pairs={{0,1},{1,0},{2,3},{3,2},{4,5},{5,4},{6,7},{7,6},{8,9},{9,8},{10,11... | collective-permute-start | bytes 25165832 | tf_op jit(solution)/shard_map/ppermute | solution.py:56
  1.7 5.5 %copy-start.27 = (s32[64]{0:T(128)S(1)}, s32[64]{0:T(128)}, u32[]{:S(2)}) copy-start(s32[64]{0:T(128)} %param.9) | copy-start | bytes 772
  1.9 14.2 %copy-start.9 = (bf16[1024,256]{1,0:T(8,128)(2,1)}, bf16[1024,256]{1,0:T(8,128)(2,1)S(1)}, u32[]{:S(2)}) copy-start(bf16[1024,256]{1,0:T(8,128)(2,1)S(1)} %get-tuple-element.61.refs_0_) | copy-start | bytes 1572868
  1.9 14.2 %copy-start.10 = (bf16[1024,256]{1,0:T(8,128)(2,1)}, bf16[1024,256]{1,0:T(8,128)(2,1)S(1)}, u32[]{:S(2)}) copy-start(bf16[1024,256]{1,0:T(8,128)(2,1)S(1)} %get-tuple-element.62.refs_1_) | copy-start | bytes 1572868
  1.9 15.5 %collective-permute-start.2 = (bf16[1024,256]{1,0:T(8,128)(2,1)S(1)}, bf16[1024,256]{1,0:T(8,128)(2,1)S(1)}, u32[]{:S(2)}, u32[]{:S(2)}) collective-permute-start(bf16[1024,256]{1,0:T(8,128)(2,1)S(1)} %get-tuple-element.61.refs_0_), channel_id=1, source_target_pairs={{0,8},{1,9},{2,10},{3,11},{4,0},{5,1},{6,2},{7,3},{8,12},{9,13},{1... | collective-permute-start | bytes 1572872 | tf_op jit(solution)/shard_map/ppermute | solution.py:56
  5.6 16.7 %collective-permute-start = (bf16[512,512]{1,0:T(8,128)(2,1)}, bf16[512,512]{1,0:T(8,128)(2,1)}, u32[]{:S(2)}, u32[]{:S(2)}) collective-permute-start(bf16[512,512]{1,0:T(8,128)(2,1)} %param.12), channel_id=1, source_target_pairs={{0,2},{1,3},{2,0},{3,1},{4,6},{5,7},{6,4},{7,5},{8,10},{9,11},{10,... | collective-permute-start | bytes 1572872 | tf_op jit(solution)/shard_map/ppermute | solution.py:56
  16.9 20.7 %copy-start.11 = (bf16[1088,256]{1,0:T(8,128)(2,1)}, bf16[1088,256]{1,0:T(8,128)(2,1)S(1)}, u32[]{:S(2)}) copy-start(bf16[1088,256]{1,0:T(8,128)(2,1)S(1)} %pad_maximum_fusion.refs_0_) | copy-start | bytes 1671172
  17.4 20.2 %copy-start.15 = (bf16[1024,256]{1,0:T(8,128)(2,1)}, bf16[1024,256]{1,0:T(8,128)(2,1)S(1)}, u32[]{:S(2)}) copy-start(bf16[1024,256]{1,0:T(8,128)(2,1)S(1)} %collective-permute-done.2.refs_2_) | copy-start | bytes 1572868
  17.4 14.5 %collective-permute-start.3 = (bf16[1024,256]{1,0:T(8,128)(2,1)S(1)}, bf16[1024,256]{1,0:T(8,128)(2,1)S(1)}, u32[]{:S(2)}, u32[]{:S(2)}) collective-permute-start(bf16[1024,256]{1,0:T(8,128)(2,1)S(1)} %collective-permute-done.2.refs_2_), channel_id=1, source_target_pairs={{0,8},{1,9},{2,10},{3,11},{4,0},{5,1},{6,2},{7,3},{8,12},{9,13},{1... | collective-permute-start | bytes 1572872 | tf_op jit(solution)/shard_map/ppermute | solution.py:56
  20.8 16.0 %collective-permute-start.12 = (bf16[1024,256]{1,0:T(8,128)(2,1)S(1)}, bf16[1024,256]{1,0:T(8,128)(2,1)S(1)}, u32[]{:S(2)}, u32[]{:S(2)}) collective-permute-start(bf16[1024,256]{1,0:T(8,128)(2,1)S(1)} %collective-permute-done.2.refs_2_), channel_id=1, source_target_pairs={{0,16},{1,17},{2,18},{3,19},{4,20},{5,21},{6,22},{7,23},{8,24},{9,... | collective-permute-start | bytes 1572872 | tf_op jit(solution)/shard_map/ppermute | solution.py:56
  24.1 15.2 %copy-start.7 = (bf16[64,256]{1,0:T(8,128)(2,1)S(1)}, bf16[64,256]{1,0:T(8,128)(2,1)}, u32[]{:S(2)}) copy-start(bf16[64,256]{1,0:T(8,128)(2,1)} %shard_map.73.refs_4_) | copy-start | bytes 98308
  24.1 13.7 %collective-permute-start.1 = (bf16[1088,256]{1,0:T(8,128)(2,1)S(1)}, bf16[1088,256]{1,0:T(8,128)(2,1)S(1)}, u32[]{:S(2)}, u32[]{:S(2)}) collective-permute-start(bf16[1088,256]{1,0:T(8,128)(2,1)S(1)} %pad_maximum_fusion.refs_0_), channel_id=1, source_target_pairs={{0,2},{1,3},{2,0},{3,1},{4,6},{5,7},{6,4},{7,5},{8,10},{9,11},{10,... | collective-permute-start | bytes 1671176 | tf_op jit(solution)/shard_map/ppermute | solution.py:56
  31.9 10.8 %copy-start.16 = (bf16[1024,256]{1,0:T(8,128)(2,1)}, bf16[1024,256]{1,0:T(8,128)(2,1)S(1)}, u32[]{:S(2)}) copy-start(bf16[1024,256]{1,0:T(8,128)(2,1)S(1)} %collective-permute-done.3.refs_4_) | copy-start | bytes 1572868
  31.9 15.8 %collective-permute-start.5 = (bf16[1024,256]{1,0:T(8,128)(2,1)S(1)}, bf16[1024,256]{1,0:T(8,128)(2,1)}, u32[]{:S(2)}, u32[]{:S(2)}) collective-permute-start(bf16[1024,256]{1,0:T(8,128)(2,1)S(1)} %collective-permute-done.3.refs_4_), channel_id=1, source_target_pairs={{0,8},{1,9},{2,10},{3,11},{4,0},{5,1},{6,2},{7,3},{8,12},{9,13},{1... | collective-permute-start | bytes 1572872 | tf_op jit(solution)/shard_map/ppermute | solution.py:56
  35.3 13.9 %collective-permute-start.9 = (bf16[1024,256]{1,0:T(8,128)(2,1)S(1)}, bf16[1024,256]{1,0:T(8,128)(2,1)}, u32[]{:S(2)}, u32[]{:S(2)}) collective-permute-start(bf16[1024,256]{1,0:T(8,128)(2,1)S(1)} %collective-permute-done.3.refs_4_), channel_id=1, source_target_pairs={{0,16},{1,17},{2,18},{3,19},{4,20},{5,21},{6,22},{7,23},{8,24},{9,... | collective-permute-start | bytes 1572872 | tf_op jit(solution)/shard_map/ppermute | solution.py:56
  36.8 0.8 copy-start.17
  37.7 12.5 %copy-start.12 = (bf16[1024,256]{1,0:T(8,128)(2,1)}, bf16[1024,256]{1,0:T(8,128)(2,1)S(1)}, u32[]{:S(2)}) copy-start(bf16[1024,256]{1,0:T(8,128)(2,1)S(1)} %pad_maximum_fusion.3.refs_2_) | copy-start | bytes 1572868
  37.8 1.5 %copy-start.19 = (bf16[1088,256]{1,0:T(8,128)(2,1)}, bf16[1088,256]{1,0:T(8,128)(2,1)S(1)}, u32[]{:S(2)}) copy-start(bf16[1088,256]{1,0:T(8,128)(2,1)S(1)} %collective-permute-done.1.refs_1_) | copy-start | bytes 1671172
  37.8 12.4 %collective-permute-start.16 = (bf16[1024,256]{1,0:T(8,128)(2,1)S(1)}, bf16[1024,256]{1,0:T(8,128)(2,1)S(1)}, u32[]{:S(2)}, u32[]{:S(2)}) collective-permute-start(bf16[1024,256]{1,0:T(8,128)(2,1)S(1)} %pad_maximum_fusion.3.refs_2_), channel_id=1, source_target_pairs={{0,2},{1,3},{2,0},{3,1},{4,6},{5,7},{6,4},{7,5},{8,10},{9,11},{10,... | collective-permute-start | bytes 1572872 | tf_op jit(solution)/shard_map/ppermute | solution.py:56
  39.4 10.8 %copy-start.1 = (bf16[640,256]{1,0:T(8,128)(2,1)}, bf16[640,256]{1,0:T(8,128)(2,1)S(1)}, u32[]{:S(2)}) copy-start(bf16[640,256]{1,0:T(8,128)(2,1)S(1)} %pad_maximum_fusion.6.refs_0_.refs_8_) | copy-start | bytes 983044
  39.4 13.1 %collective-permute-start.4 = (bf16[640,256]{1,0:T(8,128)(2,1)S(1)}, bf16[640,256]{1,0:T(8,128)(2,1)S(1)}, u32[]{:S(2)}, u32[]{:S(2)}) collective-permute-start(bf16[640,256]{1,0:T(8,128)(2,1)S(1)} %pad_maximum_fusion.6.refs_0_.refs_8_), channel_id=1, source_target_pairs={{0,8},{1,9},{2,10},{3,11},{4,0},{5,1},{6,2},{7,3},{8,12},{9,13},{1... | collective-permute-start | bytes 983048 | tf_op jit(solution)/shard_map/ppermute | solution.py:56
  47.7 16.6 %collective-permute-start.13 = (bf16[1024,256]{1,0:T(8,128)(2,1)}, bf16[1024,256]{1,0:T(8,128)(2,1)S(1)}, u32[]{:S(2)}, u32[]{:S(2)}) collective-permute-start(bf16[1024,256]{1,0:T(8,128)(2,1)} %collective-permute-done.5.refs_6_), channel_id=1, source_target_pairs={{0,16},{1,17},{2,18},{3,19},{4,20},{5,21},{6,22},{7,23},{8,24},{9,... | collective-permute-start | bytes 1572872 | tf_op jit(solution)/shard_map/ppermute | solution.py:56
  50.2 14.2 %copy-start.13 = (bf16[1024,256]{1,0:T(8,128)(2,1)}, bf16[1024,256]{1,0:T(8,128)(2,1)S(1)}, u32[]{:S(2)}) copy-start(bf16[1024,256]{1,0:T(8,128)(2,1)S(1)} %pad_maximum_fusion.4.refs_4_) | copy-start | bytes 1572868
  50.2 14.2 %copy-start.20 = (bf16[1024,256]{1,0:T(8,128)(2,1)}, bf16[1024,256]{1,0:T(8,128)(2,1)S(1)}, u32[]{:S(2)}) copy-start(bf16[1024,256]{1,0:T(8,128)(2,1)S(1)} %collective-permute-done.16.refs_3_) | copy-start | bytes 1572868
  50.2 14.2 %collective-permute-start.17 = (bf16[1024,256]{1,0:T(8,128)(2,1)S(1)}, bf16[1024,256]{1,0:T(8,128)(2,1)S(1)}, u32[]{:S(2)}, u32[]{:S(2)}) collective-permute-start(bf16[1024,256]{1,0:T(8,128)(2,1)S(1)} %pad_maximum_fusion.4.refs_4_), channel_id=1, source_target_pairs={{0,2},{1,3},{2,0},{3,1},{4,6},{5,7},{6,4},{7,5},{8,10},{9,11},{10,... | collective-permute-start | bytes 1572872 | tf_op jit(solution)/shard_map/ppermute | solution.py:56
  52.5 35.5 %copy-start.3 = (bf16[640,256]{1,0:T(8,128)(2,1)}, bf16[640,256]{1,0:T(8,128)(2,1)S(1)}, u32[]{:S(2)}) copy-start(bf16[640,256]{1,0:T(8,128)(2,1)S(1)} %collective-permute-done.4.refs_1_.refs_10_) | copy-start | bytes 983044
  52.5 8.4 %collective-permute-start.6 = (bf16[640,256]{1,0:T(8,128)(2,1)S(1)}, bf16[640,256]{1,0:T(8,128)(2,1)S(1)}, u32[]{:S(2)}, u32[]{:S(2)}) collective-permute-start(bf16[640,256]{1,0:T(8,128)(2,1)S(1)} %collective-permute-done.4.refs_1_.refs_10_), channel_id=1, source_target_pairs={{0,8},{1,9},{2,10},{3,11},{4,0},{5,1},{6,2},{7,3},{8,12},{9,13},{1... | collective-permute-start | bytes 983048 | tf_op jit(solution)/shard_map/ppermute | solution.py:56
  55.9 13.0 %collective-permute-start.10 = (bf16[512,256]{1,0:T(8,128)(2,1)S(1)}, bf16[512,256]{1,0:T(8,128)(2,1)S(1)}, u32[]{:S(2)}, u32[]{:S(2)}) collective-permute-start(bf16[512,256]{1,0:T(8,128)(2,1)S(1)} %slice.127), channel_id=1, source_target_pairs={{0,16},{1,17},{2,18},{3,19},{4,20},{5,21},{6,22},{7,23},{8,24},{9,... | collective-permute-start | bytes 786440 | tf_op jit(solution)/shard_map/ppermute | solution.py:56
  60.9 27.1 %copy-start.4 = (bf16[640,256]{1,0:T(8,128)(2,1)}, bf16[640,256]{1,0:T(8,128)(2,1)S(1)}, u32[]{:S(2)}) copy-start(bf16[640,256]{1,0:T(8,128)(2,1)S(1)} %collective-permute-done.6.refs_2_.refs_12_) | copy-start | bytes 983044
  60.9 8.0 %collective-permute-start.7 = (bf16[640,256]{1,0:T(8,128)(2,1)S(1)}, bf16[640,256]{1,0:T(8,128)(2,1)S(1)}, u32[]{:S(2)}, u32[]{:S(2)}) collective-permute-start(bf16[640,256]{1,0:T(8,128)(2,1)S(1)} %collective-permute-done.6.refs_2_.refs_12_), channel_id=1, source_target_pairs={{0,8},{1,9},{2,10},{3,11},{4,0},{5,1},{6,2},{7,3},{8,12},{9,13},{1... | collective-permute-start | bytes 983048 | tf_op jit(solution)/shard_map/ppermute | solution.py:56
  64.3 4.6 %copy-start.18 = (bf16[1024,256]{1,0:T(8,128)(2,1)}, bf16[1024,256]{1,0:T(8,128)(2,1)S(1)}, u32[]{:S(2)}) copy-start(bf16[1024,256]{1,0:T(8,128)(2,1)S(1)} %collective-permute-done.13.refs_7_) | copy-start | bytes 1572868
  64.4 13.3 %copy-start.14 = (bf16[1024,256]{1,0:T(8,128)(2,1)}, bf16[1024,256]{1,0:T(8,128)(2,1)S(1)}, u32[]{:S(2)}) copy-start(bf16[1024,256]{1,0:T(8,128)(2,1)S(1)} %pad_maximum_fusion.5.refs_6_) | copy-start | bytes 1572868
  64.4 13.3 %copy-start.21 = (bf16[1024,256]{1,0:T(8,128)(2,1)}, bf16[1024,256]{1,0:T(8,128)(2,1)S(1)}, u32[]{:S(2)}) copy-start(bf16[1024,256]{1,0:T(8,128)(2,1)S(1)} %collective-permute-done.17.refs_5_) | copy-start | bytes 1572868
  64.4 13.3 %collective-permute-start.18 = (bf16[1024,256]{1,0:T(8,128)(2,1)S(1)}, bf16[1024,256]{1,0:T(8,128)(2,1)S(1)}, u32[]{:S(2)}, u32[]{:S(2)}) collective-permute-start(bf16[1024,256]{1,0:T(8,128)(2,1)S(1)} %pad_maximum_fusion.5.refs_6_), channel_id=1, source_target_pairs={{0,2},{1,3},{2,0},{3,1},{4,6},{5,7},{6,4},{7,5},{8,10},{9,11},{10,... | collective-permute-start | bytes 1572872 | tf_op jit(solution)/shard_map/ppermute | solution.py:56
  66.0 11.7 %collective-permute-start.14 = (bf16[512,256]{1,0:T(8,128)(2,1)S(1)}, bf16[512,256]{1,0:T(8,128)(2,1)S(1)}, u32[]{:S(2)}, u32[]{:S(2)}) collective-permute-start(bf16[512,256]{1,0:T(8,128)(2,1)S(1)} %slice.128), channel_id=1, source_target_pairs={{0,16},{1,17},{2,18},{3,19},{4,20},{5,21},{6,22},{7,23},{8,24},{9,... | collective-permute-start | bytes 786440 | tf_op jit(solution)/shard_map/ppermute | solution.py:56
  68.9 19.1 %copy-start.5 = (bf16[640,256]{1,0:T(8,128)(2,1)}, bf16[640,256]{1,0:T(8,128)(2,1)S(1)}, u32[]{:S(2)}) copy-start(bf16[640,256]{1,0:T(8,128)(2,1)S(1)} %collective-permute-done.7.refs_3_.refs_14_) | copy-start | bytes 983044
  68.9 8.8 %copy-start.23 = (bf16[512,256]{1,0:T(8,128)(2,1)}, bf16[512,256]{1,0:T(8,128)(2,1)S(1)}, u32[]{:S(2)}) copy-start(bf16[512,256]{1,0:T(8,128)(2,1)S(1)} %collective-permute-done.10.refs_11_) | copy-start | bytes 786436
  68.9 8.8 %collective-permute-start.15 = (bf16[512,256]{1,0:T(8,128)(2,1)S(1)}, bf16[512,256]{1,0:T(8,128)(2,1)S(1)}, u32[]{:S(2)}, u32[]{:S(2)}) collective-permute-start(bf16[512,256]{1,0:T(8,128)(2,1)S(1)} %slice.129), channel_id=1, source_target_pairs={{0,16},{1,17},{2,18},{3,19},{4,20},{5,21},{6,22},{7,23},{8,24},{9,... | collective-permute-start | bytes 786440 | tf_op jit(solution)/shard_map/ppermute | solution.py:56
  77.7 10.3 %copy-start.2 = (bf16[640,256]{1,0:T(8,128)(2,1)S(1)}, bf16[640,256]{1,0:T(8,128)(2,1)}, u32[]{:S(2)}) copy-start(bf16[640,256]{1,0:T(8,128)(2,1)} %copy-done.1) | copy-start | bytes 983044
  77.7 10.2 %copy-start.24 = (bf16[512,256]{1,0:T(8,128)(2,1)}, bf16[512,256]{1,0:T(8,128)(2,1)S(1)}, u32[]{:S(2)}) copy-start(bf16[512,256]{1,0:T(8,128)(2,1)S(1)} %collective-permute-done.14.refs_13_) | copy-start | bytes 786436
  77.7 10.2 %copy-start.25 = (bf16[512,256]{1,0:T(8,128)(2,1)}, bf16[512,256]{1,0:T(8,128)(2,1)S(1)}, u32[]{:S(2)}) copy-start(bf16[512,256]{1,0:T(8,128)(2,1)S(1)} %collective-permute-done.15.refs_15_) | copy-start | bytes 786436
  77.8 0.8 copy-start.22
  87.9 3.2 %collective-permute-start.19 = (bf16[1088,512]{1,0:T(8,128)(2,1)}, bf16[1088,512]{1,0:T(8,128)(2,1)}, u32[]{:S(2)}, u32[]{:S(2)}) collective-permute-start(bf16[1088,512]{1,0:T(8,128)(2,1)} %shard_map.76.refs_2_), channel_id=1, source_target_pairs={{0,1},{1,0},{2,3},{3,2},{4,5},{5,4},{6,7},{7,6},{8,9},{9,8},{10,11... | collective-permute-start | bytes 3342344 | tf_op jit(solution)/shard_map/ppermute | solution.py:56
  88.4 2.7 %copy-start.6 = (bf16[4,128,256]{2,1,0:T(8,128)(2,1)}, bf16[4,128,256]{2,1,0:T(8,128)(2,1)S(1)}, u32[]{:S(2)}) copy-start(bf16[4,128,256]{2,1,0:T(8,128)(2,1)S(1)} %shard_map.74.refs_0_) | copy-start | bytes 786436
  88.4 2.7 %collective-permute-start.8 = (bf16[4,128,256]{2,1,0:T(8,128)(2,1)S(1)}, bf16[4,128,256]{2,1,0:T(8,128)(2,1)S(1)}, u32[]{:S(2)}, u32[]{:S(2)}) collective-permute-start(bf16[4,128,256]{2,1,0:T(8,128)(2,1)S(1)} %shard_map.74.refs_0_), channel_id=1, source_target_pairs={{0,1},{1,0},{2,3},{3,2},{4,5},{5,4},{6,7},{7,6},{8,9},{9,8},{10,11... | collective-permute-start | bytes 786440 | tf_op jit(solution)/shard_map/ppermute | solution.py:56
  91.1 0.7 copy-start.26
  91.8 30.1 %copy-start = (bf16[256,8192]{1,0:T(8,128)(2,1)S(1)}, bf16[256,8192]{1,0:T(8,128)(2,1)}, u32[]{:S(2)}) copy-start(bf16[256,8192]{1,0:T(8,128)(2,1)} %refs_7_.1) | copy-start | bytes 12582916
  103.1 2.4 %collective-permute-start.20 = (bf16[4,2,144,128]{3,2,1,0:T(8,128)(2,1)}, bf16[4,2,144,128]{3,2,1,0:T(8,128)(2,1)S(1)}, u32[]{:S(2)}, u32[]{:S(2)}) collective-permute-start(bf16[4,2,144,128]{3,2,1,0:T(8,128)(2,1)} %get-tuple-element.53), channel_id=1, source_target_pairs={{0,1},{1,0},{2,3},{3,2},{4,5},{5,4},{6,7},{7,6},{8,9},{9,8},{10,11... | collective-permute-start | bytes 884744 | tf_op jit(solution)/shard_map/ppermute | solution.py:56
  104.2 13.2 %collective-permute-start.25 = (f32[64,512]{1,0:T(8,128)}, f32[64,512]{1,0:T(8,128)S(1)}, u32[]{:S(2)}, u32[]{:S(2)}) collective-permute-start(f32[64,512]{1,0:T(8,128)} %get-tuple-element.60), channel_id=1, source_target_pairs={{0,1},{1,0},{2,3},{3,2},{4,5},{5,4},{6,7},{7,6},{8,9},{9,8},{10,11... | collective-permute-start | bytes 393224 | tf_op jit(solution)/shard_map/ppermute | solution.py:56
  105.5 1.0 copy-start.8
  106.5 6.0 %collective-permute-start.21 = (bf16[4,144,128]{2,1,0:T(8,128)(2,1)S(1)}, bf16[4,144,128]{2,1,0:T(8,128)(2,1)S(1)}, u32[]{:S(2)}, u32[]{:S(2)}) collective-permute-start(bf16[4,144,128]{2,1,0:T(8,128)(2,1)S(1)} %get-tuple-element.55), channel_id=1, source_target_pairs={{0,2},{1,3},{2,0},{3,1},{4,6},{5,7},{6,4},{7,5},{8,10},{9,11},{10,... | collective-permute-start | bytes 442376 | tf_op jit(solution)/shard_map/ppermute | solution.py:56
  112.6 5.7 %collective-permute-start.22 = (bf16[144,128]{1,0:T(8,128)(2,1)S(1)}, bf16[144,128]{1,0:T(8,128)(2,1)S(1)}, u32[]{:S(2)}, u32[]{:S(2)}) collective-permute-start(bf16[144,128]{1,0:T(8,128)(2,1)S(1)} %get-tuple-element.57), channel_id=1, source_target_pairs={{0,4},{1,5},{2,6},{3,7},{4,0},{5,1},{6,2},{7,3},{8,12},{9,13},{10,... | collective-permute-start | bytes 110600 | tf_op jit(solution)/shard_map/ppermute | solution.py:56
  115.0 5.6 %collective-permute-start.23 = (bf16[144,128]{1,0:T(8,128)(2,1)S(1)}, bf16[144,128]{1,0:T(8,128)(2,1)S(1)}, u32[]{:S(2)}, u32[]{:S(2)}) collective-permute-start(bf16[144,128]{1,0:T(8,128)(2,1)S(1)} %get-tuple-element.58), channel_id=1, source_target_pairs={{0,8},{1,9},{2,10},{3,11},{4,12},{5,13},{6,14},{7,15},{8,0},{9,1},... | collective-permute-start | bytes 110600 | tf_op jit(solution)/shard_map/ppermute | solution.py:56
  116.1 5.8 %collective-permute-start.24 = (bf16[144,128]{1,0:T(8,128)(2,1)S(1)}, bf16[144,128]{1,0:T(8,128)(2,1)S(1)}, u32[]{:S(2)}, u32[]{:S(2)}) collective-permute-start(bf16[144,128]{1,0:T(8,128)(2,1)S(1)} %get-tuple-element.59), channel_id=1, source_target_pairs={{0,12},{1,13},{2,14},{3,15},{4,8},{5,9},{6,10},{7,11},{8,4},{9,5},... | collective-permute-start | bytes 110600 | tf_op jit(solution)/shard_map/ppermute | solution.py:56
  123.6 2.0 %collective-permute-start.26 = (bf16[64,4096]{1,0:T(8,128)(2,1)S(1)}, bf16[64,4096]{1,0:T(8,128)(2,1)S(1)}, u32[]{:S(2)}, u32[]{:S(2)}) collective-permute-start(bf16[64,4096]{1,0:T(8,128)(2,1)S(1)} %slice.141), channel_id=1, source_target_pairs={{0,1},{1,0},{2,3},{3,2},{4,5},{5,4},{6,7},{7,6},{8,9},{9,8},{10,11... | collective-permute-start | bytes 1572872 | tf_op jit(solution)/shard_map/ppermute | solution.py:56
  125.7 8.4 %collective-permute-start.27 = (bf16[64,2048]{1,0:T(8,128)(2,1)S(1)}, bf16[64,2048]{1,0:T(8,128)(2,1)S(1)}, u32[]{:S(2)}, u32[]{:S(2)}) collective-permute-start(bf16[64,2048]{1,0:T(8,128)(2,1)S(1)} %slice.143), channel_id=1, source_target_pairs={{0,2},{1,3},{2,0},{3,1},{4,6},{5,7},{6,4},{7,5},{8,10},{9,11},{10,... | collective-permute-start | bytes 786440 | tf_op jit(solution)/shard_map/ppermute | solution.py:56
  134.2 6.7 %collective-permute-start.30 = (bf16[64,512]{1,0:T(8,128)(2,1)S(1)}, bf16[64,512]{1,0:T(8,128)(2,1)S(1)}, u32[]{:S(2)}, u32[]{:S(2)}) collective-permute-start(bf16[64,512]{1,0:T(8,128)(2,1)S(1)} %get-tuple-element.70), channel_id=1, source_target_pairs={{0,12},{1,13},{2,14},{3,15},{4,8},{5,9},{6,10},{7,11},{8,4},{9,5},... | collective-permute-start | bytes 196616 | tf_op jit(solution)/shard_map/ppermute | solution.py:56
  135.7 6.7 %collective-permute-start.29 = (bf16[64,512]{1,0:T(8,128)(2,1)S(1)}, bf16[64,512]{1,0:T(8,128)(2,1)S(1)}, u32[]{:S(2)}, u32[]{:S(2)}) collective-permute-start(bf16[64,512]{1,0:T(8,128)(2,1)S(1)} %get-tuple-element.71), channel_id=1, source_target_pairs={{0,8},{1,9},{2,10},{3,11},{4,12},{5,13},{6,14},{7,15},{8,0},{9,1},... | collective-permute-start | bytes 196616 | tf_op jit(solution)/shard_map/ppermute | solution.py:56
  135.9 6.5 %collective-permute-start.28 = (bf16[64,512]{1,0:T(8,128)(2,1)S(1)}, bf16[64,512]{1,0:T(8,128)(2,1)S(1)}, u32[]{:S(2)}, u32[]{:S(2)}) collective-permute-start(bf16[64,512]{1,0:T(8,128)(2,1)S(1)} %get-tuple-element.69), channel_id=1, source_target_pairs={{0,4},{1,5},{2,6},{3,7},{4,0},{5,1},{6,2},{7,3},{8,12},{9,13},{10,... | collective-permute-start | bytes 196616 | tf_op jit(solution)/shard_map/ppermute | solution.py:56

commit v19 on v18

--- a/solution.py
+++ b/solution.py
@@ -194,7 +194,7 @@
         return group
 
 
-AHEAD = 3
+AHEAD = 2
 
 
 def project(prompt, got, steps, blocks, width, pieces, acc, kind):

time: 144 us -> 144 us (level)
  no operation moved by 1% of the time
where the time goes in v19:
time: 144 us; the launch traced here: 143 us
  starting transfers between devices  49.1 us (34%)
  waiting for transfers between devices  38.5 us (27%)
  Pallas kernels  35 us (24%)
  other arithmetic  10.3 us (7%)
  local copies, waits for them, and re-layouts  9.85 us (7%)
    ppermute x31, starting transfers between devices, move(): return lax.ppermute(value, ('groups', 'sample'), pairs)  49.1 us
    ppermute x31, waiting for transfers between devices, move(): return lax.ppermute(value, ('groups', 'sample'), pairs)  38.5 us
    pallas_call x2, Pallas kernels, project(): pl.pallas_call(body, in_specs=[pl.BlockSpec(memory_space=pltpu.SMEM)] + [...  16.8 us
    pallas_call x1, Pallas kernels, attend(): pl.pallas_call(body, in_specs=[pl.BlockSpec(memory_space=pltpu.SMEM)] * 3...  11.3 us
    pallas_call x1, Pallas kernels, project_queries(): pl.pallas_call(body, in_specs=[whole, pl.BlockSpec(memory_space=pltpu.HBM...  4.7 us
    unnamed x56, local copies, waits for them, and re-layouts  3.36 us
    mul x1, other arithmetic, on_device(): table * HEAD_DIM ** (-0.5)  3.11 us
  transfers between devices with their start and end apart: 31, of which 15 were waited for; matrix products, arithmetic and copies ran while one was open for 11% of the time, Pallas kernels for 9%

profile of v19, /device:TPU:0, one launch (start us, length us, event | category | flops | bytes accessed | tf_op | source)
XLA Modules:
  0.0 143.3 jit_solution(11243433749280731260)
XLA Ops:
  0.0 0.5 collective-permute-start.11
  0.5 1.3 fusion.6
  1.9 3.6 %collective-permute-start.2 = (bf16[1024,256]{1,0:T(8,128)(2,1)S(1)}, bf16[1024,256]{1,0:T(8,128)(2,1)S(1)}, u32[]{:S(2)}, u32[]{:S(2)}) collective-permute-start(bf16[1024,256]{1,0:T(8,128)(2,1)S(1)} %get-tuple-element.61.refs_0_), channel_id=1, source_target_pairs={{0,8},{1,9},{2,10},{3,11},{4,0},{5,1},{6,2},{7,3},{8,12},{9,13},{1... | collective-permute-start | bytes 1572872 | tf_op jit(solution)/shard_map/ppermute | solution.py:56
  5.6 1.5 %collective-permute-start = (bf16[512,512]{1,0:T(8,128)(2,1)}, bf16[512,512]{1,0:T(8,128)(2,1)}, u32[]{:S(2)}, u32[]{:S(2)}) collective-permute-start(bf16[512,512]{1,0:T(8,128)(2,1)} %param.12), channel_id=1, source_target_pairs={{0,2},{1,3},{2,0},{3,1},{4,6},{5,7},{6,4},{7,5},{8,10},{9,11},{10,... | collective-permute-start | bytes 1572872 | tf_op jit(solution)/shard_map/ppermute | solution.py:56
  7.5 3.1 %fusion.1 = (f32[1024,64]{1,0:T(8,128)}, f32[1024,64]{1,0:T(8,128)}) fusion(f32[64]{0:T(128)S(1)} %multiply_power_fusion, f32[1024]{0:T(1024)S(1)} %convert_bitcast_fusion), kind=kLoop, calls=%fused_computation.5 | loop fusion | flops 196608 | bytes 528640 | tf_op jit(solution)/shard_map/mul | solution.py:582
  10.7 0.7 maximum_bitcast_fusion
  11.4 4.7 %shard_map.73.refs_4_ = bf16[64,256]{1,0:T(8,128)(2,1)} custom-call(bf16[64,8192]{1,0:T(8,128)(2,1)} %bitcast.40, bf16[8192,256]{1,0:T(8,128)(2,1)} %weight_ref.1, f32[2,128]{1,0:T(2,128)} %get-tuple-element.85.cosine_ref, f32[2,128]{1,0:T(2,128)} %get-tuple-element.86.sine_ref), custom_call_target="tpu_custom_call" | custom-call | flops 1 | bytes 1 | tf_op jit(solution)/shard_map/pallas_call | solution.py:113
  16.1 0.8 pad_maximum_fusion.refs_0_
  17.0 0.5 collective-permute-done.2.refs_2_
  17.4 3.4 %collective-permute-start.3 = (bf16[1024,256]{1,0:T(8,128)(2,1)S(1)}, bf16[1024,256]{1,0:T(8,128)(2,1)S(1)}, u32[]{:S(2)}, u32[]{:S(2)}) collective-permute-start(bf16[1024,256]{1,0:T(8,128)(2,1)S(1)} %collective-permute-done.2.refs_2_), channel_id=1, source_target_pairs={{0,8},{1,9},{2,10},{3,11},{4,0},{5,1},{6,2},{7,3},{8,12},{9,13},{1... | collective-permute-start | bytes 1572872 | tf_op jit(solution)/shard_map/ppermute | solution.py:56
  20.8 1.5 %collective-permute-start.12 = (bf16[1024,256]{1,0:T(8,128)(2,1)S(1)}, bf16[1024,256]{1,0:T(8,128)(2,1)S(1)}, u32[]{:S(2)}, u32[]{:S(2)}) collective-permute-start(bf16[1024,256]{1,0:T(8,128)(2,1)S(1)} %collective-permute-done.2.refs_2_), channel_id=1, source_target_pairs={{0,16},{1,17},{2,18},{3,19},{4,20},{5,21},{6,22},{7,23},{8,24},{9,... | collective-permute-start | bytes 1572872 | tf_op jit(solution)/shard_map/ppermute | solution.py:56
  22.3 1.8 %broadcast_select_fusion.2 = (bf16[512,256]{1,0:T(8,128)(2,1)}, bf16[512,256]{1,0:T(8,128)(2,1)S(1)}) fusion(pred[]{:T(512)S(6)} %eq.29, bf16[512,512]{1,0:T(8,128)(2,1)} %collective-permute-done), kind=kLoop, calls=%fused_computation.15 | loop fusion | flops 262144 | bytes 1048577 | tf_op jit(solution)/shard_map/jit(_where)/select_n | solution.py:621
  24.1 1.5 %collective-permute-start.1 = (bf16[1088,256]{1,0:T(8,128)(2,1)S(1)}, bf16[1088,256]{1,0:T(8,128)(2,1)S(1)}, u32[]{:S(2)}, u32[]{:S(2)}) collective-permute-start(bf16[1088,256]{1,0:T(8,128)(2,1)S(1)} %pad_maximum_fusion.refs_0_), channel_id=1, source_target_pairs={{0,2},{1,3},{2,0},{3,1},{4,6},{5,7},{6,4},{7,5},{8,10},{9,11},{10,... | collective-permute-start | bytes 1671176 | tf_op jit(solution)/shard_map/ppermute | solution.py:56
  25.6 6.3 %collective-permute-done.3.refs_4_ = bf16[1024,256]{1,0:T(8,128)(2,1)S(1)} collective-permute-done((bf16[1024,256]{1,0:T(8,128)(2,1)S(1)}, bf16[1024,256]{1,0:T(8,128)(2,1)S(1)}, u32[]{:S(2)}, u32[]{:S(2)}) %collective-permute-start.3) | collective-permute-done | bytes 524320 | tf_op jit(solution)/shard_map/ppermute | solution.py:56
  31.9 3.4 %collective-permute-start.5 = (bf16[1024,256]{1,0:T(8,128)(2,1)S(1)}, bf16[1024,256]{1,0:T(8,128)(2,1)}, u32[]{:S(2)}, u32[]{:S(2)}) collective-permute-start(bf16[1024,256]{1,0:T(8,128)(2,1)S(1)} %collective-permute-done.3.refs_4_), channel_id=1, source_target_pairs={{0,8},{1,9},{2,10},{3,11},{4,0},{5,1},{6,2},{7,3},{8,12},{9,13},{1... | collective-permute-start | bytes 1572872 | tf_op jit(solution)/shard_map/ppermute | solution.py:56
  35.3 1.5 %collective-permute-start.9 = (bf16[1024,256]{1,0:T(8,128)(2,1)S(1)}, bf16[1024,256]{1,0:T(8,128)(2,1)}, u32[]{:S(2)}, u32[]{:S(2)}) collective-permute-start(bf16[1024,256]{1,0:T(8,128)(2,1)S(1)} %collective-permute-done.3.refs_4_), channel_id=1, source_target_pairs={{0,16},{1,17},{2,18},{3,19},{4,20},{5,21},{6,22},{7,23},{8,24},{9,... | collective-permute-start | bytes 1572872 | tf_op jit(solution)/shard_map/ppermute | solution.py:56
  36.8 0.8 copy-done.17
  37.8 1.5 %collective-permute-start.16 = (bf16[1024,256]{1,0:T(8,128)(2,1)S(1)}, bf16[1024,256]{1,0:T(8,128)(2,1)S(1)}, u32[]{:S(2)}, u32[]{:S(2)}) collective-permute-start(bf16[1024,256]{1,0:T(8,128)(2,1)S(1)} %pad_maximum_fusion.3.refs_2_), channel_id=1, source_target_pairs={{0,2},{1,3},{2,0},{3,1},{4,6},{5,7},{6,4},{7,5},{8,10},{9,11},{10,... | collective-permute-start | bytes 1572872 | tf_op jit(solution)/shard_map/ppermute | solution.py:56
  39.4 0.8 collective-permute-start.4
  40.2 0.6 pad_add_fusion.1.block_ref
  40.8 0.6 stack.138.block_ref
  41.4 0.7 stack.139.block_ref
  42.1 0.7 and_select_fusion.1
  42.8 4.9 %collective-permute-done.5.refs_6_ = bf16[1024,256]{1,0:T(8,128)(2,1)} collective-permute-done((bf16[1024,256]{1,0:T(8,128)(2,1)S(1)}, bf16[1024,256]{1,0:T(8,128)(2,1)}, u32[]{:S(2)}, u32[]{:S(2)}) %collective-permute-start.5) | collective-permute-done | bytes 524320 | tf_op jit(solution)/shard_map/ppermute | solution.py:56
  47.7 1.5 %collective-permute-start.13 = (bf16[1024,256]{1,0:T(8,128)(2,1)}, bf16[1024,256]{1,0:T(8,128)(2,1)S(1)}, u32[]{:S(2)}, u32[]{:S(2)}) collective-permute-start(bf16[1024,256]{1,0:T(8,128)(2,1)} %collective-permute-done.5.refs_6_), channel_id=1, source_target_pairs={{0,16},{1,17},{2,18},{3,19},{4,20},{5,21},{6,22},{7,23},{8,24},{9,... | collective-permute-start | bytes 1572872 | tf_op jit(solution)/shard_map/ppermute | solution.py:56
  49.1 1.0 slice.133
  50.2 1.6 %collective-permute-start.17 = (bf16[1024,256]{1,0:T(8,128)(2,1)S(1)}, bf16[1024,256]{1,0:T(8,128)(2,1)S(1)}, u32[]{:S(2)}, u32[]{:S(2)}) collective-permute-start(bf16[1024,256]{1,0:T(8,128)(2,1)S(1)} %pad_maximum_fusion.4.refs_4_), channel_id=1, source_target_pairs={{0,2},{1,3},{2,0},{3,1},{4,6},{5,7},{6,4},{7,5},{8,10},{9,11},{10,... | collective-permute-start | bytes 1572872 | tf_op jit(solution)/shard_map/ppermute | solution.py:56
  51.8 0.7 collective-permute-done.4.refs_1_.refs_10_
  52.5 3.4 %collective-permute-start.6 = (bf16[640,256]{1,0:T(8,128)(2,1)S(1)}, bf16[640,256]{1,0:T(8,128)(2,1)S(1)}, u32[]{:S(2)}, u32[]{:S(2)}) collective-permute-start(bf16[640,256]{1,0:T(8,128)(2,1)S(1)} %collective-permute-done.4.refs_1_.refs_10_), channel_id=1, source_target_pairs={{0,8},{1,9},{2,10},{3,11},{4,0},{5,1},{6,2},{7,3},{8,12},{9,13},{1... | collective-permute-start | bytes 983048 | tf_op jit(solution)/shard_map/ppermute | solution.py:56
  55.9 1.6 %collective-permute-start.10 = (bf16[512,256]{1,0:T(8,128)(2,1)S(1)}, bf16[512,256]{1,0:T(8,128)(2,1)S(1)}, u32[]{:S(2)}, u32[]{:S(2)}) collective-permute-start(bf16[512,256]{1,0:T(8,128)(2,1)S(1)} %slice.127), channel_id=1, source_target_pairs={{0,16},{1,17},{2,18},{3,19},{4,20},{5,21},{6,22},{7,23},{8,24},{9,... | collective-permute-start | bytes 786440 | tf_op jit(solution)/shard_map/ppermute | solution.py:56
  57.4 1.0 slice.134
  58.4 2.5 %collective-permute-done.6.refs_2_.refs_12_ = bf16[640,256]{1,0:T(8,128)(2,1)S(1)} collective-permute-done((bf16[640,256]{1,0:T(8,128)(2,1)S(1)}, bf16[640,256]{1,0:T(8,128)(2,1)S(1)}, u32[]{:S(2)}, u32[]{:S(2)}) %collective-permute-start.6) | collective-permute-done | bytes 327712 | tf_op jit(solution)/shard_map/ppermute | solution.py:56
  60.9 3.4 %collective-permute-start.7 = (bf16[640,256]{1,0:T(8,128)(2,1)S(1)}, bf16[640,256]{1,0:T(8,128)(2,1)S(1)}, u32[]{:S(2)}, u32[]{:S(2)}) collective-permute-start(bf16[640,256]{1,0:T(8,128)(2,1)S(1)} %collective-permute-done.6.refs_2_.refs_12_), channel_id=1, source_target_pairs={{0,8},{1,9},{2,10},{3,11},{4,0},{5,1},{6,2},{7,3},{8,12},{9,13},{1... | collective-permute-start | bytes 983048 | tf_op jit(solution)/shard_map/ppermute | solution.py:56
  64.4 1.6 %collective-permute-start.18 = (bf16[1024,256]{1,0:T(8,128)(2,1)S(1)}, bf16[1024,256]{1,0:T(8,128)(2,1)S(1)}, u32[]{:S(2)}, u32[]{:S(2)}) collective-permute-start(bf16[1024,256]{1,0:T(8,128)(2,1)S(1)} %pad_maximum_fusion.5.refs_6_), channel_id=1, source_target_pairs={{0,2},{1,3},{2,0},{3,1},{4,6},{5,7},{6,4},{7,5},{8,10},{9,11},{10,... | collective-permute-start | bytes 1572872 | tf_op jit(solution)/shard_map/ppermute | solution.py:56
  66.0 1.6 %collective-permute-start.14 = (bf16[512,256]{1,0:T(8,128)(2,1)S(1)}, bf16[512,256]{1,0:T(8,128)(2,1)S(1)}, u32[]{:S(2)}, u32[]{:S(2)}) collective-permute-start(bf16[512,256]{1,0:T(8,128)(2,1)S(1)} %slice.128), channel_id=1, source_target_pairs={{0,16},{1,17},{2,18},{3,19},{4,20},{5,21},{6,22},{7,23},{8,24},{9,... | collective-permute-start | bytes 786440 | tf_op jit(solution)/shard_map/ppermute | solution.py:56
  67.6 1.3 collective-permute-done.7.refs_3_.refs_14_
  68.9 1.6 %collective-permute-start.15 = (bf16[512,256]{1,0:T(8,128)(2,1)S(1)}, bf16[512,256]{1,0:T(8,128)(2,1)S(1)}, u32[]{:S(2)}, u32[]{:S(2)}) collective-permute-start(bf16[512,256]{1,0:T(8,128)(2,1)S(1)} %slice.129), channel_id=1, source_target_pairs={{0,16},{1,17},{2,18},{3,19},{4,20},{5,21},{6,22},{7,23},{8,24},{9,... | collective-permute-start | bytes 786440 | tf_op jit(solution)/shard_map/ppermute | solution.py:56
  70.5 7.2 %shard_map.75.refs_9_ = bf16[1088,512]{1,0:T(8,128)(2,1)} custom-call(s32[5]{0:T(128)} %stack.139.block_ref, bf16[512,8192]{1,0:T(8,128)(2,1)} %refs_6_.1, bf16[512,8192]{1,0:T(8,128)(2,1)} %collective-permute-done.11.got_ref.refs_7_, bf16[64,8192]{1,0:T(8,128)(2,1)} %bitcast.41, bf16[1024,256]{1,0:T(8,128)(2,1)} %copy-done.9, bf16[1024,256]{1,0:T(8,128)(2,1)} %copy-done.10, ...), custom_call_target="tpu_custom_call" | custom-call | flops 1 | bytes 1 | tf_op jit(solution)/shard_map/pallas_call | solution.py:233
  77.8 0.8 copy-done.22
  78.6 9.6 %shard_map.76.refs_2_ = bf16[1088,512]{1,0:T(8,128)(2,1)} custom-call(s32[8]{0:T(128)} %stack.138.block_ref, bf16[512,8192]{1,0:T(8,128)(2,1)} %refs_6_.1, bf16[512,8192]{1,0:T(8,128)(2,1)} %collective-permute-done.11.got_ref.refs_7_, bf16[64,8192]{1,0:T(8,128)(2,1)} %bitcast.42, bf16[1088,256]{1,0:T(8,128)(2,1)} %copy-done.11, ...), custom_call_target="tpu_custom_call" | custom-call | flops 1 | bytes 1 | tf_op jit(solution)/shard_map/pallas_call | solution.py:233
  88.7 0.5 collective-permute-start.8
  89.3 2.0 %collective-permute-done.8.refs_1_ = bf16[4,128,256]{2,1,0:T(8,128)(2,1)S(1)} collective-permute-done((bf16[4,128,256]{2,1,0:T(8,128)(2,1)S(1)}, bf16[4,128,256]{2,1,0:T(8,128)(2,1)S(1)}, u32[]{:S(2)}, u32[]{:S(2)}) %collective-permute-start.8) | collective-permute-done | bytes 262176 | tf_op jit(solution)/shard_map/ppermute | solution.py:56
  91.4 0.7 copy-done.26
  92.1 11.3 %shard_map.77 = (bf16[4,2,144,128]{3,2,1,0:T(8,128)(2,1)}, bf16[4,2,144,128]{3,2,1,0:T(8,128)(2,1)}, f32[64,512]{1,0:T(8,128)}) custom-call(s32[4]{0:T(128)} %get-tuple-element.81.place_ref, s32[4]{0:T(128)} %get-tuple-element.82.turn_ref, s32[3]{0:T(128)} %pad_add_fusion.1.block_ref, bf16[4,128,256]{2,1,0:T(8,128)(2,1)} %copy-done.6, ...), custom_call_target="tpu_custom_call" | custom-call | flops 1 | bytes 1 | tf_op jit(solution)/shard_map/pallas_call | solution.py:431
  103.7 0.8 slice.136
  104.9 0.8 slice.137
  105.8 1.0 copy-done.8
  106.8 1.6 %collective-permute-start.21 = (bf16[4,144,128]{2,1,0:T(8,128)(2,1)S(1)}, bf16[4,144,128]{2,1,0:T(8,128)(2,1)S(1)}, u32[]{:S(2)}, u32[]{:S(2)}) collective-permute-start(bf16[4,144,128]{2,1,0:T(8,128)(2,1)S(1)} %get-tuple-element.55), channel_id=1, source_target_pairs={{0,2},{1,3},{2,0},{3,1},{4,6},{5,7},{6,4},{7,5},{8,10},{9,11},{10,... | collective-permute-start | bytes 442376 | tf_op jit(solution)/shard_map/ppermute | solution.py:56
  108.6 4.2 %collective-permute-done.21.far_ref = bf16[4,144,128]{2,1,0:T(8,128)(2,1)S(1)} collective-permute-done((bf16[4,144,128]{2,1,0:T(8,128)(2,1)S(1)}, bf16[4,144,128]{2,1,0:T(8,128)(2,1)S(1)}, u32[]{:S(2)}, u32[]{:S(2)}) %collective-permute-start.21) | collective-permute-done | bytes 147488 | tf_op jit(solution)/shard_map/ppermute | solution.py:56
  112.9 2.4 %collective-permute-start.22 = (bf16[144,128]{1,0:T(8,128)(2,1)S(1)}, bf16[144,128]{1,0:T(8,128)(2,1)S(1)}, u32[]{:S(2)}, u32[]{:S(2)}) collective-permute-start(bf16[144,128]{1,0:T(8,128)(2,1)S(1)} %get-tuple-element.57), channel_id=1, source_target_pairs={{0,4},{1,5},{2,6},{3,7},{4,0},{5,1},{6,2},{7,3},{8,12},{9,13},{10,... | collective-permute-start | bytes 110600 | tf_op jit(solution)/shard_map/ppermute | solution.py:56
  115.3 1.1 collective-permute-start.23
  116.4 1.4 collective-permute-start.24
  117.8 0.8 fusion.2.refs_6_
  118.5 2.3 %collective-permute-done.23.refs_2_ = bf16[144,128]{1,0:T(8,128)(2,1)S(1)} collective-permute-done((bf16[144,128]{1,0:T(8,128)(2,1)S(1)}, bf16[144,128]{1,0:T(8,128)(2,1)S(1)}, u32[]{:S(2)}, u32[]{:S(2)}) %collective-permute-start.23) | collective-permute-done | bytes 36896 | tf_op jit(solution)/shard_map/ppermute | solution.py:56
  120.9 1.3 collective-permute-done.24.refs_3_
  122.1 1.7 %shard_map.80 = bf16[64,8192]{1,0:T(8,128)(2,1)S(1)} custom-call(s32[16]{0:T(128)S(1)} %stack.123.block_ref, bf16[144,128]{1,0:T(8,128)(2,1)S(1)} %get-tuple-element.56.refs_0_, bf16[144,128]{1,0:T(8,128)(2,1)S(1)} %collective-permute-done.22.refs_1_, bf16[144,128]{1,0:T(8,128)(2,1)S(1)} %collective-permute-done.23.refs_2_, ...), custom_call_target="tpu_custom_call" | custom-call | flops 1 | bytes 1 | tf_op jit(solution)/shard_map/pallas_call | solution.py:272
  124.0 1.9 %collective-permute-done.26 = bf16[64,4096]{1,0:T(8,128)(2,1)S(1)} collective-permute-done((bf16[64,4096]{1,0:T(8,128)(2,1)S(1)}, bf16[64,4096]{1,0:T(8,128)(2,1)S(1)}, u32[]{:S(2)}, u32[]{:S(2)}) %collective-permute-start.26) | collective-permute-done | bytes 524320 | tf_op jit(solution)/shard_map/ppermute | solution.py:56
  126.0 1.6 %collective-permute-start.27 = (bf16[64,2048]{1,0:T(8,128)(2,1)S(1)}, bf16[64,2048]{1,0:T(8,128)(2,1)S(1)}, u32[]{:S(2)}, u32[]{:S(2)}) collective-permute-start(bf16[64,2048]{1,0:T(8,128)(2,1)S(1)} %slice.143), channel_id=1, source_target_pairs={{0,2},{1,3},{2,0},{3,1},{4,6},{5,7},{6,4},{7,5},{8,10},{9,11},{10,... | collective-permute-start | bytes 786440 | tf_op jit(solution)/shard_map/ppermute | solution.py:56
  127.6 6.8 %collective-permute-done.27 = bf16[64,2048]{1,0:T(8,128)(2,1)S(1)} collective-permute-done((bf16[64,2048]{1,0:T(8,128)(2,1)S(1)}, bf16[64,2048]{1,0:T(8,128)(2,1)S(1)}, u32[]{:S(2)}, u32[]{:S(2)}) %collective-permute-start.27) | collective-permute-done | bytes 262176 | tf_op jit(solution)/shard_map/ppermute | solution.py:56
  134.5 1.5 %collective-permute-start.30 = (bf16[64,512]{1,0:T(8,128)(2,1)S(1)}, bf16[64,512]{1,0:T(8,128)(2,1)S(1)}, u32[]{:S(2)}, u32[]{:S(2)}) collective-permute-start(bf16[64,512]{1,0:T(8,128)(2,1)S(1)} %get-tuple-element.70), channel_id=1, source_target_pairs={{0,12},{1,13},{2,14},{3,15},{4,8},{5,9},{6,10},{7,11},{8,4},{9,5},... | collective-permute-start | bytes 196616 | tf_op jit(solution)/shard_map/ppermute | solution.py:56
  136.2 2.8 %collective-permute-start.28 = (bf16[64,512]{1,0:T(8,128)(2,1)S(1)}, bf16[64,512]{1,0:T(8,128)(2,1)S(1)}, u32[]{:S(2)}, u32[]{:S(2)}) collective-permute-start(bf16[64,512]{1,0:T(8,128)(2,1)S(1)} %get-tuple-element.69), channel_id=1, source_target_pairs={{0,4},{1,5},{2,6},{3,7},{4,0},{5,1},{6,2},{7,3},{8,12},{9,13},{10,... | collective-permute-start | bytes 196616 | tf_op jit(solution)/shard_map/ppermute | solution.py:56
  139.0 2.2 %collective-permute-done.30 = bf16[64,512]{1,0:T(8,128)(2,1)S(1)} collective-permute-done((bf16[64,512]{1,0:T(8,128)(2,1)S(1)}, bf16[64,512]{1,0:T(8,128)(2,1)S(1)}, u32[]{:S(2)}, u32[]{:S(2)}) %collective-permute-start.30) | collective-permute-done | bytes 65568 | tf_op jit(solution)/shard_map/ppermute | solution.py:56
  141.2 1.4 %collective-permute-done.29 = bf16[64,512]{1,0:T(8,128)(2,1)S(1)} collective-permute-done((bf16[64,512]{1,0:T(8,128)(2,1)S(1)}, bf16[64,512]{1,0:T(8,128)(2,1)S(1)}, u32[]{:S(2)}, u32[]{:S(2)}) %collective-permute-start.29) | collective-permute-done | bytes 65568 | tf_op jit(solution)/shard_map/ppermute | solution.py:56
  142.7 0.7 add_convert_fusion.2
  (110 shorter events, 3.3 us)
Async XLA Ops:
  0.0 70.5 %collective-permute-start.11 = (bf16[512,8192]{1,0:T(8,128)(2,1)}, bf16[512,8192]{1,0:T(8,128)(2,1)}, u32[]{:S(2)}, u32[]{:S(2)}) collective-permute-start(bf16[512,8192]{1,0:T(8,128)(2,1)} %refs_6_.1), channel_id=1, source_target_pairs={{0,1},{1,0},{2,3},{3,2},{4,5},{5,4},{6,7},{7,6},{8,9},{9,8},{10,11... | collective-permute-start | bytes 25165832 | tf_op jit(solution)/shard_map/ppermute | solution.py:56
  1.7 5.5 %copy-start.27 = (s32[64]{0:T(128)S(1)}, s32[64]{0:T(128)}, u32[]{:S(2)}) copy-start(s32[64]{0:T(128)} %param.9) | copy-start | bytes 772
  1.9 14.2 %copy-start.9 = (bf16[1024,256]{1,0:T(8,128)(2,1)}, bf16[1024,256]{1,0:T(8,128)(2,1)S(1)}, u32[]{:S(2)}) copy-start(bf16[1024,256]{1,0:T(8,128)(2,1)S(1)} %get-tuple-element.61.refs_0_) | copy-start | bytes 1572868
  1.9 14.2 %copy-start.10 = (bf16[1024,256]{1,0:T(8,128)(2,1)}, bf16[1024,256]{1,0:T(8,128)(2,1)S(1)}, u32[]{:S(2)}) copy-start(bf16[1024,256]{1,0:T(8,128)(2,1)S(1)} %get-tuple-element.62.refs_1_) | copy-start | bytes 1572868
  1.9 15.5 %collective-permute-start.2 = (bf16[1024,256]{1,0:T(8,128)(2,1)S(1)}, bf16[1024,256]{1,0:T(8,128)(2,1)S(1)}, u32[]{:S(2)}, u32[]{:S(2)}) collective-permute-start(bf16[1024,256]{1,0:T(8,128)(2,1)S(1)} %get-tuple-element.61.refs_0_), channel_id=1, source_target_pairs={{0,8},{1,9},{2,10},{3,11},{4,0},{5,1},{6,2},{7,3},{8,12},{9,13},{1... | collective-permute-start | bytes 1572872 | tf_op jit(solution)/shard_map/ppermute | solution.py:56
  5.6 16.7 %collective-permute-start = (bf16[512,512]{1,0:T(8,128)(2,1)}, bf16[512,512]{1,0:T(8,128)(2,1)}, u32[]{:S(2)}, u32[]{:S(2)}) collective-permute-start(bf16[512,512]{1,0:T(8,128)(2,1)} %param.12), channel_id=1, source_target_pairs={{0,2},{1,3},{2,0},{3,1},{4,6},{5,7},{6,4},{7,5},{8,10},{9,11},{10,... | collective-permute-start | bytes 1572872 | tf_op jit(solution)/shard_map/ppermute | solution.py:56
  16.9 20.7 %copy-start.11 = (bf16[1088,256]{1,0:T(8,128)(2,1)}, bf16[1088,256]{1,0:T(8,128)(2,1)S(1)}, u32[]{:S(2)}) copy-start(bf16[1088,256]{1,0:T(8,128)(2,1)S(1)} %pad_maximum_fusion.refs_0_) | copy-start | bytes 1671172
  17.4 20.2 %copy-start.15 = (bf16[1024,256]{1,0:T(8,128)(2,1)}, bf16[1024,256]{1,0:T(8,128)(2,1)S(1)}, u32[]{:S(2)}) copy-start(bf16[1024,256]{1,0:T(8,128)(2,1)S(1)} %collective-permute-done.2.refs_2_) | copy-start | bytes 1572868
  17.4 14.5 %collective-permute-start.3 = (bf16[1024,256]{1,0:T(8,128)(2,1)S(1)}, bf16[1024,256]{1,0:T(8,128)(2,1)S(1)}, u32[]{:S(2)}, u32[]{:S(2)}) collective-permute-start(bf16[1024,256]{1,0:T(8,128)(2,1)S(1)} %collective-permute-done.2.refs_2_), channel_id=1, source_target_pairs={{0,8},{1,9},{2,10},{3,11},{4,0},{5,1},{6,2},{7,3},{8,12},{9,13},{1... | collective-permute-start | bytes 1572872 | tf_op jit(solution)/shard_map/ppermute | solution.py:56
  20.8 16.0 %collective-permute-start.12 = (bf16[1024,256]{1,0:T(8,128)(2,1)S(1)}, bf16[1024,256]{1,0:T(8,128)(2,1)S(1)}, u32[]{:S(2)}, u32[]{:S(2)}) collective-permute-start(bf16[1024,256]{1,0:T(8,128)(2,1)S(1)} %collective-permute-done.2.refs_2_), channel_id=1, source_target_pairs={{0,16},{1,17},{2,18},{3,19},{4,20},{5,21},{6,22},{7,23},{8,24},{9,... | collective-permute-start | bytes 1572872 | tf_op jit(solution)/shard_map/ppermute | solution.py:56
  24.1 15.2 %copy-start.7 = (bf16[64,256]{1,0:T(8,128)(2,1)S(1)}, bf16[64,256]{1,0:T(8,128)(2,1)}, u32[]{:S(2)}) copy-start(bf16[64,256]{1,0:T(8,128)(2,1)} %shard_map.73.refs_4_) | copy-start | bytes 98308
  24.1 13.7 %collective-permute-start.1 = (bf16[1088,256]{1,0:T(8,128)(2,1)S(1)}, bf16[1088,256]{1,0:T(8,128)(2,1)S(1)}, u32[]{:S(2)}, u32[]{:S(2)}) collective-permute-start(bf16[1088,256]{1,0:T(8,128)(2,1)S(1)} %pad_maximum_fusion.refs_0_), channel_id=1, source_target_pairs={{0,2},{1,3},{2,0},{3,1},{4,6},{5,7},{6,4},{7,5},{8,10},{9,11},{10,... | collective-permute-start | bytes 1671176 | tf_op jit(solution)/shard_map/ppermute | solution.py:56
  31.9 10.8 %copy-start.16 = (bf16[1024,256]{1,0:T(8,128)(2,1)}, bf16[1024,256]{1,0:T(8,128)(2,1)S(1)}, u32[]{:S(2)}) copy-start(bf16[1024,256]{1,0:T(8,128)(2,1)S(1)} %collective-permute-done.3.refs_4_) | copy-start | bytes 1572868
  31.9 15.8 %collective-permute-start.5 = (bf16[1024,256]{1,0:T(8,128)(2,1)S(1)}, bf16[1024,256]{1,0:T(8,128)(2,1)}, u32[]{:S(2)}, u32[]{:S(2)}) collective-permute-start(bf16[1024,256]{1,0:T(8,128)(2,1)S(1)} %collective-permute-done.3.refs_4_), channel_id=1, source_target_pairs={{0,8},{1,9},{2,10},{3,11},{4,0},{5,1},{6,2},{7,3},{8,12},{9,13},{1... | collective-permute-start | bytes 1572872 | tf_op jit(solution)/shard_map/ppermute | solution.py:56
  35.3 13.9 %collective-permute-start.9 = (bf16[1024,256]{1,0:T(8,128)(2,1)S(1)}, bf16[1024,256]{1,0:T(8,128)(2,1)}, u32[]{:S(2)}, u32[]{:S(2)}) collective-permute-start(bf16[1024,256]{1,0:T(8,128)(2,1)S(1)} %collective-permute-done.3.refs_4_), channel_id=1, source_target_pairs={{0,16},{1,17},{2,18},{3,19},{4,20},{5,21},{6,22},{7,23},{8,24},{9,... | collective-permute-start | bytes 1572872 | tf_op jit(solution)/shard_map/ppermute | solution.py:56
  36.8 0.8 copy-start.17
  37.7 12.5 %copy-start.12 = (bf16[1024,256]{1,0:T(8,128)(2,1)}, bf16[1024,256]{1,0:T(8,128)(2,1)S(1)}, u32[]{:S(2)}) copy-start(bf16[1024,256]{1,0:T(8,128)(2,1)S(1)} %pad_maximum_fusion.3.refs_2_) | copy-start | bytes 1572868
  37.8 1.5 %copy-start.19 = (bf16[1088,256]{1,0:T(8,128)(2,1)}, bf16[1088,256]{1,0:T(8,128)(2,1)S(1)}, u32[]{:S(2)}) copy-start(bf16[1088,256]{1,0:T(8,128)(2,1)S(1)} %collective-permute-done.1.refs_1_) | copy-start | bytes 1671172
  37.8 12.4 %collective-permute-start.16 = (bf16[1024,256]{1,0:T(8,128)(2,1)S(1)}, bf16[1024,256]{1,0:T(8,128)(2,1)S(1)}, u32[]{:S(2)}, u32[]{:S(2)}) collective-permute-start(bf16[1024,256]{1,0:T(8,128)(2,1)S(1)} %pad_maximum_fusion.3.refs_2_), channel_id=1, source_target_pairs={{0,2},{1,3},{2,0},{3,1},{4,6},{5,7},{6,4},{7,5},{8,10},{9,11},{10,... | collective-permute-start | bytes 1572872 | tf_op jit(solution)/shard_map/ppermute | solution.py:56
  39.4 10.8 %copy-start.1 = (bf16[640,256]{1,0:T(8,128)(2,1)}, bf16[640,256]{1,0:T(8,128)(2,1)S(1)}, u32[]{:S(2)}) copy-start(bf16[640,256]{1,0:T(8,128)(2,1)S(1)} %pad_maximum_fusion.6.refs_0_.refs_8_) | copy-start | bytes 983044
  39.4 13.1 %collective-permute-start.4 = (bf16[640,256]{1,0:T(8,128)(2,1)S(1)}, bf16[640,256]{1,0:T(8,128)(2,1)S(1)}, u32[]{:S(2)}, u32[]{:S(2)}) collective-permute-start(bf16[640,256]{1,0:T(8,128)(2,1)S(1)} %pad_maximum_fusion.6.refs_0_.refs_8_), channel_id=1, source_target_pairs={{0,8},{1,9},{2,10},{3,11},{4,0},{5,1},{6,2},{7,3},{8,12},{9,13},{1... | collective-permute-start | bytes 983048 | tf_op jit(solution)/shard_map/ppermute | solution.py:56
  47.7 16.6 %collective-permute-start.13 = (bf16[1024,256]{1,0:T(8,128)(2,1)}, bf16[1024,256]{1,0:T(8,128)(2,1)S(1)}, u32[]{:S(2)}, u32[]{:S(2)}) collective-permute-start(bf16[1024,256]{1,0:T(8,128)(2,1)} %collective-permute-done.5.refs_6_), channel_id=1, source_target_pairs={{0,16},{1,17},{2,18},{3,19},{4,20},{5,21},{6,22},{7,23},{8,24},{9,... | collective-permute-start | bytes 1572872 | tf_op jit(solution)/shard_map/ppermute | solution.py:56
  50.2 14.2 %copy-start.13 = (bf16[1024,256]{1,0:T(8,128)(2,1)}, bf16[1024,256]{1,0:T(8,128)(2,1)S(1)}, u32[]{:S(2)}) copy-start(bf16[1024,256]{1,0:T(8,128)(2,1)S(1)} %pad_maximum_fusion.4.refs_4_) | copy-start | bytes 1572868
  50.2 14.2 %copy-start.20 = (bf16[1024,256]{1,0:T(8,128)(2,1)}, bf16[1024,256]{1,0:T(8,128)(2,1)S(1)}, u32[]{:S(2)}) copy-start(bf16[1024,256]{1,0:T(8,128)(2,1)S(1)} %collective-permute-done.16.refs_3_) | copy-start | bytes 1572868
  50.2 14.2 %collective-permute-start.17 = (bf16[1024,256]{1,0:T(8,128)(2,1)S(1)}, bf16[1024,256]{1,0:T(8,128)(2,1)S(1)}, u32[]{:S(2)}, u32[]{:S(2)}) collective-permute-start(bf16[1024,256]{1,0:T(8,128)(2,1)S(1)} %pad_maximum_fusion.4.refs_4_), channel_id=1, source_target_pairs={{0,2},{1,3},{2,0},{3,1},{4,6},{5,7},{6,4},{7,5},{8,10},{9,11},{10,... | collective-permute-start | bytes 1572872 | tf_op jit(solution)/shard_map/ppermute | solution.py:56
  52.5 35.8 %copy-start.3 = (bf16[640,256]{1,0:T(8,128)(2,1)}, bf16[640,256]{1,0:T(8,128)(2,1)S(1)}, u32[]{:S(2)}) copy-start(bf16[640,256]{1,0:T(8,128)(2,1)S(1)} %collective-permute-done.4.refs_1_.refs_10_) | copy-start | bytes 983044
  52.5 8.4 %collective-permute-start.6 = (bf16[640,256]{1,0:T(8,128)(2,1)S(1)}, bf16[640,256]{1,0:T(8,128)(2,1)S(1)}, u32[]{:S(2)}, u32[]{:S(2)}) collective-permute-start(bf16[640,256]{1,0:T(8,128)(2,1)S(1)} %collective-permute-done.4.refs_1_.refs_10_), channel_id=1, source_target_pairs={{0,8},{1,9},{2,10},{3,11},{4,0},{5,1},{6,2},{7,3},{8,12},{9,13},{1... | collective-permute-start | bytes 983048 | tf_op jit(solution)/shard_map/ppermute | solution.py:56
  55.9 13.0 %collective-permute-start.10 = (bf16[512,256]{1,0:T(8,128)(2,1)S(1)}, bf16[512,256]{1,0:T(8,128)(2,1)S(1)}, u32[]{:S(2)}, u32[]{:S(2)}) collective-permute-start(bf16[512,256]{1,0:T(8,128)(2,1)S(1)} %slice.127), channel_id=1, source_target_pairs={{0,16},{1,17},{2,18},{3,19},{4,20},{5,21},{6,22},{7,23},{8,24},{9,... | collective-permute-start | bytes 786440 | tf_op jit(solution)/shard_map/ppermute | solution.py:56
  60.9 27.4 %copy-start.4 = (bf16[640,256]{1,0:T(8,128)(2,1)}, bf16[640,256]{1,0:T(8,128)(2,1)S(1)}, u32[]{:S(2)}) copy-start(bf16[640,256]{1,0:T(8,128)(2,1)S(1)} %collective-permute-done.6.refs_2_.refs_12_) | copy-start | bytes 983044
  60.9 8.0 %collective-permute-start.7 = (bf16[640,256]{1,0:T(8,128)(2,1)S(1)}, bf16[640,256]{1,0:T(8,128)(2,1)S(1)}, u32[]{:S(2)}, u32[]{:S(2)}) collective-permute-start(bf16[640,256]{1,0:T(8,128)(2,1)S(1)} %collective-permute-done.6.refs_2_.refs_12_), channel_id=1, source_target_pairs={{0,8},{1,9},{2,10},{3,11},{4,0},{5,1},{6,2},{7,3},{8,12},{9,13},{1... | collective-permute-start | bytes 983048 | tf_op jit(solution)/shard_map/ppermute | solution.py:56
  64.3 4.6 %copy-start.18 = (bf16[1024,256]{1,0:T(8,128)(2,1)}, bf16[1024,256]{1,0:T(8,128)(2,1)S(1)}, u32[]{:S(2)}) copy-start(bf16[1024,256]{1,0:T(8,128)(2,1)S(1)} %collective-permute-done.13.refs_7_) | copy-start | bytes 1572868
  64.4 13.3 %copy-start.14 = (bf16[1024,256]{1,0:T(8,128)(2,1)}, bf16[1024,256]{1,0:T(8,128)(2,1)S(1)}, u32[]{:S(2)}) copy-start(bf16[1024,256]{1,0:T(8,128)(2,1)S(1)} %pad_maximum_fusion.5.refs_6_) | copy-start | bytes 1572868
  64.4 13.3 %copy-start.21 = (bf16[1024,256]{1,0:T(8,128)(2,1)}, bf16[1024,256]{1,0:T(8,128)(2,1)S(1)}, u32[]{:S(2)}) copy-start(bf16[1024,256]{1,0:T(8,128)(2,1)S(1)} %collective-permute-done.17.refs_5_) | copy-start | bytes 1572868
  64.4 13.3 %collective-permute-start.18 = (bf16[1024,256]{1,0:T(8,128)(2,1)S(1)}, bf16[1024,256]{1,0:T(8,128)(2,1)S(1)}, u32[]{:S(2)}, u32[]{:S(2)}) collective-permute-start(bf16[1024,256]{1,0:T(8,128)(2,1)S(1)} %pad_maximum_fusion.5.refs_6_), channel_id=1, source_target_pairs={{0,2},{1,3},{2,0},{3,1},{4,6},{5,7},{6,4},{7,5},{8,10},{9,11},{10,... | collective-permute-start | bytes 1572872 | tf_op jit(solution)/shard_map/ppermute | solution.py:56
  66.0 11.7 %collective-permute-start.14 = (bf16[512,256]{1,0:T(8,128)(2,1)S(1)}, bf16[512,256]{1,0:T(8,128)(2,1)S(1)}, u32[]{:S(2)}, u32[]{:S(2)}) collective-permute-start(bf16[512,256]{1,0:T(8,128)(2,1)S(1)} %slice.128), channel_id=1, source_target_pairs={{0,16},{1,17},{2,18},{3,19},{4,20},{5,21},{6,22},{7,23},{8,24},{9,... | collective-permute-start | bytes 786440 | tf_op jit(solution)/shard_map/ppermute | solution.py:56
  68.9 19.4 %copy-start.5 = (bf16[640,256]{1,0:T(8,128)(2,1)}, bf16[640,256]{1,0:T(8,128)(2,1)S(1)}, u32[]{:S(2)}) copy-start(bf16[640,256]{1,0:T(8,128)(2,1)S(1)} %collective-permute-done.7.refs_3_.refs_14_) | copy-start | bytes 983044
  68.9 8.8 %copy-start.23 = (bf16[512,256]{1,0:T(8,128)(2,1)}, bf16[512,256]{1,0:T(8,128)(2,1)S(1)}, u32[]{:S(2)}) copy-start(bf16[512,256]{1,0:T(8,128)(2,1)S(1)} %collective-permute-done.10.refs_11_) | copy-start | bytes 786436
  68.9 8.8 %collective-permute-start.15 = (bf16[512,256]{1,0:T(8,128)(2,1)S(1)}, bf16[512,256]{1,0:T(8,128)(2,1)S(1)}, u32[]{:S(2)}, u32[]{:S(2)}) collective-permute-start(bf16[512,256]{1,0:T(8,128)(2,1)S(1)} %slice.129), channel_id=1, source_target_pairs={{0,16},{1,17},{2,18},{3,19},{4,20},{5,21},{6,22},{7,23},{8,24},{9,... | collective-permute-start | bytes 786440 | tf_op jit(solution)/shard_map/ppermute | solution.py:56
  77.7 10.6 %copy-start.2 = (bf16[640,256]{1,0:T(8,128)(2,1)S(1)}, bf16[640,256]{1,0:T(8,128)(2,1)}, u32[]{:S(2)}) copy-start(bf16[640,256]{1,0:T(8,128)(2,1)} %copy-done.1) | copy-start | bytes 983044
  77.7 10.5 %copy-start.24 = (bf16[512,256]{1,0:T(8,128)(2,1)}, bf16[512,256]{1,0:T(8,128)(2,1)S(1)}, u32[]{:S(2)}) copy-start(bf16[512,256]{1,0:T(8,128)(2,1)S(1)} %collective-permute-done.14.refs_13_) | copy-start | bytes 786436
  77.7 10.5 %copy-start.25 = (bf16[512,256]{1,0:T(8,128)(2,1)}, bf16[512,256]{1,0:T(8,128)(2,1)S(1)}, u32[]{:S(2)}) copy-start(bf16[512,256]{1,0:T(8,128)(2,1)S(1)} %collective-permute-done.15.refs_15_) | copy-start | bytes 786436
  77.8 0.8 copy-start.22
  88.2 3.2 %collective-permute-start.19 = (bf16[1088,512]{1,0:T(8,128)(2,1)}, bf16[1088,512]{1,0:T(8,128)(2,1)}, u32[]{:S(2)}, u32[]{:S(2)}) collective-permute-start(bf16[1088,512]{1,0:T(8,128)(2,1)} %shard_map.76.refs_2_), channel_id=1, source_target_pairs={{0,1},{1,0},{2,3},{3,2},{4,5},{5,4},{6,7},{7,6},{8,9},{9,8},{10,11... | collective-permute-start | bytes 3342344 | tf_op jit(solution)/shard_map/ppermute | solution.py:56
  88.7 2.7 %copy-start.6 = (bf16[4,128,256]{2,1,0:T(8,128)(2,1)}, bf16[4,128,256]{2,1,0:T(8,128)(2,1)S(1)}, u32[]{:S(2)}) copy-start(bf16[4,128,256]{2,1,0:T(8,128)(2,1)S(1)} %shard_map.74.refs_0_) | copy-start | bytes 786436
  88.7 2.7 %collective-permute-start.8 = (bf16[4,128,256]{2,1,0:T(8,128)(2,1)S(1)}, bf16[4,128,256]{2,1,0:T(8,128)(2,1)S(1)}, u32[]{:S(2)}, u32[]{:S(2)}) collective-permute-start(bf16[4,128,256]{2,1,0:T(8,128)(2,1)S(1)} %shard_map.74.refs_0_), channel_id=1, source_target_pairs={{0,1},{1,0},{2,3},{3,2},{4,5},{5,4},{6,7},{7,6},{8,9},{9,8},{10,11... | collective-permute-start | bytes 786440 | tf_op jit(solution)/shard_map/ppermute | solution.py:56
  91.4 0.7 copy-start.26
  92.1 30.1 %copy-start = (bf16[256,8192]{1,0:T(8,128)(2,1)S(1)}, bf16[256,8192]{1,0:T(8,128)(2,1)}, u32[]{:S(2)}) copy-start(bf16[256,8192]{1,0:T(8,128)(2,1)} %refs_7_.1) | copy-start | bytes 12582916
  103.4 2.4 %collective-permute-start.20 = (bf16[4,2,144,128]{3,2,1,0:T(8,128)(2,1)}, bf16[4,2,144,128]{3,2,1,0:T(8,128)(2,1)S(1)}, u32[]{:S(2)}, u32[]{:S(2)}) collective-permute-start(bf16[4,2,144,128]{3,2,1,0:T(8,128)(2,1)} %get-tuple-element.53), channel_id=1, source_target_pairs={{0,1},{1,0},{2,3},{3,2},{4,5},{5,4},{6,7},{7,6},{8,9},{9,8},{10,11... | collective-permute-start | bytes 884744 | tf_op jit(solution)/shard_map/ppermute | solution.py:56
  104.5 13.2 %collective-permute-start.25 = (f32[64,512]{1,0:T(8,128)}, f32[64,512]{1,0:T(8,128)S(1)}, u32[]{:S(2)}, u32[]{:S(2)}) collective-permute-start(f32[64,512]{1,0:T(8,128)} %get-tuple-element.60), channel_id=1, source_target_pairs={{0,1},{1,0},{2,3},{3,2},{4,5},{5,4},{6,7},{7,6},{8,9},{9,8},{10,11... | collective-permute-start | bytes 393224 | tf_op jit(solution)/shard_map/ppermute | solution.py:56
  105.8 1.0 copy-start.8
  106.8 5.9 %collective-permute-start.21 = (bf16[4,144,128]{2,1,0:T(8,128)(2,1)S(1)}, bf16[4,144,128]{2,1,0:T(8,128)(2,1)S(1)}, u32[]{:S(2)}, u32[]{:S(2)}) collective-permute-start(bf16[4,144,128]{2,1,0:T(8,128)(2,1)S(1)} %get-tuple-element.55), channel_id=1, source_target_pairs={{0,2},{1,3},{2,0},{3,1},{4,6},{5,7},{6,4},{7,5},{8,10},{9,11},{10,... | collective-permute-start | bytes 442376 | tf_op jit(solution)/shard_map/ppermute | solution.py:56
  112.9 5.7 %collective-permute-start.22 = (bf16[144,128]{1,0:T(8,128)(2,1)S(1)}, bf16[144,128]{1,0:T(8,128)(2,1)S(1)}, u32[]{:S(2)}, u32[]{:S(2)}) collective-permute-start(bf16[144,128]{1,0:T(8,128)(2,1)S(1)} %get-tuple-element.57), channel_id=1, source_target_pairs={{0,4},{1,5},{2,6},{3,7},{4,0},{5,1},{6,2},{7,3},{8,12},{9,13},{10,... | collective-permute-start | bytes 110600 | tf_op jit(solution)/shard_map/ppermute | solution.py:56
  115.3 5.6 %collective-permute-start.23 = (bf16[144,128]{1,0:T(8,128)(2,1)S(1)}, bf16[144,128]{1,0:T(8,128)(2,1)S(1)}, u32[]{:S(2)}, u32[]{:S(2)}) collective-permute-start(bf16[144,128]{1,0:T(8,128)(2,1)S(1)} %get-tuple-element.58), channel_id=1, source_target_pairs={{0,8},{1,9},{2,10},{3,11},{4,12},{5,13},{6,14},{7,15},{8,0},{9,1},... | collective-permute-start | bytes 110600 | tf_op jit(solution)/shard_map/ppermute | solution.py:56
  116.4 5.8 %collective-permute-start.24 = (bf16[144,128]{1,0:T(8,128)(2,1)S(1)}, bf16[144,128]{1,0:T(8,128)(2,1)S(1)}, u32[]{:S(2)}, u32[]{:S(2)}) collective-permute-start(bf16[144,128]{1,0:T(8,128)(2,1)S(1)} %get-tuple-element.59), channel_id=1, source_target_pairs={{0,12},{1,13},{2,14},{3,15},{4,8},{5,9},{6,10},{7,11},{8,4},{9,5},... | collective-permute-start | bytes 110600 | tf_op jit(solution)/shard_map/ppermute | solution.py:56
  123.9 2.0 %collective-permute-start.26 = (bf16[64,4096]{1,0:T(8,128)(2,1)S(1)}, bf16[64,4096]{1,0:T(8,128)(2,1)S(1)}, u32[]{:S(2)}, u32[]{:S(2)}) collective-permute-start(bf16[64,4096]{1,0:T(8,128)(2,1)S(1)} %slice.141), channel_id=1, source_target_pairs={{0,1},{1,0},{2,3},{3,2},{4,5},{5,4},{6,7},{7,6},{8,9},{9,8},{10,11... | collective-permute-start | bytes 1572872 | tf_op jit(solution)/shard_map/ppermute | solution.py:56
  126.0 8.4 %collective-permute-start.27 = (bf16[64,2048]{1,0:T(8,128)(2,1)S(1)}, bf16[64,2048]{1,0:T(8,128)(2,1)S(1)}, u32[]{:S(2)}, u32[]{:S(2)}) collective-permute-start(bf16[64,2048]{1,0:T(8,128)(2,1)S(1)} %slice.143), channel_id=1, source_target_pairs={{0,2},{1,3},{2,0},{3,1},{4,6},{5,7},{6,4},{7,5},{8,10},{9,11},{10,... | collective-permute-start | bytes 786440 | tf_op jit(solution)/shard_map/ppermute | solution.py:56
  134.5 6.7 %collective-permute-start.30 = (bf16[64,512]{1,0:T(8,128)(2,1)S(1)}, bf16[64,512]{1,0:T(8,128)(2,1)S(1)}, u32[]{:S(2)}, u32[]{:S(2)}) collective-permute-start(bf16[64,512]{1,0:T(8,128)(2,1)S(1)} %get-tuple-element.70), channel_id=1, source_target_pairs={{0,12},{1,13},{2,14},{3,15},{4,8},{5,9},{6,10},{7,11},{8,4},{9,5},... | collective-permute-start | bytes 196616 | tf_op jit(solution)/shard_map/ppermute | solution.py:56
  136.0 6.7 %collective-permute-start.29 = (bf16[64,512]{1,0:T(8,128)(2,1)S(1)}, bf16[64,512]{1,0:T(8,128)(2,1)S(1)}, u32[]{:S(2)}, u32[]{:S(2)}) collective-permute-start(bf16[64,512]{1,0:T(8,128)(2,1)S(1)} %get-tuple-element.71), channel_id=1, source_target_pairs={{0,8},{1,9},{2,10},{3,11},{4,12},{5,13},{6,14},{7,15},{8,0},{9,1},... | collective-permute-start | bytes 196616 | tf_op jit(solution)/shard_map/ppermute | solution.py:56
  136.2 6.5 %collective-permute-start.28 = (bf16[64,512]{1,0:T(8,128)(2,1)S(1)}, bf16[64,512]{1,0:T(8,128)(2,1)S(1)}, u32[]{:S(2)}, u32[]{:S(2)}) collective-permute-start(bf16[64,512]{1,0:T(8,128)(2,1)S(1)} %get-tuple-element.69), channel_id=1, source_target_pairs={{0,4},{1,5},{2,6},{3,7},{4,0},{5,1},{6,2},{7,3},{8,12},{9,13},{10,... | collective-permute-start | bytes 196616 | tf_op jit(solution)/shard_map/ppermute | solution.py:56

commit v20 on v19

--- a/solution.py
+++ b/solution.py
@@ -161,8 +161,8 @@
         self.height = 2 * self.row_count + self.step_count
         self.columns = sum(array.shape[1] for array, _ in pieces[0])
         self.scratch = [
-            pltpu.VMEM((self.count, self.height, width), prompt.dtype),
-            pltpu.VMEM((self.count, width, self.columns), prompt.dtype),
+            pltpu.VMEM((self.height, self.count * width), prompt.dtype),
+            pltpu.VMEM((self.count * width, self.columns), prompt.dtype),
             pltpu.SemaphoreType.DMA((self.count, 5)),
         ]
 
@@ -176,7 +176,9 @@
         ):
             group.append(
                 pltpu.make_async_copy(
-                    source.at[:, column], left.at[i, pl.ds(start, rows), :], sems.at[i, j]
+                    source.at[:, column],
+                    left.at[pl.ds(start, rows), pl.ds(i * self.width, self.width)],
+                    sems.at[i, j],
                 )
             )
             start += rows
@@ -186,7 +188,7 @@
             group.append(
                 pltpu.make_async_copy(
                     ref.at[pl.ds(first, self.width), :],
-                    weights.at[i, :, pl.ds(side, array.shape[1])],
+                    weights.at[pl.ds(i * self.width, self.width), pl.ds(side, array.shape[1])],
                     sems.at[i, 3 + j],
                 )
             )
@@ -194,7 +196,7 @@
         return group
 
 
-AHEAD = 2
+AHEAD = 4
 
 
 def project(prompt, got, steps, blocks, width, pieces, acc, kind):
@@ -216,13 +218,15 @@
             before = pltpu.make_async_copy(refs[len(held.arrays)], acc_held, acc_sem.at[0])
             before.start()
         total = None
-        for i, group in enumerate(groups):
-            for copy in group:
-                copy.wait()
-            if i + AHEAD < held.count:
-                for copy in groups[i + AHEAD]:
+        for i in range(0, held.count, 2):
+            for group in groups[i : i + 2]:
+                for copy in group:
+                    copy.wait()
+            for group in groups[i + AHEAD : i + AHEAD + 2]:
+                for copy in group:
                     copy.start()
-            product = jnp.dot(left[i], weights[i], preferred_element_type=jnp.float32)
+            depth = slice(i * width, min(i + 2, held.count) * width)
+            product = jnp.dot(left[:, depth], weights[depth, :], preferred_element_type=jnp.float32)
             total = product if total is None else total + product
         if extra:
             before.wait()
@@ -403,10 +407,14 @@
         for copy in before:
             copy.wait()
         total = sum(early_held[i].astype(jnp.float32) for i in range(len(early)))
-        for i, group in enumerate(groups):
-            for copy in group:
-                copy.wait()
-            total += jnp.dot(left[i], weight_rows[i], preferred_element_type=jnp.float32)
+        for i in range(0, held.count, 2):
+            for group in groups[i : i + 2]:
+                for copy in group:
+                    copy.wait()
+            depth = slice(i * width, min(i + 2, held.count) * width)
+            total += jnp.dot(
+                left[:, depth], weight_rows[depth, :], preferred_element_type=jnp.float32
+            )
         value_held[...] = total[:tokens].astype(jnp.bfloat16)
         step_out_ref[...] = total[tokens:]
 

time: 144 us -> 145 us (level)
  no operation moved by 1% of the time
where the time goes in v20:
time: 145 us; the launch traced here: 144 us
  starting transfers between devices  49 us (34%)
  waiting for transfers between devices  38.6 us (27%)
  Pallas kernels  36.1 us (25%)
  other arithmetic  10.3 us (7%)
  local copies, waits for them, and re-layouts  9.85 us (7%)
    ppermute x31, starting transfers between devices, move(): return lax.ppermute(value, ('groups', 'sample'), pairs)  49 us
    ppermute x31, waiting for transfers between devices, move(): return lax.ppermute(value, ('groups', 'sample'), pairs)  38.6 us
    pallas_call x2, Pallas kernels, project(): pl.pallas_call(body, in_specs=[pl.BlockSpec(memory_space=pltpu.SMEM)] + [...  17.9 us
    pallas_call x1, Pallas kernels, attend(): pl.pallas_call(body, in_specs=[pl.BlockSpec(memory_space=pltpu.SMEM)] * 3...  11.2 us
    pallas_call x1, Pallas kernels, project_queries(): pl.pallas_call(body, in_specs=[whole, pl.BlockSpec(memory_space=pltpu.HBM...  4.7 us
    unnamed x56, local copies, waits for them, and re-layouts  3.36 us
    mul x1, other arithmetic, on_device(): table * HEAD_DIM ** (-0.5)  3.11 us
  transfers between devices with their start and end apart: 31, of which 15 were waited for; matrix products, arithmetic and copies ran while one was open for 11% of the time, Pallas kernels for 9%

profile of v20, /device:TPU:0, one launch (start us, length us, event | category | flops | bytes accessed | tf_op | source)
XLA Modules:
  0.0 144.4 jit_solution(5260453114487318320)
XLA Ops:
  0.0 0.5 collective-permute-start.11
  0.5 1.3 fusion.6
  1.9 3.6 %collective-permute-start.2 = (bf16[1024,256]{1,0:T(8,128)(2,1)S(1)}, bf16[1024,256]{1,0:T(8,128)(2,1)S(1)}, u32[]{:S(2)}, u32[]{:S(2)}) collective-permute-start(bf16[1024,256]{1,0:T(8,128)(2,1)S(1)} %get-tuple-element.61.refs_0_), channel_id=1, source_target_pairs={{0,8},{1,9},{2,10},{3,11},{4,0},{5,1},{6,2},{7,3},{8,12},{9,13},{1... | collective-permute-start | bytes 1572872 | tf_op jit(solution)/shard_map/ppermute | solution.py:56
  5.6 1.5 %collective-permute-start = (bf16[512,512]{1,0:T(8,128)(2,1)}, bf16[512,512]{1,0:T(8,128)(2,1)}, u32[]{:S(2)}, u32[]{:S(2)}) collective-permute-start(bf16[512,512]{1,0:T(8,128)(2,1)} %param.12), channel_id=1, source_target_pairs={{0,2},{1,3},{2,0},{3,1},{4,6},{5,7},{6,4},{7,5},{8,10},{9,11},{10,... | collective-permute-start | bytes 1572872 | tf_op jit(solution)/shard_map/ppermute | solution.py:56
  7.5 3.1 %fusion.1 = (f32[1024,64]{1,0:T(8,128)}, f32[1024,64]{1,0:T(8,128)}) fusion(f32[64]{0:T(128)S(1)} %multiply_power_fusion, f32[1024]{0:T(1024)S(1)} %convert_bitcast_fusion), kind=kLoop, calls=%fused_computation.5 | loop fusion | flops 196608 | bytes 528640 | tf_op jit(solution)/shard_map/mul | solution.py:590
  10.7 0.7 maximum_bitcast_fusion
  11.4 4.7 %shard_map.73.refs_4_ = bf16[64,256]{1,0:T(8,128)(2,1)} custom-call(bf16[64,8192]{1,0:T(8,128)(2,1)} %bitcast.40, bf16[8192,256]{1,0:T(8,128)(2,1)} %weight_ref.1, f32[2,128]{1,0:T(2,128)} %get-tuple-element.85.cosine_ref, f32[2,128]{1,0:T(2,128)} %get-tuple-element.86.sine_ref), custom_call_target="tpu_custom_call" | custom-call | flops 1 | bytes 1 | tf_op jit(solution)/shard_map/pallas_call | solution.py:113
  16.1 0.8 pad_maximum_fusion.refs_0_
  17.0 0.5 collective-permute-done.2.refs_2_
  17.4 3.4 %collective-permute-start.3 = (bf16[1024,256]{1,0:T(8,128)(2,1)S(1)}, bf16[1024,256]{1,0:T(8,128)(2,1)S(1)}, u32[]{:S(2)}, u32[]{:S(2)}) collective-permute-start(bf16[1024,256]{1,0:T(8,128)(2,1)S(1)} %collective-permute-done.2.refs_2_), channel_id=1, source_target_pairs={{0,8},{1,9},{2,10},{3,11},{4,0},{5,1},{6,2},{7,3},{8,12},{9,13},{1... | collective-permute-start | bytes 1572872 | tf_op jit(solution)/shard_map/ppermute | solution.py:56
  20.8 1.5 %collective-permute-start.12 = (bf16[1024,256]{1,0:T(8,128)(2,1)S(1)}, bf16[1024,256]{1,0:T(8,128)(2,1)S(1)}, u32[]{:S(2)}, u32[]{:S(2)}) collective-permute-start(bf16[1024,256]{1,0:T(8,128)(2,1)S(1)} %collective-permute-done.2.refs_2_), channel_id=1, source_target_pairs={{0,16},{1,17},{2,18},{3,19},{4,20},{5,21},{6,22},{7,23},{8,24},{9,... | collective-permute-start | bytes 1572872 | tf_op jit(solution)/shard_map/ppermute | solution.py:56
  22.3 1.8 %broadcast_select_fusion.2 = (bf16[512,256]{1,0:T(8,128)(2,1)}, bf16[512,256]{1,0:T(8,128)(2,1)S(1)}) fusion(pred[]{:T(512)S(6)} %eq.29, bf16[512,512]{1,0:T(8,128)(2,1)} %collective-permute-done), kind=kLoop, calls=%fused_computation.15 | loop fusion | flops 262144 | bytes 1048577 | tf_op jit(solution)/shard_map/jit(_where)/select_n | solution.py:629
  24.1 1.5 %collective-permute-start.1 = (bf16[1088,256]{1,0:T(8,128)(2,1)S(1)}, bf16[1088,256]{1,0:T(8,128)(2,1)S(1)}, u32[]{:S(2)}, u32[]{:S(2)}) collective-permute-start(bf16[1088,256]{1,0:T(8,128)(2,1)S(1)} %pad_maximum_fusion.refs_0_), channel_id=1, source_target_pairs={{0,2},{1,3},{2,0},{3,1},{4,6},{5,7},{6,4},{7,5},{8,10},{9,11},{10,... | collective-permute-start | bytes 1671176 | tf_op jit(solution)/shard_map/ppermute | solution.py:56
  25.6 6.3 %collective-permute-done.3.refs_4_ = bf16[1024,256]{1,0:T(8,128)(2,1)S(1)} collective-permute-done((bf16[1024,256]{1,0:T(8,128)(2,1)S(1)}, bf16[1024,256]{1,0:T(8,128)(2,1)S(1)}, u32[]{:S(2)}, u32[]{:S(2)}) %collective-permute-start.3) | collective-permute-done | bytes 524320 | tf_op jit(solution)/shard_map/ppermute | solution.py:56
  31.9 3.4 %collective-permute-start.5 = (bf16[1024,256]{1,0:T(8,128)(2,1)S(1)}, bf16[1024,256]{1,0:T(8,128)(2,1)}, u32[]{:S(2)}, u32[]{:S(2)}) collective-permute-start(bf16[1024,256]{1,0:T(8,128)(2,1)S(1)} %collective-permute-done.3.refs_4_), channel_id=1, source_target_pairs={{0,8},{1,9},{2,10},{3,11},{4,0},{5,1},{6,2},{7,3},{8,12},{9,13},{1... | collective-permute-start | bytes 1572872 | tf_op jit(solution)/shard_map/ppermute | solution.py:56
  35.3 1.5 %collective-permute-start.9 = (bf16[1024,256]{1,0:T(8,128)(2,1)S(1)}, bf16[1024,256]{1,0:T(8,128)(2,1)}, u32[]{:S(2)}, u32[]{:S(2)}) collective-permute-start(bf16[1024,256]{1,0:T(8,128)(2,1)S(1)} %collective-permute-done.3.refs_4_), channel_id=1, source_target_pairs={{0,16},{1,17},{2,18},{3,19},{4,20},{5,21},{6,22},{7,23},{8,24},{9,... | collective-permute-start | bytes 1572872 | tf_op jit(solution)/shard_map/ppermute | solution.py:56
  36.8 0.8 copy-done.17
  37.8 1.5 %collective-permute-start.16 = (bf16[1024,256]{1,0:T(8,128)(2,1)S(1)}, bf16[1024,256]{1,0:T(8,128)(2,1)S(1)}, u32[]{:S(2)}, u32[]{:S(2)}) collective-permute-start(bf16[1024,256]{1,0:T(8,128)(2,1)S(1)} %pad_maximum_fusion.3.refs_2_), channel_id=1, source_target_pairs={{0,2},{1,3},{2,0},{3,1},{4,6},{5,7},{6,4},{7,5},{8,10},{9,11},{10,... | collective-permute-start | bytes 1572872 | tf_op jit(solution)/shard_map/ppermute | solution.py:56
  39.4 0.8 collective-permute-start.4
  40.2 0.6 pad_add_fusion.1.block_ref
  40.8 0.6 stack.138.block_ref
  41.4 0.7 stack.139.block_ref
  42.1 0.7 and_select_fusion.1
  42.8 4.9 %collective-permute-done.5.refs_6_ = bf16[1024,256]{1,0:T(8,128)(2,1)} collective-permute-done((bf16[1024,256]{1,0:T(8,128)(2,1)S(1)}, bf16[1024,256]{1,0:T(8,128)(2,1)}, u32[]{:S(2)}, u32[]{:S(2)}) %collective-permute-start.5) | collective-permute-done | bytes 524320 | tf_op jit(solution)/shard_map/ppermute | solution.py:56
  47.7 1.5 %collective-permute-start.13 = (bf16[1024,256]{1,0:T(8,128)(2,1)}, bf16[1024,256]{1,0:T(8,128)(2,1)S(1)}, u32[]{:S(2)}, u32[]{:S(2)}) collective-permute-start(bf16[1024,256]{1,0:T(8,128)(2,1)} %collective-permute-done.5.refs_6_), channel_id=1, source_target_pairs={{0,16},{1,17},{2,18},{3,19},{4,20},{5,21},{6,22},{7,23},{8,24},{9,... | collective-permute-start | bytes 1572872 | tf_op jit(solution)/shard_map/ppermute | solution.py:56
  49.1 1.0 slice.133
  50.2 1.6 %collective-permute-start.17 = (bf16[1024,256]{1,0:T(8,128)(2,1)S(1)}, bf16[1024,256]{1,0:T(8,128)(2,1)S(1)}, u32[]{:S(2)}, u32[]{:S(2)}) collective-permute-start(bf16[1024,256]{1,0:T(8,128)(2,1)S(1)} %pad_maximum_fusion.4.refs_4_), channel_id=1, source_target_pairs={{0,2},{1,3},{2,0},{3,1},{4,6},{5,7},{6,4},{7,5},{8,10},{9,11},{10,... | collective-permute-start | bytes 1572872 | tf_op jit(solution)/shard_map/ppermute | solution.py:56
  51.8 0.7 collective-permute-done.4.refs_1_.refs_10_
  52.5 3.4 %collective-permute-start.6 = (bf16[640,256]{1,0:T(8,128)(2,1)S(1)}, bf16[640,256]{1,0:T(8,128)(2,1)S(1)}, u32[]{:S(2)}, u32[]{:S(2)}) collective-permute-start(bf16[640,256]{1,0:T(8,128)(2,1)S(1)} %collective-permute-done.4.refs_1_.refs_10_), channel_id=1, source_target_pairs={{0,8},{1,9},{2,10},{3,11},{4,0},{5,1},{6,2},{7,3},{8,12},{9,13},{1... | collective-permute-start | bytes 983048 | tf_op jit(solution)/shard_map/ppermute | solution.py:56
  55.9 1.6 %collective-permute-start.10 = (bf16[512,256]{1,0:T(8,128)(2,1)S(1)}, bf16[512,256]{1,0:T(8,128)(2,1)S(1)}, u32[]{:S(2)}, u32[]{:S(2)}) collective-permute-start(bf16[512,256]{1,0:T(8,128)(2,1)S(1)} %slice.127), channel_id=1, source_target_pairs={{0,16},{1,17},{2,18},{3,19},{4,20},{5,21},{6,22},{7,23},{8,24},{9,... | collective-permute-start | bytes 786440 | tf_op jit(solution)/shard_map/ppermute | solution.py:56
  57.4 1.0 slice.134
  58.4 2.5 %collective-permute-done.6.refs_2_.refs_12_ = bf16[640,256]{1,0:T(8,128)(2,1)S(1)} collective-permute-done((bf16[640,256]{1,0:T(8,128)(2,1)S(1)}, bf16[640,256]{1,0:T(8,128)(2,1)S(1)}, u32[]{:S(2)}, u32[]{:S(2)}) %collective-permute-start.6) | collective-permute-done | bytes 327712 | tf_op jit(solution)/shard_map/ppermute | solution.py:56
  60.9 3.4 %collective-permute-start.7 = (bf16[640,256]{1,0:T(8,128)(2,1)S(1)}, bf16[640,256]{1,0:T(8,128)(2,1)S(1)}, u32[]{:S(2)}, u32[]{:S(2)}) collective-permute-start(bf16[640,256]{1,0:T(8,128)(2,1)S(1)} %collective-permute-done.6.refs_2_.refs_12_), channel_id=1, source_target_pairs={{0,8},{1,9},{2,10},{3,11},{4,0},{5,1},{6,2},{7,3},{8,12},{9,13},{1... | collective-permute-start | bytes 983048 | tf_op jit(solution)/shard_map/ppermute | solution.py:56
  64.4 1.6 %collective-permute-start.18 = (bf16[1024,256]{1,0:T(8,128)(2,1)S(1)}, bf16[1024,256]{1,0:T(8,128)(2,1)S(1)}, u32[]{:S(2)}, u32[]{:S(2)}) collective-permute-start(bf16[1024,256]{1,0:T(8,128)(2,1)S(1)} %pad_maximum_fusion.5.refs_6_), channel_id=1, source_target_pairs={{0,2},{1,3},{2,0},{3,1},{4,6},{5,7},{6,4},{7,5},{8,10},{9,11},{10,... | collective-permute-start | bytes 1572872 | tf_op jit(solution)/shard_map/ppermute | solution.py:56
  66.0 1.6 %collective-permute-start.14 = (bf16[512,256]{1,0:T(8,128)(2,1)S(1)}, bf16[512,256]{1,0:T(8,128)(2,1)S(1)}, u32[]{:S(2)}, u32[]{:S(2)}) collective-permute-start(bf16[512,256]{1,0:T(8,128)(2,1)S(1)} %slice.128), channel_id=1, source_target_pairs={{0,16},{1,17},{2,18},{3,19},{4,20},{5,21},{6,22},{7,23},{8,24},{9,... | collective-permute-start | bytes 786440 | tf_op jit(solution)/shard_map/ppermute | solution.py:56
  67.6 1.3 collective-permute-done.7.refs_3_.refs_14_
  68.9 1.6 %collective-permute-start.15 = (bf16[512,256]{1,0:T(8,128)(2,1)S(1)}, bf16[512,256]{1,0:T(8,128)(2,1)S(1)}, u32[]{:S(2)}, u32[]{:S(2)}) collective-permute-start(bf16[512,256]{1,0:T(8,128)(2,1)S(1)} %slice.129), channel_id=1, source_target_pairs={{0,16},{1,17},{2,18},{3,19},{4,20},{5,21},{6,22},{7,23},{8,24},{9,... | collective-permute-start | bytes 786440 | tf_op jit(solution)/shard_map/ppermute | solution.py:56
  70.5 8.0 %shard_map.75.refs_9_ = bf16[1088,512]{1,0:T(8,128)(2,1)} custom-call(s32[5]{0:T(128)} %stack.139.block_ref, bf16[512,8192]{1,0:T(8,128)(2,1)} %refs_6_.1, bf16[512,8192]{1,0:T(8,128)(2,1)} %collective-permute-done.11.got_ref.refs_7_, bf16[64,8192]{1,0:T(8,128)(2,1)} %bitcast.41, bf16[1024,256]{1,0:T(8,128)(2,1)} %copy-done.9, bf16[1024,256]{1,0:T(8,128)(2,1)} %copy-done.10, ...), custom_call_target="tpu_custom_call" | custom-call | flops 1 | bytes 1 | tf_op jit(solution)/shard_map/pallas_call | solution.py:237
  78.7 0.8 copy-done.22
  79.5 9.9 %shard_map.76.refs_2_ = bf16[1088,512]{1,0:T(8,128)(2,1)} custom-call(s32[8]{0:T(128)} %stack.138.block_ref, bf16[512,8192]{1,0:T(8,128)(2,1)} %refs_6_.1, bf16[512,8192]{1,0:T(8,128)(2,1)} %collective-permute-done.11.got_ref.refs_7_, bf16[64,8192]{1,0:T(8,128)(2,1)} %bitcast.42, bf16[1088,256]{1,0:T(8,128)(2,1)} %copy-done.11, ...), custom_call_target="tpu_custom_call" | custom-call | flops 1 | bytes 1 | tf_op jit(solution)/shard_map/pallas_call | solution.py:237
  89.9 0.5 collective-permute-start.8
  90.5 2.0 %collective-permute-done.8.refs_1_ = bf16[4,128,256]{2,1,0:T(8,128)(2,1)S(1)} collective-permute-done((bf16[4,128,256]{2,1,0:T(8,128)(2,1)S(1)}, bf16[4,128,256]{2,1,0:T(8,128)(2,1)S(1)}, u32[]{:S(2)}, u32[]{:S(2)}) %collective-permute-start.8) | collective-permute-done | bytes 262176 | tf_op jit(solution)/shard_map/ppermute | solution.py:56
  92.6 0.7 copy-done.26
  93.3 11.2 %shard_map.77 = (bf16[4,2,144,128]{3,2,1,0:T(8,128)(2,1)}, bf16[4,2,144,128]{3,2,1,0:T(8,128)(2,1)}, f32[64,512]{1,0:T(8,128)}) custom-call(s32[4]{0:T(128)} %get-tuple-element.81.place_ref, s32[4]{0:T(128)} %get-tuple-element.82.turn_ref, s32[3]{0:T(128)} %pad_add_fusion.1.block_ref, bf16[4,128,256]{2,1,0:T(8,128)(2,1)} %copy-done.6, ...), custom_call_target="tpu_custom_call" | custom-call | flops 1 | bytes 1 | tf_op jit(solution)/shard_map/pallas_call | solution.py:439
  104.8 0.8 slice.136
  106.0 0.8 slice.137
  106.9 1.0 copy-done.8
  107.9 1.5 %collective-permute-start.21 = (bf16[4,144,128]{2,1,0:T(8,128)(2,1)S(1)}, bf16[4,144,128]{2,1,0:T(8,128)(2,1)S(1)}, u32[]{:S(2)}, u32[]{:S(2)}) collective-permute-start(bf16[4,144,128]{2,1,0:T(8,128)(2,1)S(1)} %get-tuple-element.55), channel_id=1, source_target_pairs={{0,2},{1,3},{2,0},{3,1},{4,6},{5,7},{6,4},{7,5},{8,10},{9,11},{10,... | collective-permute-start | bytes 442376 | tf_op jit(solution)/shard_map/ppermute | solution.py:56
  109.6 4.2 %collective-permute-done.21.far_ref = bf16[4,144,128]{2,1,0:T(8,128)(2,1)S(1)} collective-permute-done((bf16[4,144,128]{2,1,0:T(8,128)(2,1)S(1)}, bf16[4,144,128]{2,1,0:T(8,128)(2,1)S(1)}, u32[]{:S(2)}, u32[]{:S(2)}) %collective-permute-start.21) | collective-permute-done | bytes 147488 | tf_op jit(solution)/shard_map/ppermute | solution.py:56
  113.9 2.5 %collective-permute-start.22 = (bf16[144,128]{1,0:T(8,128)(2,1)S(1)}, bf16[144,128]{1,0:T(8,128)(2,1)S(1)}, u32[]{:S(2)}, u32[]{:S(2)}) collective-permute-start(bf16[144,128]{1,0:T(8,128)(2,1)S(1)} %get-tuple-element.57), channel_id=1, source_target_pairs={{0,4},{1,5},{2,6},{3,7},{4,0},{5,1},{6,2},{7,3},{8,12},{9,13},{10,... | collective-permute-start | bytes 110600 | tf_op jit(solution)/shard_map/ppermute | solution.py:56
  116.4 1.1 collective-permute-start.23
  117.5 1.4 collective-permute-start.24
  118.9 0.8 fusion.2.refs_6_
  119.6 2.3 %collective-permute-done.23.refs_2_ = bf16[144,128]{1,0:T(8,128)(2,1)S(1)} collective-permute-done((bf16[144,128]{1,0:T(8,128)(2,1)S(1)}, bf16[144,128]{1,0:T(8,128)(2,1)S(1)}, u32[]{:S(2)}, u32[]{:S(2)}) %collective-permute-start.23) | collective-permute-done | bytes 36896 | tf_op jit(solution)/shard_map/ppermute | solution.py:56
  122.0 1.3 collective-permute-done.24.refs_3_
  123.2 1.7 %shard_map.80 = bf16[64,8192]{1,0:T(8,128)(2,1)S(1)} custom-call(s32[16]{0:T(128)S(1)} %stack.123.block_ref, bf16[144,128]{1,0:T(8,128)(2,1)S(1)} %get-tuple-element.56.refs_0_, bf16[144,128]{1,0:T(8,128)(2,1)S(1)} %collective-permute-done.22.refs_1_, bf16[144,128]{1,0:T(8,128)(2,1)S(1)} %collective-permute-done.23.refs_2_, ...), custom_call_target="tpu_custom_call" | custom-call | flops 1 | bytes 1 | tf_op jit(solution)/shard_map/pallas_call | solution.py:276
  125.1 1.9 %collective-permute-done.26 = bf16[64,4096]{1,0:T(8,128)(2,1)S(1)} collective-permute-done((bf16[64,4096]{1,0:T(8,128)(2,1)S(1)}, bf16[64,4096]{1,0:T(8,128)(2,1)S(1)}, u32[]{:S(2)}, u32[]{:S(2)}) %collective-permute-start.26) | collective-permute-done | bytes 524320 | tf_op jit(solution)/shard_map/ppermute | solution.py:56
  127.1 1.6 %collective-permute-start.27 = (bf16[64,2048]{1,0:T(8,128)(2,1)S(1)}, bf16[64,2048]{1,0:T(8,128)(2,1)S(1)}, u32[]{:S(2)}, u32[]{:S(2)}) collective-permute-start(bf16[64,2048]{1,0:T(8,128)(2,1)S(1)} %slice.143), channel_id=1, source_target_pairs={{0,2},{1,3},{2,0},{3,1},{4,6},{5,7},{6,4},{7,5},{8,10},{9,11},{10,... | collective-permute-start | bytes 786440 | tf_op jit(solution)/shard_map/ppermute | solution.py:56
  128.7 6.9 %collective-permute-done.27 = bf16[64,2048]{1,0:T(8,128)(2,1)S(1)} collective-permute-done((bf16[64,2048]{1,0:T(8,128)(2,1)S(1)}, bf16[64,2048]{1,0:T(8,128)(2,1)S(1)}, u32[]{:S(2)}, u32[]{:S(2)}) %collective-permute-start.27) | collective-permute-done | bytes 262176 | tf_op jit(solution)/shard_map/ppermute | solution.py:56
  135.6 1.5 %collective-permute-start.30 = (bf16[64,512]{1,0:T(8,128)(2,1)S(1)}, bf16[64,512]{1,0:T(8,128)(2,1)S(1)}, u32[]{:S(2)}, u32[]{:S(2)}) collective-permute-start(bf16[64,512]{1,0:T(8,128)(2,1)S(1)} %get-tuple-element.70), channel_id=1, source_target_pairs={{0,12},{1,13},{2,14},{3,15},{4,8},{5,9},{6,10},{7,11},{8,4},{9,5},... | collective-permute-start | bytes 196616 | tf_op jit(solution)/shard_map/ppermute | solution.py:56
  137.3 2.8 %collective-permute-start.28 = (bf16[64,512]{1,0:T(8,128)(2,1)S(1)}, bf16[64,512]{1,0:T(8,128)(2,1)S(1)}, u32[]{:S(2)}, u32[]{:S(2)}) collective-permute-start(bf16[64,512]{1,0:T(8,128)(2,1)S(1)} %get-tuple-element.69), channel_id=1, source_target_pairs={{0,4},{1,5},{2,6},{3,7},{4,0},{5,1},{6,2},{7,3},{8,12},{9,13},{10,... | collective-permute-start | bytes 196616 | tf_op jit(solution)/shard_map/ppermute | solution.py:56
  140.1 2.2 %collective-permute-done.30 = bf16[64,512]{1,0:T(8,128)(2,1)S(1)} collective-permute-done((bf16[64,512]{1,0:T(8,128)(2,1)S(1)}, bf16[64,512]{1,0:T(8,128)(2,1)S(1)}, u32[]{:S(2)}, u32[]{:S(2)}) %collective-permute-start.30) | collective-permute-done | bytes 65568 | tf_op jit(solution)/shard_map/ppermute | solution.py:56
  142.3 1.4 %collective-permute-done.29 = bf16[64,512]{1,0:T(8,128)(2,1)S(1)} collective-permute-done((bf16[64,512]{1,0:T(8,128)(2,1)S(1)}, bf16[64,512]{1,0:T(8,128)(2,1)S(1)}, u32[]{:S(2)}, u32[]{:S(2)}) %collective-permute-start.29) | collective-permute-done | bytes 65568 | tf_op jit(solution)/shard_map/ppermute | solution.py:56
  143.8 0.7 add_convert_fusion.2
  (110 shorter events, 3.3 us)
Async XLA Ops:
  0.0 70.5 %collective-permute-start.11 = (bf16[512,8192]{1,0:T(8,128)(2,1)}, bf16[512,8192]{1,0:T(8,128)(2,1)}, u32[]{:S(2)}, u32[]{:S(2)}) collective-permute-start(bf16[512,8192]{1,0:T(8,128)(2,1)} %refs_6_.1), channel_id=1, source_target_pairs={{0,1},{1,0},{2,3},{3,2},{4,5},{5,4},{6,7},{7,6},{8,9},{9,8},{10,11... | collective-permute-start | bytes 25165832 | tf_op jit(solution)/shard_map/ppermute | solution.py:56
  1.7 5.5 %copy-start.27 = (s32[64]{0:T(128)S(1)}, s32[64]{0:T(128)}, u32[]{:S(2)}) copy-start(s32[64]{0:T(128)} %param.9) | copy-start | bytes 772
  1.9 14.2 %copy-start.9 = (bf16[1024,256]{1,0:T(8,128)(2,1)}, bf16[1024,256]{1,0:T(8,128)(2,1)S(1)}, u32[]{:S(2)}) copy-start(bf16[1024,256]{1,0:T(8,128)(2,1)S(1)} %get-tuple-element.61.refs_0_) | copy-start | bytes 1572868
  1.9 14.2 %copy-start.10 = (bf16[1024,256]{1,0:T(8,128)(2,1)}, bf16[1024,256]{1,0:T(8,128)(2,1)S(1)}, u32[]{:S(2)}) copy-start(bf16[1024,256]{1,0:T(8,128)(2,1)S(1)} %get-tuple-element.62.refs_1_) | copy-start | bytes 1572868
  1.9 15.5 %collective-permute-start.2 = (bf16[1024,256]{1,0:T(8,128)(2,1)S(1)}, bf16[1024,256]{1,0:T(8,128)(2,1)S(1)}, u32[]{:S(2)}, u32[]{:S(2)}) collective-permute-start(bf16[1024,256]{1,0:T(8,128)(2,1)S(1)} %get-tuple-element.61.refs_0_), channel_id=1, source_target_pairs={{0,8},{1,9},{2,10},{3,11},{4,0},{5,1},{6,2},{7,3},{8,12},{9,13},{1... | collective-permute-start | bytes 1572872 | tf_op jit(solution)/shard_map/ppermute | solution.py:56
  5.6 16.7 %collective-permute-start = (bf16[512,512]{1,0:T(8,128)(2,1)}, bf16[512,512]{1,0:T(8,128)(2,1)}, u32[]{:S(2)}, u32[]{:S(2)}) collective-permute-start(bf16[512,512]{1,0:T(8,128)(2,1)} %param.12), channel_id=1, source_target_pairs={{0,2},{1,3},{2,0},{3,1},{4,6},{5,7},{6,4},{7,5},{8,10},{9,11},{10,... | collective-permute-start | bytes 1572872 | tf_op jit(solution)/shard_map/ppermute | solution.py:56
  16.9 20.7 %copy-start.11 = (bf16[1088,256]{1,0:T(8,128)(2,1)}, bf16[1088,256]{1,0:T(8,128)(2,1)S(1)}, u32[]{:S(2)}) copy-start(bf16[1088,256]{1,0:T(8,128)(2,1)S(1)} %pad_maximum_fusion.refs_0_) | copy-start | bytes 1671172
  17.4 20.2 %copy-start.15 = (bf16[1024,256]{1,0:T(8,128)(2,1)}, bf16[1024,256]{1,0:T(8,128)(2,1)S(1)}, u32[]{:S(2)}) copy-start(bf16[1024,256]{1,0:T(8,128)(2,1)S(1)} %collective-permute-done.2.refs_2_) | copy-start | bytes 1572868
  17.4 14.5 %collective-permute-start.3 = (bf16[1024,256]{1,0:T(8,128)(2,1)S(1)}, bf16[1024,256]{1,0:T(8,128)(2,1)S(1)}, u32[]{:S(2)}, u32[]{:S(2)}) collective-permute-start(bf16[1024,256]{1,0:T(8,128)(2,1)S(1)} %collective-permute-done.2.refs_2_), channel_id=1, source_target_pairs={{0,8},{1,9},{2,10},{3,11},{4,0},{5,1},{6,2},{7,3},{8,12},{9,13},{1... | collective-permute-start | bytes 1572872 | tf_op jit(solution)/shard_map/ppermute | solution.py:56
  20.8 16.0 %collective-permute-start.12 = (bf16[1024,256]{1,0:T(8,128)(2,1)S(1)}, bf16[1024,256]{1,0:T(8,128)(2,1)S(1)}, u32[]{:S(2)}, u32[]{:S(2)}) collective-permute-start(bf16[1024,256]{1,0:T(8,128)(2,1)S(1)} %collective-permute-done.2.refs_2_), channel_id=1, source_target_pairs={{0,16},{1,17},{2,18},{3,19},{4,20},{5,21},{6,22},{7,23},{8,24},{9,... | collective-permute-start | bytes 1572872 | tf_op jit(solution)/shard_map/ppermute | solution.py:56
  24.1 15.2 %copy-start.7 = (bf16[64,256]{1,0:T(8,128)(2,1)S(1)}, bf16[64,256]{1,0:T(8,128)(2,1)}, u32[]{:S(2)}) copy-start(bf16[64,256]{1,0:T(8,128)(2,1)} %shard_map.73.refs_4_) | copy-start | bytes 98308
  24.1 13.7 %collective-permute-start.1 = (bf16[1088,256]{1,0:T(8,128)(2,1)S(1)}, bf16[1088,256]{1,0:T(8,128)(2,1)S(1)}, u32[]{:S(2)}, u32[]{:S(2)}) collective-permute-start(bf16[1088,256]{1,0:T(8,128)(2,1)S(1)} %pad_maximum_fusion.refs_0_), channel_id=1, source_target_pairs={{0,2},{1,3},{2,0},{3,1},{4,6},{5,7},{6,4},{7,5},{8,10},{9,11},{10,... | collective-permute-start | bytes 1671176 | tf_op jit(solution)/shard_map/ppermute | solution.py:56
  31.9 10.8 %copy-start.16 = (bf16[1024,256]{1,0:T(8,128)(2,1)}, bf16[1024,256]{1,0:T(8,128)(2,1)S(1)}, u32[]{:S(2)}) copy-start(bf16[1024,256]{1,0:T(8,128)(2,1)S(1)} %collective-permute-done.3.refs_4_) | copy-start | bytes 1572868
  31.9 15.8 %collective-permute-start.5 = (bf16[1024,256]{1,0:T(8,128)(2,1)S(1)}, bf16[1024,256]{1,0:T(8,128)(2,1)}, u32[]{:S(2)}, u32[]{:S(2)}) collective-permute-start(bf16[1024,256]{1,0:T(8,128)(2,1)S(1)} %collective-permute-done.3.refs_4_), channel_id=1, source_target_pairs={{0,8},{1,9},{2,10},{3,11},{4,0},{5,1},{6,2},{7,3},{8,12},{9,13},{1... | collective-permute-start | bytes 1572872 | tf_op jit(solution)/shard_map/ppermute | solution.py:56
  35.3 13.9 %collective-permute-start.9 = (bf16[1024,256]{1,0:T(8,128)(2,1)S(1)}, bf16[1024,256]{1,0:T(8,128)(2,1)}, u32[]{:S(2)}, u32[]{:S(2)}) collective-permute-start(bf16[1024,256]{1,0:T(8,128)(2,1)S(1)} %collective-permute-done.3.refs_4_), channel_id=1, source_target_pairs={{0,16},{1,17},{2,18},{3,19},{4,20},{5,21},{6,22},{7,23},{8,24},{9,... | collective-permute-start | bytes 1572872 | tf_op jit(solution)/shard_map/ppermute | solution.py:56
  36.8 0.8 copy-start.17
  37.7 12.5 %copy-start.12 = (bf16[1024,256]{1,0:T(8,128)(2,1)}, bf16[1024,256]{1,0:T(8,128)(2,1)S(1)}, u32[]{:S(2)}) copy-start(bf16[1024,256]{1,0:T(8,128)(2,1)S(1)} %pad_maximum_fusion.3.refs_2_) | copy-start | bytes 1572868
  37.8 1.5 %copy-start.19 = (bf16[1088,256]{1,0:T(8,128)(2,1)}, bf16[1088,256]{1,0:T(8,128)(2,1)S(1)}, u32[]{:S(2)}) copy-start(bf16[1088,256]{1,0:T(8,128)(2,1)S(1)} %collective-permute-done.1.refs_1_) | copy-start | bytes 1671172
  37.8 12.4 %collective-permute-start.16 = (bf16[1024,256]{1,0:T(8,128)(2,1)S(1)}, bf16[1024,256]{1,0:T(8,128)(2,1)S(1)}, u32[]{:S(2)}, u32[]{:S(2)}) collective-permute-start(bf16[1024,256]{1,0:T(8,128)(2,1)S(1)} %pad_maximum_fusion.3.refs_2_), channel_id=1, source_target_pairs={{0,2},{1,3},{2,0},{3,1},{4,6},{5,7},{6,4},{7,5},{8,10},{9,11},{10,... | collective-permute-start | bytes 1572872 | tf_op jit(solution)/shard_map/ppermute | solution.py:56
  39.4 10.8 %copy-start.1 = (bf16[640,256]{1,0:T(8,128)(2,1)}, bf16[640,256]{1,0:T(8,128)(2,1)S(1)}, u32[]{:S(2)}) copy-start(bf16[640,256]{1,0:T(8,128)(2,1)S(1)} %pad_maximum_fusion.6.refs_0_.refs_8_) | copy-start | bytes 983044
  39.4 13.1 %collective-permute-start.4 = (bf16[640,256]{1,0:T(8,128)(2,1)S(1)}, bf16[640,256]{1,0:T(8,128)(2,1)S(1)}, u32[]{:S(2)}, u32[]{:S(2)}) collective-permute-start(bf16[640,256]{1,0:T(8,128)(2,1)S(1)} %pad_maximum_fusion.6.refs_0_.refs_8_), channel_id=1, source_target_pairs={{0,8},{1,9},{2,10},{3,11},{4,0},{5,1},{6,2},{7,3},{8,12},{9,13},{1... | collective-permute-start | bytes 983048 | tf_op jit(solution)/shard_map/ppermute | solution.py:56
  47.7 16.6 %collective-permute-start.13 = (bf16[1024,256]{1,0:T(8,128)(2,1)}, bf16[1024,256]{1,0:T(8,128)(2,1)S(1)}, u32[]{:S(2)}, u32[]{:S(2)}) collective-permute-start(bf16[1024,256]{1,0:T(8,128)(2,1)} %collective-permute-done.5.refs_6_), channel_id=1, source_target_pairs={{0,16},{1,17},{2,18},{3,19},{4,20},{5,21},{6,22},{7,23},{8,24},{9,... | collective-permute-start | bytes 1572872 | tf_op jit(solution)/shard_map/ppermute | solution.py:56
  50.2 14.2 %copy-start.13 = (bf16[1024,256]{1,0:T(8,128)(2,1)}, bf16[1024,256]{1,0:T(8,128)(2,1)S(1)}, u32[]{:S(2)}) copy-start(bf16[1024,256]{1,0:T(8,128)(2,1)S(1)} %pad_maximum_fusion.4.refs_4_) | copy-start | bytes 1572868
  50.2 14.2 %copy-start.20 = (bf16[1024,256]{1,0:T(8,128)(2,1)}, bf16[1024,256]{1,0:T(8,128)(2,1)S(1)}, u32[]{:S(2)}) copy-start(bf16[1024,256]{1,0:T(8,128)(2,1)S(1)} %collective-permute-done.16.refs_3_) | copy-start | bytes 1572868
  50.2 14.2 %collective-permute-start.17 = (bf16[1024,256]{1,0:T(8,128)(2,1)S(1)}, bf16[1024,256]{1,0:T(8,128)(2,1)S(1)}, u32[]{:S(2)}, u32[]{:S(2)}) collective-permute-start(bf16[1024,256]{1,0:T(8,128)(2,1)S(1)} %pad_maximum_fusion.4.refs_4_), channel_id=1, source_target_pairs={{0,2},{1,3},{2,0},{3,1},{4,6},{5,7},{6,4},{7,5},{8,10},{9,11},{10,... | collective-permute-start | bytes 1572872 | tf_op jit(solution)/shard_map/ppermute | solution.py:56
  52.5 37.0 %copy-start.3 = (bf16[640,256]{1,0:T(8,128)(2,1)}, bf16[640,256]{1,0:T(8,128)(2,1)S(1)}, u32[]{:S(2)}) copy-start(bf16[640,256]{1,0:T(8,128)(2,1)S(1)} %collective-permute-done.4.refs_1_.refs_10_) | copy-start | bytes 983044
  52.5 8.4 %collective-permute-start.6 = (bf16[640,256]{1,0:T(8,128)(2,1)S(1)}, bf16[640,256]{1,0:T(8,128)(2,1)S(1)}, u32[]{:S(2)}, u32[]{:S(2)}) collective-permute-start(bf16[640,256]{1,0:T(8,128)(2,1)S(1)} %collective-permute-done.4.refs_1_.refs_10_), channel_id=1, source_target_pairs={{0,8},{1,9},{2,10},{3,11},{4,0},{5,1},{6,2},{7,3},{8,12},{9,13},{1... | collective-permute-start | bytes 983048 | tf_op jit(solution)/shard_map/ppermute | solution.py:56
  55.9 13.0 %collective-permute-start.10 = (bf16[512,256]{1,0:T(8,128)(2,1)S(1)}, bf16[512,256]{1,0:T(8,128)(2,1)S(1)}, u32[]{:S(2)}, u32[]{:S(2)}) collective-permute-start(bf16[512,256]{1,0:T(8,128)(2,1)S(1)} %slice.127), channel_id=1, source_target_pairs={{0,16},{1,17},{2,18},{3,19},{4,20},{5,21},{6,22},{7,23},{8,24},{9,... | collective-permute-start | bytes 786440 | tf_op jit(solution)/shard_map/ppermute | solution.py:56
  60.9 28.6 %copy-start.4 = (bf16[640,256]{1,0:T(8,128)(2,1)}, bf16[640,256]{1,0:T(8,128)(2,1)S(1)}, u32[]{:S(2)}) copy-start(bf16[640,256]{1,0:T(8,128)(2,1)S(1)} %collective-permute-done.6.refs_2_.refs_12_) | copy-start | bytes 983044
  60.9 8.0 %collective-permute-start.7 = (bf16[640,256]{1,0:T(8,128)(2,1)S(1)}, bf16[640,256]{1,0:T(8,128)(2,1)S(1)}, u32[]{:S(2)}, u32[]{:S(2)}) collective-permute-start(bf16[640,256]{1,0:T(8,128)(2,1)S(1)} %collective-permute-done.6.refs_2_.refs_12_), channel_id=1, source_target_pairs={{0,8},{1,9},{2,10},{3,11},{4,0},{5,1},{6,2},{7,3},{8,12},{9,13},{1... | collective-permute-start | bytes 983048 | tf_op jit(solution)/shard_map/ppermute | solution.py:56
  64.3 4.6 %copy-start.18 = (bf16[1024,256]{1,0:T(8,128)(2,1)}, bf16[1024,256]{1,0:T(8,128)(2,1)S(1)}, u32[]{:S(2)}) copy-start(bf16[1024,256]{1,0:T(8,128)(2,1)S(1)} %collective-permute-done.13.refs_7_) | copy-start | bytes 1572868
  64.4 14.2 %copy-start.14 = (bf16[1024,256]{1,0:T(8,128)(2,1)}, bf16[1024,256]{1,0:T(8,128)(2,1)S(1)}, u32[]{:S(2)}) copy-start(bf16[1024,256]{1,0:T(8,128)(2,1)S(1)} %pad_maximum_fusion.5.refs_6_) | copy-start | bytes 1572868
  64.4 14.2 %copy-start.21 = (bf16[1024,256]{1,0:T(8,128)(2,1)}, bf16[1024,256]{1,0:T(8,128)(2,1)S(1)}, u32[]{:S(2)}) copy-start(bf16[1024,256]{1,0:T(8,128)(2,1)S(1)} %collective-permute-done.17.refs_5_) | copy-start | bytes 1572868
  64.4 14.2 %collective-permute-start.18 = (bf16[1024,256]{1,0:T(8,128)(2,1)S(1)}, bf16[1024,256]{1,0:T(8,128)(2,1)S(1)}, u32[]{:S(2)}, u32[]{:S(2)}) collective-permute-start(bf16[1024,256]{1,0:T(8,128)(2,1)S(1)} %pad_maximum_fusion.5.refs_6_), channel_id=1, source_target_pairs={{0,2},{1,3},{2,0},{3,1},{4,6},{5,7},{6,4},{7,5},{8,10},{9,11},{10,... | collective-permute-start | bytes 1572872 | tf_op jit(solution)/shard_map/ppermute | solution.py:56
  66.0 12.6 %collective-permute-start.14 = (bf16[512,256]{1,0:T(8,128)(2,1)S(1)}, bf16[512,256]{1,0:T(8,128)(2,1)S(1)}, u32[]{:S(2)}, u32[]{:S(2)}) collective-permute-start(bf16[512,256]{1,0:T(8,128)(2,1)S(1)} %slice.128), channel_id=1, source_target_pairs={{0,16},{1,17},{2,18},{3,19},{4,20},{5,21},{6,22},{7,23},{8,24},{9,... | collective-permute-start | bytes 786440 | tf_op jit(solution)/shard_map/ppermute | solution.py:56
  68.9 20.6 %copy-start.5 = (bf16[640,256]{1,0:T(8,128)(2,1)}, bf16[640,256]{1,0:T(8,128)(2,1)S(1)}, u32[]{:S(2)}) copy-start(bf16[640,256]{1,0:T(8,128)(2,1)S(1)} %collective-permute-done.7.refs_3_.refs_14_) | copy-start | bytes 983044
  68.9 9.6 %copy-start.23 = (bf16[512,256]{1,0:T(8,128)(2,1)}, bf16[512,256]{1,0:T(8,128)(2,1)S(1)}, u32[]{:S(2)}) copy-start(bf16[512,256]{1,0:T(8,128)(2,1)S(1)} %collective-permute-done.10.refs_11_) | copy-start | bytes 786436
  68.9 9.7 %collective-permute-start.15 = (bf16[512,256]{1,0:T(8,128)(2,1)S(1)}, bf16[512,256]{1,0:T(8,128)(2,1)S(1)}, u32[]{:S(2)}, u32[]{:S(2)}) collective-permute-start(bf16[512,256]{1,0:T(8,128)(2,1)S(1)} %slice.129), channel_id=1, source_target_pairs={{0,16},{1,17},{2,18},{3,19},{4,20},{5,21},{6,22},{7,23},{8,24},{9,... | collective-permute-start | bytes 786440 | tf_op jit(solution)/shard_map/ppermute | solution.py:56
  78.6 10.9 %copy-start.2 = (bf16[640,256]{1,0:T(8,128)(2,1)S(1)}, bf16[640,256]{1,0:T(8,128)(2,1)}, u32[]{:S(2)}) copy-start(bf16[640,256]{1,0:T(8,128)(2,1)} %copy-done.1) | copy-start | bytes 983044
  78.6 10.8 %copy-start.24 = (bf16[512,256]{1,0:T(8,128)(2,1)}, bf16[512,256]{1,0:T(8,128)(2,1)S(1)}, u32[]{:S(2)}) copy-start(bf16[512,256]{1,0:T(8,128)(2,1)S(1)} %collective-permute-done.14.refs_13_) | copy-start | bytes 786436
  78.6 10.7 %copy-start.25 = (bf16[512,256]{1,0:T(8,128)(2,1)}, bf16[512,256]{1,0:T(8,128)(2,1)S(1)}, u32[]{:S(2)}) copy-start(bf16[512,256]{1,0:T(8,128)(2,1)S(1)} %collective-permute-done.15.refs_15_) | copy-start | bytes 786436
  78.7 0.8 copy-start.22
  89.4 3.2 %collective-permute-start.19 = (bf16[1088,512]{1,0:T(8,128)(2,1)}, bf16[1088,512]{1,0:T(8,128)(2,1)}, u32[]{:S(2)}, u32[]{:S(2)}) collective-permute-start(bf16[1088,512]{1,0:T(8,128)(2,1)} %shard_map.76.refs_2_), channel_id=1, source_target_pairs={{0,1},{1,0},{2,3},{3,2},{4,5},{5,4},{6,7},{7,6},{8,9},{9,8},{10,11... | collective-permute-start | bytes 3342344 | tf_op jit(solution)/shard_map/ppermute | solution.py:56
  89.9 2.7 %copy-start.6 = (bf16[4,128,256]{2,1,0:T(8,128)(2,1)}, bf16[4,128,256]{2,1,0:T(8,128)(2,1)S(1)}, u32[]{:S(2)}) copy-start(bf16[4,128,256]{2,1,0:T(8,128)(2,1)S(1)} %shard_map.74.refs_0_) | copy-start | bytes 786436
  89.9 2.7 %collective-permute-start.8 = (bf16[4,128,256]{2,1,0:T(8,128)(2,1)S(1)}, bf16[4,128,256]{2,1,0:T(8,128)(2,1)S(1)}, u32[]{:S(2)}, u32[]{:S(2)}) collective-permute-start(bf16[4,128,256]{2,1,0:T(8,128)(2,1)S(1)} %shard_map.74.refs_0_), channel_id=1, source_target_pairs={{0,1},{1,0},{2,3},{3,2},{4,5},{5,4},{6,7},{7,6},{8,9},{9,8},{10,11... | collective-permute-start | bytes 786440 | tf_op jit(solution)/shard_map/ppermute | solution.py:56
  92.6 0.7 copy-start.26
  93.3 30.0 %copy-start = (bf16[256,8192]{1,0:T(8,128)(2,1)S(1)}, bf16[256,8192]{1,0:T(8,128)(2,1)}, u32[]{:S(2)}) copy-start(bf16[256,8192]{1,0:T(8,128)(2,1)} %refs_7_.1) | copy-start | bytes 12582916
  104.5 2.4 %collective-permute-start.20 = (bf16[4,2,144,128]{3,2,1,0:T(8,128)(2,1)}, bf16[4,2,144,128]{3,2,1,0:T(8,128)(2,1)S(1)}, u32[]{:S(2)}, u32[]{:S(2)}) collective-permute-start(bf16[4,2,144,128]{3,2,1,0:T(8,128)(2,1)} %get-tuple-element.53), channel_id=1, source_target_pairs={{0,1},{1,0},{2,3},{3,2},{4,5},{5,4},{6,7},{7,6},{8,9},{9,8},{10,11... | collective-permute-start | bytes 884744 | tf_op jit(solution)/shard_map/ppermute | solution.py:56
  105.6 13.2 %collective-permute-start.25 = (f32[64,512]{1,0:T(8,128)}, f32[64,512]{1,0:T(8,128)S(1)}, u32[]{:S(2)}, u32[]{:S(2)}) collective-permute-start(f32[64,512]{1,0:T(8,128)} %get-tuple-element.60), channel_id=1, source_target_pairs={{0,1},{1,0},{2,3},{3,2},{4,5},{5,4},{6,7},{7,6},{8,9},{9,8},{10,11... | collective-permute-start | bytes 393224 | tf_op jit(solution)/shard_map/ppermute | solution.py:56
  106.9 1.0 copy-start.8
  107.9 5.9 %collective-permute-start.21 = (bf16[4,144,128]{2,1,0:T(8,128)(2,1)S(1)}, bf16[4,144,128]{2,1,0:T(8,128)(2,1)S(1)}, u32[]{:S(2)}, u32[]{:S(2)}) collective-permute-start(bf16[4,144,128]{2,1,0:T(8,128)(2,1)S(1)} %get-tuple-element.55), channel_id=1, source_target_pairs={{0,2},{1,3},{2,0},{3,1},{4,6},{5,7},{6,4},{7,5},{8,10},{9,11},{10,... | collective-permute-start | bytes 442376 | tf_op jit(solution)/shard_map/ppermute | solution.py:56
  113.9 5.7 %collective-permute-start.22 = (bf16[144,128]{1,0:T(8,128)(2,1)S(1)}, bf16[144,128]{1,0:T(8,128)(2,1)S(1)}, u32[]{:S(2)}, u32[]{:S(2)}) collective-permute-start(bf16[144,128]{1,0:T(8,128)(2,1)S(1)} %get-tuple-element.57), channel_id=1, source_target_pairs={{0,4},{1,5},{2,6},{3,7},{4,0},{5,1},{6,2},{7,3},{8,12},{9,13},{10,... | collective-permute-start | bytes 110600 | tf_op jit(solution)/shard_map/ppermute | solution.py:56
  116.4 5.6 %collective-permute-start.23 = (bf16[144,128]{1,0:T(8,128)(2,1)S(1)}, bf16[144,128]{1,0:T(8,128)(2,1)S(1)}, u32[]{:S(2)}, u32[]{:S(2)}) collective-permute-start(bf16[144,128]{1,0:T(8,128)(2,1)S(1)} %get-tuple-element.58), channel_id=1, source_target_pairs={{0,8},{1,9},{2,10},{3,11},{4,12},{5,13},{6,14},{7,15},{8,0},{9,1},... | collective-permute-start | bytes 110600 | tf_op jit(solution)/shard_map/ppermute | solution.py:56
  117.5 5.8 %collective-permute-start.24 = (bf16[144,128]{1,0:T(8,128)(2,1)S(1)}, bf16[144,128]{1,0:T(8,128)(2,1)S(1)}, u32[]{:S(2)}, u32[]{:S(2)}) collective-permute-start(bf16[144,128]{1,0:T(8,128)(2,1)S(1)} %get-tuple-element.59), channel_id=1, source_target_pairs={{0,12},{1,13},{2,14},{3,15},{4,8},{5,9},{6,10},{7,11},{8,4},{9,5},... | collective-permute-start | bytes 110600 | tf_op jit(solution)/shard_map/ppermute | solution.py:56
  125.0 2.0 %collective-permute-start.26 = (bf16[64,4096]{1,0:T(8,128)(2,1)S(1)}, bf16[64,4096]{1,0:T(8,128)(2,1)S(1)}, u32[]{:S(2)}, u32[]{:S(2)}) collective-permute-start(bf16[64,4096]{1,0:T(8,128)(2,1)S(1)} %slice.141), channel_id=1, source_target_pairs={{0,1},{1,0},{2,3},{3,2},{4,5},{5,4},{6,7},{7,6},{8,9},{9,8},{10,11... | collective-permute-start | bytes 1572872 | tf_op jit(solution)/shard_map/ppermute | solution.py:56
  127.1 8.4 %collective-permute-start.27 = (bf16[64,2048]{1,0:T(8,128)(2,1)S(1)}, bf16[64,2048]{1,0:T(8,128)(2,1)S(1)}, u32[]{:S(2)}, u32[]{:S(2)}) collective-permute-start(bf16[64,2048]{1,0:T(8,128)(2,1)S(1)} %slice.143), channel_id=1, source_target_pairs={{0,2},{1,3},{2,0},{3,1},{4,6},{5,7},{6,4},{7,5},{8,10},{9,11},{10,... | collective-permute-start | bytes 786440 | tf_op jit(solution)/shard_map/ppermute | solution.py:56
  135.6 6.7 %collective-permute-start.30 = (bf16[64,512]{1,0:T(8,128)(2,1)S(1)}, bf16[64,512]{1,0:T(8,128)(2,1)S(1)}, u32[]{:S(2)}, u32[]{:S(2)}) collective-permute-start(bf16[64,512]{1,0:T(8,128)(2,1)S(1)} %get-tuple-element.70), channel_id=1, source_target_pairs={{0,12},{1,13},{2,14},{3,15},{4,8},{5,9},{6,10},{7,11},{8,4},{9,5},... | collective-permute-start | bytes 196616 | tf_op jit(solution)/shard_map/ppermute | solution.py:56
  137.1 6.7 %collective-permute-start.29 = (bf16[64,512]{1,0:T(8,128)(2,1)S(1)}, bf16[64,512]{1,0:T(8,128)(2,1)S(1)}, u32[]{:S(2)}, u32[]{:S(2)}) collective-permute-start(bf16[64,512]{1,0:T(8,128)(2,1)S(1)} %get-tuple-element.71), channel_id=1, source_target_pairs={{0,8},{1,9},{2,10},{3,11},{4,12},{5,13},{6,14},{7,15},{8,0},{9,1},... | collective-permute-start | bytes 196616 | tf_op jit(solution)/shard_map/ppermute | solution.py:56
  137.3 6.5 %collective-permute-start.28 = (bf16[64,512]{1,0:T(8,128)(2,1)S(1)}, bf16[64,512]{1,0:T(8,128)(2,1)S(1)}, u32[]{:S(2)}, u32[]{:S(2)}) collective-permute-start(bf16[64,512]{1,0:T(8,128)(2,1)S(1)} %get-tuple-element.69), channel_id=1, source_target_pairs={{0,4},{1,5},{2,6},{3,7},{4,0},{5,1},{6,2},{7,3},{8,12},{9,13},{10,... | collective-permute-start | bytes 196616 | tf_op jit(solution)/shard_map/ppermute | solution.py:56
